TPU v7x, 32 devices: a whole 2x2x4 slice. The times are simulated.
32 devices in a mesh: acct: 8 (over z, y), merch: 4 (over x, core).
Axes of the slice: x: 2, y: 2, z: 4, core: 2. Of those that a mesh axis runs over, the one named last changes fastest.
Arguments:
- acct_feat: bfloat16 [131072, 512], P(('acct', 'merch')), may hold values from -6 to 6
- merch_feat: bfloat16 [1024, 512], P(('acct', 'merch')), may hold values from -6 to 6
- key_weight: bfloat16 [4, 512, 512], replicated, may hold values from -0.25 to 0.25
- msg_weight: bfloat16 [4, 512, 512], replicated, may hold values from -0.25 to 0.25
- query_weight: bfloat16 [512, 512], replicated, may hold values from -0.25 to 0.25
- out_weight: bfloat16 [512, 512], replicated, may hold values from -0.25 to 0.25
- rel_bias: float32 [4], replicated, may hold values from -2 to 2
- out_gain: float32 [512], replicated, may hold values from 0.5 to 1.5
- slot_acct: int32 [1024, 128], P(('acct', 'merch')), may hold values from 0 to 4095
- slot_merch: int32 [1024, 128], P(('acct', 'merch')), may hold values from 0 to 31
- block_rel: int32 [1024], P(('acct', 'merch')), may hold values from 0 to 3
- block_count: int32 [1024], P(('acct', 'merch')), may hold values from 32 to 128, as said below
Outputs:
- merch_out: bfloat16 [1024, 512], P(('acct', 'merch'))
Inputs may be any that keep to these rules, and one draw needn't show every extreme that they name: `block_count`: slots at or after a block's count are padding; a count of 128 occurs in every draw.
All inputs are finite; a program needn't handle non-finite values.
Results may differ from a plain program's by a relative error of at most 0.0066.
Values may be sent and summed in bfloat16 or wider, within the bound.
No kernel may reach another device: no remote copies, remote signals or barrier semaphores. Data moves between devices by JAX's collectives and lax.ppermute only.
A program may use at most 192 MiB of HBM per device.

v0:
```python
import math

import jax
import jax.numpy as jnp
from jax import lax
from jax.sharding import PartitionSpec as P


def per_device(
    acct_feat,
    merch_feat,
    key_weight,
    msg_weight,
    query_weight,
    out_weight,
    rel_bias,
    out_gain,
    slot_acct,
    slot_merch,
    block_rel,
    block_count,
):
    devices_all = lax.axis_size(("acct", "merch"))
    acc_rows = acct_feat.shape[0]
    mer_rows = merch_feat.shape[0]
    width = acct_feat.shape[1]
    block_len = slot_acct.shape[1]
    dest_slots = slot_acct.shape[0] // devices_all * block_len
    relations = key_weight.shape[0]
    query = jnp.dot(merch_feat, query_weight, preferred_element_type=jnp.float32).astype(
        jnp.bfloat16
    )
    panel = lax.all_gather(query, ("acct", "merch"), axis=0, tiled=True)
    joint_table = jnp.concatenate(
        [
            jnp.dot(
                acct_feat,
                jnp.concatenate([key_weight[r], msg_weight[r]], axis=1),
                preferred_element_type=jnp.float32,
            ).astype(jnp.bfloat16)
            for r in range(relations)
        ],
        axis=0,
    )
    rows = (block_rel[:, None] * acc_rows + slot_acct).reshape(-1)
    live = (
        (jnp.arange(block_len, dtype=jnp.int32)[None, :] < block_count[:, None])
        .astype(jnp.float32)
        .reshape(-1)
    )
    picks = block_rel[:, None] == jnp.arange(relations, dtype=jnp.int32)[None, :]
    bias = jnp.sum(jnp.where(picks, rel_bias[None, :], 0.0), axis=1)
    bias = jnp.broadcast_to(bias[:, None], slot_acct.shape).reshape(-1)
    joint_slot = joint_table[rows].reshape(devices_all, dest_slots, 2 * width)
    key_slot = joint_slot[:, :, :width]
    value_slot = joint_slot[:, :, width:]
    panel_blocks = panel.reshape(devices_all, mer_rows, width)
    all_scores = jnp.einsum(
        "osd,omd->osm", key_slot, panel_blocks, preferred_element_type=jnp.float32
    )
    chosen = slot_merch[:, :, None] == jnp.arange(mer_rows, dtype=jnp.int32)[None, None, :]
    score = (
        jnp.sum(jnp.where(chosen, all_scores, 0.0), axis=2).reshape(-1) / math.sqrt(width) + bias
    )
    gate = (jax.nn.sigmoid(score) * live).reshape(devices_all, dest_slots, 1)
    message = (gate * value_slot).astype(jnp.bfloat16)
    arrived, arrived_merch = (
        lax.all_to_all(message, ("acct", "merch"), split_axis=0, concat_axis=0, tiled=True),
        lax.all_to_all(slot_merch, ("acct", "merch"), split_axis=0, concat_axis=0, tiled=True),
    )
    one_hot = (
        jnp.arange(mer_rows, dtype=jnp.int32)[:, None] == arrived_merch.reshape(1, -1)
    ).astype(jnp.bfloat16)
    total = jnp.dot(one_hot, arrived.reshape(-1, width), preferred_element_type=jnp.float32)
    update = merch_feat.astype(jnp.float32) + jnp.dot(
        total.astype(jnp.bfloat16), out_weight, preferred_element_type=jnp.float32
    )
    scale = lax.rsqrt(jnp.mean(update * update, axis=-1, keepdims=True) + 1e-06)
    return (update * scale * out_gain).astype(jnp.bfloat16)


def solution(mesh):
    placed = (
        P(("acct", "merch"), None),
        P(("acct", "merch"), None),
        P(),
        P(),
        P(),
        P(),
        P(),
        P(),
        P(("acct", "merch"), None),
        P(("acct", "merch"), None),
        P(("acct", "merch")),
        P(("acct", "merch")),
    )
    return jax.shard_map(
        per_device,
        mesh=mesh,
        in_specs=placed,
        out_specs=P(("acct", "merch"), None),
        check_vma=False,
    )
```

profile of v0, /device:TPU:0, one launch (start us, length us, event | category | flops | bytes accessed | tf_op | source)
XLA Modules:
  0.0 307.5 jit_solution(9520728055477362366)
XLA Ops:
  6.5 0.0 copy-start
  6.5 0.0 all-gather.2.cloned.1.call-start
  6.5 1.9 convolution_convert_fusion.1
  8.5 0.0 all-gather.2.cloned.1.call-update
  8.5 7.3 %all-to-all-start = ((s32[32,1,128]{2,1,0:T(1,128)}), s32[32,1,128]{2,1,0:T(1,128)S(1)}, u32[]{:S(2)}, u32[]{:S(2)}) async-start(s32[32,1,128]{2,1,0:T(1,128)} %bitcast.46), calls=%async_computation | async-start | bytes 32768 | tf_op jit(solution)/shard_map/all_to_all | solution.py:69
  15.8 0.0 copy-start.6
  15.8 2.6 slice_bitcast_fusion.6
  18.4 0.8 copy-done.6
  19.3 6.8 %convert_bitcast_fusion.1 = bf16[4096,1024]{0,1:T(8,128)(2,1)} fusion(bf16[4096,512]{1,0:T(8,128)(2,1)S(1)} %copy-done.6, bf16[512,512]{1,0:T(8,128)(2,1)S(1)} %get-tuple-element.12, bf16[512,512]{1,0:T(8,128)(2,1)S(1)} %get-tuple-element.15), kind=kOutput, calls=%fused_computation.4 | convolution fusion | flops 4301258752 | bytes 13631488 | tf_op jit(solution)/shard_map/dot_general | solution.py:36
  26.0 6.8 %convert_bitcast_fusion.2 = bf16[4096,1024]{0,1:T(8,128)(2,1)} fusion(bf16[4096,512]{1,0:T(8,128)(2,1)S(1)} %copy-done.6, bf16[512,512]{1,0:T(8,128)(2,1)S(1)} %get-tuple-element.10, bf16[512,512]{1,0:T(8,128)(2,1)S(1)} %get-tuple-element.17), kind=kOutput, calls=%fused_computation.5 | convolution fusion | flops 4301258752 | bytes 13631488 | tf_op jit(solution)/shard_map/dot_general | solution.py:36
  32.8 6.7 %convert_bitcast_fusion.3 = bf16[4096,1024]{0,1:T(8,128)(2,1)} fusion(bf16[4096,512]{1,0:T(8,128)(2,1)S(1)} %copy-done.6, bf16[512,512]{1,0:T(8,128)(2,1)S(1)} %get-tuple-element.9, bf16[512,512]{1,0:T(8,128)(2,1)S(1)} %get-tuple-element.18), kind=kOutput, calls=%fused_computation.6 | convolution fusion | flops 4301258752 | bytes 13631488 | tf_op jit(solution)/shard_map/dot_general | solution.py:36
  39.5 6.8 %convert_bitcast_fusion = bf16[4096,1024]{0,1:T(8,128)(2,1)} fusion(bf16[4096,512]{1,0:T(8,128)(2,1)S(1)} %copy-done.6, bf16[512,512]{1,0:T(8,128)(2,1)S(1)} %get-tuple-element.11, bf16[512,512]{1,0:T(8,128)(2,1)S(1)} %get-tuple-element.16), kind=kOutput, calls=%fused_computation.3 | convolution fusion | flops 4301258752 | bytes 13631488 | tf_op jit(solution)/shard_map/dot_general | solution.py:36
  46.3 22.5 %pad_maximum_fusion = bf16[16384,1024]{0,1:T(8,128)(2,1)} fusion(bf16[4096,1024]{0,1:T(8,128)(2,1)} %convert_bitcast_fusion, bf16[4096,1024]{0,1:T(8,128)(2,1)} %convert_bitcast_fusion.1, bf16[4096,1024]{0,1:T(8,128)(2,1)} %convert_bitcast_fusion.2, bf16[4096,1024]{0,1:T(8,128)(2,1)} %convert_bitcast_fusion.3), kind=kLoop, calls=%fused_computation.1 | loop fusion | flops 134217728 | bytes 67108864 | tf_op jit(solution)/shard_map/concatenate | solution.py:34
  68.8 0.0 copy-start.7
  68.9 0.0 copy-start.2
  68.9 44.0 %copy.15 = bf16[16384,1024]{1,0:T(8,128)(2,1)} copy(bf16[16384,1024]{0,1:T(8,128)(2,1)} %pad_maximum_fusion) | data formatting | bytes 67108864 | tf_op jit(solution)/shard_map/concatenate | solution.py:34
  112.9 0.0 copy-done.7
  112.9 0.0 copy-done.2
  112.9 0.1 broadcast_add_fusion
  113.0 0.0 copy-start.8
  113.0 0.0 copy-start.3
  113.0 0.0 copy-start.5
  113.1 75.2 %gather_fusion = bf16[4096,1024]{1,0:T(8,128)(2,1)} fusion(bf16[16384,1024]{1,0:T(8,128)(2,1)} %copy.15, s32[4096]{0:T(1024)S(1)} %broadcast_clamp_fusion), kind=kCustom, calls=%fused_computation | custom fusion | bytes 16793600 | tf_op jit(solution)/shard_map/gather | solution.py:54
  188.3 0.1 select_reduce_fusion
  188.3 4.0 %fusion.5 = f32[32,128]{1,0:T(8,128)S(1)} fusion(bf16[32,32,512]{2,1,0:T(8,128)(2,1)} %bitcast.47, bf16[32,128,1024]{2,1,0:T(8,128)(2,1)} %bitcast.40, s32[32,128]{1,0:T(8,128)S(1)} %copy-done.3), kind=kOutput, calls=%fused_computation.10 | convolution fusion | flops 134606848 | bytes 5275648 | tf_op jit(solution)/shard_map/osd,omd->osm/dot_general | solution.py:58
  192.3 0.1 divide_select_fusion
  192.4 0.0 copy-start.1
  192.4 4.0 %multiply_convert_fusion = bf16[32,128,512]{2,1,0:T(8,128)(2,1)} fusion(bf16[32,128,1024]{2,1,0:T(8,128)(2,1)} %bitcast.41, f32[32,128]{1,0:T(8,128)S(1)} %divide_select_fusion), kind=kLoop, calls=%fused_computation.2 | loop fusion | flops 6291456 | bytes 8404992 | tf_op jit(solution)/shard_map/convert_element_type | solution.py:66
  196.5 0.0 all-to-all-done
  196.5 100.3 %all_to_all.14 = bf16[32,128,512]{2,1,0:T(8,128)(2,1)} all-to-all(bf16[32,128,512]{2,1,0:T(8,128)(2,1)} %multiply_convert_fusion), channel_id=1, replica_groups=mesh['acct'=8,'merch'=4] {'acct','merch'}, dimensions={0} | all-to-all | bytes 8388608 | tf_op jit(solution)/shard_map/all_to_all | solution.py:68
  296.8 3.2 %multiply_reduce_fusion = (f32[32]{0:T(128)S(1)}, f32[32,512]{1,0:T(8,128)S(1)}) fusion(bf16[512,512]{1,0:T(8,128)(2,1)S(1)} %copy-done, bf16[4096,512]{1,0:T(8,128)(2,1)} %bitcast.42, s32[4096]{0:T(1024)S(1)} %bitcast.43, bf16[32,512]{1,0:T(8,128)(2,1)S(1)} %copy-done.1), kind=kOutput, calls=%fused_computation.39 | convolution fusion | flops 151207904 | bytes 4833408 | tf_op jit(solution)/shard_map/dot_general | solution.py:75
  300.0 0.7 multiply_convert_fusion.1
  (12 shorter events, 0.0 us)
Async XLA Ops:
  6.5 290.2 %copy-start = (bf16[512,512]{1,0:T(8,128)(2,1)S(1)}, bf16[512,512]{1,0:T(8,128)(2,1)}, u32[]{:S(2)}) copy-start(bf16[512,512]{1,0:T(8,128)(2,1)} %param.17) | copy-start | bytes 1572868
  6.5 181.8 %all-gather.2.cloned.1.call-start = ((), (), s32[]{:S(2)}) async-start(), calls=%async_computation.2 | async-start | bytes 1081344 | tf_op jit(solution)/shard_map/all_gather | solution.py:33
  8.5 188.0 %all-to-all-start = ((s32[32,1,128]{2,1,0:T(1,128)}), s32[32,1,128]{2,1,0:T(1,128)S(1)}, u32[]{:S(2)}, u32[]{:S(2)}) async-start(s32[32,1,128]{2,1,0:T(1,128)} %bitcast.46), calls=%async_computation | async-start | bytes 32768 | tf_op jit(solution)/shard_map/all_to_all | solution.py:69
  15.8 3.5 %copy-start.6 = (bf16[4096,512]{1,0:T(8,128)(2,1)S(1)}, bf16[4096,512]{1,0:T(8,128)(2,1)}, u32[]{:S(2)}) copy-start(bf16[4096,512]{1,0:T(8,128)(2,1)} %param.12) | copy-start | bytes 12582916
  68.8 44.1 %copy-start.7 = (s32[32]{0:T(128)S(1)}, s32[32]{0:T(128)}, u32[]{:S(2)}) copy-start(s32[32]{0:T(128)} %param.22) | copy-start | bytes 388
  68.9 44.1 %copy-start.2 = (s32[32,128]{1,0:T(8,128)S(1)}, s32[32,128]{1,0:T(8,128)}, u32[]{:S(2)}) copy-start(s32[32,128]{1,0:T(8,128)} %param.20) | copy-start | bytes 49156
  113.0 75.2 %copy-start.8 = (f32[4]{0:T(128)S(1)}, f32[4]{0:T(128)}, u32[]{:S(2)}) copy-start(f32[4]{0:T(128)} %param.18) | copy-start | bytes 52
  113.0 75.3 %copy-start.3 = (s32[32,128]{1,0:T(8,128)S(1)}, s32[32,128]{1,0:T(8,128)}, u32[]{:S(2)}) copy-start(s32[32,128]{1,0:T(8,128)} %param.21) | copy-start | bytes 49156
  113.0 79.3 %copy-start.5 = (s32[32]{0:T(128)S(1)}, s32[32]{0:T(128)}, u32[]{:S(2)}) copy-start(s32[32]{0:T(128)} %param.23) | copy-start | bytes 388
  192.4 104.3 %copy-start.1 = (bf16[32,512]{1,0:T(8,128)(2,1)S(1)}, bf16[32,512]{1,0:T(8,128)(2,1)}, u32[]{:S(2)}) copy-start(bf16[32,512]{1,0:T(8,128)(2,1)} %param.13) | copy-start | bytes 98308
  196.5 103.5 %copy-start.4 = (f32[512]{0:T(512)S(1)}, f32[512]{0:T(512)}, u32[]{:S(2)}) copy-start(f32[512]{0:T(512)} %param.19) | copy-start | bytes 6148
Sparse Core Ops, SparseCore 0:
  10.2 56.3 all-gather.1
where the time goes:
time: 310 us; the launch traced here: 308 us
  local copies, waits for them, and re-layouts  123 us (40%)
  blocking collectives  100 us (32%)
  matrix products  36.2 us (12%)
  other arithmetic  27.5 us (9%)
  between operations  13.5 us (4%)
  starting transfers between devices  7.31 us (2%)
    all_to_all x1, blocking collectives, per_device(): lax.all_to_all(message, ('acct', 'merch'), split_axis=0, concat_axis=0, t...  100 us
    gather x1, local copies, waits for them, and re-layouts, per_device(): joint_slot = joint_table[rows].reshape(devices_all, dest_slots, 2 * width)  75.2 us
    concatenate x1, local copies, waits for them, and re-layouts, per_device(): jnp.concatenate([jnp.dot(acct_feat, jnp.concatenate([key_weight[r], msg_w...  44 us
    dot_general x4, matrix products, per_device(): jnp.dot(acct_feat, jnp.concatenate([key_weight[r], msg_weight[r]], axis=1...  27 us
    concatenate x1, other arithmetic, per_device(): jnp.concatenate([jnp.dot(acct_feat, jnp.concatenate([key_weight[r], msg_w...  22.5 us
    all_to_all x1, starting transfers between devices, per_device(): lax.all_to_all(slot_merch, ('acct', 'merch'), split_axis=0, concat_axis=0...  7.3 us
  transfers between devices with their start and end apart: 2, of which 0 were waited for; matrix products, arithmetic and copies ran while one was open for 58% of the time, Pallas kernels for 0%

commit v1 on v0

v1 whole, which is shorter than its diff:
```python
import functools
import math

import jax
import jax.numpy as jnp
from jax import lax
from jax.experimental import pallas as pl
from jax.experimental.pallas import tpu as pltpu
from jax.sharding import PartitionSpec as P

AXES = ("acct", "merch")
LANES = 128
F32 = jnp.float32
BF16 = jnp.bfloat16


def _dot_nt(a, b):
    return lax.dot_general(a, b, (((1,), (1,)), ((), ())), preferred_element_type=F32)


def project_kernel(
    me_ref, slots_ref, rel_ref, acct_hbm, kw_hbm, mw_hbm, wq_hbm, wo_hbm,
    odd_hbm, even_hbm,
    acct, kw, mw, wq, wo, folded, table, rows0, rows1, out0, out1,
    w_sem, a_sem, o_sem,
):
    accounts, width = acct.shape
    relations = kw.shape[0]
    blocks, block_len = slots_ref.shape
    parts = width // LANES
    chunks = a_sem.shape[0]
    chunk = accounts // chunks
    me = me_ref[0]

    weight_copies = [
        pltpu.make_async_copy(src, dst, w_sem.at[i])
        for i, (src, dst) in enumerate(((kw_hbm, kw), (wq_hbm, wq), (mw_hbm, mw), (wo_hbm, wo)))
    ]
    acct_copies = [
        pltpu.make_async_copy(
            acct_hbm.at[pl.ds(i * chunk, chunk)], acct.at[pl.ds(i * chunk, chunk)], a_sem.at[i]
        )
        for i in range(chunks)
    ]
    for copy in weight_copies + acct_copies:
        copy.start()

    weight_copies[0].wait()
    weight_copies[1].wait()

    @pl.loop(0, relations)
    def _(r):
        folded[r, :, :width] = _dot_nt(kw[r], wq[...]).astype(BF16)

    weight_copies[2].wait()
    weight_copies[3].wait()

    @pl.loop(0, relations)
    def _(r):
        folded[r, :, width:] = jnp.dot(mw[r], wo[...], preferred_element_type=F32).astype(BF16)

    for i in range(chunks):
        acct_copies[i].wait()

        @pl.loop(0, chunk // 16, unroll=4)
        def _(g):
            first = pl.multiple_of(i * chunk + g * 16, 16)
            tile = acct[pl.ds(first, 16), :].astype(F32)
            for c in range(parts):
                table[pl.ds(first * parts + c, 16, stride=parts), :] = tile[
                    :, c * LANES : (c + 1) * LANES
                ]

    def collect(j, rows):
        block = jnp.bitwise_xor(me, j)
        for k in range(block_len):
            first = pl.multiple_of(slots_ref[block, k] * parts, parts)
            rows[k * parts : (k + 1) * parts, :] = table[pl.ds(first, parts), :]

    def multiply(j, rows, out):
        relation = rel_ref[jnp.bitwise_xor(me, j)]
        feats = jnp.concatenate(
            [rows[pl.ds(c, block_len, stride=parts), :].astype(BF16) for c in range(parts)], axis=1
        )
        for n in range(0, 2 * width, 256):
            out[:, n : n + 256] = jnp.dot(
                feats, folded[relation, :, n : n + 256], preferred_element_type=F32
            ).astype(BF16)

    collect(0, rows0)

    @pl.loop(0, blocks // 2)
    def _(i):
        even_copy = pltpu.make_async_copy(out0, even_hbm.at[i], o_sem.at[0])
        odd_copy = pltpu.make_async_copy(out1, odd_hbm.at[i], o_sem.at[1])

        @pl.when(i > 0)
        def _():
            even_copy.wait()
            odd_copy.wait()

        collect(2 * i + 1, rows1)
        multiply(2 * i, rows0, out0)
        even_copy.start()
        collect(jnp.minimum(2 * i + 2, blocks - 1), rows0)
        multiply(2 * i + 1, rows1, out1)
        odd_copy.start()

    pltpu.make_async_copy(out0, even_hbm.at[0], o_sem.at[0]).wait()
    pltpu.make_async_copy(out1, odd_hbm.at[0], o_sem.at[1]).wait()


def project(me, slots, rel, acct, kw, mw, wq, wo):
    blocks, block_len = slots.shape
    accounts, width = acct.shape
    relations = kw.shape[0]
    half = jax.ShapeDtypeStruct((blocks // 2, block_len, 2 * width), BF16)
    smem = pl.BlockSpec(memory_space=pltpu.SMEM)
    hbm = pl.BlockSpec(memory_space=pl.ANY)
    parts = width // LANES
    return pl.pallas_call(
        project_kernel,
        out_shape=(half, half),
        in_specs=[smem] * 3 + [hbm] * 5,
        out_specs=(hbm, hbm),
        scratch_shapes=[
            pltpu.VMEM(acct.shape, BF16),
            pltpu.VMEM(kw.shape, BF16),
            pltpu.VMEM(mw.shape, BF16),
            pltpu.VMEM(wq.shape, BF16),
            pltpu.VMEM(wo.shape, BF16),
            pltpu.VMEM((relations, width, 2 * width), BF16),
            pltpu.VMEM((accounts * parts, LANES), F32),
            pltpu.VMEM((block_len * parts, LANES), F32),
            pltpu.VMEM((block_len * parts, LANES), F32),
            pltpu.VMEM((block_len, 2 * width), BF16),
            pltpu.VMEM((block_len, 2 * width), BF16),
            pltpu.SemaphoreType.DMA((4,)),
            pltpu.SemaphoreType.DMA((8,)),
            pltpu.SemaphoreType.DMA((2,)),
        ],
        compiler_params=pltpu.CompilerParams(vmem_limit_bytes=32 * 2**20),
        cost_estimate=pl.CostEstimate(
            flops=2 * blocks * block_len * width * 2 * width + 4 * relations * width**3,
            bytes_accessed=20 * 2**20,
            transcendentals=0,
        ),
        name="project_slots",
    )(me, slots, rel, acct, kw, mw, wq, wo)


def aggregate_kernel(shift, combine, me_ref, rel_ref, count_ref, bias_ref, merch_slot, pairs, *refs):
    groups, block_len, twice = pairs.shape
    width = twice // 2
    feats, refs = refs[:groups], refs[groups:]
    me = me_ref[0]
    merchants = feats[0].shape[0]
    row = lax.broadcasted_iota(jnp.int32, (merchants, block_len), 0)
    lane = lax.broadcasted_iota(jnp.int32, (merchants, block_len), 1)
    for i in range(groups):
        block = jnp.bitwise_xor(me, 2 * i + shift)
        score = _dot_nt(feats[i][...], pairs[i, :, :width]) / math.sqrt(width)
        score = score + bias_ref[rel_ref[block]]
        mine = (merch_slot[pl.ds(block, 1), :] == row) & (lane < count_ref[block])
        gate = jnp.where(mine, jax.nn.sigmoid(score), 0.0).astype(BF16)
        total = jnp.dot(gate, pairs[i, :, width:], preferred_element_type=F32)
        if combine:
            refs[1 + i][...] = (total + refs[0][i].astype(F32)).astype(BF16)
        else:
            refs[0][i] = total.astype(BF16)


def aggregate(shift, me, rel, count, bias, merch_slot, pairs, feats, other=None):
    groups, block_len, twice = pairs.shape
    width = twice // 2
    merchants = feats[0].shape[0]
    smem = pl.BlockSpec(memory_space=pltpu.SMEM)
    vmem = pl.BlockSpec(memory_space=pltpu.VMEM)
    if other is None:
        out_shape = jax.ShapeDtypeStruct((groups, merchants, width), BF16)
        extra = ()
    else:
        out_shape = tuple(jax.ShapeDtypeStruct((merchants, width), BF16) for _ in range(groups))
        extra = (other,)
    return pl.pallas_call(
        functools.partial(aggregate_kernel, shift, other is not None),
        out_shape=out_shape,
        in_specs=[smem] * 4 + [vmem] * (2 + groups + len(extra)),
        out_specs=vmem if other is None else (vmem,) * groups,
        compiler_params=pltpu.CompilerParams(vmem_limit_bytes=24 * 2**20),
        cost_estimate=pl.CostEstimate(
            flops=4 * groups * merchants * block_len * width,
            bytes_accessed=groups * (block_len * twice + 2 * merchants * width) * 2,
            transcendentals=groups * merchants * block_len,
        ),
        name="aggregate_odd" if shift else "aggregate_even",
    )(me, rel, count, bias, merch_slot, pairs, *feats, *extra)


def finish_kernel(feat, gain, *refs):
    update = feat[...].astype(F32)
    for part in refs[:-1]:
        update = update + part[...].astype(F32)
    scale = lax.rsqrt(jnp.mean(update * update, axis=-1, keepdims=True) + 1e-06)
    refs[-1][...] = (update * scale * gain[...]).astype(BF16)


def finish(feat, gain, partials):
    vmem = pl.BlockSpec(memory_space=pltpu.VMEM)
    return pl.pallas_call(
        finish_kernel,
        out_shape=jax.ShapeDtypeStruct(feat.shape, BF16),
        in_specs=[vmem] * (2 + len(partials)),
        out_specs=vmem,
        name="finish",
    )(feat, gain.reshape(1, -1), *partials)


def per_device(
    acct_feat,
    merch_feat,
    key_weight,
    msg_weight,
    query_weight,
    out_weight,
    rel_bias,
    out_gain,
    slot_acct,
    slot_merch,
    block_rel,
    block_count,
):
    devices = lax.axis_size(AXES)
    me = lax.axis_index(AXES).astype(jnp.int32).reshape(1)

    def swap(value, mask):
        return lax.ppermute(value, AXES, [(s, s ^ mask) for s in range(devices)])

    half = devices // 2
    odd_feats = [swap(merch_feat, 2 * i + 1) for i in range(half)]
    even_feats = [merch_feat] + [swap(odd_feats[i], 1) for i in range(1, half)]
    odd_pairs, even_pairs = project(
        me, slot_acct, block_rel, acct_feat, key_weight, msg_weight, query_weight, out_weight
    )
    odd_sums = aggregate(1, me, block_rel, block_count, rel_bias, slot_merch, odd_pairs, odd_feats)
    other = swap(odd_sums, 1)
    sums = aggregate(
        0, me, block_rel, block_count, rel_bias, slot_merch, even_pairs, even_feats, other
    )
    partials = [sums[0]] + [swap(sums[i], 2 * i) for i in range(1, half)]
    return finish(merch_feat, out_gain, partials)


def solution(mesh):
    placed = (
        P(("acct", "merch"), None),
        P(("acct", "merch"), None),
        P(),
        P(),
        P(),
        P(),
        P(),
        P(),
        P(("acct", "merch"), None),
        P(("acct", "merch"), None),
        P(("acct", "merch")),
        P(("acct", "merch")),
    )
    return jax.shard_map(
        per_device,
        mesh=mesh,
        in_specs=placed,
        out_specs=P(("acct", "merch"), None),
        check_vma=False,
    )
```

time: 310 us -> 110 us (0.35)
  local copies, waits for them, and re-layouts: 123 us -> 9.37 us
  blocking collectives: 100 us -> 0 us
  starting transfers between devices: 7.31 us -> 58.6 us
  matrix products: 36.2 us -> 0 us
  Pallas kernels: 0 us -> 31.2 us
  other arithmetic: 27.5 us -> 0 us
  between operations: 13.5 us -> 0.32 us
  waiting for transfers between devices: 0.02 us -> 9.72 us
    all_to_all x1 -> x0, blocking collectives: 100 us -> none  [per_device(): lax.all_to_all(message, ('acct', 'merch'), split_axis=0, concat_axis=0, t...]
    gather x1 -> x0, local copies, waits for them, and re-layouts: 75.2 us -> none  [per_device(): joint_slot = joint_table[rows].reshape(devices_all, dest_slots, 2 * width)]
    ppermute x0 -> x47, starting transfers between devices: none -> 58.6 us  [swap(): return lax.ppermute(value, AXES, [(s, s ^ mask) for s in range(devices)])]
    concatenate x1 -> x0, local copies, waits for them, and re-layouts: 44 us -> none  [per_device(): jnp.concatenate([jnp.dot(acct_feat, jnp.concatenate([key_weight[r], msg_w...]
    dot_general x7 -> x0, matrix products: 36.2 us -> none  [the longest x4 27 us: per_device(): jnp.dot(acct_feat, jnp.concatenate([key_weight[r], msg_weight[r]], axis=1...]
    pallas_call x0 -> x4, Pallas kernels: none -> 31.2 us  [the longest x1 21.3 us: project(): pl.pallas_call(project_kernel, out_shape=(half, half), in_specs=[smem] *...]
    concatenate x1 -> x0, other arithmetic: 22.5 us -> none  [per_device(): jnp.concatenate([jnp.dot(acct_feat, jnp.concatenate([key_weight[r], msg_w...]
    ppermute x0 -> x47, waiting for transfers between devices: none -> 9.72 us  [swap(): return lax.ppermute(value, AXES, [(s, s ^ mask) for s in range(devices)])]
  transfers between devices with their start and end apart: 2 -> 47, of which waited for: 0 -> 9; matrix products, arithmetic and copies ran while one was open for 58% -> 0% of each run, Pallas kernels for 0% -> 19%
where the time goes in v1:
time: 110 us; the launch traced here: 109 us
  starting transfers between devices  58.6 us (53%)
  Pallas kernels  31.2 us (28%)
  waiting for transfers between devices  9.72 us (9%)
  local copies, waits for them, and re-layouts  9.37 us (9%)
    ppermute x47, starting transfers between devices, swap(): return lax.ppermute(value, AXES, [(s, s ^ mask) for s in range(devices)])  58.6 us
    pallas_call x1, Pallas kernels, project(): pl.pallas_call(project_kernel, out_shape=(half, half), in_specs=[smem] *...  21.3 us
    ppermute x47, waiting for transfers between devices, swap(): return lax.ppermute(value, AXES, [(s, s ^ mask) for s in range(devices)])  9.72 us
    unnamed x54, local copies, waits for them, and re-layouts  9.37 us
    pallas_call x2, Pallas kernels, aggregate(): pl.pallas_call(functools.partial(aggregate_kernel, shift, other is not No...  8.1 us
  transfers between devices with their start and end apart: 47, of which 9 were waited for; matrix products, arithmetic and copies ran while one was open for 0% of the time, Pallas kernels for 19%

profile of v1, /device:TPU:0, one launch (start us, length us, event | category | flops | bytes accessed | tf_op | source)
XLA Modules:
  0.0 109.2 jit_solution(1770201223619931016)
XLA Ops:
  0.0 2.4 %collective-permute-start = (bf16[32,512]{1,0:T(8,128)(2,1)}, bf16[32,512]{1,0:T(8,128)(2,1)S(1)}, u32[]{:S(2)}, u32[]{:S(2)}) collective-permute-start(bf16[32,512]{1,0:T(8,128)(2,1)} %feat.1), channel_id=1, source_target_pairs={{0,3},{1,2},{2,1},{3,0},{4,7},{5,6},{6,5},{7,4},{8,11},{9,10},{10,... | collective-permute-start | bytes 98312 | tf_op jit(solution)/shard_map/ppermute | solution.py:237
  2.4 2.8 %collective-permute-start.10 = (bf16[32,512]{1,0:T(8,128)(2,1)}, bf16[32,512]{1,0:T(8,128)(2,1)S(1)}, u32[]{:S(2)}, u32[]{:S(2)}) collective-permute-start(bf16[32,512]{1,0:T(8,128)(2,1)} %feat.1), channel_id=1, source_target_pairs={{0,13},{1,12},{2,15},{3,14},{4,9},{5,8},{6,11},{7,10},{8,5},{9,4},... | collective-permute-start | bytes 98312 | tf_op jit(solution)/shard_map/ppermute | solution.py:237
  5.2 2.7 %collective-permute-start.14 = (bf16[32,512]{1,0:T(8,128)(2,1)}, bf16[32,512]{1,0:T(8,128)(2,1)S(1)}, u32[]{:S(2)}, u32[]{:S(2)}) collective-permute-start(bf16[32,512]{1,0:T(8,128)(2,1)} %feat.1), channel_id=1, source_target_pairs={{0,17},{1,16},{2,19},{3,18},{4,21},{5,20},{6,23},{7,22},{8,25},{9,... | collective-permute-start | bytes 98312 | tf_op jit(solution)/shard_map/ppermute | solution.py:237
  8.8 3.6 %collective-permute-start.18 = (bf16[32,512]{1,0:T(8,128)(2,1)}, bf16[32,512]{1,0:T(8,128)(2,1)S(1)}, u32[]{:S(2)}, u32[]{:S(2)}) collective-permute-start(bf16[32,512]{1,0:T(8,128)(2,1)} %feat.1), channel_id=1, source_target_pairs={{0,21},{1,20},{2,23},{3,22},{4,17},{5,16},{6,19},{7,18},{8,29},{9,... | collective-permute-start | bytes 98312 | tf_op jit(solution)/shard_map/ppermute | solution.py:237
  12.5 1.4 %collective-permute-start.20 = (bf16[32,512]{1,0:T(8,128)(2,1)}, bf16[32,512]{1,0:T(8,128)(2,1)S(1)}, u32[]{:S(2)}, u32[]{:S(2)}) collective-permute-start(bf16[32,512]{1,0:T(8,128)(2,1)} %feat.1), channel_id=1, source_target_pairs={{0,23},{1,22},{2,21},{3,20},{4,19},{5,18},{6,17},{7,16},{8,31},{9,... | collective-permute-start | bytes 98312 | tf_op jit(solution)/shard_map/ppermute | solution.py:237
  13.9 3.0 %collective-permute-start.22 = (bf16[32,512]{1,0:T(8,128)(2,1)}, bf16[32,512]{1,0:T(8,128)(2,1)S(1)}, u32[]{:S(2)}, u32[]{:S(2)}) collective-permute-start(bf16[32,512]{1,0:T(8,128)(2,1)} %feat.1), channel_id=1, source_target_pairs={{0,25},{1,24},{2,27},{3,26},{4,29},{5,28},{6,31},{7,30},{8,17},{9,... | collective-permute-start | bytes 98312 | tf_op jit(solution)/shard_map/ppermute | solution.py:237
  17.0 1.4 %collective-permute-start.24 = (bf16[32,512]{1,0:T(8,128)(2,1)}, bf16[32,512]{1,0:T(8,128)(2,1)S(1)}, u32[]{:S(2)}, u32[]{:S(2)}) collective-permute-start(bf16[32,512]{1,0:T(8,128)(2,1)} %feat.1), channel_id=1, source_target_pairs={{0,27},{1,26},{2,25},{3,24},{4,31},{5,30},{6,29},{7,28},{8,19},{9,... | collective-permute-start | bytes 98312 | tf_op jit(solution)/shard_map/ppermute | solution.py:237
  18.4 3.1 %collective-permute-start.26 = (bf16[32,512]{1,0:T(8,128)(2,1)}, bf16[32,512]{1,0:T(8,128)(2,1)S(1)}, u32[]{:S(2)}, u32[]{:S(2)}) collective-permute-start(bf16[32,512]{1,0:T(8,128)(2,1)} %feat.1), channel_id=1, source_target_pairs={{0,29},{1,28},{2,31},{3,30},{4,25},{5,24},{6,27},{7,26},{8,21},{9,... | collective-permute-start | bytes 98312 | tf_op jit(solution)/shard_map/ppermute | solution.py:237
  21.5 1.8 %collective-permute-start.28 = (bf16[32,512]{1,0:T(8,128)(2,1)}, bf16[32,512]{1,0:T(8,128)(2,1)S(1)}, u32[]{:S(2)}, u32[]{:S(2)}) collective-permute-start(bf16[32,512]{1,0:T(8,128)(2,1)} %feat.1), channel_id=1, source_target_pairs={{0,31},{1,30},{2,29},{3,28},{4,27},{5,26},{6,25},{7,24},{8,23},{9,... | collective-permute-start | bytes 98312 | tf_op jit(solution)/shard_map/ppermute | solution.py:237
  23.3 2.5 %collective-permute-start.4 = (bf16[32,512]{1,0:T(8,128)(2,1)}, bf16[32,512]{1,0:T(8,128)(2,1)S(1)}, u32[]{:S(2)}, u32[]{:S(2)}) collective-permute-start(bf16[32,512]{1,0:T(8,128)(2,1)} %feat.1), channel_id=1, source_target_pairs={{0,7},{1,6},{2,5},{3,4},{4,3},{5,2},{6,1},{7,0},{8,15},{9,14},{10,... | collective-permute-start | bytes 98312 | tf_op jit(solution)/shard_map/ppermute | solution.py:237
  25.9 1.4 %collective-permute-start.6 = (bf16[32,512]{1,0:T(8,128)(2,1)}, bf16[32,512]{1,0:T(8,128)(2,1)S(1)}, u32[]{:S(2)}, u32[]{:S(2)}) collective-permute-start(bf16[32,512]{1,0:T(8,128)(2,1)} %feat.1), channel_id=1, source_target_pairs={{0,9},{1,8},{2,11},{3,10},{4,13},{5,12},{6,15},{7,14},{8,1},{9,0},... | collective-permute-start | bytes 98312 | tf_op jit(solution)/shard_map/ppermute | solution.py:237
  28.6 2.2 %copy-done.6 = bf16[4096,512]{1,0:T(8,128)(2,1)S(1)} copy-done((bf16[4096,512]{1,0:T(8,128)(2,1)S(1)}, bf16[4096,512]{1,0:T(8,128)(2,1)}, u32[]{:S(2)}) %copy-start.6) | copy-done | bytes 4194328
  30.8 1.6 %copy-done.7 = bf16[4,512,512]{2,1,0:T(8,128)(2,1)S(1)} copy-done((bf16[4,512,512]{2,1,0:T(8,128)(2,1)S(1)}, bf16[4,512,512]{2,1,0:T(8,128)(2,1)}, u32[]{:S(2)}) %copy-start.7) | copy-done | bytes 2097176
  32.4 1.6 %copy-done.8 = bf16[4,512,512]{2,1,0:T(8,128)(2,1)S(1)} copy-done((bf16[4,512,512]{2,1,0:T(8,128)(2,1)S(1)}, bf16[4,512,512]{2,1,0:T(8,128)(2,1)}, u32[]{:S(2)}) %copy-start.8) | copy-done | bytes 2097176
  36.8 21.3 %project_slots.1 = (bf16[16,128,1024]{2,1,0:T(8,128)(2,1)S(1)}, bf16[16,128,1024]{2,1,0:T(8,128)(2,1)S(1)}) custom-call(s32[1]{0:T(128)} %bitcast.1.me_ref, s32[32,128]{1,0:T(8,128)S(1)} %copy-done.11, s32[32]{0:T(128)S(1)} %copy-done.3, bf16[4096,512]{1,0:T(8,128)(2,1)S(1)} %copy-done.6, bf16[4,512,512]{2,1,0:T(8,128)(2,1)S(1)} %copy-done.7, ...), custom_call_target="tpu_custom_call" | custom-call | flops 6442450944 | bytes 20971520 | tf_op jit(solution)/shard_map/project_slots/pallas_call | solution.py:121
  58.2 4.1 %aggregate_odd.1 = bf16[16,32,512]{2,1,0:T(8,128)(2,1)S(1)} custom-call(s32[1]{0:T(128)} %bitcast.1.me_ref, s32[32]{0:T(128)S(1)} %copy-done.3, s32[32]{0:T(128)S(1)} %copy-done.4, f32[4]{0:T(128)S(1)} %copy-done.5, s32[32,128]{1,0:T(8,128)S(1)} %copy-done.1, bf16[16,128,1024]{2,1,0:T(8,128)(2,1)S(1)} %get-tuple-element.24.pairs, ...), custom_call_target="tpu_custom_call" | custom-call | flops 134217728 | bytes 5242880 | tf_op jit(solution)/shard_map/aggregate_odd/pallas_call | solution.py:185
  68.4 4.0 %aggregate_even.1 = (bf16[32,512]{1,0:T(8,128)(2,1)S(1)}, bf16[32,512]{1,0:T(8,128)(2,1)S(1)}, bf16[32,512]{1,0:T(8,128)(2,1)S(1)}, bf16[32,512]{1,0:T(8,128)(2,...) custom-call(s32[1]{0:T(128)} %bitcast.1.me_ref, ...), custom_call_target="tpu_custom_call" | custom-call | flops 134217728 | bytes 5242880 | tf_op jit(solution)/shard_map/aggregate_even/pallas_call | solution.py:185
  72.5 1.5 %collective-permute-start.32 = (bf16[32,512]{1,0:T(8,128)(2,1)S(1)}, bf16[32,512]{1,0:T(8,128)(2,1)S(1)}, u32[]{:S(2)}, u32[]{:S(2)}) collective-permute-start(bf16[32,512]{1,0:T(8,128)(2,1)S(1)} %get-tuple-element.26), channel_id=1, source_target_pairs={{0,2},{1,3},{2,0},{3,1},{4,6},{5,7},{6,4},{7,5},{8,10},{9,11},{10,... | collective-permute-start | bytes 98312 | tf_op jit(solution)/shard_map/ppermute | solution.py:237
  74.6 1.5 %collective-permute-start.34 = (bf16[32,512]{1,0:T(8,128)(2,1)S(1)}, bf16[32,512]{1,0:T(8,128)(2,1)S(1)}, u32[]{:S(2)}, u32[]{:S(2)}) collective-permute-start(bf16[32,512]{1,0:T(8,128)(2,1)S(1)} %get-tuple-element.28), channel_id=1, source_target_pairs={{0,6},{1,7},{2,4},{3,5},{4,2},{5,3},{6,0},{7,1},{8,14},{9,15},{10,... | collective-permute-start | bytes 98312 | tf_op jit(solution)/shard_map/ppermute | solution.py:237
  76.0 1.5 %collective-permute-start.35 = (bf16[32,512]{1,0:T(8,128)(2,1)S(1)}, bf16[32,512]{1,0:T(8,128)(2,1)S(1)}, u32[]{:S(2)}, u32[]{:S(2)}) collective-permute-start(bf16[32,512]{1,0:T(8,128)(2,1)S(1)} %get-tuple-element.29), channel_id=1, source_target_pairs={{0,8},{1,9},{2,10},{3,11},{4,12},{5,13},{6,14},{7,15},{8,0},{9,1},... | collective-permute-start | bytes 98312 | tf_op jit(solution)/shard_map/ppermute | solution.py:237
  77.5 1.5 %collective-permute-start.36 = (bf16[32,512]{1,0:T(8,128)(2,1)S(1)}, bf16[32,512]{1,0:T(8,128)(2,1)S(1)}, u32[]{:S(2)}, u32[]{:S(2)}) collective-permute-start(bf16[32,512]{1,0:T(8,128)(2,1)S(1)} %get-tuple-element.30), channel_id=1, source_target_pairs={{0,10},{1,11},{2,8},{3,9},{4,14},{5,15},{6,12},{7,13},{8,2},{9,3},... | collective-permute-start | bytes 98312 | tf_op jit(solution)/shard_map/ppermute | solution.py:237
  79.0 1.5 %collective-permute-start.37 = (bf16[32,512]{1,0:T(8,128)(2,1)S(1)}, bf16[32,512]{1,0:T(8,128)(2,1)S(1)}, u32[]{:S(2)}, u32[]{:S(2)}) collective-permute-start(bf16[32,512]{1,0:T(8,128)(2,1)S(1)} %get-tuple-element.31), channel_id=1, source_target_pairs={{0,12},{1,13},{2,14},{3,15},{4,8},{5,9},{6,10},{7,11},{8,4},{9,5},... | collective-permute-start | bytes 98312 | tf_op jit(solution)/shard_map/ppermute | solution.py:237
  80.4 1.5 %collective-permute-start.38 = (bf16[32,512]{1,0:T(8,128)(2,1)S(1)}, bf16[32,512]{1,0:T(8,128)(2,1)S(1)}, u32[]{:S(2)}, u32[]{:S(2)}) collective-permute-start(bf16[32,512]{1,0:T(8,128)(2,1)S(1)} %get-tuple-element.32), channel_id=1, source_target_pairs={{0,14},{1,15},{2,12},{3,13},{4,10},{5,11},{6,8},{7,9},{8,6},{9,7},... | collective-permute-start | bytes 98312 | tf_op jit(solution)/shard_map/ppermute | solution.py:237
  81.9 2.4 %collective-permute-start.39 = (bf16[32,512]{1,0:T(8,128)(2,1)S(1)}, bf16[32,512]{1,0:T(8,128)(2,1)S(1)}, u32[]{:S(2)}, u32[]{:S(2)}) collective-permute-start(bf16[32,512]{1,0:T(8,128)(2,1)S(1)} %get-tuple-element.33), channel_id=1, source_target_pairs={{0,16},{1,17},{2,18},{3,19},{4,20},{5,21},{6,22},{7,23},{8,24},{9,... | collective-permute-start | bytes 98312 | tf_op jit(solution)/shard_map/ppermute | solution.py:237
  84.3 1.4 %collective-permute-start.40 = (bf16[32,512]{1,0:T(8,128)(2,1)S(1)}, bf16[32,512]{1,0:T(8,128)(2,1)S(1)}, u32[]{:S(2)}, u32[]{:S(2)}) collective-permute-start(bf16[32,512]{1,0:T(8,128)(2,1)S(1)} %get-tuple-element.34), channel_id=1, source_target_pairs={{0,18},{1,19},{2,16},{3,17},{4,22},{5,23},{6,20},{7,21},{8,26},{9,... | collective-permute-start | bytes 98312 | tf_op jit(solution)/shard_map/ppermute | solution.py:237
  85.7 2.4 %collective-permute-start.41 = (bf16[32,512]{1,0:T(8,128)(2,1)S(1)}, bf16[32,512]{1,0:T(8,128)(2,1)S(1)}, u32[]{:S(2)}, u32[]{:S(2)}) collective-permute-start(bf16[32,512]{1,0:T(8,128)(2,1)S(1)} %get-tuple-element.35), channel_id=1, source_target_pairs={{0,20},{1,21},{2,22},{3,23},{4,16},{5,17},{6,18},{7,19},{8,28},{9,... | collective-permute-start | bytes 98312 | tf_op jit(solution)/shard_map/ppermute | solution.py:237
  88.1 1.5 %collective-permute-start.42 = (bf16[32,512]{1,0:T(8,128)(2,1)S(1)}, bf16[32,512]{1,0:T(8,128)(2,1)S(1)}, u32[]{:S(2)}, u32[]{:S(2)}) collective-permute-start(bf16[32,512]{1,0:T(8,128)(2,1)S(1)} %get-tuple-element.36), channel_id=1, source_target_pairs={{0,22},{1,23},{2,20},{3,21},{4,18},{5,19},{6,16},{7,17},{8,30},{9,... | collective-permute-start | bytes 98312 | tf_op jit(solution)/shard_map/ppermute | solution.py:237
  89.6 3.4 %collective-permute-start.43 = (bf16[32,512]{1,0:T(8,128)(2,1)S(1)}, bf16[32,512]{1,0:T(8,128)(2,1)S(1)}, u32[]{:S(2)}, u32[]{:S(2)}) collective-permute-start(bf16[32,512]{1,0:T(8,128)(2,1)S(1)} %get-tuple-element.37), channel_id=1, source_target_pairs={{0,24},{1,25},{2,26},{3,27},{4,28},{5,29},{6,30},{7,31},{8,16},{9,... | collective-permute-start | bytes 98312 | tf_op jit(solution)/shard_map/ppermute | solution.py:237
  94.3 3.3 %collective-permute-start.45 = (bf16[32,512]{1,0:T(8,128)(2,1)S(1)}, bf16[32,512]{1,0:T(8,128)(2,1)S(1)}, u32[]{:S(2)}, u32[]{:S(2)}) collective-permute-start(bf16[32,512]{1,0:T(8,128)(2,1)S(1)} %get-tuple-element.39), channel_id=1, source_target_pairs={{0,28},{1,29},{2,30},{3,31},{4,24},{5,25},{6,26},{7,27},{8,20},{9,... | collective-permute-start | bytes 98312 | tf_op jit(solution)/shard_map/ppermute | solution.py:237
  97.6 1.6 %collective-permute-start.46 = (bf16[32,512]{1,0:T(8,128)(2,1)S(1)}, bf16[32,512]{1,0:T(8,128)(2,1)S(1)}, u32[]{:S(2)}, u32[]{:S(2)}) collective-permute-start(bf16[32,512]{1,0:T(8,128)(2,1)S(1)} %get-tuple-element.40), channel_id=1, source_target_pairs={{0,30},{1,31},{2,28},{3,29},{4,26},{5,27},{6,24},{7,25},{8,22},{9,... | collective-permute-start | bytes 98312 | tf_op jit(solution)/shard_map/ppermute | solution.py:237
  100.9 5.8 %collective-permute-done.46.refs_15_ = bf16[32,512]{1,0:T(8,128)(2,1)S(1)} collective-permute-done((bf16[32,512]{1,0:T(8,128)(2,1)S(1)}, bf16[32,512]{1,0:T(8,128)(2,1)S(1)}, u32[]{:S(2)}, u32[]{:S(2)}) %collective-permute-start.46) | collective-permute-done | bytes 32800 | tf_op jit(solution)/shard_map/ppermute | solution.py:237
  107.4 1.8 %finish.1 = bf16[32,512]{1,0:T(8,128)(2,1)} custom-call(bf16[32,512]{1,0:T(8,128)(2,1)} %feat.1, f32[1,512]{1,0:T(1,128)} %bitcast.2, bf16[32,512]{1,0:T(8,128)(2,1)} %copy-done.2, bf16[32,512]{1,0:T(8,128)(2,1)} %copy-done.12, bf16[32,512]{1,0:T(8,128)(2,1)} %copy-done.13, bf16[32,512]{1,0:T(8,128)(2,1)} %copy-done.14, bf16[32,512]{1,0:T(8,128)(2,1)} %copy-done.15, ...), custom_call_target="tpu_custom_call" | custom-call | tf_op jit(solution)/shard_map/finish/pallas_call | solution.py:210
  (120 shorter events, 15.5 us)
Async XLA Ops:
  0.0 8.8 %collective-permute-start = (bf16[32,512]{1,0:T(8,128)(2,1)}, bf16[32,512]{1,0:T(8,128)(2,1)S(1)}, u32[]{:S(2)}, u32[]{:S(2)}) collective-permute-start(bf16[32,512]{1,0:T(8,128)(2,1)} %feat.1), channel_id=1, source_target_pairs={{0,3},{1,2},{2,1},{3,0},{4,7},{5,6},{6,5},{7,4},{8,11},{9,10},{10,... | collective-permute-start | bytes 98312 | tf_op jit(solution)/shard_map/ppermute | solution.py:237
  2.4 10.0 %collective-permute-start.10 = (bf16[32,512]{1,0:T(8,128)(2,1)}, bf16[32,512]{1,0:T(8,128)(2,1)S(1)}, u32[]{:S(2)}, u32[]{:S(2)}) collective-permute-start(bf16[32,512]{1,0:T(8,128)(2,1)} %feat.1), channel_id=1, source_target_pairs={{0,13},{1,12},{2,15},{3,14},{4,9},{5,8},{6,11},{7,10},{8,5},{9,4},... | collective-permute-start | bytes 98312 | tf_op jit(solution)/shard_map/ppermute | solution.py:237
  5.2 7.3 %collective-permute-start.12 = (bf16[32,512]{1,0:T(8,128)(2,1)}, bf16[32,512]{1,0:T(8,128)(2,1)S(1)}, u32[]{:S(2)}, u32[]{:S(2)}) collective-permute-start(bf16[32,512]{1,0:T(8,128)(2,1)} %feat.1), channel_id=1, source_target_pairs={{0,15},{1,14},{2,13},{3,12},{4,11},{5,10},{6,9},{7,8},{8,7},{9,6},... | collective-permute-start | bytes 98312 | tf_op jit(solution)/shard_map/ppermute | solution.py:237
  5.2 8.7 %collective-permute-start.14 = (bf16[32,512]{1,0:T(8,128)(2,1)}, bf16[32,512]{1,0:T(8,128)(2,1)S(1)}, u32[]{:S(2)}, u32[]{:S(2)}) collective-permute-start(bf16[32,512]{1,0:T(8,128)(2,1)} %feat.1), channel_id=1, source_target_pairs={{0,17},{1,16},{2,19},{3,18},{4,21},{5,20},{6,23},{7,22},{8,25},{9,... | collective-permute-start | bytes 98312 | tf_op jit(solution)/shard_map/ppermute | solution.py:237
  7.9 9.1 %collective-permute-start.16 = (bf16[32,512]{1,0:T(8,128)(2,1)}, bf16[32,512]{1,0:T(8,128)(2,1)S(1)}, u32[]{:S(2)}, u32[]{:S(2)}) collective-permute-start(bf16[32,512]{1,0:T(8,128)(2,1)} %feat.1), channel_id=1, source_target_pairs={{0,19},{1,18},{2,17},{3,16},{4,23},{5,22},{6,21},{7,20},{8,27},{9,... | collective-permute-start | bytes 98312 | tf_op jit(solution)/shard_map/ppermute | solution.py:237
  8.8 9.6 %collective-permute-start.18 = (bf16[32,512]{1,0:T(8,128)(2,1)}, bf16[32,512]{1,0:T(8,128)(2,1)S(1)}, u32[]{:S(2)}, u32[]{:S(2)}) collective-permute-start(bf16[32,512]{1,0:T(8,128)(2,1)} %feat.1), channel_id=1, source_target_pairs={{0,21},{1,20},{2,23},{3,22},{4,17},{5,16},{6,19},{7,18},{8,29},{9,... | collective-permute-start | bytes 98312 | tf_op jit(solution)/shard_map/ppermute | solution.py:237
  12.4 9.1 %collective-permute-start.2 = (bf16[32,512]{1,0:T(8,128)(2,1)}, bf16[32,512]{1,0:T(8,128)(2,1)S(1)}, u32[]{:S(2)}, u32[]{:S(2)}) collective-permute-start(bf16[32,512]{1,0:T(8,128)(2,1)} %feat.1), channel_id=1, source_target_pairs={{0,5},{1,4},{2,7},{3,6},{4,1},{5,0},{6,3},{7,2},{8,13},{9,12},{10,... | collective-permute-start | bytes 98312 | tf_op jit(solution)/shard_map/ppermute | solution.py:237
  12.5 10.8 %collective-permute-start.20 = (bf16[32,512]{1,0:T(8,128)(2,1)}, bf16[32,512]{1,0:T(8,128)(2,1)S(1)}, u32[]{:S(2)}, u32[]{:S(2)}) collective-permute-start(bf16[32,512]{1,0:T(8,128)(2,1)} %feat.1), channel_id=1, source_target_pairs={{0,23},{1,22},{2,21},{3,20},{4,19},{5,18},{6,17},{7,16},{8,31},{9,... | collective-permute-start | bytes 98312 | tf_op jit(solution)/shard_map/ppermute | solution.py:237
  13.9 11.9 %collective-permute-start.22 = (bf16[32,512]{1,0:T(8,128)(2,1)}, bf16[32,512]{1,0:T(8,128)(2,1)S(1)}, u32[]{:S(2)}, u32[]{:S(2)}) collective-permute-start(bf16[32,512]{1,0:T(8,128)(2,1)} %feat.1), channel_id=1, source_target_pairs={{0,25},{1,24},{2,27},{3,26},{4,29},{5,28},{6,31},{7,30},{8,17},{9,... | collective-permute-start | bytes 98312 | tf_op jit(solution)/shard_map/ppermute | solution.py:237
  17.0 10.3 %collective-permute-start.24 = (bf16[32,512]{1,0:T(8,128)(2,1)}, bf16[32,512]{1,0:T(8,128)(2,1)S(1)}, u32[]{:S(2)}, u32[]{:S(2)}) collective-permute-start(bf16[32,512]{1,0:T(8,128)(2,1)} %feat.1), channel_id=1, source_target_pairs={{0,27},{1,26},{2,25},{3,24},{4,31},{5,30},{6,29},{7,28},{8,19},{9,... | collective-permute-start | bytes 98312 | tf_op jit(solution)/shard_map/ppermute | solution.py:237
  18.4 9.2 %collective-permute-start.26 = (bf16[32,512]{1,0:T(8,128)(2,1)}, bf16[32,512]{1,0:T(8,128)(2,1)S(1)}, u32[]{:S(2)}, u32[]{:S(2)}) collective-permute-start(bf16[32,512]{1,0:T(8,128)(2,1)} %feat.1), channel_id=1, source_target_pairs={{0,29},{1,28},{2,31},{3,30},{4,25},{5,24},{6,27},{7,26},{8,21},{9,... | collective-permute-start | bytes 98312 | tf_op jit(solution)/shard_map/ppermute | solution.py:237
  21.5 36.6 %collective-permute-start.28 = (bf16[32,512]{1,0:T(8,128)(2,1)}, bf16[32,512]{1,0:T(8,128)(2,1)S(1)}, u32[]{:S(2)}, u32[]{:S(2)}) collective-permute-start(bf16[32,512]{1,0:T(8,128)(2,1)} %feat.1), channel_id=1, source_target_pairs={{0,31},{1,30},{2,29},{3,28},{4,27},{5,26},{6,25},{7,24},{8,23},{9,... | collective-permute-start | bytes 98312 | tf_op jit(solution)/shard_map/ppermute | solution.py:237
  23.3 34.8 %collective-permute-start.4 = (bf16[32,512]{1,0:T(8,128)(2,1)}, bf16[32,512]{1,0:T(8,128)(2,1)S(1)}, u32[]{:S(2)}, u32[]{:S(2)}) collective-permute-start(bf16[32,512]{1,0:T(8,128)(2,1)} %feat.1), channel_id=1, source_target_pairs={{0,7},{1,6},{2,5},{3,4},{4,3},{5,2},{6,1},{7,0},{8,15},{9,14},{10,... | collective-permute-start | bytes 98312 | tf_op jit(solution)/shard_map/ppermute | solution.py:237
  25.9 32.3 %collective-permute-start.6 = (bf16[32,512]{1,0:T(8,128)(2,1)}, bf16[32,512]{1,0:T(8,128)(2,1)S(1)}, u32[]{:S(2)}, u32[]{:S(2)}) collective-permute-start(bf16[32,512]{1,0:T(8,128)(2,1)} %feat.1), channel_id=1, source_target_pairs={{0,9},{1,8},{2,11},{3,10},{4,13},{5,12},{6,15},{7,14},{8,1},{9,0},... | collective-permute-start | bytes 98312 | tf_op jit(solution)/shard_map/ppermute | solution.py:237
  27.3 30.8 %collective-permute-start.8 = (bf16[32,512]{1,0:T(8,128)(2,1)}, bf16[32,512]{1,0:T(8,128)(2,1)S(1)}, u32[]{:S(2)}, u32[]{:S(2)}) collective-permute-start(bf16[32,512]{1,0:T(8,128)(2,1)} %feat.1), channel_id=1, source_target_pairs={{0,11},{1,10},{2,9},{3,8},{4,15},{5,14},{6,13},{7,12},{8,3},{9,2},... | collective-permute-start | bytes 98312 | tf_op jit(solution)/shard_map/ppermute | solution.py:237
  27.6 30.5 %collective-permute-start.30 = (bf16[32,512]{1,0:T(8,128)(2,1)}, bf16[32,512]{1,0:T(8,128)(2,1)S(1)}, u32[]{:S(2)}, u32[]{:S(2)}) collective-permute-start(bf16[32,512]{1,0:T(8,128)(2,1)} %feat.1), channel_id=1, source_target_pairs={{0,1},{1,0},{2,3},{3,2},{4,5},{5,4},{6,7},{7,6},{8,9},{9,8},{10,11... | collective-permute-start | bytes 98312 | tf_op jit(solution)/shard_map/ppermute | solution.py:237
  62.2 6.2 %collective-permute-start.31 = (bf16[16,32,512]{2,1,0:T(8,128)(2,1)S(1)}, bf16[16,32,512]{2,1,0:T(8,128)(2,1)S(1)}, u32[]{:S(2)}, u32[]{:S(2)}) collective-permute-start(bf16[16,32,512]{2,1,0:T(8,128)(2,1)S(1)} %aggregate_odd.1), channel_id=1, source_target_pairs={{0,1},{1,0},{2,3},{3,2},{4,5},{5,4},{6,7},{7,6},{8,9},{9,8},{10,11... | collective-permute-start | bytes 1572872 | tf_op jit(solution)/shard_map/ppermute | solution.py:237
  72.5 6.5 %collective-permute-start.32 = (bf16[32,512]{1,0:T(8,128)(2,1)S(1)}, bf16[32,512]{1,0:T(8,128)(2,1)S(1)}, u32[]{:S(2)}, u32[]{:S(2)}) collective-permute-start(bf16[32,512]{1,0:T(8,128)(2,1)S(1)} %get-tuple-element.26), channel_id=1, source_target_pairs={{0,2},{1,3},{2,0},{3,1},{4,6},{5,7},{6,4},{7,5},{8,10},{9,11},{10,... | collective-permute-start | bytes 98312 | tf_op jit(solution)/shard_map/ppermute | solution.py:237
  74.0 6.4 %collective-permute-start.33 = (bf16[32,512]{1,0:T(8,128)(2,1)S(1)}, bf16[32,512]{1,0:T(8,128)(2,1)S(1)}, u32[]{:S(2)}, u32[]{:S(2)}) collective-permute-start(bf16[32,512]{1,0:T(8,128)(2,1)S(1)} %get-tuple-element.27), channel_id=1, source_target_pairs={{0,4},{1,5},{2,6},{3,7},{4,0},{5,1},{6,2},{7,3},{8,12},{9,13},{10,... | collective-permute-start | bytes 98312 | tf_op jit(solution)/shard_map/ppermute | solution.py:237
  74.6 7.3 %collective-permute-start.34 = (bf16[32,512]{1,0:T(8,128)(2,1)S(1)}, bf16[32,512]{1,0:T(8,128)(2,1)S(1)}, u32[]{:S(2)}, u32[]{:S(2)}) collective-permute-start(bf16[32,512]{1,0:T(8,128)(2,1)S(1)} %get-tuple-element.28), channel_id=1, source_target_pairs={{0,6},{1,7},{2,4},{3,5},{4,2},{5,3},{6,0},{7,1},{8,14},{9,15},{10,... | collective-permute-start | bytes 98312 | tf_op jit(solution)/shard_map/ppermute | solution.py:237
  76.0 8.3 %collective-permute-start.35 = (bf16[32,512]{1,0:T(8,128)(2,1)S(1)}, bf16[32,512]{1,0:T(8,128)(2,1)S(1)}, u32[]{:S(2)}, u32[]{:S(2)}) collective-permute-start(bf16[32,512]{1,0:T(8,128)(2,1)S(1)} %get-tuple-element.29), channel_id=1, source_target_pairs={{0,8},{1,9},{2,10},{3,11},{4,12},{5,13},{6,14},{7,15},{8,0},{9,1},... | collective-permute-start | bytes 98312 | tf_op jit(solution)/shard_map/ppermute | solution.py:237
  77.5 8.3 %collective-permute-start.36 = (bf16[32,512]{1,0:T(8,128)(2,1)S(1)}, bf16[32,512]{1,0:T(8,128)(2,1)S(1)}, u32[]{:S(2)}, u32[]{:S(2)}) collective-permute-start(bf16[32,512]{1,0:T(8,128)(2,1)S(1)} %get-tuple-element.30), channel_id=1, source_target_pairs={{0,10},{1,11},{2,8},{3,9},{4,14},{5,15},{6,12},{7,13},{8,2},{9,3},... | collective-permute-start | bytes 98312 | tf_op jit(solution)/shard_map/ppermute | solution.py:237
  79.0 9.1 %collective-permute-start.37 = (bf16[32,512]{1,0:T(8,128)(2,1)S(1)}, bf16[32,512]{1,0:T(8,128)(2,1)S(1)}, u32[]{:S(2)}, u32[]{:S(2)}) collective-permute-start(bf16[32,512]{1,0:T(8,128)(2,1)S(1)} %get-tuple-element.31), channel_id=1, source_target_pairs={{0,12},{1,13},{2,14},{3,15},{4,8},{5,9},{6,10},{7,11},{8,4},{9,5},... | collective-permute-start | bytes 98312 | tf_op jit(solution)/shard_map/ppermute | solution.py:237
  80.4 9.1 %collective-permute-start.38 = (bf16[32,512]{1,0:T(8,128)(2,1)S(1)}, bf16[32,512]{1,0:T(8,128)(2,1)S(1)}, u32[]{:S(2)}, u32[]{:S(2)}) collective-permute-start(bf16[32,512]{1,0:T(8,128)(2,1)S(1)} %get-tuple-element.32), channel_id=1, source_target_pairs={{0,14},{1,15},{2,12},{3,13},{4,10},{5,11},{6,8},{7,9},{8,6},{9,7},... | collective-permute-start | bytes 98312 | tf_op jit(solution)/shard_map/ppermute | solution.py:237
  81.9 11.0 %collective-permute-start.39 = (bf16[32,512]{1,0:T(8,128)(2,1)S(1)}, bf16[32,512]{1,0:T(8,128)(2,1)S(1)}, u32[]{:S(2)}, u32[]{:S(2)}) collective-permute-start(bf16[32,512]{1,0:T(8,128)(2,1)S(1)} %get-tuple-element.33), channel_id=1, source_target_pairs={{0,16},{1,17},{2,18},{3,19},{4,20},{5,21},{6,22},{7,23},{8,24},{9,... | collective-permute-start | bytes 98312 | tf_op jit(solution)/shard_map/ppermute | solution.py:237
  84.3 10.0 %collective-permute-start.40 = (bf16[32,512]{1,0:T(8,128)(2,1)S(1)}, bf16[32,512]{1,0:T(8,128)(2,1)S(1)}, u32[]{:S(2)}, u32[]{:S(2)}) collective-permute-start(bf16[32,512]{1,0:T(8,128)(2,1)S(1)} %get-tuple-element.34), channel_id=1, source_target_pairs={{0,18},{1,19},{2,16},{3,17},{4,22},{5,23},{6,20},{7,21},{8,26},{9,... | collective-permute-start | bytes 98312 | tf_op jit(solution)/shard_map/ppermute | solution.py:237
  85.7 11.9 %collective-permute-start.41 = (bf16[32,512]{1,0:T(8,128)(2,1)S(1)}, bf16[32,512]{1,0:T(8,128)(2,1)S(1)}, u32[]{:S(2)}, u32[]{:S(2)}) collective-permute-start(bf16[32,512]{1,0:T(8,128)(2,1)S(1)} %get-tuple-element.35), channel_id=1, source_target_pairs={{0,20},{1,21},{2,22},{3,23},{4,16},{5,17},{6,18},{7,19},{8,28},{9,... | collective-permute-start | bytes 98312 | tf_op jit(solution)/shard_map/ppermute | solution.py:237
  88.1 11.2 %collective-permute-start.42 = (bf16[32,512]{1,0:T(8,128)(2,1)S(1)}, bf16[32,512]{1,0:T(8,128)(2,1)S(1)}, u32[]{:S(2)}, u32[]{:S(2)}) collective-permute-start(bf16[32,512]{1,0:T(8,128)(2,1)S(1)} %get-tuple-element.36), channel_id=1, source_target_pairs={{0,22},{1,23},{2,20},{3,21},{4,18},{5,19},{6,16},{7,17},{8,30},{9,... | collective-permute-start | bytes 98312 | tf_op jit(solution)/shard_map/ppermute | solution.py:237
  89.6 9.7 %collective-permute-start.43 = (bf16[32,512]{1,0:T(8,128)(2,1)S(1)}, bf16[32,512]{1,0:T(8,128)(2,1)S(1)}, u32[]{:S(2)}, u32[]{:S(2)}) collective-permute-start(bf16[32,512]{1,0:T(8,128)(2,1)S(1)} %get-tuple-element.37), channel_id=1, source_target_pairs={{0,24},{1,25},{2,26},{3,27},{4,28},{5,29},{6,30},{7,31},{8,16},{9,... | collective-permute-start | bytes 98312 | tf_op jit(solution)/shard_map/ppermute | solution.py:237
  92.9 6.6 %collective-permute-start.44 = (bf16[32,512]{1,0:T(8,128)(2,1)S(1)}, bf16[32,512]{1,0:T(8,128)(2,1)S(1)}, u32[]{:S(2)}, u32[]{:S(2)}) collective-permute-start(bf16[32,512]{1,0:T(8,128)(2,1)S(1)} %get-tuple-element.38), channel_id=1, source_target_pairs={{0,26},{1,27},{2,24},{3,25},{4,30},{5,31},{6,28},{7,29},{8,18},{9,... | collective-permute-start | bytes 98312 | tf_op jit(solution)/shard_map/ppermute | solution.py:237
  94.3 6.6 %collective-permute-start.45 = (bf16[32,512]{1,0:T(8,128)(2,1)S(1)}, bf16[32,512]{1,0:T(8,128)(2,1)S(1)}, u32[]{:S(2)}, u32[]{:S(2)}) collective-permute-start(bf16[32,512]{1,0:T(8,128)(2,1)S(1)} %get-tuple-element.39), channel_id=1, source_target_pairs={{0,28},{1,29},{2,30},{3,31},{4,24},{5,25},{6,26},{7,27},{8,20},{9,... | collective-permute-start | bytes 98312 | tf_op jit(solution)/shard_map/ppermute | solution.py:237
  97.6 9.1 %collective-permute-start.46 = (bf16[32,512]{1,0:T(8,128)(2,1)S(1)}, bf16[32,512]{1,0:T(8,128)(2,1)S(1)}, u32[]{:S(2)}, u32[]{:S(2)}) collective-permute-start(bf16[32,512]{1,0:T(8,128)(2,1)S(1)} %get-tuple-element.40), channel_id=1, source_target_pairs={{0,30},{1,31},{2,28},{3,29},{4,26},{5,27},{6,24},{7,25},{8,22},{9,... | collective-permute-start | bytes 98312 | tf_op jit(solution)/shard_map/ppermute | solution.py:237
  (42 other events, 360.9 us)

commit v2 on v0

v2 whole, which is shorter than its diff:
```python
import functools
import math

import jax
import jax.numpy as jnp
from jax import lax
from jax.experimental import pallas as pl
from jax.experimental.pallas import tpu as pltpu
from jax.sharding import PartitionSpec as P

AXES = ("acct", "merch")
LANES = 128
F32 = jnp.float32
BF16 = jnp.bfloat16
SMEM = pl.BlockSpec(memory_space=pltpu.SMEM)
VMEM = pl.BlockSpec(memory_space=pltpu.VMEM)


def _mb(n):
    return pltpu.CompilerParams(vmem_limit_bytes=n * 2**20)


def _cost(flops, bytes_accessed, transcendentals=0):
    return pl.CostEstimate(
        flops=int(flops), bytes_accessed=int(bytes_accessed), transcendentals=transcendentals
    )


def _offset(i, masks):
    out = 0
    for bit, mask in enumerate(masks):
        out = out + ((i >> bit) & 1) * mask
    return out


def table_kernel(acct, table):
    accounts, width = acct.shape
    parts = width // LANES

    @pl.loop(0, accounts // 16, unroll=4)
    def _(g):
        first = pl.multiple_of(g * 16, 16)
        tile = acct[pl.ds(first, 16), :].astype(F32)
        for c in range(parts):
            table[pl.ds(first * parts + c, 16, stride=parts), :] = tile[
                :, c * LANES : (c + 1) * LANES
            ]


def make_table(acct):
    accounts, width = acct.shape
    return pl.pallas_call(
        table_kernel,
        out_shape=jax.ShapeDtypeStruct((accounts * width // LANES, LANES), F32),
        in_specs=[VMEM],
        out_specs=VMEM,
        compiler_params=_mb(2),
        cost_estimate=_cost(0, 8 * 2**20),
        name="make_table",
    )(acct)


def gather_kernel(masks, shift, me_ref, slots_ref, table, out, rows0, rows1):
    blocks, block_len, width = out.shape
    parts = width // LANES
    me = me_ref[0]

    def collect(i, rows):
        block = jnp.bitwise_xor(me, _offset(i, masks) + shift)
        for k in range(block_len):
            first = pl.multiple_of(slots_ref[block, k] * parts, parts)
            rows[k * parts : (k + 1) * parts, :] = table[pl.ds(first, parts), :]

    def emit(i, rows):
        for c in range(parts):
            out[i, :, c * LANES : (c + 1) * LANES] = rows[
                pl.ds(c, block_len, stride=parts), :
            ].astype(BF16)

    @pl.loop(0, blocks // 2)
    def _(h):
        collect(2 * h, rows0)
        collect(2 * h + 1, rows1)
        emit(2 * h, rows0)
        emit(2 * h + 1, rows1)


def gather(masks, shift, me, slots, table, width):
    blocks, block_len = slots.shape
    rows = pltpu.VMEM((block_len * width // LANES, LANES), F32)
    return pl.pallas_call(
        functools.partial(gather_kernel, masks, shift),
        out_shape=jax.ShapeDtypeStruct((blocks // 2, block_len, width), BF16),
        in_specs=[SMEM, SMEM, VMEM],
        out_specs=VMEM,
        scratch_shapes=[rows, rows],
        compiler_params=_mb(2),
        cost_estimate=_cost(0, 8 * 2**20),
        name="gather_odd" if shift else "gather_even",
    )(me, slots, table)


def project_kernel(masks, shift, me_ref, rel_ref, feats, kw, mw, keys, values):
    blocks = feats.shape[0]
    width = feats.shape[2]
    half = width // 2
    me = me_ref[0]

    @pl.loop(0, blocks)
    def _(i):
        relation = rel_ref[jnp.bitwise_xor(me, _offset(i, masks) + shift)]
        for n in range(0, width, half):
            key = jnp.dot(feats[i], kw[relation, :, n : n + half], preferred_element_type=F32)
            keys[i, n : n + half, :] = key.T.astype(BF16)
            value = jnp.dot(feats[i], mw[relation, :, n : n + half], preferred_element_type=F32)
            values[i, :, n : n + half] = value.astype(BF16)


def project(masks, shift, me, rel, feats, kw, mw):
    blocks, block_len, width = feats.shape
    return pl.pallas_call(
        functools.partial(project_kernel, masks, shift),
        out_shape=(
            jax.ShapeDtypeStruct((blocks, width, block_len), BF16),
            jax.ShapeDtypeStruct((blocks, block_len, width), BF16),
        ),
        in_specs=[SMEM, SMEM, VMEM, VMEM, VMEM],
        out_specs=(VMEM, VMEM),
        compiler_params=_mb(4),
        cost_estimate=_cost(4 * blocks * block_len * width * width, 12 * 2**20),
        name="project_odd" if shift else "project_even",
    )(me, rel, feats, kw, mw)


def aggregate_kernel(
    masks, shift, me_ref, rel_ref, count_ref, bias_ref, merch_slot, feats, wq, keys, values,
    sums, query, gates,
):
    blocks, width, block_len = keys.shape
    merchants = feats.shape[0] // blocks
    me = me_ref[0]
    row = lax.broadcasted_iota(jnp.int32, (merchants, block_len), 0)
    lane = lax.broadcasted_iota(jnp.int32, (merchants, block_len), 1)
    query[...] = jnp.dot(feats[...], wq[...], preferred_element_type=F32).astype(BF16)
    for i in range(blocks):
        block = jnp.bitwise_xor(me, _offset(i, masks) + shift)
        score = jnp.dot(
            query[i * merchants : (i + 1) * merchants, :], keys[i], preferred_element_type=F32
        ) / math.sqrt(width)
        score = score + bias_ref[rel_ref[block]]
        mine = (merch_slot[pl.ds(block, 1), :] == row) & (lane < count_ref[block])
        gates[i * merchants : (i + 1) * merchants, :] = jnp.where(
            mine, jax.nn.sigmoid(score), 0.0
        ).astype(BF16)
    for i in range(blocks):
        sums[i * merchants : (i + 1) * merchants, :] = jnp.dot(
            gates[i * merchants : (i + 1) * merchants, :], values[i], preferred_element_type=F32
        ).astype(sums.dtype)


def aggregate(masks, shift, me, rel, count, bias, merch_slot, feats, wq, keys, values, dtype):
    blocks, width, block_len = keys.shape
    merchants = feats.shape[0] // blocks
    return pl.pallas_call(
        functools.partial(aggregate_kernel, masks, shift),
        out_shape=jax.ShapeDtypeStruct(feats.shape, dtype),
        in_specs=[SMEM] * 4 + [VMEM] * 5,
        out_specs=VMEM,
        scratch_shapes=[
            pltpu.VMEM(feats.shape, BF16),
            pltpu.VMEM((feats.shape[0], block_len), BF16),
        ],
        compiler_params=_mb(6),
        cost_estimate=_cost(
            4 * blocks * merchants * block_len * width + 2 * feats.shape[0] * width * width,
            6 * 2**20,
            blocks * merchants * block_len,
        ),
        name="aggregate_odd" if shift else "aggregate_even",
    )(me, rel, count, bias, merch_slot, feats, wq, keys, values)


def combine_kernel(masks, me_ref, mine, other, out):
    rows = out.shape[0]
    blocks = 2 ** len(masks)
    merchants = rows // blocks
    me = me_ref[0]
    for i in range(blocks):
        place = jnp.bitwise_xor(me, _offset(i, masks)) >> 1
        first = pl.multiple_of(place * merchants, merchants)
        part = slice(i * merchants, (i + 1) * merchants)
        out[pl.ds(first, merchants), :] = (mine[part, :] + other[part, :].astype(F32)).astype(BF16)


def combine(masks, me, mine, other):
    return pl.pallas_call(
        functools.partial(combine_kernel, masks),
        out_shape=jax.ShapeDtypeStruct(other.shape, BF16),
        in_specs=[SMEM, VMEM, VMEM],
        out_specs=VMEM,
        compiler_params=_mb(2),
        cost_estimate=_cost(0, 2 * 2**20),
        name="combine",
    )(me, mine, other)


def finish_kernel(feat, gain, wo, parts, out):
    merchants = feat.shape[0]
    total = parts[:merchants, :].astype(F32)
    for i in range(1, parts.shape[0] // merchants):
        total = total + parts[i * merchants : (i + 1) * merchants, :].astype(F32)
    update = feat[...].astype(F32) + jnp.dot(
        total.astype(BF16), wo[...], preferred_element_type=F32
    )
    scale = lax.rsqrt(jnp.mean(update * update, axis=-1, keepdims=True) + 1e-06)
    out[...] = (update * scale * gain[...]).astype(BF16)


def finish(feat, gain, wo, parts):
    return pl.pallas_call(
        finish_kernel,
        out_shape=jax.ShapeDtypeStruct(feat.shape, BF16),
        in_specs=[VMEM] * 4,
        out_specs=VMEM,
        compiler_params=_mb(2),
        name="finish",
    )(feat, gain.reshape(1, -1), wo, parts)


def per_device(
    acct_feat,
    merch_feat,
    key_weight,
    msg_weight,
    query_weight,
    out_weight,
    rel_bias,
    out_gain,
    slot_acct,
    slot_merch,
    block_rel,
    block_count,
):
    devices = lax.axis_size(AXES)
    me = lax.axis_index(AXES).astype(jnp.int32).reshape(1)
    width = acct_feat.shape[1]
    masks = []
    while devices >> (len(masks) + 1) > 1:
        masks.append(devices >> (len(masks) + 1))

    def swap(value, mask):
        return lax.ppermute(value, AXES, [(s, s ^ mask) for s in range(devices)])

    def after(value, *others):
        return lax.optimization_barrier((value,) + others)[0]

    feats = jnp.concatenate([swap(merch_feat, 1), swap(merch_feat, masks[0] + 1)], axis=0)
    table = make_table(acct_feat)
    feats = after(feats, table)
    feats = jnp.concatenate([feats, swap(feats, masks[1])], axis=0)
    odd_rows = gather(masks, 1, me, slot_acct, table, width)
    feats = after(feats, odd_rows)
    feats = jnp.concatenate([feats, swap(feats, masks[2])], axis=0)
    even_rows = gather(masks, 0, me, slot_acct, table, width)
    feats = after(feats, even_rows)
    for mask in masks[3:]:
        feats = jnp.concatenate([feats, swap(feats, mask)], axis=0)
    odd_keys, odd_values = project(masks, 1, me, block_rel, odd_rows, key_weight, msg_weight)
    even_keys, even_values = project(masks, 0, me, block_rel, even_rows, key_weight, msg_weight)
    feats = after(feats, even_keys)

    shared = (me, block_rel, block_count, rel_bias, slot_merch)
    even_feats = swap(feats, 1)
    odd_sums = aggregate(masks, 1, *shared, feats, query_weight, odd_keys, odd_values, BF16)
    other = swap(odd_sums, 1)
    even_sums = aggregate(masks, 0, *shared, even_feats, query_weight, even_keys, even_values, F32)
    parts = combine(masks, me, even_sums, other)
    groups = [[s for s in range(devices) if s % 2 == core] for core in range(2)]
    parts = lax.all_to_all(
        parts, AXES, split_axis=0, concat_axis=0, tiled=True, axis_index_groups=groups
    )
    return finish(merch_feat, out_gain, out_weight, parts)


def solution(mesh):
    placed = (
        P(("acct", "merch"), None),
        P(("acct", "merch"), None),
        P(),
        P(),
        P(),
        P(),
        P(),
        P(),
        P(("acct", "merch"), None),
        P(("acct", "merch"), None),
        P(("acct", "merch")),
        P(("acct", "merch")),
    )
    return jax.shard_map(
        per_device,
        mesh=mesh,
        in_specs=placed,
        out_specs=P(("acct", "merch"), None),
        check_vma=False,
    )
```

time: 310 us -> 62.5 us (0.20)
  local copies, waits for them, and re-layouts: 123 us -> 8.88 us
  blocking collectives: 100 us -> 18.3 us
  matrix products: 36.2 us -> 0 us
  other arithmetic: 27.5 us -> 0.07 us
  Pallas kernels: 0 us -> 25 us
  between operations: 13.5 us -> 0.23 us
    all_to_all x1, blocking collectives: 100 us -> 18.3 us  [per_device(): lax.all_to_all(parts, AXES, split_axis=0, concat_axis=0, tiled=True, axis...]
    gather x1 -> x0, local copies, waits for them, and re-layouts: 75.2 us -> none  [per_device(): joint_slot = joint_table[rows].reshape(devices_all, dest_slots, 2 * width)]
    concatenate x1 -> x0, local copies, waits for them, and re-layouts: 44 us -> none  [per_device(): jnp.concatenate([jnp.dot(acct_feat, jnp.concatenate([key_weight[r], msg_w...]
    dot_general x7 -> x0, matrix products: 36.2 us -> none  [the longest x4 27 us: per_device(): jnp.dot(acct_feat, jnp.concatenate([key_weight[r], msg_weight[r]], axis=1...]
    pallas_call x0 -> x9, Pallas kernels: none -> 25 us  [the longest x2 13.3 us: project(): pl.pallas_call(functools.partial(project_kernel, masks, shift), out_shape...]
    concatenate x1 -> x4, other arithmetic: 22.5 us -> 0.07 us  [the longest x1 0.04 us: per_device(): feats = jnp.concatenate([feats, swap(feats, mask)], axis=0)]
    ppermute x0 -> x7, starting transfers between devices: none -> 9.54 us  [swap(): return lax.ppermute(value, AXES, [(s, s ^ mask) for s in range(devices)])]
    unnamed x18 -> x30, local copies, waits for them, and re-layouts: 0.9 us -> 8.88 us
  transfers between devices with their start and end apart: 2 -> 7, of which waited for: 0 -> 1; matrix products, arithmetic and copies ran while one was open for 58% -> 0% of each run, Pallas kernels for 0% -> 39%
where the time goes in v2:
time: 62.5 us; the launch traced here: 62.2 us
  Pallas kernels  25 us (40%)
  blocking collectives  18.3 us (29%)
  starting transfers between devices  9.54 us (15%)
  local copies, waits for them, and re-layouts  8.88 us (14%)
    all_to_all x1, blocking collectives, per_device(): lax.all_to_all(parts, AXES, split_axis=0, concat_axis=0, tiled=True, axis...  18.3 us
    pallas_call x2, Pallas kernels, project(): pl.pallas_call(functools.partial(project_kernel, masks, shift), out_shape...  13.3 us
    ppermute x7, starting transfers between devices, swap(): return lax.ppermute(value, AXES, [(s, s ^ mask) for s in range(devices)])  9.54 us
    unnamed x30, local copies, waits for them, and re-layouts  8.88 us
    pallas_call x2, Pallas kernels, gather(): pl.pallas_call(functools.partial(gather_kernel, masks, shift), out_shape=...  6.86 us
    pallas_call x2, Pallas kernels, aggregate(): pl.pallas_call(functools.partial(aggregate_kernel, masks, shift), out_sha...  3.07 us
  transfers between devices with their start and end apart: 7, of which 1 were waited for; matrix products, arithmetic and copies ran while one was open for 0% of the time, Pallas kernels for 39%

profile of v2, /device:TPU:0, one launch (start us, length us, event | category | flops | bytes accessed | tf_op | source)
XLA Modules:
  0.0 62.2 jit_solution(1514500369534879608)
XLA Ops:
  0.0 0.5 collective-permute-start
  0.5 3.7 %collective-permute-start.1 = (bf16[32,512]{1,0:T(8,128)(2,1)}, bf16[32,512]{1,0:T(8,128)(2,1)S(1)}, u32[]{:S(2)}, u32[]{:S(2)}) collective-permute-start(bf16[32,512]{1,0:T(8,128)(2,1)} %feat.1), channel_id=1, source_target_pairs={{0,17},{1,16},{2,19},{3,18},{4,21},{5,20},{6,23},{7,22},{8,25},{9,... | collective-permute-start | bytes 98312 | tf_op jit(solution)/shard_map/ppermute | solution.py:252
  4.2 2.2 %copy-done.3 = bf16[4096,512]{1,0:T(8,128)(2,1)S(1)} copy-done((bf16[4096,512]{1,0:T(8,128)(2,1)S(1)}, bf16[4096,512]{1,0:T(8,128)(2,1)}, u32[]{:S(2)}) %copy-start.3) | copy-done | bytes 4194328
  6.3 0.8 %make_table.1.table = f32[16384,128]{1,0:T(8,128)S(1)} custom-call(bf16[4096,512]{1,0:T(8,128)(2,1)S(1)} %copy-done.3), custom_call_target="tpu_custom_call" | custom-call | bytes 8388608 | tf_op jit(solution)/shard_map/make_table/pallas_call | solution.py:52
  7.1 3.2 %copy-done = f32[16384,128]{1,0:T(8,128)} copy-done((f32[16384,128]{1,0:T(8,128)}, f32[16384,128]{1,0:T(8,128)S(1)}, u32[]{:S(2)}) %copy-start) | copy-done | bytes 8388632
  10.4 1.6 %collective-permute-start.2 = (bf16[64,512]{1,0:T(8,128)(2,1)S(1)}, bf16[64,512]{1,0:T(8,128)(2,1)S(1)}, u32[]{:S(2)}, u32[]{:S(2)}) collective-permute-start(bf16[64,512]{1,0:T(8,128)(2,1)S(1)} %pad_maximum_fusion.3), channel_id=1, source_target_pairs={{0,8},{1,9},{2,10},{3,11},{4,12},{5,13},{6,14},{7,15},{8,0},{9,1},... | collective-permute-start | bytes 196616 | tf_op jit(solution)/shard_map/ppermute | solution.py:252
  12.0 3.4 %copy-done.1 = f32[16384,128]{1,0:T(8,128)S(1)} copy-done((f32[16384,128]{1,0:T(8,128)S(1)}, f32[16384,128]{1,0:T(8,128)}, u32[]{:S(2)}) %copy-start.1) | copy-done | bytes 8388632
  15.4 3.4 %gather_odd.1.feats = bf16[16,128,512]{2,1,0:T(8,128)(2,1)S(1)} custom-call(s32[1]{0:T(128)} %bitcast.1.me_ref, s32[32,128]{1,0:T(8,128)S(1)} %copy-done.6, f32[16384,128]{1,0:T(8,128)S(1)} %copy-done.1), custom_call_target="tpu_custom_call" | custom-call | bytes 8388608 | tf_op jit(solution)/shard_map/gather_odd/pallas_call | solution.py:91
  18.9 0.0 copy-start.10
  18.9 0.0 copy-start.13
  18.9 0.0 copy-start.14
  18.9 1.6 %collective-permute-start.3 = (bf16[128,512]{1,0:T(8,128)(2,1)S(1)}, bf16[128,512]{1,0:T(8,128)(2,1)S(1)}, u32[]{:S(2)}, u32[]{:S(2)}) collective-permute-start(bf16[128,512]{1,0:T(8,128)(2,1)S(1)} %pad_maximum_fusion.2), channel_id=1, source_target_pairs={{0,4},{1,5},{2,6},{3,7},{4,0},{5,1},{6,2},{7,3},{8,12},{9,13},{10,... | collective-permute-start | bytes 393224 | tf_op jit(solution)/shard_map/ppermute | solution.py:252
  20.5 3.4 %gather_even.1.feats = bf16[16,128,512]{2,1,0:T(8,128)(2,1)S(1)} custom-call(s32[1]{0:T(128)} %bitcast.1.me_ref, s32[32,128]{1,0:T(8,128)S(1)} %copy-done.6, f32[16384,128]{1,0:T(8,128)S(1)} %copy-done.2), custom_call_target="tpu_custom_call" | custom-call | bytes 8388608 | tf_op jit(solution)/shard_map/gather_even/pallas_call | solution.py:91
  23.9 0.2 collective-permute-done.3
  24.1 1.6 %collective-permute-start.4 = (bf16[256,512]{1,0:T(8,128)(2,1)S(1)}, bf16[256,512]{1,0:T(8,128)(2,1)S(1)}, u32[]{:S(2)}, u32[]{:S(2)}) collective-permute-start(bf16[256,512]{1,0:T(8,128)(2,1)S(1)} %pad_maximum_fusion.1), channel_id=1, source_target_pairs={{0,2},{1,3},{2,0},{3,1},{4,6},{5,7},{6,4},{7,5},{8,10},{9,11},{10,... | collective-permute-start | bytes 786440 | tf_op jit(solution)/shard_map/ppermute | solution.py:252
  25.7 6.6 %project_odd.1 = (bf16[16,512,128]{2,1,0:T(8,128)(2,1)S(1)}, bf16[16,128,512]{2,1,0:T(8,128)(2,1)S(1)}) custom-call(s32[1]{0:T(128)} %bitcast.1.me_ref, s32[32]{0:T(128)S(1)} %copy-done.10, bf16[16,128,512]{2,1,0:T(8,128)(2,1)S(1)} %gather_odd.1.feats, bf16[4,512,512]{2,1,0:T(8,128)(2,1)S(1)} %copy-done.13, bf16[4,512,512]{2,1,0:T(8,128)(2,1)S(1)} %copy-done.14), custom_call_target="tpu_custom_call" | custom-call | flops 2147483648 | bytes 12582912 | tf_op jit(solution)/shard_map/project_odd/pallas_call | solution.py:121
  32.3 0.0 copy-start.4
  32.3 0.0 copy-start.7
  32.4 0.0 copy-start.11
  32.4 0.0 copy-start.12
  32.4 6.6 %project_even.1 = (bf16[16,512,128]{2,1,0:T(8,128)(2,1)S(1)}, bf16[16,128,512]{2,1,0:T(8,128)(2,1)S(1)}) custom-call(s32[1]{0:T(128)} %bitcast.1.me_ref, s32[32]{0:T(128)S(1)} %copy-done.10, bf16[16,128,512]{2,1,0:T(8,128)(2,1)S(1)} %gather_even.1.feats, bf16[4,512,512]{2,1,0:T(8,128)(2,1)S(1)} %copy-done.13, bf16[4,512,512]{2,1,0:T(8,128)(2,1)S(1)} %copy-done.14), custom_call_target="tpu_custom_call" | custom-call | flops 2147483648 | bytes 12582912 | tf_op jit(solution)/shard_map/project_even/pallas_call | solution.py:121
  39.0 0.0 collective-permute-done.4
  39.1 0.1 collective-permute-start.5
  39.2 1.5 %aggregate_odd.1 = bf16[512,512]{1,0:T(8,128)(2,1)S(1)} custom-call(s32[1]{0:T(128)} %bitcast.1.me_ref, s32[32]{0:T(128)S(1)} %copy-done.10, s32[32]{0:T(128)S(1)} %copy-done.11, f32[4]{0:T(128)S(1)} %copy-done.12, s32[32,128]{1,0:T(8,128)S(1)} %copy-done.7, bf16[512,512]{1,0:T(8,128)(2,1)S(1)} %pad_maximum_fusion.feats, bf16[512,512]{1,0:T(8,128)(2,1)S(1)} %copy-done.4, ...), custom_call_target="tpu_custom_call" | custom-call | flops 402653184 | bytes 6291456 | tf_op jit(solution)/shard_map/aggregate_odd/pallas_call | solution.py:164
  40.7 0.5 collective-permute-start.6
  41.3 1.5 %aggregate_even.1.mine = f32[512,512]{1,0:T(8,128)S(1)} custom-call(s32[1]{0:T(128)} %bitcast.1.me_ref, s32[32]{0:T(128)S(1)} %copy-done.10, s32[32]{0:T(128)S(1)} %copy-done.11, f32[4]{0:T(128)S(1)} %copy-done.12, s32[32,128]{1,0:T(8,128)S(1)} %copy-done.7, bf16[512,512]{1,0:T(8,128)(2,1)S(1)} %collective-permute-done.5.feats, ...), custom_call_target="tpu_custom_call" | custom-call | flops 402653184 | bytes 6291456 | tf_op jit(solution)/shard_map/aggregate_even/pallas_call | solution.py:164
  42.8 0.0 copy-start.5
  42.8 0.0 copy-start.8
  42.8 0.0 copy-start.9
  42.9 0.1 combine.1
  43.0 18.3 %all_to_all.11 = bf16[16,32,512]{2,1,0:T(8,128)(2,1)S(1)} all-to-all(bf16[16,32,512]{2,1,0:T(8,128)(2,1)S(1)} %bitcast.4), channel_id=1, replica_groups={{0,2,4,6,8,10,12,14,16,18,20,22,24,26,28,30},{1,3,5,7,9,11,13,15,17,19,..., dimensions={0} | all-to-all | bytes 1048576 | tf_op jit(solution)/shard_map/all_to_all | solution.py:279
  61.3 0.9 %finish.1 = bf16[32,512]{1,0:T(8,128)(2,1)} custom-call(bf16[32,512]{1,0:T(8,128)(2,1)S(1)} %copy-done.8, f32[1,512]{1,0:T(1,128)S(1)} %bitcast.6, bf16[512,512]{1,0:T(8,128)(2,1)S(1)} %copy-done.5, bf16[512,512]{1,0:T(8,128)(2,1)S(1)} %bitcast.5), custom_call_target="tpu_custom_call" | custom-call | tf_op jit(solution)/shard_map/finish/pallas_call | solution.py:220
  (26 shorter events, 0.1 us)
Async XLA Ops:
  0.0 10.4 %collective-permute-start = (bf16[32,512]{1,0:T(8,128)(2,1)}, bf16[32,512]{1,0:T(8,128)(2,1)S(1)}, u32[]{:S(2)}, u32[]{:S(2)}) collective-permute-start(bf16[32,512]{1,0:T(8,128)(2,1)} %feat.1), channel_id=1, source_target_pairs={{0,1},{1,0},{2,3},{3,2},{4,5},{5,4},{6,7},{7,6},{8,9},{9,8},{10,11... | collective-permute-start | bytes 98312 | tf_op jit(solution)/shard_map/ppermute | solution.py:252
  0.5 9.9 %collective-permute-start.1 = (bf16[32,512]{1,0:T(8,128)(2,1)}, bf16[32,512]{1,0:T(8,128)(2,1)S(1)}, u32[]{:S(2)}, u32[]{:S(2)}) collective-permute-start(bf16[32,512]{1,0:T(8,128)(2,1)} %feat.1), channel_id=1, source_target_pairs={{0,17},{1,16},{2,19},{3,18},{4,21},{5,20},{6,23},{7,22},{8,25},{9,... | collective-permute-start | bytes 98312 | tf_op jit(solution)/shard_map/ppermute | solution.py:252
  4.2 2.2 %copy-start.3 = (bf16[4096,512]{1,0:T(8,128)(2,1)S(1)}, bf16[4096,512]{1,0:T(8,128)(2,1)}, u32[]{:S(2)}) copy-start(bf16[4096,512]{1,0:T(8,128)(2,1)} %acct.1) | copy-start | bytes 12582916
  6.3 5.7 %copy-start.6 = (s32[32,128]{1,0:T(8,128)S(1)}, s32[32,128]{1,0:T(8,128)}, u32[]{:S(2)}) copy-start(s32[32,128]{1,0:T(8,128)} %slots_ref.3) | copy-start | bytes 49156
  7.1 3.3 %copy-start = (f32[16384,128]{1,0:T(8,128)}, f32[16384,128]{1,0:T(8,128)S(1)}, u32[]{:S(2)}) copy-start(f32[16384,128]{1,0:T(8,128)S(1)} %make_table.1.table) | copy-start | bytes 25165828
  10.4 8.5 %collective-permute-start.2 = (bf16[64,512]{1,0:T(8,128)(2,1)S(1)}, bf16[64,512]{1,0:T(8,128)(2,1)S(1)}, u32[]{:S(2)}, u32[]{:S(2)}) collective-permute-start(bf16[64,512]{1,0:T(8,128)(2,1)S(1)} %pad_maximum_fusion.3), channel_id=1, source_target_pairs={{0,8},{1,9},{2,10},{3,11},{4,12},{5,13},{6,14},{7,15},{8,0},{9,1},... | collective-permute-start | bytes 196616 | tf_op jit(solution)/shard_map/ppermute | solution.py:252
  12.0 3.4 %copy-start.1 = (f32[16384,128]{1,0:T(8,128)S(1)}, f32[16384,128]{1,0:T(8,128)}, u32[]{:S(2)}) copy-start(f32[16384,128]{1,0:T(8,128)} %copy-done) | copy-start | bytes 25165828
  15.4 5.1 %copy-start.2 = (f32[16384,128]{1,0:T(8,128)S(1)}, f32[16384,128]{1,0:T(8,128)}, u32[]{:S(2)}) copy-start(f32[16384,128]{1,0:T(8,128)} %copy-done) | copy-start | bytes 25165828
  18.9 6.8 %copy-start.10 = (s32[32]{0:T(128)S(1)}, s32[32]{0:T(128)}, u32[]{:S(2)}) copy-start(s32[32]{0:T(128)} %rel_ref.7) | copy-start | bytes 388
  18.9 6.8 %copy-start.13 = (bf16[4,512,512]{2,1,0:T(8,128)(2,1)S(1)}, bf16[4,512,512]{2,1,0:T(8,128)(2,1)}, u32[]{:S(2)}) copy-start(bf16[4,512,512]{2,1,0:T(8,128)(2,1)} %kw.3) | copy-start | bytes 6291460
  18.9 6.8 %copy-start.14 = (bf16[4,512,512]{2,1,0:T(8,128)(2,1)S(1)}, bf16[4,512,512]{2,1,0:T(8,128)(2,1)}, u32[]{:S(2)}) copy-start(bf16[4,512,512]{2,1,0:T(8,128)(2,1)} %mw.3) | copy-start | bytes 6291460
  18.9 5.2 %collective-permute-start.3 = (bf16[128,512]{1,0:T(8,128)(2,1)S(1)}, bf16[128,512]{1,0:T(8,128)(2,1)S(1)}, u32[]{:S(2)}, u32[]{:S(2)}) collective-permute-start(bf16[128,512]{1,0:T(8,128)(2,1)S(1)} %pad_maximum_fusion.2), channel_id=1, source_target_pairs={{0,4},{1,5},{2,6},{3,7},{4,0},{5,1},{6,2},{7,3},{8,12},{9,13},{10,... | collective-permute-start | bytes 393224 | tf_op jit(solution)/shard_map/ppermute | solution.py:252
  24.1 14.9 %collective-permute-start.4 = (bf16[256,512]{1,0:T(8,128)(2,1)S(1)}, bf16[256,512]{1,0:T(8,128)(2,1)S(1)}, u32[]{:S(2)}, u32[]{:S(2)}) collective-permute-start(bf16[256,512]{1,0:T(8,128)(2,1)S(1)} %pad_maximum_fusion.1), channel_id=1, source_target_pairs={{0,2},{1,3},{2,0},{3,1},{4,6},{5,7},{6,4},{7,5},{8,10},{9,11},{10,... | collective-permute-start | bytes 786440 | tf_op jit(solution)/shard_map/ppermute | solution.py:252
  32.3 6.8 %copy-start.4 = (bf16[512,512]{1,0:T(8,128)(2,1)S(1)}, bf16[512,512]{1,0:T(8,128)(2,1)}, u32[]{:S(2)}) copy-start(bf16[512,512]{1,0:T(8,128)(2,1)} %wq.3) | copy-start | bytes 1572868
  32.3 6.8 %copy-start.7 = (s32[32,128]{1,0:T(8,128)S(1)}, s32[32,128]{1,0:T(8,128)}, u32[]{:S(2)}) copy-start(s32[32,128]{1,0:T(8,128)} %merch_slot.3) | copy-start | bytes 49156
  32.4 6.8 %copy-start.11 = (s32[32]{0:T(128)S(1)}, s32[32]{0:T(128)}, u32[]{:S(2)}) copy-start(s32[32]{0:T(128)} %count_ref.3) | copy-start | bytes 388
  32.4 6.8 %copy-start.12 = (f32[4]{0:T(128)S(1)}, f32[4]{0:T(128)}, u32[]{:S(2)}) copy-start(f32[4]{0:T(128)} %bias_ref.3) | copy-start | bytes 52
  39.1 2.2 %collective-permute-start.5 = (bf16[512,512]{1,0:T(8,128)(2,1)S(1)}, bf16[512,512]{1,0:T(8,128)(2,1)S(1)}, u32[]{:S(2)}, u32[]{:S(2)}) collective-permute-start(bf16[512,512]{1,0:T(8,128)(2,1)S(1)} %pad_maximum_fusion.feats), channel_id=1, source_target_pairs={{0,1},{1,0},{2,3},{3,2},{4,5},{5,4},{6,7},{7,6},{8,9},{9,8},{10,11... | collective-permute-start | bytes 1572872 | tf_op jit(solution)/shard_map/ppermute | solution.py:252
  40.7 2.1 %collective-permute-start.6 = (bf16[512,512]{1,0:T(8,128)(2,1)S(1)}, bf16[512,512]{1,0:T(8,128)(2,1)S(1)}, u32[]{:S(2)}, u32[]{:S(2)}) collective-permute-start(bf16[512,512]{1,0:T(8,128)(2,1)S(1)} %aggregate_odd.1), channel_id=1, source_target_pairs={{0,1},{1,0},{2,3},{3,2},{4,5},{5,4},{6,7},{7,6},{8,9},{9,8},{10,11... | collective-permute-start | bytes 1572872 | tf_op jit(solution)/shard_map/ppermute | solution.py:252
  42.8 18.5 %copy-start.5 = (bf16[512,512]{1,0:T(8,128)(2,1)S(1)}, bf16[512,512]{1,0:T(8,128)(2,1)}, u32[]{:S(2)}) copy-start(bf16[512,512]{1,0:T(8,128)(2,1)} %wo.1) | copy-start | bytes 1572868
  42.8 18.5 %copy-start.8 = (bf16[32,512]{1,0:T(8,128)(2,1)S(1)}, bf16[32,512]{1,0:T(8,128)(2,1)}, u32[]{:S(2)}) copy-start(bf16[32,512]{1,0:T(8,128)(2,1)} %feat.1) | copy-start | bytes 98308
  42.8 18.5 %copy-start.9 = (f32[512]{0:T(512)S(1)}, f32[512]{0:T(512)}, u32[]{:S(2)}) copy-start(f32[512]{0:T(512)} %param.19) | copy-start | bytes 6148

commit v3 on v2

v3 whole, which is shorter than its diff:
```python
import functools
import math

import jax
import jax.numpy as jnp
from jax import lax
from jax.experimental import pallas as pl
from jax.experimental.pallas import tpu as pltpu
from jax.sharding import PartitionSpec as P

AXES = ("acct", "merch")
LANES = 128
F32 = jnp.float32
BF16 = jnp.bfloat16
SMEM = pl.BlockSpec(memory_space=pltpu.SMEM)
VMEM = pl.BlockSpec(memory_space=pltpu.VMEM)


def _mb(n):
    return pltpu.CompilerParams(vmem_limit_bytes=n * 2**20)


def _cost(flops, bytes_accessed, transcendentals=0):
    return pl.CostEstimate(
        flops=int(flops), bytes_accessed=int(bytes_accessed), transcendentals=transcendentals
    )


def _offset(i, outer):
    return (i // outer) * 2 + (i % outer) * 8


def gather_kernel(outer, me_ref, slots_ref, acct, odd, even, table, rows0, rows1):
    accounts, width = acct.shape
    blocks, block_len, _ = odd.shape
    parts = width // LANES
    pitch = table.shape[1]
    flat = table.reshape(accounts * pitch, LANES)
    me = me_ref[0]

    @pl.loop(0, accounts // 16, unroll=4)
    def _(g):
        first = pl.multiple_of(g * 16, 16)
        tile = acct[pl.ds(first, 16), :].astype(F32)
        for c in range(parts):
            flat[pl.ds(first * pitch + c, 16, stride=pitch), :] = tile[
                :, c * LANES : (c + 1) * LANES
            ]

    def collect(block, rows):
        for k in range(block_len):
            rows[k * parts : (k + 1) * parts, :] = table[slots_ref[block, k], :parts, :]

    def emit(i, rows, out):
        for c in range(parts):
            out[i, :, c * LANES : (c + 1) * LANES] = rows[
                pl.ds(c, block_len, stride=parts), :
            ].astype(BF16)

    @pl.loop(0, blocks)
    def _(i):
        offset = _offset(i, outer)
        collect(jnp.bitwise_xor(me, offset + 1), rows0)
        collect(jnp.bitwise_xor(me, offset), rows1)
        emit(i, rows0, odd)
        emit(i, rows1, even)


def gather(outer, me, slots, acct):
    blocks, block_len = slots.shape
    accounts, width = acct.shape
    parts = width // LANES
    rows = pltpu.VMEM((block_len * parts, LANES), F32)
    half = jax.ShapeDtypeStruct((blocks // 2, block_len, width), BF16)
    return pl.pallas_call(
        functools.partial(gather_kernel, outer),
        out_shape=(half, half),
        in_specs=[SMEM, SMEM, VMEM],
        out_specs=(VMEM, VMEM),
        scratch_shapes=[pltpu.VMEM((accounts, -(-parts // 8) * 8, LANES), F32), rows, rows],
        compiler_params=_mb(20),
        cost_estimate=_cost(0, 20 * 2**20),
        name="gather_slots",
    )(me, slots, acct)


def project_kernel(outer, shifts, me_ref, rel_ref, kw, mw, *refs):
    halves = len(shifts)
    blocks, _, width = refs[0].shape
    half = width // 2
    me = me_ref[0]

    def one(i, shift, feats, keys, values):
        relation = rel_ref[jnp.bitwise_xor(me, _offset(i, outer) + shift)]
        for n in range(0, width, half):
            key = jnp.dot(feats[i], kw[relation, :, n : n + half], preferred_element_type=F32)
            keys[i, n : n + half, :] = key.astype(BF16).T
            value = jnp.dot(feats[i], mw[relation, :, n : n + half], preferred_element_type=F32)
            values[i, :, n : n + half] = value.astype(BF16)

    @pl.loop(0, blocks, unroll=2)
    def _(i):
        for h, shift in enumerate(shifts):
            one(i, shift, refs[h], refs[halves + 2 * h], refs[halves + 2 * h + 1])


def project(outer, shifts, me, rel, feats, kw, mw):
    blocks, block_len, width = feats[0].shape
    keys = jax.ShapeDtypeStruct((blocks, width, block_len), BF16)
    values = jax.ShapeDtypeStruct((blocks, block_len, width), BF16)
    return pl.pallas_call(
        functools.partial(project_kernel, outer, shifts),
        out_shape=(keys, values) * len(shifts),
        in_specs=[SMEM, SMEM] + [VMEM] * (2 + len(shifts)),
        out_specs=(VMEM, VMEM) * len(shifts),
        compiler_params=_mb(4),
        cost_estimate=_cost(
            4 * len(shifts) * blocks * block_len * width * width, 8 * len(shifts) * 2**20
        ),
        name="project_slots",
    )(me, rel, kw, mw, *feats)


def aggregate_kernel(
    outer, shift, me_ref, rel_ref, count_ref, bias_ref, merch_slot, feats, wq, keys, values,
    sums, query, gates,
):
    blocks, width, block_len = keys.shape
    merchants = feats.shape[0] // blocks
    me = me_ref[0]
    row = lax.broadcasted_iota(jnp.int32, (merchants, block_len), 0)
    lane = lax.broadcasted_iota(jnp.int32, (merchants, block_len), 1)
    query[...] = jnp.dot(feats[...], wq[...], preferred_element_type=F32).astype(BF16)
    for i in range(blocks):
        block = jnp.bitwise_xor(me, _offset(i, outer) + shift)
        score = jnp.dot(
            query[i * merchants : (i + 1) * merchants, :], keys[i], preferred_element_type=F32
        ) / math.sqrt(width)
        score = score + bias_ref[rel_ref[block]]
        mine = (merch_slot[pl.ds(block, 1), :] == row) & (lane < count_ref[block])
        gates[i * merchants : (i + 1) * merchants, :] = jnp.where(
            mine, jax.nn.sigmoid(score), 0.0
        ).astype(BF16)
    for i in range(blocks):
        sums[i * merchants : (i + 1) * merchants, :] = jnp.dot(
            gates[i * merchants : (i + 1) * merchants, :], values[i], preferred_element_type=F32
        ).astype(sums.dtype)


def aggregate(outer, shift, me, rel, count, bias, merch_slot, feats, wq, keys, values, dtype):
    blocks, width, block_len = keys.shape
    merchants = feats.shape[0] // blocks
    return pl.pallas_call(
        functools.partial(aggregate_kernel, outer, shift),
        out_shape=jax.ShapeDtypeStruct(feats.shape, dtype),
        in_specs=[SMEM] * 4 + [VMEM] * 5,
        out_specs=VMEM,
        scratch_shapes=[
            pltpu.VMEM(feats.shape, BF16),
            pltpu.VMEM((feats.shape[0], block_len), BF16),
        ],
        compiler_params=_mb(6),
        cost_estimate=_cost(
            4 * blocks * merchants * block_len * width + 2 * feats.shape[0] * width * width,
            6 * 2**20,
            blocks * merchants * block_len,
        ),
        name="aggregate_odd" if shift else "aggregate_even",
    )(me, rel, count, bias, merch_slot, feats, wq, keys, values)


def combine_kernel(mine, other, *outs):
    rows = outs[0].shape[0]
    for j, out in enumerate(outs):
        part = slice(j * rows, (j + 1) * rows)
        out[...] = (mine[part, :] + other[part, :].astype(F32)).astype(out.dtype)


def combine(inner, mine, other):
    rows, width = mine.shape
    return pl.pallas_call(
        combine_kernel,
        out_shape=tuple(
            jax.ShapeDtypeStruct((rows // inner, width), F32 if j == 0 else BF16)
            for j in range(inner)
        ),
        in_specs=[VMEM, VMEM],
        out_specs=(VMEM,) * inner,
        compiler_params=_mb(2),
        cost_estimate=_cost(0, 2 * 2**20),
        name="combine_cores",
    )(mine, other)


def plane_kernel(inner, *refs):
    ins, outs = refs[:inner], refs[inner:]
    rows = outs[0].shape[0]
    for k, out in enumerate(outs):
        part = slice(k * rows, (k + 1) * rows)
        total = ins[0][part, :]
        for other in ins[1:]:
            total = total + other[part, :].astype(F32)
        out[...] = total.astype(out.dtype)


def combine_plane(outer, parts):
    rows, width = parts[0].shape
    return pl.pallas_call(
        functools.partial(plane_kernel, len(parts)),
        out_shape=tuple(
            jax.ShapeDtypeStruct((rows // outer, width), F32 if k == 0 else BF16)
            for k in range(outer)
        ),
        in_specs=[VMEM] * len(parts),
        out_specs=(VMEM,) * outer,
        compiler_params=_mb(2),
        cost_estimate=_cost(0, 2**20),
        name="combine_plane",
    )(*parts)


def finish_kernel(feat, gain, wo, *refs):
    out = refs[-1]
    total = refs[0][...]
    for part in refs[1:-1]:
        total = total + part[...].astype(F32)
    update = feat[...].astype(F32) + jnp.dot(
        total.astype(BF16), wo[...], preferred_element_type=F32
    )
    scale = lax.rsqrt(jnp.mean(update * update, axis=-1, keepdims=True) + 1e-06)
    out[...] = (update * scale * gain[...]).astype(BF16)


def finish(feat, gain, wo, parts):
    return pl.pallas_call(
        finish_kernel,
        out_shape=jax.ShapeDtypeStruct(feat.shape, BF16),
        in_specs=[VMEM] * (3 + len(parts)),
        out_specs=VMEM,
        compiler_params=_mb(2),
        name="finish",
    )(feat, gain.reshape(1, -1), wo, *parts)


def per_device(
    acct_feat,
    merch_feat,
    key_weight,
    msg_weight,
    query_weight,
    out_weight,
    rel_bias,
    out_gain,
    slot_acct,
    slot_merch,
    block_rel,
    block_count,
):
    devices = lax.axis_size(AXES)
    me = lax.axis_index(AXES).astype(jnp.int32).reshape(1)
    inner = 4
    outer = devices // (2 * inner)

    def swap(value, mask):
        return lax.ppermute(value, AXES, [(s, s ^ mask) for s in range(devices)])

    def after(value, *others):
        return lax.optimization_barrier((value,) + others)[0]

    feats = jnp.concatenate([swap(merch_feat, 8 * k + 1) for k in range(outer)], axis=0)
    odd_rows, even_rows = gather(outer, me, slot_acct, acct_feat)
    feats = after(feats, odd_rows)
    feats = jnp.concatenate([feats] + [swap(feats, 2 * j) for j in range(1, inner)], axis=0)
    rows = (odd_rows, even_rows)
    weights = (key_weight, msg_weight)
    if devices <= 32:
        projected = project(outer, (1, 0), me, block_rel, rows, *weights)
    else:
        projected = [
            out
            for shift, feat in zip((1, 0), rows)
            for out in project(outer, (shift,), me, block_rel, (feat,), *weights)
        ]
    odd_keys, odd_values, even_keys, even_values = projected
    feats = after(feats, even_keys)

    shared = (me, block_rel, block_count, rel_bias, slot_merch)
    even_feats = swap(feats, 1)
    odd_sums = aggregate(outer, 1, *shared, feats, query_weight, odd_keys, odd_values, BF16)
    other = swap(odd_sums, 1)
    even_sums = aggregate(outer, 0, *shared, even_feats, query_weight, even_keys, even_values, F32)
    parts = combine(inner, even_sums, other)
    parts = combine_plane(
        outer, [parts[0]] + [swap(parts[j], 2 * j) for j in reversed(range(1, inner))]
    )
    parts = [parts[0]] + [swap(parts[k], 8 * k) for k in reversed(range(1, outer))]
    return finish(merch_feat, out_gain, out_weight, parts)


def solution(mesh):
    placed = (
        P(("acct", "merch"), None),
        P(("acct", "merch"), None),
        P(),
        P(),
        P(),
        P(),
        P(),
        P(),
        P(("acct", "merch"), None),
        P(("acct", "merch"), None),
        P(("acct", "merch")),
        P(("acct", "merch")),
    )
    return jax.shard_map(
        per_device,
        mesh=mesh,
        in_specs=placed,
        out_specs=P(("acct", "merch"), None),
        check_vma=False,
    )
```

time: 62.5 us -> 50 us (0.80)
  blocking collectives: 18.3 us -> 0 us
  waiting for transfers between devices: 0.19 us -> 10.4 us
  starting transfers between devices: 9.54 us -> 17.5 us
  Pallas kernels: 25 us -> 18.6 us
  local copies, waits for them, and re-layouts: 8.88 us -> 2.95 us
    all_to_all x1 -> x0, blocking collectives: 18.3 us -> none  [per_device(): lax.all_to_all(parts, AXES, split_axis=0, concat_axis=0, tiled=True, axis...]
    ppermute x7 -> x15, waiting for transfers between devices: 0.19 us -> 10.4 us  [swap(): return lax.ppermute(value, AXES, [(s, s ^ mask) for s in range(devices)])]
    ppermute x7 -> x15, starting transfers between devices: 9.54 us -> 17.5 us  [swap(): return lax.ppermute(value, AXES, [(s, s ^ mask) for s in range(devices)])]
    pallas_call x8 -> x6, Pallas kernels: 24.1 us -> 17.7 us  [the longest x1 7.64 us: gather(): pl.pallas_call(functools.partial(gather_kernel, outer), out_shape=(half,...]
    unnamed x30 -> x24, local copies, waits for them, and re-layouts: 8.88 us -> 2.95 us
  transfers between devices with their start and end apart: 7 -> 15, of which waited for: 1 -> 5; matrix products, arithmetic and copies ran while one was open for 0% -> 0% of each run, Pallas kernels for 39% -> 35%
where the time goes in v3:
time: 50 us; the launch traced here: 49.8 us
  Pallas kernels  18.6 us (37%)
  starting transfers between devices  17.5 us (35%)
  waiting for transfers between devices  10.4 us (21%)
  local copies, waits for them, and re-layouts  2.95 us (6%)
    ppermute x15, starting transfers between devices, swap(): return lax.ppermute(value, AXES, [(s, s ^ mask) for s in range(devices)])  17.5 us
    ppermute x15, waiting for transfers between devices, swap(): return lax.ppermute(value, AXES, [(s, s ^ mask) for s in range(devices)])  10.4 us
    pallas_call x1, Pallas kernels, gather(): pl.pallas_call(functools.partial(gather_kernel, outer), out_shape=(half,...  7.64 us
    pallas_call x1, Pallas kernels, project(): pl.pallas_call(functools.partial(project_kernel, outer, shifts), out_shap...  6.87 us
    pallas_call x2, Pallas kernels, aggregate(): pl.pallas_call(functools.partial(aggregate_kernel, outer, shift), out_sha...  3.07 us
    unnamed x24, local copies, waits for them, and re-layouts  2.95 us
  transfers between devices with their start and end apart: 15, of which 5 were waited for; matrix products, arithmetic and copies ran while one was open for 0% of the time, Pallas kernels for 35%

profile of v3, /device:TPU:0, one launch (start us, length us, event | category | flops | bytes accessed | tf_op | source)
XLA Modules:
  0.0 49.8 jit_solution(15746085427148675920)
XLA Ops:
  0.0 3.5 %collective-permute-start.2 = (bf16[32,512]{1,0:T(8,128)(2,1)}, bf16[32,512]{1,0:T(8,128)(2,1)S(1)}, u32[]{:S(2)}, u32[]{:S(2)}) collective-permute-start(bf16[32,512]{1,0:T(8,128)(2,1)} %feat.1), channel_id=1, source_target_pairs={{0,17},{1,16},{2,19},{3,18},{4,21},{5,20},{6,23},{7,22},{8,25},{9,... | collective-permute-start | bytes 98312 | tf_op jit(solution)/shard_map/ppermute | solution.py:265
  3.5 1.9 %collective-permute-start.1 = (bf16[32,512]{1,0:T(8,128)(2,1)}, bf16[32,512]{1,0:T(8,128)(2,1)S(1)}, u32[]{:S(2)}, u32[]{:S(2)}) collective-permute-start(bf16[32,512]{1,0:T(8,128)(2,1)} %feat.1), channel_id=1, source_target_pairs={{0,9},{1,8},{2,11},{3,10},{4,13},{5,12},{6,15},{7,14},{8,1},{9,0},... | collective-permute-start | bytes 98312 | tf_op jit(solution)/shard_map/ppermute | solution.py:265
  5.3 2.2 %copy-done = bf16[4096,512]{1,0:T(8,128)(2,1)S(1)} copy-done((bf16[4096,512]{1,0:T(8,128)(2,1)S(1)}, bf16[4096,512]{1,0:T(8,128)(2,1)}, u32[]{:S(2)}) %copy-start) | copy-done | bytes 4194328
  7.5 0.7 %copy-done.5 = s32[32,128]{1,0:T(8,128)S(1)} copy-done((s32[32,128]{1,0:T(8,128)S(1)}, s32[32,128]{1,0:T(8,128)}, u32[]{:S(2)}) %copy-start.5) | copy-done | bytes 16408
  8.3 7.6 %gather_slots.1 = (bf16[16,128,512]{2,1,0:T(8,128)(2,1)S(1)}, bf16[16,128,512]{2,1,0:T(8,128)(2,1)S(1)}) custom-call(s32[1]{0:T(128)} %bitcast.1.me_ref, s32[32,128]{1,0:T(8,128)S(1)} %copy-done.5, bf16[4096,512]{1,0:T(8,128)(2,1)S(1)} %copy-done), custom_call_target="tpu_custom_call" | custom-call | bytes 20971520 | tf_op jit(solution)/shard_map/gather_slots/pallas_call | solution.py:75
  16.0 2.8 %collective-permute-start.6 = (bf16[128,512]{1,0:T(8,128)(2,1)S(1)}, bf16[128,512]{1,0:T(8,128)(2,1)S(1)}, u32[]{:S(2)}, u32[]{:S(2)}) collective-permute-start(bf16[128,512]{1,0:T(8,128)(2,1)S(1)} %pad_maximum_fusion.1), channel_id=1, source_target_pairs={{0,6},{1,7},{2,4},{3,5},{4,2},{5,3},{6,0},{7,1},{8,14},{9,15},{10,... | collective-permute-start | bytes 393224 | tf_op jit(solution)/shard_map/ppermute | solution.py:265
  18.8 0.5 %collective-permute-start.5 = (bf16[128,512]{1,0:T(8,128)(2,1)S(1)}, bf16[128,512]{1,0:T(8,128)(2,1)S(1)}, u32[]{:S(2)}, u32[]{:S(2)}) collective-permute-start(bf16[128,512]{1,0:T(8,128)(2,1)S(1)} %pad_maximum_fusion.1), channel_id=1, source_target_pairs={{0,4},{1,5},{2,6},{3,7},{4,0},{5,1},{6,2},{7,3},{8,12},{9,13},{10,... | collective-permute-start | bytes 393224 | tf_op jit(solution)/shard_map/ppermute | solution.py:265
  19.3 0.2 collective-permute-start.4
  19.5 0.0 copy-start.3
  19.5 0.0 copy-start.8
  19.6 0.0 copy-start.9
  19.6 6.9 %project_slots.1 = (bf16[16,512,128]{2,1,0:T(8,128)(2,1)S(1)}, bf16[16,128,512]{2,1,0:T(8,128)(2,1)S(1)}, bf16[16,512,128]{2,1,0:T(8,128)(2,1)S(1)}, bf16[16,128,512]{2,1,0:T(8,128)(2,1)S(1)}) custom-call(s32[1]{0:T(128)} %bitcast.1.me_ref, s32[32]{0:T(128)S(1)} %copy-done.7, bf16[4,512,512]{2,1,0:T(8,128)(2,1)S(1)} %copy-done.10, ...), custom_call_target="tpu_custom_call" | custom-call | flops 4294967296 | bytes 16777216 | tf_op jit(solution)/shard_map/project_slots/pallas_call | solution.py:111
  26.5 0.1 collective-permute-start.7
  26.6 1.5 %aggregate_odd.1 = bf16[512,512]{1,0:T(8,128)(2,1)S(1)} custom-call(s32[1]{0:T(128)} %bitcast.1.me_ref, s32[32]{0:T(128)S(1)} %copy-done.7, s32[32]{0:T(128)S(1)} %copy-done.8, f32[4]{0:T(128)S(1)} %copy-done.9, s32[32,128]{1,0:T(8,128)S(1)} %copy-done.3, bf16[512,512]{1,0:T(8,128)(2,1)S(1)} %pad_maximum_fusion.feats, bf16[512,512]{1,0:T(8,128)(2,1)S(1)} %copy-done.1, ...), custom_call_target="tpu_custom_call" | custom-call | flops 402653184 | bytes 6291456 | tf_op jit(solution)/shard_map/aggregate_odd/pallas_call | solution.py:153
  28.2 0.5 %collective-permute-start.8 = (bf16[512,512]{1,0:T(8,128)(2,1)S(1)}, bf16[512,512]{1,0:T(8,128)(2,1)S(1)}, u32[]{:S(2)}, u32[]{:S(2)}) collective-permute-start(bf16[512,512]{1,0:T(8,128)(2,1)S(1)} %aggregate_odd.1), channel_id=1, source_target_pairs={{0,1},{1,0},{2,3},{3,2},{4,5},{5,4},{6,7},{7,6},{8,9},{9,8},{10,11... | collective-permute-start | bytes 1572872 | tf_op jit(solution)/shard_map/ppermute | solution.py:265
  28.7 1.5 %aggregate_even.1.mine = f32[512,512]{1,0:T(8,128)S(1)} custom-call(s32[1]{0:T(128)} %bitcast.1.me_ref, s32[32]{0:T(128)S(1)} %copy-done.7, s32[32]{0:T(128)S(1)} %copy-done.8, f32[4]{0:T(128)S(1)} %copy-done.9, s32[32,128]{1,0:T(8,128)S(1)} %copy-done.3, bf16[512,512]{1,0:T(8,128)(2,1)S(1)} %collective-permute-done.7.feats, bf16[512,512]{1,0:T(8,128)(2,1)S(1)} %copy-done.1, ...), custom_call_target="tpu_custom_call" | custom-call | flops 402653184 | bytes 6291456 | tf_op jit(solution)/shard_map/aggregate_even/pallas_call | solution.py:153
  30.3 0.0 copy-start.2
  30.3 0.0 copy-start.4
  30.3 0.0 copy-start.6
  30.3 0.1 combine_cores.1
  30.4 2.8 %collective-permute-start.9 = (bf16[128,512]{1,0:T(8,128)(2,1)S(1)}, bf16[128,512]{1,0:T(8,128)(2,1)S(1)}, u32[]{:S(2)}, u32[]{:S(2)}) collective-permute-start(bf16[128,512]{1,0:T(8,128)(2,1)S(1)} %get-tuple-element.30), channel_id=1, source_target_pairs={{0,6},{1,7},{2,4},{3,5},{4,2},{5,3},{6,0},{7,1},{8,14},{9,15},{10,... | collective-permute-start | bytes 393224 | tf_op jit(solution)/shard_map/ppermute | solution.py:265
  33.2 0.5 %collective-permute-start.10 = (bf16[128,512]{1,0:T(8,128)(2,1)S(1)}, bf16[128,512]{1,0:T(8,128)(2,1)S(1)}, u32[]{:S(2)}, u32[]{:S(2)}) collective-permute-start(bf16[128,512]{1,0:T(8,128)(2,1)S(1)} %get-tuple-element.31), channel_id=1, source_target_pairs={{0,4},{1,5},{2,6},{3,7},{4,0},{5,1},{6,2},{7,3},{8,12},{9,13},{10,... | collective-permute-start | bytes 393224 | tf_op jit(solution)/shard_map/ppermute | solution.py:265
  33.7 0.2 collective-permute-start.11
  34.0 3.4 %collective-permute-done.9.refs_1_ = bf16[128,512]{1,0:T(8,128)(2,1)S(1)} collective-permute-done((bf16[128,512]{1,0:T(8,128)(2,1)S(1)}, bf16[128,512]{1,0:T(8,128)(2,1)S(1)}, u32[]{:S(2)}, u32[]{:S(2)}) %collective-permute-start.9) | collective-permute-done | bytes 131104 | tf_op jit(solution)/shard_map/ppermute | solution.py:265
  37.3 2.7 %collective-permute-done.10.refs_2_ = bf16[128,512]{1,0:T(8,128)(2,1)S(1)} collective-permute-done((bf16[128,512]{1,0:T(8,128)(2,1)S(1)}, bf16[128,512]{1,0:T(8,128)(2,1)S(1)}, u32[]{:S(2)}, u32[]{:S(2)}) %collective-permute-start.10) | collective-permute-done | bytes 131104 | tf_op jit(solution)/shard_map/ppermute | solution.py:265
  40.0 0.3 collective-permute-done.11.refs_3_
  40.3 0.1 combine_plane.1
  40.4 3.7 %collective-permute-start.12 = (bf16[32,512]{1,0:T(8,128)(2,1)S(1)}, bf16[32,512]{1,0:T(8,128)(2,1)S(1)}, u32[]{:S(2)}, u32[]{:S(2)}) collective-permute-start(bf16[32,512]{1,0:T(8,128)(2,1)S(1)} %get-tuple-element.34), channel_id=1, source_target_pairs={{0,24},{1,25},{2,26},{3,27},{4,28},{5,29},{6,30},{7,31},{8,16},{9,... | collective-permute-start | bytes 98312 | tf_op jit(solution)/shard_map/ppermute | solution.py:265
  44.0 0.8 %collective-permute-start.14 = (bf16[32,512]{1,0:T(8,128)(2,1)S(1)}, bf16[32,512]{1,0:T(8,128)(2,1)S(1)}, u32[]{:S(2)}, u32[]{:S(2)}) collective-permute-start(bf16[32,512]{1,0:T(8,128)(2,1)S(1)} %get-tuple-element.36), channel_id=1, source_target_pairs={{0,8},{1,9},{2,10},{3,11},{4,12},{5,13},{6,14},{7,15},{8,0},{9,1},... | collective-permute-start | bytes 98312 | tf_op jit(solution)/shard_map/ppermute | solution.py:265
  44.8 1.3 %collective-permute-done.12.refs_1_ = bf16[32,512]{1,0:T(8,128)(2,1)S(1)} collective-permute-done((bf16[32,512]{1,0:T(8,128)(2,1)S(1)}, bf16[32,512]{1,0:T(8,128)(2,1)S(1)}, u32[]{:S(2)}, u32[]{:S(2)}) %collective-permute-start.12) | collective-permute-done | bytes 32800 | tf_op jit(solution)/shard_map/ppermute | solution.py:265
  46.2 2.7 %collective-permute-done.13.refs_2_ = bf16[32,512]{1,0:T(8,128)(2,1)S(1)} collective-permute-done((bf16[32,512]{1,0:T(8,128)(2,1)S(1)}, bf16[32,512]{1,0:T(8,128)(2,1)S(1)}, u32[]{:S(2)}, u32[]{:S(2)}) %collective-permute-start.13) | collective-permute-done | bytes 32800 | tf_op jit(solution)/shard_map/ppermute | solution.py:265
  48.9 0.9 %finish.1 = bf16[32,512]{1,0:T(8,128)(2,1)} custom-call(bf16[32,512]{1,0:T(8,128)(2,1)S(1)} %copy-done.4, f32[1,512]{1,0:T(1,128)S(1)} %bitcast.2, bf16[512,512]{1,0:T(8,128)(2,1)S(1)} %copy-done.2, f32[32,512]{1,0:T(8,128)S(1)} %get-tuple-element.33.refs_0_, bf16[32,512]{1,0:T(8,128)(2,1)S(1)} %collective-permute-done.12.refs_1_, ...), custom_call_target="tpu_custom_call" | custom-call | tf_op jit(solution)/shard_map/finish/pallas_call | solution.py:235
  (31 shorter events, 0.1 us)
Async XLA Ops:
  0.0 15.9 %collective-permute-start.2 = (bf16[32,512]{1,0:T(8,128)(2,1)}, bf16[32,512]{1,0:T(8,128)(2,1)S(1)}, u32[]{:S(2)}, u32[]{:S(2)}) collective-permute-start(bf16[32,512]{1,0:T(8,128)(2,1)} %feat.1), channel_id=1, source_target_pairs={{0,17},{1,16},{2,19},{3,18},{4,21},{5,20},{6,23},{7,22},{8,25},{9,... | collective-permute-start | bytes 98312 | tf_op jit(solution)/shard_map/ppermute | solution.py:265
  3.5 12.4 %collective-permute-start.1 = (bf16[32,512]{1,0:T(8,128)(2,1)}, bf16[32,512]{1,0:T(8,128)(2,1)S(1)}, u32[]{:S(2)}, u32[]{:S(2)}) collective-permute-start(bf16[32,512]{1,0:T(8,128)(2,1)} %feat.1), channel_id=1, source_target_pairs={{0,9},{1,8},{2,11},{3,10},{4,13},{5,12},{6,15},{7,14},{8,1},{9,0},... | collective-permute-start | bytes 98312 | tf_op jit(solution)/shard_map/ppermute | solution.py:265
  5.3 10.6 %collective-permute-start = (bf16[32,512]{1,0:T(8,128)(2,1)}, bf16[32,512]{1,0:T(8,128)(2,1)S(1)}, u32[]{:S(2)}, u32[]{:S(2)}) collective-permute-start(bf16[32,512]{1,0:T(8,128)(2,1)} %feat.1), channel_id=1, source_target_pairs={{0,1},{1,0},{2,3},{3,2},{4,5},{5,4},{6,7},{7,6},{8,9},{9,8},{10,11... | collective-permute-start | bytes 98312 | tf_op jit(solution)/shard_map/ppermute | solution.py:265
  5.3 10.6 %collective-permute-start.3 = (bf16[32,512]{1,0:T(8,128)(2,1)}, bf16[32,512]{1,0:T(8,128)(2,1)S(1)}, u32[]{:S(2)}, u32[]{:S(2)}) collective-permute-start(bf16[32,512]{1,0:T(8,128)(2,1)} %feat.1), channel_id=1, source_target_pairs={{0,25},{1,24},{2,27},{3,26},{4,29},{5,28},{6,31},{7,30},{8,17},{9,... | collective-permute-start | bytes 98312 | tf_op jit(solution)/shard_map/ppermute | solution.py:265
  5.3 2.2 %copy-start = (bf16[4096,512]{1,0:T(8,128)(2,1)S(1)}, bf16[4096,512]{1,0:T(8,128)(2,1)}, u32[]{:S(2)}) copy-start(bf16[4096,512]{1,0:T(8,128)(2,1)} %acct.1) | copy-start | bytes 12582916
  7.5 0.7 %copy-start.5 = (s32[32,128]{1,0:T(8,128)S(1)}, s32[32,128]{1,0:T(8,128)}, u32[]{:S(2)}) copy-start(s32[32,128]{1,0:T(8,128)} %slots_ref.1) | copy-start | bytes 49156
  8.2 11.3 %copy-start.7 = (s32[32]{0:T(128)S(1)}, s32[32]{0:T(128)}, u32[]{:S(2)}) copy-start(s32[32]{0:T(128)} %rel_ref.5) | copy-start | bytes 388
  8.2 11.3 %copy-start.10 = (bf16[4,512,512]{2,1,0:T(8,128)(2,1)S(1)}, bf16[4,512,512]{2,1,0:T(8,128)(2,1)}, u32[]{:S(2)}) copy-start(bf16[4,512,512]{2,1,0:T(8,128)(2,1)} %kw.1) | copy-start | bytes 6291460
  8.3 11.3 %copy-start.11 = (bf16[4,512,512]{2,1,0:T(8,128)(2,1)S(1)}, bf16[4,512,512]{2,1,0:T(8,128)(2,1)}, u32[]{:S(2)}) copy-start(bf16[4,512,512]{2,1,0:T(8,128)(2,1)} %mw.1) | copy-start | bytes 6291460
  16.0 10.5 %collective-permute-start.6 = (bf16[128,512]{1,0:T(8,128)(2,1)S(1)}, bf16[128,512]{1,0:T(8,128)(2,1)S(1)}, u32[]{:S(2)}, u32[]{:S(2)}) collective-permute-start(bf16[128,512]{1,0:T(8,128)(2,1)S(1)} %pad_maximum_fusion.1), channel_id=1, source_target_pairs={{0,6},{1,7},{2,4},{3,5},{4,2},{5,3},{6,0},{7,1},{8,14},{9,15},{10,... | collective-permute-start | bytes 393224 | tf_op jit(solution)/shard_map/ppermute | solution.py:265
  18.8 7.7 %collective-permute-start.5 = (bf16[128,512]{1,0:T(8,128)(2,1)S(1)}, bf16[128,512]{1,0:T(8,128)(2,1)S(1)}, u32[]{:S(2)}, u32[]{:S(2)}) collective-permute-start(bf16[128,512]{1,0:T(8,128)(2,1)S(1)} %pad_maximum_fusion.1), channel_id=1, source_target_pairs={{0,4},{1,5},{2,6},{3,7},{4,0},{5,1},{6,2},{7,3},{8,12},{9,13},{10,... | collective-permute-start | bytes 393224 | tf_op jit(solution)/shard_map/ppermute | solution.py:265
  19.3 7.2 %collective-permute-start.4 = (bf16[128,512]{1,0:T(8,128)(2,1)S(1)}, bf16[128,512]{1,0:T(8,128)(2,1)S(1)}, u32[]{:S(2)}, u32[]{:S(2)}) collective-permute-start(bf16[128,512]{1,0:T(8,128)(2,1)S(1)} %pad_maximum_fusion.1), channel_id=1, source_target_pairs={{0,2},{1,3},{2,0},{3,1},{4,6},{5,7},{6,4},{7,5},{8,10},{9,11},{10,... | collective-permute-start | bytes 393224 | tf_op jit(solution)/shard_map/ppermute | solution.py:265
  19.5 7.1 %copy-start.1 = (bf16[512,512]{1,0:T(8,128)(2,1)S(1)}, bf16[512,512]{1,0:T(8,128)(2,1)}, u32[]{:S(2)}) copy-start(bf16[512,512]{1,0:T(8,128)(2,1)} %wq.3) | copy-start | bytes 1572868
  19.5 7.1 %copy-start.3 = (s32[32,128]{1,0:T(8,128)S(1)}, s32[32,128]{1,0:T(8,128)}, u32[]{:S(2)}) copy-start(s32[32,128]{1,0:T(8,128)} %merch_slot.3) | copy-start | bytes 49156
  19.5 7.1 %copy-start.8 = (s32[32]{0:T(128)S(1)}, s32[32]{0:T(128)}, u32[]{:S(2)}) copy-start(s32[32]{0:T(128)} %count_ref.3) | copy-start | bytes 388
  19.6 7.1 %copy-start.9 = (f32[4]{0:T(128)S(1)}, f32[4]{0:T(128)}, u32[]{:S(2)}) copy-start(f32[4]{0:T(128)} %bias_ref.3) | copy-start | bytes 52
  26.5 2.2 %collective-permute-start.7 = (bf16[512,512]{1,0:T(8,128)(2,1)S(1)}, bf16[512,512]{1,0:T(8,128)(2,1)S(1)}, u32[]{:S(2)}, u32[]{:S(2)}) collective-permute-start(bf16[512,512]{1,0:T(8,128)(2,1)S(1)} %pad_maximum_fusion.feats), channel_id=1, source_target_pairs={{0,1},{1,0},{2,3},{3,2},{4,5},{5,4},{6,7},{7,6},{8,9},{9,8},{10,11... | collective-permute-start | bytes 1572872 | tf_op jit(solution)/shard_map/ppermute | solution.py:265
  28.2 2.1 %collective-permute-start.8 = (bf16[512,512]{1,0:T(8,128)(2,1)S(1)}, bf16[512,512]{1,0:T(8,128)(2,1)S(1)}, u32[]{:S(2)}, u32[]{:S(2)}) collective-permute-start(bf16[512,512]{1,0:T(8,128)(2,1)S(1)} %aggregate_odd.1), channel_id=1, source_target_pairs={{0,1},{1,0},{2,3},{3,2},{4,5},{5,4},{6,7},{7,6},{8,9},{9,8},{10,11... | collective-permute-start | bytes 1572872 | tf_op jit(solution)/shard_map/ppermute | solution.py:265
  30.3 18.6 %copy-start.2 = (bf16[512,512]{1,0:T(8,128)(2,1)S(1)}, bf16[512,512]{1,0:T(8,128)(2,1)}, u32[]{:S(2)}) copy-start(bf16[512,512]{1,0:T(8,128)(2,1)} %wo.1) | copy-start | bytes 1572868
  30.3 18.6 %copy-start.4 = (bf16[32,512]{1,0:T(8,128)(2,1)S(1)}, bf16[32,512]{1,0:T(8,128)(2,1)}, u32[]{:S(2)}) copy-start(bf16[32,512]{1,0:T(8,128)(2,1)} %feat.1) | copy-start | bytes 98308
  30.3 18.6 %copy-start.6 = (f32[512]{0:T(512)S(1)}, f32[512]{0:T(512)}, u32[]{:S(2)}) copy-start(f32[512]{0:T(512)} %param.19) | copy-start | bytes 6148
  30.4 6.9 %collective-permute-start.9 = (bf16[128,512]{1,0:T(8,128)(2,1)S(1)}, bf16[128,512]{1,0:T(8,128)(2,1)S(1)}, u32[]{:S(2)}, u32[]{:S(2)}) collective-permute-start(bf16[128,512]{1,0:T(8,128)(2,1)S(1)} %get-tuple-element.30), channel_id=1, source_target_pairs={{0,6},{1,7},{2,4},{3,5},{4,2},{5,3},{6,0},{7,1},{8,14},{9,15},{10,... | collective-permute-start | bytes 393224 | tf_op jit(solution)/shard_map/ppermute | solution.py:265
  33.2 6.8 %collective-permute-start.10 = (bf16[128,512]{1,0:T(8,128)(2,1)S(1)}, bf16[128,512]{1,0:T(8,128)(2,1)S(1)}, u32[]{:S(2)}, u32[]{:S(2)}) collective-permute-start(bf16[128,512]{1,0:T(8,128)(2,1)S(1)} %get-tuple-element.31), channel_id=1, source_target_pairs={{0,4},{1,5},{2,6},{3,7},{4,0},{5,1},{6,2},{7,3},{8,12},{9,13},{10,... | collective-permute-start | bytes 393224 | tf_op jit(solution)/shard_map/ppermute | solution.py:265
  33.7 6.6 %collective-permute-start.11 = (bf16[128,512]{1,0:T(8,128)(2,1)S(1)}, bf16[128,512]{1,0:T(8,128)(2,1)S(1)}, u32[]{:S(2)}, u32[]{:S(2)}) collective-permute-start(bf16[128,512]{1,0:T(8,128)(2,1)S(1)} %get-tuple-element.32), channel_id=1, source_target_pairs={{0,2},{1,3},{2,0},{3,1},{4,6},{5,7},{6,4},{7,5},{8,10},{9,11},{10,... | collective-permute-start | bytes 393224 | tf_op jit(solution)/shard_map/ppermute | solution.py:265
  40.4 5.8 %collective-permute-start.12 = (bf16[32,512]{1,0:T(8,128)(2,1)S(1)}, bf16[32,512]{1,0:T(8,128)(2,1)S(1)}, u32[]{:S(2)}, u32[]{:S(2)}) collective-permute-start(bf16[32,512]{1,0:T(8,128)(2,1)S(1)} %get-tuple-element.34), channel_id=1, source_target_pairs={{0,24},{1,25},{2,26},{3,27},{4,28},{5,29},{6,30},{7,31},{8,16},{9,... | collective-permute-start | bytes 98312 | tf_op jit(solution)/shard_map/ppermute | solution.py:265
  44.0 4.8 %collective-permute-start.13 = (bf16[32,512]{1,0:T(8,128)(2,1)S(1)}, bf16[32,512]{1,0:T(8,128)(2,1)S(1)}, u32[]{:S(2)}, u32[]{:S(2)}) collective-permute-start(bf16[32,512]{1,0:T(8,128)(2,1)S(1)} %get-tuple-element.35), channel_id=1, source_target_pairs={{0,16},{1,17},{2,18},{3,19},{4,20},{5,21},{6,22},{7,23},{8,24},{9,... | collective-permute-start | bytes 98312 | tf_op jit(solution)/shard_map/ppermute | solution.py:265
  44.0 4.8 %collective-permute-start.14 = (bf16[32,512]{1,0:T(8,128)(2,1)S(1)}, bf16[32,512]{1,0:T(8,128)(2,1)S(1)}, u32[]{:S(2)}, u32[]{:S(2)}) collective-permute-start(bf16[32,512]{1,0:T(8,128)(2,1)S(1)} %get-tuple-element.36), channel_id=1, source_target_pairs={{0,8},{1,9},{2,10},{3,11},{4,12},{5,13},{6,14},{7,15},{8,0},{9,1},... | collective-permute-start | bytes 98312 | tf_op jit(solution)/shard_map/ppermute | solution.py:265

commit v4 on v3

--- a/solution.py
+++ b/solution.py
@@ -13,6 +13,7 @@
 F32 = jnp.float32
 BF16 = jnp.bfloat16
 SMEM = pl.BlockSpec(memory_space=pltpu.SMEM)
+ANY = pl.BlockSpec(memory_space=pl.ANY)
 VMEM = pl.BlockSpec(memory_space=pltpu.VMEM)
 
 
@@ -30,95 +31,137 @@
     return (i // outer) * 2 + (i % outer) * 8
 
 
-def gather_kernel(outer, me_ref, slots_ref, acct, odd, even, table, rows0, rows1):
+def _project(feats, relation, kw, mw, i, keys, values):
+    width = feats.shape[1]
+    half = width // 2
+    for n in range(0, width, half):
+        key = jnp.dot(feats[...], kw[relation, :, n : n + half], preferred_element_type=F32)
+        keys[i, n : n + half, :] = key.astype(BF16).T
+        value = jnp.dot(feats[...], mw[relation, :, n : n + half], preferred_element_type=F32)
+        values[i, :, n : n + half] = value.astype(BF16)
+
+
+def gather_kernel(
+    outer, me_ref, rel_ref, slots_ref, acct_hbm, kw_hbm, mw_hbm,
+    keys, values, even,
+    kw, mw, acct, table, odd_rows, even_rows, odd_feats, a_sem, w_sem,
+):
     accounts, width = acct.shape
-    blocks, block_len, _ = odd.shape
+    blocks, block_len, _ = even.shape
     parts = width // LANES
     pitch = table.shape[1]
     flat = table.reshape(accounts * pitch, LANES)
     me = me_ref[0]
-
-    @pl.loop(0, accounts // 16, unroll=4)
-    def _(g):
-        first = pl.multiple_of(g * 16, 16)
-        tile = acct[pl.ds(first, 16), :].astype(F32)
+    chunks = a_sem.shape[0]
+    chunk = accounts // chunks
+    acct_copies = [
+        pltpu.make_async_copy(
+            acct_hbm.at[pl.ds(i * chunk, chunk)], acct.at[pl.ds(i * chunk, chunk)], a_sem.at[i]
+        )
+        for i in range(chunks)
+    ]
+    weight_copies = [
+        pltpu.make_async_copy(kw_hbm, kw, w_sem.at[0]),
+        pltpu.make_async_copy(mw_hbm, mw, w_sem.at[1]),
+    ]
+    for copy in acct_copies + weight_copies:
+        copy.start()
+    for i in range(chunks):
+        acct_copies[i].wait()
+
+        @pl.loop(0, chunk // 16, unroll=4)
+        def _(g):
+            first = pl.multiple_of(i * chunk + g * 16, 16)
+            tile = acct[pl.ds(first, 16), :].astype(F32)
+            for c in range(parts):
+                flat[pl.ds(first * pitch + c, 16, stride=pitch), :] = tile[
+                    :, c * LANES : (c + 1) * LANES
+                ]
+
+    def collect(block, rows):
+        for k in range(0, block_len, 16):
+            found = [table[slots_ref[block, k + u], :parts, :] for u in range(16)]
+            for u in range(16):
+                rows[(k + u) * parts : (k + u + 1) * parts, :] = found[u]
+
+    def emit(rows, out):
         for c in range(parts):
-            flat[pl.ds(first * pitch + c, 16, stride=pitch), :] = tile[
-                :, c * LANES : (c + 1) * LANES
-            ]
-
-    def collect(block, rows):
-        for k in range(block_len):
-            rows[k * parts : (k + 1) * parts, :] = table[slots_ref[block, k], :parts, :]
-
-    def emit(i, rows, out):
-        for c in range(parts):
-            out[i, :, c * LANES : (c + 1) * LANES] = rows[
+            out[:, c * LANES : (c + 1) * LANES] = rows[
                 pl.ds(c, block_len, stride=parts), :
             ].astype(BF16)
 
+    collect(jnp.bitwise_xor(me, 1), odd_rows)
+    for copy in weight_copies:
+        copy.wait()
+
     @pl.loop(0, blocks)
     def _(i):
+        emit(odd_rows, odd_feats)
+        ahead = _offset(jnp.minimum(i + 1, blocks - 1), outer) + 1
+        collect(jnp.bitwise_xor(me, ahead), odd_rows)
         offset = _offset(i, outer)
-        collect(jnp.bitwise_xor(me, offset + 1), rows0)
-        collect(jnp.bitwise_xor(me, offset), rows1)
-        emit(i, rows0, odd)
-        emit(i, rows1, even)
-
-
-def gather(outer, me, slots, acct):
+        collect(jnp.bitwise_xor(me, offset), even_rows)
+        relation = rel_ref[jnp.bitwise_xor(me, offset + 1)]
+        _project(odd_feats, relation, kw, mw, i, keys, values)
+        emit(even_rows, even.at[i])
+
+
+def gather(outer, me, rel, slots, acct, kw, mw):
     blocks, block_len = slots.shape
     accounts, width = acct.shape
     parts = width // LANES
     rows = pltpu.VMEM((block_len * parts, LANES), F32)
-    half = jax.ShapeDtypeStruct((blocks // 2, block_len, width), BF16)
+    half = blocks // 2
     return pl.pallas_call(
         functools.partial(gather_kernel, outer),
-        out_shape=(half, half),
-        in_specs=[SMEM, SMEM, VMEM],
+        out_shape=(
+            jax.ShapeDtypeStruct((half, width, block_len), BF16),
+            jax.ShapeDtypeStruct((half, block_len, width), BF16),
+            jax.ShapeDtypeStruct((half, block_len, width), BF16),
+        ),
+        in_specs=[SMEM] * 3 + [ANY] * 3,
+        out_specs=(VMEM,) * 3,
+        scratch_shapes=[
+            pltpu.VMEM(kw.shape, BF16),
+            pltpu.VMEM(mw.shape, BF16),
+            pltpu.VMEM(acct.shape, BF16),
+            pltpu.VMEM((accounts, -(-parts // 8) * 8, LANES), F32),
+            rows,
+            rows,
+            pltpu.VMEM((block_len, width), BF16),
+            pltpu.SemaphoreType.DMA((8,)),
+            pltpu.SemaphoreType.DMA((2,)),
+        ],
+        compiler_params=_mb(47 if blocks <= 32 else 50),
+        cost_estimate=_cost(4 * half * block_len * width * width, 20 * 2**20),
+        name="gather_slots",
+    )(me, rel, slots, acct, kw, mw)
+
+
+def project_kernel(outer, me_ref, rel_ref, feats, kw, mw, keys, values):
+    blocks = feats.shape[0]
+    me = me_ref[0]
+
+    @pl.loop(0, blocks, unroll=4)
+    def _(i):
+        relation = rel_ref[jnp.bitwise_xor(me, _offset(i, outer))]
+        _project(feats.at[i], relation, kw, mw, i, keys, values)
+
+
+def project(outer, me, rel, feats, kw, mw):
+    blocks, block_len, width = feats.shape
+    return pl.pallas_call(
+        functools.partial(project_kernel, outer),
+        out_shape=(
+            jax.ShapeDtypeStruct((blocks, width, block_len), BF16),
+            jax.ShapeDtypeStruct((blocks, block_len, width), BF16),
+        ),
+        in_specs=[SMEM, SMEM] + [VMEM] * 3,
         out_specs=(VMEM, VMEM),
-        scratch_shapes=[pltpu.VMEM((accounts, -(-parts // 8) * 8, LANES), F32), rows, rows],
-        compiler_params=_mb(20),
-        cost_estimate=_cost(0, 20 * 2**20),
-        name="gather_slots",
-    )(me, slots, acct)
-
-
-def project_kernel(outer, shifts, me_ref, rel_ref, kw, mw, *refs):
-    halves = len(shifts)
-    blocks, _, width = refs[0].shape
-    half = width // 2
-    me = me_ref[0]
-
-    def one(i, shift, feats, keys, values):
-        relation = rel_ref[jnp.bitwise_xor(me, _offset(i, outer) + shift)]
-        for n in range(0, width, half):
-            key = jnp.dot(feats[i], kw[relation, :, n : n + half], preferred_element_type=F32)
-            keys[i, n : n + half, :] = key.astype(BF16).T
-            value = jnp.dot(feats[i], mw[relation, :, n : n + half], preferred_element_type=F32)
-            values[i, :, n : n + half] = value.astype(BF16)
-
-    @pl.loop(0, blocks, unroll=2)
-    def _(i):
-        for h, shift in enumerate(shifts):
-            one(i, shift, refs[h], refs[halves + 2 * h], refs[halves + 2 * h + 1])
-
-
-def project(outer, shifts, me, rel, feats, kw, mw):
-    blocks, block_len, width = feats[0].shape
-    keys = jax.ShapeDtypeStruct((blocks, width, block_len), BF16)
-    values = jax.ShapeDtypeStruct((blocks, block_len, width), BF16)
-    return pl.pallas_call(
-        functools.partial(project_kernel, outer, shifts),
-        out_shape=(keys, values) * len(shifts),
-        in_specs=[SMEM, SMEM] + [VMEM] * (2 + len(shifts)),
-        out_specs=(VMEM, VMEM) * len(shifts),
         compiler_params=_mb(4),
-        cost_estimate=_cost(
-            4 * len(shifts) * blocks * block_len * width * width, 8 * len(shifts) * 2**20
-        ),
-        name="project_slots",
-    )(me, rel, kw, mw, *feats)
+        cost_estimate=_cost(4 * blocks * block_len * width * width, 8 * 2**20),
+        name="project_even",
+    )(me, rel, feats, kw, mw)
 
 
 def aggregate_kernel(
@@ -268,20 +311,12 @@
         return lax.optimization_barrier((value,) + others)[0]
 
     feats = jnp.concatenate([swap(merch_feat, 8 * k + 1) for k in range(outer)], axis=0)
-    odd_rows, even_rows = gather(outer, me, slot_acct, acct_feat)
-    feats = after(feats, odd_rows)
+    odd_keys, odd_values, even_rows = gather(
+        outer, me, block_rel, slot_acct, acct_feat, key_weight, msg_weight
+    )
+    feats = after(feats, even_rows)
     feats = jnp.concatenate([feats] + [swap(feats, 2 * j) for j in range(1, inner)], axis=0)
-    rows = (odd_rows, even_rows)
-    weights = (key_weight, msg_weight)
-    if devices <= 32:
-        projected = project(outer, (1, 0), me, block_rel, rows, *weights)
-    else:
-        projected = [
-            out
-            for shift, feat in zip((1, 0), rows)
-            for out in project(outer, (shift,), me, block_rel, (feat,), *weights)
-        ]
-    odd_keys, odd_values, even_keys, even_values = projected
+    even_keys, even_values = project(outer, me, block_rel, even_rows, key_weight, msg_weight)
     feats = after(feats, even_keys)
 
     shared = (me, block_rel, block_count, rel_bias, slot_merch)

time: 50 us -> 52.9 us (1.058)
  Pallas kernels: 18.6 us -> 21.1 us
  waiting for transfers between devices: 10.4 us -> 12.3 us
  local copies, waits for them, and re-layouts: 2.95 us -> 1.42 us
    pallas_call x2, Pallas kernels: 14.5 us -> 17 us  [the longest x1 13.3 us: gather(): pl.pallas_call(functools.partial(gather_kernel, outer), out_shape=(jax.Sh...]
    ppermute x15, waiting for transfers between devices: 10.4 us -> 12.3 us  [swap(): return lax.ppermute(value, AXES, [(s, s ^ mask) for s in range(devices)])]
    unnamed x24 -> x22, local copies, waits for them, and re-layouts: 2.95 us -> 1.42 us
  transfers between devices with their start and end apart: 15 -> 15, of which waited for: 5 -> 6; matrix products, arithmetic and copies ran while one was open for 0% -> 0% of each run, Pallas kernels for 35% -> 38%
where the time goes in v4:
time: 52.9 us; the launch traced here: 52.6 us
  Pallas kernels  21.1 us (40%)
  starting transfers between devices  17.5 us (33%)
  waiting for transfers between devices  12.3 us (23%)
  local copies, waits for them, and re-layouts  1.42 us (3%)
    ppermute x15, starting transfers between devices, swap(): return lax.ppermute(value, AXES, [(s, s ^ mask) for s in range(devices)])  17.5 us
    pallas_call x1, Pallas kernels, gather(): pl.pallas_call(functools.partial(gather_kernel, outer), out_shape=(jax.Sh...  13.3 us
    ppermute x15, waiting for transfers between devices, swap(): return lax.ppermute(value, AXES, [(s, s ^ mask) for s in range(devices)])  12.3 us
    pallas_call x1, Pallas kernels, project(): pl.pallas_call(functools.partial(project_kernel, outer), out_shape=(jax.S...  3.67 us
    pallas_call x2, Pallas kernels, aggregate(): pl.pallas_call(functools.partial(aggregate_kernel, outer, shift), out_sha...  3.07 us
    unnamed x22, local copies, waits for them, and re-layouts  1.42 us
  transfers between devices with their start and end apart: 15, of which 6 were waited for; matrix products, arithmetic and copies ran while one was open for 0% of the time, Pallas kernels for 38%

profile of v4, /device:TPU:0, one launch (start us, length us, event | category | flops | bytes accessed | tf_op | source)
XLA Modules:
  0.0 52.6 jit_solution(12326876116006026813)
XLA Ops:
  0.0 3.5 %collective-permute-start.2 = (bf16[32,512]{1,0:T(8,128)(2,1)}, bf16[32,512]{1,0:T(8,128)(2,1)S(1)}, u32[]{:S(2)}, u32[]{:S(2)}) collective-permute-start(bf16[32,512]{1,0:T(8,128)(2,1)} %feat.1), channel_id=1, source_target_pairs={{0,17},{1,16},{2,19},{3,18},{4,21},{5,20},{6,23},{7,22},{8,25},{9,... | collective-permute-start | bytes 98312 | tf_op jit(solution)/shard_map/ppermute | solution.py:308
  3.5 1.9 %collective-permute-start.1 = (bf16[32,512]{1,0:T(8,128)(2,1)}, bf16[32,512]{1,0:T(8,128)(2,1)S(1)}, u32[]{:S(2)}, u32[]{:S(2)}) collective-permute-start(bf16[32,512]{1,0:T(8,128)(2,1)} %feat.1), channel_id=1, source_target_pairs={{0,9},{1,8},{2,11},{3,10},{4,13},{5,12},{6,15},{7,14},{8,1},{9,0},... | collective-permute-start | bytes 98312 | tf_op jit(solution)/shard_map/ppermute | solution.py:308
  5.3 0.7 %copy-done.6 = s32[32,128]{1,0:T(8,128)S(1)} copy-done((s32[32,128]{1,0:T(8,128)S(1)}, s32[32,128]{1,0:T(8,128)}, u32[]{:S(2)}) %copy-start.6) | copy-done | bytes 16408
  6.1 0.7 %copy-done.7 = s32[32]{0:T(128)S(1)} copy-done((s32[32]{0:T(128)S(1)}, s32[32]{0:T(128)}, u32[]{:S(2)}) %copy-start.7) | copy-done | bytes 152
  6.7 13.3 %gather_slots.1 = (bf16[16,512,128]{2,1,0:T(8,128)(2,1)S(1)}, bf16[16,128,512]{2,1,0:T(8,128)(2,1)S(1)}, bf16[16,128,512]{2,1,0:T(8,128)(2,1)S(1)}) custom-call(s32[1]{0:T(128)} %bitcast.1.me_ref, s32[32]{0:T(128)S(1)} %copy-done.7, s32[32,128]{1,0:T(8,128)S(1)} %copy-done.6, bf16[4096,512]{1,0:T(8,128)(2,1)} %acct_hbm.1, bf16[4,512,512]{2,1,0:T(8,128)(2,1)} %kw.1, ...), custom_call_target="tpu_custom_call" | custom-call | flops 2147483648 | bytes 20971520 | tf_op jit(solution)/shard_map/gather_slots/pallas_call | solution.py:115
  20.1 0.0 copy-start.2
  20.1 0.0 copy-start.4
  20.1 0.0 copy-start.9
  20.1 0.0 copy-start.10
  20.1 2.9 %collective-permute-start.6 = (bf16[128,512]{1,0:T(8,128)(2,1)S(1)}, bf16[128,512]{1,0:T(8,128)(2,1)S(1)}, u32[]{:S(2)}, u32[]{:S(2)}) collective-permute-start(bf16[128,512]{1,0:T(8,128)(2,1)S(1)} %pad_maximum_fusion.1), channel_id=1, source_target_pairs={{0,6},{1,7},{2,4},{3,5},{4,2},{5,3},{6,0},{7,1},{8,14},{9,15},{10,... | collective-permute-start | bytes 393224 | tf_op jit(solution)/shard_map/ppermute | solution.py:308
  23.0 0.5 collective-permute-start.5
  23.5 0.2 collective-permute-start.4
  23.7 3.7 %project_even.1 = (bf16[16,512,128]{2,1,0:T(8,128)(2,1)S(1)}, bf16[16,128,512]{2,1,0:T(8,128)(2,1)S(1)}) custom-call(s32[1]{0:T(128)} %bitcast.1.me_ref, s32[32]{0:T(128)S(1)} %copy-done.7, bf16[16,128,512]{2,1,0:T(8,128)(2,1)S(1)} %get-tuple-element.20.feats, bf16[4,512,512]{2,1,0:T(8,128)(2,1)S(1)} %copy-done, bf16[4,512,512]{2,1,0:T(8,128)(2,1)S(1)} %copy-done.1), custom_call_target="tpu_custom_call" | custom-call | flops 2147483648 | bytes 8388608 | tf_op jit(solution)/shard_map/project_even/pallas_call | solution.py:153
  27.4 2.4 %collective-permute-done.5 = bf16[128,512]{1,0:T(8,128)(2,1)S(1)} collective-permute-done((bf16[128,512]{1,0:T(8,128)(2,1)S(1)}, bf16[128,512]{1,0:T(8,128)(2,1)S(1)}, u32[]{:S(2)}, u32[]{:S(2)}) %collective-permute-start.5) | collective-permute-done | bytes 131104 | tf_op jit(solution)/shard_map/ppermute | solution.py:308
  29.8 0.1 collective-permute-done.4
  29.9 0.1 collective-permute-start.7
  30.1 1.5 %aggregate_odd.1 = bf16[512,512]{1,0:T(8,128)(2,1)S(1)} custom-call(s32[1]{0:T(128)} %bitcast.1.me_ref, s32[32]{0:T(128)S(1)} %copy-done.7, s32[32]{0:T(128)S(1)} %copy-done.9, f32[4]{0:T(128)S(1)} %copy-done.10, s32[32,128]{1,0:T(8,128)S(1)} %copy-done.4, bf16[512,512]{1,0:T(8,128)(2,1)S(1)} %pad_maximum_fusion.feats, bf16[512,512]{1,0:T(8,128)(2,1)S(1)} %copy-done.2, ...), custom_call_target="tpu_custom_call" | custom-call | flops 402653184 | bytes 6291456 | tf_op jit(solution)/shard_map/aggregate_odd/pallas_call | solution.py:196
  31.6 0.5 %collective-permute-start.8 = (bf16[512,512]{1,0:T(8,128)(2,1)S(1)}, bf16[512,512]{1,0:T(8,128)(2,1)S(1)}, u32[]{:S(2)}, u32[]{:S(2)}) collective-permute-start(bf16[512,512]{1,0:T(8,128)(2,1)S(1)} %aggregate_odd.1), channel_id=1, source_target_pairs={{0,1},{1,0},{2,3},{3,2},{4,5},{5,4},{6,7},{7,6},{8,9},{9,8},{10,11... | collective-permute-start | bytes 1572872 | tf_op jit(solution)/shard_map/ppermute | solution.py:308
  32.1 1.5 %aggregate_even.1.mine = f32[512,512]{1,0:T(8,128)S(1)} custom-call(s32[1]{0:T(128)} %bitcast.1.me_ref, s32[32]{0:T(128)S(1)} %copy-done.7, s32[32]{0:T(128)S(1)} %copy-done.9, f32[4]{0:T(128)S(1)} %copy-done.10, s32[32,128]{1,0:T(8,128)S(1)} %copy-done.4, bf16[512,512]{1,0:T(8,128)(2,1)S(1)} %collective-permute-done.7.feats, ...), custom_call_target="tpu_custom_call" | custom-call | flops 402653184 | bytes 6291456 | tf_op jit(solution)/shard_map/aggregate_even/pallas_call | solution.py:196
  33.7 0.1 combine_cores.1
  33.8 1.7 %collective-permute-start.9 = (bf16[128,512]{1,0:T(8,128)(2,1)S(1)}, bf16[128,512]{1,0:T(8,128)(2,1)S(1)}, u32[]{:S(2)}, u32[]{:S(2)}) collective-permute-start(bf16[128,512]{1,0:T(8,128)(2,1)S(1)} %get-tuple-element.28), channel_id=1, source_target_pairs={{0,6},{1,7},{2,4},{3,5},{4,2},{5,3},{6,0},{7,1},{8,14},{9,15},{10,... | collective-permute-start | bytes 393224 | tf_op jit(solution)/shard_map/ppermute | solution.py:308
  35.6 1.3 %collective-permute-start.10 = (bf16[128,512]{1,0:T(8,128)(2,1)S(1)}, bf16[128,512]{1,0:T(8,128)(2,1)S(1)}, u32[]{:S(2)}, u32[]{:S(2)}) collective-permute-start(bf16[128,512]{1,0:T(8,128)(2,1)S(1)} %get-tuple-element.29), channel_id=1, source_target_pairs={{0,4},{1,5},{2,6},{3,7},{4,0},{5,1},{6,2},{7,3},{8,12},{9,13},{10,... | collective-permute-start | bytes 393224 | tf_op jit(solution)/shard_map/ppermute | solution.py:308
  36.9 0.5 collective-permute-start.11
  37.4 3.7 %collective-permute-done.9.refs_1_ = bf16[128,512]{1,0:T(8,128)(2,1)S(1)} collective-permute-done((bf16[128,512]{1,0:T(8,128)(2,1)S(1)}, bf16[128,512]{1,0:T(8,128)(2,1)S(1)}, u32[]{:S(2)}, u32[]{:S(2)}) %collective-permute-start.9) | collective-permute-done | bytes 131104 | tf_op jit(solution)/shard_map/ppermute | solution.py:308
  41.1 2.2 %collective-permute-done.10.refs_2_ = bf16[128,512]{1,0:T(8,128)(2,1)S(1)} collective-permute-done((bf16[128,512]{1,0:T(8,128)(2,1)S(1)}, bf16[128,512]{1,0:T(8,128)(2,1)S(1)}, u32[]{:S(2)}, u32[]{:S(2)}) %collective-permute-start.10) | collective-permute-done | bytes 131104 | tf_op jit(solution)/shard_map/ppermute | solution.py:308
  43.3 0.0 collective-permute-done.11.refs_3_
  43.3 0.1 combine_plane.1
  43.4 3.5 %collective-permute-start.12 = (bf16[32,512]{1,0:T(8,128)(2,1)S(1)}, bf16[32,512]{1,0:T(8,128)(2,1)S(1)}, u32[]{:S(2)}, u32[]{:S(2)}) collective-permute-start(bf16[32,512]{1,0:T(8,128)(2,1)S(1)} %get-tuple-element.32), channel_id=1, source_target_pairs={{0,24},{1,25},{2,26},{3,27},{4,28},{5,29},{6,30},{7,31},{8,16},{9,... | collective-permute-start | bytes 98312 | tf_op jit(solution)/shard_map/ppermute | solution.py:308
  46.9 1.0 %collective-permute-start.14 = (bf16[32,512]{1,0:T(8,128)(2,1)S(1)}, bf16[32,512]{1,0:T(8,128)(2,1)S(1)}, u32[]{:S(2)}, u32[]{:S(2)}) collective-permute-start(bf16[32,512]{1,0:T(8,128)(2,1)S(1)} %get-tuple-element.34), channel_id=1, source_target_pairs={{0,8},{1,9},{2,10},{3,11},{4,12},{5,13},{6,14},{7,15},{8,0},{9,1},... | collective-permute-start | bytes 98312 | tf_op jit(solution)/shard_map/ppermute | solution.py:308
  47.9 1.3 %collective-permute-done.12.refs_1_ = bf16[32,512]{1,0:T(8,128)(2,1)S(1)} collective-permute-done((bf16[32,512]{1,0:T(8,128)(2,1)S(1)}, bf16[32,512]{1,0:T(8,128)(2,1)S(1)}, u32[]{:S(2)}, u32[]{:S(2)}) %collective-permute-start.12) | collective-permute-done | bytes 32800 | tf_op jit(solution)/shard_map/ppermute | solution.py:308
  49.2 2.5 %collective-permute-done.13.refs_2_ = bf16[32,512]{1,0:T(8,128)(2,1)S(1)} collective-permute-done((bf16[32,512]{1,0:T(8,128)(2,1)S(1)}, bf16[32,512]{1,0:T(8,128)(2,1)S(1)}, u32[]{:S(2)}, u32[]{:S(2)}) %collective-permute-start.13) | collective-permute-done | bytes 32800 | tf_op jit(solution)/shard_map/ppermute | solution.py:308
  51.7 0.9 %finish.1 = bf16[32,512]{1,0:T(8,128)(2,1)} custom-call(bf16[32,512]{1,0:T(8,128)(2,1)S(1)} %copy-done.5, f32[1,512]{1,0:T(1,128)S(1)} %bitcast.2, bf16[512,512]{1,0:T(8,128)(2,1)S(1)} %copy-done.3, f32[32,512]{1,0:T(8,128)S(1)} %get-tuple-element.31.refs_0_, bf16[32,512]{1,0:T(8,128)(2,1)S(1)} %collective-permute-done.12.refs_1_, ...), custom_call_target="tpu_custom_call" | custom-call | tf_op jit(solution)/shard_map/finish/pallas_call | solution.py:278
  (29 shorter events, 0.1 us)
Async XLA Ops:
  0.0 20.0 %collective-permute-start.2 = (bf16[32,512]{1,0:T(8,128)(2,1)}, bf16[32,512]{1,0:T(8,128)(2,1)S(1)}, u32[]{:S(2)}, u32[]{:S(2)}) collective-permute-start(bf16[32,512]{1,0:T(8,128)(2,1)} %feat.1), channel_id=1, source_target_pairs={{0,17},{1,16},{2,19},{3,18},{4,21},{5,20},{6,23},{7,22},{8,25},{9,... | collective-permute-start | bytes 98312 | tf_op jit(solution)/shard_map/ppermute | solution.py:308
  3.5 16.6 %collective-permute-start.1 = (bf16[32,512]{1,0:T(8,128)(2,1)}, bf16[32,512]{1,0:T(8,128)(2,1)S(1)}, u32[]{:S(2)}, u32[]{:S(2)}) collective-permute-start(bf16[32,512]{1,0:T(8,128)(2,1)} %feat.1), channel_id=1, source_target_pairs={{0,9},{1,8},{2,11},{3,10},{4,13},{5,12},{6,15},{7,14},{8,1},{9,0},... | collective-permute-start | bytes 98312 | tf_op jit(solution)/shard_map/ppermute | solution.py:308
  5.3 14.7 %collective-permute-start = (bf16[32,512]{1,0:T(8,128)(2,1)}, bf16[32,512]{1,0:T(8,128)(2,1)S(1)}, u32[]{:S(2)}, u32[]{:S(2)}) collective-permute-start(bf16[32,512]{1,0:T(8,128)(2,1)} %feat.1), channel_id=1, source_target_pairs={{0,1},{1,0},{2,3},{3,2},{4,5},{5,4},{6,7},{7,6},{8,9},{9,8},{10,11... | collective-permute-start | bytes 98312 | tf_op jit(solution)/shard_map/ppermute | solution.py:308
  5.3 14.7 %collective-permute-start.3 = (bf16[32,512]{1,0:T(8,128)(2,1)}, bf16[32,512]{1,0:T(8,128)(2,1)S(1)}, u32[]{:S(2)}, u32[]{:S(2)}) collective-permute-start(bf16[32,512]{1,0:T(8,128)(2,1)} %feat.1), channel_id=1, source_target_pairs={{0,25},{1,24},{2,27},{3,26},{4,29},{5,28},{6,31},{7,30},{8,17},{9,... | collective-permute-start | bytes 98312 | tf_op jit(solution)/shard_map/ppermute | solution.py:308
  5.3 0.7 %copy-start.6 = (s32[32,128]{1,0:T(8,128)S(1)}, s32[32,128]{1,0:T(8,128)}, u32[]{:S(2)}) copy-start(s32[32,128]{1,0:T(8,128)} %slots_ref.1) | copy-start | bytes 49156
  6.1 0.7 %copy-start.7 = (s32[32]{0:T(128)S(1)}, s32[32]{0:T(128)}, u32[]{:S(2)}) copy-start(s32[32]{0:T(128)} %rel_ref.7) | copy-start | bytes 388
  6.7 17.0 %copy-start = (bf16[4,512,512]{2,1,0:T(8,128)(2,1)S(1)}, bf16[4,512,512]{2,1,0:T(8,128)(2,1)}, u32[]{:S(2)}) copy-start(bf16[4,512,512]{2,1,0:T(8,128)(2,1)} %kw.1) | copy-start | bytes 6291460
  6.7 17.0 %copy-start.1 = (bf16[4,512,512]{2,1,0:T(8,128)(2,1)S(1)}, bf16[4,512,512]{2,1,0:T(8,128)(2,1)}, u32[]{:S(2)}) copy-start(bf16[4,512,512]{2,1,0:T(8,128)(2,1)} %mw.1) | copy-start | bytes 6291460
  20.1 9.9 %copy-start.2 = (bf16[512,512]{1,0:T(8,128)(2,1)S(1)}, bf16[512,512]{1,0:T(8,128)(2,1)}, u32[]{:S(2)}) copy-start(bf16[512,512]{1,0:T(8,128)(2,1)} %wq.3) | copy-start | bytes 1572868
  20.1 9.9 %copy-start.4 = (s32[32,128]{1,0:T(8,128)S(1)}, s32[32,128]{1,0:T(8,128)}, u32[]{:S(2)}) copy-start(s32[32,128]{1,0:T(8,128)} %merch_slot.3) | copy-start | bytes 49156
  20.1 9.9 %copy-start.9 = (s32[32]{0:T(128)S(1)}, s32[32]{0:T(128)}, u32[]{:S(2)}) copy-start(s32[32]{0:T(128)} %count_ref.3) | copy-start | bytes 388
  20.1 9.9 %copy-start.10 = (f32[4]{0:T(128)S(1)}, f32[4]{0:T(128)}, u32[]{:S(2)}) copy-start(f32[4]{0:T(128)} %bias_ref.3) | copy-start | bytes 52
  20.1 7.2 %collective-permute-start.6 = (bf16[128,512]{1,0:T(8,128)(2,1)S(1)}, bf16[128,512]{1,0:T(8,128)(2,1)S(1)}, u32[]{:S(2)}, u32[]{:S(2)}) collective-permute-start(bf16[128,512]{1,0:T(8,128)(2,1)S(1)} %pad_maximum_fusion.1), channel_id=1, source_target_pairs={{0,6},{1,7},{2,4},{3,5},{4,2},{5,3},{6,0},{7,1},{8,14},{9,15},{10,... | collective-permute-start | bytes 393224 | tf_op jit(solution)/shard_map/ppermute | solution.py:308
  23.0 6.8 %collective-permute-start.5 = (bf16[128,512]{1,0:T(8,128)(2,1)S(1)}, bf16[128,512]{1,0:T(8,128)(2,1)S(1)}, u32[]{:S(2)}, u32[]{:S(2)}) collective-permute-start(bf16[128,512]{1,0:T(8,128)(2,1)S(1)} %pad_maximum_fusion.1), channel_id=1, source_target_pairs={{0,4},{1,5},{2,6},{3,7},{4,0},{5,1},{6,2},{7,3},{8,12},{9,13},{10,... | collective-permute-start | bytes 393224 | tf_op jit(solution)/shard_map/ppermute | solution.py:308
  23.5 6.4 %collective-permute-start.4 = (bf16[128,512]{1,0:T(8,128)(2,1)S(1)}, bf16[128,512]{1,0:T(8,128)(2,1)S(1)}, u32[]{:S(2)}, u32[]{:S(2)}) collective-permute-start(bf16[128,512]{1,0:T(8,128)(2,1)S(1)} %pad_maximum_fusion.1), channel_id=1, source_target_pairs={{0,2},{1,3},{2,0},{3,1},{4,6},{5,7},{6,4},{7,5},{8,10},{9,11},{10,... | collective-permute-start | bytes 393224 | tf_op jit(solution)/shard_map/ppermute | solution.py:308
  29.9 2.2 %collective-permute-start.7 = (bf16[512,512]{1,0:T(8,128)(2,1)S(1)}, bf16[512,512]{1,0:T(8,128)(2,1)S(1)}, u32[]{:S(2)}, u32[]{:S(2)}) collective-permute-start(bf16[512,512]{1,0:T(8,128)(2,1)S(1)} %pad_maximum_fusion.feats), channel_id=1, source_target_pairs={{0,1},{1,0},{2,3},{3,2},{4,5},{5,4},{6,7},{7,6},{8,9},{9,8},{10,11... | collective-permute-start | bytes 1572872 | tf_op jit(solution)/shard_map/ppermute | solution.py:308
  31.6 2.1 %collective-permute-start.8 = (bf16[512,512]{1,0:T(8,128)(2,1)S(1)}, bf16[512,512]{1,0:T(8,128)(2,1)S(1)}, u32[]{:S(2)}, u32[]{:S(2)}) collective-permute-start(bf16[512,512]{1,0:T(8,128)(2,1)S(1)} %aggregate_odd.1), channel_id=1, source_target_pairs={{0,1},{1,0},{2,3},{3,2},{4,5},{5,4},{6,7},{7,6},{8,9},{9,8},{10,11... | collective-permute-start | bytes 1572872 | tf_op jit(solution)/shard_map/ppermute | solution.py:308
  33.7 18.0 %copy-start.3 = (bf16[512,512]{1,0:T(8,128)(2,1)S(1)}, bf16[512,512]{1,0:T(8,128)(2,1)}, u32[]{:S(2)}) copy-start(bf16[512,512]{1,0:T(8,128)(2,1)} %wo.1) | copy-start | bytes 1572868
  33.7 18.0 %copy-start.5 = (bf16[32,512]{1,0:T(8,128)(2,1)S(1)}, bf16[32,512]{1,0:T(8,128)(2,1)}, u32[]{:S(2)}) copy-start(bf16[32,512]{1,0:T(8,128)(2,1)} %feat.1) | copy-start | bytes 98308
  33.7 18.0 %copy-start.8 = (f32[512]{0:T(512)S(1)}, f32[512]{0:T(512)}, u32[]{:S(2)}) copy-start(f32[512]{0:T(512)} %param.19) | copy-start | bytes 6148
  33.8 7.3 %collective-permute-start.9 = (bf16[128,512]{1,0:T(8,128)(2,1)S(1)}, bf16[128,512]{1,0:T(8,128)(2,1)S(1)}, u32[]{:S(2)}, u32[]{:S(2)}) collective-permute-start(bf16[128,512]{1,0:T(8,128)(2,1)S(1)} %get-tuple-element.28), channel_id=1, source_target_pairs={{0,6},{1,7},{2,4},{3,5},{4,2},{5,3},{6,0},{7,1},{8,14},{9,15},{10,... | collective-permute-start | bytes 393224 | tf_op jit(solution)/shard_map/ppermute | solution.py:308
  35.6 7.7 %collective-permute-start.10 = (bf16[128,512]{1,0:T(8,128)(2,1)S(1)}, bf16[128,512]{1,0:T(8,128)(2,1)S(1)}, u32[]{:S(2)}, u32[]{:S(2)}) collective-permute-start(bf16[128,512]{1,0:T(8,128)(2,1)S(1)} %get-tuple-element.29), channel_id=1, source_target_pairs={{0,4},{1,5},{2,6},{3,7},{4,0},{5,1},{6,2},{7,3},{8,12},{9,13},{10,... | collective-permute-start | bytes 393224 | tf_op jit(solution)/shard_map/ppermute | solution.py:308
  36.9 6.5 %collective-permute-start.11 = (bf16[128,512]{1,0:T(8,128)(2,1)S(1)}, bf16[128,512]{1,0:T(8,128)(2,1)S(1)}, u32[]{:S(2)}, u32[]{:S(2)}) collective-permute-start(bf16[128,512]{1,0:T(8,128)(2,1)S(1)} %get-tuple-element.30), channel_id=1, source_target_pairs={{0,2},{1,3},{2,0},{3,1},{4,6},{5,7},{6,4},{7,5},{8,10},{9,11},{10,... | collective-permute-start | bytes 393224 | tf_op jit(solution)/shard_map/ppermute | solution.py:308
  43.4 5.8 %collective-permute-start.12 = (bf16[32,512]{1,0:T(8,128)(2,1)S(1)}, bf16[32,512]{1,0:T(8,128)(2,1)S(1)}, u32[]{:S(2)}, u32[]{:S(2)}) collective-permute-start(bf16[32,512]{1,0:T(8,128)(2,1)S(1)} %get-tuple-element.32), channel_id=1, source_target_pairs={{0,24},{1,25},{2,26},{3,27},{4,28},{5,29},{6,30},{7,31},{8,16},{9,... | collective-permute-start | bytes 98312 | tf_op jit(solution)/shard_map/ppermute | solution.py:308
  46.9 4.8 %collective-permute-start.13 = (bf16[32,512]{1,0:T(8,128)(2,1)S(1)}, bf16[32,512]{1,0:T(8,128)(2,1)S(1)}, u32[]{:S(2)}, u32[]{:S(2)}) collective-permute-start(bf16[32,512]{1,0:T(8,128)(2,1)S(1)} %get-tuple-element.33), channel_id=1, source_target_pairs={{0,16},{1,17},{2,18},{3,19},{4,20},{5,21},{6,22},{7,23},{8,24},{9,... | collective-permute-start | bytes 98312 | tf_op jit(solution)/shard_map/ppermute | solution.py:308
  46.9 4.8 %collective-permute-start.14 = (bf16[32,512]{1,0:T(8,128)(2,1)S(1)}, bf16[32,512]{1,0:T(8,128)(2,1)S(1)}, u32[]{:S(2)}, u32[]{:S(2)}) collective-permute-start(bf16[32,512]{1,0:T(8,128)(2,1)S(1)} %get-tuple-element.34), channel_id=1, source_target_pairs={{0,8},{1,9},{2,10},{3,11},{4,12},{5,13},{6,14},{7,15},{8,0},{9,1},... | collective-permute-start | bytes 98312 | tf_op jit(solution)/shard_map/ppermute | solution.py:308

commit v5 on v3

v5 whole, which is shorter than its diff:
```python
import functools
import math

import jax
import jax.numpy as jnp
from jax import lax
from jax.experimental import pallas as pl
from jax.experimental.pallas import tpu as pltpu
from jax.sharding import PartitionSpec as P

AXES = ("acct", "merch")
LANES = 128
F32 = jnp.float32
BF16 = jnp.bfloat16
SMEM = pl.BlockSpec(memory_space=pltpu.SMEM)
ANY = pl.BlockSpec(memory_space=pl.ANY)
VMEM = pl.BlockSpec(memory_space=pltpu.VMEM)


def _mb(n):
    return pltpu.CompilerParams(vmem_limit_bytes=n * 2**20)


def _cost(flops, bytes_accessed, transcendentals=0):
    return pl.CostEstimate(
        flops=int(flops), bytes_accessed=int(bytes_accessed), transcendentals=transcendentals
    )


def _offset(i, outer):
    return (i // outer) * 2 + (i % outer) * 8


def query_kernel(feat_hbm, wq_hbm, out, feat, wq, sem):
    copies = [
        pltpu.make_async_copy(feat_hbm, feat, sem.at[0]),
        pltpu.make_async_copy(wq_hbm, wq, sem.at[1]),
    ]
    for copy in copies:
        copy.start()
    for copy in copies:
        copy.wait()
    out[...] = jnp.dot(feat[...], wq[...], preferred_element_type=F32).astype(BF16)


def make_query(feat, wq):
    return pl.pallas_call(
        query_kernel,
        out_shape=jax.ShapeDtypeStruct(feat.shape, BF16),
        in_specs=[ANY, ANY],
        out_specs=VMEM,
        scratch_shapes=[
            pltpu.VMEM(feat.shape, BF16),
            pltpu.VMEM(wq.shape, BF16),
            pltpu.SemaphoreType.DMA((2,)),
        ],
        compiler_params=_mb(2),
        cost_estimate=_cost(2 * feat.shape[0] * wq.size, 24 * 2**20),
        name="make_query",
    )(feat, wq)


def gather_kernel(
    rel_ref, count_ref, slots_ref, acct, feats, place_ref, pair_rel_ref,
    table, rows0, rows1, next_ref,
):
    accounts, width = acct.shape
    blocks, block_len = slots_ref.shape
    relations = next_ref.shape[0]
    parts = width // LANES
    group = 16
    for r in range(relations):
        next_ref[r] = 0

    @pl.loop(0, blocks)
    def _(b):
        next_ref[rel_ref[b]] += 1

    @pl.loop(0, pair_rel_ref.shape[0])
    def _(p):
        pair_rel_ref[p] = 0

    first = jnp.int32(0)
    for r in range(relations):
        after = first + ((next_ref[r] + 1) // 2) * 2
        next_ref[r] = first
        first = after

    rows0[...] = jnp.zeros_like(rows0)
    rows1[...] = jnp.zeros_like(rows1)

    @pl.loop(0, accounts // 16, unroll=4)
    def _(g):
        start = pl.multiple_of(g * 16, 16)
        tile = acct[pl.ds(start, 16), :].astype(F32)
        for c in range(parts):
            table[pl.ds(start * parts + c, 16, stride=parts), :] = tile[
                :, c * LANES : (c + 1) * LANES
            ]

    def collect(b, rows):
        @pl.loop(0, (count_ref[b] + group - 1) // group)
        def _(g):
            base = g * group
            for u in range(group):
                source = pl.multiple_of(slots_ref[b, base + u] * parts, parts)
                target = pl.multiple_of(base * parts, group * parts) + u * parts
                rows[pl.ds(target, parts), :] = table[pl.ds(source, parts), :]

    def emit(b, rows):
        relation = rel_ref[b]
        place = next_ref[relation]
        next_ref[relation] = place + 1
        place_ref[b] = place
        pair_rel_ref[place // 2] = relation
        for c in range(parts):
            feats[place, :, c * LANES : (c + 1) * LANES] = rows[
                pl.ds(c, block_len, stride=parts), :
            ].astype(BF16)

    @pl.loop(0, blocks // 2)
    def _(h):
        collect(2 * h, rows0)
        collect(2 * h + 1, rows1)
        emit(2 * h, rows0)
        emit(2 * h + 1, rows1)


def gather(rel, count, slots, acct, relations):
    blocks, block_len = slots.shape
    accounts, width = acct.shape
    parts = width // LANES
    pairs = (blocks + relations) // 2
    rows = pltpu.VMEM((block_len * parts, LANES), F32)
    return pl.pallas_call(
        gather_kernel,
        out_shape=(
            jax.ShapeDtypeStruct((2 * pairs, block_len, width), BF16),
            jax.ShapeDtypeStruct((blocks,), jnp.int32),
            jax.ShapeDtypeStruct((pairs,), jnp.int32),
        ),
        in_specs=[SMEM] * 3 + [VMEM],
        out_specs=(VMEM, SMEM, SMEM),
        scratch_shapes=[
            pltpu.VMEM((accounts * parts, LANES), F32),
            rows,
            rows,
            pltpu.SMEM((relations,), jnp.int32),
        ],
        compiler_params=_mb(10),
        cost_estimate=_cost(0, 20 * 2**20),
        name="gather_slots",
    )(rel, count, slots, acct)


def _project_pair(feats, relation, kw, mw, keys, values):
    _, block_len, width = feats.shape
    both = feats[...].reshape(2 * block_len, width)
    for n in range(0, width, 256):
        key = jnp.dot(both, kw[relation, :, n : n + 256], preferred_element_type=F32).astype(BF16)
        value = jnp.dot(both, mw[relation, :, n : n + 256], preferred_element_type=F32).astype(BF16)
        for h in range(2):
            part = slice(h * block_len, (h + 1) * block_len)
            keys[h, n : n + 256, :] = key[part, :].T
            values[h, :, n : n + 256] = value[part, :]


def project_kernel(pair_rel_ref, feats, kw, mw, keys, values):
    @pl.loop(0, pair_rel_ref.shape[0], unroll=2)
    def _(p):
        pair = pl.ds(2 * p, 2)
        _project_pair(feats.at[pair], pair_rel_ref[p], kw, mw, keys.at[pair], values.at[pair])


def project_step_kernel(pair_rel_ref, feats, kw, mw, keys, values):
    _project_pair(feats, pair_rel_ref[pl.program_id(0)], kw, mw, keys, values)


def project(pair_rel, feats, kw, mw):
    places, block_len, width = feats.shape
    out_shape = (
        jax.ShapeDtypeStruct((places, width, block_len), BF16),
        jax.ShapeDtypeStruct((places, block_len, width), BF16),
    )
    cost = _cost(4 * places * block_len * width * width, 16 * 2**20)
    if places <= 40:
        return pl.pallas_call(
            project_kernel,
            out_shape=out_shape,
            in_specs=[SMEM] + [VMEM] * 3,
            out_specs=(VMEM, VMEM),
            compiler_params=_mb(4),
            cost_estimate=cost,
            name="project_slots",
        )(pair_rel, feats, kw, mw)
    whole = pl.BlockSpec(kw.shape, lambda p: (0, 0, 0))
    values = pl.BlockSpec((2, block_len, width), lambda p: (p, 0, 0))
    keys = pl.BlockSpec((2, width, block_len), lambda p: (p, 0, 0))
    return pl.pallas_call(
        project_step_kernel,
        grid=(places // 2,),
        out_shape=out_shape,
        in_specs=[SMEM, values, whole, whole],
        out_specs=(keys, values),
        compiler_params=_mb(20),
        cost_estimate=cost,
        name="project_slots",
    )(pair_rel, feats, kw, mw)


def aggregate_kernel(
    outer, shift, me_ref, rel_ref, count_ref, place_ref, bias_ref, merch_slot, query, keys,
    values, sums, gates,
):
    _, width, block_len = keys.shape
    blocks = merch_slot.shape[0] // 2
    merchants = query.shape[0] // blocks
    me = me_ref[0]
    row = lax.broadcasted_iota(jnp.int32, (merchants, block_len), 0)
    lane = lax.broadcasted_iota(jnp.int32, (merchants, block_len), 1)
    for i in range(blocks):
        block = jnp.bitwise_xor(me, _offset(i, outer) + shift)
        score = jnp.dot(
            query[i * merchants : (i + 1) * merchants, :],
            keys[place_ref[block]],
            preferred_element_type=F32,
        ) / math.sqrt(width)
        score = score + bias_ref[rel_ref[block]]
        mine = (merch_slot[pl.ds(block, 1), :] == row) & (lane < count_ref[block])
        gates[i * merchants : (i + 1) * merchants, :] = jnp.where(
            mine, jax.nn.sigmoid(score), 0.0
        ).astype(BF16)
    for i in range(blocks):
        block = jnp.bitwise_xor(me, _offset(i, outer) + shift)
        sums[i * merchants : (i + 1) * merchants, :] = jnp.dot(
            gates[i * merchants : (i + 1) * merchants, :],
            values[place_ref[block]],
            preferred_element_type=F32,
        ).astype(sums.dtype)


def aggregate(
    outer, shift, me, rel, count, place, bias, merch_slot, query, keys, values, dtype
):
    width, block_len = keys.shape[1:]
    rows = query.shape[0]
    return pl.pallas_call(
        functools.partial(aggregate_kernel, outer, shift),
        out_shape=jax.ShapeDtypeStruct(query.shape, dtype),
        in_specs=[SMEM] * 5 + [VMEM] * 4,
        out_specs=VMEM,
        scratch_shapes=[pltpu.VMEM((rows, block_len), BF16)],
        compiler_params=_mb(6),
        cost_estimate=_cost(
            4 * rows * block_len * width, 6 * 2**20, rows * block_len
        ),
        name="aggregate_odd" if shift else "aggregate_even",
    )(me, rel, count, place, bias, merch_slot, query, keys, values)


def combine_kernel(mine, other, *outs):
    rows = outs[0].shape[0]
    for j, out in enumerate(outs):
        part = slice(j * rows, (j + 1) * rows)
        out[...] = (mine[part, :] + other[part, :].astype(F32)).astype(out.dtype)


def combine(inner, mine, other):
    rows, width = mine.shape
    return pl.pallas_call(
        combine_kernel,
        out_shape=tuple(
            jax.ShapeDtypeStruct((rows // inner, width), F32 if j == 0 else BF16)
            for j in range(inner)
        ),
        in_specs=[VMEM, VMEM],
        out_specs=(VMEM,) * inner,
        compiler_params=_mb(2),
        cost_estimate=_cost(0, 2 * 2**20),
        name="combine_cores",
    )(mine, other)


def plane_kernel(inner, *refs):
    ins, outs = refs[:inner], refs[inner:]
    rows = outs[0].shape[0]
    for k, out in enumerate(outs):
        part = slice(k * rows, (k + 1) * rows)
        total = ins[0][part, :]
        for other in ins[1:]:
            total = total + other[part, :].astype(F32)
        out[...] = total.astype(out.dtype)


def combine_plane(outer, parts):
    rows, width = parts[0].shape
    return pl.pallas_call(
        functools.partial(plane_kernel, len(parts)),
        out_shape=tuple(
            jax.ShapeDtypeStruct((rows // outer, width), F32 if k == 0 else BF16)
            for k in range(outer)
        ),
        in_specs=[VMEM] * len(parts),
        out_specs=(VMEM,) * outer,
        compiler_params=_mb(2),
        cost_estimate=_cost(0, 2**20),
        name="combine_plane",
    )(*parts)


def finish_kernel(feat, gain, wo, *refs):
    out = refs[-1]
    total = refs[0][...]
    for part in refs[1:-1]:
        total = total + part[...].astype(F32)
    update = feat[...].astype(F32) + jnp.dot(
        total.astype(BF16), wo[...], preferred_element_type=F32
    )
    scale = lax.rsqrt(jnp.mean(update * update, axis=-1, keepdims=True) + 1e-06)
    out[...] = (update * scale * gain[...]).astype(BF16)


def finish(feat, gain, wo, parts):
    return pl.pallas_call(
        finish_kernel,
        out_shape=jax.ShapeDtypeStruct(feat.shape, BF16),
        in_specs=[VMEM] * (3 + len(parts)),
        out_specs=VMEM,
        compiler_params=_mb(2),
        name="finish",
    )(feat, gain.reshape(1, -1), wo, *parts)


def per_device(
    acct_feat,
    merch_feat,
    key_weight,
    msg_weight,
    query_weight,
    out_weight,
    rel_bias,
    out_gain,
    slot_acct,
    slot_merch,
    block_rel,
    block_count,
):
    devices = lax.axis_size(AXES)
    me = lax.axis_index(AXES).astype(jnp.int32).reshape(1)
    inner = 4
    outer = devices // (2 * inner)

    def swap(value, mask):
        return lax.ppermute(value, AXES, [(s, s ^ mask) for s in range(devices)])

    def after(value, *others):
        return lax.optimization_barrier((value,) + others)[0]

    query = make_query(merch_feat, query_weight)
    query = jnp.concatenate([swap(query, 8 * k + 1) for k in range(outer)], axis=0)
    rows, place, pair_rel = gather(
        block_rel, block_count, slot_acct, acct_feat, key_weight.shape[0]
    )
    query = after(query, rows)
    query = jnp.concatenate([query] + [swap(query, 2 * j) for j in range(1, inner)], axis=0)
    keys, values = project(pair_rel, rows, key_weight, msg_weight)
    query = after(query, keys)

    scalars = (me, block_rel, block_count, place, rel_bias, slot_merch)
    even_query = swap(query, 1)
    odd_sums = aggregate(outer, 1, *scalars, query, keys, values, BF16)
    other = swap(odd_sums, 1)
    even_sums = aggregate(outer, 0, *scalars, even_query, keys, values, F32)
    parts = combine(inner, even_sums, other)
    parts = combine_plane(
        outer, [parts[0]] + [swap(parts[j], 2 * j) for j in reversed(range(1, inner))]
    )
    parts = [parts[0]] + [swap(parts[k], 8 * k) for k in reversed(range(1, outer))]
    return finish(merch_feat, out_gain, out_weight, parts)


def solution(mesh):
    placed = (
        P(("acct", "merch"), None),
        P(("acct", "merch"), None),
        P(),
        P(),
        P(),
        P(),
        P(),
        P(),
        P(("acct", "merch"), None),
        P(("acct", "merch"), None),
        P(("acct", "merch")),
        P(("acct", "merch")),
    )
    return jax.shard_map(
        per_device,
        mesh=mesh,
        in_specs=placed,
        out_specs=P(("acct", "merch"), None),
        check_vma=False,
    )
```

time: 50 us -> 70 us (1.40)
  local copies, waits for them, and re-layouts: 2.95 us -> 18.2 us
  Pallas kernels: 18.6 us -> 22.4 us
    unnamed x24 -> x38, local copies, waits for them, and re-layouts: 2.95 us -> 18.2 us
    pallas_call x2 -> x3, Pallas kernels: 14.5 us -> 18.8 us  [the longest x1 11.1 us: gather(): pl.pallas_call(gather_kernel, out_shape=(jax.ShapeDtypeStruct((2 * pairs,...]
  transfers between devices with their start and end apart: 15 -> 15, of which waited for: 5 -> 6; matrix products, arithmetic and copies ran while one was open for 0% -> 0% of each run, Pallas kernels for 35% -> 30%
where the time goes in v5:
time: 70 us; the launch traced here: 69.5 us
  Pallas kernels  22.4 us (32%)
  local copies, waits for them, and re-layouts  18.2 us (26%)
  starting transfers between devices  17.8 us (25%)
  waiting for transfers between devices  10.8 us (15%)
    unnamed x38, local copies, waits for them, and re-layouts  18.2 us
    ppermute x15, starting transfers between devices, swap(): return lax.ppermute(value, AXES, [(s, s ^ mask) for s in range(devices)])  17.8 us
    pallas_call x1, Pallas kernels, gather(): pl.pallas_call(gather_kernel, out_shape=(jax.ShapeDtypeStruct((2 * pairs,...  11.1 us
    ppermute x15, waiting for transfers between devices, swap(): return lax.ppermute(value, AXES, [(s, s ^ mask) for s in range(devices)])  10.8 us
    pallas_call x1, Pallas kernels, project(): pl.pallas_call(project_kernel, out_shape=out_shape, in_specs=[SMEM] + [VM...  7.46 us
    pallas_call x2, Pallas kernels, aggregate(): pl.pallas_call(functools.partial(aggregate_kernel, outer, shift), out_sha...  2.54 us
  transfers between devices with their start and end apart: 15, of which 6 were waited for; matrix products, arithmetic and copies ran while one was open for 0% of the time, Pallas kernels for 30%

profile of v5, /device:TPU:0, one launch (start us, length us, event | category | flops | bytes accessed | tf_op | source)
XLA Modules:
  0.0 69.5 jit_solution(5095595552280864337)
XLA Ops:
  0.0 1.0 %copy-done.5 = bf16[512,512]{1,0:T(8,128)(2,1)S(1)} copy-done((bf16[512,512]{1,0:T(8,128)(2,1)S(1)}, bf16[512,512]{1,0:T(8,128)(2,1)}, u32[]{:S(2)}) %copy-start.5) | copy-done | bytes 524312
  1.0 0.8 %copy-done.7 = bf16[32,512]{1,0:T(8,128)(2,1)S(1)} copy-done((bf16[32,512]{1,0:T(8,128)(2,1)S(1)}, bf16[32,512]{1,0:T(8,128)(2,1)}, u32[]{:S(2)}) %copy-start.7) | copy-done | bytes 32792
  2.6 2.7 %collective-permute-start.1 = (bf16[32,512]{1,0:T(8,128)(2,1)S(1)}, bf16[32,512]{1,0:T(8,128)(2,1)S(1)}, u32[]{:S(2)}, u32[]{:S(2)}) collective-permute-start(bf16[32,512]{1,0:T(8,128)(2,1)S(1)} %make_query.1), channel_id=1, source_target_pairs={{0,9},{1,8},{2,11},{3,10},{4,13},{5,12},{6,15},{7,14},{8,1},{9,0},... | collective-permute-start | bytes 98312 | tf_op jit(solution)/shard_map/ppermute | solution.py:354
  5.3 2.3 %collective-permute-start.2 = (bf16[32,512]{1,0:T(8,128)(2,1)S(1)}, bf16[32,512]{1,0:T(8,128)(2,1)S(1)}, u32[]{:S(2)}, u32[]{:S(2)}) collective-permute-start(bf16[32,512]{1,0:T(8,128)(2,1)S(1)} %make_query.1), channel_id=1, source_target_pairs={{0,17},{1,16},{2,19},{3,18},{4,21},{5,20},{6,23},{7,22},{8,25},{9,... | collective-permute-start | bytes 98312 | tf_op jit(solution)/shard_map/ppermute | solution.py:354
  7.6 2.2 %copy-done.4 = bf16[4096,512]{1,0:T(8,128)(2,1)S(1)} copy-done((bf16[4096,512]{1,0:T(8,128)(2,1)S(1)}, bf16[4096,512]{1,0:T(8,128)(2,1)}, u32[]{:S(2)}) %copy-start.4) | copy-done | bytes 4194328
  9.7 0.7 %copy-done.10 = s32[32,128]{1,0:T(8,128)S(1)} copy-done((s32[32,128]{1,0:T(8,128)S(1)}, s32[32,128]{1,0:T(8,128)}, u32[]{:S(2)}) %copy-start.10) | copy-done | bytes 16408
  10.5 0.7 copy-done.11
  11.1 0.7 copy-done.13
  11.8 11.1 %gather_slots.1 = (bf16[36,128,512]{2,1,0:T(8,128)(2,1)S(1)}, s32[32]{0:T(128)S(1)}, s32[18]{0:T(128)S(1)}) custom-call(s32[32]{0:T(128)S(1)} %copy-done.11, s32[32]{0:T(128)S(1)} %copy-done.13, s32[32,128]{1,0:T(8,128)S(1)} %copy-done.10, bf16[4096,512]{1,0:T(8,128)(2,1)S(1)} %copy-done.4), custom_call_target="tpu_custom_call" | custom-call | bytes 20971520 | tf_op jit(solution)/shard_map/gather_slots/pallas_call | solution.py:135
  23.0 1.9 %collective-permute-start.4 = (bf16[128,512]{1,0:T(8,128)(2,1)S(1)}, bf16[128,512]{1,0:T(8,128)(2,1)S(1)}, u32[]{:S(2)}, u32[]{:S(2)}) collective-permute-start(bf16[128,512]{1,0:T(8,128)(2,1)S(1)} %pad_maximum_fusion.1), channel_id=1, source_target_pairs={{0,2},{1,3},{2,0},{3,1},{4,6},{5,7},{6,4},{7,5},{8,10},{9,11},{10,... | collective-permute-start | bytes 393224 | tf_op jit(solution)/shard_map/ppermute | solution.py:354
  24.8 0.9 %collective-permute-start.5 = (bf16[128,512]{1,0:T(8,128)(2,1)S(1)}, bf16[128,512]{1,0:T(8,128)(2,1)S(1)}, u32[]{:S(2)}, u32[]{:S(2)}) collective-permute-start(bf16[128,512]{1,0:T(8,128)(2,1)S(1)} %pad_maximum_fusion.1), channel_id=1, source_target_pairs={{0,4},{1,5},{2,6},{3,7},{4,0},{5,1},{6,2},{7,3},{8,12},{9,13},{10,... | collective-permute-start | bytes 393224 | tf_op jit(solution)/shard_map/ppermute | solution.py:354
  25.7 0.8 %collective-permute-start.6 = (bf16[128,512]{1,0:T(8,128)(2,1)S(1)}, bf16[128,512]{1,0:T(8,128)(2,1)S(1)}, u32[]{:S(2)}, u32[]{:S(2)}) collective-permute-start(bf16[128,512]{1,0:T(8,128)(2,1)S(1)} %pad_maximum_fusion.1), channel_id=1, source_target_pairs={{0,6},{1,7},{2,4},{3,5},{4,2},{5,3},{6,0},{7,1},{8,14},{9,15},{10,... | collective-permute-start | bytes 393224 | tf_op jit(solution)/shard_map/ppermute | solution.py:354
  26.5 1.6 %copy-done.17 = bf16[4,512,512]{2,1,0:T(8,128)(2,1)S(1)} copy-done((bf16[4,512,512]{2,1,0:T(8,128)(2,1)S(1)}, bf16[4,512,512]{2,1,0:T(8,128)(2,1)}, u32[]{:S(2)}) %copy-start.17) | copy-done | bytes 2097176
  28.1 1.6 %copy-done.18 = bf16[4,512,512]{2,1,0:T(8,128)(2,1)S(1)} copy-done((bf16[4,512,512]{2,1,0:T(8,128)(2,1)S(1)}, bf16[4,512,512]{2,1,0:T(8,128)(2,1)}, u32[]{:S(2)}) %copy-start.18) | copy-done | bytes 2097176
  29.7 7.5 %project_slots.1 = (bf16[36,512,128]{2,1,0:T(8,128)(2,1)S(1)}, bf16[36,128,512]{2,1,0:T(8,128)(2,1)S(1)}) custom-call(s32[18]{0:T(128)S(1)} %get-tuple-element.23.pair_rel_ref, bf16[36,128,512]{2,1,0:T(8,128)(2,1)S(1)} %get-tuple-element.21.feats, bf16[4,512,512]{2,1,0:T(8,128)(2,1)S(1)} %copy-done.17, bf16[4,512,512]{2,1,0:T(8,128)(2,1)S(1)} %copy-done.18), custom_call_target="tpu_custom_call" | custom-call | flops 4831838208 | bytes 16777216 | tf_op jit(solution)/shard_map/project_slots/pallas_call | solution.py:187
  37.2 2.1 %copy-done = bf16[36,512,128]{2,1,0:T(8,128)(2,1)} copy-done((bf16[36,512,128]{2,1,0:T(8,128)(2,1)}, bf16[36,512,128]{2,1,0:T(8,128)(2,1)S(1)}, u32[]{:S(2)}) %copy-start) | copy-done | bytes 4718616
  39.3 2.2 %copy-done.2 = bf16[36,128,512]{2,1,0:T(8,128)(2,1)} copy-done((bf16[36,128,512]{2,1,0:T(8,128)(2,1)}, bf16[36,128,512]{2,1,0:T(8,128)(2,1)S(1)}, u32[]{:S(2)}) %copy-start.2) | copy-done | bytes 4718616
  41.7 2.3 %copy-done.1 = bf16[36,512,128]{2,1,0:T(8,128)(2,1)S(1)} copy-done((bf16[36,512,128]{2,1,0:T(8,128)(2,1)S(1)}, bf16[36,512,128]{2,1,0:T(8,128)(2,1)}, u32[]{:S(2)}) %copy-start.1) | copy-done | bytes 4718616
  44.0 2.3 %copy-done.3 = bf16[36,128,512]{2,1,0:T(8,128)(2,1)S(1)} copy-done((bf16[36,128,512]{2,1,0:T(8,128)(2,1)S(1)}, bf16[36,128,512]{2,1,0:T(8,128)(2,1)}, u32[]{:S(2)}) %copy-start.3) | copy-done | bytes 4718616
  46.3 1.3 %aggregate_odd.1 = bf16[512,512]{1,0:T(8,128)(2,1)S(1)} custom-call(s32[1]{0:T(128)} %bitcast.1.me_ref, s32[32]{0:T(128)S(1)} %copy-done.12, s32[32]{0:T(128)S(1)} %copy-done.14, s32[32]{0:T(128)S(1)} %get-tuple-element.20.place_ref, f32[4]{0:T(128)S(1)} %copy-done.16, s32[32,128]{1,0:T(8,128)S(1)} %copy-done.9, bf16[512,512]{1,0:T(8,128)(2,1)S(1)} %pad_maximum_fusion.query, ...), custom_call_target="tpu_custom_call" | custom-call | flops 134217728 | bytes 6291456 | tf_op jit(solution)/shard_map/aggregate_odd/pallas_call | solution.py:247
  48.2 1.3 %aggregate_even.1.mine = f32[512,512]{1,0:T(8,128)S(1)} custom-call(s32[1]{0:T(128)} %bitcast.1.me_ref, s32[32]{0:T(128)S(1)} %copy-done.12, s32[32]{0:T(128)S(1)} %copy-done.14, s32[32]{0:T(128)S(1)} %get-tuple-element.20.place_ref, f32[4]{0:T(128)S(1)} %copy-done.16, s32[32,128]{1,0:T(8,128)S(1)} %copy-done.9, ...), custom_call_target="tpu_custom_call" | custom-call | flops 134217728 | bytes 6291456 | tf_op jit(solution)/shard_map/aggregate_even/pallas_call | solution.py:247
  49.8 1.4 %collective-permute-start.10 = (bf16[128,512]{1,0:T(8,128)(2,1)S(1)}, bf16[128,512]{1,0:T(8,128)(2,1)S(1)}, u32[]{:S(2)}, u32[]{:S(2)}) collective-permute-start(bf16[128,512]{1,0:T(8,128)(2,1)S(1)} %get-tuple-element.29), channel_id=1, source_target_pairs={{0,4},{1,5},{2,6},{3,7},{4,0},{5,1},{6,2},{7,3},{8,12},{9,13},{10,... | collective-permute-start | bytes 393224 | tf_op jit(solution)/shard_map/ppermute | solution.py:354
  51.2 1.4 %collective-permute-start.11 = (bf16[128,512]{1,0:T(8,128)(2,1)S(1)}, bf16[128,512]{1,0:T(8,128)(2,1)S(1)}, u32[]{:S(2)}, u32[]{:S(2)}) collective-permute-start(bf16[128,512]{1,0:T(8,128)(2,1)S(1)} %get-tuple-element.30), channel_id=1, source_target_pairs={{0,2},{1,3},{2,0},{3,1},{4,6},{5,7},{6,4},{7,5},{8,10},{9,11},{10,... | collective-permute-start | bytes 393224 | tf_op jit(solution)/shard_map/ppermute | solution.py:354
  52.6 0.8 %collective-permute-start.9 = (bf16[128,512]{1,0:T(8,128)(2,1)S(1)}, bf16[128,512]{1,0:T(8,128)(2,1)S(1)}, u32[]{:S(2)}, u32[]{:S(2)}) collective-permute-start(bf16[128,512]{1,0:T(8,128)(2,1)S(1)} %get-tuple-element.28), channel_id=1, source_target_pairs={{0,6},{1,7},{2,4},{3,5},{4,2},{5,3},{6,0},{7,1},{8,14},{9,15},{10,... | collective-permute-start | bytes 393224 | tf_op jit(solution)/shard_map/ppermute | solution.py:354
  53.4 2.3 %collective-permute-done.10.refs_2_ = bf16[128,512]{1,0:T(8,128)(2,1)S(1)} collective-permute-done((bf16[128,512]{1,0:T(8,128)(2,1)S(1)}, bf16[128,512]{1,0:T(8,128)(2,1)S(1)}, u32[]{:S(2)}, u32[]{:S(2)}) %collective-permute-start.10) | collective-permute-done | bytes 131104 | tf_op jit(solution)/shard_map/ppermute | solution.py:354
  55.7 1.9 %collective-permute-done.11.refs_3_ = bf16[128,512]{1,0:T(8,128)(2,1)S(1)} collective-permute-done((bf16[128,512]{1,0:T(8,128)(2,1)S(1)}, bf16[128,512]{1,0:T(8,128)(2,1)S(1)}, u32[]{:S(2)}, u32[]{:S(2)}) %collective-permute-start.11) | collective-permute-done | bytes 131104 | tf_op jit(solution)/shard_map/ppermute | solution.py:354
  57.5 2.2 %collective-permute-done.9.refs_1_ = bf16[128,512]{1,0:T(8,128)(2,1)S(1)} collective-permute-done((bf16[128,512]{1,0:T(8,128)(2,1)S(1)}, bf16[128,512]{1,0:T(8,128)(2,1)S(1)}, u32[]{:S(2)}, u32[]{:S(2)}) %collective-permute-start.9) | collective-permute-done | bytes 131104 | tf_op jit(solution)/shard_map/ppermute | solution.py:354
  59.8 4.0 %collective-permute-start.12 = (bf16[32,512]{1,0:T(8,128)(2,1)S(1)}, bf16[32,512]{1,0:T(8,128)(2,1)S(1)}, u32[]{:S(2)}, u32[]{:S(2)}) collective-permute-start(bf16[32,512]{1,0:T(8,128)(2,1)S(1)} %get-tuple-element.32), channel_id=1, source_target_pairs={{0,24},{1,25},{2,26},{3,27},{4,28},{5,29},{6,30},{7,31},{8,16},{9,... | collective-permute-start | bytes 98312 | tf_op jit(solution)/shard_map/ppermute | solution.py:354
  63.7 0.6 collective-permute-start.14
  64.4 1.7 %collective-permute-done.12.refs_1_ = bf16[32,512]{1,0:T(8,128)(2,1)S(1)} collective-permute-done((bf16[32,512]{1,0:T(8,128)(2,1)S(1)}, bf16[32,512]{1,0:T(8,128)(2,1)S(1)}, u32[]{:S(2)}, u32[]{:S(2)}) %collective-permute-start.12) | collective-permute-done | bytes 32800 | tf_op jit(solution)/shard_map/ppermute | solution.py:354
  66.0 2.5 %collective-permute-done.13.refs_2_ = bf16[32,512]{1,0:T(8,128)(2,1)S(1)} collective-permute-done((bf16[32,512]{1,0:T(8,128)(2,1)S(1)}, bf16[32,512]{1,0:T(8,128)(2,1)S(1)}, u32[]{:S(2)}, u32[]{:S(2)}) %collective-permute-start.13) | collective-permute-done | bytes 32800 | tf_op jit(solution)/shard_map/ppermute | solution.py:354
  68.6 0.9 %finish.1 = bf16[32,512]{1,0:T(8,128)(2,1)} custom-call(bf16[32,512]{1,0:T(8,128)(2,1)S(1)} %copy-done.8, f32[1,512]{1,0:T(1,128)S(1)} %bitcast.2, bf16[512,512]{1,0:T(8,128)(2,1)S(1)} %copy-done.6, f32[32,512]{1,0:T(8,128)S(1)} %get-tuple-element.31.refs_0_, bf16[32,512]{1,0:T(8,128)(2,1)S(1)} %collective-permute-done.12.refs_1_, ...), custom_call_target="tpu_custom_call" | custom-call | tf_op jit(solution)/shard_map/finish/pallas_call | solution.py:324
  (46 shorter events, 1.9 us)
Async XLA Ops:
  0.0 1.0 %copy-start.5 = (bf16[512,512]{1,0:T(8,128)(2,1)S(1)}, bf16[512,512]{1,0:T(8,128)(2,1)}, u32[]{:S(2)}) copy-start(bf16[512,512]{1,0:T(8,128)(2,1)} %wq_hbm.1) | copy-start | bytes 1572868
  1.0 0.8 %copy-start.7 = (bf16[32,512]{1,0:T(8,128)(2,1)S(1)}, bf16[32,512]{1,0:T(8,128)(2,1)}, u32[]{:S(2)}) copy-start(bf16[32,512]{1,0:T(8,128)(2,1)} %feat.1) | copy-start | bytes 98308
  2.1 20.8 %collective-permute-start = (bf16[32,512]{1,0:T(8,128)(2,1)S(1)}, bf16[32,512]{1,0:T(8,128)(2,1)S(1)}, u32[]{:S(2)}, u32[]{:S(2)}) collective-permute-start(bf16[32,512]{1,0:T(8,128)(2,1)S(1)} %make_query.1), channel_id=1, source_target_pairs={{0,1},{1,0},{2,3},{3,2},{4,5},{5,4},{6,7},{7,6},{8,9},{9,8},{10,11... | collective-permute-start | bytes 98312 | tf_op jit(solution)/shard_map/ppermute | solution.py:354
  2.6 20.3 %collective-permute-start.1 = (bf16[32,512]{1,0:T(8,128)(2,1)S(1)}, bf16[32,512]{1,0:T(8,128)(2,1)S(1)}, u32[]{:S(2)}, u32[]{:S(2)}) collective-permute-start(bf16[32,512]{1,0:T(8,128)(2,1)S(1)} %make_query.1), channel_id=1, source_target_pairs={{0,9},{1,8},{2,11},{3,10},{4,13},{5,12},{6,15},{7,14},{8,1},{9,0},... | collective-permute-start | bytes 98312 | tf_op jit(solution)/shard_map/ppermute | solution.py:354
  5.3 17.6 %collective-permute-start.2 = (bf16[32,512]{1,0:T(8,128)(2,1)S(1)}, bf16[32,512]{1,0:T(8,128)(2,1)S(1)}, u32[]{:S(2)}, u32[]{:S(2)}) collective-permute-start(bf16[32,512]{1,0:T(8,128)(2,1)S(1)} %make_query.1), channel_id=1, source_target_pairs={{0,17},{1,16},{2,19},{3,18},{4,21},{5,20},{6,23},{7,22},{8,25},{9,... | collective-permute-start | bytes 98312 | tf_op jit(solution)/shard_map/ppermute | solution.py:354
  7.6 15.4 %collective-permute-start.3 = (bf16[32,512]{1,0:T(8,128)(2,1)S(1)}, bf16[32,512]{1,0:T(8,128)(2,1)S(1)}, u32[]{:S(2)}, u32[]{:S(2)}) collective-permute-start(bf16[32,512]{1,0:T(8,128)(2,1)S(1)} %make_query.1), channel_id=1, source_target_pairs={{0,25},{1,24},{2,27},{3,26},{4,29},{5,28},{6,31},{7,30},{8,17},{9,... | collective-permute-start | bytes 98312 | tf_op jit(solution)/shard_map/ppermute | solution.py:354
  7.6 2.2 %copy-start.4 = (bf16[4096,512]{1,0:T(8,128)(2,1)S(1)}, bf16[4096,512]{1,0:T(8,128)(2,1)}, u32[]{:S(2)}) copy-start(bf16[4096,512]{1,0:T(8,128)(2,1)} %acct.1) | copy-start | bytes 12582916
  9.7 0.7 %copy-start.10 = (s32[32,128]{1,0:T(8,128)S(1)}, s32[32,128]{1,0:T(8,128)}, u32[]{:S(2)}) copy-start(s32[32,128]{1,0:T(8,128)} %slots_ref.1) | copy-start | bytes 49156
  23.0 18.5 %collective-permute-start.4 = (bf16[128,512]{1,0:T(8,128)(2,1)S(1)}, bf16[128,512]{1,0:T(8,128)(2,1)S(1)}, u32[]{:S(2)}, u32[]{:S(2)}) collective-permute-start(bf16[128,512]{1,0:T(8,128)(2,1)S(1)} %pad_maximum_fusion.1), channel_id=1, source_target_pairs={{0,2},{1,3},{2,0},{3,1},{4,6},{5,7},{6,4},{7,5},{8,10},{9,11},{10,... | collective-permute-start | bytes 393224 | tf_op jit(solution)/shard_map/ppermute | solution.py:354
  24.8 16.7 %collective-permute-start.5 = (bf16[128,512]{1,0:T(8,128)(2,1)S(1)}, bf16[128,512]{1,0:T(8,128)(2,1)S(1)}, u32[]{:S(2)}, u32[]{:S(2)}) collective-permute-start(bf16[128,512]{1,0:T(8,128)(2,1)S(1)} %pad_maximum_fusion.1), channel_id=1, source_target_pairs={{0,4},{1,5},{2,6},{3,7},{4,0},{5,1},{6,2},{7,3},{8,12},{9,13},{10,... | collective-permute-start | bytes 393224 | tf_op jit(solution)/shard_map/ppermute | solution.py:354
  25.7 15.8 %collective-permute-start.6 = (bf16[128,512]{1,0:T(8,128)(2,1)S(1)}, bf16[128,512]{1,0:T(8,128)(2,1)S(1)}, u32[]{:S(2)}, u32[]{:S(2)}) collective-permute-start(bf16[128,512]{1,0:T(8,128)(2,1)S(1)} %pad_maximum_fusion.1), channel_id=1, source_target_pairs={{0,6},{1,7},{2,4},{3,5},{4,2},{5,3},{6,0},{7,1},{8,14},{9,15},{10,... | collective-permute-start | bytes 393224 | tf_op jit(solution)/shard_map/ppermute | solution.py:354
  26.5 1.6 %copy-start.17 = (bf16[4,512,512]{2,1,0:T(8,128)(2,1)S(1)}, bf16[4,512,512]{2,1,0:T(8,128)(2,1)}, u32[]{:S(2)}) copy-start(bf16[4,512,512]{2,1,0:T(8,128)(2,1)} %kw.1) | copy-start | bytes 6291460
  28.1 1.6 %copy-start.18 = (bf16[4,512,512]{2,1,0:T(8,128)(2,1)S(1)}, bf16[4,512,512]{2,1,0:T(8,128)(2,1)}, u32[]{:S(2)}) copy-start(bf16[4,512,512]{2,1,0:T(8,128)(2,1)} %mw.1) | copy-start | bytes 6291460
  29.7 11.9 %copy-start.9 = (s32[32,128]{1,0:T(8,128)S(1)}, s32[32,128]{1,0:T(8,128)}, u32[]{:S(2)}) copy-start(s32[32,128]{1,0:T(8,128)} %merch_slot.3) | copy-start | bytes 49156
  29.7 11.9 %copy-start.12 = (s32[32]{0:T(128)S(1)}, s32[32]{0:T(128)}, u32[]{:S(2)}) copy-start(s32[32]{0:T(128)} %rel_ref.5) | copy-start | bytes 388
  29.7 12.0 %copy-start.14 = (s32[32]{0:T(128)S(1)}, s32[32]{0:T(128)}, u32[]{:S(2)}) copy-start(s32[32]{0:T(128)} %count_ref.5) | copy-start | bytes 388
  29.7 12.0 %copy-start.16 = (f32[4]{0:T(128)S(1)}, f32[4]{0:T(128)}, u32[]{:S(2)}) copy-start(f32[4]{0:T(128)} %bias_ref.3) | copy-start | bytes 52
  37.2 2.1 %copy-start = (bf16[36,512,128]{2,1,0:T(8,128)(2,1)}, bf16[36,512,128]{2,1,0:T(8,128)(2,1)S(1)}, u32[]{:S(2)}) copy-start(bf16[36,512,128]{2,1,0:T(8,128)(2,1)S(1)} %get-tuple-element.24.keys) | copy-start | bytes 14155780
  39.3 2.2 %copy-start.2 = (bf16[36,128,512]{2,1,0:T(8,128)(2,1)}, bf16[36,128,512]{2,1,0:T(8,128)(2,1)S(1)}, u32[]{:S(2)}) copy-start(bf16[36,128,512]{2,1,0:T(8,128)(2,1)S(1)} %get-tuple-element.26.values) | copy-start | bytes 14155780
  41.5 6.6 %collective-permute-start.7 = (bf16[512,512]{1,0:T(8,128)(2,1)S(1)}, bf16[512,512]{1,0:T(8,128)(2,1)S(1)}, u32[]{:S(2)}, u32[]{:S(2)}) collective-permute-start(bf16[512,512]{1,0:T(8,128)(2,1)S(1)} %pad_maximum_fusion.query), channel_id=1, source_target_pairs={{0,1},{1,0},{2,3},{3,2},{4,5},{5,4},{6,7},{7,6},{8,9},{9,8},{10,11... | collective-permute-start | bytes 1572872 | tf_op jit(solution)/shard_map/ppermute | solution.py:354
  41.7 2.3 %copy-start.1 = (bf16[36,512,128]{2,1,0:T(8,128)(2,1)S(1)}, bf16[36,512,128]{2,1,0:T(8,128)(2,1)}, u32[]{:S(2)}) copy-start(bf16[36,512,128]{2,1,0:T(8,128)(2,1)} %copy-done) | copy-start | bytes 14155780
  44.0 2.3 %copy-start.3 = (bf16[36,128,512]{2,1,0:T(8,128)(2,1)S(1)}, bf16[36,128,512]{2,1,0:T(8,128)(2,1)}, u32[]{:S(2)}) copy-start(bf16[36,128,512]{2,1,0:T(8,128)(2,1)} %copy-done.2) | copy-start | bytes 14155780
  47.6 20.9 %copy-start.6 = (bf16[512,512]{1,0:T(8,128)(2,1)S(1)}, bf16[512,512]{1,0:T(8,128)(2,1)}, u32[]{:S(2)}) copy-start(bf16[512,512]{1,0:T(8,128)(2,1)} %wo.1) | copy-start | bytes 1572868
  47.6 20.9 %copy-start.8 = (bf16[32,512]{1,0:T(8,128)(2,1)S(1)}, bf16[32,512]{1,0:T(8,128)(2,1)}, u32[]{:S(2)}) copy-start(bf16[32,512]{1,0:T(8,128)(2,1)} %feat.1) | copy-start | bytes 98308
  47.6 20.9 %copy-start.15 = (f32[512]{0:T(512)S(1)}, f32[512]{0:T(512)}, u32[]{:S(2)}) copy-start(f32[512]{0:T(512)} %param.19) | copy-start | bytes 6148
  47.7 2.1 %collective-permute-start.8 = (bf16[512,512]{1,0:T(8,128)(2,1)S(1)}, bf16[512,512]{1,0:T(8,128)(2,1)S(1)}, u32[]{:S(2)}, u32[]{:S(2)}) collective-permute-start(bf16[512,512]{1,0:T(8,128)(2,1)S(1)} %aggregate_odd.1), channel_id=1, source_target_pairs={{0,1},{1,0},{2,3},{3,2},{4,5},{5,4},{6,7},{7,6},{8,9},{9,8},{10,11... | collective-permute-start | bytes 1572872 | tf_op jit(solution)/shard_map/ppermute | solution.py:354
  49.8 5.8 %collective-permute-start.10 = (bf16[128,512]{1,0:T(8,128)(2,1)S(1)}, bf16[128,512]{1,0:T(8,128)(2,1)S(1)}, u32[]{:S(2)}, u32[]{:S(2)}) collective-permute-start(bf16[128,512]{1,0:T(8,128)(2,1)S(1)} %get-tuple-element.29), channel_id=1, source_target_pairs={{0,4},{1,5},{2,6},{3,7},{4,0},{5,1},{6,2},{7,3},{8,12},{9,13},{10,... | collective-permute-start | bytes 393224 | tf_op jit(solution)/shard_map/ppermute | solution.py:354
  51.2 6.4 %collective-permute-start.11 = (bf16[128,512]{1,0:T(8,128)(2,1)S(1)}, bf16[128,512]{1,0:T(8,128)(2,1)S(1)}, u32[]{:S(2)}, u32[]{:S(2)}) collective-permute-start(bf16[128,512]{1,0:T(8,128)(2,1)S(1)} %get-tuple-element.30), channel_id=1, source_target_pairs={{0,2},{1,3},{2,0},{3,1},{4,6},{5,7},{6,4},{7,5},{8,10},{9,11},{10,... | collective-permute-start | bytes 393224 | tf_op jit(solution)/shard_map/ppermute | solution.py:354
  52.6 7.1 %collective-permute-start.9 = (bf16[128,512]{1,0:T(8,128)(2,1)S(1)}, bf16[128,512]{1,0:T(8,128)(2,1)S(1)}, u32[]{:S(2)}, u32[]{:S(2)}) collective-permute-start(bf16[128,512]{1,0:T(8,128)(2,1)S(1)} %get-tuple-element.28), channel_id=1, source_target_pairs={{0,6},{1,7},{2,4},{3,5},{4,2},{5,3},{6,0},{7,1},{8,14},{9,15},{10,... | collective-permute-start | bytes 393224 | tf_op jit(solution)/shard_map/ppermute | solution.py:354
  59.8 6.3 %collective-permute-start.12 = (bf16[32,512]{1,0:T(8,128)(2,1)S(1)}, bf16[32,512]{1,0:T(8,128)(2,1)S(1)}, u32[]{:S(2)}, u32[]{:S(2)}) collective-permute-start(bf16[32,512]{1,0:T(8,128)(2,1)S(1)} %get-tuple-element.32), channel_id=1, source_target_pairs={{0,24},{1,25},{2,26},{3,27},{4,28},{5,29},{6,30},{7,31},{8,16},{9,... | collective-permute-start | bytes 98312 | tf_op jit(solution)/shard_map/ppermute | solution.py:354
  63.7 4.8 %collective-permute-start.13 = (bf16[32,512]{1,0:T(8,128)(2,1)S(1)}, bf16[32,512]{1,0:T(8,128)(2,1)S(1)}, u32[]{:S(2)}, u32[]{:S(2)}) collective-permute-start(bf16[32,512]{1,0:T(8,128)(2,1)S(1)} %get-tuple-element.33), channel_id=1, source_target_pairs={{0,16},{1,17},{2,18},{3,19},{4,20},{5,21},{6,22},{7,23},{8,24},{9,... | collective-permute-start | bytes 98312 | tf_op jit(solution)/shard_map/ppermute | solution.py:354
  63.7 4.8 %collective-permute-start.14 = (bf16[32,512]{1,0:T(8,128)(2,1)S(1)}, bf16[32,512]{1,0:T(8,128)(2,1)S(1)}, u32[]{:S(2)}, u32[]{:S(2)}) collective-permute-start(bf16[32,512]{1,0:T(8,128)(2,1)S(1)} %get-tuple-element.34), channel_id=1, source_target_pairs={{0,8},{1,9},{2,10},{3,11},{4,12},{5,13},{6,14},{7,15},{8,0},{9,1},... | collective-permute-start | bytes 98312 | tf_op jit(solution)/shard_map/ppermute | solution.py:354
  (2 other events, 1.3 us)

commit v6 on v3

--- a/solution.py
+++ b/solution.py
@@ -13,6 +13,7 @@
 F32 = jnp.float32
 BF16 = jnp.bfloat16
 SMEM = pl.BlockSpec(memory_space=pltpu.SMEM)
+ANY = pl.BlockSpec(memory_space=pl.ANY)
 VMEM = pl.BlockSpec(memory_space=pltpu.VMEM)
 
 
@@ -30,32 +31,53 @@
     return (i // outer) * 2 + (i % outer) * 8
 
 
-def gather_kernel(outer, me_ref, slots_ref, acct, odd, even, table, rows0, rows1):
+def gather_kernel(
+    outer, me_ref, slots_ref, acct_hbm, odd, even, acct, table, rows0, rows1, sem
+):
     accounts, width = acct.shape
     blocks, block_len, _ = odd.shape
     parts = width // LANES
     pitch = table.shape[1]
+    words = block_len // 2
     flat = table.reshape(accounts * pitch, LANES)
     me = me_ref[0]
-
-    @pl.loop(0, accounts // 16, unroll=4)
-    def _(g):
-        first = pl.multiple_of(g * 16, 16)
-        tile = acct[pl.ds(first, 16), :].astype(F32)
-        for c in range(parts):
-            flat[pl.ds(first * pitch + c, 16, stride=pitch), :] = tile[
-                :, c * LANES : (c + 1) * LANES
-            ]
+    chunks = sem.shape[0]
+    chunk = accounts // chunks
+    copies = [
+        pltpu.make_async_copy(
+            acct_hbm.at[pl.ds(i * chunk, chunk)], acct.at[pl.ds(i * chunk, chunk)], sem.at[i]
+        )
+        for i in range(chunks)
+    ]
+    for copy in copies:
+        copy.start()
+    for i in range(chunks):
+        copies[i].wait()
+
+        @pl.loop(0, chunk // 16, unroll=4)
+        def _(g):
+            first = pl.multiple_of(i * chunk + g * 16, 16)
+            tile = acct[pl.ds(first, 16), :].astype(F32)
+            for c in range(parts):
+                piece = tile[:, c * LANES : (c + 1) * LANES]
+                for twin in (c, c + parts):
+                    flat[pl.ds(first * pitch + twin, 16, stride=pitch), :] = piece
+
+    lower = lax.broadcasted_iota(jnp.int32, (pitch, LANES), 0) < parts
 
     def collect(block, rows):
-        for k in range(block_len):
-            rows[k * parts : (k + 1) * parts, :] = table[slots_ref[block, k], :parts, :]
+        for k in range(words):
+            word = slots_ref[block, k]
+            rows[k * pitch : (k + 1) * pitch, :] = jnp.where(
+                lower, table[word & 0xFFFF], table[lax.shift_right_logical(word, 16)]
+            )
 
     def emit(i, rows, out):
         for c in range(parts):
-            out[i, :, c * LANES : (c + 1) * LANES] = rows[
-                pl.ds(c, block_len, stride=parts), :
-            ].astype(BF16)
+            for h in range(2):
+                out[i, h * words : (h + 1) * words, c * LANES : (c + 1) * LANES] = rows[
+                    pl.ds(h * parts + c, words, stride=pitch), :
+                ].astype(BF16)
 
     @pl.loop(0, blocks)
     def _(i):
@@ -69,19 +91,27 @@
 def gather(outer, me, slots, acct):
     blocks, block_len = slots.shape
     accounts, width = acct.shape
-    parts = width // LANES
-    rows = pltpu.VMEM((block_len * parts, LANES), F32)
+    words = block_len // 2
+    packed = slots[:, :words] | (slots[:, words:] << 16)
+    pitch = 2 * width // LANES
+    rows = pltpu.VMEM((words * pitch, LANES), F32)
     half = jax.ShapeDtypeStruct((blocks // 2, block_len, width), BF16)
     return pl.pallas_call(
         functools.partial(gather_kernel, outer),
         out_shape=(half, half),
-        in_specs=[SMEM, SMEM, VMEM],
+        in_specs=[SMEM, SMEM, ANY],
         out_specs=(VMEM, VMEM),
-        scratch_shapes=[pltpu.VMEM((accounts, -(-parts // 8) * 8, LANES), F32), rows, rows],
-        compiler_params=_mb(20),
+        scratch_shapes=[
+            pltpu.VMEM(acct.shape, BF16),
+            pltpu.VMEM((accounts, pitch, LANES), F32),
+            rows,
+            rows,
+            pltpu.SemaphoreType.DMA((8,)),
+        ],
+        compiler_params=_mb(47 if blocks <= 32 else 28),
         cost_estimate=_cost(0, 20 * 2**20),
         name="gather_slots",
-    )(me, slots, acct)
+    )(me, packed, acct)
 
 
 def project_kernel(outer, shifts, me_ref, rel_ref, kw, mw, *refs):

time: 50 us -> 51.3 us (1.026)
  Pallas kernels: 18.6 us -> 21.9 us
  local copies, waits for them, and re-layouts: 2.95 us -> 0.05 us
  other arithmetic: 0.05 us -> 0.92 us
    pallas_call x1, Pallas kernels: 7.64 us -> 10.9 us  [gather(): pl.pallas_call(functools.partial(gather_kernel, outer), out_shape=(half,...]
    unnamed x24 -> x20, local copies, waits for them, and re-layouts: 2.95 us -> 0.05 us
    or x0 -> x1, other arithmetic: none -> 0.87 us  [gather(): packed = slots[:, :words] | slots[:, words:] << 16]
  transfers between devices with their start and end apart: 15 -> 15, of which waited for: 5 -> 5; matrix products, arithmetic and copies ran while one was open for 0% -> 2% of each run, Pallas kernels for 35% -> 41%
where the time goes in v6:
time: 51.3 us; the launch traced here: 51 us
  Pallas kernels  21.9 us (43%)
  starting transfers between devices  17.5 us (34%)
  waiting for transfers between devices  10.4 us (20%)
  other arithmetic  0.92 us (2%)
    ppermute x15, starting transfers between devices, swap(): return lax.ppermute(value, AXES, [(s, s ^ mask) for s in range(devices)])  17.5 us
    pallas_call x1, Pallas kernels, gather(): pl.pallas_call(functools.partial(gather_kernel, outer), out_shape=(half,...  10.9 us
    ppermute x15, waiting for transfers between devices, swap(): return lax.ppermute(value, AXES, [(s, s ^ mask) for s in range(devices)])  10.4 us
    pallas_call x1, Pallas kernels, project(): pl.pallas_call(functools.partial(project_kernel, outer, shifts), out_shap...  6.86 us
    pallas_call x2, Pallas kernels, aggregate(): pl.pallas_call(functools.partial(aggregate_kernel, outer, shift), out_sha...  3.07 us
  transfers between devices with their start and end apart: 15, of which 5 were waited for; matrix products, arithmetic and copies ran while one was open for 2% of the time, Pallas kernels for 41%

profile of v6, /device:TPU:0, one launch (start us, length us, event | category | flops | bytes accessed | tf_op | source)
XLA Modules:
  0.0 51.0 jit_solution(11612823540121441971)
XLA Ops:
  0.0 3.5 %collective-permute-start.2 = (bf16[32,512]{1,0:T(8,128)(2,1)}, bf16[32,512]{1,0:T(8,128)(2,1)S(1)}, u32[]{:S(2)}, u32[]{:S(2)}) collective-permute-start(bf16[32,512]{1,0:T(8,128)(2,1)} %feat.1), channel_id=1, source_target_pairs={{0,17},{1,16},{2,19},{3,18},{4,21},{5,20},{6,23},{7,22},{8,25},{9,... | collective-permute-start | bytes 98312 | tf_op jit(solution)/shard_map/ppermute | solution.py:295
  3.5 1.9 %collective-permute-start.1 = (bf16[32,512]{1,0:T(8,128)(2,1)}, bf16[32,512]{1,0:T(8,128)(2,1)S(1)}, u32[]{:S(2)}, u32[]{:S(2)}) collective-permute-start(bf16[32,512]{1,0:T(8,128)(2,1)} %feat.1), channel_id=1, source_target_pairs={{0,9},{1,8},{2,11},{3,10},{4,13},{5,12},{6,15},{7,14},{8,1},{9,0},... | collective-permute-start | bytes 98312 | tf_op jit(solution)/shard_map/ppermute | solution.py:295
  5.3 0.9 %shift-left_or_fusion.slots_ref = s32[32,64]{1,0:T(8,128)S(1)} fusion(s32[32,128]{1,0:T(8,128)} %param.20), kind=kLoop, calls=%fused_computation.2 | loop fusion | flops 4096 | bytes 24576 | tf_op jit(solution)/shard_map/or | solution.py:95
  6.2 10.9 %gather_slots.1 = (bf16[16,128,512]{2,1,0:T(8,128)(2,1)S(1)}, bf16[16,128,512]{2,1,0:T(8,128)(2,1)S(1)}) custom-call(s32[1]{0:T(128)} %bitcast.1.me_ref, s32[32,64]{1,0:T(8,128)S(1)} %shift-left_or_fusion.slots_ref, bf16[4096,512]{1,0:T(8,128)(2,1)} %acct_hbm.1), custom_call_target="tpu_custom_call" | custom-call | bytes 20971520 | tf_op jit(solution)/shard_map/gather_slots/pallas_call | solution.py:99
  17.1 0.0 collective-permute-done.2
  17.2 2.8 %collective-permute-start.6 = (bf16[128,512]{1,0:T(8,128)(2,1)S(1)}, bf16[128,512]{1,0:T(8,128)(2,1)S(1)}, u32[]{:S(2)}, u32[]{:S(2)}) collective-permute-start(bf16[128,512]{1,0:T(8,128)(2,1)S(1)} %pad_maximum_fusion.1), channel_id=1, source_target_pairs={{0,6},{1,7},{2,4},{3,5},{4,2},{5,3},{6,0},{7,1},{8,14},{9,15},{10,... | collective-permute-start | bytes 393224 | tf_op jit(solution)/shard_map/ppermute | solution.py:295
  20.0 0.5 collective-permute-start.5
  20.5 0.2 collective-permute-start.4
  20.7 0.0 copy-start.2
  20.8 0.0 copy-start.6
  20.8 0.0 copy-start.7
  20.8 6.9 %project_slots.1 = (bf16[16,512,128]{2,1,0:T(8,128)(2,1)S(1)}, bf16[16,128,512]{2,1,0:T(8,128)(2,1)S(1)}, bf16[16,512,128]{2,1,0:T(8,128)(2,1)S(1)}, bf16[16,128,512]{2,1,0:T(8,128)(2,1)S(1)}) custom-call(s32[1]{0:T(128)} %bitcast.1.me_ref, s32[32]{0:T(128)S(1)} %copy-done.5, bf16[4,512,512]{2,1,0:T(8,128)(2,1)S(1)} %copy-done.8, ...), custom_call_target="tpu_custom_call" | custom-call | flops 4294967296 | bytes 16777216 | tf_op jit(solution)/shard_map/project_slots/pallas_call | solution.py:141
  27.7 0.1 collective-permute-start.7
  27.8 1.5 %aggregate_odd.1 = bf16[512,512]{1,0:T(8,128)(2,1)S(1)} custom-call(s32[1]{0:T(128)} %bitcast.1.me_ref, s32[32]{0:T(128)S(1)} %copy-done.5, s32[32]{0:T(128)S(1)} %copy-done.6, f32[4]{0:T(128)S(1)} %copy-done.7, s32[32,128]{1,0:T(8,128)S(1)} %copy-done.2, bf16[512,512]{1,0:T(8,128)(2,1)S(1)} %pad_maximum_fusion.feats, bf16[512,512]{1,0:T(8,128)(2,1)S(1)} %copy-done, ...), custom_call_target="tpu_custom_call" | custom-call | flops 402653184 | bytes 6291456 | tf_op jit(solution)/shard_map/aggregate_odd/pallas_call | solution.py:183
  29.4 0.5 %collective-permute-start.8 = (bf16[512,512]{1,0:T(8,128)(2,1)S(1)}, bf16[512,512]{1,0:T(8,128)(2,1)S(1)}, u32[]{:S(2)}, u32[]{:S(2)}) collective-permute-start(bf16[512,512]{1,0:T(8,128)(2,1)S(1)} %aggregate_odd.1), channel_id=1, source_target_pairs={{0,1},{1,0},{2,3},{3,2},{4,5},{5,4},{6,7},{7,6},{8,9},{9,8},{10,11... | collective-permute-start | bytes 1572872 | tf_op jit(solution)/shard_map/ppermute | solution.py:295
  29.9 1.5 %aggregate_even.1.mine = f32[512,512]{1,0:T(8,128)S(1)} custom-call(s32[1]{0:T(128)} %bitcast.1.me_ref, s32[32]{0:T(128)S(1)} %copy-done.5, s32[32]{0:T(128)S(1)} %copy-done.6, f32[4]{0:T(128)S(1)} %copy-done.7, s32[32,128]{1,0:T(8,128)S(1)} %copy-done.2, bf16[512,512]{1,0:T(8,128)(2,1)S(1)} %collective-permute-done.7.feats, bf16[512,512]{1,0:T(8,128)(2,1)S(1)} %copy-done, ...), custom_call_target="tpu_custom_call" | custom-call | flops 402653184 | bytes 6291456 | tf_op jit(solution)/shard_map/aggregate_even/pallas_call | solution.py:183
  31.5 0.0 copy-start.1
  31.5 0.0 copy-start.3
  31.5 0.0 copy-start.4
  31.5 0.1 combine_cores.1
  31.6 2.8 %collective-permute-start.9 = (bf16[128,512]{1,0:T(8,128)(2,1)S(1)}, bf16[128,512]{1,0:T(8,128)(2,1)S(1)}, u32[]{:S(2)}, u32[]{:S(2)}) collective-permute-start(bf16[128,512]{1,0:T(8,128)(2,1)S(1)} %get-tuple-element.30), channel_id=1, source_target_pairs={{0,6},{1,7},{2,4},{3,5},{4,2},{5,3},{6,0},{7,1},{8,14},{9,15},{10,... | collective-permute-start | bytes 393224 | tf_op jit(solution)/shard_map/ppermute | solution.py:295
  34.5 0.5 collective-permute-start.10
  35.0 0.2 collective-permute-start.11
  35.2 3.4 %collective-permute-done.9.refs_1_ = bf16[128,512]{1,0:T(8,128)(2,1)S(1)} collective-permute-done((bf16[128,512]{1,0:T(8,128)(2,1)S(1)}, bf16[128,512]{1,0:T(8,128)(2,1)S(1)}, u32[]{:S(2)}, u32[]{:S(2)}) %collective-permute-start.9) | collective-permute-done | bytes 131104 | tf_op jit(solution)/shard_map/ppermute | solution.py:295
  38.5 2.7 %collective-permute-done.10.refs_2_ = bf16[128,512]{1,0:T(8,128)(2,1)S(1)} collective-permute-done((bf16[128,512]{1,0:T(8,128)(2,1)S(1)}, bf16[128,512]{1,0:T(8,128)(2,1)S(1)}, u32[]{:S(2)}, u32[]{:S(2)}) %collective-permute-start.10) | collective-permute-done | bytes 131104 | tf_op jit(solution)/shard_map/ppermute | solution.py:295
  41.2 0.3 collective-permute-done.11.refs_3_
  41.5 0.1 combine_plane.1
  41.6 3.7 %collective-permute-start.12 = (bf16[32,512]{1,0:T(8,128)(2,1)S(1)}, bf16[32,512]{1,0:T(8,128)(2,1)S(1)}, u32[]{:S(2)}, u32[]{:S(2)}) collective-permute-start(bf16[32,512]{1,0:T(8,128)(2,1)S(1)} %get-tuple-element.34), channel_id=1, source_target_pairs={{0,24},{1,25},{2,26},{3,27},{4,28},{5,29},{6,30},{7,31},{8,16},{9,... | collective-permute-start | bytes 98312 | tf_op jit(solution)/shard_map/ppermute | solution.py:295
  45.3 0.8 %collective-permute-start.14 = (bf16[32,512]{1,0:T(8,128)(2,1)S(1)}, bf16[32,512]{1,0:T(8,128)(2,1)S(1)}, u32[]{:S(2)}, u32[]{:S(2)}) collective-permute-start(bf16[32,512]{1,0:T(8,128)(2,1)S(1)} %get-tuple-element.36), channel_id=1, source_target_pairs={{0,8},{1,9},{2,10},{3,11},{4,12},{5,13},{6,14},{7,15},{8,0},{9,1},... | collective-permute-start | bytes 98312 | tf_op jit(solution)/shard_map/ppermute | solution.py:295
  46.0 1.3 %collective-permute-done.12.refs_1_ = bf16[32,512]{1,0:T(8,128)(2,1)S(1)} collective-permute-done((bf16[32,512]{1,0:T(8,128)(2,1)S(1)}, bf16[32,512]{1,0:T(8,128)(2,1)S(1)}, u32[]{:S(2)}, u32[]{:S(2)}) %collective-permute-start.12) | collective-permute-done | bytes 32800 | tf_op jit(solution)/shard_map/ppermute | solution.py:295
  47.4 2.7 %collective-permute-done.13.refs_2_ = bf16[32,512]{1,0:T(8,128)(2,1)S(1)} collective-permute-done((bf16[32,512]{1,0:T(8,128)(2,1)S(1)}, bf16[32,512]{1,0:T(8,128)(2,1)S(1)}, u32[]{:S(2)}, u32[]{:S(2)}) %collective-permute-start.13) | collective-permute-done | bytes 32800 | tf_op jit(solution)/shard_map/ppermute | solution.py:295
  50.1 0.9 %finish.1 = bf16[32,512]{1,0:T(8,128)(2,1)} custom-call(bf16[32,512]{1,0:T(8,128)(2,1)S(1)} %copy-done.3, f32[1,512]{1,0:T(1,128)S(1)} %bitcast.2, bf16[512,512]{1,0:T(8,128)(2,1)S(1)} %copy-done.1, f32[32,512]{1,0:T(8,128)S(1)} %get-tuple-element.33.refs_0_, bf16[32,512]{1,0:T(8,128)(2,1)S(1)} %collective-permute-done.12.refs_1_, ...), custom_call_target="tpu_custom_call" | custom-call | tf_op jit(solution)/shard_map/finish/pallas_call | solution.py:265
  (28 shorter events, 0.1 us)
Async XLA Ops:
  0.0 17.1 %collective-permute-start.2 = (bf16[32,512]{1,0:T(8,128)(2,1)}, bf16[32,512]{1,0:T(8,128)(2,1)S(1)}, u32[]{:S(2)}, u32[]{:S(2)}) collective-permute-start(bf16[32,512]{1,0:T(8,128)(2,1)} %feat.1), channel_id=1, source_target_pairs={{0,17},{1,16},{2,19},{3,18},{4,21},{5,20},{6,23},{7,22},{8,25},{9,... | collective-permute-start | bytes 98312 | tf_op jit(solution)/shard_map/ppermute | solution.py:295
  3.5 13.6 %collective-permute-start.1 = (bf16[32,512]{1,0:T(8,128)(2,1)}, bf16[32,512]{1,0:T(8,128)(2,1)S(1)}, u32[]{:S(2)}, u32[]{:S(2)}) collective-permute-start(bf16[32,512]{1,0:T(8,128)(2,1)} %feat.1), channel_id=1, source_target_pairs={{0,9},{1,8},{2,11},{3,10},{4,13},{5,12},{6,15},{7,14},{8,1},{9,0},... | collective-permute-start | bytes 98312 | tf_op jit(solution)/shard_map/ppermute | solution.py:295
  5.3 11.8 %collective-permute-start = (bf16[32,512]{1,0:T(8,128)(2,1)}, bf16[32,512]{1,0:T(8,128)(2,1)S(1)}, u32[]{:S(2)}, u32[]{:S(2)}) collective-permute-start(bf16[32,512]{1,0:T(8,128)(2,1)} %feat.1), channel_id=1, source_target_pairs={{0,1},{1,0},{2,3},{3,2},{4,5},{5,4},{6,7},{7,6},{8,9},{9,8},{10,11... | collective-permute-start | bytes 98312 | tf_op jit(solution)/shard_map/ppermute | solution.py:295
  5.3 11.8 %collective-permute-start.3 = (bf16[32,512]{1,0:T(8,128)(2,1)}, bf16[32,512]{1,0:T(8,128)(2,1)S(1)}, u32[]{:S(2)}, u32[]{:S(2)}) collective-permute-start(bf16[32,512]{1,0:T(8,128)(2,1)} %feat.1), channel_id=1, source_target_pairs={{0,25},{1,24},{2,27},{3,26},{4,29},{5,28},{6,31},{7,30},{8,17},{9,... | collective-permute-start | bytes 98312 | tf_op jit(solution)/shard_map/ppermute | solution.py:295
  6.2 14.5 %copy-start.5 = (s32[32]{0:T(128)S(1)}, s32[32]{0:T(128)}, u32[]{:S(2)}) copy-start(s32[32]{0:T(128)} %rel_ref.5) | copy-start | bytes 388
  6.2 14.5 %copy-start.8 = (bf16[4,512,512]{2,1,0:T(8,128)(2,1)S(1)}, bf16[4,512,512]{2,1,0:T(8,128)(2,1)}, u32[]{:S(2)}) copy-start(bf16[4,512,512]{2,1,0:T(8,128)(2,1)} %kw.1) | copy-start | bytes 6291460
  6.2 14.5 %copy-start.9 = (bf16[4,512,512]{2,1,0:T(8,128)(2,1)S(1)}, bf16[4,512,512]{2,1,0:T(8,128)(2,1)}, u32[]{:S(2)}) copy-start(bf16[4,512,512]{2,1,0:T(8,128)(2,1)} %mw.1) | copy-start | bytes 6291460
  17.2 10.5 %collective-permute-start.6 = (bf16[128,512]{1,0:T(8,128)(2,1)S(1)}, bf16[128,512]{1,0:T(8,128)(2,1)S(1)}, u32[]{:S(2)}, u32[]{:S(2)}) collective-permute-start(bf16[128,512]{1,0:T(8,128)(2,1)S(1)} %pad_maximum_fusion.1), channel_id=1, source_target_pairs={{0,6},{1,7},{2,4},{3,5},{4,2},{5,3},{6,0},{7,1},{8,14},{9,15},{10,... | collective-permute-start | bytes 393224 | tf_op jit(solution)/shard_map/ppermute | solution.py:295
  20.0 7.6 %collective-permute-start.5 = (bf16[128,512]{1,0:T(8,128)(2,1)S(1)}, bf16[128,512]{1,0:T(8,128)(2,1)S(1)}, u32[]{:S(2)}, u32[]{:S(2)}) collective-permute-start(bf16[128,512]{1,0:T(8,128)(2,1)S(1)} %pad_maximum_fusion.1), channel_id=1, source_target_pairs={{0,4},{1,5},{2,6},{3,7},{4,0},{5,1},{6,2},{7,3},{8,12},{9,13},{10,... | collective-permute-start | bytes 393224 | tf_op jit(solution)/shard_map/ppermute | solution.py:295
  20.5 7.1 %collective-permute-start.4 = (bf16[128,512]{1,0:T(8,128)(2,1)S(1)}, bf16[128,512]{1,0:T(8,128)(2,1)S(1)}, u32[]{:S(2)}, u32[]{:S(2)}) collective-permute-start(bf16[128,512]{1,0:T(8,128)(2,1)S(1)} %pad_maximum_fusion.1), channel_id=1, source_target_pairs={{0,2},{1,3},{2,0},{3,1},{4,6},{5,7},{6,4},{7,5},{8,10},{9,11},{10,... | collective-permute-start | bytes 393224 | tf_op jit(solution)/shard_map/ppermute | solution.py:295
  20.7 7.1 %copy-start = (bf16[512,512]{1,0:T(8,128)(2,1)S(1)}, bf16[512,512]{1,0:T(8,128)(2,1)}, u32[]{:S(2)}) copy-start(bf16[512,512]{1,0:T(8,128)(2,1)} %wq.3) | copy-start | bytes 1572868
  20.7 7.1 %copy-start.2 = (s32[32,128]{1,0:T(8,128)S(1)}, s32[32,128]{1,0:T(8,128)}, u32[]{:S(2)}) copy-start(s32[32,128]{1,0:T(8,128)} %merch_slot.3) | copy-start | bytes 49156
  20.8 7.1 %copy-start.6 = (s32[32]{0:T(128)S(1)}, s32[32]{0:T(128)}, u32[]{:S(2)}) copy-start(s32[32]{0:T(128)} %count_ref.3) | copy-start | bytes 388
  20.8 7.1 %copy-start.7 = (f32[4]{0:T(128)S(1)}, f32[4]{0:T(128)}, u32[]{:S(2)}) copy-start(f32[4]{0:T(128)} %bias_ref.3) | copy-start | bytes 52
  27.7 2.2 %collective-permute-start.7 = (bf16[512,512]{1,0:T(8,128)(2,1)S(1)}, bf16[512,512]{1,0:T(8,128)(2,1)S(1)}, u32[]{:S(2)}, u32[]{:S(2)}) collective-permute-start(bf16[512,512]{1,0:T(8,128)(2,1)S(1)} %pad_maximum_fusion.feats), channel_id=1, source_target_pairs={{0,1},{1,0},{2,3},{3,2},{4,5},{5,4},{6,7},{7,6},{8,9},{9,8},{10,11... | collective-permute-start | bytes 1572872 | tf_op jit(solution)/shard_map/ppermute | solution.py:295
  29.4 2.1 %collective-permute-start.8 = (bf16[512,512]{1,0:T(8,128)(2,1)S(1)}, bf16[512,512]{1,0:T(8,128)(2,1)S(1)}, u32[]{:S(2)}, u32[]{:S(2)}) collective-permute-start(bf16[512,512]{1,0:T(8,128)(2,1)S(1)} %aggregate_odd.1), channel_id=1, source_target_pairs={{0,1},{1,0},{2,3},{3,2},{4,5},{5,4},{6,7},{7,6},{8,9},{9,8},{10,11... | collective-permute-start | bytes 1572872 | tf_op jit(solution)/shard_map/ppermute | solution.py:295
  31.5 18.6 %copy-start.1 = (bf16[512,512]{1,0:T(8,128)(2,1)S(1)}, bf16[512,512]{1,0:T(8,128)(2,1)}, u32[]{:S(2)}) copy-start(bf16[512,512]{1,0:T(8,128)(2,1)} %wo.1) | copy-start | bytes 1572868
  31.5 18.6 %copy-start.3 = (bf16[32,512]{1,0:T(8,128)(2,1)S(1)}, bf16[32,512]{1,0:T(8,128)(2,1)}, u32[]{:S(2)}) copy-start(bf16[32,512]{1,0:T(8,128)(2,1)} %feat.1) | copy-start | bytes 98308
  31.5 18.6 %copy-start.4 = (f32[512]{0:T(512)S(1)}, f32[512]{0:T(512)}, u32[]{:S(2)}) copy-start(f32[512]{0:T(512)} %param.19) | copy-start | bytes 6148
  31.6 6.9 %collective-permute-start.9 = (bf16[128,512]{1,0:T(8,128)(2,1)S(1)}, bf16[128,512]{1,0:T(8,128)(2,1)S(1)}, u32[]{:S(2)}, u32[]{:S(2)}) collective-permute-start(bf16[128,512]{1,0:T(8,128)(2,1)S(1)} %get-tuple-element.30), channel_id=1, source_target_pairs={{0,6},{1,7},{2,4},{3,5},{4,2},{5,3},{6,0},{7,1},{8,14},{9,15},{10,... | collective-permute-start | bytes 393224 | tf_op jit(solution)/shard_map/ppermute | solution.py:295
  34.5 6.8 %collective-permute-start.10 = (bf16[128,512]{1,0:T(8,128)(2,1)S(1)}, bf16[128,512]{1,0:T(8,128)(2,1)S(1)}, u32[]{:S(2)}, u32[]{:S(2)}) collective-permute-start(bf16[128,512]{1,0:T(8,128)(2,1)S(1)} %get-tuple-element.31), channel_id=1, source_target_pairs={{0,4},{1,5},{2,6},{3,7},{4,0},{5,1},{6,2},{7,3},{8,12},{9,13},{10,... | collective-permute-start | bytes 393224 | tf_op jit(solution)/shard_map/ppermute | solution.py:295
  35.0 6.6 %collective-permute-start.11 = (bf16[128,512]{1,0:T(8,128)(2,1)S(1)}, bf16[128,512]{1,0:T(8,128)(2,1)S(1)}, u32[]{:S(2)}, u32[]{:S(2)}) collective-permute-start(bf16[128,512]{1,0:T(8,128)(2,1)S(1)} %get-tuple-element.32), channel_id=1, source_target_pairs={{0,2},{1,3},{2,0},{3,1},{4,6},{5,7},{6,4},{7,5},{8,10},{9,11},{10,... | collective-permute-start | bytes 393224 | tf_op jit(solution)/shard_map/ppermute | solution.py:295
  41.6 5.8 %collective-permute-start.12 = (bf16[32,512]{1,0:T(8,128)(2,1)S(1)}, bf16[32,512]{1,0:T(8,128)(2,1)S(1)}, u32[]{:S(2)}, u32[]{:S(2)}) collective-permute-start(bf16[32,512]{1,0:T(8,128)(2,1)S(1)} %get-tuple-element.34), channel_id=1, source_target_pairs={{0,24},{1,25},{2,26},{3,27},{4,28},{5,29},{6,30},{7,31},{8,16},{9,... | collective-permute-start | bytes 98312 | tf_op jit(solution)/shard_map/ppermute | solution.py:295
  45.3 4.8 %collective-permute-start.13 = (bf16[32,512]{1,0:T(8,128)(2,1)S(1)}, bf16[32,512]{1,0:T(8,128)(2,1)S(1)}, u32[]{:S(2)}, u32[]{:S(2)}) collective-permute-start(bf16[32,512]{1,0:T(8,128)(2,1)S(1)} %get-tuple-element.35), channel_id=1, source_target_pairs={{0,16},{1,17},{2,18},{3,19},{4,20},{5,21},{6,22},{7,23},{8,24},{9,... | collective-permute-start | bytes 98312 | tf_op jit(solution)/shard_map/ppermute | solution.py:295
  45.3 4.8 %collective-permute-start.14 = (bf16[32,512]{1,0:T(8,128)(2,1)S(1)}, bf16[32,512]{1,0:T(8,128)(2,1)S(1)}, u32[]{:S(2)}, u32[]{:S(2)}) collective-permute-start(bf16[32,512]{1,0:T(8,128)(2,1)S(1)} %get-tuple-element.36), channel_id=1, source_target_pairs={{0,8},{1,9},{2,10},{3,11},{4,12},{5,13},{6,14},{7,15},{8,0},{9,1},... | collective-permute-start | bytes 98312 | tf_op jit(solution)/shard_map/ppermute | solution.py:295

commit v7 on v6

--- a/solution.py
+++ b/solution.py
@@ -38,7 +38,7 @@
     blocks, block_len, _ = odd.shape
     parts = width // LANES
     pitch = table.shape[1]
-    words = block_len // 2
+    batch = 32
     flat = table.reshape(accounts * pitch, LANES)
     me = me_ref[0]
     chunks = sem.shape[0]
@@ -59,25 +59,21 @@
             first = pl.multiple_of(i * chunk + g * 16, 16)
             tile = acct[pl.ds(first, 16), :].astype(F32)
             for c in range(parts):
-                piece = tile[:, c * LANES : (c + 1) * LANES]
-                for twin in (c, c + parts):
-                    flat[pl.ds(first * pitch + twin, 16, stride=pitch), :] = piece
-
-    lower = lax.broadcasted_iota(jnp.int32, (pitch, LANES), 0) < parts
+                flat[pl.ds(first * pitch + c, 16, stride=pitch), :] = tile[
+                    :, c * LANES : (c + 1) * LANES
+                ]
 
     def collect(block, rows):
-        for k in range(words):
-            word = slots_ref[block, k]
-            rows[k * pitch : (k + 1) * pitch, :] = jnp.where(
-                lower, table[word & 0xFFFF], table[lax.shift_right_logical(word, 16)]
-            )
+        for k in range(0, block_len, batch):
+            found = [table[slots_ref[block, k + u], :parts, :] for u in range(batch)]
+            for u in range(batch):
+                rows[(k + u) * parts : (k + u + 1) * parts, :] = found[u]
 
     def emit(i, rows, out):
         for c in range(parts):
-            for h in range(2):
-                out[i, h * words : (h + 1) * words, c * LANES : (c + 1) * LANES] = rows[
-                    pl.ds(h * parts + c, words, stride=pitch), :
-                ].astype(BF16)
+            out[i, :, c * LANES : (c + 1) * LANES] = rows[
+                pl.ds(c, block_len, stride=parts), :
+            ].astype(BF16)
 
     @pl.loop(0, blocks)
     def _(i):
@@ -91,10 +87,9 @@
 def gather(outer, me, slots, acct):
     blocks, block_len = slots.shape
     accounts, width = acct.shape
-    words = block_len // 2
-    packed = slots[:, :words] | (slots[:, words:] << 16)
-    pitch = 2 * width // LANES
-    rows = pltpu.VMEM((words * pitch, LANES), F32)
+    parts = width // LANES
+    pitch = -(-parts // 8) * 8
+    rows = pltpu.VMEM((block_len * parts, LANES), F32)
     half = jax.ShapeDtypeStruct((blocks // 2, block_len, width), BF16)
     return pl.pallas_call(
         functools.partial(gather_kernel, outer),
@@ -111,7 +106,7 @@
         compiler_params=_mb(47 if blocks <= 32 else 28),
         cost_estimate=_cost(0, 20 * 2**20),
         name="gather_slots",
-    )(me, packed, acct)
+    )(me, slots, acct)
 
 
 def project_kernel(outer, shifts, me_ref, rel_ref, kw, mw, *refs):
@@ -124,7 +119,7 @@
         relation = rel_ref[jnp.bitwise_xor(me, _offset(i, outer) + shift)]
         for n in range(0, width, half):
             key = jnp.dot(feats[i], kw[relation, :, n : n + half], preferred_element_type=F32)
-            keys[i, n : n + half, :] = key.astype(BF16).T
+            keys[i, :, n : n + half] = key.astype(BF16)
             value = jnp.dot(feats[i], mw[relation, :, n : n + half], preferred_element_type=F32)
             values[i, :, n : n + half] = value.astype(BF16)
 
@@ -136,8 +131,7 @@
 
 def project(outer, shifts, me, rel, feats, kw, mw):
     blocks, block_len, width = feats[0].shape
-    keys = jax.ShapeDtypeStruct((blocks, width, block_len), BF16)
-    values = jax.ShapeDtypeStruct((blocks, block_len, width), BF16)
+    keys = values = jax.ShapeDtypeStruct(feats[0].shape, BF16)
     return pl.pallas_call(
         functools.partial(project_kernel, outer, shifts),
         out_shape=(keys, values) * len(shifts),
@@ -153,9 +147,9 @@
 
 def aggregate_kernel(
     outer, shift, me_ref, rel_ref, count_ref, bias_ref, merch_slot, feats, wq, keys, values,
-    sums, query, gates,
+    sums, query,
 ):
-    blocks, width, block_len = keys.shape
+    blocks, block_len, width = keys.shape
     merchants = feats.shape[0] // blocks
     me = me_ref[0]
     row = lax.broadcasted_iota(jnp.int32, (merchants, block_len), 0)
@@ -163,37 +157,32 @@
     query[...] = jnp.dot(feats[...], wq[...], preferred_element_type=F32).astype(BF16)
     for i in range(blocks):
         block = jnp.bitwise_xor(me, _offset(i, outer) + shift)
-        score = jnp.dot(
-            query[i * merchants : (i + 1) * merchants, :], keys[i], preferred_element_type=F32
-        ) / math.sqrt(width)
-        score = score + bias_ref[rel_ref[block]]
+        part = slice(i * merchants, (i + 1) * merchants)
         mine = (merch_slot[pl.ds(block, 1), :] == row) & (lane < count_ref[block])
-        gates[i * merchants : (i + 1) * merchants, :] = jnp.where(
-            mine, jax.nn.sigmoid(score), 0.0
-        ).astype(BF16)
-    for i in range(blocks):
-        sums[i * merchants : (i + 1) * merchants, :] = jnp.dot(
-            gates[i * merchants : (i + 1) * merchants, :], values[i], preferred_element_type=F32
+        mine = jnp.where(mine, 1.0, 0.0)
+        queries = jnp.dot(mine.T.astype(BF16), query[part, :], preferred_element_type=F32)
+        score = jnp.sum(keys[i].astype(F32) * queries, axis=1, keepdims=True) / math.sqrt(width)
+        gate = jax.nn.sigmoid(score + bias_ref[rel_ref[block]])
+        message = (gate * values[i].astype(F32)).astype(BF16)
+        sums[part, :] = jnp.dot(
+            mine.astype(BF16), message, preferred_element_type=F32
         ).astype(sums.dtype)
 
 
 def aggregate(outer, shift, me, rel, count, bias, merch_slot, feats, wq, keys, values, dtype):
-    blocks, width, block_len = keys.shape
-    merchants = feats.shape[0] // blocks
+    blocks, block_len, width = keys.shape
+    rows = feats.shape[0]
     return pl.pallas_call(
         functools.partial(aggregate_kernel, outer, shift),
         out_shape=jax.ShapeDtypeStruct(feats.shape, dtype),
         in_specs=[SMEM] * 4 + [VMEM] * 5,
         out_specs=VMEM,
-        scratch_shapes=[
-            pltpu.VMEM(feats.shape, BF16),
-            pltpu.VMEM((feats.shape[0], block_len), BF16),
-        ],
+        scratch_shapes=[pltpu.VMEM(feats.shape, BF16)],
         compiler_params=_mb(6),
         cost_estimate=_cost(
-            4 * blocks * merchants * block_len * width + 2 * feats.shape[0] * width * width,
+            4 * rows * block_len * width + 2 * rows * width * width,
             6 * 2**20,
-            blocks * merchants * block_len,
+            blocks * block_len,
         ),
         name="aggregate_odd" if shift else "aggregate_even",
     )(me, rel, count, bias, merch_slot, feats, wq, keys, values)

time: 51.3 us -> 56.1 us (1.094)
  Pallas kernels: 21.9 us -> 27.3 us
  other arithmetic: 0.92 us -> 0.05 us
  local copies, waits for them, and re-layouts: 0.05 us -> 0.76 us
    pallas_call x2, Pallas kernels: 3.07 us -> 10.4 us  [aggregate(): pl.pallas_call(functools.partial(aggregate_kernel, outer, shift), out_sha...]
    pallas_call x1, Pallas kernels: 10.9 us -> 9.21 us  [gather(): pl.pallas_call(functools.partial(gather_kernel, outer), out_shape=(half,...]
    or x1 -> x0, other arithmetic: 0.87 us -> none  [gather(): packed = slots[:, :words] | slots[:, words:] << 16]
    unnamed x20 -> x22, local copies, waits for them, and re-layouts: 0.05 us -> 0.76 us
  transfers between devices with their start and end apart: 15 -> 15, of which waited for: 5 -> 5; matrix products, arithmetic and copies ran while one was open for 2% -> 0% of each run, Pallas kernels for 41% -> 47%
where the time goes in v7:
time: 56.1 us; the launch traced here: 55.9 us
  Pallas kernels  27.3 us (49%)
  starting transfers between devices  17.4 us (31%)
  waiting for transfers between devices  10.1 us (18%)
  local copies, waits for them, and re-layouts  0.76 us (1%)
    ppermute x15, starting transfers between devices, swap(): return lax.ppermute(value, AXES, [(s, s ^ mask) for s in range(devices)])  17.4 us
    pallas_call x2, Pallas kernels, aggregate(): pl.pallas_call(functools.partial(aggregate_kernel, outer, shift), out_sha...  10.4 us
    ppermute x15, waiting for transfers between devices, swap(): return lax.ppermute(value, AXES, [(s, s ^ mask) for s in range(devices)])  10.1 us
    pallas_call x1, Pallas kernels, gather(): pl.pallas_call(functools.partial(gather_kernel, outer), out_shape=(half,...  9.21 us
    pallas_call x1, Pallas kernels, project(): pl.pallas_call(functools.partial(project_kernel, outer, shifts), out_shap...  6.61 us
  transfers between devices with their start and end apart: 15, of which 5 were waited for; matrix products, arithmetic and copies ran while one was open for 0% of the time, Pallas kernels for 47%

profile of v7, /device:TPU:0, one launch (start us, length us, event | category | flops | bytes accessed | tf_op | source)
XLA Modules:
  0.0 55.9 jit_solution(17021567310637678788)
XLA Ops:
  0.0 3.5 %collective-permute-start.2 = (bf16[32,512]{1,0:T(8,128)(2,1)}, bf16[32,512]{1,0:T(8,128)(2,1)S(1)}, u32[]{:S(2)}, u32[]{:S(2)}) collective-permute-start(bf16[32,512]{1,0:T(8,128)(2,1)} %feat.1), channel_id=1, source_target_pairs={{0,17},{1,16},{2,19},{3,18},{4,21},{5,20},{6,23},{7,22},{8,25},{9,... | collective-permute-start | bytes 98312 | tf_op jit(solution)/shard_map/ppermute | solution.py:284
  3.5 1.9 %collective-permute-start.1 = (bf16[32,512]{1,0:T(8,128)(2,1)}, bf16[32,512]{1,0:T(8,128)(2,1)S(1)}, u32[]{:S(2)}, u32[]{:S(2)}) collective-permute-start(bf16[32,512]{1,0:T(8,128)(2,1)} %feat.1), channel_id=1, source_target_pairs={{0,9},{1,8},{2,11},{3,10},{4,13},{5,12},{6,15},{7,14},{8,1},{9,0},... | collective-permute-start | bytes 98312 | tf_op jit(solution)/shard_map/ppermute | solution.py:284
  5.3 0.0 collective-permute-start
  5.3 0.0 collective-permute-start.3
  5.3 0.7 %copy-done.4 = s32[32,128]{1,0:T(8,128)S(1)} copy-done((s32[32,128]{1,0:T(8,128)S(1)}, s32[32,128]{1,0:T(8,128)}, u32[]{:S(2)}) %copy-start.4) | copy-done | bytes 16408
  6.1 9.2 %gather_slots.1 = (bf16[16,128,512]{2,1,0:T(8,128)(2,1)S(1)}, bf16[16,128,512]{2,1,0:T(8,128)(2,1)S(1)}) custom-call(s32[1]{0:T(128)} %bitcast.1.me_ref, s32[32,128]{1,0:T(8,128)S(1)} %copy-done.4, bf16[4096,512]{1,0:T(8,128)(2,1)} %acct_hbm.1), custom_call_target="tpu_custom_call" | custom-call | bytes 20971520 | tf_op jit(solution)/shard_map/gather_slots/pallas_call | solution.py:94
  15.3 2.8 %collective-permute-start.6 = (bf16[128,512]{1,0:T(8,128)(2,1)S(1)}, bf16[128,512]{1,0:T(8,128)(2,1)S(1)}, u32[]{:S(2)}, u32[]{:S(2)}) collective-permute-start(bf16[128,512]{1,0:T(8,128)(2,1)S(1)} %pad_maximum_fusion.1), channel_id=1, source_target_pairs={{0,6},{1,7},{2,4},{3,5},{4,2},{5,3},{6,0},{7,1},{8,14},{9,15},{10,... | collective-permute-start | bytes 393224 | tf_op jit(solution)/shard_map/ppermute | solution.py:284
  18.2 0.5 collective-permute-start.5
  18.7 0.2 collective-permute-start.4
  18.9 0.0 copy-start.2
  18.9 0.0 copy-start.7
  18.9 0.0 copy-start.8
  19.0 6.6 %project_slots.1 = (bf16[16,128,512]{2,1,0:T(8,128)(2,1)S(1)}, bf16[16,128,512]{2,1,0:T(8,128)(2,1)S(1)}, bf16[16,128,512]{2,1,0:T(8,128)(2,1)S(1)}, bf16[16,128,512]{2,1,0:T(8,128)(2,1)S(1)}) custom-call(s32[1]{0:T(128)} %bitcast.1.me_ref, s32[32]{0:T(128)S(1)} %copy-done.6, bf16[4,512,512]{2,1,0:T(8,128)(2,1)S(1)} %copy-done.9, ...), custom_call_target="tpu_custom_call" | custom-call | flops 4294967296 | bytes 16777216 | tf_op jit(solution)/shard_map/project_slots/pallas_call | solution.py:135
  25.6 0.1 collective-permute-start.7
  25.8 5.2 %aggregate_odd.1 = bf16[512,512]{1,0:T(8,128)(2,1)S(1)} custom-call(s32[1]{0:T(128)} %bitcast.1.me_ref, s32[32]{0:T(128)S(1)} %copy-done.6, s32[32]{0:T(128)S(1)} %copy-done.7, f32[4]{0:T(128)S(1)} %copy-done.8, s32[32,128]{1,0:T(8,128)S(1)} %copy-done.2, bf16[512,512]{1,0:T(8,128)(2,1)S(1)} %pad_maximum_fusion.feats, bf16[512,512]{1,0:T(8,128)(2,1)S(1)} %copy-done, ...), custom_call_target="tpu_custom_call" | custom-call | flops 402653184 | bytes 6291456 | tf_op jit(solution)/shard_map/aggregate_odd/pallas_call | solution.py:175
  31.0 0.5 collective-permute-start.8
  31.4 5.2 %aggregate_even.1.mine = f32[512,512]{1,0:T(8,128)S(1)} custom-call(s32[1]{0:T(128)} %bitcast.1.me_ref, s32[32]{0:T(128)S(1)} %copy-done.6, s32[32]{0:T(128)S(1)} %copy-done.7, f32[4]{0:T(128)S(1)} %copy-done.8, s32[32,128]{1,0:T(8,128)S(1)} %copy-done.2, bf16[512,512]{1,0:T(8,128)(2,1)S(1)} %collective-permute-done.7.feats, bf16[512,512]{1,0:T(8,128)(2,1)S(1)} %copy-done, ...), custom_call_target="tpu_custom_call" | custom-call | flops 402653184 | bytes 6291456 | tf_op jit(solution)/shard_map/aggregate_even/pallas_call | solution.py:175
  36.6 0.0 copy-start.3
  36.7 0.0 copy-start.5
  36.7 0.1 combine_cores.1
  36.8 2.8 %collective-permute-start.9 = (bf16[128,512]{1,0:T(8,128)(2,1)S(1)}, bf16[128,512]{1,0:T(8,128)(2,1)S(1)}, u32[]{:S(2)}, u32[]{:S(2)}) collective-permute-start(bf16[128,512]{1,0:T(8,128)(2,1)S(1)} %get-tuple-element.30), channel_id=1, source_target_pairs={{0,6},{1,7},{2,4},{3,5},{4,2},{5,3},{6,0},{7,1},{8,14},{9,15},{10,... | collective-permute-start | bytes 393224 | tf_op jit(solution)/shard_map/ppermute | solution.py:284
  39.6 0.5 collective-permute-start.10
  40.1 0.2 collective-permute-start.11
  40.3 3.2 %collective-permute-done.9.refs_1_ = bf16[128,512]{1,0:T(8,128)(2,1)S(1)} collective-permute-done((bf16[128,512]{1,0:T(8,128)(2,1)S(1)}, bf16[128,512]{1,0:T(8,128)(2,1)S(1)}, u32[]{:S(2)}, u32[]{:S(2)}) %collective-permute-start.9) | collective-permute-done | bytes 131104 | tf_op jit(solution)/shard_map/ppermute | solution.py:284
  43.6 2.6 %collective-permute-done.10.refs_2_ = bf16[128,512]{1,0:T(8,128)(2,1)S(1)} collective-permute-done((bf16[128,512]{1,0:T(8,128)(2,1)S(1)}, bf16[128,512]{1,0:T(8,128)(2,1)S(1)}, u32[]{:S(2)}, u32[]{:S(2)}) %collective-permute-start.10) | collective-permute-done | bytes 131104 | tf_op jit(solution)/shard_map/ppermute | solution.py:284
  46.1 0.3 collective-permute-done.11.refs_3_
  46.4 0.1 combine_plane.1
  46.5 3.7 %collective-permute-start.12 = (bf16[32,512]{1,0:T(8,128)(2,1)S(1)}, bf16[32,512]{1,0:T(8,128)(2,1)S(1)}, u32[]{:S(2)}, u32[]{:S(2)}) collective-permute-start(bf16[32,512]{1,0:T(8,128)(2,1)S(1)} %get-tuple-element.34), channel_id=1, source_target_pairs={{0,24},{1,25},{2,26},{3,27},{4,28},{5,29},{6,30},{7,31},{8,16},{9,... | collective-permute-start | bytes 98312 | tf_op jit(solution)/shard_map/ppermute | solution.py:284
  50.1 0.8 %collective-permute-start.14 = (bf16[32,512]{1,0:T(8,128)(2,1)S(1)}, bf16[32,512]{1,0:T(8,128)(2,1)S(1)}, u32[]{:S(2)}, u32[]{:S(2)}) collective-permute-start(bf16[32,512]{1,0:T(8,128)(2,1)S(1)} %get-tuple-element.36), channel_id=1, source_target_pairs={{0,8},{1,9},{2,10},{3,11},{4,12},{5,13},{6,14},{7,15},{8,0},{9,1},... | collective-permute-start | bytes 98312 | tf_op jit(solution)/shard_map/ppermute | solution.py:284
  50.9 1.3 %collective-permute-done.12.refs_1_ = bf16[32,512]{1,0:T(8,128)(2,1)S(1)} collective-permute-done((bf16[32,512]{1,0:T(8,128)(2,1)S(1)}, bf16[32,512]{1,0:T(8,128)(2,1)S(1)}, u32[]{:S(2)}, u32[]{:S(2)}) %collective-permute-start.12) | collective-permute-done | bytes 32800 | tf_op jit(solution)/shard_map/ppermute | solution.py:284
  52.2 2.7 %collective-permute-done.13.refs_2_ = bf16[32,512]{1,0:T(8,128)(2,1)S(1)} collective-permute-done((bf16[32,512]{1,0:T(8,128)(2,1)S(1)}, bf16[32,512]{1,0:T(8,128)(2,1)S(1)}, u32[]{:S(2)}, u32[]{:S(2)}) %collective-permute-start.13) | collective-permute-done | bytes 32800 | tf_op jit(solution)/shard_map/ppermute | solution.py:284
  55.0 0.9 %finish.1 = bf16[32,512]{1,0:T(8,128)(2,1)} custom-call(bf16[32,512]{1,0:T(8,128)(2,1)S(1)} %copy-done.3, f32[1,512]{1,0:T(1,128)S(1)} %bitcast.2, bf16[512,512]{1,0:T(8,128)(2,1)S(1)} %copy-done.1, f32[32,512]{1,0:T(8,128)S(1)} %get-tuple-element.33.refs_0_, bf16[32,512]{1,0:T(8,128)(2,1)S(1)} %collective-permute-done.12.refs_1_, ...), custom_call_target="tpu_custom_call" | custom-call | tf_op jit(solution)/shard_map/finish/pallas_call | solution.py:254
  (29 shorter events, 0.1 us)
Async XLA Ops:
  0.0 15.3 %collective-permute-start.2 = (bf16[32,512]{1,0:T(8,128)(2,1)}, bf16[32,512]{1,0:T(8,128)(2,1)S(1)}, u32[]{:S(2)}, u32[]{:S(2)}) collective-permute-start(bf16[32,512]{1,0:T(8,128)(2,1)} %feat.1), channel_id=1, source_target_pairs={{0,17},{1,16},{2,19},{3,18},{4,21},{5,20},{6,23},{7,22},{8,25},{9,... | collective-permute-start | bytes 98312 | tf_op jit(solution)/shard_map/ppermute | solution.py:284
  3.5 11.8 %collective-permute-start.1 = (bf16[32,512]{1,0:T(8,128)(2,1)}, bf16[32,512]{1,0:T(8,128)(2,1)S(1)}, u32[]{:S(2)}, u32[]{:S(2)}) collective-permute-start(bf16[32,512]{1,0:T(8,128)(2,1)} %feat.1), channel_id=1, source_target_pairs={{0,9},{1,8},{2,11},{3,10},{4,13},{5,12},{6,15},{7,14},{8,1},{9,0},... | collective-permute-start | bytes 98312 | tf_op jit(solution)/shard_map/ppermute | solution.py:284
  5.3 10.0 %collective-permute-start = (bf16[32,512]{1,0:T(8,128)(2,1)}, bf16[32,512]{1,0:T(8,128)(2,1)S(1)}, u32[]{:S(2)}, u32[]{:S(2)}) collective-permute-start(bf16[32,512]{1,0:T(8,128)(2,1)} %feat.1), channel_id=1, source_target_pairs={{0,1},{1,0},{2,3},{3,2},{4,5},{5,4},{6,7},{7,6},{8,9},{9,8},{10,11... | collective-permute-start | bytes 98312 | tf_op jit(solution)/shard_map/ppermute | solution.py:284
  5.3 10.0 %collective-permute-start.3 = (bf16[32,512]{1,0:T(8,128)(2,1)}, bf16[32,512]{1,0:T(8,128)(2,1)S(1)}, u32[]{:S(2)}, u32[]{:S(2)}) collective-permute-start(bf16[32,512]{1,0:T(8,128)(2,1)} %feat.1), channel_id=1, source_target_pairs={{0,25},{1,24},{2,27},{3,26},{4,29},{5,28},{6,31},{7,30},{8,17},{9,... | collective-permute-start | bytes 98312 | tf_op jit(solution)/shard_map/ppermute | solution.py:284
  5.3 0.7 %copy-start.4 = (s32[32,128]{1,0:T(8,128)S(1)}, s32[32,128]{1,0:T(8,128)}, u32[]{:S(2)}) copy-start(s32[32,128]{1,0:T(8,128)} %slots_ref.1) | copy-start | bytes 49156
  6.1 12.8 %copy-start.6 = (s32[32]{0:T(128)S(1)}, s32[32]{0:T(128)}, u32[]{:S(2)}) copy-start(s32[32]{0:T(128)} %rel_ref.5) | copy-start | bytes 388
  6.1 12.8 %copy-start.9 = (bf16[4,512,512]{2,1,0:T(8,128)(2,1)S(1)}, bf16[4,512,512]{2,1,0:T(8,128)(2,1)}, u32[]{:S(2)}) copy-start(bf16[4,512,512]{2,1,0:T(8,128)(2,1)} %kw.1) | copy-start | bytes 6291460
  6.1 12.8 %copy-start.10 = (bf16[4,512,512]{2,1,0:T(8,128)(2,1)S(1)}, bf16[4,512,512]{2,1,0:T(8,128)(2,1)}, u32[]{:S(2)}) copy-start(bf16[4,512,512]{2,1,0:T(8,128)(2,1)} %mw.1) | copy-start | bytes 6291460
  15.3 10.2 %collective-permute-start.6 = (bf16[128,512]{1,0:T(8,128)(2,1)S(1)}, bf16[128,512]{1,0:T(8,128)(2,1)S(1)}, u32[]{:S(2)}, u32[]{:S(2)}) collective-permute-start(bf16[128,512]{1,0:T(8,128)(2,1)S(1)} %pad_maximum_fusion.1), channel_id=1, source_target_pairs={{0,6},{1,7},{2,4},{3,5},{4,2},{5,3},{6,0},{7,1},{8,14},{9,15},{10,... | collective-permute-start | bytes 393224 | tf_op jit(solution)/shard_map/ppermute | solution.py:284
  18.2 7.4 %collective-permute-start.5 = (bf16[128,512]{1,0:T(8,128)(2,1)S(1)}, bf16[128,512]{1,0:T(8,128)(2,1)S(1)}, u32[]{:S(2)}, u32[]{:S(2)}) collective-permute-start(bf16[128,512]{1,0:T(8,128)(2,1)S(1)} %pad_maximum_fusion.1), channel_id=1, source_target_pairs={{0,4},{1,5},{2,6},{3,7},{4,0},{5,1},{6,2},{7,3},{8,12},{9,13},{10,... | collective-permute-start | bytes 393224 | tf_op jit(solution)/shard_map/ppermute | solution.py:284
  18.7 6.9 %collective-permute-start.4 = (bf16[128,512]{1,0:T(8,128)(2,1)S(1)}, bf16[128,512]{1,0:T(8,128)(2,1)S(1)}, u32[]{:S(2)}, u32[]{:S(2)}) collective-permute-start(bf16[128,512]{1,0:T(8,128)(2,1)S(1)} %pad_maximum_fusion.1), channel_id=1, source_target_pairs={{0,2},{1,3},{2,0},{3,1},{4,6},{5,7},{6,4},{7,5},{8,10},{9,11},{10,... | collective-permute-start | bytes 393224 | tf_op jit(solution)/shard_map/ppermute | solution.py:284
  18.9 6.8 %copy-start = (bf16[512,512]{1,0:T(8,128)(2,1)S(1)}, bf16[512,512]{1,0:T(8,128)(2,1)}, u32[]{:S(2)}) copy-start(bf16[512,512]{1,0:T(8,128)(2,1)} %wq.3) | copy-start | bytes 1572868
  18.9 6.8 %copy-start.2 = (s32[32,128]{1,0:T(8,128)S(1)}, s32[32,128]{1,0:T(8,128)}, u32[]{:S(2)}) copy-start(s32[32,128]{1,0:T(8,128)} %merch_slot.3) | copy-start | bytes 49156
  18.9 6.8 %copy-start.7 = (s32[32]{0:T(128)S(1)}, s32[32]{0:T(128)}, u32[]{:S(2)}) copy-start(s32[32]{0:T(128)} %count_ref.3) | copy-start | bytes 388
  18.9 6.8 %copy-start.8 = (f32[4]{0:T(128)S(1)}, f32[4]{0:T(128)}, u32[]{:S(2)}) copy-start(f32[4]{0:T(128)} %bias_ref.3) | copy-start | bytes 52
  25.6 5.8 %collective-permute-start.7 = (bf16[512,512]{1,0:T(8,128)(2,1)S(1)}, bf16[512,512]{1,0:T(8,128)(2,1)S(1)}, u32[]{:S(2)}, u32[]{:S(2)}) collective-permute-start(bf16[512,512]{1,0:T(8,128)(2,1)S(1)} %pad_maximum_fusion.feats), channel_id=1, source_target_pairs={{0,1},{1,0},{2,3},{3,2},{4,5},{5,4},{6,7},{7,6},{8,9},{9,8},{10,11... | collective-permute-start | bytes 1572872 | tf_op jit(solution)/shard_map/ppermute | solution.py:284
  31.0 5.7 %collective-permute-start.8 = (bf16[512,512]{1,0:T(8,128)(2,1)S(1)}, bf16[512,512]{1,0:T(8,128)(2,1)S(1)}, u32[]{:S(2)}, u32[]{:S(2)}) collective-permute-start(bf16[512,512]{1,0:T(8,128)(2,1)S(1)} %aggregate_odd.1), channel_id=1, source_target_pairs={{0,1},{1,0},{2,3},{3,2},{4,5},{5,4},{6,7},{7,6},{8,9},{9,8},{10,11... | collective-permute-start | bytes 1572872 | tf_op jit(solution)/shard_map/ppermute | solution.py:284
  36.6 18.3 %copy-start.1 = (bf16[512,512]{1,0:T(8,128)(2,1)S(1)}, bf16[512,512]{1,0:T(8,128)(2,1)}, u32[]{:S(2)}) copy-start(bf16[512,512]{1,0:T(8,128)(2,1)} %wo.1) | copy-start | bytes 1572868
  36.6 18.3 %copy-start.3 = (bf16[32,512]{1,0:T(8,128)(2,1)S(1)}, bf16[32,512]{1,0:T(8,128)(2,1)}, u32[]{:S(2)}) copy-start(bf16[32,512]{1,0:T(8,128)(2,1)} %feat.1) | copy-start | bytes 98308
  36.7 18.3 %copy-start.5 = (f32[512]{0:T(512)S(1)}, f32[512]{0:T(512)}, u32[]{:S(2)}) copy-start(f32[512]{0:T(512)} %param.19) | copy-start | bytes 6148
  36.8 6.8 %collective-permute-start.9 = (bf16[128,512]{1,0:T(8,128)(2,1)S(1)}, bf16[128,512]{1,0:T(8,128)(2,1)S(1)}, u32[]{:S(2)}, u32[]{:S(2)}) collective-permute-start(bf16[128,512]{1,0:T(8,128)(2,1)S(1)} %get-tuple-element.30), channel_id=1, source_target_pairs={{0,6},{1,7},{2,4},{3,5},{4,2},{5,3},{6,0},{7,1},{8,14},{9,15},{10,... | collective-permute-start | bytes 393224 | tf_op jit(solution)/shard_map/ppermute | solution.py:284
  39.6 6.5 %collective-permute-start.10 = (bf16[128,512]{1,0:T(8,128)(2,1)S(1)}, bf16[128,512]{1,0:T(8,128)(2,1)S(1)}, u32[]{:S(2)}, u32[]{:S(2)}) collective-permute-start(bf16[128,512]{1,0:T(8,128)(2,1)S(1)} %get-tuple-element.31), channel_id=1, source_target_pairs={{0,4},{1,5},{2,6},{3,7},{4,0},{5,1},{6,2},{7,3},{8,12},{9,13},{10,... | collective-permute-start | bytes 393224 | tf_op jit(solution)/shard_map/ppermute | solution.py:284
  40.1 6.3 %collective-permute-start.11 = (bf16[128,512]{1,0:T(8,128)(2,1)S(1)}, bf16[128,512]{1,0:T(8,128)(2,1)S(1)}, u32[]{:S(2)}, u32[]{:S(2)}) collective-permute-start(bf16[128,512]{1,0:T(8,128)(2,1)S(1)} %get-tuple-element.32), channel_id=1, source_target_pairs={{0,2},{1,3},{2,0},{3,1},{4,6},{5,7},{6,4},{7,5},{8,10},{9,11},{10,... | collective-permute-start | bytes 393224 | tf_op jit(solution)/shard_map/ppermute | solution.py:284
  46.5 5.8 %collective-permute-start.12 = (bf16[32,512]{1,0:T(8,128)(2,1)S(1)}, bf16[32,512]{1,0:T(8,128)(2,1)S(1)}, u32[]{:S(2)}, u32[]{:S(2)}) collective-permute-start(bf16[32,512]{1,0:T(8,128)(2,1)S(1)} %get-tuple-element.34), channel_id=1, source_target_pairs={{0,24},{1,25},{2,26},{3,27},{4,28},{5,29},{6,30},{7,31},{8,16},{9,... | collective-permute-start | bytes 98312 | tf_op jit(solution)/shard_map/ppermute | solution.py:284
  50.1 4.8 %collective-permute-start.13 = (bf16[32,512]{1,0:T(8,128)(2,1)S(1)}, bf16[32,512]{1,0:T(8,128)(2,1)S(1)}, u32[]{:S(2)}, u32[]{:S(2)}) collective-permute-start(bf16[32,512]{1,0:T(8,128)(2,1)S(1)} %get-tuple-element.35), channel_id=1, source_target_pairs={{0,16},{1,17},{2,18},{3,19},{4,20},{5,21},{6,22},{7,23},{8,24},{9,... | collective-permute-start | bytes 98312 | tf_op jit(solution)/shard_map/ppermute | solution.py:284
  50.1 4.8 %collective-permute-start.14 = (bf16[32,512]{1,0:T(8,128)(2,1)S(1)}, bf16[32,512]{1,0:T(8,128)(2,1)S(1)}, u32[]{:S(2)}, u32[]{:S(2)}) collective-permute-start(bf16[32,512]{1,0:T(8,128)(2,1)S(1)} %get-tuple-element.36), channel_id=1, source_target_pairs={{0,8},{1,9},{2,10},{3,11},{4,12},{5,13},{6,14},{7,15},{8,0},{9,1},... | collective-permute-start | bytes 98312 | tf_op jit(solution)/shard_map/ppermute | solution.py:284

commit v8 on v6

--- a/solution.py
+++ b/solution.py
@@ -38,7 +38,7 @@
     blocks, block_len, _ = odd.shape
     parts = width // LANES
     pitch = table.shape[1]
-    words = block_len // 2
+    batch = 16
     flat = table.reshape(accounts * pitch, LANES)
     me = me_ref[0]
     chunks = sem.shape[0]
@@ -59,25 +59,21 @@
             first = pl.multiple_of(i * chunk + g * 16, 16)
             tile = acct[pl.ds(first, 16), :].astype(F32)
             for c in range(parts):
-                piece = tile[:, c * LANES : (c + 1) * LANES]
-                for twin in (c, c + parts):
-                    flat[pl.ds(first * pitch + twin, 16, stride=pitch), :] = piece
-
-    lower = lax.broadcasted_iota(jnp.int32, (pitch, LANES), 0) < parts
+                flat[pl.ds(first * pitch + c, 16, stride=pitch), :] = tile[
+                    :, c * LANES : (c + 1) * LANES
+                ]
 
     def collect(block, rows):
-        for k in range(words):
-            word = slots_ref[block, k]
-            rows[k * pitch : (k + 1) * pitch, :] = jnp.where(
-                lower, table[word & 0xFFFF], table[lax.shift_right_logical(word, 16)]
-            )
+        for k in range(0, block_len, batch):
+            found = [table[slots_ref[block, k + u], :parts, :] for u in range(batch)]
+            for u in range(batch):
+                rows[pl.ds(k + u, parts, stride=block_len), :] = found[u]
 
     def emit(i, rows, out):
         for c in range(parts):
-            for h in range(2):
-                out[i, h * words : (h + 1) * words, c * LANES : (c + 1) * LANES] = rows[
-                    pl.ds(h * parts + c, words, stride=pitch), :
-                ].astype(BF16)
+            out[i, :, c * LANES : (c + 1) * LANES] = rows[
+                c * block_len : (c + 1) * block_len, :
+            ].astype(BF16)
 
     @pl.loop(0, blocks)
     def _(i):
@@ -91,10 +87,9 @@
 def gather(outer, me, slots, acct):
     blocks, block_len = slots.shape
     accounts, width = acct.shape
-    words = block_len // 2
-    packed = slots[:, :words] | (slots[:, words:] << 16)
-    pitch = 2 * width // LANES
-    rows = pltpu.VMEM((words * pitch, LANES), F32)
+    parts = width // LANES
+    pitch = -(-parts // 8) * 8
+    rows = pltpu.VMEM((block_len * parts, LANES), F32)
     half = jax.ShapeDtypeStruct((blocks // 2, block_len, width), BF16)
     return pl.pallas_call(
         functools.partial(gather_kernel, outer),
@@ -111,7 +106,7 @@
         compiler_params=_mb(47 if blocks <= 32 else 28),
         cost_estimate=_cost(0, 20 * 2**20),
         name="gather_slots",
-    )(me, packed, acct)
+    )(me, slots, acct)
 
 
 def project_kernel(outer, shifts, me_ref, rel_ref, kw, mw, *refs):

time: 51.3 us -> 52.9 us (1.031)
  Pallas kernels: 21.9 us -> 23.7 us
  other arithmetic: 0.92 us -> 0.05 us
  local copies, waits for them, and re-layouts: 0.05 us -> 0.77 us
    pallas_call x1, Pallas kernels: 10.9 us -> 12.7 us  [gather(): pl.pallas_call(functools.partial(gather_kernel, outer), out_shape=(half,...]
    or x1 -> x0, other arithmetic: 0.87 us -> none  [gather(): packed = slots[:, :words] | slots[:, words:] << 16]
    unnamed x20 -> x22, local copies, waits for them, and re-layouts: 0.05 us -> 0.77 us
  transfers between devices with their start and end apart: 15 -> 15, of which waited for: 5 -> 5; matrix products, arithmetic and copies ran while one was open for 2% -> 0% of each run, Pallas kernels for 41% -> 43%
where the time goes in v8:
time: 52.9 us; the launch traced here: 52.6 us
  Pallas kernels  23.7 us (45%)
  starting transfers between devices  17.5 us (33%)
  waiting for transfers between devices  10.4 us (20%)
  local copies, waits for them, and re-layouts  0.77 us (1%)
    ppermute x15, starting transfers between devices, swap(): return lax.ppermute(value, AXES, [(s, s ^ mask) for s in range(devices)])  17.5 us
    pallas_call x1, Pallas kernels, gather(): pl.pallas_call(functools.partial(gather_kernel, outer), out_shape=(half,...  12.7 us
    ppermute x15, waiting for transfers between devices, swap(): return lax.ppermute(value, AXES, [(s, s ^ mask) for s in range(devices)])  10.4 us
    pallas_call x1, Pallas kernels, project(): pl.pallas_call(functools.partial(project_kernel, outer, shifts), out_shap...  6.86 us
    pallas_call x2, Pallas kernels, aggregate(): pl.pallas_call(functools.partial(aggregate_kernel, outer, shift), out_sha...  3.07 us
  transfers between devices with their start and end apart: 15, of which 5 were waited for; matrix products, arithmetic and copies ran while one was open for 0% of the time, Pallas kernels for 43%

profile of v8, /device:TPU:0, one launch (start us, length us, event | category | flops | bytes accessed | tf_op | source)
XLA Modules:
  0.0 52.6 jit_solution(2178210232040923792)
XLA Ops:
  0.0 3.5 %collective-permute-start.2 = (bf16[32,512]{1,0:T(8,128)(2,1)}, bf16[32,512]{1,0:T(8,128)(2,1)S(1)}, u32[]{:S(2)}, u32[]{:S(2)}) collective-permute-start(bf16[32,512]{1,0:T(8,128)(2,1)} %feat.1), channel_id=1, source_target_pairs={{0,17},{1,16},{2,19},{3,18},{4,21},{5,20},{6,23},{7,22},{8,25},{9,... | collective-permute-start | bytes 98312 | tf_op jit(solution)/shard_map/ppermute | solution.py:290
  3.5 1.9 %collective-permute-start.1 = (bf16[32,512]{1,0:T(8,128)(2,1)}, bf16[32,512]{1,0:T(8,128)(2,1)S(1)}, u32[]{:S(2)}, u32[]{:S(2)}) collective-permute-start(bf16[32,512]{1,0:T(8,128)(2,1)} %feat.1), channel_id=1, source_target_pairs={{0,9},{1,8},{2,11},{3,10},{4,13},{5,12},{6,15},{7,14},{8,1},{9,0},... | collective-permute-start | bytes 98312 | tf_op jit(solution)/shard_map/ppermute | solution.py:290
  5.3 0.7 %copy-done.4 = s32[32,128]{1,0:T(8,128)S(1)} copy-done((s32[32,128]{1,0:T(8,128)S(1)}, s32[32,128]{1,0:T(8,128)}, u32[]{:S(2)}) %copy-start.4) | copy-done | bytes 16408
  6.1 12.7 %gather_slots.1 = (bf16[16,128,512]{2,1,0:T(8,128)(2,1)S(1)}, bf16[16,128,512]{2,1,0:T(8,128)(2,1)S(1)}) custom-call(s32[1]{0:T(128)} %bitcast.1.me_ref, s32[32,128]{1,0:T(8,128)S(1)} %copy-done.4, bf16[4096,512]{1,0:T(8,128)(2,1)} %acct_hbm.1), custom_call_target="tpu_custom_call" | custom-call | bytes 20971520 | tf_op jit(solution)/shard_map/gather_slots/pallas_call | solution.py:94
  18.7 0.0 collective-permute-done.2
  18.8 2.8 %collective-permute-start.6 = (bf16[128,512]{1,0:T(8,128)(2,1)S(1)}, bf16[128,512]{1,0:T(8,128)(2,1)S(1)}, u32[]{:S(2)}, u32[]{:S(2)}) collective-permute-start(bf16[128,512]{1,0:T(8,128)(2,1)S(1)} %pad_maximum_fusion.1), channel_id=1, source_target_pairs={{0,6},{1,7},{2,4},{3,5},{4,2},{5,3},{6,0},{7,1},{8,14},{9,15},{10,... | collective-permute-start | bytes 393224 | tf_op jit(solution)/shard_map/ppermute | solution.py:290
  21.6 0.5 collective-permute-start.5
  22.1 0.2 collective-permute-start.4
  22.4 0.0 copy-start.2
  22.4 0.0 copy-start.7
  22.4 0.0 copy-start.8
  22.4 6.9 %project_slots.1 = (bf16[16,512,128]{2,1,0:T(8,128)(2,1)S(1)}, bf16[16,128,512]{2,1,0:T(8,128)(2,1)S(1)}, bf16[16,512,128]{2,1,0:T(8,128)(2,1)S(1)}, bf16[16,128,512]{2,1,0:T(8,128)(2,1)S(1)}) custom-call(s32[1]{0:T(128)} %bitcast.1.me_ref, s32[32]{0:T(128)S(1)} %copy-done.6, bf16[4,512,512]{2,1,0:T(8,128)(2,1)S(1)} %copy-done.9, ...), custom_call_target="tpu_custom_call" | custom-call | flops 4294967296 | bytes 16777216 | tf_op jit(solution)/shard_map/project_slots/pallas_call | solution.py:136
  29.4 0.1 collective-permute-start.7
  29.5 1.5 %aggregate_odd.1 = bf16[512,512]{1,0:T(8,128)(2,1)S(1)} custom-call(s32[1]{0:T(128)} %bitcast.1.me_ref, s32[32]{0:T(128)S(1)} %copy-done.6, s32[32]{0:T(128)S(1)} %copy-done.7, f32[4]{0:T(128)S(1)} %copy-done.8, s32[32,128]{1,0:T(8,128)S(1)} %copy-done.2, bf16[512,512]{1,0:T(8,128)(2,1)S(1)} %pad_maximum_fusion.feats, bf16[512,512]{1,0:T(8,128)(2,1)S(1)} %copy-done, ...), custom_call_target="tpu_custom_call" | custom-call | flops 402653184 | bytes 6291456 | tf_op jit(solution)/shard_map/aggregate_odd/pallas_call | solution.py:178
  31.0 0.5 %collective-permute-start.8 = (bf16[512,512]{1,0:T(8,128)(2,1)S(1)}, bf16[512,512]{1,0:T(8,128)(2,1)S(1)}, u32[]{:S(2)}, u32[]{:S(2)}) collective-permute-start(bf16[512,512]{1,0:T(8,128)(2,1)S(1)} %aggregate_odd.1), channel_id=1, source_target_pairs={{0,1},{1,0},{2,3},{3,2},{4,5},{5,4},{6,7},{7,6},{8,9},{9,8},{10,11... | collective-permute-start | bytes 1572872 | tf_op jit(solution)/shard_map/ppermute | solution.py:290
  31.6 1.5 %aggregate_even.1.mine = f32[512,512]{1,0:T(8,128)S(1)} custom-call(s32[1]{0:T(128)} %bitcast.1.me_ref, s32[32]{0:T(128)S(1)} %copy-done.6, s32[32]{0:T(128)S(1)} %copy-done.7, f32[4]{0:T(128)S(1)} %copy-done.8, s32[32,128]{1,0:T(8,128)S(1)} %copy-done.2, bf16[512,512]{1,0:T(8,128)(2,1)S(1)} %collective-permute-done.7.feats, bf16[512,512]{1,0:T(8,128)(2,1)S(1)} %copy-done, ...), custom_call_target="tpu_custom_call" | custom-call | flops 402653184 | bytes 6291456 | tf_op jit(solution)/shard_map/aggregate_even/pallas_call | solution.py:178
  33.1 0.0 copy-start.1
  33.1 0.0 copy-start.3
  33.1 0.0 copy-start.5
  33.1 0.1 combine_cores.1
  33.2 2.8 %collective-permute-start.9 = (bf16[128,512]{1,0:T(8,128)(2,1)S(1)}, bf16[128,512]{1,0:T(8,128)(2,1)S(1)}, u32[]{:S(2)}, u32[]{:S(2)}) collective-permute-start(bf16[128,512]{1,0:T(8,128)(2,1)S(1)} %get-tuple-element.30), channel_id=1, source_target_pairs={{0,6},{1,7},{2,4},{3,5},{4,2},{5,3},{6,0},{7,1},{8,14},{9,15},{10,... | collective-permute-start | bytes 393224 | tf_op jit(solution)/shard_map/ppermute | solution.py:290
  36.1 0.5 collective-permute-start.10
  36.6 0.2 collective-permute-start.11
  36.8 3.4 %collective-permute-done.9.refs_1_ = bf16[128,512]{1,0:T(8,128)(2,1)S(1)} collective-permute-done((bf16[128,512]{1,0:T(8,128)(2,1)S(1)}, bf16[128,512]{1,0:T(8,128)(2,1)S(1)}, u32[]{:S(2)}, u32[]{:S(2)}) %collective-permute-start.9) | collective-permute-done | bytes 131104 | tf_op jit(solution)/shard_map/ppermute | solution.py:290
  40.2 2.7 %collective-permute-done.10.refs_2_ = bf16[128,512]{1,0:T(8,128)(2,1)S(1)} collective-permute-done((bf16[128,512]{1,0:T(8,128)(2,1)S(1)}, bf16[128,512]{1,0:T(8,128)(2,1)S(1)}, u32[]{:S(2)}, u32[]{:S(2)}) %collective-permute-start.10) | collective-permute-done | bytes 131104 | tf_op jit(solution)/shard_map/ppermute | solution.py:290
  42.9 0.3 collective-permute-done.11.refs_3_
  43.2 0.1 combine_plane.1
  43.2 3.7 %collective-permute-start.12 = (bf16[32,512]{1,0:T(8,128)(2,1)S(1)}, bf16[32,512]{1,0:T(8,128)(2,1)S(1)}, u32[]{:S(2)}, u32[]{:S(2)}) collective-permute-start(bf16[32,512]{1,0:T(8,128)(2,1)S(1)} %get-tuple-element.34), channel_id=1, source_target_pairs={{0,24},{1,25},{2,26},{3,27},{4,28},{5,29},{6,30},{7,31},{8,16},{9,... | collective-permute-start | bytes 98312 | tf_op jit(solution)/shard_map/ppermute | solution.py:290
  46.9 0.8 %collective-permute-start.14 = (bf16[32,512]{1,0:T(8,128)(2,1)S(1)}, bf16[32,512]{1,0:T(8,128)(2,1)S(1)}, u32[]{:S(2)}, u32[]{:S(2)}) collective-permute-start(bf16[32,512]{1,0:T(8,128)(2,1)S(1)} %get-tuple-element.36), channel_id=1, source_target_pairs={{0,8},{1,9},{2,10},{3,11},{4,12},{5,13},{6,14},{7,15},{8,0},{9,1},... | collective-permute-start | bytes 98312 | tf_op jit(solution)/shard_map/ppermute | solution.py:290
  47.7 1.3 %collective-permute-done.12.refs_1_ = bf16[32,512]{1,0:T(8,128)(2,1)S(1)} collective-permute-done((bf16[32,512]{1,0:T(8,128)(2,1)S(1)}, bf16[32,512]{1,0:T(8,128)(2,1)S(1)}, u32[]{:S(2)}, u32[]{:S(2)}) %collective-permute-start.12) | collective-permute-done | bytes 32800 | tf_op jit(solution)/shard_map/ppermute | solution.py:290
  49.0 2.7 %collective-permute-done.13.refs_2_ = bf16[32,512]{1,0:T(8,128)(2,1)S(1)} collective-permute-done((bf16[32,512]{1,0:T(8,128)(2,1)S(1)}, bf16[32,512]{1,0:T(8,128)(2,1)S(1)}, u32[]{:S(2)}, u32[]{:S(2)}) %collective-permute-start.13) | collective-permute-done | bytes 32800 | tf_op jit(solution)/shard_map/ppermute | solution.py:290
  51.7 0.9 %finish.1 = bf16[32,512]{1,0:T(8,128)(2,1)} custom-call(bf16[32,512]{1,0:T(8,128)(2,1)S(1)} %copy-done.3, f32[1,512]{1,0:T(1,128)S(1)} %bitcast.2, bf16[512,512]{1,0:T(8,128)(2,1)S(1)} %copy-done.1, f32[32,512]{1,0:T(8,128)S(1)} %get-tuple-element.33.refs_0_, bf16[32,512]{1,0:T(8,128)(2,1)S(1)} %collective-permute-done.12.refs_1_, ...), custom_call_target="tpu_custom_call" | custom-call | tf_op jit(solution)/shard_map/finish/pallas_call | solution.py:260
  (29 shorter events, 0.1 us)
Async XLA Ops:
  0.0 18.7 %collective-permute-start.2 = (bf16[32,512]{1,0:T(8,128)(2,1)}, bf16[32,512]{1,0:T(8,128)(2,1)S(1)}, u32[]{:S(2)}, u32[]{:S(2)}) collective-permute-start(bf16[32,512]{1,0:T(8,128)(2,1)} %feat.1), channel_id=1, source_target_pairs={{0,17},{1,16},{2,19},{3,18},{4,21},{5,20},{6,23},{7,22},{8,25},{9,... | collective-permute-start | bytes 98312 | tf_op jit(solution)/shard_map/ppermute | solution.py:290
  3.5 15.3 %collective-permute-start.1 = (bf16[32,512]{1,0:T(8,128)(2,1)}, bf16[32,512]{1,0:T(8,128)(2,1)S(1)}, u32[]{:S(2)}, u32[]{:S(2)}) collective-permute-start(bf16[32,512]{1,0:T(8,128)(2,1)} %feat.1), channel_id=1, source_target_pairs={{0,9},{1,8},{2,11},{3,10},{4,13},{5,12},{6,15},{7,14},{8,1},{9,0},... | collective-permute-start | bytes 98312 | tf_op jit(solution)/shard_map/ppermute | solution.py:290
  5.3 13.4 %collective-permute-start = (bf16[32,512]{1,0:T(8,128)(2,1)}, bf16[32,512]{1,0:T(8,128)(2,1)S(1)}, u32[]{:S(2)}, u32[]{:S(2)}) collective-permute-start(bf16[32,512]{1,0:T(8,128)(2,1)} %feat.1), channel_id=1, source_target_pairs={{0,1},{1,0},{2,3},{3,2},{4,5},{5,4},{6,7},{7,6},{8,9},{9,8},{10,11... | collective-permute-start | bytes 98312 | tf_op jit(solution)/shard_map/ppermute | solution.py:290
  5.3 13.4 %collective-permute-start.3 = (bf16[32,512]{1,0:T(8,128)(2,1)}, bf16[32,512]{1,0:T(8,128)(2,1)S(1)}, u32[]{:S(2)}, u32[]{:S(2)}) collective-permute-start(bf16[32,512]{1,0:T(8,128)(2,1)} %feat.1), channel_id=1, source_target_pairs={{0,25},{1,24},{2,27},{3,26},{4,29},{5,28},{6,31},{7,30},{8,17},{9,... | collective-permute-start | bytes 98312 | tf_op jit(solution)/shard_map/ppermute | solution.py:290
  5.3 0.7 %copy-start.4 = (s32[32,128]{1,0:T(8,128)S(1)}, s32[32,128]{1,0:T(8,128)}, u32[]{:S(2)}) copy-start(s32[32,128]{1,0:T(8,128)} %slots_ref.1) | copy-start | bytes 49156
  6.1 16.3 %copy-start.6 = (s32[32]{0:T(128)S(1)}, s32[32]{0:T(128)}, u32[]{:S(2)}) copy-start(s32[32]{0:T(128)} %rel_ref.5) | copy-start | bytes 388
  6.1 16.3 %copy-start.9 = (bf16[4,512,512]{2,1,0:T(8,128)(2,1)S(1)}, bf16[4,512,512]{2,1,0:T(8,128)(2,1)}, u32[]{:S(2)}) copy-start(bf16[4,512,512]{2,1,0:T(8,128)(2,1)} %kw.1) | copy-start | bytes 6291460
  6.1 16.3 %copy-start.10 = (bf16[4,512,512]{2,1,0:T(8,128)(2,1)S(1)}, bf16[4,512,512]{2,1,0:T(8,128)(2,1)}, u32[]{:S(2)}) copy-start(bf16[4,512,512]{2,1,0:T(8,128)(2,1)} %mw.1) | copy-start | bytes 6291460
  18.8 10.5 %collective-permute-start.6 = (bf16[128,512]{1,0:T(8,128)(2,1)S(1)}, bf16[128,512]{1,0:T(8,128)(2,1)S(1)}, u32[]{:S(2)}, u32[]{:S(2)}) collective-permute-start(bf16[128,512]{1,0:T(8,128)(2,1)S(1)} %pad_maximum_fusion.1), channel_id=1, source_target_pairs={{0,6},{1,7},{2,4},{3,5},{4,2},{5,3},{6,0},{7,1},{8,14},{9,15},{10,... | collective-permute-start | bytes 393224 | tf_op jit(solution)/shard_map/ppermute | solution.py:290
  21.6 7.6 %collective-permute-start.5 = (bf16[128,512]{1,0:T(8,128)(2,1)S(1)}, bf16[128,512]{1,0:T(8,128)(2,1)S(1)}, u32[]{:S(2)}, u32[]{:S(2)}) collective-permute-start(bf16[128,512]{1,0:T(8,128)(2,1)S(1)} %pad_maximum_fusion.1), channel_id=1, source_target_pairs={{0,4},{1,5},{2,6},{3,7},{4,0},{5,1},{6,2},{7,3},{8,12},{9,13},{10,... | collective-permute-start | bytes 393224 | tf_op jit(solution)/shard_map/ppermute | solution.py:290
  22.1 7.2 %collective-permute-start.4 = (bf16[128,512]{1,0:T(8,128)(2,1)S(1)}, bf16[128,512]{1,0:T(8,128)(2,1)S(1)}, u32[]{:S(2)}, u32[]{:S(2)}) collective-permute-start(bf16[128,512]{1,0:T(8,128)(2,1)S(1)} %pad_maximum_fusion.1), channel_id=1, source_target_pairs={{0,2},{1,3},{2,0},{3,1},{4,6},{5,7},{6,4},{7,5},{8,10},{9,11},{10,... | collective-permute-start | bytes 393224 | tf_op jit(solution)/shard_map/ppermute | solution.py:290
  22.4 7.1 %copy-start = (bf16[512,512]{1,0:T(8,128)(2,1)S(1)}, bf16[512,512]{1,0:T(8,128)(2,1)}, u32[]{:S(2)}) copy-start(bf16[512,512]{1,0:T(8,128)(2,1)} %wq.3) | copy-start | bytes 1572868
  22.4 7.1 %copy-start.2 = (s32[32,128]{1,0:T(8,128)S(1)}, s32[32,128]{1,0:T(8,128)}, u32[]{:S(2)}) copy-start(s32[32,128]{1,0:T(8,128)} %merch_slot.3) | copy-start | bytes 49156
  22.4 7.1 %copy-start.7 = (s32[32]{0:T(128)S(1)}, s32[32]{0:T(128)}, u32[]{:S(2)}) copy-start(s32[32]{0:T(128)} %count_ref.3) | copy-start | bytes 388
  22.4 7.1 %copy-start.8 = (f32[4]{0:T(128)S(1)}, f32[4]{0:T(128)}, u32[]{:S(2)}) copy-start(f32[4]{0:T(128)} %bias_ref.3) | copy-start | bytes 52
  29.4 2.2 %collective-permute-start.7 = (bf16[512,512]{1,0:T(8,128)(2,1)S(1)}, bf16[512,512]{1,0:T(8,128)(2,1)S(1)}, u32[]{:S(2)}, u32[]{:S(2)}) collective-permute-start(bf16[512,512]{1,0:T(8,128)(2,1)S(1)} %pad_maximum_fusion.feats), channel_id=1, source_target_pairs={{0,1},{1,0},{2,3},{3,2},{4,5},{5,4},{6,7},{7,6},{8,9},{9,8},{10,11... | collective-permute-start | bytes 1572872 | tf_op jit(solution)/shard_map/ppermute | solution.py:290
  31.0 2.1 %collective-permute-start.8 = (bf16[512,512]{1,0:T(8,128)(2,1)S(1)}, bf16[512,512]{1,0:T(8,128)(2,1)S(1)}, u32[]{:S(2)}, u32[]{:S(2)}) collective-permute-start(bf16[512,512]{1,0:T(8,128)(2,1)S(1)} %aggregate_odd.1), channel_id=1, source_target_pairs={{0,1},{1,0},{2,3},{3,2},{4,5},{5,4},{6,7},{7,6},{8,9},{9,8},{10,11... | collective-permute-start | bytes 1572872 | tf_op jit(solution)/shard_map/ppermute | solution.py:290
  33.1 18.6 %copy-start.1 = (bf16[512,512]{1,0:T(8,128)(2,1)S(1)}, bf16[512,512]{1,0:T(8,128)(2,1)}, u32[]{:S(2)}) copy-start(bf16[512,512]{1,0:T(8,128)(2,1)} %wo.1) | copy-start | bytes 1572868
  33.1 18.6 %copy-start.3 = (bf16[32,512]{1,0:T(8,128)(2,1)S(1)}, bf16[32,512]{1,0:T(8,128)(2,1)}, u32[]{:S(2)}) copy-start(bf16[32,512]{1,0:T(8,128)(2,1)} %feat.1) | copy-start | bytes 98308
  33.1 18.6 %copy-start.5 = (f32[512]{0:T(512)S(1)}, f32[512]{0:T(512)}, u32[]{:S(2)}) copy-start(f32[512]{0:T(512)} %param.19) | copy-start | bytes 6148
  33.2 6.9 %collective-permute-start.9 = (bf16[128,512]{1,0:T(8,128)(2,1)S(1)}, bf16[128,512]{1,0:T(8,128)(2,1)S(1)}, u32[]{:S(2)}, u32[]{:S(2)}) collective-permute-start(bf16[128,512]{1,0:T(8,128)(2,1)S(1)} %get-tuple-element.30), channel_id=1, source_target_pairs={{0,6},{1,7},{2,4},{3,5},{4,2},{5,3},{6,0},{7,1},{8,14},{9,15},{10,... | collective-permute-start | bytes 393224 | tf_op jit(solution)/shard_map/ppermute | solution.py:290
  36.1 6.8 %collective-permute-start.10 = (bf16[128,512]{1,0:T(8,128)(2,1)S(1)}, bf16[128,512]{1,0:T(8,128)(2,1)S(1)}, u32[]{:S(2)}, u32[]{:S(2)}) collective-permute-start(bf16[128,512]{1,0:T(8,128)(2,1)S(1)} %get-tuple-element.31), channel_id=1, source_target_pairs={{0,4},{1,5},{2,6},{3,7},{4,0},{5,1},{6,2},{7,3},{8,12},{9,13},{10,... | collective-permute-start | bytes 393224 | tf_op jit(solution)/shard_map/ppermute | solution.py:290
  36.6 6.6 %collective-permute-start.11 = (bf16[128,512]{1,0:T(8,128)(2,1)S(1)}, bf16[128,512]{1,0:T(8,128)(2,1)S(1)}, u32[]{:S(2)}, u32[]{:S(2)}) collective-permute-start(bf16[128,512]{1,0:T(8,128)(2,1)S(1)} %get-tuple-element.32), channel_id=1, source_target_pairs={{0,2},{1,3},{2,0},{3,1},{4,6},{5,7},{6,4},{7,5},{8,10},{9,11},{10,... | collective-permute-start | bytes 393224 | tf_op jit(solution)/shard_map/ppermute | solution.py:290
  43.2 5.8 %collective-permute-start.12 = (bf16[32,512]{1,0:T(8,128)(2,1)S(1)}, bf16[32,512]{1,0:T(8,128)(2,1)S(1)}, u32[]{:S(2)}, u32[]{:S(2)}) collective-permute-start(bf16[32,512]{1,0:T(8,128)(2,1)S(1)} %get-tuple-element.34), channel_id=1, source_target_pairs={{0,24},{1,25},{2,26},{3,27},{4,28},{5,29},{6,30},{7,31},{8,16},{9,... | collective-permute-start | bytes 98312 | tf_op jit(solution)/shard_map/ppermute | solution.py:290
  46.9 4.8 %collective-permute-start.13 = (bf16[32,512]{1,0:T(8,128)(2,1)S(1)}, bf16[32,512]{1,0:T(8,128)(2,1)S(1)}, u32[]{:S(2)}, u32[]{:S(2)}) collective-permute-start(bf16[32,512]{1,0:T(8,128)(2,1)S(1)} %get-tuple-element.35), channel_id=1, source_target_pairs={{0,16},{1,17},{2,18},{3,19},{4,20},{5,21},{6,22},{7,23},{8,24},{9,... | collective-permute-start | bytes 98312 | tf_op jit(solution)/shard_map/ppermute | solution.py:290
  46.9 4.8 %collective-permute-start.14 = (bf16[32,512]{1,0:T(8,128)(2,1)S(1)}, bf16[32,512]{1,0:T(8,128)(2,1)S(1)}, u32[]{:S(2)}, u32[]{:S(2)}) collective-permute-start(bf16[32,512]{1,0:T(8,128)(2,1)S(1)} %get-tuple-element.36), channel_id=1, source_target_pairs={{0,8},{1,9},{2,10},{3,11},{4,12},{5,13},{6,14},{7,15},{8,0},{9,1},... | collective-permute-start | bytes 98312 | tf_op jit(solution)/shard_map/ppermute | solution.py:290

commit v9 on v8

--- a/solution.py
+++ b/solution.py
@@ -32,13 +32,13 @@
 
 
 def gather_kernel(
-    outer, me_ref, slots_ref, acct_hbm, odd, even, acct, table, rows0, rows1, sem
+    outer, me_ref, count_ref, slots_ref, acct_hbm, odd, even, acct, table, rows0, rows1, sem
 ):
     accounts, width = acct.shape
     blocks, block_len, _ = odd.shape
     parts = width // LANES
     pitch = table.shape[1]
-    batch = 16
+    group = 32
     flat = table.reshape(accounts * pitch, LANES)
     me = me_ref[0]
     chunks = sem.shape[0]
@@ -51,6 +51,8 @@
     ]
     for copy in copies:
         copy.start()
+    rows0[...] = jnp.zeros_like(rows0)
+    rows1[...] = jnp.zeros_like(rows1)
     for i in range(chunks):
         copies[i].wait()
 
@@ -64,15 +66,19 @@
                 ]
 
     def collect(block, rows):
-        for k in range(0, block_len, batch):
-            found = [table[slots_ref[block, k + u], :parts, :] for u in range(batch)]
-            for u in range(batch):
-                rows[pl.ds(k + u, parts, stride=block_len), :] = found[u]
+        count = count_ref[block]
+        start = block * block_len
+        for k in range(0, block_len, group):
+
+            @pl.when(count > k)
+            def _():
+                for u in range(k, k + group):
+                    rows[u * parts : (u + 1) * parts, :] = table[slots_ref[start + u], :parts, :]
 
     def emit(i, rows, out):
         for c in range(parts):
             out[i, :, c * LANES : (c + 1) * LANES] = rows[
-                c * block_len : (c + 1) * block_len, :
+                pl.ds(c, block_len, stride=parts), :
             ].astype(BF16)
 
     @pl.loop(0, blocks)
@@ -84,7 +90,7 @@
         emit(i, rows1, even)
 
 
-def gather(outer, me, slots, acct):
+def gather(outer, me, count, slots, acct):
     blocks, block_len = slots.shape
     accounts, width = acct.shape
     parts = width // LANES
@@ -94,7 +100,7 @@
     return pl.pallas_call(
         functools.partial(gather_kernel, outer),
         out_shape=(half, half),
-        in_specs=[SMEM, SMEM, ANY],
+        in_specs=[SMEM, SMEM, SMEM, ANY],
         out_specs=(VMEM, VMEM),
         scratch_shapes=[
             pltpu.VMEM(acct.shape, BF16),
@@ -106,7 +112,7 @@
         compiler_params=_mb(47 if blocks <= 32 else 28),
         cost_estimate=_cost(0, 20 * 2**20),
         name="gather_slots",
-    )(me, slots, acct)
+    )(me, count, slots.reshape(-1), acct)
 
 
 def project_kernel(outer, shifts, me_ref, rel_ref, kw, mw, *refs):
@@ -293,7 +299,7 @@
         return lax.optimization_barrier((value,) + others)[0]
 
     feats = jnp.concatenate([swap(merch_feat, 8 * k + 1) for k in range(outer)], axis=0)
-    odd_rows, even_rows = gather(outer, me, slot_acct, acct_feat)
+    odd_rows, even_rows = gather(outer, me, block_count, slot_acct, acct_feat)
     feats = after(feats, odd_rows)
     feats = jnp.concatenate([feats] + [swap(feats, 2 * j) for j in range(1, inner)], axis=0)
     rows = (odd_rows, even_rows)

time: 52.9 us -> 49.7 us (0.940)
  Pallas kernels: 23.7 us -> 20 us
  local copies, waits for them, and re-layouts: 0.77 us -> 1.42 us
    pallas_call x1, Pallas kernels: 12.7 us -> 8.97 us  [gather(): pl.pallas_call(functools.partial(gather_kernel, outer), out_shape=(half,...]
    unnamed x22, local copies, waits for them, and re-layouts: 0.77 us -> 1.42 us
  transfers between devices with their start and end apart: 15 -> 15, of which waited for: 5 -> 5; matrix products, arithmetic and copies ran while one was open for 0% -> 0% of each run, Pallas kernels for 43% -> 38%
where the time goes in v9:
time: 49.7 us; the launch traced here: 49.2 us
  Pallas kernels  20 us (40%)
  starting transfers between devices  17.5 us (35%)
  waiting for transfers between devices  10.1 us (20%)
  local copies, waits for them, and re-layouts  1.42 us (3%)
    ppermute x15, starting transfers between devices, swap(): return lax.ppermute(value, AXES, [(s, s ^ mask) for s in range(devices)])  17.5 us
    ppermute x15, waiting for transfers between devices, swap(): return lax.ppermute(value, AXES, [(s, s ^ mask) for s in range(devices)])  10.1 us
    pallas_call x1, Pallas kernels, gather(): pl.pallas_call(functools.partial(gather_kernel, outer), out_shape=(half,...  8.97 us
    pallas_call x1, Pallas kernels, project(): pl.pallas_call(functools.partial(project_kernel, outer, shifts), out_shap...  6.86 us
    pallas_call x2, Pallas kernels, aggregate(): pl.pallas_call(functools.partial(aggregate_kernel, outer, shift), out_sha...  3.07 us
    unnamed x22, local copies, waits for them, and re-layouts  1.42 us
  transfers between devices with their start and end apart: 15, of which 5 were waited for; matrix products, arithmetic and copies ran while one was open for 0% of the time, Pallas kernels for 38%

profile of v9, /device:TPU:0, one launch (start us, length us, event | category | flops | bytes accessed | tf_op | source)
XLA Modules:
  0.0 49.2 jit_solution(18421538752612079209)
XLA Ops:
  0.0 3.5 %collective-permute-start.2 = (bf16[32,512]{1,0:T(8,128)(2,1)}, bf16[32,512]{1,0:T(8,128)(2,1)S(1)}, u32[]{:S(2)}, u32[]{:S(2)}) collective-permute-start(bf16[32,512]{1,0:T(8,128)(2,1)} %feat.1), channel_id=1, source_target_pairs={{0,17},{1,16},{2,19},{3,18},{4,21},{5,20},{6,23},{7,22},{8,25},{9,... | collective-permute-start | bytes 98312 | tf_op jit(solution)/shard_map/ppermute | solution.py:296
  3.5 1.9 %collective-permute-start.1 = (bf16[32,512]{1,0:T(8,128)(2,1)}, bf16[32,512]{1,0:T(8,128)(2,1)S(1)}, u32[]{:S(2)}, u32[]{:S(2)}) collective-permute-start(bf16[32,512]{1,0:T(8,128)(2,1)} %feat.1), channel_id=1, source_target_pairs={{0,9},{1,8},{2,11},{3,10},{4,13},{5,12},{6,15},{7,14},{8,1},{9,0},... | collective-permute-start | bytes 98312 | tf_op jit(solution)/shard_map/ppermute | solution.py:296
  5.3 0.7 %copy-done.4 = s32[32,128]{1,0:T(8,128)S(1)} copy-done((s32[32,128]{1,0:T(8,128)S(1)}, s32[32,128]{1,0:T(8,128)}, u32[]{:S(2)}) %copy-start.4) | copy-done | bytes 16408
  6.1 0.7 %copy-done.5 = s32[32]{0:T(128)S(1)} copy-done((s32[32]{0:T(128)S(1)}, s32[32]{0:T(128)}, u32[]{:S(2)}) %copy-start.5) | copy-done | bytes 152
  6.7 9.0 %gather_slots.1 = (bf16[16,128,512]{2,1,0:T(8,128)(2,1)S(1)}, bf16[16,128,512]{2,1,0:T(8,128)(2,1)S(1)}) custom-call(s32[1]{0:T(128)} %bitcast.1.me_ref, s32[32]{0:T(128)S(1)} %copy-done.5, s32[4096]{0:T(1024)S(1)} %bitcast.3, bf16[4096,512]{1,0:T(8,128)(2,1)} %acct_hbm.1), custom_call_target="tpu_custom_call" | custom-call | bytes 20971520 | tf_op jit(solution)/shard_map/gather_slots/pallas_call | solution.py:100
  15.7 0.0 collective-permute-done.2
  15.8 2.6 %collective-permute-start.6 = (bf16[128,512]{1,0:T(8,128)(2,1)S(1)}, bf16[128,512]{1,0:T(8,128)(2,1)S(1)}, u32[]{:S(2)}, u32[]{:S(2)}) collective-permute-start(bf16[128,512]{1,0:T(8,128)(2,1)S(1)} %pad_maximum_fusion.1), channel_id=1, source_target_pairs={{0,6},{1,7},{2,4},{3,5},{4,2},{5,3},{6,0},{7,1},{8,14},{9,15},{10,... | collective-permute-start | bytes 393224 | tf_op jit(solution)/shard_map/ppermute | solution.py:296
  18.4 0.4 collective-permute-start.5
  18.8 0.6 %collective-permute-start.4 = (bf16[128,512]{1,0:T(8,128)(2,1)S(1)}, bf16[128,512]{1,0:T(8,128)(2,1)S(1)}, u32[]{:S(2)}, u32[]{:S(2)}) collective-permute-start(bf16[128,512]{1,0:T(8,128)(2,1)S(1)} %pad_maximum_fusion.1), channel_id=1, source_target_pairs={{0,2},{1,3},{2,0},{3,1},{4,6},{5,7},{6,4},{7,5},{8,10},{9,11},{10,... | collective-permute-start | bytes 393224 | tf_op jit(solution)/shard_map/ppermute | solution.py:296
  19.3 0.0 copy-start.2
  19.3 0.0 copy-start.8
  19.4 6.9 %project_slots.1 = (bf16[16,512,128]{2,1,0:T(8,128)(2,1)S(1)}, bf16[16,128,512]{2,1,0:T(8,128)(2,1)S(1)}, bf16[16,512,128]{2,1,0:T(8,128)(2,1)S(1)}, bf16[16,128,512]{2,1,0:T(8,128)(2,1)S(1)}) custom-call(s32[1]{0:T(128)} %bitcast.1.me_ref, s32[32]{0:T(128)S(1)} %copy-done.7, bf16[4,512,512]{2,1,0:T(8,128)(2,1)S(1)} %copy-done.9, ...), custom_call_target="tpu_custom_call" | custom-call | flops 4294967296 | bytes 16777216 | tf_op jit(solution)/shard_map/project_slots/pallas_call | solution.py:142
  26.3 0.1 collective-permute-start.7
  26.4 1.5 %aggregate_odd.1 = bf16[512,512]{1,0:T(8,128)(2,1)S(1)} custom-call(s32[1]{0:T(128)} %bitcast.1.me_ref, s32[32]{0:T(128)S(1)} %copy-done.7, s32[32]{0:T(128)S(1)} %copy-done.5, f32[4]{0:T(128)S(1)} %copy-done.8, s32[32,128]{1,0:T(8,128)S(1)} %copy-done.2, bf16[512,512]{1,0:T(8,128)(2,1)S(1)} %pad_maximum_fusion.feats, bf16[512,512]{1,0:T(8,128)(2,1)S(1)} %copy-done, ...), custom_call_target="tpu_custom_call" | custom-call | flops 402653184 | bytes 6291456 | tf_op jit(solution)/shard_map/aggregate_odd/pallas_call | solution.py:184
  27.9 0.5 %collective-permute-start.8 = (bf16[512,512]{1,0:T(8,128)(2,1)S(1)}, bf16[512,512]{1,0:T(8,128)(2,1)S(1)}, u32[]{:S(2)}, u32[]{:S(2)}) collective-permute-start(bf16[512,512]{1,0:T(8,128)(2,1)S(1)} %aggregate_odd.1), channel_id=1, source_target_pairs={{0,1},{1,0},{2,3},{3,2},{4,5},{5,4},{6,7},{7,6},{8,9},{9,8},{10,11... | collective-permute-start | bytes 1572872 | tf_op jit(solution)/shard_map/ppermute | solution.py:296
  28.5 1.5 %aggregate_even.1.mine = f32[512,512]{1,0:T(8,128)S(1)} custom-call(s32[1]{0:T(128)} %bitcast.1.me_ref, s32[32]{0:T(128)S(1)} %copy-done.7, s32[32]{0:T(128)S(1)} %copy-done.5, f32[4]{0:T(128)S(1)} %copy-done.8, s32[32,128]{1,0:T(8,128)S(1)} %copy-done.2, bf16[512,512]{1,0:T(8,128)(2,1)S(1)} %collective-permute-done.7.feats, bf16[512,512]{1,0:T(8,128)(2,1)S(1)} %copy-done, ...), custom_call_target="tpu_custom_call" | custom-call | flops 402653184 | bytes 6291456 | tf_op jit(solution)/shard_map/aggregate_even/pallas_call | solution.py:184
  30.0 0.0 copy-start.1
  30.0 0.0 copy-start.3
  30.1 0.0 copy-start.6
  30.1 0.1 combine_cores.1
  30.2 2.6 %collective-permute-start.9 = (bf16[128,512]{1,0:T(8,128)(2,1)S(1)}, bf16[128,512]{1,0:T(8,128)(2,1)S(1)}, u32[]{:S(2)}, u32[]{:S(2)}) collective-permute-start(bf16[128,512]{1,0:T(8,128)(2,1)S(1)} %get-tuple-element.30), channel_id=1, source_target_pairs={{0,6},{1,7},{2,4},{3,5},{4,2},{5,3},{6,0},{7,1},{8,14},{9,15},{10,... | collective-permute-start | bytes 393224 | tf_op jit(solution)/shard_map/ppermute | solution.py:296
  32.8 0.4 collective-permute-start.10
  33.2 0.6 %collective-permute-start.11 = (bf16[128,512]{1,0:T(8,128)(2,1)S(1)}, bf16[128,512]{1,0:T(8,128)(2,1)S(1)}, u32[]{:S(2)}, u32[]{:S(2)}) collective-permute-start(bf16[128,512]{1,0:T(8,128)(2,1)S(1)} %get-tuple-element.32), channel_id=1, source_target_pairs={{0,2},{1,3},{2,0},{3,1},{4,6},{5,7},{6,4},{7,5},{8,10},{9,11},{10,... | collective-permute-start | bytes 393224 | tf_op jit(solution)/shard_map/ppermute | solution.py:296
  33.7 3.3 %collective-permute-done.9.refs_1_ = bf16[128,512]{1,0:T(8,128)(2,1)S(1)} collective-permute-done((bf16[128,512]{1,0:T(8,128)(2,1)S(1)}, bf16[128,512]{1,0:T(8,128)(2,1)S(1)}, u32[]{:S(2)}, u32[]{:S(2)}) %collective-permute-start.9) | collective-permute-done | bytes 131104 | tf_op jit(solution)/shard_map/ppermute | solution.py:296
  37.1 2.6 %collective-permute-done.10.refs_2_ = bf16[128,512]{1,0:T(8,128)(2,1)S(1)} collective-permute-done((bf16[128,512]{1,0:T(8,128)(2,1)S(1)}, bf16[128,512]{1,0:T(8,128)(2,1)S(1)}, u32[]{:S(2)}, u32[]{:S(2)}) %collective-permute-start.10) | collective-permute-done | bytes 131104 | tf_op jit(solution)/shard_map/ppermute | solution.py:296
  39.7 0.3 collective-permute-done.11.refs_3_
  39.9 0.1 combine_plane.1
  40.0 3.5 %collective-permute-start.12 = (bf16[32,512]{1,0:T(8,128)(2,1)S(1)}, bf16[32,512]{1,0:T(8,128)(2,1)S(1)}, u32[]{:S(2)}, u32[]{:S(2)}) collective-permute-start(bf16[32,512]{1,0:T(8,128)(2,1)S(1)} %get-tuple-element.34), channel_id=1, source_target_pairs={{0,24},{1,25},{2,26},{3,27},{4,28},{5,29},{6,30},{7,31},{8,16},{9,... | collective-permute-start | bytes 98312 | tf_op jit(solution)/shard_map/ppermute | solution.py:296
  43.5 0.9 %collective-permute-start.14 = (bf16[32,512]{1,0:T(8,128)(2,1)S(1)}, bf16[32,512]{1,0:T(8,128)(2,1)S(1)}, u32[]{:S(2)}, u32[]{:S(2)}) collective-permute-start(bf16[32,512]{1,0:T(8,128)(2,1)S(1)} %get-tuple-element.36), channel_id=1, source_target_pairs={{0,8},{1,9},{2,10},{3,11},{4,12},{5,13},{6,14},{7,15},{8,0},{9,1},... | collective-permute-start | bytes 98312 | tf_op jit(solution)/shard_map/ppermute | solution.py:296
  44.4 1.3 %collective-permute-done.12.refs_1_ = bf16[32,512]{1,0:T(8,128)(2,1)S(1)} collective-permute-done((bf16[32,512]{1,0:T(8,128)(2,1)S(1)}, bf16[32,512]{1,0:T(8,128)(2,1)S(1)}, u32[]{:S(2)}, u32[]{:S(2)}) %collective-permute-start.12) | collective-permute-done | bytes 32800 | tf_op jit(solution)/shard_map/ppermute | solution.py:296
  45.8 2.5 %collective-permute-done.13.refs_2_ = bf16[32,512]{1,0:T(8,128)(2,1)S(1)} collective-permute-done((bf16[32,512]{1,0:T(8,128)(2,1)S(1)}, bf16[32,512]{1,0:T(8,128)(2,1)S(1)}, u32[]{:S(2)}, u32[]{:S(2)}) %collective-permute-start.13) | collective-permute-done | bytes 32800 | tf_op jit(solution)/shard_map/ppermute | solution.py:296
  48.3 0.9 %finish.1 = bf16[32,512]{1,0:T(8,128)(2,1)} custom-call(bf16[32,512]{1,0:T(8,128)(2,1)S(1)} %copy-done.3, f32[1,512]{1,0:T(1,128)S(1)} %bitcast.4, bf16[512,512]{1,0:T(8,128)(2,1)S(1)} %copy-done.1, f32[32,512]{1,0:T(8,128)S(1)} %get-tuple-element.33.refs_0_, bf16[32,512]{1,0:T(8,128)(2,1)S(1)} %collective-permute-done.12.refs_1_, ...), custom_call_target="tpu_custom_call" | custom-call | tf_op jit(solution)/shard_map/finish/pallas_call | solution.py:266
  (29 shorter events, 0.1 us)
Async XLA Ops:
  0.0 15.7 %collective-permute-start.2 = (bf16[32,512]{1,0:T(8,128)(2,1)}, bf16[32,512]{1,0:T(8,128)(2,1)S(1)}, u32[]{:S(2)}, u32[]{:S(2)}) collective-permute-start(bf16[32,512]{1,0:T(8,128)(2,1)} %feat.1), channel_id=1, source_target_pairs={{0,17},{1,16},{2,19},{3,18},{4,21},{5,20},{6,23},{7,22},{8,25},{9,... | collective-permute-start | bytes 98312 | tf_op jit(solution)/shard_map/ppermute | solution.py:296
  3.5 12.2 %collective-permute-start.1 = (bf16[32,512]{1,0:T(8,128)(2,1)}, bf16[32,512]{1,0:T(8,128)(2,1)S(1)}, u32[]{:S(2)}, u32[]{:S(2)}) collective-permute-start(bf16[32,512]{1,0:T(8,128)(2,1)} %feat.1), channel_id=1, source_target_pairs={{0,9},{1,8},{2,11},{3,10},{4,13},{5,12},{6,15},{7,14},{8,1},{9,0},... | collective-permute-start | bytes 98312 | tf_op jit(solution)/shard_map/ppermute | solution.py:296
  5.3 10.4 %collective-permute-start = (bf16[32,512]{1,0:T(8,128)(2,1)}, bf16[32,512]{1,0:T(8,128)(2,1)S(1)}, u32[]{:S(2)}, u32[]{:S(2)}) collective-permute-start(bf16[32,512]{1,0:T(8,128)(2,1)} %feat.1), channel_id=1, source_target_pairs={{0,1},{1,0},{2,3},{3,2},{4,5},{5,4},{6,7},{7,6},{8,9},{9,8},{10,11... | collective-permute-start | bytes 98312 | tf_op jit(solution)/shard_map/ppermute | solution.py:296
  5.3 10.4 %collective-permute-start.3 = (bf16[32,512]{1,0:T(8,128)(2,1)}, bf16[32,512]{1,0:T(8,128)(2,1)S(1)}, u32[]{:S(2)}, u32[]{:S(2)}) collective-permute-start(bf16[32,512]{1,0:T(8,128)(2,1)} %feat.1), channel_id=1, source_target_pairs={{0,25},{1,24},{2,27},{3,26},{4,29},{5,28},{6,31},{7,30},{8,17},{9,... | collective-permute-start | bytes 98312 | tf_op jit(solution)/shard_map/ppermute | solution.py:296
  5.3 0.7 %copy-start.4 = (s32[32,128]{1,0:T(8,128)S(1)}, s32[32,128]{1,0:T(8,128)}, u32[]{:S(2)}) copy-start(s32[32,128]{1,0:T(8,128)} %param.20) | copy-start | bytes 49156
  6.1 0.7 %copy-start.5 = (s32[32]{0:T(128)S(1)}, s32[32]{0:T(128)}, u32[]{:S(2)}) copy-start(s32[32]{0:T(128)} %count_ref.5) | copy-start | bytes 388
  6.7 12.6 %copy-start.7 = (s32[32]{0:T(128)S(1)}, s32[32]{0:T(128)}, u32[]{:S(2)}) copy-start(s32[32]{0:T(128)} %rel_ref.5) | copy-start | bytes 388
  6.7 12.6 %copy-start.9 = (bf16[4,512,512]{2,1,0:T(8,128)(2,1)S(1)}, bf16[4,512,512]{2,1,0:T(8,128)(2,1)}, u32[]{:S(2)}) copy-start(bf16[4,512,512]{2,1,0:T(8,128)(2,1)} %kw.1) | copy-start | bytes 6291460
  6.7 12.6 %copy-start.10 = (bf16[4,512,512]{2,1,0:T(8,128)(2,1)S(1)}, bf16[4,512,512]{2,1,0:T(8,128)(2,1)}, u32[]{:S(2)}) copy-start(bf16[4,512,512]{2,1,0:T(8,128)(2,1)} %mw.1) | copy-start | bytes 6291460
  15.8 10.5 %collective-permute-start.6 = (bf16[128,512]{1,0:T(8,128)(2,1)S(1)}, bf16[128,512]{1,0:T(8,128)(2,1)S(1)}, u32[]{:S(2)}, u32[]{:S(2)}) collective-permute-start(bf16[128,512]{1,0:T(8,128)(2,1)S(1)} %pad_maximum_fusion.1), channel_id=1, source_target_pairs={{0,6},{1,7},{2,4},{3,5},{4,2},{5,3},{6,0},{7,1},{8,14},{9,15},{10,... | collective-permute-start | bytes 393224 | tf_op jit(solution)/shard_map/ppermute | solution.py:296
  18.4 7.9 %collective-permute-start.5 = (bf16[128,512]{1,0:T(8,128)(2,1)S(1)}, bf16[128,512]{1,0:T(8,128)(2,1)S(1)}, u32[]{:S(2)}, u32[]{:S(2)}) collective-permute-start(bf16[128,512]{1,0:T(8,128)(2,1)S(1)} %pad_maximum_fusion.1), channel_id=1, source_target_pairs={{0,4},{1,5},{2,6},{3,7},{4,0},{5,1},{6,2},{7,3},{8,12},{9,13},{10,... | collective-permute-start | bytes 393224 | tf_op jit(solution)/shard_map/ppermute | solution.py:296
  18.8 7.5 %collective-permute-start.4 = (bf16[128,512]{1,0:T(8,128)(2,1)S(1)}, bf16[128,512]{1,0:T(8,128)(2,1)S(1)}, u32[]{:S(2)}, u32[]{:S(2)}) collective-permute-start(bf16[128,512]{1,0:T(8,128)(2,1)S(1)} %pad_maximum_fusion.1), channel_id=1, source_target_pairs={{0,2},{1,3},{2,0},{3,1},{4,6},{5,7},{6,4},{7,5},{8,10},{9,11},{10,... | collective-permute-start | bytes 393224 | tf_op jit(solution)/shard_map/ppermute | solution.py:296
  19.3 7.1 %copy-start = (bf16[512,512]{1,0:T(8,128)(2,1)S(1)}, bf16[512,512]{1,0:T(8,128)(2,1)}, u32[]{:S(2)}) copy-start(bf16[512,512]{1,0:T(8,128)(2,1)} %wq.3) | copy-start | bytes 1572868
  19.3 7.1 %copy-start.2 = (s32[32,128]{1,0:T(8,128)S(1)}, s32[32,128]{1,0:T(8,128)}, u32[]{:S(2)}) copy-start(s32[32,128]{1,0:T(8,128)} %merch_slot.3) | copy-start | bytes 49156
  19.3 7.1 %copy-start.8 = (f32[4]{0:T(128)S(1)}, f32[4]{0:T(128)}, u32[]{:S(2)}) copy-start(f32[4]{0:T(128)} %bias_ref.3) | copy-start | bytes 52
  26.3 2.2 %collective-permute-start.7 = (bf16[512,512]{1,0:T(8,128)(2,1)S(1)}, bf16[512,512]{1,0:T(8,128)(2,1)S(1)}, u32[]{:S(2)}, u32[]{:S(2)}) collective-permute-start(bf16[512,512]{1,0:T(8,128)(2,1)S(1)} %pad_maximum_fusion.feats), channel_id=1, source_target_pairs={{0,1},{1,0},{2,3},{3,2},{4,5},{5,4},{6,7},{7,6},{8,9},{9,8},{10,11... | collective-permute-start | bytes 1572872 | tf_op jit(solution)/shard_map/ppermute | solution.py:296
  27.9 2.1 %collective-permute-start.8 = (bf16[512,512]{1,0:T(8,128)(2,1)S(1)}, bf16[512,512]{1,0:T(8,128)(2,1)S(1)}, u32[]{:S(2)}, u32[]{:S(2)}) collective-permute-start(bf16[512,512]{1,0:T(8,128)(2,1)S(1)} %aggregate_odd.1), channel_id=1, source_target_pairs={{0,1},{1,0},{2,3},{3,2},{4,5},{5,4},{6,7},{7,6},{8,9},{9,8},{10,11... | collective-permute-start | bytes 1572872 | tf_op jit(solution)/shard_map/ppermute | solution.py:296
  30.0 18.3 %copy-start.1 = (bf16[512,512]{1,0:T(8,128)(2,1)S(1)}, bf16[512,512]{1,0:T(8,128)(2,1)}, u32[]{:S(2)}) copy-start(bf16[512,512]{1,0:T(8,128)(2,1)} %wo.1) | copy-start | bytes 1572868
  30.0 18.3 %copy-start.3 = (bf16[32,512]{1,0:T(8,128)(2,1)S(1)}, bf16[32,512]{1,0:T(8,128)(2,1)}, u32[]{:S(2)}) copy-start(bf16[32,512]{1,0:T(8,128)(2,1)} %feat.1) | copy-start | bytes 98308
  30.1 18.3 %copy-start.6 = (f32[512]{0:T(512)S(1)}, f32[512]{0:T(512)}, u32[]{:S(2)}) copy-start(f32[512]{0:T(512)} %param.19) | copy-start | bytes 6148
  30.2 6.9 %collective-permute-start.9 = (bf16[128,512]{1,0:T(8,128)(2,1)S(1)}, bf16[128,512]{1,0:T(8,128)(2,1)S(1)}, u32[]{:S(2)}, u32[]{:S(2)}) collective-permute-start(bf16[128,512]{1,0:T(8,128)(2,1)S(1)} %get-tuple-element.30), channel_id=1, source_target_pairs={{0,6},{1,7},{2,4},{3,5},{4,2},{5,3},{6,0},{7,1},{8,14},{9,15},{10,... | collective-permute-start | bytes 393224 | tf_op jit(solution)/shard_map/ppermute | solution.py:296
  32.8 6.9 %collective-permute-start.10 = (bf16[128,512]{1,0:T(8,128)(2,1)S(1)}, bf16[128,512]{1,0:T(8,128)(2,1)S(1)}, u32[]{:S(2)}, u32[]{:S(2)}) collective-permute-start(bf16[128,512]{1,0:T(8,128)(2,1)S(1)} %get-tuple-element.31), channel_id=1, source_target_pairs={{0,4},{1,5},{2,6},{3,7},{4,0},{5,1},{6,2},{7,3},{8,12},{9,13},{10,... | collective-permute-start | bytes 393224 | tf_op jit(solution)/shard_map/ppermute | solution.py:296
  33.2 6.8 %collective-permute-start.11 = (bf16[128,512]{1,0:T(8,128)(2,1)S(1)}, bf16[128,512]{1,0:T(8,128)(2,1)S(1)}, u32[]{:S(2)}, u32[]{:S(2)}) collective-permute-start(bf16[128,512]{1,0:T(8,128)(2,1)S(1)} %get-tuple-element.32), channel_id=1, source_target_pairs={{0,2},{1,3},{2,0},{3,1},{4,6},{5,7},{6,4},{7,5},{8,10},{9,11},{10,... | collective-permute-start | bytes 393224 | tf_op jit(solution)/shard_map/ppermute | solution.py:296
  40.0 5.8 %collective-permute-start.12 = (bf16[32,512]{1,0:T(8,128)(2,1)S(1)}, bf16[32,512]{1,0:T(8,128)(2,1)S(1)}, u32[]{:S(2)}, u32[]{:S(2)}) collective-permute-start(bf16[32,512]{1,0:T(8,128)(2,1)S(1)} %get-tuple-element.34), channel_id=1, source_target_pairs={{0,24},{1,25},{2,26},{3,27},{4,28},{5,29},{6,30},{7,31},{8,16},{9,... | collective-permute-start | bytes 98312 | tf_op jit(solution)/shard_map/ppermute | solution.py:296
  43.5 4.8 %collective-permute-start.13 = (bf16[32,512]{1,0:T(8,128)(2,1)S(1)}, bf16[32,512]{1,0:T(8,128)(2,1)S(1)}, u32[]{:S(2)}, u32[]{:S(2)}) collective-permute-start(bf16[32,512]{1,0:T(8,128)(2,1)S(1)} %get-tuple-element.35), channel_id=1, source_target_pairs={{0,16},{1,17},{2,18},{3,19},{4,20},{5,21},{6,22},{7,23},{8,24},{9,... | collective-permute-start | bytes 98312 | tf_op jit(solution)/shard_map/ppermute | solution.py:296
  43.5 4.8 %collective-permute-start.14 = (bf16[32,512]{1,0:T(8,128)(2,1)S(1)}, bf16[32,512]{1,0:T(8,128)(2,1)S(1)}, u32[]{:S(2)}, u32[]{:S(2)}) collective-permute-start(bf16[32,512]{1,0:T(8,128)(2,1)S(1)} %get-tuple-element.36), channel_id=1, source_target_pairs={{0,8},{1,9},{2,10},{3,11},{4,12},{5,13},{6,14},{7,15},{8,0},{9,1},... | collective-permute-start | bytes 98312 | tf_op jit(solution)/shard_map/ppermute | solution.py:296

commit v10 on v8

--- a/solution.py
+++ b/solution.py
@@ -38,7 +38,7 @@
     blocks, block_len, _ = odd.shape
     parts = width // LANES
     pitch = table.shape[1]
-    batch = 16
+    apart = block_len + 2
     flat = table.reshape(accounts * pitch, LANES)
     me = me_ref[0]
     chunks = sem.shape[0]
@@ -64,15 +64,15 @@
                 ]
 
     def collect(block, rows):
-        for k in range(0, block_len, batch):
-            found = [table[slots_ref[block, k + u], :parts, :] for u in range(batch)]
-            for u in range(batch):
-                rows[pl.ds(k + u, parts, stride=block_len), :] = found[u]
+        start = block * block_len
+        for k in range(block_len):
+            rows[pl.ds(k, parts, stride=apart), :] = table[slots_ref[start + k], :parts, :]
 
     def emit(i, rows, out):
+        origin = jnp.minimum(me, 0)
         for c in range(parts):
             out[i, :, c * LANES : (c + 1) * LANES] = rows[
-                c * block_len : (c + 1) * block_len, :
+                pl.ds(origin + c * apart, block_len), :
             ].astype(BF16)
 
     @pl.loop(0, blocks)
@@ -89,7 +89,7 @@
     accounts, width = acct.shape
     parts = width // LANES
     pitch = -(-parts // 8) * 8
-    rows = pltpu.VMEM((block_len * parts, LANES), F32)
+    rows = pltpu.VMEM(((block_len + 2) * parts, LANES), F32)
     half = jax.ShapeDtypeStruct((blocks // 2, block_len, width), BF16)
     return pl.pallas_call(
         functools.partial(gather_kernel, outer),
@@ -106,7 +106,7 @@
         compiler_params=_mb(47 if blocks <= 32 else 28),
         cost_estimate=_cost(0, 20 * 2**20),
         name="gather_slots",
-    )(me, slots, acct)
+    )(me, slots.reshape(-1), acct)
 
 
 def project_kernel(outer, shifts, me_ref, rel_ref, kw, mw, *refs):

time: 52.9 us -> 49.7 us (0.940)
  Pallas kernels: 23.7 us -> 20.5 us
    pallas_call x1, Pallas kernels: 12.7 us -> 9.52 us  [gather(): pl.pallas_call(functools.partial(gather_kernel, outer), out_shape=(half,...]
  transfers between devices with their start and end apart: 15 -> 15, of which waited for: 5 -> 5; matrix products, arithmetic and copies ran while one was open for 0% -> 0% of each run, Pallas kernels for 43% -> 39%
where the time goes in v10:
time: 49.7 us; the launch traced here: 49.5 us
  Pallas kernels  20.5 us (41%)
  starting transfers between devices  17.5 us (35%)
  waiting for transfers between devices  10.4 us (21%)
  local copies, waits for them, and re-layouts  0.77 us (2%)
    ppermute x15, starting transfers between devices, swap(): return lax.ppermute(value, AXES, [(s, s ^ mask) for s in range(devices)])  17.5 us
    ppermute x15, waiting for transfers between devices, swap(): return lax.ppermute(value, AXES, [(s, s ^ mask) for s in range(devices)])  10.4 us
    pallas_call x1, Pallas kernels, gather(): pl.pallas_call(functools.partial(gather_kernel, outer), out_shape=(half,...  9.52 us
    pallas_call x1, Pallas kernels, project(): pl.pallas_call(functools.partial(project_kernel, outer, shifts), out_shap...  6.86 us
    pallas_call x2, Pallas kernels, aggregate(): pl.pallas_call(functools.partial(aggregate_kernel, outer, shift), out_sha...  3.07 us
  transfers between devices with their start and end apart: 15, of which 5 were waited for; matrix products, arithmetic and copies ran while one was open for 0% of the time, Pallas kernels for 39%

profile of v10, /device:TPU:0, one launch (start us, length us, event | category | flops | bytes accessed | tf_op | source)
XLA Modules:
  0.0 49.5 jit_solution(8329334874816546499)
XLA Ops:
  0.0 3.5 %collective-permute-start.2 = (bf16[32,512]{1,0:T(8,128)(2,1)}, bf16[32,512]{1,0:T(8,128)(2,1)S(1)}, u32[]{:S(2)}, u32[]{:S(2)}) collective-permute-start(bf16[32,512]{1,0:T(8,128)(2,1)} %feat.1), channel_id=1, source_target_pairs={{0,17},{1,16},{2,19},{3,18},{4,21},{5,20},{6,23},{7,22},{8,25},{9,... | collective-permute-start | bytes 98312 | tf_op jit(solution)/shard_map/ppermute | solution.py:290
  3.5 1.9 %collective-permute-start.1 = (bf16[32,512]{1,0:T(8,128)(2,1)}, bf16[32,512]{1,0:T(8,128)(2,1)S(1)}, u32[]{:S(2)}, u32[]{:S(2)}) collective-permute-start(bf16[32,512]{1,0:T(8,128)(2,1)} %feat.1), channel_id=1, source_target_pairs={{0,9},{1,8},{2,11},{3,10},{4,13},{5,12},{6,15},{7,14},{8,1},{9,0},... | collective-permute-start | bytes 98312 | tf_op jit(solution)/shard_map/ppermute | solution.py:290
  5.3 0.7 %copy-done.4 = s32[32,128]{1,0:T(8,128)S(1)} copy-done((s32[32,128]{1,0:T(8,128)S(1)}, s32[32,128]{1,0:T(8,128)}, u32[]{:S(2)}) %copy-start.4) | copy-done | bytes 16408
  6.1 9.5 %gather_slots.1 = (bf16[16,128,512]{2,1,0:T(8,128)(2,1)S(1)}, bf16[16,128,512]{2,1,0:T(8,128)(2,1)S(1)}) custom-call(s32[1]{0:T(128)} %bitcast.1.me_ref, s32[4096]{0:T(1024)S(1)} %bitcast.3, bf16[4096,512]{1,0:T(8,128)(2,1)} %acct_hbm.1), custom_call_target="tpu_custom_call" | custom-call | bytes 20971520 | tf_op jit(solution)/shard_map/gather_slots/pallas_call | solution.py:94
  15.6 0.0 collective-permute-done.1
  15.7 2.8 %collective-permute-start.6 = (bf16[128,512]{1,0:T(8,128)(2,1)S(1)}, bf16[128,512]{1,0:T(8,128)(2,1)S(1)}, u32[]{:S(2)}, u32[]{:S(2)}) collective-permute-start(bf16[128,512]{1,0:T(8,128)(2,1)S(1)} %pad_maximum_fusion.1), channel_id=1, source_target_pairs={{0,6},{1,7},{2,4},{3,5},{4,2},{5,3},{6,0},{7,1},{8,14},{9,15},{10,... | collective-permute-start | bytes 393224 | tf_op jit(solution)/shard_map/ppermute | solution.py:290
  18.5 0.5 %collective-permute-start.5 = (bf16[128,512]{1,0:T(8,128)(2,1)S(1)}, bf16[128,512]{1,0:T(8,128)(2,1)S(1)}, u32[]{:S(2)}, u32[]{:S(2)}) collective-permute-start(bf16[128,512]{1,0:T(8,128)(2,1)S(1)} %pad_maximum_fusion.1), channel_id=1, source_target_pairs={{0,4},{1,5},{2,6},{3,7},{4,0},{5,1},{6,2},{7,3},{8,12},{9,13},{10,... | collective-permute-start | bytes 393224 | tf_op jit(solution)/shard_map/ppermute | solution.py:290
  19.0 0.2 collective-permute-start.4
  19.2 0.0 copy-start.2
  19.2 0.0 copy-start.7
  19.3 0.0 copy-start.8
  19.3 6.9 %project_slots.1 = (bf16[16,512,128]{2,1,0:T(8,128)(2,1)S(1)}, bf16[16,128,512]{2,1,0:T(8,128)(2,1)S(1)}, bf16[16,512,128]{2,1,0:T(8,128)(2,1)S(1)}, bf16[16,128,512]{2,1,0:T(8,128)(2,1)S(1)}) custom-call(s32[1]{0:T(128)} %bitcast.1.me_ref, s32[32]{0:T(128)S(1)} %copy-done.6, bf16[4,512,512]{2,1,0:T(8,128)(2,1)S(1)} %copy-done.9, ...), custom_call_target="tpu_custom_call" | custom-call | flops 4294967296 | bytes 16777216 | tf_op jit(solution)/shard_map/project_slots/pallas_call | solution.py:136
  26.2 0.1 collective-permute-start.7
  26.3 1.5 %aggregate_odd.1 = bf16[512,512]{1,0:T(8,128)(2,1)S(1)} custom-call(s32[1]{0:T(128)} %bitcast.1.me_ref, s32[32]{0:T(128)S(1)} %copy-done.6, s32[32]{0:T(128)S(1)} %copy-done.7, f32[4]{0:T(128)S(1)} %copy-done.8, s32[32,128]{1,0:T(8,128)S(1)} %copy-done.2, bf16[512,512]{1,0:T(8,128)(2,1)S(1)} %pad_maximum_fusion.feats, bf16[512,512]{1,0:T(8,128)(2,1)S(1)} %copy-done, ...), custom_call_target="tpu_custom_call" | custom-call | flops 402653184 | bytes 6291456 | tf_op jit(solution)/shard_map/aggregate_odd/pallas_call | solution.py:178
  27.9 0.5 %collective-permute-start.8 = (bf16[512,512]{1,0:T(8,128)(2,1)S(1)}, bf16[512,512]{1,0:T(8,128)(2,1)S(1)}, u32[]{:S(2)}, u32[]{:S(2)}) collective-permute-start(bf16[512,512]{1,0:T(8,128)(2,1)S(1)} %aggregate_odd.1), channel_id=1, source_target_pairs={{0,1},{1,0},{2,3},{3,2},{4,5},{5,4},{6,7},{7,6},{8,9},{9,8},{10,11... | collective-permute-start | bytes 1572872 | tf_op jit(solution)/shard_map/ppermute | solution.py:290
  28.4 1.5 %aggregate_even.1.mine = f32[512,512]{1,0:T(8,128)S(1)} custom-call(s32[1]{0:T(128)} %bitcast.1.me_ref, s32[32]{0:T(128)S(1)} %copy-done.6, s32[32]{0:T(128)S(1)} %copy-done.7, f32[4]{0:T(128)S(1)} %copy-done.8, s32[32,128]{1,0:T(8,128)S(1)} %copy-done.2, bf16[512,512]{1,0:T(8,128)(2,1)S(1)} %collective-permute-done.7.feats, bf16[512,512]{1,0:T(8,128)(2,1)S(1)} %copy-done, ...), custom_call_target="tpu_custom_call" | custom-call | flops 402653184 | bytes 6291456 | tf_op jit(solution)/shard_map/aggregate_even/pallas_call | solution.py:178
  30.0 0.0 copy-start.1
  30.0 0.0 copy-start.3
  30.0 0.0 copy-start.5
  30.0 0.1 combine_cores.1
  30.1 2.8 %collective-permute-start.9 = (bf16[128,512]{1,0:T(8,128)(2,1)S(1)}, bf16[128,512]{1,0:T(8,128)(2,1)S(1)}, u32[]{:S(2)}, u32[]{:S(2)}) collective-permute-start(bf16[128,512]{1,0:T(8,128)(2,1)S(1)} %get-tuple-element.30), channel_id=1, source_target_pairs={{0,6},{1,7},{2,4},{3,5},{4,2},{5,3},{6,0},{7,1},{8,14},{9,15},{10,... | collective-permute-start | bytes 393224 | tf_op jit(solution)/shard_map/ppermute | solution.py:290
  32.9 0.5 %collective-permute-start.10 = (bf16[128,512]{1,0:T(8,128)(2,1)S(1)}, bf16[128,512]{1,0:T(8,128)(2,1)S(1)}, u32[]{:S(2)}, u32[]{:S(2)}) collective-permute-start(bf16[128,512]{1,0:T(8,128)(2,1)S(1)} %get-tuple-element.31), channel_id=1, source_target_pairs={{0,4},{1,5},{2,6},{3,7},{4,0},{5,1},{6,2},{7,3},{8,12},{9,13},{10,... | collective-permute-start | bytes 393224 | tf_op jit(solution)/shard_map/ppermute | solution.py:290
  33.4 0.2 collective-permute-start.11
  33.6 3.4 %collective-permute-done.9.refs_1_ = bf16[128,512]{1,0:T(8,128)(2,1)S(1)} collective-permute-done((bf16[128,512]{1,0:T(8,128)(2,1)S(1)}, bf16[128,512]{1,0:T(8,128)(2,1)S(1)}, u32[]{:S(2)}, u32[]{:S(2)}) %collective-permute-start.9) | collective-permute-done | bytes 131104 | tf_op jit(solution)/shard_map/ppermute | solution.py:290
  37.0 2.7 %collective-permute-done.10.refs_2_ = bf16[128,512]{1,0:T(8,128)(2,1)S(1)} collective-permute-done((bf16[128,512]{1,0:T(8,128)(2,1)S(1)}, bf16[128,512]{1,0:T(8,128)(2,1)S(1)}, u32[]{:S(2)}, u32[]{:S(2)}) %collective-permute-start.10) | collective-permute-done | bytes 131104 | tf_op jit(solution)/shard_map/ppermute | solution.py:290
  39.7 0.3 collective-permute-done.11.refs_3_
  40.0 0.1 combine_plane.1
  40.1 3.7 %collective-permute-start.12 = (bf16[32,512]{1,0:T(8,128)(2,1)S(1)}, bf16[32,512]{1,0:T(8,128)(2,1)S(1)}, u32[]{:S(2)}, u32[]{:S(2)}) collective-permute-start(bf16[32,512]{1,0:T(8,128)(2,1)S(1)} %get-tuple-element.34), channel_id=1, source_target_pairs={{0,24},{1,25},{2,26},{3,27},{4,28},{5,29},{6,30},{7,31},{8,16},{9,... | collective-permute-start | bytes 98312 | tf_op jit(solution)/shard_map/ppermute | solution.py:290
  43.7 0.8 %collective-permute-start.14 = (bf16[32,512]{1,0:T(8,128)(2,1)S(1)}, bf16[32,512]{1,0:T(8,128)(2,1)S(1)}, u32[]{:S(2)}, u32[]{:S(2)}) collective-permute-start(bf16[32,512]{1,0:T(8,128)(2,1)S(1)} %get-tuple-element.36), channel_id=1, source_target_pairs={{0,8},{1,9},{2,10},{3,11},{4,12},{5,13},{6,14},{7,15},{8,0},{9,1},... | collective-permute-start | bytes 98312 | tf_op jit(solution)/shard_map/ppermute | solution.py:290
  44.5 1.3 %collective-permute-done.12.refs_1_ = bf16[32,512]{1,0:T(8,128)(2,1)S(1)} collective-permute-done((bf16[32,512]{1,0:T(8,128)(2,1)S(1)}, bf16[32,512]{1,0:T(8,128)(2,1)S(1)}, u32[]{:S(2)}, u32[]{:S(2)}) %collective-permute-start.12) | collective-permute-done | bytes 32800 | tf_op jit(solution)/shard_map/ppermute | solution.py:290
  45.9 2.7 %collective-permute-done.13.refs_2_ = bf16[32,512]{1,0:T(8,128)(2,1)S(1)} collective-permute-done((bf16[32,512]{1,0:T(8,128)(2,1)S(1)}, bf16[32,512]{1,0:T(8,128)(2,1)S(1)}, u32[]{:S(2)}, u32[]{:S(2)}) %collective-permute-start.13) | collective-permute-done | bytes 32800 | tf_op jit(solution)/shard_map/ppermute | solution.py:290
  48.6 0.9 %finish.1 = bf16[32,512]{1,0:T(8,128)(2,1)} custom-call(bf16[32,512]{1,0:T(8,128)(2,1)S(1)} %copy-done.3, f32[1,512]{1,0:T(1,128)S(1)} %bitcast.4, bf16[512,512]{1,0:T(8,128)(2,1)S(1)} %copy-done.1, f32[32,512]{1,0:T(8,128)S(1)} %get-tuple-element.33.refs_0_, bf16[32,512]{1,0:T(8,128)(2,1)S(1)} %collective-permute-done.12.refs_1_, ...), custom_call_target="tpu_custom_call" | custom-call | tf_op jit(solution)/shard_map/finish/pallas_call | solution.py:260
  (29 shorter events, 0.1 us)
Async XLA Ops:
  0.0 15.6 %collective-permute-start.2 = (bf16[32,512]{1,0:T(8,128)(2,1)}, bf16[32,512]{1,0:T(8,128)(2,1)S(1)}, u32[]{:S(2)}, u32[]{:S(2)}) collective-permute-start(bf16[32,512]{1,0:T(8,128)(2,1)} %feat.1), channel_id=1, source_target_pairs={{0,17},{1,16},{2,19},{3,18},{4,21},{5,20},{6,23},{7,22},{8,25},{9,... | collective-permute-start | bytes 98312 | tf_op jit(solution)/shard_map/ppermute | solution.py:290
  3.5 12.1 %collective-permute-start.1 = (bf16[32,512]{1,0:T(8,128)(2,1)}, bf16[32,512]{1,0:T(8,128)(2,1)S(1)}, u32[]{:S(2)}, u32[]{:S(2)}) collective-permute-start(bf16[32,512]{1,0:T(8,128)(2,1)} %feat.1), channel_id=1, source_target_pairs={{0,9},{1,8},{2,11},{3,10},{4,13},{5,12},{6,15},{7,14},{8,1},{9,0},... | collective-permute-start | bytes 98312 | tf_op jit(solution)/shard_map/ppermute | solution.py:290
  5.3 10.3 %collective-permute-start = (bf16[32,512]{1,0:T(8,128)(2,1)}, bf16[32,512]{1,0:T(8,128)(2,1)S(1)}, u32[]{:S(2)}, u32[]{:S(2)}) collective-permute-start(bf16[32,512]{1,0:T(8,128)(2,1)} %feat.1), channel_id=1, source_target_pairs={{0,1},{1,0},{2,3},{3,2},{4,5},{5,4},{6,7},{7,6},{8,9},{9,8},{10,11... | collective-permute-start | bytes 98312 | tf_op jit(solution)/shard_map/ppermute | solution.py:290
  5.3 10.3 %collective-permute-start.3 = (bf16[32,512]{1,0:T(8,128)(2,1)}, bf16[32,512]{1,0:T(8,128)(2,1)S(1)}, u32[]{:S(2)}, u32[]{:S(2)}) collective-permute-start(bf16[32,512]{1,0:T(8,128)(2,1)} %feat.1), channel_id=1, source_target_pairs={{0,25},{1,24},{2,27},{3,26},{4,29},{5,28},{6,31},{7,30},{8,17},{9,... | collective-permute-start | bytes 98312 | tf_op jit(solution)/shard_map/ppermute | solution.py:290
  5.3 0.7 %copy-start.4 = (s32[32,128]{1,0:T(8,128)S(1)}, s32[32,128]{1,0:T(8,128)}, u32[]{:S(2)}) copy-start(s32[32,128]{1,0:T(8,128)} %param.20) | copy-start | bytes 49156
  6.1 13.2 %copy-start.6 = (s32[32]{0:T(128)S(1)}, s32[32]{0:T(128)}, u32[]{:S(2)}) copy-start(s32[32]{0:T(128)} %rel_ref.5) | copy-start | bytes 388
  6.1 13.2 %copy-start.9 = (bf16[4,512,512]{2,1,0:T(8,128)(2,1)S(1)}, bf16[4,512,512]{2,1,0:T(8,128)(2,1)}, u32[]{:S(2)}) copy-start(bf16[4,512,512]{2,1,0:T(8,128)(2,1)} %kw.1) | copy-start | bytes 6291460
  6.1 13.2 %copy-start.10 = (bf16[4,512,512]{2,1,0:T(8,128)(2,1)S(1)}, bf16[4,512,512]{2,1,0:T(8,128)(2,1)}, u32[]{:S(2)}) copy-start(bf16[4,512,512]{2,1,0:T(8,128)(2,1)} %mw.1) | copy-start | bytes 6291460
  15.7 10.5 %collective-permute-start.6 = (bf16[128,512]{1,0:T(8,128)(2,1)S(1)}, bf16[128,512]{1,0:T(8,128)(2,1)S(1)}, u32[]{:S(2)}, u32[]{:S(2)}) collective-permute-start(bf16[128,512]{1,0:T(8,128)(2,1)S(1)} %pad_maximum_fusion.1), channel_id=1, source_target_pairs={{0,6},{1,7},{2,4},{3,5},{4,2},{5,3},{6,0},{7,1},{8,14},{9,15},{10,... | collective-permute-start | bytes 393224 | tf_op jit(solution)/shard_map/ppermute | solution.py:290
  18.5 7.6 %collective-permute-start.5 = (bf16[128,512]{1,0:T(8,128)(2,1)S(1)}, bf16[128,512]{1,0:T(8,128)(2,1)S(1)}, u32[]{:S(2)}, u32[]{:S(2)}) collective-permute-start(bf16[128,512]{1,0:T(8,128)(2,1)S(1)} %pad_maximum_fusion.1), channel_id=1, source_target_pairs={{0,4},{1,5},{2,6},{3,7},{4,0},{5,1},{6,2},{7,3},{8,12},{9,13},{10,... | collective-permute-start | bytes 393224 | tf_op jit(solution)/shard_map/ppermute | solution.py:290
  19.0 7.2 %collective-permute-start.4 = (bf16[128,512]{1,0:T(8,128)(2,1)S(1)}, bf16[128,512]{1,0:T(8,128)(2,1)S(1)}, u32[]{:S(2)}, u32[]{:S(2)}) collective-permute-start(bf16[128,512]{1,0:T(8,128)(2,1)S(1)} %pad_maximum_fusion.1), channel_id=1, source_target_pairs={{0,2},{1,3},{2,0},{3,1},{4,6},{5,7},{6,4},{7,5},{8,10},{9,11},{10,... | collective-permute-start | bytes 393224 | tf_op jit(solution)/shard_map/ppermute | solution.py:290
  19.2 7.1 %copy-start = (bf16[512,512]{1,0:T(8,128)(2,1)S(1)}, bf16[512,512]{1,0:T(8,128)(2,1)}, u32[]{:S(2)}) copy-start(bf16[512,512]{1,0:T(8,128)(2,1)} %wq.3) | copy-start | bytes 1572868
  19.2 7.1 %copy-start.2 = (s32[32,128]{1,0:T(8,128)S(1)}, s32[32,128]{1,0:T(8,128)}, u32[]{:S(2)}) copy-start(s32[32,128]{1,0:T(8,128)} %merch_slot.3) | copy-start | bytes 49156
  19.2 7.1 %copy-start.7 = (s32[32]{0:T(128)S(1)}, s32[32]{0:T(128)}, u32[]{:S(2)}) copy-start(s32[32]{0:T(128)} %count_ref.3) | copy-start | bytes 388
  19.3 7.1 %copy-start.8 = (f32[4]{0:T(128)S(1)}, f32[4]{0:T(128)}, u32[]{:S(2)}) copy-start(f32[4]{0:T(128)} %bias_ref.3) | copy-start | bytes 52
  26.2 2.2 %collective-permute-start.7 = (bf16[512,512]{1,0:T(8,128)(2,1)S(1)}, bf16[512,512]{1,0:T(8,128)(2,1)S(1)}, u32[]{:S(2)}, u32[]{:S(2)}) collective-permute-start(bf16[512,512]{1,0:T(8,128)(2,1)S(1)} %pad_maximum_fusion.feats), channel_id=1, source_target_pairs={{0,1},{1,0},{2,3},{3,2},{4,5},{5,4},{6,7},{7,6},{8,9},{9,8},{10,11... | collective-permute-start | bytes 1572872 | tf_op jit(solution)/shard_map/ppermute | solution.py:290
  27.9 2.1 %collective-permute-start.8 = (bf16[512,512]{1,0:T(8,128)(2,1)S(1)}, bf16[512,512]{1,0:T(8,128)(2,1)S(1)}, u32[]{:S(2)}, u32[]{:S(2)}) collective-permute-start(bf16[512,512]{1,0:T(8,128)(2,1)S(1)} %aggregate_odd.1), channel_id=1, source_target_pairs={{0,1},{1,0},{2,3},{3,2},{4,5},{5,4},{6,7},{7,6},{8,9},{9,8},{10,11... | collective-permute-start | bytes 1572872 | tf_op jit(solution)/shard_map/ppermute | solution.py:290
  30.0 18.6 %copy-start.1 = (bf16[512,512]{1,0:T(8,128)(2,1)S(1)}, bf16[512,512]{1,0:T(8,128)(2,1)}, u32[]{:S(2)}) copy-start(bf16[512,512]{1,0:T(8,128)(2,1)} %wo.1) | copy-start | bytes 1572868
  30.0 18.6 %copy-start.3 = (bf16[32,512]{1,0:T(8,128)(2,1)S(1)}, bf16[32,512]{1,0:T(8,128)(2,1)}, u32[]{:S(2)}) copy-start(bf16[32,512]{1,0:T(8,128)(2,1)} %feat.1) | copy-start | bytes 98308
  30.0 18.6 %copy-start.5 = (f32[512]{0:T(512)S(1)}, f32[512]{0:T(512)}, u32[]{:S(2)}) copy-start(f32[512]{0:T(512)} %param.19) | copy-start | bytes 6148
  30.1 6.9 %collective-permute-start.9 = (bf16[128,512]{1,0:T(8,128)(2,1)S(1)}, bf16[128,512]{1,0:T(8,128)(2,1)S(1)}, u32[]{:S(2)}, u32[]{:S(2)}) collective-permute-start(bf16[128,512]{1,0:T(8,128)(2,1)S(1)} %get-tuple-element.30), channel_id=1, source_target_pairs={{0,6},{1,7},{2,4},{3,5},{4,2},{5,3},{6,0},{7,1},{8,14},{9,15},{10,... | collective-permute-start | bytes 393224 | tf_op jit(solution)/shard_map/ppermute | solution.py:290
  32.9 6.8 %collective-permute-start.10 = (bf16[128,512]{1,0:T(8,128)(2,1)S(1)}, bf16[128,512]{1,0:T(8,128)(2,1)S(1)}, u32[]{:S(2)}, u32[]{:S(2)}) collective-permute-start(bf16[128,512]{1,0:T(8,128)(2,1)S(1)} %get-tuple-element.31), channel_id=1, source_target_pairs={{0,4},{1,5},{2,6},{3,7},{4,0},{5,1},{6,2},{7,3},{8,12},{9,13},{10,... | collective-permute-start | bytes 393224 | tf_op jit(solution)/shard_map/ppermute | solution.py:290
  33.4 6.6 %collective-permute-start.11 = (bf16[128,512]{1,0:T(8,128)(2,1)S(1)}, bf16[128,512]{1,0:T(8,128)(2,1)S(1)}, u32[]{:S(2)}, u32[]{:S(2)}) collective-permute-start(bf16[128,512]{1,0:T(8,128)(2,1)S(1)} %get-tuple-element.32), channel_id=1, source_target_pairs={{0,2},{1,3},{2,0},{3,1},{4,6},{5,7},{6,4},{7,5},{8,10},{9,11},{10,... | collective-permute-start | bytes 393224 | tf_op jit(solution)/shard_map/ppermute | solution.py:290
  40.1 5.8 %collective-permute-start.12 = (bf16[32,512]{1,0:T(8,128)(2,1)S(1)}, bf16[32,512]{1,0:T(8,128)(2,1)S(1)}, u32[]{:S(2)}, u32[]{:S(2)}) collective-permute-start(bf16[32,512]{1,0:T(8,128)(2,1)S(1)} %get-tuple-element.34), channel_id=1, source_target_pairs={{0,24},{1,25},{2,26},{3,27},{4,28},{5,29},{6,30},{7,31},{8,16},{9,... | collective-permute-start | bytes 98312 | tf_op jit(solution)/shard_map/ppermute | solution.py:290
  43.7 4.8 %collective-permute-start.13 = (bf16[32,512]{1,0:T(8,128)(2,1)S(1)}, bf16[32,512]{1,0:T(8,128)(2,1)S(1)}, u32[]{:S(2)}, u32[]{:S(2)}) collective-permute-start(bf16[32,512]{1,0:T(8,128)(2,1)S(1)} %get-tuple-element.35), channel_id=1, source_target_pairs={{0,16},{1,17},{2,18},{3,19},{4,20},{5,21},{6,22},{7,23},{8,24},{9,... | collective-permute-start | bytes 98312 | tf_op jit(solution)/shard_map/ppermute | solution.py:290
  43.7 4.8 %collective-permute-start.14 = (bf16[32,512]{1,0:T(8,128)(2,1)S(1)}, bf16[32,512]{1,0:T(8,128)(2,1)S(1)}, u32[]{:S(2)}, u32[]{:S(2)}) collective-permute-start(bf16[32,512]{1,0:T(8,128)(2,1)S(1)} %get-tuple-element.36), channel_id=1, source_target_pairs={{0,8},{1,9},{2,10},{3,11},{4,12},{5,13},{6,14},{7,15},{8,0},{9,1},... | collective-permute-start | bytes 98312 | tf_op jit(solution)/shard_map/ppermute | solution.py:290

commit v11 on v7

--- a/solution.py
+++ b/solution.py
@@ -109,104 +109,73 @@
     )(me, slots, acct)
 
 
-def project_kernel(outer, shifts, me_ref, rel_ref, kw, mw, *refs):
-    halves = len(shifts)
-    blocks, _, width = refs[0].shape
+def sums_kernel(
+    outer, group, shift, me_ref, rel_ref, count_ref, bias_ref, merch_slot, feats, wq, rows, kw, mw,
+    sums, query, keys, values, gates,
+):
+    owners, width, block_len = keys.shape
+    merchants = sums.shape[0] // owners
     half = width // 2
-    me = me_ref[0]
-
-    def one(i, shift, feats, keys, values):
-        relation = rel_ref[jnp.bitwise_xor(me, _offset(i, outer) + shift)]
-        for n in range(0, width, half):
-            key = jnp.dot(feats[i], kw[relation, :, n : n + half], preferred_element_type=F32)
-            keys[i, :, n : n + half] = key.astype(BF16)
-            value = jnp.dot(feats[i], mw[relation, :, n : n + half], preferred_element_type=F32)
-            values[i, :, n : n + half] = value.astype(BF16)
-
-    @pl.loop(0, blocks, unroll=2)
-    def _(i):
-        for h, shift in enumerate(shifts):
-            one(i, shift, refs[h], refs[halves + 2 * h], refs[halves + 2 * h + 1])
-
-
-def project(outer, shifts, me, rel, feats, kw, mw):
-    blocks, block_len, width = feats[0].shape
-    keys = values = jax.ShapeDtypeStruct(feats[0].shape, BF16)
-    return pl.pallas_call(
-        functools.partial(project_kernel, outer, shifts),
-        out_shape=(keys, values) * len(shifts),
-        in_specs=[SMEM, SMEM] + [VMEM] * (2 + len(shifts)),
-        out_specs=(VMEM, VMEM) * len(shifts),
-        compiler_params=_mb(4),
-        cost_estimate=_cost(
-            4 * len(shifts) * blocks * block_len * width * width, 8 * len(shifts) * 2**20
-        ),
-        name="project_slots",
-    )(me, rel, kw, mw, *feats)
-
-
-def aggregate_kernel(
-    outer, shift, me_ref, rel_ref, count_ref, bias_ref, merch_slot, feats, wq, keys, values,
-    sums, query,
-):
-    blocks, block_len, width = keys.shape
-    merchants = feats.shape[0] // blocks
     me = me_ref[0]
     row = lax.broadcasted_iota(jnp.int32, (merchants, block_len), 0)
     lane = lax.broadcasted_iota(jnp.int32, (merchants, block_len), 1)
-    query[...] = jnp.dot(feats[...], wq[...], preferred_element_type=F32).astype(BF16)
-    for i in range(blocks):
-        block = jnp.bitwise_xor(me, _offset(i, outer) + shift)
-        part = slice(i * merchants, (i + 1) * merchants)
-        mine = (merch_slot[pl.ds(block, 1), :] == row) & (lane < count_ref[block])
-        mine = jnp.where(mine, 1.0, 0.0)
-        queries = jnp.dot(mine.T.astype(BF16), query[part, :], preferred_element_type=F32)
-        score = jnp.sum(keys[i].astype(F32) * queries, axis=1, keepdims=True) / math.sqrt(width)
-        gate = jax.nn.sigmoid(score + bias_ref[rel_ref[block]])
-        message = (gate * values[i].astype(F32)).astype(BF16)
-        sums[part, :] = jnp.dot(
-            mine.astype(BF16), message, preferred_element_type=F32
+    blocks = [jnp.bitwise_xor(me, 2 * group + 8 * i + shift) for i in range(owners)]
+    parts = [slice(i * merchants, (i + 1) * merchants) for i in range(owners)]
+    mine = slice(group * owners * merchants, (group + 1) * owners * merchants)
+    query[...] = jnp.dot(feats[mine, :], wq[...], preferred_element_type=F32).astype(BF16)
+    for i in range(owners):
+        relation = rel_ref[blocks[i]]
+        found = rows.at[group * owners + i]
+        for n in range(0, width, half):
+            key = jnp.dot(found[...], kw[relation, :, n : n + half], preferred_element_type=F32)
+            keys[i, n : n + half, :] = key.astype(BF16).T
+            value = jnp.dot(found[...], mw[relation, :, n : n + half], preferred_element_type=F32)
+            values[i, :, n : n + half] = value.astype(BF16)
+    for i in range(owners):
+        score = jnp.dot(query[parts[i], :], keys[i], preferred_element_type=F32) / math.sqrt(width)
+        score = score + bias_ref[rel_ref[blocks[i]]]
+        live = (merch_slot[pl.ds(blocks[i], 1), :] == row) & (lane < count_ref[blocks[i]])
+        gates[parts[i], :] = jnp.where(live, jax.nn.sigmoid(score), 0.0).astype(BF16)
+    for i in range(owners):
+        sums[parts[i], :] = jnp.dot(
+            gates[parts[i], :], values[i], preferred_element_type=F32
         ).astype(sums.dtype)
 
 
-def aggregate(outer, shift, me, rel, count, bias, merch_slot, feats, wq, keys, values, dtype):
-    blocks, block_len, width = keys.shape
-    rows = feats.shape[0]
-    return pl.pallas_call(
-        functools.partial(aggregate_kernel, outer, shift),
-        out_shape=jax.ShapeDtypeStruct(feats.shape, dtype),
-        in_specs=[SMEM] * 4 + [VMEM] * 5,
+def group_sums(
+    outer, inner, group, shift, me, rel, count, bias, merch_slot, feats, wq, rows, kw, mw, dtype
+):
+    _, block_len, width = rows.shape
+    merchants = feats.shape[0] // (outer * inner)
+    return pl.pallas_call(
+        functools.partial(sums_kernel, outer, group, shift),
+        out_shape=jax.ShapeDtypeStruct((outer * merchants, width), dtype),
+        in_specs=[SMEM] * 4 + [VMEM] * 6,
         out_specs=VMEM,
-        scratch_shapes=[pltpu.VMEM(feats.shape, BF16)],
-        compiler_params=_mb(6),
-        cost_estimate=_cost(
-            4 * rows * block_len * width + 2 * rows * width * width,
-            6 * 2**20,
-            blocks * block_len,
-        ),
-        name="aggregate_odd" if shift else "aggregate_even",
-    )(me, rel, count, bias, merch_slot, feats, wq, keys, values)
-
-
-def combine_kernel(mine, other, *outs):
-    rows = outs[0].shape[0]
-    for j, out in enumerate(outs):
-        part = slice(j * rows, (j + 1) * rows)
-        out[...] = (mine[part, :] + other[part, :].astype(F32)).astype(out.dtype)
-
-
-def combine(inner, mine, other):
-    rows, width = mine.shape
+        scratch_shapes=[
+            pltpu.VMEM((outer * merchants, width), BF16),
+            pltpu.VMEM((outer, width, block_len), BF16),
+            pltpu.VMEM((outer, block_len, width), BF16),
+            pltpu.VMEM((outer * merchants, block_len), BF16),
+        ],
+        compiler_params=_mb(8),
+        cost_estimate=_cost(1000, 1000),
+        name="group_sums",
+    )(me, rel, count, bias, merch_slot, feats, wq, rows, kw, mw)
+
+
+def combine_kernel(mine, other, out):
+    out[...] = (mine[...] + other[...].astype(F32)).astype(out.dtype)
+
+
+def combine(mine, other, dtype):
     return pl.pallas_call(
         combine_kernel,
-        out_shape=tuple(
-            jax.ShapeDtypeStruct((rows // inner, width), F32 if j == 0 else BF16)
-            for j in range(inner)
-        ),
+        out_shape=jax.ShapeDtypeStruct(mine.shape, dtype),
         in_specs=[VMEM, VMEM],
-        out_specs=(VMEM,) * inner,
+        out_specs=VMEM,
         compiler_params=_mb(2),
-        cost_estimate=_cost(0, 2 * 2**20),
+        cost_estimate=_cost(0, 2**19),
         name="combine_cores",
     )(mine, other)
 
@@ -287,28 +256,27 @@
         return lax.optimization_barrier((value,) + others)[0]
 
     feats = jnp.concatenate([swap(merch_feat, 8 * k + 1) for k in range(outer)], axis=0)
+    feats = jnp.concatenate(
+        [feats] + [swap(feats, 2 * j) for j in reversed(range(1, inner))][::-1], axis=0
+    )
     odd_rows, even_rows = gather(outer, me, slot_acct, acct_feat)
     feats = after(feats, odd_rows)
-    feats = jnp.concatenate([feats] + [swap(feats, 2 * j) for j in range(1, inner)], axis=0)
-    rows = (odd_rows, even_rows)
+    even_feats = swap(feats, 1)
+
     weights = (key_weight, msg_weight)
-    if devices <= 32:
-        projected = project(outer, (1, 0), me, block_rel, rows, *weights)
-    else:
-        projected = [
-            out
-            for shift, feat in zip((1, 0), rows)
-            for out in project(outer, (shift,), me, block_rel, (feat,), *weights)
-        ]
-    odd_keys, odd_values, even_keys, even_values = projected
-    feats = after(feats, even_keys)
-
-    shared = (me, block_rel, block_count, rel_bias, slot_merch)
-    even_feats = swap(feats, 1)
-    odd_sums = aggregate(outer, 1, *shared, feats, query_weight, odd_keys, odd_values, BF16)
-    other = swap(odd_sums, 1)
-    even_sums = aggregate(outer, 0, *shared, even_feats, query_weight, even_keys, even_values, F32)
-    parts = combine(inner, even_sums, other)
+    rest = (block_rel, block_count, rel_bias, slot_merch)
+    parts = [None] * inner
+    here = me
+    for j in reversed(range(inner)):
+        odd = group_sums(
+            outer, inner, j, 1, here, *rest, feats, query_weight, odd_rows, *weights, BF16
+        )
+        here = after(here, odd)
+        even = group_sums(
+            outer, inner, j, 0, here, *rest, even_feats, query_weight, even_rows, *weights, F32
+        )
+        parts[j] = combine(even, swap(odd, 1), BF16 if j else F32)
+        here = after(here, parts[j])
     parts = combine_plane(
         outer, [parts[0]] + [swap(parts[j], 2 * j) for j in reversed(range(1, inner))]
     )

time: 56.1 us -> 60 us (1.070)
  waiting for transfers between devices: 10.1 us -> 16.8 us
  Pallas kernels: 27.3 us -> 23.9 us
  starting transfers between devices: 17.4 us -> 18 us
    ppermute x15 -> x18, waiting for transfers between devices: 10.1 us -> 16.8 us  [swap(): return lax.ppermute(value, AXES, [(s, s ^ mask) for s in range(devices)])]
    pallas_call x4 -> x12, Pallas kernels: 17.1 us -> 13.7 us  [the longest x8 13.6 us: group_sums(): pl.pallas_call(functools.partial(sums_kernel, outer, group, shift), out_s...]
    ppermute x15 -> x18, starting transfers between devices: 17.4 us -> 18 us  [swap(): return lax.ppermute(value, AXES, [(s, s ^ mask) for s in range(devices)])]
  transfers between devices with their start and end apart: 15 -> 18, of which waited for: 5 -> 7; matrix products, arithmetic and copies ran while one was open for 0% -> 0% of each run, Pallas kernels for 47% -> 30%
where the time goes in v11:
time: 60 us; the launch traced here: 59.8 us
  Pallas kernels  23.9 us (40%)
  starting transfers between devices  18 us (30%)
  waiting for transfers between devices  16.8 us (28%)
  local copies, waits for them, and re-layouts  0.82 us (1%)
    ppermute x18, starting transfers between devices, swap(): return lax.ppermute(value, AXES, [(s, s ^ mask) for s in range(devices)])  18 us
    ppermute x18, waiting for transfers between devices, swap(): return lax.ppermute(value, AXES, [(s, s ^ mask) for s in range(devices)])  16.8 us
    pallas_call x8, Pallas kernels, group_sums(): pl.pallas_call(functools.partial(sums_kernel, outer, group, shift), out_s...  13.6 us
    pallas_call x1, Pallas kernels, gather(): pl.pallas_call(functools.partial(gather_kernel, outer), out_shape=(half,...  9.22 us
  transfers between devices with their start and end apart: 18, of which 7 were waited for; matrix products, arithmetic and copies ran while one was open for 0% of the time, Pallas kernels for 30%

profile of v11, /device:TPU:0, one launch (start us, length us, event | category | flops | bytes accessed | tf_op | source)
XLA Modules:
  0.0 59.8 jit_solution(997142751827511238)
XLA Ops:
  0.0 0.5 collective-permute-start
  0.5 3.7 %collective-permute-start.2 = (bf16[32,512]{1,0:T(8,128)(2,1)}, bf16[32,512]{1,0:T(8,128)(2,1)S(1)}, u32[]{:S(2)}, u32[]{:S(2)}) collective-permute-start(bf16[32,512]{1,0:T(8,128)(2,1)} %feat.1), channel_id=1, source_target_pairs={{0,17},{1,16},{2,19},{3,18},{4,21},{5,20},{6,23},{7,22},{8,25},{9,... | collective-permute-start | bytes 98312 | tf_op jit(solution)/shard_map/ppermute | solution.py:253
  4.2 1.2 %collective-permute-start.1 = (bf16[32,512]{1,0:T(8,128)(2,1)}, bf16[32,512]{1,0:T(8,128)(2,1)S(1)}, u32[]{:S(2)}, u32[]{:S(2)}) collective-permute-start(bf16[32,512]{1,0:T(8,128)(2,1)} %feat.1), channel_id=1, source_target_pairs={{0,9},{1,8},{2,11},{3,10},{4,13},{5,12},{6,15},{7,14},{8,1},{9,0},... | collective-permute-start | bytes 98312 | tf_op jit(solution)/shard_map/ppermute | solution.py:253
  5.4 2.5 %collective-permute-done.1 = bf16[32,512]{1,0:T(8,128)(2,1)S(1)} collective-permute-done((bf16[32,512]{1,0:T(8,128)(2,1)}, bf16[32,512]{1,0:T(8,128)(2,1)S(1)}, u32[]{:S(2)}, u32[]{:S(2)}) %collective-permute-start.1) | collective-permute-done | bytes 32800 | tf_op jit(solution)/shard_map/ppermute | solution.py:253
  7.9 2.8 %collective-permute-done.3 = bf16[32,512]{1,0:T(8,128)(2,1)S(1)} collective-permute-done((bf16[32,512]{1,0:T(8,128)(2,1)}, bf16[32,512]{1,0:T(8,128)(2,1)S(1)}, u32[]{:S(2)}, u32[]{:S(2)}) %collective-permute-start.3) | collective-permute-done | bytes 32800 | tf_op jit(solution)/shard_map/ppermute | solution.py:253
  10.7 1.5 %collective-permute-start.4 = (bf16[128,512]{1,0:T(8,128)(2,1)S(1)}, bf16[128,512]{1,0:T(8,128)(2,1)S(1)}, u32[]{:S(2)}, u32[]{:S(2)}) collective-permute-start(bf16[128,512]{1,0:T(8,128)(2,1)S(1)} %get-tuple-element.33), channel_id=1, source_target_pairs={{0,2},{1,3},{2,0},{3,1},{4,6},{5,7},{6,4},{7,5},{8,10},{9,11},{10,... | collective-permute-start | bytes 393224 | tf_op jit(solution)/shard_map/ppermute | solution.py:253
  12.2 1.5 %collective-permute-start.5 = (bf16[128,512]{1,0:T(8,128)(2,1)S(1)}, bf16[128,512]{1,0:T(8,128)(2,1)S(1)}, u32[]{:S(2)}, u32[]{:S(2)}) collective-permute-start(bf16[128,512]{1,0:T(8,128)(2,1)S(1)} %get-tuple-element.33), channel_id=1, source_target_pairs={{0,4},{1,5},{2,6},{3,7},{4,0},{5,1},{6,2},{7,3},{8,12},{9,13},{10,... | collective-permute-start | bytes 393224 | tf_op jit(solution)/shard_map/ppermute | solution.py:253
  13.7 0.7 %copy-done.9 = s32[32,128]{1,0:T(8,128)S(1)} copy-done((s32[32,128]{1,0:T(8,128)S(1)}, s32[32,128]{1,0:T(8,128)}, u32[]{:S(2)}) %copy-start.9) | copy-done | bytes 16408
  14.5 9.2 %gather_slots.1 = (bf16[16,128,512]{2,1,0:T(8,128)(2,1)S(1)}, bf16[16,128,512]{2,1,0:T(8,128)(2,1)S(1)}) custom-call(s32[1]{0:T(128)} %bitcast.1.me_ref, s32[32,128]{1,0:T(8,128)S(1)} %copy-done.9, bf16[4096,512]{1,0:T(8,128)(2,1)} %acct_hbm.1), custom_call_target="tpu_custom_call" | custom-call | bytes 20971520 | tf_op jit(solution)/shard_map/gather_slots/pallas_call | solution.py:94
  23.7 0.5 collective-permute-start.6
  24.3 5.7 %collective-permute-done.6 = bf16[128,512]{1,0:T(8,128)(2,1)S(1)} collective-permute-done((bf16[128,512]{1,0:T(8,128)(2,1)S(1)}, bf16[128,512]{1,0:T(8,128)(2,1)S(1)}, u32[]{:S(2)}, u32[]{:S(2)}) %collective-permute-start.6) | collective-permute-done | bytes 131104 | tf_op jit(solution)/shard_map/ppermute | solution.py:253
  30.2 1.7 %group_sums.8 = bf16[128,512]{1,0:T(8,128)(2,1)S(1)} custom-call(s32[1]{0:T(128)} %bitcast.1.me_ref, s32[32]{0:T(128)S(1)} %copy-done.5, s32[32]{0:T(128)S(1)} %copy-done.6, f32[4]{0:T(128)S(1)} %copy-done.7, s32[32,128]{1,0:T(8,128)S(1)} %copy-done.3, bf16[512,512]{1,0:T(8,128)(2,1)S(1)} %constant_dynamic-update-slice_fusion.4.feats, ...), custom_call_target="tpu_custom_call" | custom-call | flops 1000 | bytes 1000 | tf_op jit(solution)/shard_map/group_sums/pallas_call | solution.py:150
  31.9 0.5 collective-permute-start.8
  32.4 1.7 %group_sums.9.mine = f32[128,512]{1,0:T(8,128)S(1)} custom-call(s32[1]{0:T(128)} %bitcast.1.me_ref, s32[32]{0:T(128)S(1)} %copy-done.5, s32[32]{0:T(128)S(1)} %copy-done.6, f32[4]{0:T(128)S(1)} %copy-done.7, s32[32,128]{1,0:T(8,128)S(1)} %copy-done.3, bf16[512,512]{1,0:T(8,128)(2,1)S(1)} %collective-permute-done.7.feats, bf16[512,512]{1,0:T(8,128)(2,1)S(1)} %copy-done.2, ...), custom_call_target="tpu_custom_call" | custom-call | flops 1000 | bytes 1000 | tf_op jit(solution)/shard_map/group_sums/pallas_call | solution.py:150
  34.1 1.7 %group_sums.10 = bf16[128,512]{1,0:T(8,128)(2,1)S(1)} custom-call(s32[1]{0:T(128)} %bitcast.1.me_ref, s32[32]{0:T(128)S(1)} %copy-done.5, s32[32]{0:T(128)S(1)} %copy-done.6, f32[4]{0:T(128)S(1)} %copy-done.7, s32[32,128]{1,0:T(8,128)S(1)} %copy-done.3, bf16[512,512]{1,0:T(8,128)(2,1)S(1)} %constant_dynamic-update-slice_fusion.4.feats, ...), custom_call_target="tpu_custom_call" | custom-call | flops 1000 | bytes 1000 | tf_op jit(solution)/shard_map/group_sums/pallas_call | solution.py:150
  35.8 1.7 %group_sums.11.mine = f32[128,512]{1,0:T(8,128)S(1)} custom-call(s32[1]{0:T(128)} %bitcast.1.me_ref, s32[32]{0:T(128)S(1)} %copy-done.5, s32[32]{0:T(128)S(1)} %copy-done.6, f32[4]{0:T(128)S(1)} %copy-done.7, s32[32,128]{1,0:T(8,128)S(1)} %copy-done.3, bf16[512,512]{1,0:T(8,128)(2,1)S(1)} %collective-permute-done.7.feats, bf16[512,512]{1,0:T(8,128)(2,1)S(1)} %copy-done.2, ...), custom_call_target="tpu_custom_call" | custom-call | flops 1000 | bytes 1000 | tf_op jit(solution)/shard_map/group_sums/pallas_call | solution.py:150
  37.6 1.7 %group_sums.12 = bf16[128,512]{1,0:T(8,128)(2,1)S(1)} custom-call(s32[1]{0:T(128)} %bitcast.1.me_ref, s32[32]{0:T(128)S(1)} %copy-done.5, s32[32]{0:T(128)S(1)} %copy-done.6, f32[4]{0:T(128)S(1)} %copy-done.7, s32[32,128]{1,0:T(8,128)S(1)} %copy-done.3, bf16[512,512]{1,0:T(8,128)(2,1)S(1)} %constant_dynamic-update-slice_fusion.4.feats, ...), custom_call_target="tpu_custom_call" | custom-call | flops 1000 | bytes 1000 | tf_op jit(solution)/shard_map/group_sums/pallas_call | solution.py:150
  39.3 0.5 collective-permute-start.10
  39.8 1.7 %group_sums.13.mine = f32[128,512]{1,0:T(8,128)S(1)} custom-call(s32[1]{0:T(128)} %bitcast.1.me_ref, s32[32]{0:T(128)S(1)} %copy-done.5, s32[32]{0:T(128)S(1)} %copy-done.6, f32[4]{0:T(128)S(1)} %copy-done.7, s32[32,128]{1,0:T(8,128)S(1)} %copy-done.3, bf16[512,512]{1,0:T(8,128)(2,1)S(1)} %collective-permute-done.7.feats, bf16[512,512]{1,0:T(8,128)(2,1)S(1)} %copy-done.2, ...), custom_call_target="tpu_custom_call" | custom-call | flops 1000 | bytes 1000 | tf_op jit(solution)/shard_map/group_sums/pallas_call | solution.py:150
  41.5 1.7 %group_sums.14 = bf16[128,512]{1,0:T(8,128)(2,1)S(1)} custom-call(s32[1]{0:T(128)} %bitcast.1.me_ref, s32[32]{0:T(128)S(1)} %copy-done.5, s32[32]{0:T(128)S(1)} %copy-done.6, f32[4]{0:T(128)S(1)} %copy-done.7, s32[32,128]{1,0:T(8,128)S(1)} %copy-done.3, bf16[512,512]{1,0:T(8,128)(2,1)S(1)} %constant_dynamic-update-slice_fusion.4.feats, ...), custom_call_target="tpu_custom_call" | custom-call | flops 1000 | bytes 1000 | tf_op jit(solution)/shard_map/group_sums/pallas_call | solution.py:150
  43.2 0.1 collective-permute-start.11
  43.3 0.5 collective-permute-start.12
  43.8 1.5 %collective-permute-start.13 = (bf16[128,512]{1,0:T(8,128)(2,1)S(1)}, bf16[128,512]{1,0:T(8,128)(2,1)S(1)}, u32[]{:S(2)}, u32[]{:S(2)}) collective-permute-start(bf16[128,512]{1,0:T(8,128)(2,1)S(1)} %combine_cores.5), channel_id=1, source_target_pairs={{0,4},{1,5},{2,6},{3,7},{4,0},{5,1},{6,2},{7,3},{8,12},{9,13},{10,... | collective-permute-start | bytes 393224 | tf_op jit(solution)/shard_map/ppermute | solution.py:253
  45.4 1.5 %collective-permute-start.14 = (bf16[128,512]{1,0:T(8,128)(2,1)S(1)}, bf16[128,512]{1,0:T(8,128)(2,1)S(1)}, u32[]{:S(2)}, u32[]{:S(2)}) collective-permute-start(bf16[128,512]{1,0:T(8,128)(2,1)S(1)} %combine_cores.6), channel_id=1, source_target_pairs={{0,2},{1,3},{2,0},{3,1},{4,6},{5,7},{6,4},{7,5},{8,10},{9,11},{10,... | collective-permute-start | bytes 393224 | tf_op jit(solution)/shard_map/ppermute | solution.py:253
  46.9 1.7 %group_sums.15.mine = f32[128,512]{1,0:T(8,128)S(1)} custom-call(s32[1]{0:T(128)} %bitcast.1.me_ref, s32[32]{0:T(128)S(1)} %copy-done.5, s32[32]{0:T(128)S(1)} %copy-done.6, f32[4]{0:T(128)S(1)} %copy-done.7, s32[32,128]{1,0:T(8,128)S(1)} %copy-done.3, bf16[512,512]{1,0:T(8,128)(2,1)S(1)} %collective-permute-done.7.feats, bf16[512,512]{1,0:T(8,128)(2,1)S(1)} %copy-done.2, ...), custom_call_target="tpu_custom_call" | custom-call | flops 1000 | bytes 1000 | tf_op jit(solution)/shard_map/group_sums/pallas_call | solution.py:150
  48.6 2.0 %collective-permute-done.12.refs_1_ = bf16[128,512]{1,0:T(8,128)(2,1)S(1)} collective-permute-done((bf16[128,512]{1,0:T(8,128)(2,1)S(1)}, bf16[128,512]{1,0:T(8,128)(2,1)S(1)}, u32[]{:S(2)}, u32[]{:S(2)}) %collective-permute-start.12) | collective-permute-done | bytes 131104 | tf_op jit(solution)/shard_map/ppermute | solution.py:253
  50.6 1.6 %collective-permute-done.13.refs_2_ = bf16[128,512]{1,0:T(8,128)(2,1)S(1)} collective-permute-done((bf16[128,512]{1,0:T(8,128)(2,1)S(1)}, bf16[128,512]{1,0:T(8,128)(2,1)S(1)}, u32[]{:S(2)}, u32[]{:S(2)}) %collective-permute-start.13) | collective-permute-done | bytes 131104 | tf_op jit(solution)/shard_map/ppermute | solution.py:253
  52.3 0.9 %collective-permute-start.15 = (bf16[32,512]{1,0:T(8,128)(2,1)S(1)}, bf16[32,512]{1,0:T(8,128)(2,1)S(1)}, u32[]{:S(2)}, u32[]{:S(2)}) collective-permute-start(bf16[32,512]{1,0:T(8,128)(2,1)S(1)} %get-tuple-element.30), channel_id=1, source_target_pairs={{0,24},{1,25},{2,26},{3,27},{4,28},{5,29},{6,30},{7,31},{8,16},{9,... | collective-permute-start | bytes 98312 | tf_op jit(solution)/shard_map/ppermute | solution.py:253
  53.2 3.5 %collective-permute-start.17 = (bf16[32,512]{1,0:T(8,128)(2,1)S(1)}, bf16[32,512]{1,0:T(8,128)(2,1)S(1)}, u32[]{:S(2)}, u32[]{:S(2)}) collective-permute-start(bf16[32,512]{1,0:T(8,128)(2,1)S(1)} %get-tuple-element.32), channel_id=1, source_target_pairs={{0,8},{1,9},{2,10},{3,11},{4,12},{5,13},{6,14},{7,15},{8,0},{9,1},... | collective-permute-start | bytes 98312 | tf_op jit(solution)/shard_map/ppermute | solution.py:253
  56.7 1.4 %collective-permute-done.15.refs_1_ = bf16[32,512]{1,0:T(8,128)(2,1)S(1)} collective-permute-done((bf16[32,512]{1,0:T(8,128)(2,1)S(1)}, bf16[32,512]{1,0:T(8,128)(2,1)S(1)}, u32[]{:S(2)}, u32[]{:S(2)}) %collective-permute-start.15) | collective-permute-done | bytes 32800 | tf_op jit(solution)/shard_map/ppermute | solution.py:253
  58.2 0.7 %collective-permute-done.16.refs_2_ = bf16[32,512]{1,0:T(8,128)(2,1)S(1)} collective-permute-done((bf16[32,512]{1,0:T(8,128)(2,1)S(1)}, bf16[32,512]{1,0:T(8,128)(2,1)S(1)}, u32[]{:S(2)}, u32[]{:S(2)}) %collective-permute-start.16) | collective-permute-done | bytes 32800 | tf_op jit(solution)/shard_map/ppermute | solution.py:253
  58.9 0.9 %finish.1 = bf16[32,512]{1,0:T(8,128)(2,1)} custom-call(bf16[32,512]{1,0:T(8,128)(2,1)S(1)} %copy-done.8, f32[1,512]{1,0:T(1,128)S(1)} %bitcast.2, bf16[512,512]{1,0:T(8,128)(2,1)S(1)} %copy-done.4, f32[32,512]{1,0:T(8,128)S(1)} %get-tuple-element.29.refs_0_, bf16[32,512]{1,0:T(8,128)(2,1)S(1)} %collective-permute-done.15.refs_1_, ...), custom_call_target="tpu_custom_call" | custom-call | tf_op jit(solution)/shard_map/finish/pallas_call | solution.py:223
  (48 shorter events, 0.5 us)
Async XLA Ops:
  0.0 5.3 %collective-permute-start = (bf16[32,512]{1,0:T(8,128)(2,1)}, bf16[32,512]{1,0:T(8,128)(2,1)S(1)}, u32[]{:S(2)}, u32[]{:S(2)}) collective-permute-start(bf16[32,512]{1,0:T(8,128)(2,1)} %feat.1), channel_id=1, source_target_pairs={{0,1},{1,0},{2,3},{3,2},{4,5},{5,4},{6,7},{7,6},{8,9},{9,8},{10,11... | collective-permute-start | bytes 98312 | tf_op jit(solution)/shard_map/ppermute | solution.py:253
  0.5 7.4 %collective-permute-start.2 = (bf16[32,512]{1,0:T(8,128)(2,1)}, bf16[32,512]{1,0:T(8,128)(2,1)S(1)}, u32[]{:S(2)}, u32[]{:S(2)}) collective-permute-start(bf16[32,512]{1,0:T(8,128)(2,1)} %feat.1), channel_id=1, source_target_pairs={{0,17},{1,16},{2,19},{3,18},{4,21},{5,20},{6,23},{7,22},{8,25},{9,... | collective-permute-start | bytes 98312 | tf_op jit(solution)/shard_map/ppermute | solution.py:253
  4.2 3.7 %collective-permute-start.1 = (bf16[32,512]{1,0:T(8,128)(2,1)}, bf16[32,512]{1,0:T(8,128)(2,1)S(1)}, u32[]{:S(2)}, u32[]{:S(2)}) collective-permute-start(bf16[32,512]{1,0:T(8,128)(2,1)} %feat.1), channel_id=1, source_target_pairs={{0,9},{1,8},{2,11},{3,10},{4,13},{5,12},{6,15},{7,14},{8,1},{9,0},... | collective-permute-start | bytes 98312 | tf_op jit(solution)/shard_map/ppermute | solution.py:253
  5.3 5.3 %collective-permute-start.3 = (bf16[32,512]{1,0:T(8,128)(2,1)}, bf16[32,512]{1,0:T(8,128)(2,1)S(1)}, u32[]{:S(2)}, u32[]{:S(2)}) collective-permute-start(bf16[32,512]{1,0:T(8,128)(2,1)} %feat.1), channel_id=1, source_target_pairs={{0,25},{1,24},{2,27},{3,26},{4,29},{5,28},{6,31},{7,30},{8,17},{9,... | collective-permute-start | bytes 98312 | tf_op jit(solution)/shard_map/ppermute | solution.py:253
  10.7 13.6 %collective-permute-start.4 = (bf16[128,512]{1,0:T(8,128)(2,1)S(1)}, bf16[128,512]{1,0:T(8,128)(2,1)S(1)}, u32[]{:S(2)}, u32[]{:S(2)}) collective-permute-start(bf16[128,512]{1,0:T(8,128)(2,1)S(1)} %get-tuple-element.33), channel_id=1, source_target_pairs={{0,2},{1,3},{2,0},{3,1},{4,6},{5,7},{6,4},{7,5},{8,10},{9,11},{10,... | collective-permute-start | bytes 393224 | tf_op jit(solution)/shard_map/ppermute | solution.py:253
  12.2 12.1 %collective-permute-start.5 = (bf16[128,512]{1,0:T(8,128)(2,1)S(1)}, bf16[128,512]{1,0:T(8,128)(2,1)S(1)}, u32[]{:S(2)}, u32[]{:S(2)}) collective-permute-start(bf16[128,512]{1,0:T(8,128)(2,1)S(1)} %get-tuple-element.33), channel_id=1, source_target_pairs={{0,4},{1,5},{2,6},{3,7},{4,0},{5,1},{6,2},{7,3},{8,12},{9,13},{10,... | collective-permute-start | bytes 393224 | tf_op jit(solution)/shard_map/ppermute | solution.py:253
  13.7 0.7 %copy-start.9 = (s32[32,128]{1,0:T(8,128)S(1)}, s32[32,128]{1,0:T(8,128)}, u32[]{:S(2)}) copy-start(s32[32,128]{1,0:T(8,128)} %slots_ref.1) | copy-start | bytes 49156
  14.4 15.7 %copy-start = (bf16[4,512,512]{2,1,0:T(8,128)(2,1)S(1)}, bf16[4,512,512]{2,1,0:T(8,128)(2,1)}, u32[]{:S(2)}) copy-start(bf16[4,512,512]{2,1,0:T(8,128)(2,1)} %kw.15) | copy-start | bytes 6291460
  14.4 15.7 %copy-start.1 = (bf16[4,512,512]{2,1,0:T(8,128)(2,1)S(1)}, bf16[4,512,512]{2,1,0:T(8,128)(2,1)}, u32[]{:S(2)}) copy-start(bf16[4,512,512]{2,1,0:T(8,128)(2,1)} %mw.15) | copy-start | bytes 6291460
  14.4 15.7 %copy-start.2 = (bf16[512,512]{1,0:T(8,128)(2,1)S(1)}, bf16[512,512]{1,0:T(8,128)(2,1)}, u32[]{:S(2)}) copy-start(bf16[512,512]{1,0:T(8,128)(2,1)} %wq.15) | copy-start | bytes 1572868
  14.4 15.7 %copy-start.3 = (s32[32,128]{1,0:T(8,128)S(1)}, s32[32,128]{1,0:T(8,128)}, u32[]{:S(2)}) copy-start(s32[32,128]{1,0:T(8,128)} %merch_slot.15) | copy-start | bytes 49156
  14.4 15.7 %copy-start.5 = (s32[32]{0:T(128)S(1)}, s32[32]{0:T(128)}, u32[]{:S(2)}) copy-start(s32[32]{0:T(128)} %rel_ref.15) | copy-start | bytes 388
  14.4 15.7 %copy-start.6 = (s32[32]{0:T(128)S(1)}, s32[32]{0:T(128)}, u32[]{:S(2)}) copy-start(s32[32]{0:T(128)} %count_ref.15) | copy-start | bytes 388
  14.5 15.7 %copy-start.7 = (f32[4]{0:T(128)S(1)}, f32[4]{0:T(128)}, u32[]{:S(2)}) copy-start(f32[4]{0:T(128)} %bias_ref.15) | copy-start | bytes 52
  23.7 6.3 %collective-permute-start.6 = (bf16[128,512]{1,0:T(8,128)(2,1)S(1)}, bf16[128,512]{1,0:T(8,128)(2,1)S(1)}, u32[]{:S(2)}, u32[]{:S(2)}) collective-permute-start(bf16[128,512]{1,0:T(8,128)(2,1)S(1)} %get-tuple-element.33), channel_id=1, source_target_pairs={{0,6},{1,7},{2,4},{3,5},{4,2},{5,3},{6,0},{7,1},{8,14},{9,15},{10,... | collective-permute-start | bytes 393224 | tf_op jit(solution)/shard_map/ppermute | solution.py:253
  30.0 2.3 %collective-permute-start.7 = (bf16[512,512]{1,0:T(8,128)(2,1)S(1)}, bf16[512,512]{1,0:T(8,128)(2,1)S(1)}, u32[]{:S(2)}, u32[]{:S(2)}) collective-permute-start(bf16[512,512]{1,0:T(8,128)(2,1)S(1)} %constant_dynamic-update-slice_fusion.4.feats), channel_id=1, source_target_pairs={{0,1},{1,0},{2,3},{3,2},{4,5},{5,4},{6,7},{7,6},{8,9},{9,8},{10,11... | collective-permute-start | bytes 1572872 | tf_op jit(solution)/shard_map/ppermute | solution.py:253
  31.9 2.2 %collective-permute-start.8 = (bf16[128,512]{1,0:T(8,128)(2,1)S(1)}, bf16[128,512]{1,0:T(8,128)(2,1)S(1)}, u32[]{:S(2)}, u32[]{:S(2)}) collective-permute-start(bf16[128,512]{1,0:T(8,128)(2,1)S(1)} %group_sums.8), channel_id=1, source_target_pairs={{0,1},{1,0},{2,3},{3,2},{4,5},{5,4},{6,7},{7,6},{8,9},{9,8},{10,11... | collective-permute-start | bytes 393224 | tf_op jit(solution)/shard_map/ppermute | solution.py:253
  35.8 1.8 %collective-permute-start.9 = (bf16[128,512]{1,0:T(8,128)(2,1)S(1)}, bf16[128,512]{1,0:T(8,128)(2,1)S(1)}, u32[]{:S(2)}, u32[]{:S(2)}) collective-permute-start(bf16[128,512]{1,0:T(8,128)(2,1)S(1)} %group_sums.10), channel_id=1, source_target_pairs={{0,1},{1,0},{2,3},{3,2},{4,5},{5,4},{6,7},{7,6},{8,9},{9,8},{10,11... | collective-permute-start | bytes 393224 | tf_op jit(solution)/shard_map/ppermute | solution.py:253
  39.3 2.2 %collective-permute-start.10 = (bf16[128,512]{1,0:T(8,128)(2,1)S(1)}, bf16[128,512]{1,0:T(8,128)(2,1)S(1)}, u32[]{:S(2)}, u32[]{:S(2)}) collective-permute-start(bf16[128,512]{1,0:T(8,128)(2,1)S(1)} %group_sums.12), channel_id=1, source_target_pairs={{0,1},{1,0},{2,3},{3,2},{4,5},{5,4},{6,7},{7,6},{8,9},{9,8},{10,11... | collective-permute-start | bytes 393224 | tf_op jit(solution)/shard_map/ppermute | solution.py:253
  43.2 15.7 %copy-start.4 = (bf16[512,512]{1,0:T(8,128)(2,1)S(1)}, bf16[512,512]{1,0:T(8,128)(2,1)}, u32[]{:S(2)}) copy-start(bf16[512,512]{1,0:T(8,128)(2,1)} %wo.1) | copy-start | bytes 1572868
  43.2 15.7 %copy-start.8 = (bf16[32,512]{1,0:T(8,128)(2,1)S(1)}, bf16[32,512]{1,0:T(8,128)(2,1)}, u32[]{:S(2)}) copy-start(bf16[32,512]{1,0:T(8,128)(2,1)} %feat.1) | copy-start | bytes 98308
  43.2 15.6 %copy-start.10 = (f32[512]{0:T(512)S(1)}, f32[512]{0:T(512)}, u32[]{:S(2)}) copy-start(f32[512]{0:T(512)} %param.19) | copy-start | bytes 6148
  43.2 5.3 %collective-permute-start.11 = (bf16[128,512]{1,0:T(8,128)(2,1)S(1)}, bf16[128,512]{1,0:T(8,128)(2,1)S(1)}, u32[]{:S(2)}, u32[]{:S(2)}) collective-permute-start(bf16[128,512]{1,0:T(8,128)(2,1)S(1)} %group_sums.14), channel_id=1, source_target_pairs={{0,1},{1,0},{2,3},{3,2},{4,5},{5,4},{6,7},{7,6},{8,9},{9,8},{10,11... | collective-permute-start | bytes 393224 | tf_op jit(solution)/shard_map/ppermute | solution.py:253
  43.3 7.3 %collective-permute-start.12 = (bf16[128,512]{1,0:T(8,128)(2,1)S(1)}, bf16[128,512]{1,0:T(8,128)(2,1)S(1)}, u32[]{:S(2)}, u32[]{:S(2)}) collective-permute-start(bf16[128,512]{1,0:T(8,128)(2,1)S(1)} %combine_cores.4), channel_id=1, source_target_pairs={{0,6},{1,7},{2,4},{3,5},{4,2},{5,3},{6,0},{7,1},{8,14},{9,15},{10,... | collective-permute-start | bytes 393224 | tf_op jit(solution)/shard_map/ppermute | solution.py:253
  43.8 8.4 %collective-permute-start.13 = (bf16[128,512]{1,0:T(8,128)(2,1)S(1)}, bf16[128,512]{1,0:T(8,128)(2,1)S(1)}, u32[]{:S(2)}, u32[]{:S(2)}) collective-permute-start(bf16[128,512]{1,0:T(8,128)(2,1)S(1)} %combine_cores.5), channel_id=1, source_target_pairs={{0,4},{1,5},{2,6},{3,7},{4,0},{5,1},{6,2},{7,3},{8,12},{9,13},{10,... | collective-permute-start | bytes 393224 | tf_op jit(solution)/shard_map/ppermute | solution.py:253
  45.4 6.9 %collective-permute-start.14 = (bf16[128,512]{1,0:T(8,128)(2,1)S(1)}, bf16[128,512]{1,0:T(8,128)(2,1)S(1)}, u32[]{:S(2)}, u32[]{:S(2)}) collective-permute-start(bf16[128,512]{1,0:T(8,128)(2,1)S(1)} %combine_cores.6), channel_id=1, source_target_pairs={{0,2},{1,3},{2,0},{3,1},{4,6},{5,7},{6,4},{7,5},{8,10},{9,11},{10,... | collective-permute-start | bytes 393224 | tf_op jit(solution)/shard_map/ppermute | solution.py:253
  52.3 5.9 %collective-permute-start.15 = (bf16[32,512]{1,0:T(8,128)(2,1)S(1)}, bf16[32,512]{1,0:T(8,128)(2,1)S(1)}, u32[]{:S(2)}, u32[]{:S(2)}) collective-permute-start(bf16[32,512]{1,0:T(8,128)(2,1)S(1)} %get-tuple-element.30), channel_id=1, source_target_pairs={{0,24},{1,25},{2,26},{3,27},{4,28},{5,29},{6,30},{7,31},{8,16},{9,... | collective-permute-start | bytes 98312 | tf_op jit(solution)/shard_map/ppermute | solution.py:253
  53.2 5.6 %collective-permute-start.16 = (bf16[32,512]{1,0:T(8,128)(2,1)S(1)}, bf16[32,512]{1,0:T(8,128)(2,1)S(1)}, u32[]{:S(2)}, u32[]{:S(2)}) collective-permute-start(bf16[32,512]{1,0:T(8,128)(2,1)S(1)} %get-tuple-element.31), channel_id=1, source_target_pairs={{0,16},{1,17},{2,18},{3,19},{4,20},{5,21},{6,22},{7,23},{8,24},{9,... | collective-permute-start | bytes 98312 | tf_op jit(solution)/shard_map/ppermute | solution.py:253
  53.2 5.6 %collective-permute-start.17 = (bf16[32,512]{1,0:T(8,128)(2,1)S(1)}, bf16[32,512]{1,0:T(8,128)(2,1)S(1)}, u32[]{:S(2)}, u32[]{:S(2)}) collective-permute-start(bf16[32,512]{1,0:T(8,128)(2,1)S(1)} %get-tuple-element.32), channel_id=1, source_target_pairs={{0,8},{1,9},{2,10},{3,11},{4,12},{5,13},{6,14},{7,15},{8,0},{9,1},... | collective-permute-start | bytes 98312 | tf_op jit(solution)/shard_map/ppermute | solution.py:253

commit v12 on v8

v12 whole, which is shorter than its diff:
```python
import functools
import math

import jax
import jax.numpy as jnp
from jax import lax
from jax.experimental import pallas as pl
from jax.experimental.pallas import tpu as pltpu
from jax.sharding import PartitionSpec as P

AXES = ("acct", "merch")
LANES = 128
F32 = jnp.float32
BF16 = jnp.bfloat16
SMEM = pl.BlockSpec(memory_space=pltpu.SMEM)
ANY = pl.BlockSpec(memory_space=pl.ANY)
VMEM = pl.BlockSpec(memory_space=pltpu.VMEM)


def _mb(n):
    return pltpu.CompilerParams(vmem_limit_bytes=n * 2**20)


def _cost(flops, bytes_accessed, transcendentals=0):
    return pl.CostEstimate(
        flops=int(flops), bytes_accessed=int(bytes_accessed), transcendentals=transcendentals
    )


def _offset(i, outer):
    return (i // outer) * 2 + (i % outer) * 8


def gather_kernel(
    outer, me_ref, slots_ref, acct_hbm, odd, even, acct, table, rows0, rows1, sem
):
    accounts, width = acct.shape
    blocks, block_len, _ = odd.shape
    parts = width // LANES
    pitch = table.shape[1]
    batch = 32
    flat = table.reshape(accounts * pitch, LANES)
    me = me_ref[0]
    chunks = sem.shape[0]
    chunk = accounts // chunks
    copies = [
        pltpu.make_async_copy(
            acct_hbm.at[pl.ds(i * chunk, chunk)], acct.at[pl.ds(i * chunk, chunk)], sem.at[i]
        )
        for i in range(chunks)
    ]
    for copy in copies:
        copy.start()
    for i in range(chunks):
        copies[i].wait()

        @pl.loop(0, chunk // 16, unroll=4)
        def _(g):
            first = pl.multiple_of(i * chunk + g * 16, 16)
            tile = acct[pl.ds(first, 16), :].astype(F32)
            for c in range(parts):
                flat[pl.ds(first * pitch + c, 16, stride=pitch), :] = tile[
                    :, c * LANES : (c + 1) * LANES
                ]

    def collect(block, rows):
        for k in range(0, block_len, batch):
            found = [table[slots_ref[block, k + u], :parts, :] for u in range(batch)]
            for u in range(batch):
                rows[(k + u) * parts : (k + u + 1) * parts, :] = found[u]

    def emit(i, rows, out):
        for c in range(parts):
            out[i, :, c * LANES : (c + 1) * LANES] = rows[
                pl.ds(c, block_len, stride=parts), :
            ].astype(BF16)

    @pl.loop(0, blocks)
    def _(i):
        offset = _offset(i, outer)
        collect(jnp.bitwise_xor(me, offset + 1), rows0)
        collect(jnp.bitwise_xor(me, offset), rows1)
        emit(i, rows0, odd)
        emit(i, rows1, even)


def gather(outer, me, slots, acct):
    blocks, block_len = slots.shape
    accounts, width = acct.shape
    parts = width // LANES
    pitch = -(-parts // 8) * 8
    rows = pltpu.VMEM((block_len * parts, LANES), F32)
    half = jax.ShapeDtypeStruct((blocks // 2, block_len, width), BF16)
    return pl.pallas_call(
        functools.partial(gather_kernel, outer),
        out_shape=(half, half),
        in_specs=[SMEM, SMEM, ANY],
        out_specs=(VMEM, VMEM),
        scratch_shapes=[
            pltpu.VMEM(acct.shape, BF16),
            pltpu.VMEM((accounts, pitch, LANES), F32),
            rows,
            rows,
            pltpu.SemaphoreType.DMA((8,)),
        ],
        compiler_params=_mb(47 if blocks <= 32 else 28),
        cost_estimate=_cost(0, 20 * 2**20),
        name="gather_slots",
    )(me, slots, acct)


def project_kernel(outer, spans, me_ref, rel_ref, kw, mw, *refs):
    width = refs[0].shape[2]
    half = width // 2
    me = me_ref[0]
    count = len(spans)

    def one(i, first, shift, feats, keys, values):
        relation = rel_ref[jnp.bitwise_xor(me, _offset(first + i, outer) + shift)]
        for n in range(0, width, half):
            key = jnp.dot(
                feats[first + i], kw[relation, :, n : n + half], preferred_element_type=F32
            )
            keys[i, n : n + half, :] = key.astype(BF16).T
            value = jnp.dot(
                feats[first + i], mw[relation, :, n : n + half], preferred_element_type=F32
            )
            values[i, :, n : n + half] = value.astype(BF16)

    for s, (first, last, shift) in enumerate(spans):
        outs = refs[count + 2 * s : count + 2 * s + 2]

        @pl.loop(0, last - first, unroll=4)
        def _(i):
            one(i, first, shift, refs[s], *outs)


def project(outer, spans, me, rel, feats, kw, mw):
    _, block_len, width = feats[0].shape
    out_shape = []
    for first, last, _ in spans:
        out_shape.append(jax.ShapeDtypeStruct((last - first, width, block_len), BF16))
        out_shape.append(jax.ShapeDtypeStruct((last - first, block_len, width), BF16))
    blocks = sum(last - first for first, last, _ in spans)
    return pl.pallas_call(
        functools.partial(project_kernel, outer, spans),
        out_shape=tuple(out_shape),
        in_specs=[SMEM, SMEM] + [VMEM] * (2 + len(spans)),
        out_specs=(VMEM,) * len(out_shape),
        compiler_params=_mb(4),
        cost_estimate=_cost(4 * blocks * block_len * width * width, blocks * 2**19),
        name="project_slots",
    )(me, rel, kw, mw, *feats)


def aggregate_kernel(
    outer, first, shift, me_ref, rel_ref, count_ref, bias_ref, merch_slot, feats, wq, keys, values,
    sums, query, gates,
):
    blocks, width, block_len = keys.shape
    merchants = sums.shape[0] // blocks
    me = me_ref[0]
    row = lax.broadcasted_iota(jnp.int32, (merchants, block_len), 0)
    lane = lax.broadcasted_iota(jnp.int32, (merchants, block_len), 1)
    query[...] = jnp.dot(
        feats[first * merchants : (first + blocks) * merchants, :],
        wq[...],
        preferred_element_type=F32,
    ).astype(BF16)
    parts = [slice(i * merchants, (i + 1) * merchants) for i in range(blocks)]
    for i in range(blocks):
        block = jnp.bitwise_xor(me, _offset(first + i, outer) + shift)
        score = jnp.dot(query[parts[i], :], keys[i], preferred_element_type=F32) / math.sqrt(width)
        score = score + bias_ref[rel_ref[block]]
        mine = (merch_slot[pl.ds(block, 1), :] == row) & (lane < count_ref[block])
        gates[parts[i], :] = jnp.where(mine, jax.nn.sigmoid(score), 0.0).astype(BF16)
    for i in range(blocks):
        sums[parts[i], :] = jnp.dot(
            gates[parts[i], :], values[i], preferred_element_type=F32
        ).astype(sums.dtype)


def aggregate(outer, first, shift, me, rel, count, bias, merch_slot, feats, wq, keys, values, dtype):
    blocks, width, block_len = keys.shape
    rows = feats.shape[0] * blocks // (merch_slot.shape[0] // 2)
    return pl.pallas_call(
        functools.partial(aggregate_kernel, outer, first, shift),
        out_shape=jax.ShapeDtypeStruct((rows, width), dtype),
        in_specs=[SMEM] * 4 + [VMEM] * 5,
        out_specs=VMEM,
        scratch_shapes=[
            pltpu.VMEM((rows, width), BF16),
            pltpu.VMEM((rows, block_len), BF16),
        ],
        compiler_params=_mb(6),
        cost_estimate=_cost(
            4 * rows * block_len * width + 2 * rows * width * width, 6 * 2**20, rows * block_len
        ),
        name="aggregate_odd" if shift else "aggregate_even",
    )(me, rel, count, bias, merch_slot, feats, wq, keys, values)


def combine_kernel(skip, mine, other, *outs):
    rows = outs[0].shape[0]
    for j, out in enumerate(outs):
        part = slice(j * rows, (j + 1) * rows)
        theirs = slice(skip + j * rows, skip + (j + 1) * rows)
        out[...] = (mine[part, :] + other[theirs, :].astype(F32)).astype(out.dtype)


def combine(groups, skip, mine, other, dtype):
    rows, width = mine.shape
    return pl.pallas_call(
        functools.partial(combine_kernel, skip),
        out_shape=(jax.ShapeDtypeStruct((rows // groups, width), dtype),) * groups,
        in_specs=[VMEM, VMEM],
        out_specs=(VMEM,) * groups,
        compiler_params=_mb(2),
        cost_estimate=_cost(0, 2 * 2**20),
        name="combine_cores",
    )(mine, other)


def plane_kernel(outer, me_ref, *refs):
    ins, out = refs[:-1], refs[-1]
    rows = out.shape[0] // outer
    for k in range(outer):
        part = slice(k * rows, (k + 1) * rows)
        total = ins[0][part, :]
        for other in ins[1:]:
            total = total + other[part, :].astype(F32)
        place = jnp.bitwise_xor(me_ref[0] >> 3, k)
        out[pl.ds(pl.multiple_of(place * rows, rows), rows), :] = total.astype(BF16)


def combine_plane(outer, me, parts):
    return pl.pallas_call(
        functools.partial(plane_kernel, outer),
        out_shape=jax.ShapeDtypeStruct(parts[0].shape, BF16),
        in_specs=[SMEM] + [VMEM] * len(parts),
        out_specs=VMEM,
        compiler_params=_mb(2),
        cost_estimate=_cost(0, 2**20),
        name="combine_plane",
    )(me, *parts)


def finish_kernel(feat, gain, wo, parts, out):
    merchants = feat.shape[0]
    total = parts[:merchants, :].astype(F32)
    for k in range(1, parts.shape[0] // merchants):
        total = total + parts[k * merchants : (k + 1) * merchants, :].astype(F32)
    update = feat[...].astype(F32) + jnp.dot(
        total.astype(BF16), wo[...], preferred_element_type=F32
    )
    scale = lax.rsqrt(jnp.mean(update * update, axis=-1, keepdims=True) + 1e-06)
    out[...] = (update * scale * gain[...]).astype(BF16)


def finish(feat, gain, wo, parts):
    return pl.pallas_call(
        finish_kernel,
        out_shape=jax.ShapeDtypeStruct(feat.shape, BF16),
        in_specs=[VMEM] * 4,
        out_specs=VMEM,
        compiler_params=_mb(2),
        name="finish",
    )(feat, gain.reshape(1, -1), wo, parts)


def per_device(
    acct_feat,
    merch_feat,
    key_weight,
    msg_weight,
    query_weight,
    out_weight,
    rel_bias,
    out_gain,
    slot_acct,
    slot_merch,
    block_rel,
    block_count,
):
    devices = lax.axis_size(AXES)
    me = lax.axis_index(AXES).astype(jnp.int32).reshape(1)
    inner = 4
    outer = devices // (2 * inner)

    def swap(value, mask):
        return lax.ppermute(value, AXES, [(s, s ^ mask) for s in range(devices)])

    def after(value, *others):
        return lax.optimization_barrier((value,) + others)[0]

    feats = jnp.concatenate([swap(merch_feat, 8 * k + 1) for k in range(outer)], axis=0)
    rows = gather(outer, me, slot_acct, acct_feat)
    feats = after(feats, rows[0])
    feats = jnp.concatenate([feats] + [swap(feats, 2 * j) for j in range(1, inner)], axis=0)

    weights = (key_weight, msg_weight)
    rest = (block_rel, block_count, rel_bias, slot_merch)
    blocks = inner * outer
    odd_keys, odd_values, far_keys, far_values = project(
        outer, ((0, blocks, 1), (outer, blocks, 0)), me, block_rel, rows, *weights
    )
    feats = after(feats, far_keys)
    even_feats = swap(feats, 1)
    odd = aggregate(outer, 0, 1, me, *rest, feats, query_weight, odd_keys, odd_values, BF16)
    other = swap(odd, 1)
    far = aggregate(
        outer, outer, 0, me, *rest, even_feats, query_weight, far_keys, far_values, F32
    )
    parts = combine(inner - 1, outer * merch_feat.shape[0], far, other, BF16)

    here = after(me, *parts)
    near_keys, near_values = project(
        outer, ((0, outer, 0),), here, block_rel, rows[1:], *weights
    )
    near = aggregate(
        outer, 0, 0, here, *rest, even_feats, query_weight, near_keys, near_values, F32
    )
    (near,) = combine(1, 0, near, other, F32)
    parts = combine_plane(
        outer, me, [near] + [swap(parts[j - 1], 2 * j) for j in reversed(range(1, inner))]
    )
    groups = [[base + 8 * k for k in range(outer)] for base in range(8)]
    parts = lax.all_to_all(
        parts, AXES, split_axis=0, concat_axis=0, tiled=True, axis_index_groups=groups
    )
    return finish(merch_feat, out_gain, out_weight, parts)


def solution(mesh):
    placed = (
        P(("acct", "merch"), None),
        P(("acct", "merch"), None),
        P(),
        P(),
        P(),
        P(),
        P(),
        P(),
        P(("acct", "merch"), None),
        P(("acct", "merch"), None),
        P(("acct", "merch")),
        P(("acct", "merch")),
    )
    return jax.shard_map(
        per_device,
        mesh=mesh,
        in_specs=placed,
        out_specs=P(("acct", "merch"), None),
        check_vma=False,
    )
```

time: 52.9 us -> 50.9 us (0.962)
  blocking collectives: 0 us -> 10.6 us
  waiting for transfers between devices: 10.4 us -> 4.35 us
  starting transfers between devices: 17.5 us -> 13.1 us
  Pallas kernels: 23.7 us -> 21.6 us
    all_to_all x0 -> x1, blocking collectives: none -> 10.6 us  [per_device(): lax.all_to_all(parts, AXES, split_axis=0, concat_axis=0, tiled=True, axis...]
    ppermute x15 -> x12, waiting for transfers between devices: 10.4 us -> 4.35 us  [swap(): return lax.ppermute(value, AXES, [(s, s ^ mask) for s in range(devices)])]
    ppermute x15 -> x12, starting transfers between devices: 17.5 us -> 13.1 us  [swap(): return lax.ppermute(value, AXES, [(s, s ^ mask) for s in range(devices)])]
    pallas_call x1, Pallas kernels: 12.7 us -> 9.2 us  [gather(): pl.pallas_call(functools.partial(gather_kernel, outer), out_shape=(half,...]
    pallas_call x5 -> x8, Pallas kernels: 10.1 us -> 11.5 us  [the longest x2 7.32 us: project(): pl.pallas_call(functools.partial(project_kernel, outer, spans), out_shape...]
  transfers between devices with their start and end apart: 15 -> 12, of which waited for: 5 -> 4; matrix products, arithmetic and copies ran while one was open for 0% -> 0% of each run, Pallas kernels for 43% -> 41%
where the time goes in v12:
time: 50.9 us; the launch traced here: 50.6 us
  Pallas kernels  21.6 us (42%)
  starting transfers between devices  13.1 us (26%)
  blocking collectives  10.6 us (21%)
  waiting for transfers between devices  4.35 us (9%)
  local copies, waits for them, and re-layouts  0.77 us (2%)
    ppermute x12, starting transfers between devices, swap(): return lax.ppermute(value, AXES, [(s, s ^ mask) for s in range(devices)])  13.1 us
    all_to_all x1, blocking collectives, per_device(): lax.all_to_all(parts, AXES, split_axis=0, concat_axis=0, tiled=True, axis...  10.6 us
    pallas_call x1, Pallas kernels, gather(): pl.pallas_call(functools.partial(gather_kernel, outer), out_shape=(half,...  9.2 us
    pallas_call x2, Pallas kernels, project(): pl.pallas_call(functools.partial(project_kernel, outer, spans), out_shape...  7.32 us
    ppermute x12, waiting for transfers between devices, swap(): return lax.ppermute(value, AXES, [(s, s ^ mask) for s in range(devices)])  4.35 us
    pallas_call x3, Pallas kernels, aggregate(): pl.pallas_call(functools.partial(aggregate_kernel, outer, first, shift),...  3.97 us
  transfers between devices with their start and end apart: 12, of which 4 were waited for; matrix products, arithmetic and copies ran while one was open for 0% of the time, Pallas kernels for 41%

profile of v12, /device:TPU:0, one launch (start us, length us, event | category | flops | bytes accessed | tf_op | source)
XLA Modules:
  0.0 50.6 jit_solution(1183518117689568177)
XLA Ops:
  0.0 3.5 %collective-permute-start.2 = (bf16[32,512]{1,0:T(8,128)(2,1)}, bf16[32,512]{1,0:T(8,128)(2,1)S(1)}, u32[]{:S(2)}, u32[]{:S(2)}) collective-permute-start(bf16[32,512]{1,0:T(8,128)(2,1)} %feat.1), channel_id=1, source_target_pairs={{0,17},{1,16},{2,19},{3,18},{4,21},{5,20},{6,23},{7,22},{8,25},{9,... | collective-permute-start | bytes 98312 | tf_op jit(solution)/shard_map/ppermute | solution.py:291
  3.5 1.9 %collective-permute-start.1 = (bf16[32,512]{1,0:T(8,128)(2,1)}, bf16[32,512]{1,0:T(8,128)(2,1)S(1)}, u32[]{:S(2)}, u32[]{:S(2)}) collective-permute-start(bf16[32,512]{1,0:T(8,128)(2,1)} %feat.1), channel_id=1, source_target_pairs={{0,9},{1,8},{2,11},{3,10},{4,13},{5,12},{6,15},{7,14},{8,1},{9,0},... | collective-permute-start | bytes 98312 | tf_op jit(solution)/shard_map/ppermute | solution.py:291
  5.3 0.0 collective-permute-start
  5.3 0.7 %copy-done.6 = s32[32,128]{1,0:T(8,128)S(1)} copy-done((s32[32,128]{1,0:T(8,128)S(1)}, s32[32,128]{1,0:T(8,128)}, u32[]{:S(2)}) %copy-start.6) | copy-done | bytes 16408
  6.1 9.2 %gather_slots.1 = (bf16[16,128,512]{2,1,0:T(8,128)(2,1)S(1)}, bf16[16,128,512]{2,1,0:T(8,128)(2,1)S(1)}) custom-call(s32[1]{0:T(128)} %bitcast.1.me_ref, s32[32,128]{1,0:T(8,128)S(1)} %copy-done.6, bf16[4096,512]{1,0:T(8,128)(2,1)} %acct_hbm.1), custom_call_target="tpu_custom_call" | custom-call | bytes 20971520 | tf_op jit(solution)/shard_map/gather_slots/pallas_call | solution.py:94
  15.3 2.8 %collective-permute-start.6 = (bf16[128,512]{1,0:T(8,128)(2,1)S(1)}, bf16[128,512]{1,0:T(8,128)(2,1)S(1)}, u32[]{:S(2)}, u32[]{:S(2)}) collective-permute-start(bf16[128,512]{1,0:T(8,128)(2,1)S(1)} %pad_maximum_fusion.1), channel_id=1, source_target_pairs={{0,6},{1,7},{2,4},{3,5},{4,2},{5,3},{6,0},{7,1},{8,14},{9,15},{10,... | collective-permute-start | bytes 393224 | tf_op jit(solution)/shard_map/ppermute | solution.py:291
  18.2 0.5 collective-permute-start.5
  18.7 0.2 collective-permute-start.4
  18.9 0.0 copy-start.4
  18.9 0.0 copy-start.8
  18.9 0.0 copy-start.9
  18.9 6.0 %project_slots.2 = (bf16[16,512,128]{2,1,0:T(8,128)(2,1)S(1)}, bf16[16,128,512]{2,1,0:T(8,128)(2,1)S(1)}, bf16[12,512,128]{2,1,0:T(8,128)(2,1)S(1)}, bf16[12,128,512]{2,1,0:T(8,128)(2,1)S(1)}) custom-call(s32[1]{0:T(128)} %bitcast.1.me_ref, s32[32]{0:T(128)S(1)} %copy-done.7, bf16[4,512,512]{2,1,0:T(8,128)(2,1)S(1)} %copy-done.1, ...), custom_call_target="tpu_custom_call" | custom-call | flops 3758096384 | bytes 14680064 | tf_op jit(solution)/shard_map/project_slots/pallas_call | solution.py:145
  25.0 0.1 collective-permute-done.5
  25.0 0.1 collective-permute-done.4
  25.1 0.1 collective-permute-start.7
  25.3 1.5 %aggregate_odd.1 = bf16[512,512]{1,0:T(8,128)(2,1)S(1)} custom-call(s32[1]{0:T(128)} %bitcast.1.me_ref, s32[32]{0:T(128)S(1)} %copy-done.7, s32[32]{0:T(128)S(1)} %copy-done.8, f32[4]{0:T(128)S(1)} %copy-done.9, s32[32,128]{1,0:T(8,128)S(1)} %copy-done.4, bf16[512,512]{1,0:T(8,128)(2,1)S(1)} %pad_maximum_fusion.feats, bf16[512,512]{1,0:T(8,128)(2,1)S(1)} %copy-done, ...), custom_call_target="tpu_custom_call" | custom-call | flops 402653184 | bytes 6291456 | tf_op jit(solution)/shard_map/aggregate_odd/pallas_call | solution.py:186
  26.8 0.5 %collective-permute-start.8 = (bf16[512,512]{1,0:T(8,128)(2,1)S(1)}, bf16[512,512]{1,0:T(8,128)(2,1)S(1)}, u32[]{:S(2)}, u32[]{:S(2)}) collective-permute-start(bf16[512,512]{1,0:T(8,128)(2,1)S(1)} %aggregate_odd.1), channel_id=1, source_target_pairs={{0,1},{1,0},{2,3},{3,2},{4,5},{5,4},{6,7},{7,6},{8,9},{9,8},{10,11... | collective-permute-start | bytes 1572872 | tf_op jit(solution)/shard_map/ppermute | solution.py:291
  27.3 1.3 %aggregate_even.2.mine = f32[384,512]{1,0:T(8,128)S(1)} custom-call(s32[1]{0:T(128)} %bitcast.1.me_ref, s32[32]{0:T(128)S(1)} %copy-done.7, s32[32]{0:T(128)S(1)} %copy-done.8, f32[4]{0:T(128)S(1)} %copy-done.9, s32[32,128]{1,0:T(8,128)S(1)} %copy-done.4, bf16[512,512]{1,0:T(8,128)(2,1)S(1)} %collective-permute-done.7.feats, bf16[512,512]{1,0:T(8,128)(2,1)S(1)} %copy-done, ...), custom_call_target="tpu_custom_call" | custom-call | flops 301989888 | bytes 6291456 | tf_op jit(solution)/shard_map/aggregate_even/pallas_call | solution.py:186
  28.7 0.2 collective-permute-done.8.other
  28.9 0.1 combine_cores.2
  29.0 1.8 %collective-permute-start.11 = (bf16[128,512]{1,0:T(8,128)(2,1)S(1)}, bf16[128,512]{1,0:T(8,128)(2,1)S(1)}, u32[]{:S(2)}, u32[]{:S(2)}) collective-permute-start(bf16[128,512]{1,0:T(8,128)(2,1)S(1)} %get-tuple-element.27), channel_id=1, source_target_pairs={{0,2},{1,3},{2,0},{3,1},{4,6},{5,7},{6,4},{7,5},{8,10},{9,11},{10,... | collective-permute-start | bytes 393224 | tf_op jit(solution)/shard_map/ppermute | solution.py:291
  30.7 1.5 %collective-permute-start.10 = (bf16[128,512]{1,0:T(8,128)(2,1)S(1)}, bf16[128,512]{1,0:T(8,128)(2,1)S(1)}, u32[]{:S(2)}, u32[]{:S(2)}) collective-permute-start(bf16[128,512]{1,0:T(8,128)(2,1)S(1)} %get-tuple-element.28), channel_id=1, source_target_pairs={{0,4},{1,5},{2,6},{3,7},{4,0},{5,1},{6,2},{7,3},{8,12},{9,13},{10,... | collective-permute-start | bytes 393224 | tf_op jit(solution)/shard_map/ppermute | solution.py:291
  32.3 0.3 collective-permute-start.9
  32.5 1.3 %project_slots.3 = (bf16[4,512,128]{2,1,0:T(8,128)(2,1)S(1)}, bf16[4,128,512]{2,1,0:T(8,128)(2,1)S(1)}) custom-call(s32[1]{0:T(128)} %bitcast.1.me_ref, s32[32]{0:T(128)S(1)} %copy-done.7, bf16[4,512,512]{2,1,0:T(8,128)(2,1)S(1)} %copy-done.1, bf16[4,512,512]{2,1,0:T(8,128)(2,1)S(1)} %copy-done.2, bf16[16,128,512]{2,1,0:T(8,128)(2,1)S(1)} %get-tuple-element.21.refs_1_.refs_0_), custom_call_target="tpu_custom_call" | custom-call | flops 536870912 | bytes 2097152 | tf_op jit(solution)/shard_map/project_slots/pallas_call | solution.py:145
  33.9 0.0 copy-start.3
  33.9 0.0 copy-start.5
  33.9 0.0 copy-start.10
  33.9 1.1 %aggregate_even.3.mine = f32[128,512]{1,0:T(8,128)S(1)} custom-call(s32[1]{0:T(128)} %bitcast.1.me_ref, s32[32]{0:T(128)S(1)} %copy-done.7, s32[32]{0:T(128)S(1)} %copy-done.8, f32[4]{0:T(128)S(1)} %copy-done.9, s32[32,128]{1,0:T(8,128)S(1)} %copy-done.4, bf16[512,512]{1,0:T(8,128)(2,1)S(1)} %collective-permute-done.7.feats, bf16[512,512]{1,0:T(8,128)(2,1)S(1)} %copy-done, ...), custom_call_target="tpu_custom_call" | custom-call | flops 100663296 | bytes 6291456 | tf_op jit(solution)/shard_map/aggregate_even/pallas_call | solution.py:186
  35.0 4.0 %collective-permute-done.10.refs_2_ = bf16[128,512]{1,0:T(8,128)(2,1)S(1)} collective-permute-done((bf16[128,512]{1,0:T(8,128)(2,1)S(1)}, bf16[128,512]{1,0:T(8,128)(2,1)S(1)}, u32[]{:S(2)}, u32[]{:S(2)}) %collective-permute-start.10) | collective-permute-done | bytes 131104 | tf_op jit(solution)/shard_map/ppermute | solution.py:291
  39.0 0.1 combine_plane.1
  39.1 10.6 %all_to_all.11 = bf16[4,32,512]{2,1,0:T(8,128)(2,1)S(1)} all-to-all(bf16[4,32,512]{2,1,0:T(8,128)(2,1)S(1)} %bitcast.4), channel_id=1, replica_groups={{0,8,16,24},{1,9,17,25},{2,10,18,26},{3,11,19,27},{4,12,20,28},{5,13,21..., dimensions={0} | all-to-all | bytes 262144 | tf_op jit(solution)/shard_map/all_to_all | solution.py:328
  49.7 0.9 %finish.1 = bf16[32,512]{1,0:T(8,128)(2,1)} custom-call(bf16[32,512]{1,0:T(8,128)(2,1)S(1)} %copy-done.5, f32[1,512]{1,0:T(1,128)S(1)} %bitcast.6, bf16[512,512]{1,0:T(8,128)(2,1)S(1)} %copy-done.3, bf16[128,512]{1,0:T(8,128)(2,1)S(1)} %bitcast.5), custom_call_target="tpu_custom_call" | custom-call | tf_op jit(solution)/shard_map/finish/pallas_call | solution.py:261
  (27 shorter events, 0.1 us)
Async XLA Ops:
  0.0 15.3 %collective-permute-start.2 = (bf16[32,512]{1,0:T(8,128)(2,1)}, bf16[32,512]{1,0:T(8,128)(2,1)S(1)}, u32[]{:S(2)}, u32[]{:S(2)}) collective-permute-start(bf16[32,512]{1,0:T(8,128)(2,1)} %feat.1), channel_id=1, source_target_pairs={{0,17},{1,16},{2,19},{3,18},{4,21},{5,20},{6,23},{7,22},{8,25},{9,... | collective-permute-start | bytes 98312 | tf_op jit(solution)/shard_map/ppermute | solution.py:291
  3.5 11.8 %collective-permute-start.1 = (bf16[32,512]{1,0:T(8,128)(2,1)}, bf16[32,512]{1,0:T(8,128)(2,1)S(1)}, u32[]{:S(2)}, u32[]{:S(2)}) collective-permute-start(bf16[32,512]{1,0:T(8,128)(2,1)} %feat.1), channel_id=1, source_target_pairs={{0,9},{1,8},{2,11},{3,10},{4,13},{5,12},{6,15},{7,14},{8,1},{9,0},... | collective-permute-start | bytes 98312 | tf_op jit(solution)/shard_map/ppermute | solution.py:291
  5.3 10.0 %collective-permute-start = (bf16[32,512]{1,0:T(8,128)(2,1)}, bf16[32,512]{1,0:T(8,128)(2,1)S(1)}, u32[]{:S(2)}, u32[]{:S(2)}) collective-permute-start(bf16[32,512]{1,0:T(8,128)(2,1)} %feat.1), channel_id=1, source_target_pairs={{0,1},{1,0},{2,3},{3,2},{4,5},{5,4},{6,7},{7,6},{8,9},{9,8},{10,11... | collective-permute-start | bytes 98312 | tf_op jit(solution)/shard_map/ppermute | solution.py:291
  5.3 10.0 %collective-permute-start.3 = (bf16[32,512]{1,0:T(8,128)(2,1)}, bf16[32,512]{1,0:T(8,128)(2,1)S(1)}, u32[]{:S(2)}, u32[]{:S(2)}) collective-permute-start(bf16[32,512]{1,0:T(8,128)(2,1)} %feat.1), channel_id=1, source_target_pairs={{0,25},{1,24},{2,27},{3,26},{4,29},{5,28},{6,31},{7,30},{8,17},{9,... | collective-permute-start | bytes 98312 | tf_op jit(solution)/shard_map/ppermute | solution.py:291
  5.3 0.7 %copy-start.6 = (s32[32,128]{1,0:T(8,128)S(1)}, s32[32,128]{1,0:T(8,128)}, u32[]{:S(2)}) copy-start(s32[32,128]{1,0:T(8,128)} %slots_ref.1) | copy-start | bytes 49156
  6.1 12.8 %copy-start.1 = (bf16[4,512,512]{2,1,0:T(8,128)(2,1)S(1)}, bf16[4,512,512]{2,1,0:T(8,128)(2,1)}, u32[]{:S(2)}) copy-start(bf16[4,512,512]{2,1,0:T(8,128)(2,1)} %kw.3) | copy-start | bytes 6291460
  6.1 12.8 %copy-start.2 = (bf16[4,512,512]{2,1,0:T(8,128)(2,1)S(1)}, bf16[4,512,512]{2,1,0:T(8,128)(2,1)}, u32[]{:S(2)}) copy-start(bf16[4,512,512]{2,1,0:T(8,128)(2,1)} %mw.3) | copy-start | bytes 6291460
  6.1 12.8 %copy-start.7 = (s32[32]{0:T(128)S(1)}, s32[32]{0:T(128)}, u32[]{:S(2)}) copy-start(s32[32]{0:T(128)} %rel_ref.9) | copy-start | bytes 388
  15.3 9.6 %collective-permute-start.6 = (bf16[128,512]{1,0:T(8,128)(2,1)S(1)}, bf16[128,512]{1,0:T(8,128)(2,1)S(1)}, u32[]{:S(2)}, u32[]{:S(2)}) collective-permute-start(bf16[128,512]{1,0:T(8,128)(2,1)S(1)} %pad_maximum_fusion.1), channel_id=1, source_target_pairs={{0,6},{1,7},{2,4},{3,5},{4,2},{5,3},{6,0},{7,1},{8,14},{9,15},{10,... | collective-permute-start | bytes 393224 | tf_op jit(solution)/shard_map/ppermute | solution.py:291
  18.2 6.8 %collective-permute-start.5 = (bf16[128,512]{1,0:T(8,128)(2,1)S(1)}, bf16[128,512]{1,0:T(8,128)(2,1)S(1)}, u32[]{:S(2)}, u32[]{:S(2)}) collective-permute-start(bf16[128,512]{1,0:T(8,128)(2,1)S(1)} %pad_maximum_fusion.1), channel_id=1, source_target_pairs={{0,4},{1,5},{2,6},{3,7},{4,0},{5,1},{6,2},{7,3},{8,12},{9,13},{10,... | collective-permute-start | bytes 393224 | tf_op jit(solution)/shard_map/ppermute | solution.py:291
  18.7 6.4 %collective-permute-start.4 = (bf16[128,512]{1,0:T(8,128)(2,1)S(1)}, bf16[128,512]{1,0:T(8,128)(2,1)S(1)}, u32[]{:S(2)}, u32[]{:S(2)}) collective-permute-start(bf16[128,512]{1,0:T(8,128)(2,1)S(1)} %pad_maximum_fusion.1), channel_id=1, source_target_pairs={{0,2},{1,3},{2,0},{3,1},{4,6},{5,7},{6,4},{7,5},{8,10},{9,11},{10,... | collective-permute-start | bytes 393224 | tf_op jit(solution)/shard_map/ppermute | solution.py:291
  18.9 6.3 %copy-start = (bf16[512,512]{1,0:T(8,128)(2,1)S(1)}, bf16[512,512]{1,0:T(8,128)(2,1)}, u32[]{:S(2)}) copy-start(bf16[512,512]{1,0:T(8,128)(2,1)} %wq.5) | copy-start | bytes 1572868
  18.9 6.3 %copy-start.4 = (s32[32,128]{1,0:T(8,128)S(1)}, s32[32,128]{1,0:T(8,128)}, u32[]{:S(2)}) copy-start(s32[32,128]{1,0:T(8,128)} %merch_slot.5) | copy-start | bytes 49156
  18.9 6.3 %copy-start.8 = (s32[32]{0:T(128)S(1)}, s32[32]{0:T(128)}, u32[]{:S(2)}) copy-start(s32[32]{0:T(128)} %count_ref.5) | copy-start | bytes 388
  18.9 6.3 %copy-start.9 = (f32[4]{0:T(128)S(1)}, f32[4]{0:T(128)}, u32[]{:S(2)}) copy-start(f32[4]{0:T(128)} %bias_ref.5) | copy-start | bytes 52
  25.1 2.2 %collective-permute-start.7 = (bf16[512,512]{1,0:T(8,128)(2,1)S(1)}, bf16[512,512]{1,0:T(8,128)(2,1)S(1)}, u32[]{:S(2)}, u32[]{:S(2)}) collective-permute-start(bf16[512,512]{1,0:T(8,128)(2,1)S(1)} %pad_maximum_fusion.feats), channel_id=1, source_target_pairs={{0,1},{1,0},{2,3},{3,2},{4,5},{5,4},{6,7},{7,6},{8,9},{9,8},{10,11... | collective-permute-start | bytes 1572872 | tf_op jit(solution)/shard_map/ppermute | solution.py:291
  26.8 2.1 %collective-permute-start.8 = (bf16[512,512]{1,0:T(8,128)(2,1)S(1)}, bf16[512,512]{1,0:T(8,128)(2,1)S(1)}, u32[]{:S(2)}, u32[]{:S(2)}) collective-permute-start(bf16[512,512]{1,0:T(8,128)(2,1)S(1)} %aggregate_odd.1), channel_id=1, source_target_pairs={{0,1},{1,0},{2,3},{3,2},{4,5},{5,4},{6,7},{7,6},{8,9},{9,8},{10,11... | collective-permute-start | bytes 1572872 | tf_op jit(solution)/shard_map/ppermute | solution.py:291
  29.0 6.1 %collective-permute-start.11 = (bf16[128,512]{1,0:T(8,128)(2,1)S(1)}, bf16[128,512]{1,0:T(8,128)(2,1)S(1)}, u32[]{:S(2)}, u32[]{:S(2)}) collective-permute-start(bf16[128,512]{1,0:T(8,128)(2,1)S(1)} %get-tuple-element.27), channel_id=1, source_target_pairs={{0,2},{1,3},{2,0},{3,1},{4,6},{5,7},{6,4},{7,5},{8,10},{9,11},{10,... | collective-permute-start | bytes 393224 | tf_op jit(solution)/shard_map/ppermute | solution.py:291
  30.7 8.3 %collective-permute-start.10 = (bf16[128,512]{1,0:T(8,128)(2,1)S(1)}, bf16[128,512]{1,0:T(8,128)(2,1)S(1)}, u32[]{:S(2)}, u32[]{:S(2)}) collective-permute-start(bf16[128,512]{1,0:T(8,128)(2,1)S(1)} %get-tuple-element.28), channel_id=1, source_target_pairs={{0,4},{1,5},{2,6},{3,7},{4,0},{5,1},{6,2},{7,3},{8,12},{9,13},{10,... | collective-permute-start | bytes 393224 | tf_op jit(solution)/shard_map/ppermute | solution.py:291
  32.3 6.8 %collective-permute-start.9 = (bf16[128,512]{1,0:T(8,128)(2,1)S(1)}, bf16[128,512]{1,0:T(8,128)(2,1)S(1)}, u32[]{:S(2)}, u32[]{:S(2)}) collective-permute-start(bf16[128,512]{1,0:T(8,128)(2,1)S(1)} %get-tuple-element.29), channel_id=1, source_target_pairs={{0,6},{1,7},{2,4},{3,5},{4,2},{5,3},{6,0},{7,1},{8,14},{9,15},{10,... | collective-permute-start | bytes 393224 | tf_op jit(solution)/shard_map/ppermute | solution.py:291
  33.9 15.9 %copy-start.3 = (bf16[512,512]{1,0:T(8,128)(2,1)S(1)}, bf16[512,512]{1,0:T(8,128)(2,1)}, u32[]{:S(2)}) copy-start(bf16[512,512]{1,0:T(8,128)(2,1)} %wo.1) | copy-start | bytes 1572868
  33.9 15.9 %copy-start.5 = (bf16[32,512]{1,0:T(8,128)(2,1)S(1)}, bf16[32,512]{1,0:T(8,128)(2,1)}, u32[]{:S(2)}) copy-start(bf16[32,512]{1,0:T(8,128)(2,1)} %feat.1) | copy-start | bytes 98308
  33.9 15.8 %copy-start.10 = (f32[512]{0:T(512)S(1)}, f32[512]{0:T(512)}, u32[]{:S(2)}) copy-start(f32[512]{0:T(512)} %param.19) | copy-start | bytes 6148

commit v13 on v12

--- a/solution.py
+++ b/solution.py
@@ -221,35 +221,38 @@
     )(mine, other)
 
 
-def plane_kernel(outer, me_ref, *refs):
-    ins, out = refs[:-1], refs[-1]
-    rows = out.shape[0] // outer
-    for k in range(outer):
+def halve_kernel(rows, *refs):
+    ins, keep, send = refs[:-2], refs[-2], refs[-1]
+    for k in range(ins[0].shape[0] // rows):
         part = slice(k * rows, (k + 1) * rows)
         total = ins[0][part, :]
         for other in ins[1:]:
             total = total + other[part, :].astype(F32)
-        place = jnp.bitwise_xor(me_ref[0] >> 3, k)
-        out[pl.ds(pl.multiple_of(place * rows, rows), rows), :] = total.astype(BF16)
-
-
-def combine_plane(outer, me, parts):
-    return pl.pallas_call(
-        functools.partial(plane_kernel, outer),
-        out_shape=jax.ShapeDtypeStruct(parts[0].shape, BF16),
-        in_specs=[SMEM] + [VMEM] * len(parts),
-        out_specs=VMEM,
+        to = slice(k // 2 * rows, (k // 2 + 1) * rows)
+        if k % 2:
+            send[to, :] = total.astype(BF16)
+        else:
+            keep[to, :] = total
+
+
+def halve(rows, parts):
+    held, width = parts[0].shape
+    return pl.pallas_call(
+        functools.partial(halve_kernel, rows),
+        out_shape=(
+            jax.ShapeDtypeStruct((held // 2, width), F32),
+            jax.ShapeDtypeStruct((held // 2, width), BF16),
+        ),
+        in_specs=[VMEM] * len(parts),
+        out_specs=(VMEM, VMEM),
         compiler_params=_mb(2),
         cost_estimate=_cost(0, 2**20),
-        name="combine_plane",
-    )(me, *parts)
-
-
-def finish_kernel(feat, gain, wo, parts, out):
-    merchants = feat.shape[0]
-    total = parts[:merchants, :].astype(F32)
-    for k in range(1, parts.shape[0] // merchants):
-        total = total + parts[k * merchants : (k + 1) * merchants, :].astype(F32)
+        name="halve_sums",
+    )(*parts)
+
+
+def finish_kernel(feat, gain, wo, mine, other, out):
+    total = mine[...] + other[...].astype(F32)
     update = feat[...].astype(F32) + jnp.dot(
         total.astype(BF16), wo[...], preferred_element_type=F32
     )
@@ -257,15 +260,15 @@
     out[...] = (update * scale * gain[...]).astype(BF16)
 
 
-def finish(feat, gain, wo, parts):
+def finish(feat, gain, wo, mine, other):
     return pl.pallas_call(
         finish_kernel,
         out_shape=jax.ShapeDtypeStruct(feat.shape, BF16),
-        in_specs=[VMEM] * 4,
+        in_specs=[VMEM] * 5,
         out_specs=VMEM,
         compiler_params=_mb(2),
         name="finish",
-    )(feat, gain.reshape(1, -1), wo, parts)
+    )(feat, gain.reshape(1, -1), wo, mine, other)
 
 
 def per_device(
@@ -321,14 +324,13 @@
         outer, 0, 0, here, *rest, even_feats, query_weight, near_keys, near_values, F32
     )
     (near,) = combine(1, 0, near, other, F32)
-    parts = combine_plane(
-        outer, me, [near] + [swap(parts[j - 1], 2 * j) for j in reversed(range(1, inner))]
-    )
-    groups = [[base + 8 * k for k in range(outer)] for base in range(8)]
-    parts = lax.all_to_all(
-        parts, AXES, split_axis=0, concat_axis=0, tiled=True, axis_index_groups=groups
-    )
-    return finish(merch_feat, out_gain, out_weight, parts)
+    parts = [near] + [swap(parts[j - 1], 2 * j) for j in reversed(range(1, inner))]
+    mask = 8
+    while mask < devices:
+        keep, send = halve(merch_feat.shape[0], parts)
+        parts = [keep, swap(send, mask)]
+        mask *= 2
+    return finish(merch_feat, out_gain, out_weight, *parts)
 
 
 def solution(mesh):

time: 50.9 us -> 49.5 us (0.972)
  blocking collectives: 10.6 us -> 0 us
  waiting for transfers between devices: 4.35 us -> 10.6 us
  starting transfers between devices: 13.1 us -> 16 us
    all_to_all x1 -> x0, blocking collectives: 10.6 us -> none  [per_device(): lax.all_to_all(parts, AXES, split_axis=0, concat_axis=0, tiled=True, axis...]
    ppermute x12 -> x14, waiting for transfers between devices: 4.35 us -> 10.6 us  [swap(): return lax.ppermute(value, AXES, [(s, s ^ mask) for s in range(devices)])]
    ppermute x12 -> x14, starting transfers between devices: 13.1 us -> 16 us  [swap(): return lax.ppermute(value, AXES, [(s, s ^ mask) for s in range(devices)])]
  transfers between devices with their start and end apart: 12 -> 14, of which waited for: 4 -> 6; matrix products, arithmetic and copies ran while one was open for 0% -> 0% of each run, Pallas kernels for 41% -> 42%
where the time goes in v13:
time: 49.5 us; the launch traced here: 49.3 us
  Pallas kernels  21.6 us (44%)
  starting transfers between devices  16 us (32%)
  waiting for transfers between devices  10.6 us (21%)
  local copies, waits for them, and re-layouts  0.77 us (2%)
    ppermute x14, starting transfers between devices, swap(): return lax.ppermute(value, AXES, [(s, s ^ mask) for s in range(devices)])  16 us
    ppermute x14, waiting for transfers between devices, swap(): return lax.ppermute(value, AXES, [(s, s ^ mask) for s in range(devices)])  10.6 us
    pallas_call x1, Pallas kernels, gather(): pl.pallas_call(functools.partial(gather_kernel, outer), out_shape=(half,...  9.2 us
    pallas_call x2, Pallas kernels, project(): pl.pallas_call(functools.partial(project_kernel, outer, spans), out_shape...  7.31 us
    pallas_call x3, Pallas kernels, aggregate(): pl.pallas_call(functools.partial(aggregate_kernel, outer, first, shift),...  3.97 us
  transfers between devices with their start and end apart: 14, of which 6 were waited for; matrix products, arithmetic and copies ran while one was open for 0% of the time, Pallas kernels for 42%

profile of v13, /device:TPU:0, one launch (start us, length us, event | category | flops | bytes accessed | tf_op | source)
XLA Modules:
  0.0 49.3 jit_solution(8593823177908881049)
XLA Ops:
  0.0 3.5 %collective-permute-start.2 = (bf16[32,512]{1,0:T(8,128)(2,1)}, bf16[32,512]{1,0:T(8,128)(2,1)S(1)}, u32[]{:S(2)}, u32[]{:S(2)}) collective-permute-start(bf16[32,512]{1,0:T(8,128)(2,1)} %feat.1), channel_id=1, source_target_pairs={{0,17},{1,16},{2,19},{3,18},{4,21},{5,20},{6,23},{7,22},{8,25},{9,... | collective-permute-start | bytes 98312 | tf_op jit(solution)/shard_map/ppermute | solution.py:294
  3.5 1.9 %collective-permute-start.1 = (bf16[32,512]{1,0:T(8,128)(2,1)}, bf16[32,512]{1,0:T(8,128)(2,1)S(1)}, u32[]{:S(2)}, u32[]{:S(2)}) collective-permute-start(bf16[32,512]{1,0:T(8,128)(2,1)} %feat.1), channel_id=1, source_target_pairs={{0,9},{1,8},{2,11},{3,10},{4,13},{5,12},{6,15},{7,14},{8,1},{9,0},... | collective-permute-start | bytes 98312 | tf_op jit(solution)/shard_map/ppermute | solution.py:294
  5.3 0.7 %copy-done.6 = s32[32,128]{1,0:T(8,128)S(1)} copy-done((s32[32,128]{1,0:T(8,128)S(1)}, s32[32,128]{1,0:T(8,128)}, u32[]{:S(2)}) %copy-start.6) | copy-done | bytes 16408
  6.1 9.2 %gather_slots.1 = (bf16[16,128,512]{2,1,0:T(8,128)(2,1)S(1)}, bf16[16,128,512]{2,1,0:T(8,128)(2,1)S(1)}) custom-call(s32[1]{0:T(128)} %bitcast.1.me_ref, s32[32,128]{1,0:T(8,128)S(1)} %copy-done.6, bf16[4096,512]{1,0:T(8,128)(2,1)} %acct_hbm.1), custom_call_target="tpu_custom_call" | custom-call | bytes 20971520 | tf_op jit(solution)/shard_map/gather_slots/pallas_call | solution.py:94
  15.3 2.8 %collective-permute-start.6 = (bf16[128,512]{1,0:T(8,128)(2,1)S(1)}, bf16[128,512]{1,0:T(8,128)(2,1)S(1)}, u32[]{:S(2)}, u32[]{:S(2)}) collective-permute-start(bf16[128,512]{1,0:T(8,128)(2,1)S(1)} %pad_maximum_fusion.1), channel_id=1, source_target_pairs={{0,6},{1,7},{2,4},{3,5},{4,2},{5,3},{6,0},{7,1},{8,14},{9,15},{10,... | collective-permute-start | bytes 393224 | tf_op jit(solution)/shard_map/ppermute | solution.py:294
  18.2 0.5 %collective-permute-start.5 = (bf16[128,512]{1,0:T(8,128)(2,1)S(1)}, bf16[128,512]{1,0:T(8,128)(2,1)S(1)}, u32[]{:S(2)}, u32[]{:S(2)}) collective-permute-start(bf16[128,512]{1,0:T(8,128)(2,1)S(1)} %pad_maximum_fusion.1), channel_id=1, source_target_pairs={{0,4},{1,5},{2,6},{3,7},{4,0},{5,1},{6,2},{7,3},{8,12},{9,13},{10,... | collective-permute-start | bytes 393224 | tf_op jit(solution)/shard_map/ppermute | solution.py:294
  18.7 0.2 collective-permute-start.4
  18.9 0.0 copy-start.4
  18.9 0.0 copy-start.8
  18.9 0.0 copy-start.9
  18.9 6.0 %project_slots.2 = (bf16[16,512,128]{2,1,0:T(8,128)(2,1)S(1)}, bf16[16,128,512]{2,1,0:T(8,128)(2,1)S(1)}, bf16[12,512,128]{2,1,0:T(8,128)(2,1)S(1)}, bf16[12,128,512]{2,1,0:T(8,128)(2,1)S(1)}) custom-call(s32[1]{0:T(128)} %bitcast.1.me_ref, s32[32]{0:T(128)S(1)} %copy-done.7, bf16[4,512,512]{2,1,0:T(8,128)(2,1)S(1)} %copy-done.1, ...), custom_call_target="tpu_custom_call" | custom-call | flops 3758096384 | bytes 14680064 | tf_op jit(solution)/shard_map/project_slots/pallas_call | solution.py:145
  25.0 0.1 collective-permute-done.5
  25.0 0.1 collective-permute-done.4
  25.1 0.1 collective-permute-start.7
  25.3 1.5 %aggregate_odd.1 = bf16[512,512]{1,0:T(8,128)(2,1)S(1)} custom-call(s32[1]{0:T(128)} %bitcast.1.me_ref, s32[32]{0:T(128)S(1)} %copy-done.7, s32[32]{0:T(128)S(1)} %copy-done.8, f32[4]{0:T(128)S(1)} %copy-done.9, s32[32,128]{1,0:T(8,128)S(1)} %copy-done.4, bf16[512,512]{1,0:T(8,128)(2,1)S(1)} %pad_maximum_fusion.feats, bf16[512,512]{1,0:T(8,128)(2,1)S(1)} %copy-done, ...), custom_call_target="tpu_custom_call" | custom-call | flops 402653184 | bytes 6291456 | tf_op jit(solution)/shard_map/aggregate_odd/pallas_call | solution.py:186
  26.8 0.5 %collective-permute-start.8 = (bf16[512,512]{1,0:T(8,128)(2,1)S(1)}, bf16[512,512]{1,0:T(8,128)(2,1)S(1)}, u32[]{:S(2)}, u32[]{:S(2)}) collective-permute-start(bf16[512,512]{1,0:T(8,128)(2,1)S(1)} %aggregate_odd.1), channel_id=1, source_target_pairs={{0,1},{1,0},{2,3},{3,2},{4,5},{5,4},{6,7},{7,6},{8,9},{9,8},{10,11... | collective-permute-start | bytes 1572872 | tf_op jit(solution)/shard_map/ppermute | solution.py:294
  27.3 1.3 %aggregate_even.2.mine = f32[384,512]{1,0:T(8,128)S(1)} custom-call(s32[1]{0:T(128)} %bitcast.1.me_ref, s32[32]{0:T(128)S(1)} %copy-done.7, s32[32]{0:T(128)S(1)} %copy-done.8, f32[4]{0:T(128)S(1)} %copy-done.9, s32[32,128]{1,0:T(8,128)S(1)} %copy-done.4, bf16[512,512]{1,0:T(8,128)(2,1)S(1)} %collective-permute-done.7.feats, bf16[512,512]{1,0:T(8,128)(2,1)S(1)} %copy-done, ...), custom_call_target="tpu_custom_call" | custom-call | flops 301989888 | bytes 6291456 | tf_op jit(solution)/shard_map/aggregate_even/pallas_call | solution.py:186
  28.7 0.2 collective-permute-done.8.other
  28.9 0.1 combine_cores.2
  29.0 1.8 %collective-permute-start.11 = (bf16[128,512]{1,0:T(8,128)(2,1)S(1)}, bf16[128,512]{1,0:T(8,128)(2,1)S(1)}, u32[]{:S(2)}, u32[]{:S(2)}) collective-permute-start(bf16[128,512]{1,0:T(8,128)(2,1)S(1)} %get-tuple-element.31), channel_id=1, source_target_pairs={{0,2},{1,3},{2,0},{3,1},{4,6},{5,7},{6,4},{7,5},{8,10},{9,11},{10,... | collective-permute-start | bytes 393224 | tf_op jit(solution)/shard_map/ppermute | solution.py:294
  30.7 1.5 %collective-permute-start.10 = (bf16[128,512]{1,0:T(8,128)(2,1)S(1)}, bf16[128,512]{1,0:T(8,128)(2,1)S(1)}, u32[]{:S(2)}, u32[]{:S(2)}) collective-permute-start(bf16[128,512]{1,0:T(8,128)(2,1)S(1)} %get-tuple-element.32), channel_id=1, source_target_pairs={{0,4},{1,5},{2,6},{3,7},{4,0},{5,1},{6,2},{7,3},{8,12},{9,13},{10,... | collective-permute-start | bytes 393224 | tf_op jit(solution)/shard_map/ppermute | solution.py:294
  32.3 0.3 collective-permute-start.9
  32.5 1.3 %project_slots.3 = (bf16[4,512,128]{2,1,0:T(8,128)(2,1)S(1)}, bf16[4,128,512]{2,1,0:T(8,128)(2,1)S(1)}) custom-call(s32[1]{0:T(128)} %bitcast.1.me_ref, s32[32]{0:T(128)S(1)} %copy-done.7, bf16[4,512,512]{2,1,0:T(8,128)(2,1)S(1)} %copy-done.1, bf16[4,512,512]{2,1,0:T(8,128)(2,1)S(1)} %copy-done.2, bf16[16,128,512]{2,1,0:T(8,128)(2,1)S(1)} %get-tuple-element.25.refs_1_.refs_0_), custom_call_target="tpu_custom_call" | custom-call | flops 536870912 | bytes 2097152 | tf_op jit(solution)/shard_map/project_slots/pallas_call | solution.py:145
  33.9 0.0 copy-start.3
  33.9 1.1 %aggregate_even.3.mine = f32[128,512]{1,0:T(8,128)S(1)} custom-call(s32[1]{0:T(128)} %bitcast.1.me_ref, s32[32]{0:T(128)S(1)} %copy-done.7, s32[32]{0:T(128)S(1)} %copy-done.8, f32[4]{0:T(128)S(1)} %copy-done.9, s32[32,128]{1,0:T(8,128)S(1)} %copy-done.4, bf16[512,512]{1,0:T(8,128)(2,1)S(1)} %collective-permute-done.7.feats, bf16[512,512]{1,0:T(8,128)(2,1)S(1)} %copy-done, ...), custom_call_target="tpu_custom_call" | custom-call | flops 100663296 | bytes 6291456 | tf_op jit(solution)/shard_map/aggregate_even/pallas_call | solution.py:186
  35.0 4.0 %collective-permute-done.10.refs_2_ = bf16[128,512]{1,0:T(8,128)(2,1)S(1)} collective-permute-done((bf16[128,512]{1,0:T(8,128)(2,1)S(1)}, bf16[128,512]{1,0:T(8,128)(2,1)S(1)}, u32[]{:S(2)}, u32[]{:S(2)}) %collective-permute-start.10) | collective-permute-done | bytes 131104 | tf_op jit(solution)/shard_map/ppermute | solution.py:294
  39.0 0.1 halve_sums.2
  39.1 0.7 %collective-permute-start.12 = (bf16[64,512]{1,0:T(8,128)(2,1)S(1)}, bf16[64,512]{1,0:T(8,128)(2,1)S(1)}, u32[]{:S(2)}, u32[]{:S(2)}) collective-permute-start(bf16[64,512]{1,0:T(8,128)(2,1)S(1)} %get-tuple-element.38), channel_id=1, source_target_pairs={{0,8},{1,9},{2,10},{3,11},{4,12},{5,13},{6,14},{7,15},{8,0},{9,1},... | collective-permute-start | bytes 196616 | tf_op jit(solution)/shard_map/ppermute | solution.py:294
  39.8 3.6 %collective-permute-done.12.refs_1_ = bf16[64,512]{1,0:T(8,128)(2,1)S(1)} collective-permute-done((bf16[64,512]{1,0:T(8,128)(2,1)S(1)}, bf16[64,512]{1,0:T(8,128)(2,1)S(1)}, u32[]{:S(2)}, u32[]{:S(2)}) %collective-permute-start.12) | collective-permute-done | bytes 65568 | tf_op jit(solution)/shard_map/ppermute | solution.py:294
  43.5 2.2 %collective-permute-start.13 = (bf16[32,512]{1,0:T(8,128)(2,1)S(1)}, bf16[32,512]{1,0:T(8,128)(2,1)S(1)}, u32[]{:S(2)}, u32[]{:S(2)}) collective-permute-start(bf16[32,512]{1,0:T(8,128)(2,1)S(1)} %get-tuple-element.40), channel_id=1, source_target_pairs={{0,16},{1,17},{2,18},{3,19},{4,20},{5,21},{6,22},{7,23},{8,24},{9,... | collective-permute-start | bytes 98312 | tf_op jit(solution)/shard_map/ppermute | solution.py:294
  45.7 2.7 %collective-permute-done.13.other = bf16[32,512]{1,0:T(8,128)(2,1)S(1)} collective-permute-done((bf16[32,512]{1,0:T(8,128)(2,1)S(1)}, bf16[32,512]{1,0:T(8,128)(2,1)S(1)}, u32[]{:S(2)}, u32[]{:S(2)}) %collective-permute-start.13) | collective-permute-done | bytes 32800 | tf_op jit(solution)/shard_map/ppermute | solution.py:294
  48.3 0.9 %finish.1 = bf16[32,512]{1,0:T(8,128)(2,1)} custom-call(bf16[32,512]{1,0:T(8,128)(2,1)S(1)} %copy-done.5, f32[1,512]{1,0:T(1,128)S(1)} %bitcast.2, bf16[512,512]{1,0:T(8,128)(2,1)S(1)} %copy-done.3, f32[32,512]{1,0:T(8,128)S(1)} %get-tuple-element.39.mine, bf16[32,512]{1,0:T(8,128)(2,1)S(1)} %collective-permute-done.13.other), custom_call_target="tpu_custom_call" | custom-call | tf_op jit(solution)/shard_map/finish/pallas_call | solution.py:264
  (31 shorter events, 0.2 us)
Async XLA Ops:
  0.0 15.3 %collective-permute-start.2 = (bf16[32,512]{1,0:T(8,128)(2,1)}, bf16[32,512]{1,0:T(8,128)(2,1)S(1)}, u32[]{:S(2)}, u32[]{:S(2)}) collective-permute-start(bf16[32,512]{1,0:T(8,128)(2,1)} %feat.1), channel_id=1, source_target_pairs={{0,17},{1,16},{2,19},{3,18},{4,21},{5,20},{6,23},{7,22},{8,25},{9,... | collective-permute-start | bytes 98312 | tf_op jit(solution)/shard_map/ppermute | solution.py:294
  3.5 11.8 %collective-permute-start.1 = (bf16[32,512]{1,0:T(8,128)(2,1)}, bf16[32,512]{1,0:T(8,128)(2,1)S(1)}, u32[]{:S(2)}, u32[]{:S(2)}) collective-permute-start(bf16[32,512]{1,0:T(8,128)(2,1)} %feat.1), channel_id=1, source_target_pairs={{0,9},{1,8},{2,11},{3,10},{4,13},{5,12},{6,15},{7,14},{8,1},{9,0},... | collective-permute-start | bytes 98312 | tf_op jit(solution)/shard_map/ppermute | solution.py:294
  5.3 10.0 %collective-permute-start = (bf16[32,512]{1,0:T(8,128)(2,1)}, bf16[32,512]{1,0:T(8,128)(2,1)S(1)}, u32[]{:S(2)}, u32[]{:S(2)}) collective-permute-start(bf16[32,512]{1,0:T(8,128)(2,1)} %feat.1), channel_id=1, source_target_pairs={{0,1},{1,0},{2,3},{3,2},{4,5},{5,4},{6,7},{7,6},{8,9},{9,8},{10,11... | collective-permute-start | bytes 98312 | tf_op jit(solution)/shard_map/ppermute | solution.py:294
  5.3 10.0 %collective-permute-start.3 = (bf16[32,512]{1,0:T(8,128)(2,1)}, bf16[32,512]{1,0:T(8,128)(2,1)S(1)}, u32[]{:S(2)}, u32[]{:S(2)}) collective-permute-start(bf16[32,512]{1,0:T(8,128)(2,1)} %feat.1), channel_id=1, source_target_pairs={{0,25},{1,24},{2,27},{3,26},{4,29},{5,28},{6,31},{7,30},{8,17},{9,... | collective-permute-start | bytes 98312 | tf_op jit(solution)/shard_map/ppermute | solution.py:294
  5.3 0.7 %copy-start.6 = (s32[32,128]{1,0:T(8,128)S(1)}, s32[32,128]{1,0:T(8,128)}, u32[]{:S(2)}) copy-start(s32[32,128]{1,0:T(8,128)} %slots_ref.1) | copy-start | bytes 49156
  6.1 12.8 %copy-start.1 = (bf16[4,512,512]{2,1,0:T(8,128)(2,1)S(1)}, bf16[4,512,512]{2,1,0:T(8,128)(2,1)}, u32[]{:S(2)}) copy-start(bf16[4,512,512]{2,1,0:T(8,128)(2,1)} %kw.3) | copy-start | bytes 6291460
  6.1 12.8 %copy-start.2 = (bf16[4,512,512]{2,1,0:T(8,128)(2,1)S(1)}, bf16[4,512,512]{2,1,0:T(8,128)(2,1)}, u32[]{:S(2)}) copy-start(bf16[4,512,512]{2,1,0:T(8,128)(2,1)} %mw.3) | copy-start | bytes 6291460
  6.1 12.8 %copy-start.7 = (s32[32]{0:T(128)S(1)}, s32[32]{0:T(128)}, u32[]{:S(2)}) copy-start(s32[32]{0:T(128)} %rel_ref.9) | copy-start | bytes 388
  15.3 9.6 %collective-permute-start.6 = (bf16[128,512]{1,0:T(8,128)(2,1)S(1)}, bf16[128,512]{1,0:T(8,128)(2,1)S(1)}, u32[]{:S(2)}, u32[]{:S(2)}) collective-permute-start(bf16[128,512]{1,0:T(8,128)(2,1)S(1)} %pad_maximum_fusion.1), channel_id=1, source_target_pairs={{0,6},{1,7},{2,4},{3,5},{4,2},{5,3},{6,0},{7,1},{8,14},{9,15},{10,... | collective-permute-start | bytes 393224 | tf_op jit(solution)/shard_map/ppermute | solution.py:294
  18.2 6.8 %collective-permute-start.5 = (bf16[128,512]{1,0:T(8,128)(2,1)S(1)}, bf16[128,512]{1,0:T(8,128)(2,1)S(1)}, u32[]{:S(2)}, u32[]{:S(2)}) collective-permute-start(bf16[128,512]{1,0:T(8,128)(2,1)S(1)} %pad_maximum_fusion.1), channel_id=1, source_target_pairs={{0,4},{1,5},{2,6},{3,7},{4,0},{5,1},{6,2},{7,3},{8,12},{9,13},{10,... | collective-permute-start | bytes 393224 | tf_op jit(solution)/shard_map/ppermute | solution.py:294
  18.7 6.4 %collective-permute-start.4 = (bf16[128,512]{1,0:T(8,128)(2,1)S(1)}, bf16[128,512]{1,0:T(8,128)(2,1)S(1)}, u32[]{:S(2)}, u32[]{:S(2)}) collective-permute-start(bf16[128,512]{1,0:T(8,128)(2,1)S(1)} %pad_maximum_fusion.1), channel_id=1, source_target_pairs={{0,2},{1,3},{2,0},{3,1},{4,6},{5,7},{6,4},{7,5},{8,10},{9,11},{10,... | collective-permute-start | bytes 393224 | tf_op jit(solution)/shard_map/ppermute | solution.py:294
  18.9 6.3 %copy-start = (bf16[512,512]{1,0:T(8,128)(2,1)S(1)}, bf16[512,512]{1,0:T(8,128)(2,1)}, u32[]{:S(2)}) copy-start(bf16[512,512]{1,0:T(8,128)(2,1)} %wq.5) | copy-start | bytes 1572868
  18.9 6.3 %copy-start.4 = (s32[32,128]{1,0:T(8,128)S(1)}, s32[32,128]{1,0:T(8,128)}, u32[]{:S(2)}) copy-start(s32[32,128]{1,0:T(8,128)} %merch_slot.5) | copy-start | bytes 49156
  18.9 6.3 %copy-start.8 = (s32[32]{0:T(128)S(1)}, s32[32]{0:T(128)}, u32[]{:S(2)}) copy-start(s32[32]{0:T(128)} %count_ref.5) | copy-start | bytes 388
  18.9 6.3 %copy-start.9 = (f32[4]{0:T(128)S(1)}, f32[4]{0:T(128)}, u32[]{:S(2)}) copy-start(f32[4]{0:T(128)} %bias_ref.5) | copy-start | bytes 52
  25.1 2.2 %collective-permute-start.7 = (bf16[512,512]{1,0:T(8,128)(2,1)S(1)}, bf16[512,512]{1,0:T(8,128)(2,1)S(1)}, u32[]{:S(2)}, u32[]{:S(2)}) collective-permute-start(bf16[512,512]{1,0:T(8,128)(2,1)S(1)} %pad_maximum_fusion.feats), channel_id=1, source_target_pairs={{0,1},{1,0},{2,3},{3,2},{4,5},{5,4},{6,7},{7,6},{8,9},{9,8},{10,11... | collective-permute-start | bytes 1572872 | tf_op jit(solution)/shard_map/ppermute | solution.py:294
  26.8 2.1 %collective-permute-start.8 = (bf16[512,512]{1,0:T(8,128)(2,1)S(1)}, bf16[512,512]{1,0:T(8,128)(2,1)S(1)}, u32[]{:S(2)}, u32[]{:S(2)}) collective-permute-start(bf16[512,512]{1,0:T(8,128)(2,1)S(1)} %aggregate_odd.1), channel_id=1, source_target_pairs={{0,1},{1,0},{2,3},{3,2},{4,5},{5,4},{6,7},{7,6},{8,9},{9,8},{10,11... | collective-permute-start | bytes 1572872 | tf_op jit(solution)/shard_map/ppermute | solution.py:294
  29.0 6.1 %collective-permute-start.11 = (bf16[128,512]{1,0:T(8,128)(2,1)S(1)}, bf16[128,512]{1,0:T(8,128)(2,1)S(1)}, u32[]{:S(2)}, u32[]{:S(2)}) collective-permute-start(bf16[128,512]{1,0:T(8,128)(2,1)S(1)} %get-tuple-element.31), channel_id=1, source_target_pairs={{0,2},{1,3},{2,0},{3,1},{4,6},{5,7},{6,4},{7,5},{8,10},{9,11},{10,... | collective-permute-start | bytes 393224 | tf_op jit(solution)/shard_map/ppermute | solution.py:294
  30.7 8.3 %collective-permute-start.10 = (bf16[128,512]{1,0:T(8,128)(2,1)S(1)}, bf16[128,512]{1,0:T(8,128)(2,1)S(1)}, u32[]{:S(2)}, u32[]{:S(2)}) collective-permute-start(bf16[128,512]{1,0:T(8,128)(2,1)S(1)} %get-tuple-element.32), channel_id=1, source_target_pairs={{0,4},{1,5},{2,6},{3,7},{4,0},{5,1},{6,2},{7,3},{8,12},{9,13},{10,... | collective-permute-start | bytes 393224 | tf_op jit(solution)/shard_map/ppermute | solution.py:294
  32.3 6.8 %collective-permute-start.9 = (bf16[128,512]{1,0:T(8,128)(2,1)S(1)}, bf16[128,512]{1,0:T(8,128)(2,1)S(1)}, u32[]{:S(2)}, u32[]{:S(2)}) collective-permute-start(bf16[128,512]{1,0:T(8,128)(2,1)S(1)} %get-tuple-element.33), channel_id=1, source_target_pairs={{0,6},{1,7},{2,4},{3,5},{4,2},{5,3},{6,0},{7,1},{8,14},{9,15},{10,... | collective-permute-start | bytes 393224 | tf_op jit(solution)/shard_map/ppermute | solution.py:294
  33.9 14.5 %copy-start.3 = (bf16[512,512]{1,0:T(8,128)(2,1)S(1)}, bf16[512,512]{1,0:T(8,128)(2,1)}, u32[]{:S(2)}) copy-start(bf16[512,512]{1,0:T(8,128)(2,1)} %wo.1) | copy-start | bytes 1572868
  33.9 14.5 %copy-start.5 = (bf16[32,512]{1,0:T(8,128)(2,1)S(1)}, bf16[32,512]{1,0:T(8,128)(2,1)}, u32[]{:S(2)}) copy-start(bf16[32,512]{1,0:T(8,128)(2,1)} %feat.1) | copy-start | bytes 98308
  33.9 14.5 %copy-start.10 = (f32[512]{0:T(512)S(1)}, f32[512]{0:T(512)}, u32[]{:S(2)}) copy-start(f32[512]{0:T(512)} %param.19) | copy-start | bytes 6148
  39.1 4.3 %collective-permute-start.12 = (bf16[64,512]{1,0:T(8,128)(2,1)S(1)}, bf16[64,512]{1,0:T(8,128)(2,1)S(1)}, u32[]{:S(2)}, u32[]{:S(2)}) collective-permute-start(bf16[64,512]{1,0:T(8,128)(2,1)S(1)} %get-tuple-element.38), channel_id=1, source_target_pairs={{0,8},{1,9},{2,10},{3,11},{4,12},{5,13},{6,14},{7,15},{8,0},{9,1},... | collective-permute-start | bytes 196616 | tf_op jit(solution)/shard_map/ppermute | solution.py:294
  43.5 4.9 %collective-permute-start.13 = (bf16[32,512]{1,0:T(8,128)(2,1)S(1)}, bf16[32,512]{1,0:T(8,128)(2,1)S(1)}, u32[]{:S(2)}, u32[]{:S(2)}) collective-permute-start(bf16[32,512]{1,0:T(8,128)(2,1)S(1)} %get-tuple-element.40), channel_id=1, source_target_pairs={{0,16},{1,17},{2,18},{3,19},{4,20},{5,21},{6,22},{7,23},{8,24},{9,... | collective-permute-start | bytes 98312 | tf_op jit(solution)/shard_map/ppermute | solution.py:294

commit v14 on v4

v14 whole, which is shorter than its diff:
```python
import functools
import math

import jax
import jax.numpy as jnp
from jax import lax
from jax.experimental import pallas as pl
from jax.experimental.pallas import tpu as pltpu
from jax.sharding import PartitionSpec as P

AXES = ("acct", "merch")
LANES = 128
F32 = jnp.float32
BF16 = jnp.bfloat16
SMEM = pl.BlockSpec(memory_space=pltpu.SMEM)
ANY = pl.BlockSpec(memory_space=pl.ANY)
VMEM = pl.BlockSpec(memory_space=pltpu.VMEM)


def _mb(n):
    return pltpu.CompilerParams(vmem_limit_bytes=n * 2**20)


def _cost(flops, bytes_accessed, transcendentals=0):
    return pl.CostEstimate(
        flops=int(flops), bytes_accessed=int(bytes_accessed), transcendentals=transcendentals
    )


def _offset(i, outer):
    return (i // outer) * 2 + (i % outer) * 8


def project_kernel(
    outer, me_ref, rel_ref, slots_ref, acct_hbm, kw_hbm, mw_hbm,
    odd_keys, odd_values, even_keys, even_values,
    acct, kw, mw, table, odd_rows, even_rows, odd_feats, even_feats, a_sem, w_sem,
):
    accounts, width = acct.shape
    blocks, block_len, _ = odd_values.shape
    parts = width // LANES
    wide = 256
    group = 2 * block_len * wide // (4 * width)
    me = me_ref[0]
    chunks = a_sem.shape[0]
    chunk = accounts // chunks
    copies = [
        pltpu.make_async_copy(
            acct_hbm.at[pl.ds(i * chunk, chunk)], acct.at[pl.ds(i * chunk, chunk)], a_sem.at[i]
        )
        for i in range(chunks)
    ]
    weight_copies = [
        pltpu.make_async_copy(kw_hbm, kw, w_sem.at[0]),
        pltpu.make_async_copy(mw_hbm, mw, w_sem.at[1]),
    ]
    for copy in copies + weight_copies:
        copy.start()
    for i in range(chunks):
        copies[i].wait()

        @pl.loop(0, chunk // 16, unroll=4)
        def _(g):
            first = pl.multiple_of(i * chunk + g * 16, 16)
            tile = acct[pl.ds(first, 16), :].astype(F32)
            for c in range(parts):
                table[pl.ds(first * parts + c, 16, stride=parts), :] = tile[
                    :, c * LANES : (c + 1) * LANES
                ]

    def collect(block, rows, first, last):
        start = block * block_len
        found = []
        for k in range(first, last):
            source = pl.multiple_of(slots_ref[start + k] * parts, parts)
            found.append(table[pl.ds(source, parts), :])
        for k in range(first, last):
            rows[k * parts : (k + 1) * parts, :] = found[k - first]

    def emit(rows, out):
        for c in range(parts):
            out[:, c * LANES : (c + 1) * LANES] = rows[
                pl.ds(c, block_len, stride=parts), :
            ].astype(BF16)

    collect(jnp.bitwise_xor(me, 1), odd_rows, 0, block_len)
    collect(me, even_rows, 0, block_len)
    for copy in weight_copies:
        copy.wait()

    @pl.loop(0, blocks)
    def _(i):
        emit(odd_rows, odd_feats)
        emit(even_rows, even_feats)
        offset = _offset(i, outer)
        ahead = _offset(jnp.minimum(i + 1, blocks - 1), outer)
        step = 0
        for shift, feats, rows, keys, values in (
            (1, odd_feats, odd_rows, odd_keys, odd_values),
            (0, even_feats, even_rows, even_keys, even_values),
        ):
            relation = rel_ref[jnp.bitwise_xor(me, offset + shift)]
            nearby = jnp.bitwise_xor(me, ahead + shift)
            step = 0
            for weight, transposed, out in ((kw, True, keys), (mw, False, values)):
                for n in range(0, width, wide):
                    result = jnp.dot(
                        feats[...], weight[relation, :, n : n + wide], preferred_element_type=F32
                    ).astype(BF16)
                    collect(nearby, rows, step * group, (step + 1) * group)
                    step += 1
                    if transposed:
                        out[i, n : n + wide, :] = result.T
                    else:
                        out[i, :, n : n + wide] = result


def project(outer, me, rel, slots, acct, kw, mw):
    blocks, block_len = slots.shape
    accounts, width = acct.shape
    parts = width // LANES
    rows = pltpu.VMEM((block_len * parts, LANES), F32)
    feats = pltpu.VMEM((block_len, width), BF16)
    keys = jax.ShapeDtypeStruct((blocks // 2, width, block_len), BF16)
    values = jax.ShapeDtypeStruct((blocks // 2, block_len, width), BF16)
    return pl.pallas_call(
        functools.partial(project_kernel, outer),
        out_shape=(keys, values, keys, values),
        in_specs=[SMEM] * 3 + [ANY] * 3,
        out_specs=(VMEM,) * 4,
        scratch_shapes=[
            pltpu.VMEM(acct.shape, BF16),
            pltpu.VMEM(kw.shape, BF16),
            pltpu.VMEM(mw.shape, BF16),
            pltpu.VMEM((accounts * parts, LANES), F32),
            rows,
            rows,
            feats,
            feats,
            pltpu.SemaphoreType.DMA((8,)),
            pltpu.SemaphoreType.DMA((2,)),
        ],
        compiler_params=_mb(44 if blocks <= 32 else 50),
        cost_estimate=_cost(4 * blocks * block_len * width * width, 40 * 2**20),
        name="project_slots",
    )(me, rel, slots.reshape(-1), acct, kw, mw)


def assemble_kernel(*refs):
    rows = refs[0].shape[0]
    for i, part in enumerate(refs[:-1]):
        refs[-1][i * rows : (i + 1) * rows, :] = part[...]


def assemble(parts):
    rows, width = parts[0].shape
    return pl.pallas_call(
        assemble_kernel,
        out_shape=jax.ShapeDtypeStruct((len(parts) * rows, width), parts[0].dtype),
        in_specs=[VMEM] * len(parts),
        out_specs=VMEM,
        compiler_params=_mb(2),
        cost_estimate=_cost(1, 1),
        name="assemble",
    )(*parts)


def aggregate_kernel(
    outer, first, shift, me_ref, rel_ref, count_ref, bias_ref, merch_slot, feats, wq, keys, values,
    sums, query, gates,
):
    blocks, width, block_len = keys.shape
    merchants = sums.shape[0] // blocks
    me = me_ref[0]
    row = lax.broadcasted_iota(jnp.int32, (merchants, block_len), 0)
    lane = lax.broadcasted_iota(jnp.int32, (merchants, block_len), 1)
    query[...] = jnp.dot(
        feats[first * merchants : (first + blocks) * merchants, :],
        wq[...],
        preferred_element_type=F32,
    ).astype(BF16)
    parts = [slice(i * merchants, (i + 1) * merchants) for i in range(blocks)]
    for i in range(blocks):
        block = jnp.bitwise_xor(me, _offset(first + i, outer) + shift)
        score = jnp.dot(query[parts[i], :], keys[i], preferred_element_type=F32) / math.sqrt(width)
        score = score + bias_ref[rel_ref[block]]
        mine = (merch_slot[pl.ds(block, 1), :] == row) & (lane < count_ref[block])
        gates[parts[i], :] = jnp.where(mine, jax.nn.sigmoid(score), 0.0).astype(BF16)
    for i in range(blocks):
        sums[parts[i], :] = jnp.dot(
            gates[parts[i], :], values[i], preferred_element_type=F32
        ).astype(sums.dtype)


def aggregate(outer, first, shift, me, rel, count, bias, merch_slot, feats, wq, keys, values, dtype):
    blocks, width, block_len = keys.shape
    rows = feats.shape[0] * blocks // (merch_slot.shape[0] // 2)
    return pl.pallas_call(
        functools.partial(aggregate_kernel, outer, first, shift),
        out_shape=jax.ShapeDtypeStruct((rows, width), dtype),
        in_specs=[SMEM] * 4 + [VMEM] * 5,
        out_specs=VMEM,
        scratch_shapes=[
            pltpu.VMEM((rows, width), BF16),
            pltpu.VMEM((rows, block_len), BF16),
        ],
        compiler_params=_mb(6),
        cost_estimate=_cost(
            4 * rows * block_len * width + 2 * rows * width * width, 6 * 2**20, rows * block_len
        ),
        name="aggregate_odd" if shift else "aggregate_even",
    )(me, rel, count, bias, merch_slot, feats, wq, keys, values)


def combine_kernel(skip, mine, other, *outs):
    rows = outs[0].shape[0]
    for j, out in enumerate(outs):
        part = slice(j * rows, (j + 1) * rows)
        theirs = slice(skip + j * rows, skip + (j + 1) * rows)
        out[...] = (mine[part, :] + other[theirs, :].astype(F32)).astype(out.dtype)


def combine(groups, skip, mine, other):
    rows, width = mine.shape
    return pl.pallas_call(
        functools.partial(combine_kernel, skip),
        out_shape=tuple(
            jax.ShapeDtypeStruct((rows // groups, width), BF16 if j else F32)
            for j in range(groups)
        ),
        in_specs=[VMEM, VMEM],
        out_specs=(VMEM,) * groups,
        compiler_params=_mb(2),
        cost_estimate=_cost(0, 2 * 2**20),
        name="combine_cores",
    )(mine, other)


def plane_kernel(inner, *refs):
    ins, outs = refs[:inner], refs[inner:]
    rows = outs[0].shape[0]
    for k, out in enumerate(outs):
        part = slice(k * rows, (k + 1) * rows)
        total = ins[0][part, :]
        for other in ins[1:]:
            total = total + other[part, :].astype(F32)
        out[...] = total.astype(out.dtype)


def combine_plane(outer, parts):
    rows, width = parts[0].shape
    return pl.pallas_call(
        functools.partial(plane_kernel, len(parts)),
        out_shape=tuple(
            jax.ShapeDtypeStruct((rows // outer, width), F32 if k == 0 else BF16)
            for k in range(outer)
        ),
        in_specs=[VMEM] * len(parts),
        out_specs=(VMEM,) * outer,
        compiler_params=_mb(2),
        cost_estimate=_cost(0, 2**20),
        name="combine_plane",
    )(*parts)


def finish_kernel(feat, gain, wo, *refs):
    out = refs[-1]
    total = refs[0][...]
    for part in refs[1:-1]:
        total = total + part[...].astype(F32)
    update = feat[...].astype(F32) + jnp.dot(
        total.astype(BF16), wo[...], preferred_element_type=F32
    )
    scale = lax.rsqrt(jnp.mean(update * update, axis=-1, keepdims=True) + 1e-06)
    out[...] = (update * scale * gain[...]).astype(BF16)


def finish(feat, gain, wo, parts):
    return pl.pallas_call(
        finish_kernel,
        out_shape=jax.ShapeDtypeStruct(feat.shape, BF16),
        in_specs=[VMEM] * (3 + len(parts)),
        out_specs=VMEM,
        compiler_params=_mb(2),
        name="finish",
    )(feat, gain.reshape(1, -1), wo, *parts)


def per_device(
    acct_feat,
    merch_feat,
    key_weight,
    msg_weight,
    query_weight,
    out_weight,
    rel_bias,
    out_gain,
    slot_acct,
    slot_merch,
    block_rel,
    block_count,
):
    devices = lax.axis_size(AXES)
    me = lax.axis_index(AXES).astype(jnp.int32).reshape(1)
    inner = 4
    outer = devices // (2 * inner)

    def swap(value, mask):
        return lax.ppermute(value, AXES, [(s, s ^ mask) for s in range(devices)])

    def after(value, *others):
        return lax.optimization_barrier((value,) + others)[0]

    feats = jnp.concatenate([swap(merch_feat, 8 * k + 1) for k in range(outer)], axis=0)
    here = after(me, feats)
    feats = [feats] + [swap(feats, 2 * j) for j in range(1, inner)]
    odd_keys, odd_values, even_keys, even_values = project(
        outer, here, block_rel, slot_acct, acct_feat, key_weight, msg_weight
    )
    feats = assemble(after(tuple(feats), odd_keys))
    even_feats = swap(feats, 1)

    rest = (block_rel, block_count, rel_bias, slot_merch)
    odd = aggregate(outer, 0, 1, me, *rest, feats, query_weight, odd_keys, odd_values, BF16)
    other = swap(odd, 1)
    even = aggregate(
        outer, 0, 0, me, *rest, even_feats, query_weight, even_keys, even_values, F32
    )
    parts = combine(inner, 0, even, other)
    parts = combine_plane(
        outer, [parts[0]] + [swap(parts[j], 2 * j) for j in reversed(range(1, inner))]
    )
    parts = [parts[0]] + [swap(parts[k], 8 * k) for k in reversed(range(1, outer))]
    return finish(merch_feat, out_gain, out_weight, parts)


def solution(mesh):
    placed = (
        P(("acct", "merch"), None),
        P(("acct", "merch"), None),
        P(),
        P(),
        P(),
        P(),
        P(),
        P(),
        P(("acct", "merch"), None),
        P(("acct", "merch"), None),
        P(("acct", "merch")),
        P(("acct", "merch")),
    )
    return jax.shard_map(
        per_device,
        mesh=mesh,
        in_specs=placed,
        out_specs=P(("acct", "merch"), None),
        check_vma=False,
    )
```

time: 52.9 us -> 50.8 us (0.960)
  Pallas kernels: 21.1 us -> 18 us
  waiting for transfers between devices: 12.3 us -> 13.5 us
    pallas_call x5, Pallas kernels: 20.1 us -> 17 us  [the longest x1 13.8 us: project(): pl.pallas_call(functools.partial(project_kernel, outer), out_shape=(keys,...]
    ppermute x15, waiting for transfers between devices: 12.3 us -> 13.5 us  [swap(): return lax.ppermute(value, AXES, [(s, s ^ mask) for s in range(devices)])]
    unnamed x22 -> x21, local copies, waits for them, and re-layouts: 1.42 us -> 1.41 us
  transfers between devices with their start and end apart: 15 -> 15, of which waited for: 6 -> 7; matrix products, arithmetic and copies ran while one was open for 0% -> 0% of each run, Pallas kernels for 38% -> 33%
where the time goes in v14:
time: 50.8 us; the launch traced here: 50.5 us
  Pallas kernels  18 us (35%)
  starting transfers between devices  17.4 us (34%)
  waiting for transfers between devices  13.5 us (27%)
  local copies, waits for them, and re-layouts  1.42 us (3%)
    ppermute x15, starting transfers between devices, swap(): return lax.ppermute(value, AXES, [(s, s ^ mask) for s in range(devices)])  17.4 us
    pallas_call x1, Pallas kernels, project(): pl.pallas_call(functools.partial(project_kernel, outer), out_shape=(keys,...  13.8 us
    ppermute x15, waiting for transfers between devices, swap(): return lax.ppermute(value, AXES, [(s, s ^ mask) for s in range(devices)])  13.5 us
    pallas_call x2, Pallas kernels, aggregate(): pl.pallas_call(functools.partial(aggregate_kernel, outer, first, shift),...  3.07 us
    unnamed x21, local copies, waits for them, and re-layouts  1.41 us
  transfers between devices with their start and end apart: 15, of which 7 were waited for; matrix products, arithmetic and copies ran while one was open for 0% of the time, Pallas kernels for 33%

profile of v14, /device:TPU:0, one launch (start us, length us, event | category | flops | bytes accessed | tf_op | source)
XLA Modules:
  0.0 50.5 jit_solution(15181723359847720215)
XLA Ops:
  0.0 0.5 collective-permute-start
  0.5 3.7 %collective-permute-start.2 = (bf16[32,512]{1,0:T(8,128)(2,1)}, bf16[32,512]{1,0:T(8,128)(2,1)S(1)}, u32[]{:S(2)}, u32[]{:S(2)}) collective-permute-start(bf16[32,512]{1,0:T(8,128)(2,1)} %feat.1), channel_id=1, source_target_pairs={{0,17},{1,16},{2,19},{3,18},{4,21},{5,20},{6,23},{7,22},{8,25},{9,... | collective-permute-start | bytes 98312 | tf_op jit(solution)/shard_map/ppermute | solution.py:309
  4.2 1.2 %collective-permute-start.1 = (bf16[32,512]{1,0:T(8,128)(2,1)}, bf16[32,512]{1,0:T(8,128)(2,1)S(1)}, u32[]{:S(2)}, u32[]{:S(2)}) collective-permute-start(bf16[32,512]{1,0:T(8,128)(2,1)} %feat.1), channel_id=1, source_target_pairs={{0,9},{1,8},{2,11},{3,10},{4,13},{5,12},{6,15},{7,14},{8,1},{9,0},... | collective-permute-start | bytes 98312 | tf_op jit(solution)/shard_map/ppermute | solution.py:309
  5.3 2.5 %collective-permute-done.1 = bf16[32,512]{1,0:T(8,128)(2,1)S(1)} collective-permute-done((bf16[32,512]{1,0:T(8,128)(2,1)}, bf16[32,512]{1,0:T(8,128)(2,1)S(1)}, u32[]{:S(2)}, u32[]{:S(2)}) %collective-permute-start.1) | collective-permute-done | bytes 32800 | tf_op jit(solution)/shard_map/ppermute | solution.py:309
  7.9 2.8 %collective-permute-done.3 = bf16[32,512]{1,0:T(8,128)(2,1)S(1)} collective-permute-done((bf16[32,512]{1,0:T(8,128)(2,1)}, bf16[32,512]{1,0:T(8,128)(2,1)S(1)}, u32[]{:S(2)}, u32[]{:S(2)}) %collective-permute-start.3) | collective-permute-done | bytes 32800 | tf_op jit(solution)/shard_map/ppermute | solution.py:309
  10.7 2.4 %collective-permute-start.6 = (bf16[128,512]{1,0:T(8,128)(2,1)S(1)}, bf16[128,512]{1,0:T(8,128)(2,1)S(1)}, u32[]{:S(2)}, u32[]{:S(2)}) collective-permute-start(bf16[128,512]{1,0:T(8,128)(2,1)S(1)} %constant_dynamic-update-slice_fusion.refs_0_), channel_id=1, source_target_pairs={{0,6},{1,7},{2,4},{3,5},{4,2},{5,3},{6,0},{7,1},{8,14},{9,15},{10,... | collective-permute-start | bytes 393224 | tf_op jit(solution)/shard_map/ppermute | solution.py:309
  13.1 0.5 %collective-permute-start.5 = (bf16[128,512]{1,0:T(8,128)(2,1)S(1)}, bf16[128,512]{1,0:T(8,128)(2,1)S(1)}, u32[]{:S(2)}, u32[]{:S(2)}) collective-permute-start(bf16[128,512]{1,0:T(8,128)(2,1)S(1)} %constant_dynamic-update-slice_fusion.refs_0_), channel_id=1, source_target_pairs={{0,4},{1,5},{2,6},{3,7},{4,0},{5,1},{6,2},{7,3},{8,12},{9,13},{10,... | collective-permute-start | bytes 393224 | tf_op jit(solution)/shard_map/ppermute | solution.py:309
  13.6 0.5 %collective-permute-start.4 = (bf16[128,512]{1,0:T(8,128)(2,1)S(1)}, bf16[128,512]{1,0:T(8,128)(2,1)S(1)}, u32[]{:S(2)}, u32[]{:S(2)}) collective-permute-start(bf16[128,512]{1,0:T(8,128)(2,1)S(1)} %constant_dynamic-update-slice_fusion.refs_0_), channel_id=1, source_target_pairs={{0,2},{1,3},{2,0},{3,1},{4,6},{5,7},{6,4},{7,5},{8,10},{9,11},{10,... | collective-permute-start | bytes 393224 | tf_op jit(solution)/shard_map/ppermute | solution.py:309
  14.2 0.7 %copy-done.5 = s32[32]{0:T(128)S(1)} copy-done((s32[32]{0:T(128)S(1)}, s32[32]{0:T(128)}, u32[]{:S(2)}) %copy-start.5) | copy-done | bytes 152
  14.8 0.7 %copy-done.8 = s32[32,128]{1,0:T(8,128)S(1)} copy-done((s32[32,128]{1,0:T(8,128)S(1)}, s32[32,128]{1,0:T(8,128)}, u32[]{:S(2)}) %copy-start.8) | copy-done | bytes 16408
  15.6 13.8 %project_slots.1 = (bf16[16,512,128]{2,1,0:T(8,128)(2,1)S(1)}, bf16[16,128,512]{2,1,0:T(8,128)(2,1)S(1)}, bf16[16,512,128]{2,1,0:T(8,128)(2,1)S(1)}, bf16[16,128,512]{2,1,0:T(8,128)(2,1)S(1)}) custom-call(s32[1]{0:T(128)} %bitcast.1.me_ref, s32[32]{0:T(128)S(1)} %copy-done.5, s32[4096]{0:T(1024)S(1)} %bitcast.4, bf16[4096,512]{1,0:T(8,128)(2,1)} %acct_hbm.1, ...), custom_call_target="tpu_custom_call" | custom-call | flops 4294967296 | bytes 41943040 | tf_op jit(solution)/shard_map/project_slots/pallas_call | solution.py:126
  29.4 0.1 collective-permute-start.7
  29.5 1.5 %aggregate_odd.1 = bf16[512,512]{1,0:T(8,128)(2,1)S(1)} custom-call(s32[1]{0:T(128)} %bitcast.1.me_ref, s32[32]{0:T(128)S(1)} %copy-done.5, s32[32]{0:T(128)S(1)} %copy-done.6, f32[4]{0:T(128)S(1)} %copy-done.7, s32[32,128]{1,0:T(8,128)S(1)} %copy-done.2, bf16[512,512]{1,0:T(8,128)(2,1)S(1)} %assemble.1.feats, bf16[512,512]{1,0:T(8,128)(2,1)S(1)} %copy-done, ...), custom_call_target="tpu_custom_call" | custom-call | flops 402653184 | bytes 6291456 | tf_op jit(solution)/shard_map/aggregate_odd/pallas_call | solution.py:198
  31.1 0.5 %collective-permute-start.8 = (bf16[512,512]{1,0:T(8,128)(2,1)S(1)}, bf16[512,512]{1,0:T(8,128)(2,1)S(1)}, u32[]{:S(2)}, u32[]{:S(2)}) collective-permute-start(bf16[512,512]{1,0:T(8,128)(2,1)S(1)} %aggregate_odd.1), channel_id=1, source_target_pairs={{0,1},{1,0},{2,3},{3,2},{4,5},{5,4},{6,7},{7,6},{8,9},{9,8},{10,11... | collective-permute-start | bytes 1572872 | tf_op jit(solution)/shard_map/ppermute | solution.py:309
  31.6 1.5 %aggregate_even.1.mine = f32[512,512]{1,0:T(8,128)S(1)} custom-call(s32[1]{0:T(128)} %bitcast.1.me_ref, s32[32]{0:T(128)S(1)} %copy-done.5, s32[32]{0:T(128)S(1)} %copy-done.6, f32[4]{0:T(128)S(1)} %copy-done.7, s32[32,128]{1,0:T(8,128)S(1)} %copy-done.2, bf16[512,512]{1,0:T(8,128)(2,1)S(1)} %collective-permute-done.7.feats, bf16[512,512]{1,0:T(8,128)(2,1)S(1)} %copy-done, ...), custom_call_target="tpu_custom_call" | custom-call | flops 402653184 | bytes 6291456 | tf_op jit(solution)/shard_map/aggregate_even/pallas_call | solution.py:198
  33.1 0.0 copy-start.1
  33.2 0.0 copy-start.3
  33.2 0.0 copy-start.4
  33.2 0.1 combine_cores.1
  33.3 2.5 %collective-permute-start.9 = (bf16[128,512]{1,0:T(8,128)(2,1)S(1)}, bf16[128,512]{1,0:T(8,128)(2,1)S(1)}, u32[]{:S(2)}, u32[]{:S(2)}) collective-permute-start(bf16[128,512]{1,0:T(8,128)(2,1)S(1)} %get-tuple-element.32), channel_id=1, source_target_pairs={{0,6},{1,7},{2,4},{3,5},{4,2},{5,3},{6,0},{7,1},{8,14},{9,15},{10,... | collective-permute-start | bytes 393224 | tf_op jit(solution)/shard_map/ppermute | solution.py:309
  35.8 0.5 collective-permute-start.10
  36.3 0.5 %collective-permute-start.11 = (bf16[128,512]{1,0:T(8,128)(2,1)S(1)}, bf16[128,512]{1,0:T(8,128)(2,1)S(1)}, u32[]{:S(2)}, u32[]{:S(2)}) collective-permute-start(bf16[128,512]{1,0:T(8,128)(2,1)S(1)} %get-tuple-element.34), channel_id=1, source_target_pairs={{0,2},{1,3},{2,0},{3,1},{4,6},{5,7},{6,4},{7,5},{8,10},{9,11},{10,... | collective-permute-start | bytes 393224 | tf_op jit(solution)/shard_map/ppermute | solution.py:309
  36.9 3.4 %collective-permute-done.9.refs_1_ = bf16[128,512]{1,0:T(8,128)(2,1)S(1)} collective-permute-done((bf16[128,512]{1,0:T(8,128)(2,1)S(1)}, bf16[128,512]{1,0:T(8,128)(2,1)S(1)}, u32[]{:S(2)}, u32[]{:S(2)}) %collective-permute-start.9) | collective-permute-done | bytes 131104 | tf_op jit(solution)/shard_map/ppermute | solution.py:309
  40.3 2.5 %collective-permute-done.10.refs_2_ = bf16[128,512]{1,0:T(8,128)(2,1)S(1)} collective-permute-done((bf16[128,512]{1,0:T(8,128)(2,1)S(1)}, bf16[128,512]{1,0:T(8,128)(2,1)S(1)}, u32[]{:S(2)}, u32[]{:S(2)}) %collective-permute-start.10) | collective-permute-done | bytes 131104 | tf_op jit(solution)/shard_map/ppermute | solution.py:309
  42.8 0.1 collective-permute-done.11.refs_3_
  42.9 0.1 combine_plane.1
  43.0 1.3 %collective-permute-start.12 = (bf16[32,512]{1,0:T(8,128)(2,1)S(1)}, bf16[32,512]{1,0:T(8,128)(2,1)S(1)}, u32[]{:S(2)}, u32[]{:S(2)}) collective-permute-start(bf16[32,512]{1,0:T(8,128)(2,1)S(1)} %get-tuple-element.36), channel_id=1, source_target_pairs={{0,24},{1,25},{2,26},{3,27},{4,28},{5,29},{6,30},{7,31},{8,16},{9,... | collective-permute-start | bytes 98312 | tf_op jit(solution)/shard_map/ppermute | solution.py:309
  44.3 3.1 %collective-permute-start.14 = (bf16[32,512]{1,0:T(8,128)(2,1)S(1)}, bf16[32,512]{1,0:T(8,128)(2,1)S(1)}, u32[]{:S(2)}, u32[]{:S(2)}) collective-permute-start(bf16[32,512]{1,0:T(8,128)(2,1)S(1)} %get-tuple-element.38), channel_id=1, source_target_pairs={{0,8},{1,9},{2,10},{3,11},{4,12},{5,13},{6,14},{7,15},{8,0},{9,1},... | collective-permute-start | bytes 98312 | tf_op jit(solution)/shard_map/ppermute | solution.py:309
  47.4 1.5 %collective-permute-done.12.refs_1_ = bf16[32,512]{1,0:T(8,128)(2,1)S(1)} collective-permute-done((bf16[32,512]{1,0:T(8,128)(2,1)S(1)}, bf16[32,512]{1,0:T(8,128)(2,1)S(1)}, u32[]{:S(2)}, u32[]{:S(2)}) %collective-permute-start.12) | collective-permute-done | bytes 32800 | tf_op jit(solution)/shard_map/ppermute | solution.py:309
  48.9 0.7 %collective-permute-done.13.refs_2_ = bf16[32,512]{1,0:T(8,128)(2,1)S(1)} collective-permute-done((bf16[32,512]{1,0:T(8,128)(2,1)S(1)}, bf16[32,512]{1,0:T(8,128)(2,1)S(1)}, u32[]{:S(2)}, u32[]{:S(2)}) %collective-permute-start.13) | collective-permute-done | bytes 32800 | tf_op jit(solution)/shard_map/ppermute | solution.py:309
  49.6 0.0 collective-permute-done.14.refs_3_
  49.6 0.9 %finish.1 = bf16[32,512]{1,0:T(8,128)(2,1)} custom-call(bf16[32,512]{1,0:T(8,128)(2,1)S(1)} %copy-done.3, f32[1,512]{1,0:T(1,128)S(1)} %bitcast.3, bf16[512,512]{1,0:T(8,128)(2,1)S(1)} %copy-done.1, f32[32,512]{1,0:T(8,128)S(1)} %get-tuple-element.35.refs_0_, bf16[32,512]{1,0:T(8,128)(2,1)S(1)} %collective-permute-done.12.refs_1_, ...), custom_call_target="tpu_custom_call" | custom-call | tf_op jit(solution)/shard_map/finish/pallas_call | solution.py:279
  (27 shorter events, 0.1 us)
Async XLA Ops:
  0.0 5.3 %collective-permute-start = (bf16[32,512]{1,0:T(8,128)(2,1)}, bf16[32,512]{1,0:T(8,128)(2,1)S(1)}, u32[]{:S(2)}, u32[]{:S(2)}) collective-permute-start(bf16[32,512]{1,0:T(8,128)(2,1)} %feat.1), channel_id=1, source_target_pairs={{0,1},{1,0},{2,3},{3,2},{4,5},{5,4},{6,7},{7,6},{8,9},{9,8},{10,11... | collective-permute-start | bytes 98312 | tf_op jit(solution)/shard_map/ppermute | solution.py:309
  0.5 7.4 %collective-permute-start.2 = (bf16[32,512]{1,0:T(8,128)(2,1)}, bf16[32,512]{1,0:T(8,128)(2,1)S(1)}, u32[]{:S(2)}, u32[]{:S(2)}) collective-permute-start(bf16[32,512]{1,0:T(8,128)(2,1)} %feat.1), channel_id=1, source_target_pairs={{0,17},{1,16},{2,19},{3,18},{4,21},{5,20},{6,23},{7,22},{8,25},{9,... | collective-permute-start | bytes 98312 | tf_op jit(solution)/shard_map/ppermute | solution.py:309
  4.2 3.7 %collective-permute-start.1 = (bf16[32,512]{1,0:T(8,128)(2,1)}, bf16[32,512]{1,0:T(8,128)(2,1)S(1)}, u32[]{:S(2)}, u32[]{:S(2)}) collective-permute-start(bf16[32,512]{1,0:T(8,128)(2,1)} %feat.1), channel_id=1, source_target_pairs={{0,9},{1,8},{2,11},{3,10},{4,13},{5,12},{6,15},{7,14},{8,1},{9,0},... | collective-permute-start | bytes 98312 | tf_op jit(solution)/shard_map/ppermute | solution.py:309
  5.3 5.3 %collective-permute-start.3 = (bf16[32,512]{1,0:T(8,128)(2,1)}, bf16[32,512]{1,0:T(8,128)(2,1)S(1)}, u32[]{:S(2)}, u32[]{:S(2)}) collective-permute-start(bf16[32,512]{1,0:T(8,128)(2,1)} %feat.1), channel_id=1, source_target_pairs={{0,25},{1,24},{2,27},{3,26},{4,29},{5,28},{6,31},{7,30},{8,17},{9,... | collective-permute-start | bytes 98312 | tf_op jit(solution)/shard_map/ppermute | solution.py:309
  10.7 18.6 %collective-permute-start.6 = (bf16[128,512]{1,0:T(8,128)(2,1)S(1)}, bf16[128,512]{1,0:T(8,128)(2,1)S(1)}, u32[]{:S(2)}, u32[]{:S(2)}) collective-permute-start(bf16[128,512]{1,0:T(8,128)(2,1)S(1)} %constant_dynamic-update-slice_fusion.refs_0_), channel_id=1, source_target_pairs={{0,6},{1,7},{2,4},{3,5},{4,2},{5,3},{6,0},{7,1},{8,14},{9,15},{10,... | collective-permute-start | bytes 393224 | tf_op jit(solution)/shard_map/ppermute | solution.py:309
  13.1 16.2 %collective-permute-start.5 = (bf16[128,512]{1,0:T(8,128)(2,1)S(1)}, bf16[128,512]{1,0:T(8,128)(2,1)S(1)}, u32[]{:S(2)}, u32[]{:S(2)}) collective-permute-start(bf16[128,512]{1,0:T(8,128)(2,1)S(1)} %constant_dynamic-update-slice_fusion.refs_0_), channel_id=1, source_target_pairs={{0,4},{1,5},{2,6},{3,7},{4,0},{5,1},{6,2},{7,3},{8,12},{9,13},{10,... | collective-permute-start | bytes 393224 | tf_op jit(solution)/shard_map/ppermute | solution.py:309
  13.6 15.7 %collective-permute-start.4 = (bf16[128,512]{1,0:T(8,128)(2,1)S(1)}, bf16[128,512]{1,0:T(8,128)(2,1)S(1)}, u32[]{:S(2)}, u32[]{:S(2)}) collective-permute-start(bf16[128,512]{1,0:T(8,128)(2,1)S(1)} %constant_dynamic-update-slice_fusion.refs_0_), channel_id=1, source_target_pairs={{0,2},{1,3},{2,0},{3,1},{4,6},{5,7},{6,4},{7,5},{8,10},{9,11},{10,... | collective-permute-start | bytes 393224 | tf_op jit(solution)/shard_map/ppermute | solution.py:309
  14.2 0.7 %copy-start.5 = (s32[32]{0:T(128)S(1)}, s32[32]{0:T(128)}, u32[]{:S(2)}) copy-start(s32[32]{0:T(128)} %rel_ref.5) | copy-start | bytes 388
  14.8 0.7 %copy-start.8 = (s32[32,128]{1,0:T(8,128)S(1)}, s32[32,128]{1,0:T(8,128)}, u32[]{:S(2)}) copy-start(s32[32,128]{1,0:T(8,128)} %param.20) | copy-start | bytes 49156
  15.6 13.9 %copy-start = (bf16[512,512]{1,0:T(8,128)(2,1)S(1)}, bf16[512,512]{1,0:T(8,128)(2,1)}, u32[]{:S(2)}) copy-start(bf16[512,512]{1,0:T(8,128)(2,1)} %wq.3) | copy-start | bytes 1572868
  15.6 13.9 %copy-start.2 = (s32[32,128]{1,0:T(8,128)S(1)}, s32[32,128]{1,0:T(8,128)}, u32[]{:S(2)}) copy-start(s32[32,128]{1,0:T(8,128)} %merch_slot.3) | copy-start | bytes 49156
  15.6 14.0 %copy-start.6 = (s32[32]{0:T(128)S(1)}, s32[32]{0:T(128)}, u32[]{:S(2)}) copy-start(s32[32]{0:T(128)} %count_ref.3) | copy-start | bytes 388
  15.6 14.0 %copy-start.7 = (f32[4]{0:T(128)S(1)}, f32[4]{0:T(128)}, u32[]{:S(2)}) copy-start(f32[4]{0:T(128)} %bias_ref.3) | copy-start | bytes 52
  29.4 2.2 %collective-permute-start.7 = (bf16[512,512]{1,0:T(8,128)(2,1)S(1)}, bf16[512,512]{1,0:T(8,128)(2,1)S(1)}, u32[]{:S(2)}, u32[]{:S(2)}) collective-permute-start(bf16[512,512]{1,0:T(8,128)(2,1)S(1)} %assemble.1.feats), channel_id=1, source_target_pairs={{0,1},{1,0},{2,3},{3,2},{4,5},{5,4},{6,7},{7,6},{8,9},{9,8},{10,11... | collective-permute-start | bytes 1572872 | tf_op jit(solution)/shard_map/ppermute | solution.py:309
  31.1 2.1 %collective-permute-start.8 = (bf16[512,512]{1,0:T(8,128)(2,1)S(1)}, bf16[512,512]{1,0:T(8,128)(2,1)S(1)}, u32[]{:S(2)}, u32[]{:S(2)}) collective-permute-start(bf16[512,512]{1,0:T(8,128)(2,1)S(1)} %aggregate_odd.1), channel_id=1, source_target_pairs={{0,1},{1,0},{2,3},{3,2},{4,5},{5,4},{6,7},{7,6},{8,9},{9,8},{10,11... | collective-permute-start | bytes 1572872 | tf_op jit(solution)/shard_map/ppermute | solution.py:309
  33.1 16.5 %copy-start.1 = (bf16[512,512]{1,0:T(8,128)(2,1)S(1)}, bf16[512,512]{1,0:T(8,128)(2,1)}, u32[]{:S(2)}) copy-start(bf16[512,512]{1,0:T(8,128)(2,1)} %wo.1) | copy-start | bytes 1572868
  33.2 16.4 %copy-start.3 = (bf16[32,512]{1,0:T(8,128)(2,1)S(1)}, bf16[32,512]{1,0:T(8,128)(2,1)}, u32[]{:S(2)}) copy-start(bf16[32,512]{1,0:T(8,128)(2,1)} %feat.1) | copy-start | bytes 98308
  33.2 16.4 %copy-start.4 = (f32[512]{0:T(512)S(1)}, f32[512]{0:T(512)}, u32[]{:S(2)}) copy-start(f32[512]{0:T(512)} %param.19) | copy-start | bytes 6148
  33.3 7.0 %collective-permute-start.9 = (bf16[128,512]{1,0:T(8,128)(2,1)S(1)}, bf16[128,512]{1,0:T(8,128)(2,1)S(1)}, u32[]{:S(2)}, u32[]{:S(2)}) collective-permute-start(bf16[128,512]{1,0:T(8,128)(2,1)S(1)} %get-tuple-element.32), channel_id=1, source_target_pairs={{0,6},{1,7},{2,4},{3,5},{4,2},{5,3},{6,0},{7,1},{8,14},{9,15},{10,... | collective-permute-start | bytes 393224 | tf_op jit(solution)/shard_map/ppermute | solution.py:309
  35.8 7.0 %collective-permute-start.10 = (bf16[128,512]{1,0:T(8,128)(2,1)S(1)}, bf16[128,512]{1,0:T(8,128)(2,1)S(1)}, u32[]{:S(2)}, u32[]{:S(2)}) collective-permute-start(bf16[128,512]{1,0:T(8,128)(2,1)S(1)} %get-tuple-element.33), channel_id=1, source_target_pairs={{0,4},{1,5},{2,6},{3,7},{4,0},{5,1},{6,2},{7,3},{8,12},{9,13},{10,... | collective-permute-start | bytes 393224 | tf_op jit(solution)/shard_map/ppermute | solution.py:309
  36.3 6.6 %collective-permute-start.11 = (bf16[128,512]{1,0:T(8,128)(2,1)S(1)}, bf16[128,512]{1,0:T(8,128)(2,1)S(1)}, u32[]{:S(2)}, u32[]{:S(2)}) collective-permute-start(bf16[128,512]{1,0:T(8,128)(2,1)S(1)} %get-tuple-element.34), channel_id=1, source_target_pairs={{0,2},{1,3},{2,0},{3,1},{4,6},{5,7},{6,4},{7,5},{8,10},{9,11},{10,... | collective-permute-start | bytes 393224 | tf_op jit(solution)/shard_map/ppermute | solution.py:309
  43.0 5.9 %collective-permute-start.12 = (bf16[32,512]{1,0:T(8,128)(2,1)S(1)}, bf16[32,512]{1,0:T(8,128)(2,1)S(1)}, u32[]{:S(2)}, u32[]{:S(2)}) collective-permute-start(bf16[32,512]{1,0:T(8,128)(2,1)S(1)} %get-tuple-element.36), channel_id=1, source_target_pairs={{0,24},{1,25},{2,26},{3,27},{4,28},{5,29},{6,30},{7,31},{8,16},{9,... | collective-permute-start | bytes 98312 | tf_op jit(solution)/shard_map/ppermute | solution.py:309
  44.3 5.2 %collective-permute-start.13 = (bf16[32,512]{1,0:T(8,128)(2,1)S(1)}, bf16[32,512]{1,0:T(8,128)(2,1)S(1)}, u32[]{:S(2)}, u32[]{:S(2)}) collective-permute-start(bf16[32,512]{1,0:T(8,128)(2,1)S(1)} %get-tuple-element.37), channel_id=1, source_target_pairs={{0,16},{1,17},{2,18},{3,19},{4,20},{5,21},{6,22},{7,23},{8,24},{9,... | collective-permute-start | bytes 98312 | tf_op jit(solution)/shard_map/ppermute | solution.py:309
  44.3 5.3 %collective-permute-start.14 = (bf16[32,512]{1,0:T(8,128)(2,1)S(1)}, bf16[32,512]{1,0:T(8,128)(2,1)S(1)}, u32[]{:S(2)}, u32[]{:S(2)}) collective-permute-start(bf16[32,512]{1,0:T(8,128)(2,1)S(1)} %get-tuple-element.38), channel_id=1, source_target_pairs={{0,8},{1,9},{2,10},{3,11},{4,12},{5,13},{6,14},{7,15},{8,0},{9,1},... | collective-permute-start | bytes 98312 | tf_op jit(solution)/shard_map/ppermute | solution.py:309

commit v15 on v14

--- a/solution.py
+++ b/solution.py
@@ -70,53 +70,50 @@
 
     def collect(block, rows, first, last):
         start = block * block_len
-        found = []
         for k in range(first, last):
             source = pl.multiple_of(slots_ref[start + k] * parts, parts)
-            found.append(table[pl.ds(source, parts), :])
-        for k in range(first, last):
-            rows[k * parts : (k + 1) * parts, :] = found[k - first]
-
-    def emit(rows, out):
-        for c in range(parts):
-            out[:, c * LANES : (c + 1) * LANES] = rows[
-                pl.ds(c, block_len, stride=parts), :
-            ].astype(BF16)
+            rows[k * parts : (k + 1) * parts, :] = table[pl.ds(source, parts), :]
+
+    def emit(rows, out, c):
+        out[:, c * LANES : (c + 1) * LANES] = rows[pl.ds(c, block_len, stride=parts), :].astype(
+            BF16
+        )
 
     collect(jnp.bitwise_xor(me, 1), odd_rows, 0, block_len)
     collect(me, even_rows, 0, block_len)
+    for c in range(parts):
+        emit(odd_rows, odd_feats, c)
     for copy in weight_copies:
         copy.wait()
 
+    def phase(i, shift, feats, rows, keys, values, idle_rows, idle_feats):
+        relation = rel_ref[jnp.bitwise_xor(me, _offset(i, outer) + shift)]
+        ahead = _offset(jnp.minimum(i + 1, blocks - 1), outer) + shift
+        nearby = jnp.bitwise_xor(me, ahead)
+        step = 0
+        for weight, transposed, out in ((kw, True, keys), (mw, False, values)):
+            for n in range(0, width, wide):
+                result = jnp.dot(
+                    feats[...], weight[relation, :, n : n + wide], preferred_element_type=F32
+                ).astype(BF16)
+                collect(nearby, rows, step * group, (step + 1) * group)
+                for c in range(step * parts * wide // (2 * width), (step + 1) * parts * wide // (2 * width)):
+                    emit(idle_rows, idle_feats, c)
+                step += 1
+                if transposed:
+                    out[i, n : n + wide, :] = result.T
+                else:
+                    out[i, :, n : n + wide] = result
+
     @pl.loop(0, blocks)
     def _(i):
-        emit(odd_rows, odd_feats)
-        emit(even_rows, even_feats)
-        offset = _offset(i, outer)
-        ahead = _offset(jnp.minimum(i + 1, blocks - 1), outer)
-        step = 0
-        for shift, feats, rows, keys, values in (
-            (1, odd_feats, odd_rows, odd_keys, odd_values),
-            (0, even_feats, even_rows, even_keys, even_values),
-        ):
-            relation = rel_ref[jnp.bitwise_xor(me, offset + shift)]
-            nearby = jnp.bitwise_xor(me, ahead + shift)
-            step = 0
-            for weight, transposed, out in ((kw, True, keys), (mw, False, values)):
-                for n in range(0, width, wide):
-                    result = jnp.dot(
-                        feats[...], weight[relation, :, n : n + wide], preferred_element_type=F32
-                    ).astype(BF16)
-                    collect(nearby, rows, step * group, (step + 1) * group)
-                    step += 1
-                    if transposed:
-                        out[i, n : n + wide, :] = result.T
-                    else:
-                        out[i, :, n : n + wide] = result
+        phase(i, 1, odd_feats, odd_rows, odd_keys, odd_values, even_rows, even_feats)
+        phase(i, 0, even_feats, even_rows, even_keys, even_values, odd_rows, odd_feats)
 
 
 def project(outer, me, rel, slots, acct, kw, mw):
-    blocks, block_len = slots.shape
+    blocks = rel.shape[0]
+    block_len = slots.shape[0] // blocks
     accounts, width = acct.shape
     parts = width // LANES
     rows = pltpu.VMEM((block_len * parts, LANES), F32)
@@ -143,7 +140,24 @@
         compiler_params=_mb(44 if blocks <= 32 else 50),
         cost_estimate=_cost(4 * blocks * block_len * width * width, 40 * 2**20),
         name="project_slots",
-    )(me, rel, slots.reshape(-1), acct, kw, mw)
+    )(me, rel, slots, acct, kw, mw)
+
+
+def stage_kernel(rel, slots, rel_out, slots_out):
+    rel_out[...] = rel[...]
+    slots_out[...] = slots[...]
+
+
+def stage(rel, slots):
+    return pl.pallas_call(
+        stage_kernel,
+        out_shape=tuple(jax.ShapeDtypeStruct(x.shape, x.dtype) for x in (rel, slots)),
+        in_specs=[VMEM, VMEM],
+        out_specs=(VMEM, VMEM),
+        compiler_params=_mb(2),
+        cost_estimate=_cost(0, 2**16),
+        name="stage_indices",
+    )(rel, slots)
 
 
 def assemble_kernel(*refs):
@@ -312,10 +326,12 @@
         return lax.optimization_barrier((value,) + others)[0]
 
     feats = jnp.concatenate([swap(merch_feat, 8 * k + 1) for k in range(outer)], axis=0)
+    staged_rel, staged_slots = stage(block_rel, slot_acct)
+    feats = after(feats, staged_rel)
     here = after(me, feats)
     feats = [feats] + [swap(feats, 2 * j) for j in range(1, inner)]
     odd_keys, odd_values, even_keys, even_values = project(
-        outer, here, block_rel, slot_acct, acct_feat, key_weight, msg_weight
+        outer, here, staged_rel, staged_slots.reshape(-1), acct_feat, key_weight, msg_weight
     )
     feats = assemble(after(tuple(feats), odd_keys))
     even_feats = swap(feats, 1)

time: 50.8 us -> 49.6 us (0.976)
  waiting for transfers between devices: 13.5 us -> 11.9 us
    ppermute x15, waiting for transfers between devices: 13.5 us -> 11.9 us  [swap(): return lax.ppermute(value, AXES, [(s, s ^ mask) for s in range(devices)])]
    unnamed x21 -> x20, local copies, waits for them, and re-layouts: 1.41 us -> 1.41 us
  transfers between devices with their start and end apart: 15 -> 15, of which waited for: 7 -> 7; matrix products, arithmetic and copies ran while one was open for 0% -> 0% of each run, Pallas kernels for 33% -> 35%
where the time goes in v15:
time: 49.6 us; the launch traced here: 49.4 us
  Pallas kernels  18.4 us (37%)
  starting transfers between devices  17.5 us (35%)
  waiting for transfers between devices  11.9 us (24%)
  local copies, waits for them, and re-layouts  1.41 us (3%)
    ppermute x15, starting transfers between devices, swap(): return lax.ppermute(value, AXES, [(s, s ^ mask) for s in range(devices)])  17.5 us
    pallas_call x1, Pallas kernels, project(): pl.pallas_call(functools.partial(project_kernel, outer), out_shape=(keys,...  14.2 us
    ppermute x15, waiting for transfers between devices, swap(): return lax.ppermute(value, AXES, [(s, s ^ mask) for s in range(devices)])  11.9 us
    pallas_call x2, Pallas kernels, aggregate(): pl.pallas_call(functools.partial(aggregate_kernel, outer, first, shift),...  3.07 us
    unnamed x20, local copies, waits for them, and re-layouts  1.41 us
  transfers between devices with their start and end apart: 15, of which 7 were waited for; matrix products, arithmetic and copies ran while one was open for 0% of the time, Pallas kernels for 35%

profile of v15, /device:TPU:0, one launch (start us, length us, event | category | flops | bytes accessed | tf_op | source)
XLA Modules:
  0.0 49.4 jit_solution(13339152503416219066)
XLA Ops:
  0.0 3.5 %collective-permute-start.2 = (bf16[32,512]{1,0:T(8,128)(2,1)}, bf16[32,512]{1,0:T(8,128)(2,1)S(1)}, u32[]{:S(2)}, u32[]{:S(2)}) collective-permute-start(bf16[32,512]{1,0:T(8,128)(2,1)} %feat.1), channel_id=1, source_target_pairs={{0,17},{1,16},{2,19},{3,18},{4,21},{5,20},{6,23},{7,22},{8,25},{9,... | collective-permute-start | bytes 98312 | tf_op jit(solution)/shard_map/ppermute | solution.py:323
  3.5 1.9 %collective-permute-start.1 = (bf16[32,512]{1,0:T(8,128)(2,1)}, bf16[32,512]{1,0:T(8,128)(2,1)S(1)}, u32[]{:S(2)}, u32[]{:S(2)}) collective-permute-start(bf16[32,512]{1,0:T(8,128)(2,1)} %feat.1), channel_id=1, source_target_pairs={{0,9},{1,8},{2,11},{3,10},{4,13},{5,12},{6,15},{7,14},{8,1},{9,0},... | collective-permute-start | bytes 98312 | tf_op jit(solution)/shard_map/ppermute | solution.py:323
  5.3 0.0 collective-permute-start
  5.3 0.7 %copy-done.4 = s32[32,128]{1,0:T(8,128)S(1)} copy-done((s32[32,128]{1,0:T(8,128)S(1)}, s32[32,128]{1,0:T(8,128)}, u32[]{:S(2)}) %copy-start.4) | copy-done | bytes 16408
  6.1 0.7 %copy-done.5 = s32[32]{0:T(128)S(1)} copy-done((s32[32]{0:T(128)S(1)}, s32[32]{0:T(128)}, u32[]{:S(2)}) %copy-start.5) | copy-done | bytes 152
  6.7 0.5 %collective-permute-done.1 = bf16[32,512]{1,0:T(8,128)(2,1)S(1)} collective-permute-done((bf16[32,512]{1,0:T(8,128)(2,1)}, bf16[32,512]{1,0:T(8,128)(2,1)S(1)}, u32[]{:S(2)}, u32[]{:S(2)}) %collective-permute-start.1) | collective-permute-done | bytes 32800 | tf_op jit(solution)/shard_map/ppermute | solution.py:323
  7.3 3.4 %collective-permute-done.3 = bf16[32,512]{1,0:T(8,128)(2,1)S(1)} collective-permute-done((bf16[32,512]{1,0:T(8,128)(2,1)}, bf16[32,512]{1,0:T(8,128)(2,1)S(1)}, u32[]{:S(2)}, u32[]{:S(2)}) %collective-permute-start.3) | collective-permute-done | bytes 32800 | tf_op jit(solution)/shard_map/ppermute | solution.py:323
  10.7 2.5 %collective-permute-start.6 = (bf16[128,512]{1,0:T(8,128)(2,1)S(1)}, bf16[128,512]{1,0:T(8,128)(2,1)S(1)}, u32[]{:S(2)}, u32[]{:S(2)}) collective-permute-start(bf16[128,512]{1,0:T(8,128)(2,1)S(1)} %pad_maximum_fusion.refs_0_), channel_id=1, source_target_pairs={{0,6},{1,7},{2,4},{3,5},{4,2},{5,3},{6,0},{7,1},{8,14},{9,15},{10,... | collective-permute-start | bytes 393224 | tf_op jit(solution)/shard_map/ppermute | solution.py:323
  13.2 0.5 %collective-permute-start.5 = (bf16[128,512]{1,0:T(8,128)(2,1)S(1)}, bf16[128,512]{1,0:T(8,128)(2,1)S(1)}, u32[]{:S(2)}, u32[]{:S(2)}) collective-permute-start(bf16[128,512]{1,0:T(8,128)(2,1)S(1)} %pad_maximum_fusion.refs_0_), channel_id=1, source_target_pairs={{0,4},{1,5},{2,6},{3,7},{4,0},{5,1},{6,2},{7,3},{8,12},{9,13},{10,... | collective-permute-start | bytes 393224 | tf_op jit(solution)/shard_map/ppermute | solution.py:323
  13.7 0.5 %collective-permute-start.4 = (bf16[128,512]{1,0:T(8,128)(2,1)S(1)}, bf16[128,512]{1,0:T(8,128)(2,1)S(1)}, u32[]{:S(2)}, u32[]{:S(2)}) collective-permute-start(bf16[128,512]{1,0:T(8,128)(2,1)S(1)} %pad_maximum_fusion.refs_0_), channel_id=1, source_target_pairs={{0,2},{1,3},{2,0},{3,1},{4,6},{5,7},{6,4},{7,5},{8,10},{9,11},{10,... | collective-permute-start | bytes 393224 | tf_op jit(solution)/shard_map/ppermute | solution.py:323
  14.3 0.0 copy-start.9
  14.3 14.2 %project_slots.1 = (bf16[16,512,128]{2,1,0:T(8,128)(2,1)S(1)}, bf16[16,128,512]{2,1,0:T(8,128)(2,1)S(1)}, bf16[16,512,128]{2,1,0:T(8,128)(2,1)S(1)}, bf16[16,128,512]{2,1,0:T(8,128)(2,1)S(1)}) custom-call(s32[1]{0:T(128)} %bitcast.1.me_ref, s32[32]{0:T(128)S(1)} %get-tuple-element.25.rel_ref, s32[4096]{0:T(1024)S(1)} %bitcast.4, bf16[4096,512]{1,0:T(8,128)(2,1)} %acct_hbm.1, ...), custom_call_target="tpu_custom_call" | custom-call | flops 4294967296 | bytes 41943040 | tf_op jit(solution)/shard_map/project_slots/pallas_call | solution.py:123
  28.5 0.1 collective-permute-start.7
  28.6 1.5 %aggregate_odd.1 = bf16[512,512]{1,0:T(8,128)(2,1)S(1)} custom-call(s32[1]{0:T(128)} %bitcast.1.me_ref, s32[32]{0:T(128)S(1)} %copy-done.6, s32[32]{0:T(128)S(1)} %copy-done.8, f32[4]{0:T(128)S(1)} %copy-done.9, s32[32,128]{1,0:T(8,128)S(1)} %copy-done.2, bf16[512,512]{1,0:T(8,128)(2,1)S(1)} %assemble.1.feats, bf16[512,512]{1,0:T(8,128)(2,1)S(1)} %copy-done, ...), custom_call_target="tpu_custom_call" | custom-call | flops 402653184 | bytes 6291456 | tf_op jit(solution)/shard_map/aggregate_odd/pallas_call | solution.py:212
  30.2 0.5 %collective-permute-start.8 = (bf16[512,512]{1,0:T(8,128)(2,1)S(1)}, bf16[512,512]{1,0:T(8,128)(2,1)S(1)}, u32[]{:S(2)}, u32[]{:S(2)}) collective-permute-start(bf16[512,512]{1,0:T(8,128)(2,1)S(1)} %aggregate_odd.1), channel_id=1, source_target_pairs={{0,1},{1,0},{2,3},{3,2},{4,5},{5,4},{6,7},{7,6},{8,9},{9,8},{10,11... | collective-permute-start | bytes 1572872 | tf_op jit(solution)/shard_map/ppermute | solution.py:323
  30.7 1.5 %aggregate_even.1.mine = f32[512,512]{1,0:T(8,128)S(1)} custom-call(s32[1]{0:T(128)} %bitcast.1.me_ref, s32[32]{0:T(128)S(1)} %copy-done.6, s32[32]{0:T(128)S(1)} %copy-done.8, f32[4]{0:T(128)S(1)} %copy-done.9, s32[32,128]{1,0:T(8,128)S(1)} %copy-done.2, bf16[512,512]{1,0:T(8,128)(2,1)S(1)} %collective-permute-done.7.feats, bf16[512,512]{1,0:T(8,128)(2,1)S(1)} %copy-done, ...), custom_call_target="tpu_custom_call" | custom-call | flops 402653184 | bytes 6291456 | tf_op jit(solution)/shard_map/aggregate_even/pallas_call | solution.py:212
  32.3 0.0 copy-start.1
  32.3 0.0 copy-start.3
  32.3 0.0 copy-start.7
  32.3 0.1 combine_cores.1
  32.4 2.5 %collective-permute-start.9 = (bf16[128,512]{1,0:T(8,128)(2,1)S(1)}, bf16[128,512]{1,0:T(8,128)(2,1)S(1)}, u32[]{:S(2)}, u32[]{:S(2)}) collective-permute-start(bf16[128,512]{1,0:T(8,128)(2,1)S(1)} %get-tuple-element.38), channel_id=1, source_target_pairs={{0,6},{1,7},{2,4},{3,5},{4,2},{5,3},{6,0},{7,1},{8,14},{9,15},{10,... | collective-permute-start | bytes 393224 | tf_op jit(solution)/shard_map/ppermute | solution.py:323
  35.0 0.5 %collective-permute-start.10 = (bf16[128,512]{1,0:T(8,128)(2,1)S(1)}, bf16[128,512]{1,0:T(8,128)(2,1)S(1)}, u32[]{:S(2)}, u32[]{:S(2)}) collective-permute-start(bf16[128,512]{1,0:T(8,128)(2,1)S(1)} %get-tuple-element.39), channel_id=1, source_target_pairs={{0,4},{1,5},{2,6},{3,7},{4,0},{5,1},{6,2},{7,3},{8,12},{9,13},{10,... | collective-permute-start | bytes 393224 | tf_op jit(solution)/shard_map/ppermute | solution.py:323
  35.5 0.5 collective-permute-start.11
  36.0 3.4 %collective-permute-done.9.refs_1_ = bf16[128,512]{1,0:T(8,128)(2,1)S(1)} collective-permute-done((bf16[128,512]{1,0:T(8,128)(2,1)S(1)}, bf16[128,512]{1,0:T(8,128)(2,1)S(1)}, u32[]{:S(2)}, u32[]{:S(2)}) %collective-permute-start.9) | collective-permute-done | bytes 131104 | tf_op jit(solution)/shard_map/ppermute | solution.py:323
  39.4 2.5 %collective-permute-done.10.refs_2_ = bf16[128,512]{1,0:T(8,128)(2,1)S(1)} collective-permute-done((bf16[128,512]{1,0:T(8,128)(2,1)S(1)}, bf16[128,512]{1,0:T(8,128)(2,1)S(1)}, u32[]{:S(2)}, u32[]{:S(2)}) %collective-permute-start.10) | collective-permute-done | bytes 131104 | tf_op jit(solution)/shard_map/ppermute | solution.py:323
  41.9 0.1 collective-permute-done.11.refs_3_
  42.1 0.1 combine_plane.1
  42.1 0.7 %collective-permute-start.12 = (bf16[32,512]{1,0:T(8,128)(2,1)S(1)}, bf16[32,512]{1,0:T(8,128)(2,1)S(1)}, u32[]{:S(2)}, u32[]{:S(2)}) collective-permute-start(bf16[32,512]{1,0:T(8,128)(2,1)S(1)} %get-tuple-element.42), channel_id=1, source_target_pairs={{0,24},{1,25},{2,26},{3,27},{4,28},{5,29},{6,30},{7,31},{8,16},{9,... | collective-permute-start | bytes 98312 | tf_op jit(solution)/shard_map/ppermute | solution.py:323
  42.8 3.8 %collective-permute-start.14 = (bf16[32,512]{1,0:T(8,128)(2,1)S(1)}, bf16[32,512]{1,0:T(8,128)(2,1)S(1)}, u32[]{:S(2)}, u32[]{:S(2)}) collective-permute-start(bf16[32,512]{1,0:T(8,128)(2,1)S(1)} %get-tuple-element.44), channel_id=1, source_target_pairs={{0,8},{1,9},{2,10},{3,11},{4,12},{5,13},{6,14},{7,15},{8,0},{9,1},... | collective-permute-start | bytes 98312 | tf_op jit(solution)/shard_map/ppermute | solution.py:323
  46.6 1.4 %collective-permute-done.12.refs_1_ = bf16[32,512]{1,0:T(8,128)(2,1)S(1)} collective-permute-done((bf16[32,512]{1,0:T(8,128)(2,1)S(1)}, bf16[32,512]{1,0:T(8,128)(2,1)S(1)}, u32[]{:S(2)}, u32[]{:S(2)}) %collective-permute-start.12) | collective-permute-done | bytes 32800 | tf_op jit(solution)/shard_map/ppermute | solution.py:323
  48.0 0.5 %collective-permute-done.14.refs_3_ = bf16[32,512]{1,0:T(8,128)(2,1)S(1)} collective-permute-done((bf16[32,512]{1,0:T(8,128)(2,1)S(1)}, bf16[32,512]{1,0:T(8,128)(2,1)S(1)}, u32[]{:S(2)}, u32[]{:S(2)}) %collective-permute-start.14) | collective-permute-done | bytes 32800 | tf_op jit(solution)/shard_map/ppermute | solution.py:323
  48.5 0.9 %finish.1 = bf16[32,512]{1,0:T(8,128)(2,1)} custom-call(bf16[32,512]{1,0:T(8,128)(2,1)S(1)} %copy-done.3, f32[1,512]{1,0:T(1,128)S(1)} %bitcast.3, bf16[512,512]{1,0:T(8,128)(2,1)S(1)} %copy-done.1, f32[32,512]{1,0:T(8,128)S(1)} %get-tuple-element.41.refs_0_, bf16[32,512]{1,0:T(8,128)(2,1)S(1)} %collective-permute-done.12.refs_1_, ...), custom_call_target="tpu_custom_call" | custom-call | tf_op jit(solution)/shard_map/finish/pallas_call | solution.py:293
  (27 shorter events, 0.1 us)
Async XLA Ops:
  0.0 6.7 %collective-permute-start.2 = (bf16[32,512]{1,0:T(8,128)(2,1)}, bf16[32,512]{1,0:T(8,128)(2,1)S(1)}, u32[]{:S(2)}, u32[]{:S(2)}) collective-permute-start(bf16[32,512]{1,0:T(8,128)(2,1)} %feat.1), channel_id=1, source_target_pairs={{0,17},{1,16},{2,19},{3,18},{4,21},{5,20},{6,23},{7,22},{8,25},{9,... | collective-permute-start | bytes 98312 | tf_op jit(solution)/shard_map/ppermute | solution.py:323
  3.5 3.8 %collective-permute-start.1 = (bf16[32,512]{1,0:T(8,128)(2,1)}, bf16[32,512]{1,0:T(8,128)(2,1)S(1)}, u32[]{:S(2)}, u32[]{:S(2)}) collective-permute-start(bf16[32,512]{1,0:T(8,128)(2,1)} %feat.1), channel_id=1, source_target_pairs={{0,9},{1,8},{2,11},{3,10},{4,13},{5,12},{6,15},{7,14},{8,1},{9,0},... | collective-permute-start | bytes 98312 | tf_op jit(solution)/shard_map/ppermute | solution.py:323
  5.3 1.9 %collective-permute-start = (bf16[32,512]{1,0:T(8,128)(2,1)}, bf16[32,512]{1,0:T(8,128)(2,1)S(1)}, u32[]{:S(2)}, u32[]{:S(2)}) collective-permute-start(bf16[32,512]{1,0:T(8,128)(2,1)} %feat.1), channel_id=1, source_target_pairs={{0,1},{1,0},{2,3},{3,2},{4,5},{5,4},{6,7},{7,6},{8,9},{9,8},{10,11... | collective-permute-start | bytes 98312 | tf_op jit(solution)/shard_map/ppermute | solution.py:323
  5.3 5.3 %collective-permute-start.3 = (bf16[32,512]{1,0:T(8,128)(2,1)}, bf16[32,512]{1,0:T(8,128)(2,1)S(1)}, u32[]{:S(2)}, u32[]{:S(2)}) collective-permute-start(bf16[32,512]{1,0:T(8,128)(2,1)} %feat.1), channel_id=1, source_target_pairs={{0,25},{1,24},{2,27},{3,26},{4,29},{5,28},{6,31},{7,30},{8,17},{9,... | collective-permute-start | bytes 98312 | tf_op jit(solution)/shard_map/ppermute | solution.py:323
  5.3 0.7 %copy-start.4 = (s32[32,128]{1,0:T(8,128)S(1)}, s32[32,128]{1,0:T(8,128)}, u32[]{:S(2)}) copy-start(s32[32,128]{1,0:T(8,128)} %slots.1) | copy-start | bytes 49156
  6.1 0.7 %copy-start.5 = (s32[32]{0:T(128)S(1)}, s32[32]{0:T(128)}, u32[]{:S(2)}) copy-start(s32[32]{0:T(128)} %rel_ref.3) | copy-start | bytes 388
  10.7 17.7 %collective-permute-start.6 = (bf16[128,512]{1,0:T(8,128)(2,1)S(1)}, bf16[128,512]{1,0:T(8,128)(2,1)S(1)}, u32[]{:S(2)}, u32[]{:S(2)}) collective-permute-start(bf16[128,512]{1,0:T(8,128)(2,1)S(1)} %pad_maximum_fusion.refs_0_), channel_id=1, source_target_pairs={{0,6},{1,7},{2,4},{3,5},{4,2},{5,3},{6,0},{7,1},{8,14},{9,15},{10,... | collective-permute-start | bytes 393224 | tf_op jit(solution)/shard_map/ppermute | solution.py:323
  13.2 15.2 %collective-permute-start.5 = (bf16[128,512]{1,0:T(8,128)(2,1)S(1)}, bf16[128,512]{1,0:T(8,128)(2,1)S(1)}, u32[]{:S(2)}, u32[]{:S(2)}) collective-permute-start(bf16[128,512]{1,0:T(8,128)(2,1)S(1)} %pad_maximum_fusion.refs_0_), channel_id=1, source_target_pairs={{0,4},{1,5},{2,6},{3,7},{4,0},{5,1},{6,2},{7,3},{8,12},{9,13},{10,... | collective-permute-start | bytes 393224 | tf_op jit(solution)/shard_map/ppermute | solution.py:323
  13.7 14.7 %collective-permute-start.4 = (bf16[128,512]{1,0:T(8,128)(2,1)S(1)}, bf16[128,512]{1,0:T(8,128)(2,1)S(1)}, u32[]{:S(2)}, u32[]{:S(2)}) collective-permute-start(bf16[128,512]{1,0:T(8,128)(2,1)S(1)} %pad_maximum_fusion.refs_0_), channel_id=1, source_target_pairs={{0,2},{1,3},{2,0},{3,1},{4,6},{5,7},{6,4},{7,5},{8,10},{9,11},{10,... | collective-permute-start | bytes 393224 | tf_op jit(solution)/shard_map/ppermute | solution.py:323
  14.3 14.3 %copy-start = (bf16[512,512]{1,0:T(8,128)(2,1)S(1)}, bf16[512,512]{1,0:T(8,128)(2,1)}, u32[]{:S(2)}) copy-start(bf16[512,512]{1,0:T(8,128)(2,1)} %wq.3) | copy-start | bytes 1572868
  14.3 14.4 %copy-start.2 = (s32[32,128]{1,0:T(8,128)S(1)}, s32[32,128]{1,0:T(8,128)}, u32[]{:S(2)}) copy-start(s32[32,128]{1,0:T(8,128)} %merch_slot.3) | copy-start | bytes 49156
  14.3 14.4 %copy-start.6 = (s32[32]{0:T(128)S(1)}, s32[32]{0:T(128)}, u32[]{:S(2)}) copy-start(s32[32]{0:T(128)} %rel_ref.3) | copy-start | bytes 388
  14.3 14.4 %copy-start.8 = (s32[32]{0:T(128)S(1)}, s32[32]{0:T(128)}, u32[]{:S(2)}) copy-start(s32[32]{0:T(128)} %count_ref.3) | copy-start | bytes 388
  14.3 14.4 %copy-start.9 = (f32[4]{0:T(128)S(1)}, f32[4]{0:T(128)}, u32[]{:S(2)}) copy-start(f32[4]{0:T(128)} %bias_ref.3) | copy-start | bytes 52
  28.5 2.2 %collective-permute-start.7 = (bf16[512,512]{1,0:T(8,128)(2,1)S(1)}, bf16[512,512]{1,0:T(8,128)(2,1)S(1)}, u32[]{:S(2)}, u32[]{:S(2)}) collective-permute-start(bf16[512,512]{1,0:T(8,128)(2,1)S(1)} %assemble.1.feats), channel_id=1, source_target_pairs={{0,1},{1,0},{2,3},{3,2},{4,5},{5,4},{6,7},{7,6},{8,9},{9,8},{10,11... | collective-permute-start | bytes 1572872 | tf_op jit(solution)/shard_map/ppermute | solution.py:323
  30.2 2.1 %collective-permute-start.8 = (bf16[512,512]{1,0:T(8,128)(2,1)S(1)}, bf16[512,512]{1,0:T(8,128)(2,1)S(1)}, u32[]{:S(2)}, u32[]{:S(2)}) collective-permute-start(bf16[512,512]{1,0:T(8,128)(2,1)S(1)} %aggregate_odd.1), channel_id=1, source_target_pairs={{0,1},{1,0},{2,3},{3,2},{4,5},{5,4},{6,7},{7,6},{8,9},{9,8},{10,11... | collective-permute-start | bytes 1572872 | tf_op jit(solution)/shard_map/ppermute | solution.py:323
  32.3 16.2 %copy-start.1 = (bf16[512,512]{1,0:T(8,128)(2,1)S(1)}, bf16[512,512]{1,0:T(8,128)(2,1)}, u32[]{:S(2)}) copy-start(bf16[512,512]{1,0:T(8,128)(2,1)} %wo.1) | copy-start | bytes 1572868
  32.3 16.2 %copy-start.3 = (bf16[32,512]{1,0:T(8,128)(2,1)S(1)}, bf16[32,512]{1,0:T(8,128)(2,1)}, u32[]{:S(2)}) copy-start(bf16[32,512]{1,0:T(8,128)(2,1)} %feat.1) | copy-start | bytes 98308
  32.3 16.2 %copy-start.7 = (f32[512]{0:T(512)S(1)}, f32[512]{0:T(512)}, u32[]{:S(2)}) copy-start(f32[512]{0:T(512)} %param.19) | copy-start | bytes 6148
  32.4 7.0 %collective-permute-start.9 = (bf16[128,512]{1,0:T(8,128)(2,1)S(1)}, bf16[128,512]{1,0:T(8,128)(2,1)S(1)}, u32[]{:S(2)}, u32[]{:S(2)}) collective-permute-start(bf16[128,512]{1,0:T(8,128)(2,1)S(1)} %get-tuple-element.38), channel_id=1, source_target_pairs={{0,6},{1,7},{2,4},{3,5},{4,2},{5,3},{6,0},{7,1},{8,14},{9,15},{10,... | collective-permute-start | bytes 393224 | tf_op jit(solution)/shard_map/ppermute | solution.py:323
  35.0 7.0 %collective-permute-start.10 = (bf16[128,512]{1,0:T(8,128)(2,1)S(1)}, bf16[128,512]{1,0:T(8,128)(2,1)S(1)}, u32[]{:S(2)}, u32[]{:S(2)}) collective-permute-start(bf16[128,512]{1,0:T(8,128)(2,1)S(1)} %get-tuple-element.39), channel_id=1, source_target_pairs={{0,4},{1,5},{2,6},{3,7},{4,0},{5,1},{6,2},{7,3},{8,12},{9,13},{10,... | collective-permute-start | bytes 393224 | tf_op jit(solution)/shard_map/ppermute | solution.py:323
  35.5 6.6 %collective-permute-start.11 = (bf16[128,512]{1,0:T(8,128)(2,1)S(1)}, bf16[128,512]{1,0:T(8,128)(2,1)S(1)}, u32[]{:S(2)}, u32[]{:S(2)}) collective-permute-start(bf16[128,512]{1,0:T(8,128)(2,1)S(1)} %get-tuple-element.40), channel_id=1, source_target_pairs={{0,2},{1,3},{2,0},{3,1},{4,6},{5,7},{6,4},{7,5},{8,10},{9,11},{10,... | collective-permute-start | bytes 393224 | tf_op jit(solution)/shard_map/ppermute | solution.py:323
  42.1 5.8 %collective-permute-start.12 = (bf16[32,512]{1,0:T(8,128)(2,1)S(1)}, bf16[32,512]{1,0:T(8,128)(2,1)S(1)}, u32[]{:S(2)}, u32[]{:S(2)}) collective-permute-start(bf16[32,512]{1,0:T(8,128)(2,1)S(1)} %get-tuple-element.42), channel_id=1, source_target_pairs={{0,24},{1,25},{2,26},{3,27},{4,28},{5,29},{6,30},{7,31},{8,16},{9,... | collective-permute-start | bytes 98312 | tf_op jit(solution)/shard_map/ppermute | solution.py:323
  42.8 5.2 %collective-permute-start.13 = (bf16[32,512]{1,0:T(8,128)(2,1)S(1)}, bf16[32,512]{1,0:T(8,128)(2,1)S(1)}, u32[]{:S(2)}, u32[]{:S(2)}) collective-permute-start(bf16[32,512]{1,0:T(8,128)(2,1)S(1)} %get-tuple-element.43), channel_id=1, source_target_pairs={{0,16},{1,17},{2,18},{3,19},{4,20},{5,21},{6,22},{7,23},{8,24},{9,... | collective-permute-start | bytes 98312 | tf_op jit(solution)/shard_map/ppermute | solution.py:323
  42.8 5.7 %collective-permute-start.14 = (bf16[32,512]{1,0:T(8,128)(2,1)S(1)}, bf16[32,512]{1,0:T(8,128)(2,1)S(1)}, u32[]{:S(2)}, u32[]{:S(2)}) collective-permute-start(bf16[32,512]{1,0:T(8,128)(2,1)S(1)} %get-tuple-element.44), channel_id=1, source_target_pairs={{0,8},{1,9},{2,10},{3,11},{4,12},{5,13},{6,14},{7,15},{8,0},{9,1},... | collective-permute-start | bytes 98312 | tf_op jit(solution)/shard_map/ppermute | solution.py:323

commit v16 on v15

--- a/solution.py
+++ b/solution.py
@@ -70,9 +70,13 @@
 
     def collect(block, rows, first, last):
         start = block * block_len
-        for k in range(first, last):
-            source = pl.multiple_of(slots_ref[start + k] * parts, parts)
-            rows[k * parts : (k + 1) * parts, :] = table[pl.ds(source, parts), :]
+        for low in range(first, last, 16):
+            found = []
+            for k in range(low, low + 16):
+                source = pl.multiple_of(slots_ref[start + k] * parts, parts)
+                found.append(table[pl.ds(source, parts), :])
+            for k in range(low, low + 16):
+                rows[k * parts : (k + 1) * parts, :] = found[k - low]
 
     def emit(rows, out, c):
         out[:, c * LANES : (c + 1) * LANES] = rows[pl.ds(c, block_len, stride=parts), :].astype(
@@ -86,29 +90,42 @@
     for copy in weight_copies:
         copy.wait()
 
-    def phase(i, shift, feats, rows, keys, values, idle_rows, idle_feats):
+    def put(i, pending):
+        out, n, transposed, result = pending
+        if transposed:
+            out[i, n : n + wide, :] = result.T
+        else:
+            out[i, :, n : n + wide] = result
+
+    def phase(i, shift, feats, rows, keys, values, idle_rows, idle_feats, pending):
         relation = rel_ref[jnp.bitwise_xor(me, _offset(i, outer) + shift)]
         ahead = _offset(jnp.minimum(i + 1, blocks - 1), outer) + shift
         nearby = jnp.bitwise_xor(me, ahead)
-        step = 0
-        for weight, transposed, out in ((kw, True, keys), (mw, False, values)):
-            for n in range(0, width, wide):
-                result = jnp.dot(
-                    feats[...], weight[relation, :, n : n + wide], preferred_element_type=F32
-                ).astype(BF16)
-                collect(nearby, rows, step * group, (step + 1) * group)
-                for c in range(step * parts * wide // (2 * width), (step + 1) * parts * wide // (2 * width)):
-                    emit(idle_rows, idle_feats, c)
-                step += 1
-                if transposed:
-                    out[i, n : n + wide, :] = result.T
-                else:
-                    out[i, :, n : n + wide] = result
+        steps = 2 * width // wide
+        for step in range(steps):
+            transposed = step < steps // 2
+            weight, out = (kw, keys) if transposed else (mw, values)
+            n = step % (steps // 2) * wide
+            result = jnp.dot(
+                feats[...], weight[relation, :, n : n + wide], preferred_element_type=F32
+            ).astype(BF16)
+            collect(nearby, rows, step * group, (step + 1) * group)
+            for c in range(step * parts // steps, (step + 1) * parts // steps):
+                emit(idle_rows, idle_feats, c)
+            if pending is not None:
+                put(i, pending)
+            pending = (out, n, transposed, result)
+        return pending
 
     @pl.loop(0, blocks)
     def _(i):
-        phase(i, 1, odd_feats, odd_rows, odd_keys, odd_values, even_rows, even_feats)
-        phase(i, 0, even_feats, even_rows, even_keys, even_values, odd_rows, odd_feats)
+        pending = phase(
+            i, 1, odd_feats, odd_rows, odd_keys, odd_values, even_rows, even_feats, None
+        )
+        pending = phase(
+            i, 0, even_feats, even_rows, even_keys, even_values, odd_rows, odd_feats, pending
+        )
+        put(i, pending)
 
 
 def project(outer, me, rel, slots, acct, kw, mw):

time: 49.6 us -> 49.6 us (level)
  no operation moved by 1% of the time
where the time goes in v16:
time: 49.6 us; the launch traced here: 49.4 us
  Pallas kernels  18.4 us (37%)
  starting transfers between devices  17.5 us (35%)
  waiting for transfers between devices  11.9 us (24%)
  local copies, waits for them, and re-layouts  1.41 us (3%)
    ppermute x15, starting transfers between devices, swap(): return lax.ppermute(value, AXES, [(s, s ^ mask) for s in range(devices)])  17.5 us
    pallas_call x1, Pallas kernels, project(): pl.pallas_call(functools.partial(project_kernel, outer), out_shape=(keys,...  14.2 us
    ppermute x15, waiting for transfers between devices, swap(): return lax.ppermute(value, AXES, [(s, s ^ mask) for s in range(devices)])  11.9 us
    pallas_call x2, Pallas kernels, aggregate(): pl.pallas_call(functools.partial(aggregate_kernel, outer, first, shift),...  3.07 us
    unnamed x20, local copies, waits for them, and re-layouts  1.41 us
  transfers between devices with their start and end apart: 15, of which 7 were waited for; matrix products, arithmetic and copies ran while one was open for 0% of the time, Pallas kernels for 35%

profile of v16, /device:TPU:0, one launch (start us, length us, event | category | flops | bytes accessed | tf_op | source)
XLA Modules:
  0.0 49.4 jit_solution(17935320491411348732)
XLA Ops:
  0.0 3.5 %collective-permute-start.2 = (bf16[32,512]{1,0:T(8,128)(2,1)}, bf16[32,512]{1,0:T(8,128)(2,1)S(1)}, u32[]{:S(2)}, u32[]{:S(2)}) collective-permute-start(bf16[32,512]{1,0:T(8,128)(2,1)} %feat.1), channel_id=1, source_target_pairs={{0,17},{1,16},{2,19},{3,18},{4,21},{5,20},{6,23},{7,22},{8,25},{9,... | collective-permute-start | bytes 98312 | tf_op jit(solution)/shard_map/ppermute | solution.py:340
  3.5 1.9 %collective-permute-start.1 = (bf16[32,512]{1,0:T(8,128)(2,1)}, bf16[32,512]{1,0:T(8,128)(2,1)S(1)}, u32[]{:S(2)}, u32[]{:S(2)}) collective-permute-start(bf16[32,512]{1,0:T(8,128)(2,1)} %feat.1), channel_id=1, source_target_pairs={{0,9},{1,8},{2,11},{3,10},{4,13},{5,12},{6,15},{7,14},{8,1},{9,0},... | collective-permute-start | bytes 98312 | tf_op jit(solution)/shard_map/ppermute | solution.py:340
  5.3 0.0 collective-permute-start
  5.3 0.7 %copy-done.4 = s32[32,128]{1,0:T(8,128)S(1)} copy-done((s32[32,128]{1,0:T(8,128)S(1)}, s32[32,128]{1,0:T(8,128)}, u32[]{:S(2)}) %copy-start.4) | copy-done | bytes 16408
  6.1 0.7 %copy-done.5 = s32[32]{0:T(128)S(1)} copy-done((s32[32]{0:T(128)S(1)}, s32[32]{0:T(128)}, u32[]{:S(2)}) %copy-start.5) | copy-done | bytes 152
  6.7 0.5 %collective-permute-done.1 = bf16[32,512]{1,0:T(8,128)(2,1)S(1)} collective-permute-done((bf16[32,512]{1,0:T(8,128)(2,1)}, bf16[32,512]{1,0:T(8,128)(2,1)S(1)}, u32[]{:S(2)}, u32[]{:S(2)}) %collective-permute-start.1) | collective-permute-done | bytes 32800 | tf_op jit(solution)/shard_map/ppermute | solution.py:340
  7.3 3.4 %collective-permute-done.3 = bf16[32,512]{1,0:T(8,128)(2,1)S(1)} collective-permute-done((bf16[32,512]{1,0:T(8,128)(2,1)}, bf16[32,512]{1,0:T(8,128)(2,1)S(1)}, u32[]{:S(2)}, u32[]{:S(2)}) %collective-permute-start.3) | collective-permute-done | bytes 32800 | tf_op jit(solution)/shard_map/ppermute | solution.py:340
  10.7 2.5 %collective-permute-start.6 = (bf16[128,512]{1,0:T(8,128)(2,1)S(1)}, bf16[128,512]{1,0:T(8,128)(2,1)S(1)}, u32[]{:S(2)}, u32[]{:S(2)}) collective-permute-start(bf16[128,512]{1,0:T(8,128)(2,1)S(1)} %pad_maximum_fusion.refs_0_), channel_id=1, source_target_pairs={{0,6},{1,7},{2,4},{3,5},{4,2},{5,3},{6,0},{7,1},{8,14},{9,15},{10,... | collective-permute-start | bytes 393224 | tf_op jit(solution)/shard_map/ppermute | solution.py:340
  13.2 0.5 %collective-permute-start.5 = (bf16[128,512]{1,0:T(8,128)(2,1)S(1)}, bf16[128,512]{1,0:T(8,128)(2,1)S(1)}, u32[]{:S(2)}, u32[]{:S(2)}) collective-permute-start(bf16[128,512]{1,0:T(8,128)(2,1)S(1)} %pad_maximum_fusion.refs_0_), channel_id=1, source_target_pairs={{0,4},{1,5},{2,6},{3,7},{4,0},{5,1},{6,2},{7,3},{8,12},{9,13},{10,... | collective-permute-start | bytes 393224 | tf_op jit(solution)/shard_map/ppermute | solution.py:340
  13.7 0.5 %collective-permute-start.4 = (bf16[128,512]{1,0:T(8,128)(2,1)S(1)}, bf16[128,512]{1,0:T(8,128)(2,1)S(1)}, u32[]{:S(2)}, u32[]{:S(2)}) collective-permute-start(bf16[128,512]{1,0:T(8,128)(2,1)S(1)} %pad_maximum_fusion.refs_0_), channel_id=1, source_target_pairs={{0,2},{1,3},{2,0},{3,1},{4,6},{5,7},{6,4},{7,5},{8,10},{9,11},{10,... | collective-permute-start | bytes 393224 | tf_op jit(solution)/shard_map/ppermute | solution.py:340
  14.3 0.0 copy-start.9
  14.3 14.2 %project_slots.1 = (bf16[16,512,128]{2,1,0:T(8,128)(2,1)S(1)}, bf16[16,128,512]{2,1,0:T(8,128)(2,1)S(1)}, bf16[16,512,128]{2,1,0:T(8,128)(2,1)S(1)}, bf16[16,128,512]{2,1,0:T(8,128)(2,1)S(1)}) custom-call(s32[1]{0:T(128)} %bitcast.1.me_ref, s32[32]{0:T(128)S(1)} %get-tuple-element.25.rel_ref, s32[4096]{0:T(1024)S(1)} %bitcast.4, bf16[4096,512]{1,0:T(8,128)(2,1)} %acct_hbm.1, ...), custom_call_target="tpu_custom_call" | custom-call | flops 4294967296 | bytes 41943040 | tf_op jit(solution)/shard_map/project_slots/pallas_call | solution.py:140
  28.5 0.1 collective-permute-start.7
  28.6 1.5 %aggregate_odd.1 = bf16[512,512]{1,0:T(8,128)(2,1)S(1)} custom-call(s32[1]{0:T(128)} %bitcast.1.me_ref, s32[32]{0:T(128)S(1)} %copy-done.6, s32[32]{0:T(128)S(1)} %copy-done.8, f32[4]{0:T(128)S(1)} %copy-done.9, s32[32,128]{1,0:T(8,128)S(1)} %copy-done.2, bf16[512,512]{1,0:T(8,128)(2,1)S(1)} %assemble.1.feats, bf16[512,512]{1,0:T(8,128)(2,1)S(1)} %copy-done, ...), custom_call_target="tpu_custom_call" | custom-call | flops 402653184 | bytes 6291456 | tf_op jit(solution)/shard_map/aggregate_odd/pallas_call | solution.py:229
  30.2 0.5 %collective-permute-start.8 = (bf16[512,512]{1,0:T(8,128)(2,1)S(1)}, bf16[512,512]{1,0:T(8,128)(2,1)S(1)}, u32[]{:S(2)}, u32[]{:S(2)}) collective-permute-start(bf16[512,512]{1,0:T(8,128)(2,1)S(1)} %aggregate_odd.1), channel_id=1, source_target_pairs={{0,1},{1,0},{2,3},{3,2},{4,5},{5,4},{6,7},{7,6},{8,9},{9,8},{10,11... | collective-permute-start | bytes 1572872 | tf_op jit(solution)/shard_map/ppermute | solution.py:340
  30.7 1.5 %aggregate_even.1.mine = f32[512,512]{1,0:T(8,128)S(1)} custom-call(s32[1]{0:T(128)} %bitcast.1.me_ref, s32[32]{0:T(128)S(1)} %copy-done.6, s32[32]{0:T(128)S(1)} %copy-done.8, f32[4]{0:T(128)S(1)} %copy-done.9, s32[32,128]{1,0:T(8,128)S(1)} %copy-done.2, bf16[512,512]{1,0:T(8,128)(2,1)S(1)} %collective-permute-done.7.feats, bf16[512,512]{1,0:T(8,128)(2,1)S(1)} %copy-done, ...), custom_call_target="tpu_custom_call" | custom-call | flops 402653184 | bytes 6291456 | tf_op jit(solution)/shard_map/aggregate_even/pallas_call | solution.py:229
  32.3 0.0 copy-start.1
  32.3 0.0 copy-start.3
  32.3 0.0 copy-start.7
  32.3 0.1 combine_cores.1
  32.4 2.5 %collective-permute-start.9 = (bf16[128,512]{1,0:T(8,128)(2,1)S(1)}, bf16[128,512]{1,0:T(8,128)(2,1)S(1)}, u32[]{:S(2)}, u32[]{:S(2)}) collective-permute-start(bf16[128,512]{1,0:T(8,128)(2,1)S(1)} %get-tuple-element.38), channel_id=1, source_target_pairs={{0,6},{1,7},{2,4},{3,5},{4,2},{5,3},{6,0},{7,1},{8,14},{9,15},{10,... | collective-permute-start | bytes 393224 | tf_op jit(solution)/shard_map/ppermute | solution.py:340
  34.9 0.5 %collective-permute-start.10 = (bf16[128,512]{1,0:T(8,128)(2,1)S(1)}, bf16[128,512]{1,0:T(8,128)(2,1)S(1)}, u32[]{:S(2)}, u32[]{:S(2)}) collective-permute-start(bf16[128,512]{1,0:T(8,128)(2,1)S(1)} %get-tuple-element.39), channel_id=1, source_target_pairs={{0,4},{1,5},{2,6},{3,7},{4,0},{5,1},{6,2},{7,3},{8,12},{9,13},{10,... | collective-permute-start | bytes 393224 | tf_op jit(solution)/shard_map/ppermute | solution.py:340
  35.4 0.6 %collective-permute-start.11 = (bf16[128,512]{1,0:T(8,128)(2,1)S(1)}, bf16[128,512]{1,0:T(8,128)(2,1)S(1)}, u32[]{:S(2)}, u32[]{:S(2)}) collective-permute-start(bf16[128,512]{1,0:T(8,128)(2,1)S(1)} %get-tuple-element.40), channel_id=1, source_target_pairs={{0,2},{1,3},{2,0},{3,1},{4,6},{5,7},{6,4},{7,5},{8,10},{9,11},{10,... | collective-permute-start | bytes 393224 | tf_op jit(solution)/shard_map/ppermute | solution.py:340
  36.0 3.5 %collective-permute-done.9.refs_1_ = bf16[128,512]{1,0:T(8,128)(2,1)S(1)} collective-permute-done((bf16[128,512]{1,0:T(8,128)(2,1)S(1)}, bf16[128,512]{1,0:T(8,128)(2,1)S(1)}, u32[]{:S(2)}, u32[]{:S(2)}) %collective-permute-start.9) | collective-permute-done | bytes 131104 | tf_op jit(solution)/shard_map/ppermute | solution.py:340
  39.5 2.5 %collective-permute-done.10.refs_2_ = bf16[128,512]{1,0:T(8,128)(2,1)S(1)} collective-permute-done((bf16[128,512]{1,0:T(8,128)(2,1)S(1)}, bf16[128,512]{1,0:T(8,128)(2,1)S(1)}, u32[]{:S(2)}, u32[]{:S(2)}) %collective-permute-start.10) | collective-permute-done | bytes 131104 | tf_op jit(solution)/shard_map/ppermute | solution.py:340
  41.9 0.1 collective-permute-done.11.refs_3_
  42.0 0.1 combine_plane.1
  42.1 0.6 %collective-permute-start.12 = (bf16[32,512]{1,0:T(8,128)(2,1)S(1)}, bf16[32,512]{1,0:T(8,128)(2,1)S(1)}, u32[]{:S(2)}, u32[]{:S(2)}) collective-permute-start(bf16[32,512]{1,0:T(8,128)(2,1)S(1)} %get-tuple-element.42), channel_id=1, source_target_pairs={{0,24},{1,25},{2,26},{3,27},{4,28},{5,29},{6,30},{7,31},{8,16},{9,... | collective-permute-start | bytes 98312 | tf_op jit(solution)/shard_map/ppermute | solution.py:340
  42.7 3.8 %collective-permute-start.14 = (bf16[32,512]{1,0:T(8,128)(2,1)S(1)}, bf16[32,512]{1,0:T(8,128)(2,1)S(1)}, u32[]{:S(2)}, u32[]{:S(2)}) collective-permute-start(bf16[32,512]{1,0:T(8,128)(2,1)S(1)} %get-tuple-element.44), channel_id=1, source_target_pairs={{0,8},{1,9},{2,10},{3,11},{4,12},{5,13},{6,14},{7,15},{8,0},{9,1},... | collective-permute-start | bytes 98312 | tf_op jit(solution)/shard_map/ppermute | solution.py:340
  46.5 1.4 %collective-permute-done.12.refs_1_ = bf16[32,512]{1,0:T(8,128)(2,1)S(1)} collective-permute-done((bf16[32,512]{1,0:T(8,128)(2,1)S(1)}, bf16[32,512]{1,0:T(8,128)(2,1)S(1)}, u32[]{:S(2)}, u32[]{:S(2)}) %collective-permute-start.12) | collective-permute-done | bytes 32800 | tf_op jit(solution)/shard_map/ppermute | solution.py:340
  47.9 0.5 %collective-permute-done.14.refs_3_ = bf16[32,512]{1,0:T(8,128)(2,1)S(1)} collective-permute-done((bf16[32,512]{1,0:T(8,128)(2,1)S(1)}, bf16[32,512]{1,0:T(8,128)(2,1)S(1)}, u32[]{:S(2)}, u32[]{:S(2)}) %collective-permute-start.14) | collective-permute-done | bytes 32800 | tf_op jit(solution)/shard_map/ppermute | solution.py:340
  48.5 0.9 %finish.1 = bf16[32,512]{1,0:T(8,128)(2,1)} custom-call(bf16[32,512]{1,0:T(8,128)(2,1)S(1)} %copy-done.3, f32[1,512]{1,0:T(1,128)S(1)} %bitcast.3, bf16[512,512]{1,0:T(8,128)(2,1)S(1)} %copy-done.1, f32[32,512]{1,0:T(8,128)S(1)} %get-tuple-element.41.refs_0_, bf16[32,512]{1,0:T(8,128)(2,1)S(1)} %collective-permute-done.12.refs_1_, ...), custom_call_target="tpu_custom_call" | custom-call | tf_op jit(solution)/shard_map/finish/pallas_call | solution.py:310
  (27 shorter events, 0.1 us)
Async XLA Ops:
  0.0 6.7 %collective-permute-start.2 = (bf16[32,512]{1,0:T(8,128)(2,1)}, bf16[32,512]{1,0:T(8,128)(2,1)S(1)}, u32[]{:S(2)}, u32[]{:S(2)}) collective-permute-start(bf16[32,512]{1,0:T(8,128)(2,1)} %feat.1), channel_id=1, source_target_pairs={{0,17},{1,16},{2,19},{3,18},{4,21},{5,20},{6,23},{7,22},{8,25},{9,... | collective-permute-start | bytes 98312 | tf_op jit(solution)/shard_map/ppermute | solution.py:340
  3.5 3.8 %collective-permute-start.1 = (bf16[32,512]{1,0:T(8,128)(2,1)}, bf16[32,512]{1,0:T(8,128)(2,1)S(1)}, u32[]{:S(2)}, u32[]{:S(2)}) collective-permute-start(bf16[32,512]{1,0:T(8,128)(2,1)} %feat.1), channel_id=1, source_target_pairs={{0,9},{1,8},{2,11},{3,10},{4,13},{5,12},{6,15},{7,14},{8,1},{9,0},... | collective-permute-start | bytes 98312 | tf_op jit(solution)/shard_map/ppermute | solution.py:340
  5.3 1.9 %collective-permute-start = (bf16[32,512]{1,0:T(8,128)(2,1)}, bf16[32,512]{1,0:T(8,128)(2,1)S(1)}, u32[]{:S(2)}, u32[]{:S(2)}) collective-permute-start(bf16[32,512]{1,0:T(8,128)(2,1)} %feat.1), channel_id=1, source_target_pairs={{0,1},{1,0},{2,3},{3,2},{4,5},{5,4},{6,7},{7,6},{8,9},{9,8},{10,11... | collective-permute-start | bytes 98312 | tf_op jit(solution)/shard_map/ppermute | solution.py:340
  5.3 5.3 %collective-permute-start.3 = (bf16[32,512]{1,0:T(8,128)(2,1)}, bf16[32,512]{1,0:T(8,128)(2,1)S(1)}, u32[]{:S(2)}, u32[]{:S(2)}) collective-permute-start(bf16[32,512]{1,0:T(8,128)(2,1)} %feat.1), channel_id=1, source_target_pairs={{0,25},{1,24},{2,27},{3,26},{4,29},{5,28},{6,31},{7,30},{8,17},{9,... | collective-permute-start | bytes 98312 | tf_op jit(solution)/shard_map/ppermute | solution.py:340
  5.3 0.7 %copy-start.4 = (s32[32,128]{1,0:T(8,128)S(1)}, s32[32,128]{1,0:T(8,128)}, u32[]{:S(2)}) copy-start(s32[32,128]{1,0:T(8,128)} %slots.1) | copy-start | bytes 49156
  6.1 0.7 %copy-start.5 = (s32[32]{0:T(128)S(1)}, s32[32]{0:T(128)}, u32[]{:S(2)}) copy-start(s32[32]{0:T(128)} %rel_ref.3) | copy-start | bytes 388
  10.7 17.7 %collective-permute-start.6 = (bf16[128,512]{1,0:T(8,128)(2,1)S(1)}, bf16[128,512]{1,0:T(8,128)(2,1)S(1)}, u32[]{:S(2)}, u32[]{:S(2)}) collective-permute-start(bf16[128,512]{1,0:T(8,128)(2,1)S(1)} %pad_maximum_fusion.refs_0_), channel_id=1, source_target_pairs={{0,6},{1,7},{2,4},{3,5},{4,2},{5,3},{6,0},{7,1},{8,14},{9,15},{10,... | collective-permute-start | bytes 393224 | tf_op jit(solution)/shard_map/ppermute | solution.py:340
  13.2 15.2 %collective-permute-start.5 = (bf16[128,512]{1,0:T(8,128)(2,1)S(1)}, bf16[128,512]{1,0:T(8,128)(2,1)S(1)}, u32[]{:S(2)}, u32[]{:S(2)}) collective-permute-start(bf16[128,512]{1,0:T(8,128)(2,1)S(1)} %pad_maximum_fusion.refs_0_), channel_id=1, source_target_pairs={{0,4},{1,5},{2,6},{3,7},{4,0},{5,1},{6,2},{7,3},{8,12},{9,13},{10,... | collective-permute-start | bytes 393224 | tf_op jit(solution)/shard_map/ppermute | solution.py:340
  13.7 14.7 %collective-permute-start.4 = (bf16[128,512]{1,0:T(8,128)(2,1)S(1)}, bf16[128,512]{1,0:T(8,128)(2,1)S(1)}, u32[]{:S(2)}, u32[]{:S(2)}) collective-permute-start(bf16[128,512]{1,0:T(8,128)(2,1)S(1)} %pad_maximum_fusion.refs_0_), channel_id=1, source_target_pairs={{0,2},{1,3},{2,0},{3,1},{4,6},{5,7},{6,4},{7,5},{8,10},{9,11},{10,... | collective-permute-start | bytes 393224 | tf_op jit(solution)/shard_map/ppermute | solution.py:340
  14.3 14.3 %copy-start = (bf16[512,512]{1,0:T(8,128)(2,1)S(1)}, bf16[512,512]{1,0:T(8,128)(2,1)}, u32[]{:S(2)}) copy-start(bf16[512,512]{1,0:T(8,128)(2,1)} %wq.3) | copy-start | bytes 1572868
  14.3 14.4 %copy-start.2 = (s32[32,128]{1,0:T(8,128)S(1)}, s32[32,128]{1,0:T(8,128)}, u32[]{:S(2)}) copy-start(s32[32,128]{1,0:T(8,128)} %merch_slot.3) | copy-start | bytes 49156
  14.3 14.4 %copy-start.6 = (s32[32]{0:T(128)S(1)}, s32[32]{0:T(128)}, u32[]{:S(2)}) copy-start(s32[32]{0:T(128)} %rel_ref.3) | copy-start | bytes 388
  14.3 14.4 %copy-start.8 = (s32[32]{0:T(128)S(1)}, s32[32]{0:T(128)}, u32[]{:S(2)}) copy-start(s32[32]{0:T(128)} %count_ref.3) | copy-start | bytes 388
  14.3 14.4 %copy-start.9 = (f32[4]{0:T(128)S(1)}, f32[4]{0:T(128)}, u32[]{:S(2)}) copy-start(f32[4]{0:T(128)} %bias_ref.3) | copy-start | bytes 52
  28.5 2.2 %collective-permute-start.7 = (bf16[512,512]{1,0:T(8,128)(2,1)S(1)}, bf16[512,512]{1,0:T(8,128)(2,1)S(1)}, u32[]{:S(2)}, u32[]{:S(2)}) collective-permute-start(bf16[512,512]{1,0:T(8,128)(2,1)S(1)} %assemble.1.feats), channel_id=1, source_target_pairs={{0,1},{1,0},{2,3},{3,2},{4,5},{5,4},{6,7},{7,6},{8,9},{9,8},{10,11... | collective-permute-start | bytes 1572872 | tf_op jit(solution)/shard_map/ppermute | solution.py:340
  30.2 2.1 %collective-permute-start.8 = (bf16[512,512]{1,0:T(8,128)(2,1)S(1)}, bf16[512,512]{1,0:T(8,128)(2,1)S(1)}, u32[]{:S(2)}, u32[]{:S(2)}) collective-permute-start(bf16[512,512]{1,0:T(8,128)(2,1)S(1)} %aggregate_odd.1), channel_id=1, source_target_pairs={{0,1},{1,0},{2,3},{3,2},{4,5},{5,4},{6,7},{7,6},{8,9},{9,8},{10,11... | collective-permute-start | bytes 1572872 | tf_op jit(solution)/shard_map/ppermute | solution.py:340
  32.3 16.2 %copy-start.1 = (bf16[512,512]{1,0:T(8,128)(2,1)S(1)}, bf16[512,512]{1,0:T(8,128)(2,1)}, u32[]{:S(2)}) copy-start(bf16[512,512]{1,0:T(8,128)(2,1)} %wo.1) | copy-start | bytes 1572868
  32.3 16.2 %copy-start.3 = (bf16[32,512]{1,0:T(8,128)(2,1)S(1)}, bf16[32,512]{1,0:T(8,128)(2,1)}, u32[]{:S(2)}) copy-start(bf16[32,512]{1,0:T(8,128)(2,1)} %feat.1) | copy-start | bytes 98308
  32.3 16.2 %copy-start.7 = (f32[512]{0:T(512)S(1)}, f32[512]{0:T(512)}, u32[]{:S(2)}) copy-start(f32[512]{0:T(512)} %param.19) | copy-start | bytes 6148
  32.4 7.0 %collective-permute-start.9 = (bf16[128,512]{1,0:T(8,128)(2,1)S(1)}, bf16[128,512]{1,0:T(8,128)(2,1)S(1)}, u32[]{:S(2)}, u32[]{:S(2)}) collective-permute-start(bf16[128,512]{1,0:T(8,128)(2,1)S(1)} %get-tuple-element.38), channel_id=1, source_target_pairs={{0,6},{1,7},{2,4},{3,5},{4,2},{5,3},{6,0},{7,1},{8,14},{9,15},{10,... | collective-permute-start | bytes 393224 | tf_op jit(solution)/shard_map/ppermute | solution.py:340
  34.9 7.0 %collective-permute-start.10 = (bf16[128,512]{1,0:T(8,128)(2,1)S(1)}, bf16[128,512]{1,0:T(8,128)(2,1)S(1)}, u32[]{:S(2)}, u32[]{:S(2)}) collective-permute-start(bf16[128,512]{1,0:T(8,128)(2,1)S(1)} %get-tuple-element.39), channel_id=1, source_target_pairs={{0,4},{1,5},{2,6},{3,7},{4,0},{5,1},{6,2},{7,3},{8,12},{9,13},{10,... | collective-permute-start | bytes 393224 | tf_op jit(solution)/shard_map/ppermute | solution.py:340
  35.4 6.6 %collective-permute-start.11 = (bf16[128,512]{1,0:T(8,128)(2,1)S(1)}, bf16[128,512]{1,0:T(8,128)(2,1)S(1)}, u32[]{:S(2)}, u32[]{:S(2)}) collective-permute-start(bf16[128,512]{1,0:T(8,128)(2,1)S(1)} %get-tuple-element.40), channel_id=1, source_target_pairs={{0,2},{1,3},{2,0},{3,1},{4,6},{5,7},{6,4},{7,5},{8,10},{9,11},{10,... | collective-permute-start | bytes 393224 | tf_op jit(solution)/shard_map/ppermute | solution.py:340
  42.1 5.8 %collective-permute-start.12 = (bf16[32,512]{1,0:T(8,128)(2,1)S(1)}, bf16[32,512]{1,0:T(8,128)(2,1)S(1)}, u32[]{:S(2)}, u32[]{:S(2)}) collective-permute-start(bf16[32,512]{1,0:T(8,128)(2,1)S(1)} %get-tuple-element.42), channel_id=1, source_target_pairs={{0,24},{1,25},{2,26},{3,27},{4,28},{5,29},{6,30},{7,31},{8,16},{9,... | collective-permute-start | bytes 98312 | tf_op jit(solution)/shard_map/ppermute | solution.py:340
  42.7 5.2 %collective-permute-start.13 = (bf16[32,512]{1,0:T(8,128)(2,1)S(1)}, bf16[32,512]{1,0:T(8,128)(2,1)S(1)}, u32[]{:S(2)}, u32[]{:S(2)}) collective-permute-start(bf16[32,512]{1,0:T(8,128)(2,1)S(1)} %get-tuple-element.43), channel_id=1, source_target_pairs={{0,16},{1,17},{2,18},{3,19},{4,20},{5,21},{6,22},{7,23},{8,24},{9,... | collective-permute-start | bytes 98312 | tf_op jit(solution)/shard_map/ppermute | solution.py:340
  42.7 5.7 %collective-permute-start.14 = (bf16[32,512]{1,0:T(8,128)(2,1)S(1)}, bf16[32,512]{1,0:T(8,128)(2,1)S(1)}, u32[]{:S(2)}, u32[]{:S(2)}) collective-permute-start(bf16[32,512]{1,0:T(8,128)(2,1)S(1)} %get-tuple-element.44), channel_id=1, source_target_pairs={{0,8},{1,9},{2,10},{3,11},{4,12},{5,13},{6,14},{7,15},{8,0},{9,1},... | collective-permute-start | bytes 98312 | tf_op jit(solution)/shard_map/ppermute | solution.py:340

commit v17 on v12

--- a/solution.py
+++ b/solution.py
@@ -221,35 +221,38 @@
     )(mine, other)
 
 
-def plane_kernel(outer, me_ref, *refs):
-    ins, out = refs[:-1], refs[-1]
-    rows = out.shape[0] // outer
-    for k in range(outer):
+def plane_kernel(inner, *refs):
+    ins, outs = refs[:inner], refs[inner:]
+    rows = outs[0].shape[0]
+    for k, out in enumerate(outs):
         part = slice(k * rows, (k + 1) * rows)
         total = ins[0][part, :]
         for other in ins[1:]:
             total = total + other[part, :].astype(F32)
-        place = jnp.bitwise_xor(me_ref[0] >> 3, k)
-        out[pl.ds(pl.multiple_of(place * rows, rows), rows), :] = total.astype(BF16)
-
-
-def combine_plane(outer, me, parts):
-    return pl.pallas_call(
-        functools.partial(plane_kernel, outer),
-        out_shape=jax.ShapeDtypeStruct(parts[0].shape, BF16),
-        in_specs=[SMEM] + [VMEM] * len(parts),
-        out_specs=VMEM,
+        out[...] = total.astype(out.dtype)
+
+
+def combine_plane(outer, parts):
+    rows, width = parts[0].shape
+    return pl.pallas_call(
+        functools.partial(plane_kernel, len(parts)),
+        out_shape=tuple(
+            jax.ShapeDtypeStruct((rows // outer, width), F32 if k == 0 else BF16)
+            for k in range(outer)
+        ),
+        in_specs=[VMEM] * len(parts),
+        out_specs=(VMEM,) * outer,
         compiler_params=_mb(2),
         cost_estimate=_cost(0, 2**20),
         name="combine_plane",
-    )(me, *parts)
-
-
-def finish_kernel(feat, gain, wo, parts, out):
-    merchants = feat.shape[0]
-    total = parts[:merchants, :].astype(F32)
-    for k in range(1, parts.shape[0] // merchants):
-        total = total + parts[k * merchants : (k + 1) * merchants, :].astype(F32)
+    )(*parts)
+
+
+def finish_kernel(feat, gain, wo, *refs):
+    out = refs[-1]
+    total = refs[0][...]
+    for part in refs[1:-1]:
+        total = total + part[...].astype(F32)
     update = feat[...].astype(F32) + jnp.dot(
         total.astype(BF16), wo[...], preferred_element_type=F32
     )
@@ -261,11 +264,11 @@
     return pl.pallas_call(
         finish_kernel,
         out_shape=jax.ShapeDtypeStruct(feat.shape, BF16),
-        in_specs=[VMEM] * 4,
+        in_specs=[VMEM] * (3 + len(parts)),
         out_specs=VMEM,
         compiler_params=_mb(2),
         name="finish",
-    )(feat, gain.reshape(1, -1), wo, parts)
+    )(feat, gain.reshape(1, -1), wo, *parts)
 
 
 def per_device(
@@ -322,12 +325,9 @@
     )
     (near,) = combine(1, 0, near, other, F32)
     parts = combine_plane(
-        outer, me, [near] + [swap(parts[j - 1], 2 * j) for j in reversed(range(1, inner))]
-    )
-    groups = [[base + 8 * k for k in range(outer)] for base in range(8)]
-    parts = lax.all_to_all(
-        parts, AXES, split_axis=0, concat_axis=0, tiled=True, axis_index_groups=groups
-    )
+        outer, [near] + [swap(parts[j - 1], 2 * j) for j in reversed(range(1, inner))]
+    )
+    parts = [parts[0]] + [swap(parts[k], 8 * k) for k in reversed(range(1, outer))]
     return finish(merch_feat, out_gain, out_weight, parts)
 
 

time: 50.9 us -> 48.7 us (0.957)
  blocking collectives: 10.6 us -> 0 us
  starting transfers between devices: 13.1 us -> 17.5 us
  waiting for transfers between devices: 4.35 us -> 8.39 us
    all_to_all x1 -> x0, blocking collectives: 10.6 us -> none  [per_device(): lax.all_to_all(parts, AXES, split_axis=0, concat_axis=0, tiled=True, axis...]
    ppermute x12 -> x15, starting transfers between devices: 13.1 us -> 17.5 us  [swap(): return lax.ppermute(value, AXES, [(s, s ^ mask) for s in range(devices)])]
    ppermute x12 -> x15, waiting for transfers between devices: 4.35 us -> 8.39 us  [swap(): return lax.ppermute(value, AXES, [(s, s ^ mask) for s in range(devices)])]
  transfers between devices with their start and end apart: 12 -> 15, of which waited for: 4 -> 6; matrix products, arithmetic and copies ran while one was open for 0% -> 0% of each run, Pallas kernels for 41% -> 42%
where the time goes in v17:
time: 48.7 us; the launch traced here: 48.5 us
  Pallas kernels  21.6 us (44%)
  starting transfers between devices  17.5 us (36%)
  waiting for transfers between devices  8.39 us (17%)
  local copies, waits for them, and re-layouts  0.77 us (2%)
    ppermute x15, starting transfers between devices, swap(): return lax.ppermute(value, AXES, [(s, s ^ mask) for s in range(devices)])  17.5 us
    pallas_call x1, Pallas kernels, gather(): pl.pallas_call(functools.partial(gather_kernel, outer), out_shape=(half,...  9.2 us
    ppermute x15, waiting for transfers between devices, swap(): return lax.ppermute(value, AXES, [(s, s ^ mask) for s in range(devices)])  8.39 us
    pallas_call x2, Pallas kernels, project(): pl.pallas_call(functools.partial(project_kernel, outer, spans), out_shape...  7.32 us
    pallas_call x3, Pallas kernels, aggregate(): pl.pallas_call(functools.partial(aggregate_kernel, outer, first, shift),...  3.97 us
  transfers between devices with their start and end apart: 15, of which 6 were waited for; matrix products, arithmetic and copies ran while one was open for 0% of the time, Pallas kernels for 42%

profile of v17, /device:TPU:0, one launch (start us, length us, event | category | flops | bytes accessed | tf_op | source)
XLA Modules:
  0.0 48.5 jit_solution(4431610284228985764)
XLA Ops:
  0.0 3.5 %collective-permute-start.2 = (bf16[32,512]{1,0:T(8,128)(2,1)}, bf16[32,512]{1,0:T(8,128)(2,1)S(1)}, u32[]{:S(2)}, u32[]{:S(2)}) collective-permute-start(bf16[32,512]{1,0:T(8,128)(2,1)} %feat.1), channel_id=1, source_target_pairs={{0,17},{1,16},{2,19},{3,18},{4,21},{5,20},{6,23},{7,22},{8,25},{9,... | collective-permute-start | bytes 98312 | tf_op jit(solution)/shard_map/ppermute | solution.py:294
  3.5 1.9 %collective-permute-start.1 = (bf16[32,512]{1,0:T(8,128)(2,1)}, bf16[32,512]{1,0:T(8,128)(2,1)S(1)}, u32[]{:S(2)}, u32[]{:S(2)}) collective-permute-start(bf16[32,512]{1,0:T(8,128)(2,1)} %feat.1), channel_id=1, source_target_pairs={{0,9},{1,8},{2,11},{3,10},{4,13},{5,12},{6,15},{7,14},{8,1},{9,0},... | collective-permute-start | bytes 98312 | tf_op jit(solution)/shard_map/ppermute | solution.py:294
  5.3 0.7 %copy-done.6 = s32[32,128]{1,0:T(8,128)S(1)} copy-done((s32[32,128]{1,0:T(8,128)S(1)}, s32[32,128]{1,0:T(8,128)}, u32[]{:S(2)}) %copy-start.6) | copy-done | bytes 16408
  6.1 9.2 %gather_slots.1 = (bf16[16,128,512]{2,1,0:T(8,128)(2,1)S(1)}, bf16[16,128,512]{2,1,0:T(8,128)(2,1)S(1)}) custom-call(s32[1]{0:T(128)} %bitcast.1.me_ref, s32[32,128]{1,0:T(8,128)S(1)} %copy-done.6, bf16[4096,512]{1,0:T(8,128)(2,1)} %acct_hbm.1), custom_call_target="tpu_custom_call" | custom-call | bytes 20971520 | tf_op jit(solution)/shard_map/gather_slots/pallas_call | solution.py:94
  15.3 2.8 %collective-permute-start.6 = (bf16[128,512]{1,0:T(8,128)(2,1)S(1)}, bf16[128,512]{1,0:T(8,128)(2,1)S(1)}, u32[]{:S(2)}, u32[]{:S(2)}) collective-permute-start(bf16[128,512]{1,0:T(8,128)(2,1)S(1)} %pad_maximum_fusion.1), channel_id=1, source_target_pairs={{0,6},{1,7},{2,4},{3,5},{4,2},{5,3},{6,0},{7,1},{8,14},{9,15},{10,... | collective-permute-start | bytes 393224 | tf_op jit(solution)/shard_map/ppermute | solution.py:294
  18.2 0.5 %collective-permute-start.5 = (bf16[128,512]{1,0:T(8,128)(2,1)S(1)}, bf16[128,512]{1,0:T(8,128)(2,1)S(1)}, u32[]{:S(2)}, u32[]{:S(2)}) collective-permute-start(bf16[128,512]{1,0:T(8,128)(2,1)S(1)} %pad_maximum_fusion.1), channel_id=1, source_target_pairs={{0,4},{1,5},{2,6},{3,7},{4,0},{5,1},{6,2},{7,3},{8,12},{9,13},{10,... | collective-permute-start | bytes 393224 | tf_op jit(solution)/shard_map/ppermute | solution.py:294
  18.7 0.2 collective-permute-start.4
  18.9 0.0 copy-start.4
  18.9 0.0 copy-start.8
  18.9 0.0 copy-start.9
  18.9 6.0 %project_slots.2 = (bf16[16,512,128]{2,1,0:T(8,128)(2,1)S(1)}, bf16[16,128,512]{2,1,0:T(8,128)(2,1)S(1)}, bf16[12,512,128]{2,1,0:T(8,128)(2,1)S(1)}, bf16[12,128,512]{2,1,0:T(8,128)(2,1)S(1)}) custom-call(s32[1]{0:T(128)} %bitcast.1.me_ref, s32[32]{0:T(128)S(1)} %copy-done.7, bf16[4,512,512]{2,1,0:T(8,128)(2,1)S(1)} %copy-done.1, ...), custom_call_target="tpu_custom_call" | custom-call | flops 3758096384 | bytes 14680064 | tf_op jit(solution)/shard_map/project_slots/pallas_call | solution.py:145
  25.0 0.1 collective-permute-done.5
  25.0 0.1 collective-permute-done.4
  25.1 0.1 collective-permute-start.7
  25.3 1.5 %aggregate_odd.1 = bf16[512,512]{1,0:T(8,128)(2,1)S(1)} custom-call(s32[1]{0:T(128)} %bitcast.1.me_ref, s32[32]{0:T(128)S(1)} %copy-done.7, s32[32]{0:T(128)S(1)} %copy-done.8, f32[4]{0:T(128)S(1)} %copy-done.9, s32[32,128]{1,0:T(8,128)S(1)} %copy-done.4, bf16[512,512]{1,0:T(8,128)(2,1)S(1)} %pad_maximum_fusion.feats, bf16[512,512]{1,0:T(8,128)(2,1)S(1)} %copy-done, ...), custom_call_target="tpu_custom_call" | custom-call | flops 402653184 | bytes 6291456 | tf_op jit(solution)/shard_map/aggregate_odd/pallas_call | solution.py:186
  26.8 0.5 %collective-permute-start.8 = (bf16[512,512]{1,0:T(8,128)(2,1)S(1)}, bf16[512,512]{1,0:T(8,128)(2,1)S(1)}, u32[]{:S(2)}, u32[]{:S(2)}) collective-permute-start(bf16[512,512]{1,0:T(8,128)(2,1)S(1)} %aggregate_odd.1), channel_id=1, source_target_pairs={{0,1},{1,0},{2,3},{3,2},{4,5},{5,4},{6,7},{7,6},{8,9},{9,8},{10,11... | collective-permute-start | bytes 1572872 | tf_op jit(solution)/shard_map/ppermute | solution.py:294
  27.3 1.3 %aggregate_even.2.mine = f32[384,512]{1,0:T(8,128)S(1)} custom-call(s32[1]{0:T(128)} %bitcast.1.me_ref, s32[32]{0:T(128)S(1)} %copy-done.7, s32[32]{0:T(128)S(1)} %copy-done.8, f32[4]{0:T(128)S(1)} %copy-done.9, s32[32,128]{1,0:T(8,128)S(1)} %copy-done.4, bf16[512,512]{1,0:T(8,128)(2,1)S(1)} %collective-permute-done.7.feats, bf16[512,512]{1,0:T(8,128)(2,1)S(1)} %copy-done, ...), custom_call_target="tpu_custom_call" | custom-call | flops 301989888 | bytes 6291456 | tf_op jit(solution)/shard_map/aggregate_even/pallas_call | solution.py:186
  28.7 0.2 collective-permute-done.8.other
  28.9 0.1 combine_cores.2
  29.0 1.8 %collective-permute-start.11 = (bf16[128,512]{1,0:T(8,128)(2,1)S(1)}, bf16[128,512]{1,0:T(8,128)(2,1)S(1)}, u32[]{:S(2)}, u32[]{:S(2)}) collective-permute-start(bf16[128,512]{1,0:T(8,128)(2,1)S(1)} %get-tuple-element.31), channel_id=1, source_target_pairs={{0,2},{1,3},{2,0},{3,1},{4,6},{5,7},{6,4},{7,5},{8,10},{9,11},{10,... | collective-permute-start | bytes 393224 | tf_op jit(solution)/shard_map/ppermute | solution.py:294
  30.7 1.5 %collective-permute-start.10 = (bf16[128,512]{1,0:T(8,128)(2,1)S(1)}, bf16[128,512]{1,0:T(8,128)(2,1)S(1)}, u32[]{:S(2)}, u32[]{:S(2)}) collective-permute-start(bf16[128,512]{1,0:T(8,128)(2,1)S(1)} %get-tuple-element.32), channel_id=1, source_target_pairs={{0,4},{1,5},{2,6},{3,7},{4,0},{5,1},{6,2},{7,3},{8,12},{9,13},{10,... | collective-permute-start | bytes 393224 | tf_op jit(solution)/shard_map/ppermute | solution.py:294
  32.3 0.3 collective-permute-start.9
  32.5 1.3 %project_slots.3 = (bf16[4,512,128]{2,1,0:T(8,128)(2,1)S(1)}, bf16[4,128,512]{2,1,0:T(8,128)(2,1)S(1)}) custom-call(s32[1]{0:T(128)} %bitcast.1.me_ref, s32[32]{0:T(128)S(1)} %copy-done.7, bf16[4,512,512]{2,1,0:T(8,128)(2,1)S(1)} %copy-done.1, bf16[4,512,512]{2,1,0:T(8,128)(2,1)S(1)} %copy-done.2, bf16[16,128,512]{2,1,0:T(8,128)(2,1)S(1)} %get-tuple-element.25.refs_1_.refs_0_), custom_call_target="tpu_custom_call" | custom-call | flops 536870912 | bytes 2097152 | tf_op jit(solution)/shard_map/project_slots/pallas_call | solution.py:145
  33.9 0.0 copy-start.10
  33.9 1.1 %aggregate_even.3.mine = f32[128,512]{1,0:T(8,128)S(1)} custom-call(s32[1]{0:T(128)} %bitcast.1.me_ref, s32[32]{0:T(128)S(1)} %copy-done.7, s32[32]{0:T(128)S(1)} %copy-done.8, f32[4]{0:T(128)S(1)} %copy-done.9, s32[32,128]{1,0:T(8,128)S(1)} %copy-done.4, bf16[512,512]{1,0:T(8,128)(2,1)S(1)} %collective-permute-done.7.feats, bf16[512,512]{1,0:T(8,128)(2,1)S(1)} %copy-done, ...), custom_call_target="tpu_custom_call" | custom-call | flops 100663296 | bytes 6291456 | tf_op jit(solution)/shard_map/aggregate_even/pallas_call | solution.py:186
  35.0 4.0 %collective-permute-done.10.refs_2_ = bf16[128,512]{1,0:T(8,128)(2,1)S(1)} collective-permute-done((bf16[128,512]{1,0:T(8,128)(2,1)S(1)}, bf16[128,512]{1,0:T(8,128)(2,1)S(1)}, u32[]{:S(2)}, u32[]{:S(2)}) %collective-permute-start.10) | collective-permute-done | bytes 131104 | tf_op jit(solution)/shard_map/ppermute | solution.py:294
  39.0 0.1 combine_plane.1
  39.1 3.7 %collective-permute-start.12 = (bf16[32,512]{1,0:T(8,128)(2,1)S(1)}, bf16[32,512]{1,0:T(8,128)(2,1)S(1)}, u32[]{:S(2)}, u32[]{:S(2)}) collective-permute-start(bf16[32,512]{1,0:T(8,128)(2,1)S(1)} %get-tuple-element.38), channel_id=1, source_target_pairs={{0,24},{1,25},{2,26},{3,27},{4,28},{5,29},{6,30},{7,31},{8,16},{9,... | collective-permute-start | bytes 98312 | tf_op jit(solution)/shard_map/ppermute | solution.py:294
  42.8 0.8 %collective-permute-start.14 = (bf16[32,512]{1,0:T(8,128)(2,1)S(1)}, bf16[32,512]{1,0:T(8,128)(2,1)S(1)}, u32[]{:S(2)}, u32[]{:S(2)}) collective-permute-start(bf16[32,512]{1,0:T(8,128)(2,1)S(1)} %get-tuple-element.40), channel_id=1, source_target_pairs={{0,8},{1,9},{2,10},{3,11},{4,12},{5,13},{6,14},{7,15},{8,0},{9,1},... | collective-permute-start | bytes 98312 | tf_op jit(solution)/shard_map/ppermute | solution.py:294
  43.6 1.4 %collective-permute-done.12.refs_1_ = bf16[32,512]{1,0:T(8,128)(2,1)S(1)} collective-permute-done((bf16[32,512]{1,0:T(8,128)(2,1)S(1)}, bf16[32,512]{1,0:T(8,128)(2,1)S(1)}, u32[]{:S(2)}, u32[]{:S(2)}) %collective-permute-start.12) | collective-permute-done | bytes 32800 | tf_op jit(solution)/shard_map/ppermute | solution.py:294
  44.9 2.7 %collective-permute-done.13.refs_2_ = bf16[32,512]{1,0:T(8,128)(2,1)S(1)} collective-permute-done((bf16[32,512]{1,0:T(8,128)(2,1)S(1)}, bf16[32,512]{1,0:T(8,128)(2,1)S(1)}, u32[]{:S(2)}, u32[]{:S(2)}) %collective-permute-start.13) | collective-permute-done | bytes 32800 | tf_op jit(solution)/shard_map/ppermute | solution.py:294
  47.6 0.9 %finish.1 = bf16[32,512]{1,0:T(8,128)(2,1)} custom-call(bf16[32,512]{1,0:T(8,128)(2,1)S(1)} %copy-done.5, f32[1,512]{1,0:T(1,128)S(1)} %bitcast.2, bf16[512,512]{1,0:T(8,128)(2,1)S(1)} %copy-done.3, f32[32,512]{1,0:T(8,128)S(1)} %get-tuple-element.37.refs_0_, bf16[32,512]{1,0:T(8,128)(2,1)S(1)} %collective-permute-done.12.refs_1_, ...), custom_call_target="tpu_custom_call" | custom-call | tf_op jit(solution)/shard_map/finish/pallas_call | solution.py:264
  (32 shorter events, 0.2 us)
Async XLA Ops:
  0.0 15.3 %collective-permute-start.2 = (bf16[32,512]{1,0:T(8,128)(2,1)}, bf16[32,512]{1,0:T(8,128)(2,1)S(1)}, u32[]{:S(2)}, u32[]{:S(2)}) collective-permute-start(bf16[32,512]{1,0:T(8,128)(2,1)} %feat.1), channel_id=1, source_target_pairs={{0,17},{1,16},{2,19},{3,18},{4,21},{5,20},{6,23},{7,22},{8,25},{9,... | collective-permute-start | bytes 98312 | tf_op jit(solution)/shard_map/ppermute | solution.py:294
  3.5 11.8 %collective-permute-start.1 = (bf16[32,512]{1,0:T(8,128)(2,1)}, bf16[32,512]{1,0:T(8,128)(2,1)S(1)}, u32[]{:S(2)}, u32[]{:S(2)}) collective-permute-start(bf16[32,512]{1,0:T(8,128)(2,1)} %feat.1), channel_id=1, source_target_pairs={{0,9},{1,8},{2,11},{3,10},{4,13},{5,12},{6,15},{7,14},{8,1},{9,0},... | collective-permute-start | bytes 98312 | tf_op jit(solution)/shard_map/ppermute | solution.py:294
  5.3 10.0 %collective-permute-start = (bf16[32,512]{1,0:T(8,128)(2,1)}, bf16[32,512]{1,0:T(8,128)(2,1)S(1)}, u32[]{:S(2)}, u32[]{:S(2)}) collective-permute-start(bf16[32,512]{1,0:T(8,128)(2,1)} %feat.1), channel_id=1, source_target_pairs={{0,1},{1,0},{2,3},{3,2},{4,5},{5,4},{6,7},{7,6},{8,9},{9,8},{10,11... | collective-permute-start | bytes 98312 | tf_op jit(solution)/shard_map/ppermute | solution.py:294
  5.3 10.0 %collective-permute-start.3 = (bf16[32,512]{1,0:T(8,128)(2,1)}, bf16[32,512]{1,0:T(8,128)(2,1)S(1)}, u32[]{:S(2)}, u32[]{:S(2)}) collective-permute-start(bf16[32,512]{1,0:T(8,128)(2,1)} %feat.1), channel_id=1, source_target_pairs={{0,25},{1,24},{2,27},{3,26},{4,29},{5,28},{6,31},{7,30},{8,17},{9,... | collective-permute-start | bytes 98312 | tf_op jit(solution)/shard_map/ppermute | solution.py:294
  5.3 0.7 %copy-start.6 = (s32[32,128]{1,0:T(8,128)S(1)}, s32[32,128]{1,0:T(8,128)}, u32[]{:S(2)}) copy-start(s32[32,128]{1,0:T(8,128)} %slots_ref.1) | copy-start | bytes 49156
  6.1 12.8 %copy-start.1 = (bf16[4,512,512]{2,1,0:T(8,128)(2,1)S(1)}, bf16[4,512,512]{2,1,0:T(8,128)(2,1)}, u32[]{:S(2)}) copy-start(bf16[4,512,512]{2,1,0:T(8,128)(2,1)} %kw.3) | copy-start | bytes 6291460
  6.1 12.8 %copy-start.2 = (bf16[4,512,512]{2,1,0:T(8,128)(2,1)S(1)}, bf16[4,512,512]{2,1,0:T(8,128)(2,1)}, u32[]{:S(2)}) copy-start(bf16[4,512,512]{2,1,0:T(8,128)(2,1)} %mw.3) | copy-start | bytes 6291460
  6.1 12.8 %copy-start.7 = (s32[32]{0:T(128)S(1)}, s32[32]{0:T(128)}, u32[]{:S(2)}) copy-start(s32[32]{0:T(128)} %rel_ref.9) | copy-start | bytes 388
  15.3 9.6 %collective-permute-start.6 = (bf16[128,512]{1,0:T(8,128)(2,1)S(1)}, bf16[128,512]{1,0:T(8,128)(2,1)S(1)}, u32[]{:S(2)}, u32[]{:S(2)}) collective-permute-start(bf16[128,512]{1,0:T(8,128)(2,1)S(1)} %pad_maximum_fusion.1), channel_id=1, source_target_pairs={{0,6},{1,7},{2,4},{3,5},{4,2},{5,3},{6,0},{7,1},{8,14},{9,15},{10,... | collective-permute-start | bytes 393224 | tf_op jit(solution)/shard_map/ppermute | solution.py:294
  18.2 6.8 %collective-permute-start.5 = (bf16[128,512]{1,0:T(8,128)(2,1)S(1)}, bf16[128,512]{1,0:T(8,128)(2,1)S(1)}, u32[]{:S(2)}, u32[]{:S(2)}) collective-permute-start(bf16[128,512]{1,0:T(8,128)(2,1)S(1)} %pad_maximum_fusion.1), channel_id=1, source_target_pairs={{0,4},{1,5},{2,6},{3,7},{4,0},{5,1},{6,2},{7,3},{8,12},{9,13},{10,... | collective-permute-start | bytes 393224 | tf_op jit(solution)/shard_map/ppermute | solution.py:294
  18.7 6.4 %collective-permute-start.4 = (bf16[128,512]{1,0:T(8,128)(2,1)S(1)}, bf16[128,512]{1,0:T(8,128)(2,1)S(1)}, u32[]{:S(2)}, u32[]{:S(2)}) collective-permute-start(bf16[128,512]{1,0:T(8,128)(2,1)S(1)} %pad_maximum_fusion.1), channel_id=1, source_target_pairs={{0,2},{1,3},{2,0},{3,1},{4,6},{5,7},{6,4},{7,5},{8,10},{9,11},{10,... | collective-permute-start | bytes 393224 | tf_op jit(solution)/shard_map/ppermute | solution.py:294
  18.9 6.3 %copy-start = (bf16[512,512]{1,0:T(8,128)(2,1)S(1)}, bf16[512,512]{1,0:T(8,128)(2,1)}, u32[]{:S(2)}) copy-start(bf16[512,512]{1,0:T(8,128)(2,1)} %wq.5) | copy-start | bytes 1572868
  18.9 6.3 %copy-start.4 = (s32[32,128]{1,0:T(8,128)S(1)}, s32[32,128]{1,0:T(8,128)}, u32[]{:S(2)}) copy-start(s32[32,128]{1,0:T(8,128)} %merch_slot.5) | copy-start | bytes 49156
  18.9 6.3 %copy-start.8 = (s32[32]{0:T(128)S(1)}, s32[32]{0:T(128)}, u32[]{:S(2)}) copy-start(s32[32]{0:T(128)} %count_ref.5) | copy-start | bytes 388
  18.9 6.3 %copy-start.9 = (f32[4]{0:T(128)S(1)}, f32[4]{0:T(128)}, u32[]{:S(2)}) copy-start(f32[4]{0:T(128)} %bias_ref.5) | copy-start | bytes 52
  25.1 2.2 %collective-permute-start.7 = (bf16[512,512]{1,0:T(8,128)(2,1)S(1)}, bf16[512,512]{1,0:T(8,128)(2,1)S(1)}, u32[]{:S(2)}, u32[]{:S(2)}) collective-permute-start(bf16[512,512]{1,0:T(8,128)(2,1)S(1)} %pad_maximum_fusion.feats), channel_id=1, source_target_pairs={{0,1},{1,0},{2,3},{3,2},{4,5},{5,4},{6,7},{7,6},{8,9},{9,8},{10,11... | collective-permute-start | bytes 1572872 | tf_op jit(solution)/shard_map/ppermute | solution.py:294
  26.8 2.1 %collective-permute-start.8 = (bf16[512,512]{1,0:T(8,128)(2,1)S(1)}, bf16[512,512]{1,0:T(8,128)(2,1)S(1)}, u32[]{:S(2)}, u32[]{:S(2)}) collective-permute-start(bf16[512,512]{1,0:T(8,128)(2,1)S(1)} %aggregate_odd.1), channel_id=1, source_target_pairs={{0,1},{1,0},{2,3},{3,2},{4,5},{5,4},{6,7},{7,6},{8,9},{9,8},{10,11... | collective-permute-start | bytes 1572872 | tf_op jit(solution)/shard_map/ppermute | solution.py:294
  29.0 6.1 %collective-permute-start.11 = (bf16[128,512]{1,0:T(8,128)(2,1)S(1)}, bf16[128,512]{1,0:T(8,128)(2,1)S(1)}, u32[]{:S(2)}, u32[]{:S(2)}) collective-permute-start(bf16[128,512]{1,0:T(8,128)(2,1)S(1)} %get-tuple-element.31), channel_id=1, source_target_pairs={{0,2},{1,3},{2,0},{3,1},{4,6},{5,7},{6,4},{7,5},{8,10},{9,11},{10,... | collective-permute-start | bytes 393224 | tf_op jit(solution)/shard_map/ppermute | solution.py:294
  30.7 8.3 %collective-permute-start.10 = (bf16[128,512]{1,0:T(8,128)(2,1)S(1)}, bf16[128,512]{1,0:T(8,128)(2,1)S(1)}, u32[]{:S(2)}, u32[]{:S(2)}) collective-permute-start(bf16[128,512]{1,0:T(8,128)(2,1)S(1)} %get-tuple-element.32), channel_id=1, source_target_pairs={{0,4},{1,5},{2,6},{3,7},{4,0},{5,1},{6,2},{7,3},{8,12},{9,13},{10,... | collective-permute-start | bytes 393224 | tf_op jit(solution)/shard_map/ppermute | solution.py:294
  32.3 6.8 %collective-permute-start.9 = (bf16[128,512]{1,0:T(8,128)(2,1)S(1)}, bf16[128,512]{1,0:T(8,128)(2,1)S(1)}, u32[]{:S(2)}, u32[]{:S(2)}) collective-permute-start(bf16[128,512]{1,0:T(8,128)(2,1)S(1)} %get-tuple-element.33), channel_id=1, source_target_pairs={{0,6},{1,7},{2,4},{3,5},{4,2},{5,3},{6,0},{7,1},{8,14},{9,15},{10,... | collective-permute-start | bytes 393224 | tf_op jit(solution)/shard_map/ppermute | solution.py:294
  33.9 13.7 %copy-start.3 = (bf16[512,512]{1,0:T(8,128)(2,1)S(1)}, bf16[512,512]{1,0:T(8,128)(2,1)}, u32[]{:S(2)}) copy-start(bf16[512,512]{1,0:T(8,128)(2,1)} %wo.1) | copy-start | bytes 1572868
  33.9 13.7 %copy-start.5 = (bf16[32,512]{1,0:T(8,128)(2,1)S(1)}, bf16[32,512]{1,0:T(8,128)(2,1)}, u32[]{:S(2)}) copy-start(bf16[32,512]{1,0:T(8,128)(2,1)} %feat.1) | copy-start | bytes 98308
  33.9 13.7 %copy-start.10 = (f32[512]{0:T(512)S(1)}, f32[512]{0:T(512)}, u32[]{:S(2)}) copy-start(f32[512]{0:T(512)} %param.19) | copy-start | bytes 6148
  39.1 5.8 %collective-permute-start.12 = (bf16[32,512]{1,0:T(8,128)(2,1)S(1)}, bf16[32,512]{1,0:T(8,128)(2,1)S(1)}, u32[]{:S(2)}, u32[]{:S(2)}) collective-permute-start(bf16[32,512]{1,0:T(8,128)(2,1)S(1)} %get-tuple-element.38), channel_id=1, source_target_pairs={{0,24},{1,25},{2,26},{3,27},{4,28},{5,29},{6,30},{7,31},{8,16},{9,... | collective-permute-start | bytes 98312 | tf_op jit(solution)/shard_map/ppermute | solution.py:294
  42.8 4.8 %collective-permute-start.13 = (bf16[32,512]{1,0:T(8,128)(2,1)S(1)}, bf16[32,512]{1,0:T(8,128)(2,1)S(1)}, u32[]{:S(2)}, u32[]{:S(2)}) collective-permute-start(bf16[32,512]{1,0:T(8,128)(2,1)S(1)} %get-tuple-element.39), channel_id=1, source_target_pairs={{0,16},{1,17},{2,18},{3,19},{4,20},{5,21},{6,22},{7,23},{8,24},{9,... | collective-permute-start | bytes 98312 | tf_op jit(solution)/shard_map/ppermute | solution.py:294
  42.8 4.8 %collective-permute-start.14 = (bf16[32,512]{1,0:T(8,128)(2,1)S(1)}, bf16[32,512]{1,0:T(8,128)(2,1)S(1)}, u32[]{:S(2)}, u32[]{:S(2)}) collective-permute-start(bf16[32,512]{1,0:T(8,128)(2,1)S(1)} %get-tuple-element.40), channel_id=1, source_target_pairs={{0,8},{1,9},{2,10},{3,11},{4,12},{5,13},{6,14},{7,15},{8,0},{9,1},... | collective-permute-start | bytes 98312 | tf_op jit(solution)/shard_map/ppermute | solution.py:294

commit v18 on v17

--- a/solution.py
+++ b/solution.py
@@ -155,29 +155,52 @@
 
 def aggregate_kernel(
     outer, first, shift, me_ref, rel_ref, count_ref, bias_ref, merch_slot, feats, wq, keys, values,
-    sums, query, gates,
+    sums,
 ):
     blocks, width, block_len = keys.shape
     merchants = sums.shape[0] // blocks
     me = me_ref[0]
     row = lax.broadcasted_iota(jnp.int32, (merchants, block_len), 0)
     lane = lax.broadcasted_iota(jnp.int32, (merchants, block_len), 1)
-    query[...] = jnp.dot(
-        feats[first * merchants : (first + blocks) * merchants, :],
-        wq[...],
-        preferred_element_type=F32,
-    ).astype(BF16)
-    parts = [slice(i * merchants, (i + 1) * merchants) for i in range(blocks)]
-    for i in range(blocks):
-        block = jnp.bitwise_xor(me, _offset(first + i, outer) + shift)
-        score = jnp.dot(query[parts[i], :], keys[i], preferred_element_type=F32) / math.sqrt(width)
-        score = score + bias_ref[rel_ref[block]]
-        mine = (merch_slot[pl.ds(block, 1), :] == row) & (lane < count_ref[block])
-        gates[parts[i], :] = jnp.where(mine, jax.nn.sigmoid(score), 0.0).astype(BF16)
-    for i in range(blocks):
-        sums[parts[i], :] = jnp.dot(
-            gates[parts[i], :], values[i], preferred_element_type=F32
-        ).astype(sums.dtype)
+    size = 4
+    groups = blocks // size
+
+    def project(g):
+        start = (first + g * size) * merchants
+        return jnp.dot(
+            feats[start : start + size * merchants, :], wq[...], preferred_element_type=F32
+        ).astype(BF16)
+
+    def gate(g, query):
+        gates = []
+        for u in range(size):
+            i = g * size + u
+            block = jnp.bitwise_xor(me, _offset(first + i, outer) + shift)
+            score = jnp.dot(
+                query[u * merchants : (u + 1) * merchants, :],
+                keys[i],
+                preferred_element_type=F32,
+            ) / math.sqrt(width)
+            score = score + bias_ref[rel_ref[block]]
+            mine = (merch_slot[pl.ds(block, 1), :] == row) & (lane < count_ref[block])
+            gates.append(jnp.where(mine, jax.nn.sigmoid(score), 0.0).astype(BF16))
+        return gates
+
+    def add(g, gates):
+        for u in range(size):
+            i = g * size + u
+            sums[i * merchants : (i + 1) * merchants, :] = jnp.dot(
+                gates[u], values[i], preferred_element_type=F32
+            ).astype(sums.dtype)
+
+    queries, gates = {}, {}
+    for g in range(groups + 2):
+        if g < groups:
+            queries[g] = project(g)
+        if 0 <= g - 1 < groups:
+            gates[g - 1] = gate(g - 1, queries.pop(g - 1))
+        if g >= 2:
+            add(g - 2, gates.pop(g - 2))
 
 
 def aggregate(outer, first, shift, me, rel, count, bias, merch_slot, feats, wq, keys, values, dtype):
@@ -188,10 +211,6 @@
         out_shape=jax.ShapeDtypeStruct((rows, width), dtype),
         in_specs=[SMEM] * 4 + [VMEM] * 5,
         out_specs=VMEM,
-        scratch_shapes=[
-            pltpu.VMEM((rows, width), BF16),
-            pltpu.VMEM((rows, block_len), BF16),
-        ],
         compiler_params=_mb(6),
         cost_estimate=_cost(
             4 * rows * block_len * width + 2 * rows * width * width, 6 * 2**20, rows * block_len

time: 48.7 us -> 48.9 us (level)
  no operation moved by 1% of the time
where the time goes in v18:
time: 48.9 us; the launch traced here: 48.6 us
  Pallas kernels  21.7 us (44%)
  starting transfers between devices  17.5 us (36%)
  waiting for transfers between devices  8.37 us (17%)
  local copies, waits for them, and re-layouts  0.77 us (2%)
    ppermute x15, starting transfers between devices, swap(): return lax.ppermute(value, AXES, [(s, s ^ mask) for s in range(devices)])  17.5 us
    pallas_call x1, Pallas kernels, gather(): pl.pallas_call(functools.partial(gather_kernel, outer), out_shape=(half,...  9.2 us
    ppermute x15, waiting for transfers between devices, swap(): return lax.ppermute(value, AXES, [(s, s ^ mask) for s in range(devices)])  8.37 us
    pallas_call x2, Pallas kernels, project(): pl.pallas_call(functools.partial(project_kernel, outer, spans), out_shape...  7.32 us
    pallas_call x3, Pallas kernels, aggregate(): pl.pallas_call(functools.partial(aggregate_kernel, outer, first, shift),...  4.1 us
  transfers between devices with their start and end apart: 15, of which 6 were waited for; matrix products, arithmetic and copies ran while one was open for 0% of the time, Pallas kernels for 42%

profile of v18, /device:TPU:0, one launch (start us, length us, event | category | flops | bytes accessed | tf_op | source)
XLA Modules:
  0.0 48.6 jit_solution(10123805349575019695)
XLA Ops:
  0.0 3.5 %collective-permute-start.2 = (bf16[32,512]{1,0:T(8,128)(2,1)}, bf16[32,512]{1,0:T(8,128)(2,1)S(1)}, u32[]{:S(2)}, u32[]{:S(2)}) collective-permute-start(bf16[32,512]{1,0:T(8,128)(2,1)} %feat.1), channel_id=1, source_target_pairs={{0,17},{1,16},{2,19},{3,18},{4,21},{5,20},{6,23},{7,22},{8,25},{9,... | collective-permute-start | bytes 98312 | tf_op jit(solution)/shard_map/ppermute | solution.py:313
  3.5 1.9 %collective-permute-start.1 = (bf16[32,512]{1,0:T(8,128)(2,1)}, bf16[32,512]{1,0:T(8,128)(2,1)S(1)}, u32[]{:S(2)}, u32[]{:S(2)}) collective-permute-start(bf16[32,512]{1,0:T(8,128)(2,1)} %feat.1), channel_id=1, source_target_pairs={{0,9},{1,8},{2,11},{3,10},{4,13},{5,12},{6,15},{7,14},{8,1},{9,0},... | collective-permute-start | bytes 98312 | tf_op jit(solution)/shard_map/ppermute | solution.py:313
  5.3 0.7 %copy-done.6 = s32[32,128]{1,0:T(8,128)S(1)} copy-done((s32[32,128]{1,0:T(8,128)S(1)}, s32[32,128]{1,0:T(8,128)}, u32[]{:S(2)}) %copy-start.6) | copy-done | bytes 16408
  6.1 9.2 %gather_slots.1 = (bf16[16,128,512]{2,1,0:T(8,128)(2,1)S(1)}, bf16[16,128,512]{2,1,0:T(8,128)(2,1)S(1)}) custom-call(s32[1]{0:T(128)} %bitcast.1.me_ref, s32[32,128]{1,0:T(8,128)S(1)} %copy-done.6, bf16[4096,512]{1,0:T(8,128)(2,1)} %acct_hbm.1), custom_call_target="tpu_custom_call" | custom-call | bytes 20971520 | tf_op jit(solution)/shard_map/gather_slots/pallas_call | solution.py:94
  15.3 2.8 %collective-permute-start.6 = (bf16[128,512]{1,0:T(8,128)(2,1)S(1)}, bf16[128,512]{1,0:T(8,128)(2,1)S(1)}, u32[]{:S(2)}, u32[]{:S(2)}) collective-permute-start(bf16[128,512]{1,0:T(8,128)(2,1)S(1)} %pad_maximum_fusion.1), channel_id=1, source_target_pairs={{0,6},{1,7},{2,4},{3,5},{4,2},{5,3},{6,0},{7,1},{8,14},{9,15},{10,... | collective-permute-start | bytes 393224 | tf_op jit(solution)/shard_map/ppermute | solution.py:313
  18.2 0.5 %collective-permute-start.5 = (bf16[128,512]{1,0:T(8,128)(2,1)S(1)}, bf16[128,512]{1,0:T(8,128)(2,1)S(1)}, u32[]{:S(2)}, u32[]{:S(2)}) collective-permute-start(bf16[128,512]{1,0:T(8,128)(2,1)S(1)} %pad_maximum_fusion.1), channel_id=1, source_target_pairs={{0,4},{1,5},{2,6},{3,7},{4,0},{5,1},{6,2},{7,3},{8,12},{9,13},{10,... | collective-permute-start | bytes 393224 | tf_op jit(solution)/shard_map/ppermute | solution.py:313
  18.7 0.2 collective-permute-start.4
  18.9 0.0 copy-start.4
  18.9 0.0 copy-start.8
  18.9 0.0 copy-start.9
  18.9 6.0 %project_slots.2 = (bf16[16,512,128]{2,1,0:T(8,128)(2,1)S(1)}, bf16[16,128,512]{2,1,0:T(8,128)(2,1)S(1)}, bf16[12,512,128]{2,1,0:T(8,128)(2,1)S(1)}, bf16[12,128,512]{2,1,0:T(8,128)(2,1)S(1)}) custom-call(s32[1]{0:T(128)} %bitcast.1.me_ref, s32[32]{0:T(128)S(1)} %copy-done.7, bf16[4,512,512]{2,1,0:T(8,128)(2,1)S(1)} %copy-done.1, ...), custom_call_target="tpu_custom_call" | custom-call | flops 3758096384 | bytes 14680064 | tf_op jit(solution)/shard_map/project_slots/pallas_call | solution.py:145
  25.0 0.1 collective-permute-done.5
  25.0 0.1 collective-permute-done.4
  25.1 0.1 collective-permute-start.7
  25.3 1.6 %aggregate_odd.1 = bf16[512,512]{1,0:T(8,128)(2,1)S(1)} custom-call(s32[1]{0:T(128)} %bitcast.1.me_ref, s32[32]{0:T(128)S(1)} %copy-done.7, s32[32]{0:T(128)S(1)} %copy-done.8, f32[4]{0:T(128)S(1)} %copy-done.9, s32[32,128]{1,0:T(8,128)S(1)} %copy-done.4, bf16[512,512]{1,0:T(8,128)(2,1)S(1)} %pad_maximum_fusion.feats, bf16[512,512]{1,0:T(8,128)(2,1)S(1)} %copy-done, ...), custom_call_target="tpu_custom_call" | custom-call | flops 402653184 | bytes 6291456 | tf_op jit(solution)/shard_map/aggregate_odd/pallas_call | solution.py:209
  26.9 0.5 %collective-permute-start.8 = (bf16[512,512]{1,0:T(8,128)(2,1)S(1)}, bf16[512,512]{1,0:T(8,128)(2,1)S(1)}, u32[]{:S(2)}, u32[]{:S(2)}) collective-permute-start(bf16[512,512]{1,0:T(8,128)(2,1)S(1)} %aggregate_odd.1), channel_id=1, source_target_pairs={{0,1},{1,0},{2,3},{3,2},{4,5},{5,4},{6,7},{7,6},{8,9},{9,8},{10,11... | collective-permute-start | bytes 1572872 | tf_op jit(solution)/shard_map/ppermute | solution.py:313
  27.4 1.4 %aggregate_even.2.mine = f32[384,512]{1,0:T(8,128)S(1)} custom-call(s32[1]{0:T(128)} %bitcast.1.me_ref, s32[32]{0:T(128)S(1)} %copy-done.7, s32[32]{0:T(128)S(1)} %copy-done.8, f32[4]{0:T(128)S(1)} %copy-done.9, s32[32,128]{1,0:T(8,128)S(1)} %copy-done.4, bf16[512,512]{1,0:T(8,128)(2,1)S(1)} %collective-permute-done.7.feats, bf16[512,512]{1,0:T(8,128)(2,1)S(1)} %copy-done, ...), custom_call_target="tpu_custom_call" | custom-call | flops 301989888 | bytes 6291456 | tf_op jit(solution)/shard_map/aggregate_even/pallas_call | solution.py:209
  28.8 0.1 collective-permute-done.8.other
  29.0 0.1 combine_cores.2
  29.1 1.8 %collective-permute-start.11 = (bf16[128,512]{1,0:T(8,128)(2,1)S(1)}, bf16[128,512]{1,0:T(8,128)(2,1)S(1)}, u32[]{:S(2)}, u32[]{:S(2)}) collective-permute-start(bf16[128,512]{1,0:T(8,128)(2,1)S(1)} %get-tuple-element.31), channel_id=1, source_target_pairs={{0,2},{1,3},{2,0},{3,1},{4,6},{5,7},{6,4},{7,5},{8,10},{9,11},{10,... | collective-permute-start | bytes 393224 | tf_op jit(solution)/shard_map/ppermute | solution.py:313
  30.9 1.5 %collective-permute-start.10 = (bf16[128,512]{1,0:T(8,128)(2,1)S(1)}, bf16[128,512]{1,0:T(8,128)(2,1)S(1)}, u32[]{:S(2)}, u32[]{:S(2)}) collective-permute-start(bf16[128,512]{1,0:T(8,128)(2,1)S(1)} %get-tuple-element.32), channel_id=1, source_target_pairs={{0,4},{1,5},{2,6},{3,7},{4,0},{5,1},{6,2},{7,3},{8,12},{9,13},{10,... | collective-permute-start | bytes 393224 | tf_op jit(solution)/shard_map/ppermute | solution.py:313
  32.4 0.3 collective-permute-start.9
  32.6 1.3 %project_slots.3 = (bf16[4,512,128]{2,1,0:T(8,128)(2,1)S(1)}, bf16[4,128,512]{2,1,0:T(8,128)(2,1)S(1)}) custom-call(s32[1]{0:T(128)} %bitcast.1.me_ref, s32[32]{0:T(128)S(1)} %copy-done.7, bf16[4,512,512]{2,1,0:T(8,128)(2,1)S(1)} %copy-done.1, bf16[4,512,512]{2,1,0:T(8,128)(2,1)S(1)} %copy-done.2, bf16[16,128,512]{2,1,0:T(8,128)(2,1)S(1)} %get-tuple-element.25.refs_1_.refs_0_), custom_call_target="tpu_custom_call" | custom-call | flops 536870912 | bytes 2097152 | tf_op jit(solution)/shard_map/project_slots/pallas_call | solution.py:145
  34.0 0.0 copy-start.3
  34.0 1.1 %aggregate_even.3.mine = f32[128,512]{1,0:T(8,128)S(1)} custom-call(s32[1]{0:T(128)} %bitcast.1.me_ref, s32[32]{0:T(128)S(1)} %copy-done.7, s32[32]{0:T(128)S(1)} %copy-done.8, f32[4]{0:T(128)S(1)} %copy-done.9, s32[32,128]{1,0:T(8,128)S(1)} %copy-done.4, bf16[512,512]{1,0:T(8,128)(2,1)S(1)} %collective-permute-done.7.feats, bf16[512,512]{1,0:T(8,128)(2,1)S(1)} %copy-done, ...), custom_call_target="tpu_custom_call" | custom-call | flops 100663296 | bytes 6291456 | tf_op jit(solution)/shard_map/aggregate_even/pallas_call | solution.py:209
  35.1 4.0 %collective-permute-done.10.refs_2_ = bf16[128,512]{1,0:T(8,128)(2,1)S(1)} collective-permute-done((bf16[128,512]{1,0:T(8,128)(2,1)S(1)}, bf16[128,512]{1,0:T(8,128)(2,1)S(1)}, u32[]{:S(2)}, u32[]{:S(2)}) %collective-permute-start.10) | collective-permute-done | bytes 131104 | tf_op jit(solution)/shard_map/ppermute | solution.py:313
  39.2 0.1 combine_plane.1
  39.2 3.7 %collective-permute-start.12 = (bf16[32,512]{1,0:T(8,128)(2,1)S(1)}, bf16[32,512]{1,0:T(8,128)(2,1)S(1)}, u32[]{:S(2)}, u32[]{:S(2)}) collective-permute-start(bf16[32,512]{1,0:T(8,128)(2,1)S(1)} %get-tuple-element.38), channel_id=1, source_target_pairs={{0,24},{1,25},{2,26},{3,27},{4,28},{5,29},{6,30},{7,31},{8,16},{9,... | collective-permute-start | bytes 98312 | tf_op jit(solution)/shard_map/ppermute | solution.py:313
  42.9 0.8 %collective-permute-start.14 = (bf16[32,512]{1,0:T(8,128)(2,1)S(1)}, bf16[32,512]{1,0:T(8,128)(2,1)S(1)}, u32[]{:S(2)}, u32[]{:S(2)}) collective-permute-start(bf16[32,512]{1,0:T(8,128)(2,1)S(1)} %get-tuple-element.40), channel_id=1, source_target_pairs={{0,8},{1,9},{2,10},{3,11},{4,12},{5,13},{6,14},{7,15},{8,0},{9,1},... | collective-permute-start | bytes 98312 | tf_op jit(solution)/shard_map/ppermute | solution.py:313
  43.7 1.4 %collective-permute-done.12.refs_1_ = bf16[32,512]{1,0:T(8,128)(2,1)S(1)} collective-permute-done((bf16[32,512]{1,0:T(8,128)(2,1)S(1)}, bf16[32,512]{1,0:T(8,128)(2,1)S(1)}, u32[]{:S(2)}, u32[]{:S(2)}) %collective-permute-start.12) | collective-permute-done | bytes 32800 | tf_op jit(solution)/shard_map/ppermute | solution.py:313
  45.0 2.7 %collective-permute-done.13.refs_2_ = bf16[32,512]{1,0:T(8,128)(2,1)S(1)} collective-permute-done((bf16[32,512]{1,0:T(8,128)(2,1)S(1)}, bf16[32,512]{1,0:T(8,128)(2,1)S(1)}, u32[]{:S(2)}, u32[]{:S(2)}) %collective-permute-start.13) | collective-permute-done | bytes 32800 | tf_op jit(solution)/shard_map/ppermute | solution.py:313
  47.7 0.9 %finish.1 = bf16[32,512]{1,0:T(8,128)(2,1)} custom-call(bf16[32,512]{1,0:T(8,128)(2,1)S(1)} %copy-done.5, f32[1,512]{1,0:T(1,128)S(1)} %bitcast.2, bf16[512,512]{1,0:T(8,128)(2,1)S(1)} %copy-done.3, f32[32,512]{1,0:T(8,128)S(1)} %get-tuple-element.37.refs_0_, bf16[32,512]{1,0:T(8,128)(2,1)S(1)} %collective-permute-done.12.refs_1_, ...), custom_call_target="tpu_custom_call" | custom-call | tf_op jit(solution)/shard_map/finish/pallas_call | solution.py:283
  (32 shorter events, 0.1 us)
Async XLA Ops:
  0.0 15.3 %collective-permute-start.2 = (bf16[32,512]{1,0:T(8,128)(2,1)}, bf16[32,512]{1,0:T(8,128)(2,1)S(1)}, u32[]{:S(2)}, u32[]{:S(2)}) collective-permute-start(bf16[32,512]{1,0:T(8,128)(2,1)} %feat.1), channel_id=1, source_target_pairs={{0,17},{1,16},{2,19},{3,18},{4,21},{5,20},{6,23},{7,22},{8,25},{9,... | collective-permute-start | bytes 98312 | tf_op jit(solution)/shard_map/ppermute | solution.py:313
  3.5 11.8 %collective-permute-start.1 = (bf16[32,512]{1,0:T(8,128)(2,1)}, bf16[32,512]{1,0:T(8,128)(2,1)S(1)}, u32[]{:S(2)}, u32[]{:S(2)}) collective-permute-start(bf16[32,512]{1,0:T(8,128)(2,1)} %feat.1), channel_id=1, source_target_pairs={{0,9},{1,8},{2,11},{3,10},{4,13},{5,12},{6,15},{7,14},{8,1},{9,0},... | collective-permute-start | bytes 98312 | tf_op jit(solution)/shard_map/ppermute | solution.py:313
  5.3 10.0 %collective-permute-start = (bf16[32,512]{1,0:T(8,128)(2,1)}, bf16[32,512]{1,0:T(8,128)(2,1)S(1)}, u32[]{:S(2)}, u32[]{:S(2)}) collective-permute-start(bf16[32,512]{1,0:T(8,128)(2,1)} %feat.1), channel_id=1, source_target_pairs={{0,1},{1,0},{2,3},{3,2},{4,5},{5,4},{6,7},{7,6},{8,9},{9,8},{10,11... | collective-permute-start | bytes 98312 | tf_op jit(solution)/shard_map/ppermute | solution.py:313
  5.3 10.0 %collective-permute-start.3 = (bf16[32,512]{1,0:T(8,128)(2,1)}, bf16[32,512]{1,0:T(8,128)(2,1)S(1)}, u32[]{:S(2)}, u32[]{:S(2)}) collective-permute-start(bf16[32,512]{1,0:T(8,128)(2,1)} %feat.1), channel_id=1, source_target_pairs={{0,25},{1,24},{2,27},{3,26},{4,29},{5,28},{6,31},{7,30},{8,17},{9,... | collective-permute-start | bytes 98312 | tf_op jit(solution)/shard_map/ppermute | solution.py:313
  5.3 0.7 %copy-start.6 = (s32[32,128]{1,0:T(8,128)S(1)}, s32[32,128]{1,0:T(8,128)}, u32[]{:S(2)}) copy-start(s32[32,128]{1,0:T(8,128)} %slots_ref.1) | copy-start | bytes 49156
  6.1 12.8 %copy-start.1 = (bf16[4,512,512]{2,1,0:T(8,128)(2,1)S(1)}, bf16[4,512,512]{2,1,0:T(8,128)(2,1)}, u32[]{:S(2)}) copy-start(bf16[4,512,512]{2,1,0:T(8,128)(2,1)} %kw.3) | copy-start | bytes 6291460
  6.1 12.8 %copy-start.2 = (bf16[4,512,512]{2,1,0:T(8,128)(2,1)S(1)}, bf16[4,512,512]{2,1,0:T(8,128)(2,1)}, u32[]{:S(2)}) copy-start(bf16[4,512,512]{2,1,0:T(8,128)(2,1)} %mw.3) | copy-start | bytes 6291460
  6.1 12.8 %copy-start.7 = (s32[32]{0:T(128)S(1)}, s32[32]{0:T(128)}, u32[]{:S(2)}) copy-start(s32[32]{0:T(128)} %rel_ref.9) | copy-start | bytes 388
  15.3 9.6 %collective-permute-start.6 = (bf16[128,512]{1,0:T(8,128)(2,1)S(1)}, bf16[128,512]{1,0:T(8,128)(2,1)S(1)}, u32[]{:S(2)}, u32[]{:S(2)}) collective-permute-start(bf16[128,512]{1,0:T(8,128)(2,1)S(1)} %pad_maximum_fusion.1), channel_id=1, source_target_pairs={{0,6},{1,7},{2,4},{3,5},{4,2},{5,3},{6,0},{7,1},{8,14},{9,15},{10,... | collective-permute-start | bytes 393224 | tf_op jit(solution)/shard_map/ppermute | solution.py:313
  18.2 6.8 %collective-permute-start.5 = (bf16[128,512]{1,0:T(8,128)(2,1)S(1)}, bf16[128,512]{1,0:T(8,128)(2,1)S(1)}, u32[]{:S(2)}, u32[]{:S(2)}) collective-permute-start(bf16[128,512]{1,0:T(8,128)(2,1)S(1)} %pad_maximum_fusion.1), channel_id=1, source_target_pairs={{0,4},{1,5},{2,6},{3,7},{4,0},{5,1},{6,2},{7,3},{8,12},{9,13},{10,... | collective-permute-start | bytes 393224 | tf_op jit(solution)/shard_map/ppermute | solution.py:313
  18.7 6.4 %collective-permute-start.4 = (bf16[128,512]{1,0:T(8,128)(2,1)S(1)}, bf16[128,512]{1,0:T(8,128)(2,1)S(1)}, u32[]{:S(2)}, u32[]{:S(2)}) collective-permute-start(bf16[128,512]{1,0:T(8,128)(2,1)S(1)} %pad_maximum_fusion.1), channel_id=1, source_target_pairs={{0,2},{1,3},{2,0},{3,1},{4,6},{5,7},{6,4},{7,5},{8,10},{9,11},{10,... | collective-permute-start | bytes 393224 | tf_op jit(solution)/shard_map/ppermute | solution.py:313
  18.9 6.3 %copy-start = (bf16[512,512]{1,0:T(8,128)(2,1)S(1)}, bf16[512,512]{1,0:T(8,128)(2,1)}, u32[]{:S(2)}) copy-start(bf16[512,512]{1,0:T(8,128)(2,1)} %wq.5) | copy-start | bytes 1572868
  18.9 6.3 %copy-start.4 = (s32[32,128]{1,0:T(8,128)S(1)}, s32[32,128]{1,0:T(8,128)}, u32[]{:S(2)}) copy-start(s32[32,128]{1,0:T(8,128)} %merch_slot.5) | copy-start | bytes 49156
  18.9 6.3 %copy-start.8 = (s32[32]{0:T(128)S(1)}, s32[32]{0:T(128)}, u32[]{:S(2)}) copy-start(s32[32]{0:T(128)} %count_ref.5) | copy-start | bytes 388
  18.9 6.3 %copy-start.9 = (f32[4]{0:T(128)S(1)}, f32[4]{0:T(128)}, u32[]{:S(2)}) copy-start(f32[4]{0:T(128)} %bias_ref.5) | copy-start | bytes 52
  25.1 2.3 %collective-permute-start.7 = (bf16[512,512]{1,0:T(8,128)(2,1)S(1)}, bf16[512,512]{1,0:T(8,128)(2,1)S(1)}, u32[]{:S(2)}, u32[]{:S(2)}) collective-permute-start(bf16[512,512]{1,0:T(8,128)(2,1)S(1)} %pad_maximum_fusion.feats), channel_id=1, source_target_pairs={{0,1},{1,0},{2,3},{3,2},{4,5},{5,4},{6,7},{7,6},{8,9},{9,8},{10,11... | collective-permute-start | bytes 1572872 | tf_op jit(solution)/shard_map/ppermute | solution.py:313
  26.9 2.1 %collective-permute-start.8 = (bf16[512,512]{1,0:T(8,128)(2,1)S(1)}, bf16[512,512]{1,0:T(8,128)(2,1)S(1)}, u32[]{:S(2)}, u32[]{:S(2)}) collective-permute-start(bf16[512,512]{1,0:T(8,128)(2,1)S(1)} %aggregate_odd.1), channel_id=1, source_target_pairs={{0,1},{1,0},{2,3},{3,2},{4,5},{5,4},{6,7},{7,6},{8,9},{9,8},{10,11... | collective-permute-start | bytes 1572872 | tf_op jit(solution)/shard_map/ppermute | solution.py:313
  29.1 6.0 %collective-permute-start.11 = (bf16[128,512]{1,0:T(8,128)(2,1)S(1)}, bf16[128,512]{1,0:T(8,128)(2,1)S(1)}, u32[]{:S(2)}, u32[]{:S(2)}) collective-permute-start(bf16[128,512]{1,0:T(8,128)(2,1)S(1)} %get-tuple-element.31), channel_id=1, source_target_pairs={{0,2},{1,3},{2,0},{3,1},{4,6},{5,7},{6,4},{7,5},{8,10},{9,11},{10,... | collective-permute-start | bytes 393224 | tf_op jit(solution)/shard_map/ppermute | solution.py:313
  30.9 8.3 %collective-permute-start.10 = (bf16[128,512]{1,0:T(8,128)(2,1)S(1)}, bf16[128,512]{1,0:T(8,128)(2,1)S(1)}, u32[]{:S(2)}, u32[]{:S(2)}) collective-permute-start(bf16[128,512]{1,0:T(8,128)(2,1)S(1)} %get-tuple-element.32), channel_id=1, source_target_pairs={{0,4},{1,5},{2,6},{3,7},{4,0},{5,1},{6,2},{7,3},{8,12},{9,13},{10,... | collective-permute-start | bytes 393224 | tf_op jit(solution)/shard_map/ppermute | solution.py:313
  32.4 6.8 %collective-permute-start.9 = (bf16[128,512]{1,0:T(8,128)(2,1)S(1)}, bf16[128,512]{1,0:T(8,128)(2,1)S(1)}, u32[]{:S(2)}, u32[]{:S(2)}) collective-permute-start(bf16[128,512]{1,0:T(8,128)(2,1)S(1)} %get-tuple-element.33), channel_id=1, source_target_pairs={{0,6},{1,7},{2,4},{3,5},{4,2},{5,3},{6,0},{7,1},{8,14},{9,15},{10,... | collective-permute-start | bytes 393224 | tf_op jit(solution)/shard_map/ppermute | solution.py:313
  34.0 13.7 %copy-start.3 = (bf16[512,512]{1,0:T(8,128)(2,1)S(1)}, bf16[512,512]{1,0:T(8,128)(2,1)}, u32[]{:S(2)}) copy-start(bf16[512,512]{1,0:T(8,128)(2,1)} %wo.1) | copy-start | bytes 1572868
  34.0 13.7 %copy-start.5 = (bf16[32,512]{1,0:T(8,128)(2,1)S(1)}, bf16[32,512]{1,0:T(8,128)(2,1)}, u32[]{:S(2)}) copy-start(bf16[32,512]{1,0:T(8,128)(2,1)} %feat.1) | copy-start | bytes 98308
  34.0 13.7 %copy-start.10 = (f32[512]{0:T(512)S(1)}, f32[512]{0:T(512)}, u32[]{:S(2)}) copy-start(f32[512]{0:T(512)} %param.19) | copy-start | bytes 6148
  39.2 5.8 %collective-permute-start.12 = (bf16[32,512]{1,0:T(8,128)(2,1)S(1)}, bf16[32,512]{1,0:T(8,128)(2,1)S(1)}, u32[]{:S(2)}, u32[]{:S(2)}) collective-permute-start(bf16[32,512]{1,0:T(8,128)(2,1)S(1)} %get-tuple-element.38), channel_id=1, source_target_pairs={{0,24},{1,25},{2,26},{3,27},{4,28},{5,29},{6,30},{7,31},{8,16},{9,... | collective-permute-start | bytes 98312 | tf_op jit(solution)/shard_map/ppermute | solution.py:313
  42.9 4.8 %collective-permute-start.13 = (bf16[32,512]{1,0:T(8,128)(2,1)S(1)}, bf16[32,512]{1,0:T(8,128)(2,1)S(1)}, u32[]{:S(2)}, u32[]{:S(2)}) collective-permute-start(bf16[32,512]{1,0:T(8,128)(2,1)S(1)} %get-tuple-element.39), channel_id=1, source_target_pairs={{0,16},{1,17},{2,18},{3,19},{4,20},{5,21},{6,22},{7,23},{8,24},{9,... | collective-permute-start | bytes 98312 | tf_op jit(solution)/shard_map/ppermute | solution.py:313
  42.9 4.8 %collective-permute-start.14 = (bf16[32,512]{1,0:T(8,128)(2,1)S(1)}, bf16[32,512]{1,0:T(8,128)(2,1)S(1)}, u32[]{:S(2)}, u32[]{:S(2)}) collective-permute-start(bf16[32,512]{1,0:T(8,128)(2,1)S(1)} %get-tuple-element.40), channel_id=1, source_target_pairs={{0,8},{1,9},{2,10},{3,11},{4,12},{5,13},{6,14},{7,15},{8,0},{9,1},... | collective-permute-start | bytes 98312 | tf_op jit(solution)/shard_map/ppermute | solution.py:313

commit v19 on v17

--- a/solution.py
+++ b/solution.py
@@ -29,6 +29,22 @@
 
 def _offset(i, outer):
     return (i // outer) * 2 + (i % outer) * 8
+
+
+def stage_kernel(slots, out):
+    out[...] = slots[...]
+
+
+def stage(slots):
+    return pl.pallas_call(
+        stage_kernel,
+        out_shape=jax.ShapeDtypeStruct(slots.shape, slots.dtype),
+        in_specs=[VMEM],
+        out_specs=VMEM,
+        compiler_params=_mb(2),
+        cost_estimate=_cost(0, 2**16),
+        name="stage_slots",
+    )(slots)
 
 
 def gather_kernel(
@@ -296,8 +312,14 @@
     def after(value, *others):
         return lax.optimization_barrier((value,) + others)[0]
 
-    feats = jnp.concatenate([swap(merch_feat, 8 * k + 1) for k in range(outer)], axis=0)
-    rows = gather(outer, me, slot_acct, acct_feat)
+    feats = jnp.concatenate([swap(merch_feat, 1), swap(merch_feat, 9)], axis=0)
+    slots = stage(slot_acct)
+    feats = after(feats, slots)
+    mask = 16
+    while mask < devices:
+        feats = jnp.concatenate([feats, swap(feats, mask)], axis=0)
+        mask *= 2
+    rows = gather(outer, me, slots, acct_feat)
     feats = after(feats, rows[0])
     feats = jnp.concatenate([feats] + [swap(feats, 2 * j) for j in range(1, inner)], axis=0)
 
@@ -327,7 +349,8 @@
     parts = combine_plane(
         outer, [near] + [swap(parts[j - 1], 2 * j) for j in reversed(range(1, inner))]
     )
-    parts = [parts[0]] + [swap(parts[k], 8 * k) for k in reversed(range(1, outer))]
+    order = [2, 3, 1] + list(range(4, outer))
+    parts = [parts[0]] + [swap(parts[k], 8 * k) for k in order]
     return finish(merch_feat, out_gain, out_weight, parts)
 
 

time: 48.7 us -> 49.4 us (1.014)
  waiting for transfers between devices: 8.39 us -> 9.16 us
    ppermute x15 -> x14, waiting for transfers between devices: 8.39 us -> 9.16 us  [swap(): return lax.ppermute(value, AXES, [(s, s ^ mask) for s in range(devices)])]
    ppermute x15 -> x14, starting transfers between devices: 17.5 us -> 17.4 us  [swap(): return lax.ppermute(value, AXES, [(s, s ^ mask) for s in range(devices)])]
  transfers between devices with their start and end apart: 15 -> 14, of which waited for: 6 -> 7; matrix products, arithmetic and copies ran while one was open for 0% -> 0% of each run, Pallas kernels for 42% -> 42%
where the time goes in v19:
time: 49.4 us; the launch traced here: 49.1 us
  Pallas kernels  21.6 us (44%)
  starting transfers between devices  17.4 us (35%)
  waiting for transfers between devices  9.16 us (19%)
  local copies, waits for them, and re-layouts  0.77 us (2%)
    ppermute x14, starting transfers between devices, swap(): return lax.ppermute(value, AXES, [(s, s ^ mask) for s in range(devices)])  17.4 us
    pallas_call x1, Pallas kernels, gather(): pl.pallas_call(functools.partial(gather_kernel, outer), out_shape=(half,...  9.2 us
    ppermute x14, waiting for transfers between devices, swap(): return lax.ppermute(value, AXES, [(s, s ^ mask) for s in range(devices)])  9.16 us
    pallas_call x2, Pallas kernels, project(): pl.pallas_call(functools.partial(project_kernel, outer, spans), out_shape...  7.32 us
    pallas_call x3, Pallas kernels, aggregate(): pl.pallas_call(functools.partial(aggregate_kernel, outer, first, shift),...  3.97 us
  transfers between devices with their start and end apart: 14, of which 7 were waited for; matrix products, arithmetic and copies ran while one was open for 0% of the time, Pallas kernels for 42%

profile of v19, /device:TPU:0, one launch (start us, length us, event | category | flops | bytes accessed | tf_op | source)
XLA Modules:
  0.0 49.1 jit_solution(4577130280513496696)
XLA Ops:
  0.0 0.5 collective-permute-start
  0.5 2.7 %collective-permute-start.1 = (bf16[32,512]{1,0:T(8,128)(2,1)}, bf16[32,512]{1,0:T(8,128)(2,1)S(1)}, u32[]{:S(2)}, u32[]{:S(2)}) collective-permute-start(bf16[32,512]{1,0:T(8,128)(2,1)} %feat.1), channel_id=1, source_target_pairs={{0,9},{1,8},{2,11},{3,10},{4,13},{5,12},{6,15},{7,14},{8,1},{9,0},... | collective-permute-start | bytes 98312 | tf_op jit(solution)/shard_map/ppermute | solution.py:310
  3.1 0.7 %copy-done.6 = s32[32,128]{1,0:T(8,128)S(1)} copy-done((s32[32,128]{1,0:T(8,128)S(1)}, s32[32,128]{1,0:T(8,128)}, u32[]{:S(2)}) %copy-start.6) | copy-done | bytes 16408
  3.9 1.2 %collective-permute-done.1 = bf16[32,512]{1,0:T(8,128)(2,1)S(1)} collective-permute-done((bf16[32,512]{1,0:T(8,128)(2,1)}, bf16[32,512]{1,0:T(8,128)(2,1)S(1)}, u32[]{:S(2)}, u32[]{:S(2)}) %collective-permute-start.1) | collective-permute-done | bytes 32800 | tf_op jit(solution)/shard_map/ppermute | solution.py:310
  5.1 2.5 %collective-permute-start.2 = (bf16[64,512]{1,0:T(8,128)(2,1)S(1)}, bf16[64,512]{1,0:T(8,128)(2,1)S(1)}, u32[]{:S(2)}, u32[]{:S(2)}) collective-permute-start(bf16[64,512]{1,0:T(8,128)(2,1)S(1)} %pad_maximum_fusion.2), channel_id=1, source_target_pairs={{0,16},{1,17},{2,18},{3,19},{4,20},{5,21},{6,22},{7,23},{8,24},{9,... | collective-permute-start | bytes 196616 | tf_op jit(solution)/shard_map/ppermute | solution.py:310
  7.7 9.2 %gather_slots.1 = (bf16[16,128,512]{2,1,0:T(8,128)(2,1)S(1)}, bf16[16,128,512]{2,1,0:T(8,128)(2,1)S(1)}) custom-call(s32[1]{0:T(128)} %bitcast.1.me_ref, s32[32,128]{1,0:T(8,128)S(1)} %stage_slots.1.slots_ref, bf16[4096,512]{1,0:T(8,128)(2,1)} %acct_hbm.1), custom_call_target="tpu_custom_call" | custom-call | bytes 20971520 | tf_op jit(solution)/shard_map/gather_slots/pallas_call | solution.py:110
  16.9 2.5 %collective-permute-start.5 = (bf16[128,512]{1,0:T(8,128)(2,1)S(1)}, bf16[128,512]{1,0:T(8,128)(2,1)S(1)}, u32[]{:S(2)}, u32[]{:S(2)}) collective-permute-start(bf16[128,512]{1,0:T(8,128)(2,1)S(1)} %pad_maximum_fusion.1), channel_id=1, source_target_pairs={{0,6},{1,7},{2,4},{3,5},{4,2},{5,3},{6,0},{7,1},{8,14},{9,15},{10,... | collective-permute-start | bytes 393224 | tf_op jit(solution)/shard_map/ppermute | solution.py:310
  19.4 0.5 %collective-permute-start.4 = (bf16[128,512]{1,0:T(8,128)(2,1)S(1)}, bf16[128,512]{1,0:T(8,128)(2,1)S(1)}, u32[]{:S(2)}, u32[]{:S(2)}) collective-permute-start(bf16[128,512]{1,0:T(8,128)(2,1)S(1)} %pad_maximum_fusion.1), channel_id=1, source_target_pairs={{0,4},{1,5},{2,6},{3,7},{4,0},{5,1},{6,2},{7,3},{8,12},{9,13},{10,... | collective-permute-start | bytes 393224 | tf_op jit(solution)/shard_map/ppermute | solution.py:310
  19.9 0.5 %collective-permute-start.3 = (bf16[128,512]{1,0:T(8,128)(2,1)S(1)}, bf16[128,512]{1,0:T(8,128)(2,1)S(1)}, u32[]{:S(2)}, u32[]{:S(2)}) collective-permute-start(bf16[128,512]{1,0:T(8,128)(2,1)S(1)} %pad_maximum_fusion.1), channel_id=1, source_target_pairs={{0,2},{1,3},{2,0},{3,1},{4,6},{5,7},{6,4},{7,5},{8,10},{9,11},{10,... | collective-permute-start | bytes 393224 | tf_op jit(solution)/shard_map/ppermute | solution.py:310
  20.5 0.0 copy-start.4
  20.5 0.0 copy-start.8
  20.5 6.0 %project_slots.2 = (bf16[16,512,128]{2,1,0:T(8,128)(2,1)S(1)}, bf16[16,128,512]{2,1,0:T(8,128)(2,1)S(1)}, bf16[12,512,128]{2,1,0:T(8,128)(2,1)S(1)}, bf16[12,128,512]{2,1,0:T(8,128)(2,1)S(1)}) custom-call(s32[1]{0:T(128)} %bitcast.1.me_ref, s32[32]{0:T(128)S(1)} %copy-done.7, bf16[4,512,512]{2,1,0:T(8,128)(2,1)S(1)} %copy-done.1, ...), custom_call_target="tpu_custom_call" | custom-call | flops 3758096384 | bytes 14680064 | tf_op jit(solution)/shard_map/project_slots/pallas_call | solution.py:161
  26.6 0.1 collective-permute-start.6
  26.7 1.5 %aggregate_odd.1 = bf16[512,512]{1,0:T(8,128)(2,1)S(1)} custom-call(s32[1]{0:T(128)} %bitcast.1.me_ref, s32[32]{0:T(128)S(1)} %copy-done.7, s32[32]{0:T(128)S(1)} %copy-done.8, f32[4]{0:T(128)S(1)} %copy-done.9, s32[32,128]{1,0:T(8,128)S(1)} %copy-done.4, bf16[512,512]{1,0:T(8,128)(2,1)S(1)} %pad_maximum_fusion.feats, bf16[512,512]{1,0:T(8,128)(2,1)S(1)} %copy-done, ...), custom_call_target="tpu_custom_call" | custom-call | flops 402653184 | bytes 6291456 | tf_op jit(solution)/shard_map/aggregate_odd/pallas_call | solution.py:202
  28.2 0.5 %collective-permute-start.7 = (bf16[512,512]{1,0:T(8,128)(2,1)S(1)}, bf16[512,512]{1,0:T(8,128)(2,1)S(1)}, u32[]{:S(2)}, u32[]{:S(2)}) collective-permute-start(bf16[512,512]{1,0:T(8,128)(2,1)S(1)} %aggregate_odd.1), channel_id=1, source_target_pairs={{0,1},{1,0},{2,3},{3,2},{4,5},{5,4},{6,7},{7,6},{8,9},{9,8},{10,11... | collective-permute-start | bytes 1572872 | tf_op jit(solution)/shard_map/ppermute | solution.py:310
  28.8 1.3 %aggregate_even.2.mine = f32[384,512]{1,0:T(8,128)S(1)} custom-call(s32[1]{0:T(128)} %bitcast.1.me_ref, s32[32]{0:T(128)S(1)} %copy-done.7, s32[32]{0:T(128)S(1)} %copy-done.8, f32[4]{0:T(128)S(1)} %copy-done.9, s32[32,128]{1,0:T(8,128)S(1)} %copy-done.4, bf16[512,512]{1,0:T(8,128)(2,1)S(1)} %collective-permute-done.6.feats, bf16[512,512]{1,0:T(8,128)(2,1)S(1)} %copy-done, ...), custom_call_target="tpu_custom_call" | custom-call | flops 301989888 | bytes 6291456 | tf_op jit(solution)/shard_map/aggregate_even/pallas_call | solution.py:202
  30.1 0.2 collective-permute-done.7.other
  30.3 0.1 combine_cores.2
  30.4 1.6 %collective-permute-start.10 = (bf16[128,512]{1,0:T(8,128)(2,1)S(1)}, bf16[128,512]{1,0:T(8,128)(2,1)S(1)}, u32[]{:S(2)}, u32[]{:S(2)}) collective-permute-start(bf16[128,512]{1,0:T(8,128)(2,1)S(1)} %get-tuple-element.33), channel_id=1, source_target_pairs={{0,2},{1,3},{2,0},{3,1},{4,6},{5,7},{6,4},{7,5},{8,10},{9,11},{10,... | collective-permute-start | bytes 393224 | tf_op jit(solution)/shard_map/ppermute | solution.py:310
  32.0 1.5 %collective-permute-start.9 = (bf16[128,512]{1,0:T(8,128)(2,1)S(1)}, bf16[128,512]{1,0:T(8,128)(2,1)S(1)}, u32[]{:S(2)}, u32[]{:S(2)}) collective-permute-start(bf16[128,512]{1,0:T(8,128)(2,1)S(1)} %get-tuple-element.34), channel_id=1, source_target_pairs={{0,4},{1,5},{2,6},{3,7},{4,0},{5,1},{6,2},{7,3},{8,12},{9,13},{10,... | collective-permute-start | bytes 393224 | tf_op jit(solution)/shard_map/ppermute | solution.py:310
  33.5 0.5 collective-permute-start.8
  34.0 1.3 %project_slots.3 = (bf16[4,512,128]{2,1,0:T(8,128)(2,1)S(1)}, bf16[4,128,512]{2,1,0:T(8,128)(2,1)S(1)}) custom-call(s32[1]{0:T(128)} %bitcast.1.me_ref, s32[32]{0:T(128)S(1)} %copy-done.7, bf16[4,512,512]{2,1,0:T(8,128)(2,1)S(1)} %copy-done.1, bf16[4,512,512]{2,1,0:T(8,128)(2,1)S(1)} %copy-done.2, bf16[16,128,512]{2,1,0:T(8,128)(2,1)S(1)} %get-tuple-element.27.refs_1_.refs_0_), custom_call_target="tpu_custom_call" | custom-call | flops 536870912 | bytes 2097152 | tf_op jit(solution)/shard_map/project_slots/pallas_call | solution.py:161
  35.3 1.1 %aggregate_even.3.mine = f32[128,512]{1,0:T(8,128)S(1)} custom-call(s32[1]{0:T(128)} %bitcast.1.me_ref, s32[32]{0:T(128)S(1)} %copy-done.7, s32[32]{0:T(128)S(1)} %copy-done.8, f32[4]{0:T(128)S(1)} %copy-done.9, s32[32,128]{1,0:T(8,128)S(1)} %copy-done.4, bf16[512,512]{1,0:T(8,128)(2,1)S(1)} %collective-permute-done.6.feats, bf16[512,512]{1,0:T(8,128)(2,1)S(1)} %copy-done, ...), custom_call_target="tpu_custom_call" | custom-call | flops 100663296 | bytes 6291456 | tf_op jit(solution)/shard_map/aggregate_even/pallas_call | solution.py:202
  36.5 0.1 collective-permute-done.10.refs_3_
  36.6 3.7 %collective-permute-done.9.refs_2_ = bf16[128,512]{1,0:T(8,128)(2,1)S(1)} collective-permute-done((bf16[128,512]{1,0:T(8,128)(2,1)S(1)}, bf16[128,512]{1,0:T(8,128)(2,1)S(1)}, u32[]{:S(2)}, u32[]{:S(2)}) %collective-permute-start.9) | collective-permute-done | bytes 131104 | tf_op jit(solution)/shard_map/ppermute | solution.py:310
  40.3 0.1 combine_plane.1
  40.3 0.4 collective-permute-start.11
  40.7 3.6 %collective-permute-start.12 = (bf16[32,512]{1,0:T(8,128)(2,1)S(1)}, bf16[32,512]{1,0:T(8,128)(2,1)S(1)}, u32[]{:S(2)}, u32[]{:S(2)}) collective-permute-start(bf16[32,512]{1,0:T(8,128)(2,1)S(1)} %get-tuple-element.41), channel_id=1, source_target_pairs={{0,24},{1,25},{2,26},{3,27},{4,28},{5,29},{6,30},{7,31},{8,16},{9,... | collective-permute-start | bytes 98312 | tf_op jit(solution)/shard_map/ppermute | solution.py:310
  44.3 0.9 %collective-permute-done.11.refs_1_ = bf16[32,512]{1,0:T(8,128)(2,1)S(1)} collective-permute-done((bf16[32,512]{1,0:T(8,128)(2,1)S(1)}, bf16[32,512]{1,0:T(8,128)(2,1)S(1)}, u32[]{:S(2)}, u32[]{:S(2)}) %collective-permute-start.11) | collective-permute-done | bytes 32800 | tf_op jit(solution)/shard_map/ppermute | solution.py:310
  45.2 1.3 %collective-permute-done.12.refs_2_ = bf16[32,512]{1,0:T(8,128)(2,1)S(1)} collective-permute-done((bf16[32,512]{1,0:T(8,128)(2,1)S(1)}, bf16[32,512]{1,0:T(8,128)(2,1)S(1)}, u32[]{:S(2)}, u32[]{:S(2)}) %collective-permute-start.12) | collective-permute-done | bytes 32800 | tf_op jit(solution)/shard_map/ppermute | solution.py:310
  46.5 1.7 %collective-permute-done.13.refs_3_ = bf16[32,512]{1,0:T(8,128)(2,1)S(1)} collective-permute-done((bf16[32,512]{1,0:T(8,128)(2,1)S(1)}, bf16[32,512]{1,0:T(8,128)(2,1)S(1)}, u32[]{:S(2)}, u32[]{:S(2)}) %collective-permute-start.13) | collective-permute-done | bytes 32800 | tf_op jit(solution)/shard_map/ppermute | solution.py:310
  48.2 0.9 %finish.1 = bf16[32,512]{1,0:T(8,128)(2,1)} custom-call(bf16[32,512]{1,0:T(8,128)(2,1)S(1)} %copy-done.5, f32[1,512]{1,0:T(1,128)S(1)} %bitcast.2, bf16[512,512]{1,0:T(8,128)(2,1)S(1)} %copy-done.3, f32[32,512]{1,0:T(8,128)S(1)} %get-tuple-element.39.refs_0_, bf16[32,512]{1,0:T(8,128)(2,1)S(1)} %collective-permute-done.11.refs_1_, ...), custom_call_target="tpu_custom_call" | custom-call | tf_op jit(solution)/shard_map/finish/pallas_call | solution.py:280
  (32 shorter events, 0.2 us)
Async XLA Ops:
  0.0 3.9 %collective-permute-start = (bf16[32,512]{1,0:T(8,128)(2,1)}, bf16[32,512]{1,0:T(8,128)(2,1)S(1)}, u32[]{:S(2)}, u32[]{:S(2)}) collective-permute-start(bf16[32,512]{1,0:T(8,128)(2,1)} %feat.1), channel_id=1, source_target_pairs={{0,1},{1,0},{2,3},{3,2},{4,5},{5,4},{6,7},{7,6},{8,9},{9,8},{10,11... | collective-permute-start | bytes 98312 | tf_op jit(solution)/shard_map/ppermute | solution.py:310
  0.5 4.7 %collective-permute-start.1 = (bf16[32,512]{1,0:T(8,128)(2,1)}, bf16[32,512]{1,0:T(8,128)(2,1)S(1)}, u32[]{:S(2)}, u32[]{:S(2)}) collective-permute-start(bf16[32,512]{1,0:T(8,128)(2,1)} %feat.1), channel_id=1, source_target_pairs={{0,9},{1,8},{2,11},{3,10},{4,13},{5,12},{6,15},{7,14},{8,1},{9,0},... | collective-permute-start | bytes 98312 | tf_op jit(solution)/shard_map/ppermute | solution.py:310
  3.1 0.7 %copy-start.6 = (s32[32,128]{1,0:T(8,128)S(1)}, s32[32,128]{1,0:T(8,128)}, u32[]{:S(2)}) copy-start(s32[32,128]{1,0:T(8,128)} %slots.1) | copy-start | bytes 49156
  5.1 11.7 %collective-permute-start.2 = (bf16[64,512]{1,0:T(8,128)(2,1)S(1)}, bf16[64,512]{1,0:T(8,128)(2,1)S(1)}, u32[]{:S(2)}, u32[]{:S(2)}) collective-permute-start(bf16[64,512]{1,0:T(8,128)(2,1)S(1)} %pad_maximum_fusion.2), channel_id=1, source_target_pairs={{0,16},{1,17},{2,18},{3,19},{4,20},{5,21},{6,22},{7,23},{8,24},{9,... | collective-permute-start | bytes 196616 | tf_op jit(solution)/shard_map/ppermute | solution.py:310
  7.6 12.8 %copy-start.1 = (bf16[4,512,512]{2,1,0:T(8,128)(2,1)S(1)}, bf16[4,512,512]{2,1,0:T(8,128)(2,1)}, u32[]{:S(2)}) copy-start(bf16[4,512,512]{2,1,0:T(8,128)(2,1)} %kw.3) | copy-start | bytes 6291460
  7.7 12.8 %copy-start.2 = (bf16[4,512,512]{2,1,0:T(8,128)(2,1)S(1)}, bf16[4,512,512]{2,1,0:T(8,128)(2,1)}, u32[]{:S(2)}) copy-start(bf16[4,512,512]{2,1,0:T(8,128)(2,1)} %mw.3) | copy-start | bytes 6291460
  7.7 12.8 %copy-start.7 = (s32[32]{0:T(128)S(1)}, s32[32]{0:T(128)}, u32[]{:S(2)}) copy-start(s32[32]{0:T(128)} %rel_ref.9) | copy-start | bytes 388
  16.9 9.6 %collective-permute-start.5 = (bf16[128,512]{1,0:T(8,128)(2,1)S(1)}, bf16[128,512]{1,0:T(8,128)(2,1)S(1)}, u32[]{:S(2)}, u32[]{:S(2)}) collective-permute-start(bf16[128,512]{1,0:T(8,128)(2,1)S(1)} %pad_maximum_fusion.1), channel_id=1, source_target_pairs={{0,6},{1,7},{2,4},{3,5},{4,2},{5,3},{6,0},{7,1},{8,14},{9,15},{10,... | collective-permute-start | bytes 393224 | tf_op jit(solution)/shard_map/ppermute | solution.py:310
  19.4 7.1 %collective-permute-start.4 = (bf16[128,512]{1,0:T(8,128)(2,1)S(1)}, bf16[128,512]{1,0:T(8,128)(2,1)S(1)}, u32[]{:S(2)}, u32[]{:S(2)}) collective-permute-start(bf16[128,512]{1,0:T(8,128)(2,1)S(1)} %pad_maximum_fusion.1), channel_id=1, source_target_pairs={{0,4},{1,5},{2,6},{3,7},{4,0},{5,1},{6,2},{7,3},{8,12},{9,13},{10,... | collective-permute-start | bytes 393224 | tf_op jit(solution)/shard_map/ppermute | solution.py:310
  19.9 6.6 %collective-permute-start.3 = (bf16[128,512]{1,0:T(8,128)(2,1)S(1)}, bf16[128,512]{1,0:T(8,128)(2,1)S(1)}, u32[]{:S(2)}, u32[]{:S(2)}) collective-permute-start(bf16[128,512]{1,0:T(8,128)(2,1)S(1)} %pad_maximum_fusion.1), channel_id=1, source_target_pairs={{0,2},{1,3},{2,0},{3,1},{4,6},{5,7},{6,4},{7,5},{8,10},{9,11},{10,... | collective-permute-start | bytes 393224 | tf_op jit(solution)/shard_map/ppermute | solution.py:310
  20.5 6.2 %copy-start = (bf16[512,512]{1,0:T(8,128)(2,1)S(1)}, bf16[512,512]{1,0:T(8,128)(2,1)}, u32[]{:S(2)}) copy-start(bf16[512,512]{1,0:T(8,128)(2,1)} %wq.5) | copy-start | bytes 1572868
  20.5 6.2 %copy-start.4 = (s32[32,128]{1,0:T(8,128)S(1)}, s32[32,128]{1,0:T(8,128)}, u32[]{:S(2)}) copy-start(s32[32,128]{1,0:T(8,128)} %merch_slot.5) | copy-start | bytes 49156
  20.5 6.2 %copy-start.8 = (s32[32]{0:T(128)S(1)}, s32[32]{0:T(128)}, u32[]{:S(2)}) copy-start(s32[32]{0:T(128)} %count_ref.5) | copy-start | bytes 388
  20.5 6.2 %copy-start.9 = (f32[4]{0:T(128)S(1)}, f32[4]{0:T(128)}, u32[]{:S(2)}) copy-start(f32[4]{0:T(128)} %bias_ref.5) | copy-start | bytes 52
  26.6 2.2 %collective-permute-start.6 = (bf16[512,512]{1,0:T(8,128)(2,1)S(1)}, bf16[512,512]{1,0:T(8,128)(2,1)S(1)}, u32[]{:S(2)}, u32[]{:S(2)}) collective-permute-start(bf16[512,512]{1,0:T(8,128)(2,1)S(1)} %pad_maximum_fusion.feats), channel_id=1, source_target_pairs={{0,1},{1,0},{2,3},{3,2},{4,5},{5,4},{6,7},{7,6},{8,9},{9,8},{10,11... | collective-permute-start | bytes 1572872 | tf_op jit(solution)/shard_map/ppermute | solution.py:310
  28.2 2.1 %collective-permute-start.7 = (bf16[512,512]{1,0:T(8,128)(2,1)S(1)}, bf16[512,512]{1,0:T(8,128)(2,1)S(1)}, u32[]{:S(2)}, u32[]{:S(2)}) collective-permute-start(bf16[512,512]{1,0:T(8,128)(2,1)S(1)} %aggregate_odd.1), channel_id=1, source_target_pairs={{0,1},{1,0},{2,3},{3,2},{4,5},{5,4},{6,7},{7,6},{8,9},{9,8},{10,11... | collective-permute-start | bytes 1572872 | tf_op jit(solution)/shard_map/ppermute | solution.py:310
  30.4 6.2 %collective-permute-start.10 = (bf16[128,512]{1,0:T(8,128)(2,1)S(1)}, bf16[128,512]{1,0:T(8,128)(2,1)S(1)}, u32[]{:S(2)}, u32[]{:S(2)}) collective-permute-start(bf16[128,512]{1,0:T(8,128)(2,1)S(1)} %get-tuple-element.33), channel_id=1, source_target_pairs={{0,2},{1,3},{2,0},{3,1},{4,6},{5,7},{6,4},{7,5},{8,10},{9,11},{10,... | collective-permute-start | bytes 393224 | tf_op jit(solution)/shard_map/ppermute | solution.py:310
  32.0 8.3 %collective-permute-start.9 = (bf16[128,512]{1,0:T(8,128)(2,1)S(1)}, bf16[128,512]{1,0:T(8,128)(2,1)S(1)}, u32[]{:S(2)}, u32[]{:S(2)}) collective-permute-start(bf16[128,512]{1,0:T(8,128)(2,1)S(1)} %get-tuple-element.34), channel_id=1, source_target_pairs={{0,4},{1,5},{2,6},{3,7},{4,0},{5,1},{6,2},{7,3},{8,12},{9,13},{10,... | collective-permute-start | bytes 393224 | tf_op jit(solution)/shard_map/ppermute | solution.py:310
  33.5 6.8 %collective-permute-start.8 = (bf16[128,512]{1,0:T(8,128)(2,1)S(1)}, bf16[128,512]{1,0:T(8,128)(2,1)S(1)}, u32[]{:S(2)}, u32[]{:S(2)}) collective-permute-start(bf16[128,512]{1,0:T(8,128)(2,1)S(1)} %get-tuple-element.35), channel_id=1, source_target_pairs={{0,6},{1,7},{2,4},{3,5},{4,2},{5,3},{6,0},{7,1},{8,14},{9,15},{10,... | collective-permute-start | bytes 393224 | tf_op jit(solution)/shard_map/ppermute | solution.py:310
  35.3 12.9 %copy-start.3 = (bf16[512,512]{1,0:T(8,128)(2,1)S(1)}, bf16[512,512]{1,0:T(8,128)(2,1)}, u32[]{:S(2)}) copy-start(bf16[512,512]{1,0:T(8,128)(2,1)} %wo.1) | copy-start | bytes 1572868
  35.3 12.9 %copy-start.5 = (bf16[32,512]{1,0:T(8,128)(2,1)S(1)}, bf16[32,512]{1,0:T(8,128)(2,1)}, u32[]{:S(2)}) copy-start(bf16[32,512]{1,0:T(8,128)(2,1)} %feat.1) | copy-start | bytes 98308
  35.3 12.9 %copy-start.10 = (f32[512]{0:T(512)S(1)}, f32[512]{0:T(512)}, u32[]{:S(2)}) copy-start(f32[512]{0:T(512)} %param.19) | copy-start | bytes 6148
  40.3 4.9 %collective-permute-start.11 = (bf16[32,512]{1,0:T(8,128)(2,1)S(1)}, bf16[32,512]{1,0:T(8,128)(2,1)S(1)}, u32[]{:S(2)}, u32[]{:S(2)}) collective-permute-start(bf16[32,512]{1,0:T(8,128)(2,1)S(1)} %get-tuple-element.40), channel_id=1, source_target_pairs={{0,16},{1,17},{2,18},{3,19},{4,20},{5,21},{6,22},{7,23},{8,24},{9,... | collective-permute-start | bytes 98312 | tf_op jit(solution)/shard_map/ppermute | solution.py:310
  40.7 5.8 %collective-permute-start.12 = (bf16[32,512]{1,0:T(8,128)(2,1)S(1)}, bf16[32,512]{1,0:T(8,128)(2,1)S(1)}, u32[]{:S(2)}, u32[]{:S(2)}) collective-permute-start(bf16[32,512]{1,0:T(8,128)(2,1)S(1)} %get-tuple-element.41), channel_id=1, source_target_pairs={{0,24},{1,25},{2,26},{3,27},{4,28},{5,29},{6,30},{7,31},{8,16},{9,... | collective-permute-start | bytes 98312 | tf_op jit(solution)/shard_map/ppermute | solution.py:310
  44.3 3.9 %collective-permute-start.13 = (bf16[32,512]{1,0:T(8,128)(2,1)S(1)}, bf16[32,512]{1,0:T(8,128)(2,1)S(1)}, u32[]{:S(2)}, u32[]{:S(2)}) collective-permute-start(bf16[32,512]{1,0:T(8,128)(2,1)S(1)} %get-tuple-element.42), channel_id=1, source_target_pairs={{0,8},{1,9},{2,10},{3,11},{4,12},{5,13},{6,14},{7,15},{8,0},{9,1},... | collective-permute-start | bytes 98312 | tf_op jit(solution)/shard_map/ppermute | solution.py:310

commit v20 on v17

--- a/solution.py
+++ b/solution.py
@@ -151,6 +151,25 @@
         cost_estimate=_cost(4 * blocks * block_len * width * width, blocks * 2**19),
         name="project_slots",
     )(me, rel, kw, mw, *feats)
+
+
+def assemble_kernel(places, *refs):
+    rows = refs[0].shape[0]
+    for place, part in zip(places, refs[:-1]):
+        refs[-1][place * rows : (place + 1) * rows, :] = part[...]
+
+
+def assemble(places, parts):
+    rows, width = parts[0].shape
+    return pl.pallas_call(
+        functools.partial(assemble_kernel, places),
+        out_shape=jax.ShapeDtypeStruct((len(parts) * rows, width), parts[0].dtype),
+        in_specs=[VMEM] * len(parts),
+        out_specs=VMEM,
+        compiler_params=_mb(2),
+        cost_estimate=_cost(1, 1),
+        name="assemble",
+    )(*parts)
 
 
 def aggregate_kernel(
@@ -296,7 +315,8 @@
     def after(value, *others):
         return lax.optimization_barrier((value,) + others)[0]
 
-    feats = jnp.concatenate([swap(merch_feat, 8 * k + 1) for k in range(outer)], axis=0)
+    order = [1, 3, 2, 0] + list(range(4, outer))
+    feats = assemble(order, [swap(merch_feat, 8 * k + 1) for k in order])
     rows = gather(outer, me, slot_acct, acct_feat)
     feats = after(feats, rows[0])
     feats = jnp.concatenate([feats] + [swap(feats, 2 * j) for j in range(1, inner)], axis=0)

time: 48.7 us -> 48.1 us (0.988)
  waiting for transfers between devices: 8.39 us -> 7.73 us
    ppermute x15, waiting for transfers between devices: 8.39 us -> 7.73 us  [swap(): return lax.ppermute(value, AXES, [(s, s ^ mask) for s in range(devices)])]
  transfers between devices with their start and end apart: 15 -> 15, of which waited for: 6 -> 6; matrix products, arithmetic and copies ran while one was open for 0% -> 0% of each run, Pallas kernels for 42% -> 43%
where the time goes in v20:
time: 48.1 us; the launch traced here: 47.9 us
  Pallas kernels  21.6 us (45%)
  starting transfers between devices  17.5 us (36%)
  waiting for transfers between devices  7.73 us (16%)
  local copies, waits for them, and re-layouts  0.77 us (2%)
    ppermute x15, starting transfers between devices, swap(): return lax.ppermute(value, AXES, [(s, s ^ mask) for s in range(devices)])  17.5 us
    pallas_call x1, Pallas kernels, gather(): pl.pallas_call(functools.partial(gather_kernel, outer), out_shape=(half,...  9.2 us
    ppermute x15, waiting for transfers between devices, swap(): return lax.ppermute(value, AXES, [(s, s ^ mask) for s in range(devices)])  7.73 us
    pallas_call x2, Pallas kernels, project(): pl.pallas_call(functools.partial(project_kernel, outer, spans), out_shape...  7.32 us
    pallas_call x3, Pallas kernels, aggregate(): pl.pallas_call(functools.partial(aggregate_kernel, outer, first, shift),...  3.97 us
  transfers between devices with their start and end apart: 15, of which 6 were waited for; matrix products, arithmetic and copies ran while one was open for 0% of the time, Pallas kernels for 43%

profile of v20, /device:TPU:0, one launch (start us, length us, event | category | flops | bytes accessed | tf_op | source)
XLA Modules:
  0.0 47.9 jit_solution(5300533876918883775)
XLA Ops:
  0.0 3.5 %collective-permute-start.2 = (bf16[32,512]{1,0:T(8,128)(2,1)}, bf16[32,512]{1,0:T(8,128)(2,1)S(1)}, u32[]{:S(2)}, u32[]{:S(2)}) collective-permute-start(bf16[32,512]{1,0:T(8,128)(2,1)} %feat.1), channel_id=1, source_target_pairs={{0,17},{1,16},{2,19},{3,18},{4,21},{5,20},{6,23},{7,22},{8,25},{9,... | collective-permute-start | bytes 98312 | tf_op jit(solution)/shard_map/ppermute | solution.py:313
  3.5 1.6 %collective-permute-start.1 = (bf16[32,512]{1,0:T(8,128)(2,1)}, bf16[32,512]{1,0:T(8,128)(2,1)S(1)}, u32[]{:S(2)}, u32[]{:S(2)}) collective-permute-start(bf16[32,512]{1,0:T(8,128)(2,1)} %feat.1), channel_id=1, source_target_pairs={{0,25},{1,24},{2,27},{3,26},{4,29},{5,28},{6,31},{7,30},{8,17},{9,... | collective-permute-start | bytes 98312 | tf_op jit(solution)/shard_map/ppermute | solution.py:313
  5.1 0.2 collective-permute-start
  5.3 0.7 %copy-done.6 = s32[32,128]{1,0:T(8,128)S(1)} copy-done((s32[32,128]{1,0:T(8,128)S(1)}, s32[32,128]{1,0:T(8,128)}, u32[]{:S(2)}) %copy-start.6) | copy-done | bytes 16408
  6.1 9.2 %gather_slots.1 = (bf16[16,128,512]{2,1,0:T(8,128)(2,1)S(1)}, bf16[16,128,512]{2,1,0:T(8,128)(2,1)S(1)}) custom-call(s32[1]{0:T(128)} %bitcast.1.me_ref, s32[32,128]{1,0:T(8,128)S(1)} %copy-done.6, bf16[4096,512]{1,0:T(8,128)(2,1)} %acct_hbm.1), custom_call_target="tpu_custom_call" | custom-call | bytes 20971520 | tf_op jit(solution)/shard_map/gather_slots/pallas_call | solution.py:94
  15.3 2.5 %collective-permute-start.6 = (bf16[128,512]{1,0:T(8,128)(2,1)S(1)}, bf16[128,512]{1,0:T(8,128)(2,1)S(1)}, u32[]{:S(2)}, u32[]{:S(2)}) collective-permute-start(bf16[128,512]{1,0:T(8,128)(2,1)S(1)} %assemble.1), channel_id=1, source_target_pairs={{0,6},{1,7},{2,4},{3,5},{4,2},{5,3},{6,0},{7,1},{8,14},{9,15},{10,... | collective-permute-start | bytes 393224 | tf_op jit(solution)/shard_map/ppermute | solution.py:313
  17.8 0.5 %collective-permute-start.5 = (bf16[128,512]{1,0:T(8,128)(2,1)S(1)}, bf16[128,512]{1,0:T(8,128)(2,1)S(1)}, u32[]{:S(2)}, u32[]{:S(2)}) collective-permute-start(bf16[128,512]{1,0:T(8,128)(2,1)S(1)} %assemble.1), channel_id=1, source_target_pairs={{0,4},{1,5},{2,6},{3,7},{4,0},{5,1},{6,2},{7,3},{8,12},{9,13},{10,... | collective-permute-start | bytes 393224 | tf_op jit(solution)/shard_map/ppermute | solution.py:313
  18.4 0.5 %collective-permute-start.4 = (bf16[128,512]{1,0:T(8,128)(2,1)S(1)}, bf16[128,512]{1,0:T(8,128)(2,1)S(1)}, u32[]{:S(2)}, u32[]{:S(2)}) collective-permute-start(bf16[128,512]{1,0:T(8,128)(2,1)S(1)} %assemble.1), channel_id=1, source_target_pairs={{0,2},{1,3},{2,0},{3,1},{4,6},{5,7},{6,4},{7,5},{8,10},{9,11},{10,... | collective-permute-start | bytes 393224 | tf_op jit(solution)/shard_map/ppermute | solution.py:313
  18.9 0.0 copy-start.8
  18.9 6.0 %project_slots.2 = (bf16[16,512,128]{2,1,0:T(8,128)(2,1)S(1)}, bf16[16,128,512]{2,1,0:T(8,128)(2,1)S(1)}, bf16[12,512,128]{2,1,0:T(8,128)(2,1)S(1)}, bf16[12,128,512]{2,1,0:T(8,128)(2,1)S(1)}) custom-call(s32[1]{0:T(128)} %bitcast.1.me_ref, s32[32]{0:T(128)S(1)} %copy-done.7, bf16[4,512,512]{2,1,0:T(8,128)(2,1)S(1)} %copy-done.1, ...), custom_call_target="tpu_custom_call" | custom-call | flops 3758096384 | bytes 14680064 | tf_op jit(solution)/shard_map/project_slots/pallas_call | solution.py:145
  25.0 0.1 collective-permute-done.5
  25.0 0.1 collective-permute-done.4
  25.2 0.1 collective-permute-start.7
  25.3 1.5 %aggregate_odd.1 = bf16[512,512]{1,0:T(8,128)(2,1)S(1)} custom-call(s32[1]{0:T(128)} %bitcast.1.me_ref, s32[32]{0:T(128)S(1)} %copy-done.7, s32[32]{0:T(128)S(1)} %copy-done.8, f32[4]{0:T(128)S(1)} %copy-done.9, s32[32,128]{1,0:T(8,128)S(1)} %copy-done.4, bf16[512,512]{1,0:T(8,128)(2,1)S(1)} %pad_maximum_fusion.feats, bf16[512,512]{1,0:T(8,128)(2,1)S(1)} %copy-done, ...), custom_call_target="tpu_custom_call" | custom-call | flops 402653184 | bytes 6291456 | tf_op jit(solution)/shard_map/aggregate_odd/pallas_call | solution.py:205
  26.8 0.5 %collective-permute-start.8 = (bf16[512,512]{1,0:T(8,128)(2,1)S(1)}, bf16[512,512]{1,0:T(8,128)(2,1)S(1)}, u32[]{:S(2)}, u32[]{:S(2)}) collective-permute-start(bf16[512,512]{1,0:T(8,128)(2,1)S(1)} %aggregate_odd.1), channel_id=1, source_target_pairs={{0,1},{1,0},{2,3},{3,2},{4,5},{5,4},{6,7},{7,6},{8,9},{9,8},{10,11... | collective-permute-start | bytes 1572872 | tf_op jit(solution)/shard_map/ppermute | solution.py:313
  27.4 1.3 %aggregate_even.2.mine = f32[384,512]{1,0:T(8,128)S(1)} custom-call(s32[1]{0:T(128)} %bitcast.1.me_ref, s32[32]{0:T(128)S(1)} %copy-done.7, s32[32]{0:T(128)S(1)} %copy-done.8, f32[4]{0:T(128)S(1)} %copy-done.9, s32[32,128]{1,0:T(8,128)S(1)} %copy-done.4, bf16[512,512]{1,0:T(8,128)(2,1)S(1)} %collective-permute-done.7.feats, bf16[512,512]{1,0:T(8,128)(2,1)S(1)} %copy-done, ...), custom_call_target="tpu_custom_call" | custom-call | flops 301989888 | bytes 6291456 | tf_op jit(solution)/shard_map/aggregate_even/pallas_call | solution.py:205
  28.7 0.2 collective-permute-done.8.other
  28.9 0.1 combine_cores.2
  29.0 1.6 %collective-permute-start.11 = (bf16[128,512]{1,0:T(8,128)(2,1)S(1)}, bf16[128,512]{1,0:T(8,128)(2,1)S(1)}, u32[]{:S(2)}, u32[]{:S(2)}) collective-permute-start(bf16[128,512]{1,0:T(8,128)(2,1)S(1)} %get-tuple-element.31), channel_id=1, source_target_pairs={{0,2},{1,3},{2,0},{3,1},{4,6},{5,7},{6,4},{7,5},{8,10},{9,11},{10,... | collective-permute-start | bytes 393224 | tf_op jit(solution)/shard_map/ppermute | solution.py:313
  30.5 1.4 %collective-permute-start.10 = (bf16[128,512]{1,0:T(8,128)(2,1)S(1)}, bf16[128,512]{1,0:T(8,128)(2,1)S(1)}, u32[]{:S(2)}, u32[]{:S(2)}) collective-permute-start(bf16[128,512]{1,0:T(8,128)(2,1)S(1)} %get-tuple-element.32), channel_id=1, source_target_pairs={{0,4},{1,5},{2,6},{3,7},{4,0},{5,1},{6,2},{7,3},{8,12},{9,13},{10,... | collective-permute-start | bytes 393224 | tf_op jit(solution)/shard_map/ppermute | solution.py:313
  31.9 0.6 %collective-permute-start.9 = (bf16[128,512]{1,0:T(8,128)(2,1)S(1)}, bf16[128,512]{1,0:T(8,128)(2,1)S(1)}, u32[]{:S(2)}, u32[]{:S(2)}) collective-permute-start(bf16[128,512]{1,0:T(8,128)(2,1)S(1)} %get-tuple-element.33), channel_id=1, source_target_pairs={{0,6},{1,7},{2,4},{3,5},{4,2},{5,3},{6,0},{7,1},{8,14},{9,15},{10,... | collective-permute-start | bytes 393224 | tf_op jit(solution)/shard_map/ppermute | solution.py:313
  32.5 1.3 %project_slots.3 = (bf16[4,512,128]{2,1,0:T(8,128)(2,1)S(1)}, bf16[4,128,512]{2,1,0:T(8,128)(2,1)S(1)}) custom-call(s32[1]{0:T(128)} %bitcast.1.me_ref, s32[32]{0:T(128)S(1)} %copy-done.7, bf16[4,512,512]{2,1,0:T(8,128)(2,1)S(1)} %copy-done.1, bf16[4,512,512]{2,1,0:T(8,128)(2,1)S(1)} %copy-done.2, bf16[16,128,512]{2,1,0:T(8,128)(2,1)S(1)} %get-tuple-element.25.refs_1_.refs_0_), custom_call_target="tpu_custom_call" | custom-call | flops 536870912 | bytes 2097152 | tf_op jit(solution)/shard_map/project_slots/pallas_call | solution.py:145
  33.9 1.1 %aggregate_even.3.mine = f32[128,512]{1,0:T(8,128)S(1)} custom-call(s32[1]{0:T(128)} %bitcast.1.me_ref, s32[32]{0:T(128)S(1)} %copy-done.7, s32[32]{0:T(128)S(1)} %copy-done.8, f32[4]{0:T(128)S(1)} %copy-done.9, s32[32,128]{1,0:T(8,128)S(1)} %copy-done.4, bf16[512,512]{1,0:T(8,128)(2,1)S(1)} %collective-permute-done.7.feats, bf16[512,512]{1,0:T(8,128)(2,1)S(1)} %copy-done, ...), custom_call_target="tpu_custom_call" | custom-call | flops 100663296 | bytes 6291456 | tf_op jit(solution)/shard_map/aggregate_even/pallas_call | solution.py:205
  35.0 0.1 collective-permute-done.11.refs_3_
  35.2 3.7 %collective-permute-done.10.refs_2_ = bf16[128,512]{1,0:T(8,128)(2,1)S(1)} collective-permute-done((bf16[128,512]{1,0:T(8,128)(2,1)S(1)}, bf16[128,512]{1,0:T(8,128)(2,1)S(1)}, u32[]{:S(2)}, u32[]{:S(2)}) %collective-permute-start.10) | collective-permute-done | bytes 131104 | tf_op jit(solution)/shard_map/ppermute | solution.py:313
  38.8 0.1 combine_plane.1
  38.9 3.0 %collective-permute-start.12 = (bf16[32,512]{1,0:T(8,128)(2,1)S(1)}, bf16[32,512]{1,0:T(8,128)(2,1)S(1)}, u32[]{:S(2)}, u32[]{:S(2)}) collective-permute-start(bf16[32,512]{1,0:T(8,128)(2,1)S(1)} %get-tuple-element.38), channel_id=1, source_target_pairs={{0,24},{1,25},{2,26},{3,27},{4,28},{5,29},{6,30},{7,31},{8,16},{9,... | collective-permute-start | bytes 98312 | tf_op jit(solution)/shard_map/ppermute | solution.py:313
  41.9 0.3 collective-permute-start.13
  42.2 1.1 %collective-permute-start.14 = (bf16[32,512]{1,0:T(8,128)(2,1)S(1)}, bf16[32,512]{1,0:T(8,128)(2,1)S(1)}, u32[]{:S(2)}, u32[]{:S(2)}) collective-permute-start(bf16[32,512]{1,0:T(8,128)(2,1)S(1)} %get-tuple-element.40), channel_id=1, source_target_pairs={{0,8},{1,9},{2,10},{3,11},{4,12},{5,13},{6,14},{7,15},{8,0},{9,1},... | collective-permute-start | bytes 98312 | tf_op jit(solution)/shard_map/ppermute | solution.py:313
  43.4 1.5 %collective-permute-done.12.refs_1_ = bf16[32,512]{1,0:T(8,128)(2,1)S(1)} collective-permute-done((bf16[32,512]{1,0:T(8,128)(2,1)S(1)}, bf16[32,512]{1,0:T(8,128)(2,1)S(1)}, u32[]{:S(2)}, u32[]{:S(2)}) %collective-permute-start.12) | collective-permute-done | bytes 32800 | tf_op jit(solution)/shard_map/ppermute | solution.py:313
  44.9 2.1 %collective-permute-done.13.refs_2_ = bf16[32,512]{1,0:T(8,128)(2,1)S(1)} collective-permute-done((bf16[32,512]{1,0:T(8,128)(2,1)S(1)}, bf16[32,512]{1,0:T(8,128)(2,1)S(1)}, u32[]{:S(2)}, u32[]{:S(2)}) %collective-permute-start.13) | collective-permute-done | bytes 32800 | tf_op jit(solution)/shard_map/ppermute | solution.py:313
  46.9 0.9 %finish.1 = bf16[32,512]{1,0:T(8,128)(2,1)} custom-call(bf16[32,512]{1,0:T(8,128)(2,1)S(1)} %copy-done.5, f32[1,512]{1,0:T(1,128)S(1)} %bitcast.2, bf16[512,512]{1,0:T(8,128)(2,1)S(1)} %copy-done.3, f32[32,512]{1,0:T(8,128)S(1)} %get-tuple-element.37.refs_0_, bf16[32,512]{1,0:T(8,128)(2,1)S(1)} %collective-permute-done.12.refs_1_, ...), custom_call_target="tpu_custom_call" | custom-call | tf_op jit(solution)/shard_map/finish/pallas_call | solution.py:283
  (32 shorter events, 0.2 us)
Async XLA Ops:
  0.0 15.3 %collective-permute-start.2 = (bf16[32,512]{1,0:T(8,128)(2,1)}, bf16[32,512]{1,0:T(8,128)(2,1)S(1)}, u32[]{:S(2)}, u32[]{:S(2)}) collective-permute-start(bf16[32,512]{1,0:T(8,128)(2,1)} %feat.1), channel_id=1, source_target_pairs={{0,17},{1,16},{2,19},{3,18},{4,21},{5,20},{6,23},{7,22},{8,25},{9,... | collective-permute-start | bytes 98312 | tf_op jit(solution)/shard_map/ppermute | solution.py:313
  3.5 11.8 %collective-permute-start.1 = (bf16[32,512]{1,0:T(8,128)(2,1)}, bf16[32,512]{1,0:T(8,128)(2,1)S(1)}, u32[]{:S(2)}, u32[]{:S(2)}) collective-permute-start(bf16[32,512]{1,0:T(8,128)(2,1)} %feat.1), channel_id=1, source_target_pairs={{0,25},{1,24},{2,27},{3,26},{4,29},{5,28},{6,31},{7,30},{8,17},{9,... | collective-permute-start | bytes 98312 | tf_op jit(solution)/shard_map/ppermute | solution.py:313
  5.1 10.2 %collective-permute-start = (bf16[32,512]{1,0:T(8,128)(2,1)}, bf16[32,512]{1,0:T(8,128)(2,1)S(1)}, u32[]{:S(2)}, u32[]{:S(2)}) collective-permute-start(bf16[32,512]{1,0:T(8,128)(2,1)} %feat.1), channel_id=1, source_target_pairs={{0,9},{1,8},{2,11},{3,10},{4,13},{5,12},{6,15},{7,14},{8,1},{9,0},... | collective-permute-start | bytes 98312 | tf_op jit(solution)/shard_map/ppermute | solution.py:313
  5.3 10.0 %collective-permute-start.3 = (bf16[32,512]{1,0:T(8,128)(2,1)}, bf16[32,512]{1,0:T(8,128)(2,1)S(1)}, u32[]{:S(2)}, u32[]{:S(2)}) collective-permute-start(bf16[32,512]{1,0:T(8,128)(2,1)} %feat.1), channel_id=1, source_target_pairs={{0,1},{1,0},{2,3},{3,2},{4,5},{5,4},{6,7},{7,6},{8,9},{9,8},{10,11... | collective-permute-start | bytes 98312 | tf_op jit(solution)/shard_map/ppermute | solution.py:313
  5.3 0.7 %copy-start.6 = (s32[32,128]{1,0:T(8,128)S(1)}, s32[32,128]{1,0:T(8,128)}, u32[]{:S(2)}) copy-start(s32[32,128]{1,0:T(8,128)} %slots_ref.1) | copy-start | bytes 49156
  6.1 12.8 %copy-start.1 = (bf16[4,512,512]{2,1,0:T(8,128)(2,1)S(1)}, bf16[4,512,512]{2,1,0:T(8,128)(2,1)}, u32[]{:S(2)}) copy-start(bf16[4,512,512]{2,1,0:T(8,128)(2,1)} %kw.3) | copy-start | bytes 6291460
  6.1 12.8 %copy-start.2 = (bf16[4,512,512]{2,1,0:T(8,128)(2,1)S(1)}, bf16[4,512,512]{2,1,0:T(8,128)(2,1)}, u32[]{:S(2)}) copy-start(bf16[4,512,512]{2,1,0:T(8,128)(2,1)} %mw.3) | copy-start | bytes 6291460
  6.1 12.8 %copy-start.7 = (s32[32]{0:T(128)S(1)}, s32[32]{0:T(128)}, u32[]{:S(2)}) copy-start(s32[32]{0:T(128)} %rel_ref.9) | copy-start | bytes 388
  15.3 9.6 %collective-permute-start.6 = (bf16[128,512]{1,0:T(8,128)(2,1)S(1)}, bf16[128,512]{1,0:T(8,128)(2,1)S(1)}, u32[]{:S(2)}, u32[]{:S(2)}) collective-permute-start(bf16[128,512]{1,0:T(8,128)(2,1)S(1)} %assemble.1), channel_id=1, source_target_pairs={{0,6},{1,7},{2,4},{3,5},{4,2},{5,3},{6,0},{7,1},{8,14},{9,15},{10,... | collective-permute-start | bytes 393224 | tf_op jit(solution)/shard_map/ppermute | solution.py:313
  17.8 7.2 %collective-permute-start.5 = (bf16[128,512]{1,0:T(8,128)(2,1)S(1)}, bf16[128,512]{1,0:T(8,128)(2,1)S(1)}, u32[]{:S(2)}, u32[]{:S(2)}) collective-permute-start(bf16[128,512]{1,0:T(8,128)(2,1)S(1)} %assemble.1), channel_id=1, source_target_pairs={{0,4},{1,5},{2,6},{3,7},{4,0},{5,1},{6,2},{7,3},{8,12},{9,13},{10,... | collective-permute-start | bytes 393224 | tf_op jit(solution)/shard_map/ppermute | solution.py:313
  18.4 6.8 %collective-permute-start.4 = (bf16[128,512]{1,0:T(8,128)(2,1)S(1)}, bf16[128,512]{1,0:T(8,128)(2,1)S(1)}, u32[]{:S(2)}, u32[]{:S(2)}) collective-permute-start(bf16[128,512]{1,0:T(8,128)(2,1)S(1)} %assemble.1), channel_id=1, source_target_pairs={{0,2},{1,3},{2,0},{3,1},{4,6},{5,7},{6,4},{7,5},{8,10},{9,11},{10,... | collective-permute-start | bytes 393224 | tf_op jit(solution)/shard_map/ppermute | solution.py:313
  18.9 6.3 %copy-start = (bf16[512,512]{1,0:T(8,128)(2,1)S(1)}, bf16[512,512]{1,0:T(8,128)(2,1)}, u32[]{:S(2)}) copy-start(bf16[512,512]{1,0:T(8,128)(2,1)} %wq.5) | copy-start | bytes 1572868
  18.9 6.3 %copy-start.4 = (s32[32,128]{1,0:T(8,128)S(1)}, s32[32,128]{1,0:T(8,128)}, u32[]{:S(2)}) copy-start(s32[32,128]{1,0:T(8,128)} %merch_slot.5) | copy-start | bytes 49156
  18.9 6.3 %copy-start.8 = (s32[32]{0:T(128)S(1)}, s32[32]{0:T(128)}, u32[]{:S(2)}) copy-start(s32[32]{0:T(128)} %count_ref.5) | copy-start | bytes 388
  18.9 6.3 %copy-start.9 = (f32[4]{0:T(128)S(1)}, f32[4]{0:T(128)}, u32[]{:S(2)}) copy-start(f32[4]{0:T(128)} %bias_ref.5) | copy-start | bytes 52
  25.2 2.2 %collective-permute-start.7 = (bf16[512,512]{1,0:T(8,128)(2,1)S(1)}, bf16[512,512]{1,0:T(8,128)(2,1)S(1)}, u32[]{:S(2)}, u32[]{:S(2)}) collective-permute-start(bf16[512,512]{1,0:T(8,128)(2,1)S(1)} %pad_maximum_fusion.feats), channel_id=1, source_target_pairs={{0,1},{1,0},{2,3},{3,2},{4,5},{5,4},{6,7},{7,6},{8,9},{9,8},{10,11... | collective-permute-start | bytes 1572872 | tf_op jit(solution)/shard_map/ppermute | solution.py:313
  26.8 2.1 %collective-permute-start.8 = (bf16[512,512]{1,0:T(8,128)(2,1)S(1)}, bf16[512,512]{1,0:T(8,128)(2,1)S(1)}, u32[]{:S(2)}, u32[]{:S(2)}) collective-permute-start(bf16[512,512]{1,0:T(8,128)(2,1)S(1)} %aggregate_odd.1), channel_id=1, source_target_pairs={{0,1},{1,0},{2,3},{3,2},{4,5},{5,4},{6,7},{7,6},{8,9},{9,8},{10,11... | collective-permute-start | bytes 1572872 | tf_op jit(solution)/shard_map/ppermute | solution.py:313
  29.0 6.2 %collective-permute-start.11 = (bf16[128,512]{1,0:T(8,128)(2,1)S(1)}, bf16[128,512]{1,0:T(8,128)(2,1)S(1)}, u32[]{:S(2)}, u32[]{:S(2)}) collective-permute-start(bf16[128,512]{1,0:T(8,128)(2,1)S(1)} %get-tuple-element.31), channel_id=1, source_target_pairs={{0,2},{1,3},{2,0},{3,1},{4,6},{5,7},{6,4},{7,5},{8,10},{9,11},{10,... | collective-permute-start | bytes 393224 | tf_op jit(solution)/shard_map/ppermute | solution.py:313
  30.5 8.3 %collective-permute-start.10 = (bf16[128,512]{1,0:T(8,128)(2,1)S(1)}, bf16[128,512]{1,0:T(8,128)(2,1)S(1)}, u32[]{:S(2)}, u32[]{:S(2)}) collective-permute-start(bf16[128,512]{1,0:T(8,128)(2,1)S(1)} %get-tuple-element.32), channel_id=1, source_target_pairs={{0,4},{1,5},{2,6},{3,7},{4,0},{5,1},{6,2},{7,3},{8,12},{9,13},{10,... | collective-permute-start | bytes 393224 | tf_op jit(solution)/shard_map/ppermute | solution.py:313
  31.9 6.9 %collective-permute-start.9 = (bf16[128,512]{1,0:T(8,128)(2,1)S(1)}, bf16[128,512]{1,0:T(8,128)(2,1)S(1)}, u32[]{:S(2)}, u32[]{:S(2)}) collective-permute-start(bf16[128,512]{1,0:T(8,128)(2,1)S(1)} %get-tuple-element.33), channel_id=1, source_target_pairs={{0,6},{1,7},{2,4},{3,5},{4,2},{5,3},{6,0},{7,1},{8,14},{9,15},{10,... | collective-permute-start | bytes 393224 | tf_op jit(solution)/shard_map/ppermute | solution.py:313
  33.9 13.1 %copy-start.3 = (bf16[512,512]{1,0:T(8,128)(2,1)S(1)}, bf16[512,512]{1,0:T(8,128)(2,1)}, u32[]{:S(2)}) copy-start(bf16[512,512]{1,0:T(8,128)(2,1)} %wo.1) | copy-start | bytes 1572868
  33.9 13.1 %copy-start.5 = (bf16[32,512]{1,0:T(8,128)(2,1)S(1)}, bf16[32,512]{1,0:T(8,128)(2,1)}, u32[]{:S(2)}) copy-start(bf16[32,512]{1,0:T(8,128)(2,1)} %feat.1) | copy-start | bytes 98308
  33.9 13.1 %copy-start.10 = (f32[512]{0:T(512)S(1)}, f32[512]{0:T(512)}, u32[]{:S(2)}) copy-start(f32[512]{0:T(512)} %param.19) | copy-start | bytes 6148
  38.9 6.0 %collective-permute-start.12 = (bf16[32,512]{1,0:T(8,128)(2,1)S(1)}, bf16[32,512]{1,0:T(8,128)(2,1)S(1)}, u32[]{:S(2)}, u32[]{:S(2)}) collective-permute-start(bf16[32,512]{1,0:T(8,128)(2,1)S(1)} %get-tuple-element.38), channel_id=1, source_target_pairs={{0,24},{1,25},{2,26},{3,27},{4,28},{5,29},{6,30},{7,31},{8,16},{9,... | collective-permute-start | bytes 98312 | tf_op jit(solution)/shard_map/ppermute | solution.py:313
  41.9 5.1 %collective-permute-start.13 = (bf16[32,512]{1,0:T(8,128)(2,1)S(1)}, bf16[32,512]{1,0:T(8,128)(2,1)S(1)}, u32[]{:S(2)}, u32[]{:S(2)}) collective-permute-start(bf16[32,512]{1,0:T(8,128)(2,1)S(1)} %get-tuple-element.39), channel_id=1, source_target_pairs={{0,16},{1,17},{2,18},{3,19},{4,20},{5,21},{6,22},{7,23},{8,24},{9,... | collective-permute-start | bytes 98312 | tf_op jit(solution)/shard_map/ppermute | solution.py:313
  42.2 4.7 %collective-permute-start.14 = (bf16[32,512]{1,0:T(8,128)(2,1)S(1)}, bf16[32,512]{1,0:T(8,128)(2,1)S(1)}, u32[]{:S(2)}, u32[]{:S(2)}) collective-permute-start(bf16[32,512]{1,0:T(8,128)(2,1)S(1)} %get-tuple-element.40), channel_id=1, source_target_pairs={{0,8},{1,9},{2,10},{3,11},{4,12},{5,13},{6,14},{7,15},{8,0},{9,1},... | collective-permute-start | bytes 98312 | tf_op jit(solution)/shard_map/ppermute | solution.py:313

commit v21 on v20

--- a/solution.py
+++ b/solution.py
@@ -221,7 +221,7 @@
 
 def combine_kernel(skip, mine, other, *outs):
     rows = outs[0].shape[0]
-    for j, out in enumerate(outs):
+    for j, out in enumerate(reversed(outs)):
         part = slice(j * rows, (j + 1) * rows)
         theirs = slice(skip + j * rows, skip + (j + 1) * rows)
         out[...] = (mine[part, :] + other[theirs, :].astype(F32)).astype(out.dtype)
@@ -345,7 +345,7 @@
     )
     (near,) = combine(1, 0, near, other, F32)
     parts = combine_plane(
-        outer, [near] + [swap(parts[j - 1], 2 * j) for j in reversed(range(1, inner))]
+        outer, [near] + [swap(parts[inner - 1 - j], 2 * j) for j in reversed(range(1, inner))]
     )
     parts = [parts[0]] + [swap(parts[k], 8 * k) for k in reversed(range(1, outer))]
     return finish(merch_feat, out_gain, out_weight, parts)

time: 48.1 us -> 47.9 us (level)
  no operation moved by 1% of the time
where the time goes in v21:
time: 47.9 us; the launch traced here: 47.7 us
  Pallas kernels  21.6 us (45%)
  starting transfers between devices  17.5 us (37%)
  waiting for transfers between devices  7.56 us (16%)
  local copies, waits for them, and re-layouts  0.77 us (2%)
    ppermute x15, starting transfers between devices, swap(): return lax.ppermute(value, AXES, [(s, s ^ mask) for s in range(devices)])  17.5 us
    pallas_call x1, Pallas kernels, gather(): pl.pallas_call(functools.partial(gather_kernel, outer), out_shape=(half,...  9.2 us
    ppermute x15, waiting for transfers between devices, swap(): return lax.ppermute(value, AXES, [(s, s ^ mask) for s in range(devices)])  7.56 us
    pallas_call x2, Pallas kernels, project(): pl.pallas_call(functools.partial(project_kernel, outer, spans), out_shape...  7.32 us
    pallas_call x3, Pallas kernels, aggregate(): pl.pallas_call(functools.partial(aggregate_kernel, outer, first, shift),...  3.97 us
  transfers between devices with their start and end apart: 15, of which 6 were waited for; matrix products, arithmetic and copies ran while one was open for 0% of the time, Pallas kernels for 43%

profile of v21, /device:TPU:0, one launch (start us, length us, event | category | flops | bytes accessed | tf_op | source)
XLA Modules:
  0.0 47.7 jit_solution(14303676636115508753)
XLA Ops:
  0.0 3.5 %collective-permute-start.2 = (bf16[32,512]{1,0:T(8,128)(2,1)}, bf16[32,512]{1,0:T(8,128)(2,1)S(1)}, u32[]{:S(2)}, u32[]{:S(2)}) collective-permute-start(bf16[32,512]{1,0:T(8,128)(2,1)} %feat.1), channel_id=1, source_target_pairs={{0,17},{1,16},{2,19},{3,18},{4,21},{5,20},{6,23},{7,22},{8,25},{9,... | collective-permute-start | bytes 98312 | tf_op jit(solution)/shard_map/ppermute | solution.py:313
  3.5 1.6 %collective-permute-start.1 = (bf16[32,512]{1,0:T(8,128)(2,1)}, bf16[32,512]{1,0:T(8,128)(2,1)S(1)}, u32[]{:S(2)}, u32[]{:S(2)}) collective-permute-start(bf16[32,512]{1,0:T(8,128)(2,1)} %feat.1), channel_id=1, source_target_pairs={{0,25},{1,24},{2,27},{3,26},{4,29},{5,28},{6,31},{7,30},{8,17},{9,... | collective-permute-start | bytes 98312 | tf_op jit(solution)/shard_map/ppermute | solution.py:313
  5.1 0.2 collective-permute-start
  5.3 0.7 %copy-done.6 = s32[32,128]{1,0:T(8,128)S(1)} copy-done((s32[32,128]{1,0:T(8,128)S(1)}, s32[32,128]{1,0:T(8,128)}, u32[]{:S(2)}) %copy-start.6) | copy-done | bytes 16408
  6.1 9.2 %gather_slots.1 = (bf16[16,128,512]{2,1,0:T(8,128)(2,1)S(1)}, bf16[16,128,512]{2,1,0:T(8,128)(2,1)S(1)}) custom-call(s32[1]{0:T(128)} %bitcast.1.me_ref, s32[32,128]{1,0:T(8,128)S(1)} %copy-done.6, bf16[4096,512]{1,0:T(8,128)(2,1)} %acct_hbm.1), custom_call_target="tpu_custom_call" | custom-call | bytes 20971520 | tf_op jit(solution)/shard_map/gather_slots/pallas_call | solution.py:94
  15.3 2.5 %collective-permute-start.6 = (bf16[128,512]{1,0:T(8,128)(2,1)S(1)}, bf16[128,512]{1,0:T(8,128)(2,1)S(1)}, u32[]{:S(2)}, u32[]{:S(2)}) collective-permute-start(bf16[128,512]{1,0:T(8,128)(2,1)S(1)} %assemble.1), channel_id=1, source_target_pairs={{0,6},{1,7},{2,4},{3,5},{4,2},{5,3},{6,0},{7,1},{8,14},{9,15},{10,... | collective-permute-start | bytes 393224 | tf_op jit(solution)/shard_map/ppermute | solution.py:313
  17.8 0.5 %collective-permute-start.5 = (bf16[128,512]{1,0:T(8,128)(2,1)S(1)}, bf16[128,512]{1,0:T(8,128)(2,1)S(1)}, u32[]{:S(2)}, u32[]{:S(2)}) collective-permute-start(bf16[128,512]{1,0:T(8,128)(2,1)S(1)} %assemble.1), channel_id=1, source_target_pairs={{0,4},{1,5},{2,6},{3,7},{4,0},{5,1},{6,2},{7,3},{8,12},{9,13},{10,... | collective-permute-start | bytes 393224 | tf_op jit(solution)/shard_map/ppermute | solution.py:313
  18.4 0.5 %collective-permute-start.4 = (bf16[128,512]{1,0:T(8,128)(2,1)S(1)}, bf16[128,512]{1,0:T(8,128)(2,1)S(1)}, u32[]{:S(2)}, u32[]{:S(2)}) collective-permute-start(bf16[128,512]{1,0:T(8,128)(2,1)S(1)} %assemble.1), channel_id=1, source_target_pairs={{0,2},{1,3},{2,0},{3,1},{4,6},{5,7},{6,4},{7,5},{8,10},{9,11},{10,... | collective-permute-start | bytes 393224 | tf_op jit(solution)/shard_map/ppermute | solution.py:313
  18.9 0.0 copy-start.4
  18.9 6.0 %project_slots.2 = (bf16[16,512,128]{2,1,0:T(8,128)(2,1)S(1)}, bf16[16,128,512]{2,1,0:T(8,128)(2,1)S(1)}, bf16[12,512,128]{2,1,0:T(8,128)(2,1)S(1)}, bf16[12,128,512]{2,1,0:T(8,128)(2,1)S(1)}) custom-call(s32[1]{0:T(128)} %bitcast.1.me_ref, s32[32]{0:T(128)S(1)} %copy-done.7, bf16[4,512,512]{2,1,0:T(8,128)(2,1)S(1)} %copy-done.1, ...), custom_call_target="tpu_custom_call" | custom-call | flops 3758096384 | bytes 14680064 | tf_op jit(solution)/shard_map/project_slots/pallas_call | solution.py:145
  25.0 0.0 collective-permute-done.5
  25.0 0.1 collective-permute-done.4
  25.2 0.1 collective-permute-start.7
  25.3 1.5 %aggregate_odd.1 = bf16[512,512]{1,0:T(8,128)(2,1)S(1)} custom-call(s32[1]{0:T(128)} %bitcast.1.me_ref, s32[32]{0:T(128)S(1)} %copy-done.7, s32[32]{0:T(128)S(1)} %copy-done.8, f32[4]{0:T(128)S(1)} %copy-done.9, s32[32,128]{1,0:T(8,128)S(1)} %copy-done.4, bf16[512,512]{1,0:T(8,128)(2,1)S(1)} %pad_maximum_fusion.feats, bf16[512,512]{1,0:T(8,128)(2,1)S(1)} %copy-done, ...), custom_call_target="tpu_custom_call" | custom-call | flops 402653184 | bytes 6291456 | tf_op jit(solution)/shard_map/aggregate_odd/pallas_call | solution.py:205
  26.8 0.5 %collective-permute-start.8 = (bf16[512,512]{1,0:T(8,128)(2,1)S(1)}, bf16[512,512]{1,0:T(8,128)(2,1)S(1)}, u32[]{:S(2)}, u32[]{:S(2)}) collective-permute-start(bf16[512,512]{1,0:T(8,128)(2,1)S(1)} %aggregate_odd.1), channel_id=1, source_target_pairs={{0,1},{1,0},{2,3},{3,2},{4,5},{5,4},{6,7},{7,6},{8,9},{9,8},{10,11... | collective-permute-start | bytes 1572872 | tf_op jit(solution)/shard_map/ppermute | solution.py:313
  27.4 1.3 %aggregate_even.2.mine = f32[384,512]{1,0:T(8,128)S(1)} custom-call(s32[1]{0:T(128)} %bitcast.1.me_ref, s32[32]{0:T(128)S(1)} %copy-done.7, s32[32]{0:T(128)S(1)} %copy-done.8, f32[4]{0:T(128)S(1)} %copy-done.9, s32[32,128]{1,0:T(8,128)S(1)} %copy-done.4, bf16[512,512]{1,0:T(8,128)(2,1)S(1)} %collective-permute-done.7.feats, bf16[512,512]{1,0:T(8,128)(2,1)S(1)} %copy-done, ...), custom_call_target="tpu_custom_call" | custom-call | flops 301989888 | bytes 6291456 | tf_op jit(solution)/shard_map/aggregate_even/pallas_call | solution.py:205
  28.7 0.2 collective-permute-done.8.other
  28.9 0.1 combine_cores.2
  29.0 2.4 %collective-permute-start.9 = (bf16[128,512]{1,0:T(8,128)(2,1)S(1)}, bf16[128,512]{1,0:T(8,128)(2,1)S(1)}, u32[]{:S(2)}, u32[]{:S(2)}) collective-permute-start(bf16[128,512]{1,0:T(8,128)(2,1)S(1)} %get-tuple-element.31), channel_id=1, source_target_pairs={{0,6},{1,7},{2,4},{3,5},{4,2},{5,3},{6,0},{7,1},{8,14},{9,15},{10,... | collective-permute-start | bytes 393224 | tf_op jit(solution)/shard_map/ppermute | solution.py:313
  31.4 0.6 %collective-permute-start.10 = (bf16[128,512]{1,0:T(8,128)(2,1)S(1)}, bf16[128,512]{1,0:T(8,128)(2,1)S(1)}, u32[]{:S(2)}, u32[]{:S(2)}) collective-permute-start(bf16[128,512]{1,0:T(8,128)(2,1)S(1)} %get-tuple-element.32), channel_id=1, source_target_pairs={{0,4},{1,5},{2,6},{3,7},{4,0},{5,1},{6,2},{7,3},{8,12},{9,13},{10,... | collective-permute-start | bytes 393224 | tf_op jit(solution)/shard_map/ppermute | solution.py:313
  32.0 0.5 %collective-permute-start.11 = (bf16[128,512]{1,0:T(8,128)(2,1)S(1)}, bf16[128,512]{1,0:T(8,128)(2,1)S(1)}, u32[]{:S(2)}, u32[]{:S(2)}) collective-permute-start(bf16[128,512]{1,0:T(8,128)(2,1)S(1)} %get-tuple-element.33), channel_id=1, source_target_pairs={{0,2},{1,3},{2,0},{3,1},{4,6},{5,7},{6,4},{7,5},{8,10},{9,11},{10,... | collective-permute-start | bytes 393224 | tf_op jit(solution)/shard_map/ppermute | solution.py:313
  32.5 1.3 %project_slots.3 = (bf16[4,512,128]{2,1,0:T(8,128)(2,1)S(1)}, bf16[4,128,512]{2,1,0:T(8,128)(2,1)S(1)}) custom-call(s32[1]{0:T(128)} %bitcast.1.me_ref, s32[32]{0:T(128)S(1)} %copy-done.7, bf16[4,512,512]{2,1,0:T(8,128)(2,1)S(1)} %copy-done.1, bf16[4,512,512]{2,1,0:T(8,128)(2,1)S(1)} %copy-done.2, bf16[16,128,512]{2,1,0:T(8,128)(2,1)S(1)} %get-tuple-element.25.refs_1_.refs_0_), custom_call_target="tpu_custom_call" | custom-call | flops 536870912 | bytes 2097152 | tf_op jit(solution)/shard_map/project_slots/pallas_call | solution.py:145
  33.9 1.1 %aggregate_even.3.mine = f32[128,512]{1,0:T(8,128)S(1)} custom-call(s32[1]{0:T(128)} %bitcast.1.me_ref, s32[32]{0:T(128)S(1)} %copy-done.7, s32[32]{0:T(128)S(1)} %copy-done.8, f32[4]{0:T(128)S(1)} %copy-done.9, s32[32,128]{1,0:T(8,128)S(1)} %copy-done.4, bf16[512,512]{1,0:T(8,128)(2,1)S(1)} %collective-permute-done.7.feats, bf16[512,512]{1,0:T(8,128)(2,1)S(1)} %copy-done, ...), custom_call_target="tpu_custom_call" | custom-call | flops 100663296 | bytes 6291456 | tf_op jit(solution)/shard_map/aggregate_even/pallas_call | solution.py:205
  35.0 1.1 %collective-permute-done.9.refs_1_ = bf16[128,512]{1,0:T(8,128)(2,1)S(1)} collective-permute-done((bf16[128,512]{1,0:T(8,128)(2,1)S(1)}, bf16[128,512]{1,0:T(8,128)(2,1)S(1)}, u32[]{:S(2)}, u32[]{:S(2)}) %collective-permute-start.9) | collective-permute-done | bytes 131104 | tf_op jit(solution)/shard_map/ppermute | solution.py:313
  36.1 2.4 %collective-permute-done.10.refs_2_ = bf16[128,512]{1,0:T(8,128)(2,1)S(1)} collective-permute-done((bf16[128,512]{1,0:T(8,128)(2,1)S(1)}, bf16[128,512]{1,0:T(8,128)(2,1)S(1)}, u32[]{:S(2)}, u32[]{:S(2)}) %collective-permute-start.10) | collective-permute-done | bytes 131104 | tf_op jit(solution)/shard_map/ppermute | solution.py:313
  38.5 0.1 combine_plane.1
  38.6 3.1 %collective-permute-start.12 = (bf16[32,512]{1,0:T(8,128)(2,1)S(1)}, bf16[32,512]{1,0:T(8,128)(2,1)S(1)}, u32[]{:S(2)}, u32[]{:S(2)}) collective-permute-start(bf16[32,512]{1,0:T(8,128)(2,1)S(1)} %get-tuple-element.38), channel_id=1, source_target_pairs={{0,24},{1,25},{2,26},{3,27},{4,28},{5,29},{6,30},{7,31},{8,16},{9,... | collective-permute-start | bytes 98312 | tf_op jit(solution)/shard_map/ppermute | solution.py:313
  41.7 0.3 collective-permute-start.13
  42.0 1.0 %collective-permute-start.14 = (bf16[32,512]{1,0:T(8,128)(2,1)S(1)}, bf16[32,512]{1,0:T(8,128)(2,1)S(1)}, u32[]{:S(2)}, u32[]{:S(2)}) collective-permute-start(bf16[32,512]{1,0:T(8,128)(2,1)S(1)} %get-tuple-element.40), channel_id=1, source_target_pairs={{0,8},{1,9},{2,10},{3,11},{4,12},{5,13},{6,14},{7,15},{8,0},{9,1},... | collective-permute-start | bytes 98312 | tf_op jit(solution)/shard_map/ppermute | solution.py:313
  43.0 1.4 %collective-permute-done.12.refs_1_ = bf16[32,512]{1,0:T(8,128)(2,1)S(1)} collective-permute-done((bf16[32,512]{1,0:T(8,128)(2,1)S(1)}, bf16[32,512]{1,0:T(8,128)(2,1)S(1)}, u32[]{:S(2)}, u32[]{:S(2)}) %collective-permute-start.12) | collective-permute-done | bytes 32800 | tf_op jit(solution)/shard_map/ppermute | solution.py:313
  44.5 2.3 %collective-permute-done.13.refs_2_ = bf16[32,512]{1,0:T(8,128)(2,1)S(1)} collective-permute-done((bf16[32,512]{1,0:T(8,128)(2,1)S(1)}, bf16[32,512]{1,0:T(8,128)(2,1)S(1)}, u32[]{:S(2)}, u32[]{:S(2)}) %collective-permute-start.13) | collective-permute-done | bytes 32800 | tf_op jit(solution)/shard_map/ppermute | solution.py:313
  46.8 0.9 %finish.1 = bf16[32,512]{1,0:T(8,128)(2,1)} custom-call(bf16[32,512]{1,0:T(8,128)(2,1)S(1)} %copy-done.5, f32[1,512]{1,0:T(1,128)S(1)} %bitcast.2, bf16[512,512]{1,0:T(8,128)(2,1)S(1)} %copy-done.3, f32[32,512]{1,0:T(8,128)S(1)} %get-tuple-element.37.refs_0_, bf16[32,512]{1,0:T(8,128)(2,1)S(1)} %collective-permute-done.12.refs_1_, ...), custom_call_target="tpu_custom_call" | custom-call | tf_op jit(solution)/shard_map/finish/pallas_call | solution.py:283
  (32 shorter events, 0.2 us)
Async XLA Ops:
  0.0 15.3 %collective-permute-start.2 = (bf16[32,512]{1,0:T(8,128)(2,1)}, bf16[32,512]{1,0:T(8,128)(2,1)S(1)}, u32[]{:S(2)}, u32[]{:S(2)}) collective-permute-start(bf16[32,512]{1,0:T(8,128)(2,1)} %feat.1), channel_id=1, source_target_pairs={{0,17},{1,16},{2,19},{3,18},{4,21},{5,20},{6,23},{7,22},{8,25},{9,... | collective-permute-start | bytes 98312 | tf_op jit(solution)/shard_map/ppermute | solution.py:313
  3.5 11.8 %collective-permute-start.1 = (bf16[32,512]{1,0:T(8,128)(2,1)}, bf16[32,512]{1,0:T(8,128)(2,1)S(1)}, u32[]{:S(2)}, u32[]{:S(2)}) collective-permute-start(bf16[32,512]{1,0:T(8,128)(2,1)} %feat.1), channel_id=1, source_target_pairs={{0,25},{1,24},{2,27},{3,26},{4,29},{5,28},{6,31},{7,30},{8,17},{9,... | collective-permute-start | bytes 98312 | tf_op jit(solution)/shard_map/ppermute | solution.py:313
  5.1 10.2 %collective-permute-start = (bf16[32,512]{1,0:T(8,128)(2,1)}, bf16[32,512]{1,0:T(8,128)(2,1)S(1)}, u32[]{:S(2)}, u32[]{:S(2)}) collective-permute-start(bf16[32,512]{1,0:T(8,128)(2,1)} %feat.1), channel_id=1, source_target_pairs={{0,9},{1,8},{2,11},{3,10},{4,13},{5,12},{6,15},{7,14},{8,1},{9,0},... | collective-permute-start | bytes 98312 | tf_op jit(solution)/shard_map/ppermute | solution.py:313
  5.3 10.0 %collective-permute-start.3 = (bf16[32,512]{1,0:T(8,128)(2,1)}, bf16[32,512]{1,0:T(8,128)(2,1)S(1)}, u32[]{:S(2)}, u32[]{:S(2)}) collective-permute-start(bf16[32,512]{1,0:T(8,128)(2,1)} %feat.1), channel_id=1, source_target_pairs={{0,1},{1,0},{2,3},{3,2},{4,5},{5,4},{6,7},{7,6},{8,9},{9,8},{10,11... | collective-permute-start | bytes 98312 | tf_op jit(solution)/shard_map/ppermute | solution.py:313
  5.3 0.7 %copy-start.6 = (s32[32,128]{1,0:T(8,128)S(1)}, s32[32,128]{1,0:T(8,128)}, u32[]{:S(2)}) copy-start(s32[32,128]{1,0:T(8,128)} %slots_ref.1) | copy-start | bytes 49156
  6.1 12.8 %copy-start.1 = (bf16[4,512,512]{2,1,0:T(8,128)(2,1)S(1)}, bf16[4,512,512]{2,1,0:T(8,128)(2,1)}, u32[]{:S(2)}) copy-start(bf16[4,512,512]{2,1,0:T(8,128)(2,1)} %kw.3) | copy-start | bytes 6291460
  6.1 12.8 %copy-start.2 = (bf16[4,512,512]{2,1,0:T(8,128)(2,1)S(1)}, bf16[4,512,512]{2,1,0:T(8,128)(2,1)}, u32[]{:S(2)}) copy-start(bf16[4,512,512]{2,1,0:T(8,128)(2,1)} %mw.3) | copy-start | bytes 6291460
  6.1 12.8 %copy-start.7 = (s32[32]{0:T(128)S(1)}, s32[32]{0:T(128)}, u32[]{:S(2)}) copy-start(s32[32]{0:T(128)} %rel_ref.9) | copy-start | bytes 388
  15.3 9.6 %collective-permute-start.6 = (bf16[128,512]{1,0:T(8,128)(2,1)S(1)}, bf16[128,512]{1,0:T(8,128)(2,1)S(1)}, u32[]{:S(2)}, u32[]{:S(2)}) collective-permute-start(bf16[128,512]{1,0:T(8,128)(2,1)S(1)} %assemble.1), channel_id=1, source_target_pairs={{0,6},{1,7},{2,4},{3,5},{4,2},{5,3},{6,0},{7,1},{8,14},{9,15},{10,... | collective-permute-start | bytes 393224 | tf_op jit(solution)/shard_map/ppermute | solution.py:313
  17.8 7.2 %collective-permute-start.5 = (bf16[128,512]{1,0:T(8,128)(2,1)S(1)}, bf16[128,512]{1,0:T(8,128)(2,1)S(1)}, u32[]{:S(2)}, u32[]{:S(2)}) collective-permute-start(bf16[128,512]{1,0:T(8,128)(2,1)S(1)} %assemble.1), channel_id=1, source_target_pairs={{0,4},{1,5},{2,6},{3,7},{4,0},{5,1},{6,2},{7,3},{8,12},{9,13},{10,... | collective-permute-start | bytes 393224 | tf_op jit(solution)/shard_map/ppermute | solution.py:313
  18.4 6.8 %collective-permute-start.4 = (bf16[128,512]{1,0:T(8,128)(2,1)S(1)}, bf16[128,512]{1,0:T(8,128)(2,1)S(1)}, u32[]{:S(2)}, u32[]{:S(2)}) collective-permute-start(bf16[128,512]{1,0:T(8,128)(2,1)S(1)} %assemble.1), channel_id=1, source_target_pairs={{0,2},{1,3},{2,0},{3,1},{4,6},{5,7},{6,4},{7,5},{8,10},{9,11},{10,... | collective-permute-start | bytes 393224 | tf_op jit(solution)/shard_map/ppermute | solution.py:313
  18.9 6.3 %copy-start = (bf16[512,512]{1,0:T(8,128)(2,1)S(1)}, bf16[512,512]{1,0:T(8,128)(2,1)}, u32[]{:S(2)}) copy-start(bf16[512,512]{1,0:T(8,128)(2,1)} %wq.5) | copy-start | bytes 1572868
  18.9 6.3 %copy-start.4 = (s32[32,128]{1,0:T(8,128)S(1)}, s32[32,128]{1,0:T(8,128)}, u32[]{:S(2)}) copy-start(s32[32,128]{1,0:T(8,128)} %merch_slot.5) | copy-start | bytes 49156
  18.9 6.3 %copy-start.8 = (s32[32]{0:T(128)S(1)}, s32[32]{0:T(128)}, u32[]{:S(2)}) copy-start(s32[32]{0:T(128)} %count_ref.5) | copy-start | bytes 388
  18.9 6.3 %copy-start.9 = (f32[4]{0:T(128)S(1)}, f32[4]{0:T(128)}, u32[]{:S(2)}) copy-start(f32[4]{0:T(128)} %bias_ref.5) | copy-start | bytes 52
  25.2 2.2 %collective-permute-start.7 = (bf16[512,512]{1,0:T(8,128)(2,1)S(1)}, bf16[512,512]{1,0:T(8,128)(2,1)S(1)}, u32[]{:S(2)}, u32[]{:S(2)}) collective-permute-start(bf16[512,512]{1,0:T(8,128)(2,1)S(1)} %pad_maximum_fusion.feats), channel_id=1, source_target_pairs={{0,1},{1,0},{2,3},{3,2},{4,5},{5,4},{6,7},{7,6},{8,9},{9,8},{10,11... | collective-permute-start | bytes 1572872 | tf_op jit(solution)/shard_map/ppermute | solution.py:313
  26.8 2.1 %collective-permute-start.8 = (bf16[512,512]{1,0:T(8,128)(2,1)S(1)}, bf16[512,512]{1,0:T(8,128)(2,1)S(1)}, u32[]{:S(2)}, u32[]{:S(2)}) collective-permute-start(bf16[512,512]{1,0:T(8,128)(2,1)S(1)} %aggregate_odd.1), channel_id=1, source_target_pairs={{0,1},{1,0},{2,3},{3,2},{4,5},{5,4},{6,7},{7,6},{8,9},{9,8},{10,11... | collective-permute-start | bytes 1572872 | tf_op jit(solution)/shard_map/ppermute | solution.py:313
  29.0 7.2 %collective-permute-start.9 = (bf16[128,512]{1,0:T(8,128)(2,1)S(1)}, bf16[128,512]{1,0:T(8,128)(2,1)S(1)}, u32[]{:S(2)}, u32[]{:S(2)}) collective-permute-start(bf16[128,512]{1,0:T(8,128)(2,1)S(1)} %get-tuple-element.31), channel_id=1, source_target_pairs={{0,6},{1,7},{2,4},{3,5},{4,2},{5,3},{6,0},{7,1},{8,14},{9,15},{10,... | collective-permute-start | bytes 393224 | tf_op jit(solution)/shard_map/ppermute | solution.py:313
  31.4 7.2 %collective-permute-start.10 = (bf16[128,512]{1,0:T(8,128)(2,1)S(1)}, bf16[128,512]{1,0:T(8,128)(2,1)S(1)}, u32[]{:S(2)}, u32[]{:S(2)}) collective-permute-start(bf16[128,512]{1,0:T(8,128)(2,1)S(1)} %get-tuple-element.32), channel_id=1, source_target_pairs={{0,4},{1,5},{2,6},{3,7},{4,0},{5,1},{6,2},{7,3},{8,12},{9,13},{10,... | collective-permute-start | bytes 393224 | tf_op jit(solution)/shard_map/ppermute | solution.py:313
  32.0 6.5 %collective-permute-start.11 = (bf16[128,512]{1,0:T(8,128)(2,1)S(1)}, bf16[128,512]{1,0:T(8,128)(2,1)S(1)}, u32[]{:S(2)}, u32[]{:S(2)}) collective-permute-start(bf16[128,512]{1,0:T(8,128)(2,1)S(1)} %get-tuple-element.33), channel_id=1, source_target_pairs={{0,2},{1,3},{2,0},{3,1},{4,6},{5,7},{6,4},{7,5},{8,10},{9,11},{10,... | collective-permute-start | bytes 393224 | tf_op jit(solution)/shard_map/ppermute | solution.py:313
  33.9 12.9 %copy-start.3 = (bf16[512,512]{1,0:T(8,128)(2,1)S(1)}, bf16[512,512]{1,0:T(8,128)(2,1)}, u32[]{:S(2)}) copy-start(bf16[512,512]{1,0:T(8,128)(2,1)} %wo.1) | copy-start | bytes 1572868
  33.9 12.9 %copy-start.5 = (bf16[32,512]{1,0:T(8,128)(2,1)S(1)}, bf16[32,512]{1,0:T(8,128)(2,1)}, u32[]{:S(2)}) copy-start(bf16[32,512]{1,0:T(8,128)(2,1)} %feat.1) | copy-start | bytes 98308
  33.9 12.9 %copy-start.10 = (f32[512]{0:T(512)S(1)}, f32[512]{0:T(512)}, u32[]{:S(2)}) copy-start(f32[512]{0:T(512)} %param.19) | copy-start | bytes 6148
  38.6 5.9 %collective-permute-start.12 = (bf16[32,512]{1,0:T(8,128)(2,1)S(1)}, bf16[32,512]{1,0:T(8,128)(2,1)S(1)}, u32[]{:S(2)}, u32[]{:S(2)}) collective-permute-start(bf16[32,512]{1,0:T(8,128)(2,1)S(1)} %get-tuple-element.38), channel_id=1, source_target_pairs={{0,24},{1,25},{2,26},{3,27},{4,28},{5,29},{6,30},{7,31},{8,16},{9,... | collective-permute-start | bytes 98312 | tf_op jit(solution)/shard_map/ppermute | solution.py:313
  41.7 5.1 %collective-permute-start.13 = (bf16[32,512]{1,0:T(8,128)(2,1)S(1)}, bf16[32,512]{1,0:T(8,128)(2,1)S(1)}, u32[]{:S(2)}, u32[]{:S(2)}) collective-permute-start(bf16[32,512]{1,0:T(8,128)(2,1)S(1)} %get-tuple-element.39), channel_id=1, source_target_pairs={{0,16},{1,17},{2,18},{3,19},{4,20},{5,21},{6,22},{7,23},{8,24},{9,... | collective-permute-start | bytes 98312 | tf_op jit(solution)/shard_map/ppermute | solution.py:313
  42.0 4.8 %collective-permute-start.14 = (bf16[32,512]{1,0:T(8,128)(2,1)S(1)}, bf16[32,512]{1,0:T(8,128)(2,1)S(1)}, u32[]{:S(2)}, u32[]{:S(2)}) collective-permute-start(bf16[32,512]{1,0:T(8,128)(2,1)S(1)} %get-tuple-element.40), channel_id=1, source_target_pairs={{0,8},{1,9},{2,10},{3,11},{4,12},{5,13},{6,14},{7,15},{8,0},{9,1},... | collective-permute-start | bytes 98312 | tf_op jit(solution)/shard_map/ppermute | solution.py:313

commit v22 on v21

--- a/solution.py
+++ b/solution.py
@@ -32,7 +32,7 @@
 
 
 def gather_kernel(
-    outer, me_ref, slots_ref, acct_hbm, odd, even, acct, table, rows0, rows1, sem
+    outer, me_ref, slots_ref, acct_hbm, odd, far, acct, table, rows0, rows1, sem
 ):
     accounts, width = acct.shape
     blocks, block_len, _ = odd.shape
@@ -75,13 +75,22 @@
                 pl.ds(c, block_len, stride=parts), :
             ].astype(BF16)
 
-    @pl.loop(0, blocks)
+    def odd_block(i):
+        return jnp.bitwise_xor(me, _offset(i, outer) + 1)
+
+    @pl.loop(0, outer // 2)
+    def _(h):
+        collect(odd_block(2 * h), rows0)
+        collect(odd_block(2 * h + 1), rows1)
+        emit(2 * h, rows0, odd)
+        emit(2 * h + 1, rows1, odd)
+
+    @pl.loop(outer, blocks)
     def _(i):
-        offset = _offset(i, outer)
-        collect(jnp.bitwise_xor(me, offset + 1), rows0)
-        collect(jnp.bitwise_xor(me, offset), rows1)
+        collect(odd_block(i), rows0)
+        collect(jnp.bitwise_xor(me, _offset(i, outer)), rows1)
         emit(i, rows0, odd)
-        emit(i, rows1, even)
+        emit(i - outer, rows1, far)
 
 
 def gather(outer, me, slots, acct):
@@ -90,10 +99,13 @@
     parts = width // LANES
     pitch = -(-parts // 8) * 8
     rows = pltpu.VMEM((block_len * parts, LANES), F32)
-    half = jax.ShapeDtypeStruct((blocks // 2, block_len, width), BF16)
+    half = blocks // 2
     return pl.pallas_call(
         functools.partial(gather_kernel, outer),
-        out_shape=(half, half),
+        out_shape=(
+            jax.ShapeDtypeStruct((half, block_len, width), BF16),
+            jax.ShapeDtypeStruct((half - outer, block_len, width), BF16),
+        ),
         in_specs=[SMEM, SMEM, ANY],
         out_specs=(VMEM, VMEM),
         scratch_shapes=[
@@ -109,6 +121,43 @@
     )(me, slots, acct)
 
 
+def pick_kernel(outer, me_ref, slots, acct, out, index):
+    accounts, width = acct.shape
+    block_len = slots.shape[1]
+    span = 512
+    me = me_ref[0]
+    index[...] = jnp.zeros_like(index)
+    for i in range(outer):
+        block = jnp.bitwise_xor(me, 8 * i)
+        index[pl.ds(i, 1), :] = slots[pl.ds(block, 1), :].astype(F32)
+    column = index[...].T
+    for i in range(outer):
+        mine = column[:, i : i + 1]
+        lane = lax.broadcasted_iota(jnp.int32, (block_len, span), 1).astype(F32)
+        total = jnp.zeros((block_len, width), F32)
+        for first in range(0, accounts, span):
+            hot = jnp.where(mine - first == lane, 1.0, 0.0).astype(BF16)
+            total = total + jnp.dot(
+                hot, acct[first : first + span, :], preferred_element_type=F32
+            )
+        out[i] = total.astype(BF16)
+
+
+def pick(outer, me, slots, acct):
+    block_len = slots.shape[1]
+    width = acct.shape[1]
+    return pl.pallas_call(
+        functools.partial(pick_kernel, outer),
+        out_shape=jax.ShapeDtypeStruct((outer, block_len, width), BF16),
+        in_specs=[SMEM, VMEM, VMEM],
+        out_specs=VMEM,
+        scratch_shapes=[pltpu.VMEM((block_len, block_len), F32)],
+        compiler_params=_mb(8),
+        cost_estimate=_cost(2 * outer * block_len * acct.size, 8 * 2**20),
+        name="pick_rows",
+    )(me, slots, acct)
+
+
 def project_kernel(outer, spans, me_ref, rel_ref, kw, mw, *refs):
     width = refs[0].shape[2]
     half = width // 2
@@ -119,11 +168,11 @@
         relation = rel_ref[jnp.bitwise_xor(me, _offset(first + i, outer) + shift)]
         for n in range(0, width, half):
             key = jnp.dot(
-                feats[first + i], kw[relation, :, n : n + half], preferred_element_type=F32
+                feats[i], kw[relation, :, n : n + half], preferred_element_type=F32
             )
             keys[i, n : n + half, :] = key.astype(BF16).T
             value = jnp.dot(
-                feats[first + i], mw[relation, :, n : n + half], preferred_element_type=F32
+                feats[i], mw[relation, :, n : n + half], preferred_element_type=F32
             )
             values[i, :, n : n + half] = value.astype(BF16)
 
@@ -337,8 +386,9 @@
     parts = combine(inner - 1, outer * merch_feat.shape[0], far, other, BF16)
 
     here = after(me, *parts)
+    picked = (pick(outer, here, slot_acct, acct_feat),)
     near_keys, near_values = project(
-        outer, ((0, outer, 0),), here, block_rel, rows[1:], *weights
+        outer, ((0, outer, 0),), here, block_rel, picked, *weights
     )
     near = aggregate(
         outer, 0, 0, here, *rest, even_feats, query_weight, near_keys, near_values, F32

time: 47.9 us -> 47.3 us (0.987)
  waiting for transfers between devices: 7.56 us -> 5.02 us
  Pallas kernels: 21.6 us -> 23.5 us
    ppermute x15, waiting for transfers between devices: 7.56 us -> 5.02 us  [swap(): return lax.ppermute(value, AXES, [(s, s ^ mask) for s in range(devices)])]
    pallas_call x1 -> x2, Pallas kernels: 9.2 us -> 11.1 us  [the longest x1 8.57 us: gather(): pl.pallas_call(functools.partial(gather_kernel, outer), out_shape=(jax.Sh...]
  transfers between devices with their start and end apart: 15 -> 15, of which waited for: 6 -> 6; matrix products, arithmetic and copies ran while one was open for 0% -> 0% of each run, Pallas kernels for 43% -> 48%
where the time goes in v22:
time: 47.3 us; the launch traced here: 47 us
  Pallas kernels  23.5 us (50%)
  starting transfers between devices  17.5 us (37%)
  waiting for transfers between devices  5.02 us (11%)
  local copies, waits for them, and re-layouts  0.77 us (2%)
    ppermute x15, starting transfers between devices, swap(): return lax.ppermute(value, AXES, [(s, s ^ mask) for s in range(devices)])  17.5 us
    pallas_call x1, Pallas kernels, gather(): pl.pallas_call(functools.partial(gather_kernel, outer), out_shape=(jax.Sh...  8.57 us
    pallas_call x2, Pallas kernels, project(): pl.pallas_call(functools.partial(project_kernel, outer, spans), out_shape...  7.33 us
    ppermute x15, waiting for transfers between devices, swap(): return lax.ppermute(value, AXES, [(s, s ^ mask) for s in range(devices)])  5.02 us
    pallas_call x3, Pallas kernels, aggregate(): pl.pallas_call(functools.partial(aggregate_kernel, outer, first, shift),...  3.97 us
    pallas_call x1, Pallas kernels, pick(): pl.pallas_call(functools.partial(pick_kernel, outer), out_shape=jax.Shape...  2.51 us
  transfers between devices with their start and end apart: 15, of which 6 were waited for; matrix products, arithmetic and copies ran while one was open for 0% of the time, Pallas kernels for 48%

profile of v22, /device:TPU:0, one launch (start us, length us, event | category | flops | bytes accessed | tf_op | source)
XLA Modules:
  0.0 47.0 jit_solution(6171450140421084374)
XLA Ops:
  0.0 3.5 %collective-permute-start.2 = (bf16[32,512]{1,0:T(8,128)(2,1)}, bf16[32,512]{1,0:T(8,128)(2,1)S(1)}, u32[]{:S(2)}, u32[]{:S(2)}) collective-permute-start(bf16[32,512]{1,0:T(8,128)(2,1)} %feat.1), channel_id=1, source_target_pairs={{0,17},{1,16},{2,19},{3,18},{4,21},{5,20},{6,23},{7,22},{8,25},{9,... | collective-permute-start | bytes 98312 | tf_op jit(solution)/shard_map/ppermute | solution.py:362
  3.5 1.6 %collective-permute-start.1 = (bf16[32,512]{1,0:T(8,128)(2,1)}, bf16[32,512]{1,0:T(8,128)(2,1)S(1)}, u32[]{:S(2)}, u32[]{:S(2)}) collective-permute-start(bf16[32,512]{1,0:T(8,128)(2,1)} %feat.1), channel_id=1, source_target_pairs={{0,25},{1,24},{2,27},{3,26},{4,29},{5,28},{6,31},{7,30},{8,17},{9,... | collective-permute-start | bytes 98312 | tf_op jit(solution)/shard_map/ppermute | solution.py:362
  5.1 0.2 collective-permute-start
  5.3 0.7 %copy-done.7 = s32[32,128]{1,0:T(8,128)S(1)} copy-done((s32[32,128]{1,0:T(8,128)S(1)}, s32[32,128]{1,0:T(8,128)}, u32[]{:S(2)}) %copy-start.7) | copy-done | bytes 16408
  6.1 8.6 %gather_slots.1 = (bf16[16,128,512]{2,1,0:T(8,128)(2,1)S(1)}, bf16[12,128,512]{2,1,0:T(8,128)(2,1)S(1)}) custom-call(s32[1]{0:T(128)} %bitcast.1.me_ref, s32[32,128]{1,0:T(8,128)S(1)} %copy-done.7, bf16[4096,512]{1,0:T(8,128)(2,1)} %acct.1), custom_call_target="tpu_custom_call" | custom-call | bytes 20971520 | tf_op jit(solution)/shard_map/gather_slots/pallas_call | solution.py:103
  14.7 2.5 %collective-permute-start.6 = (bf16[128,512]{1,0:T(8,128)(2,1)S(1)}, bf16[128,512]{1,0:T(8,128)(2,1)S(1)}, u32[]{:S(2)}, u32[]{:S(2)}) collective-permute-start(bf16[128,512]{1,0:T(8,128)(2,1)S(1)} %assemble.1), channel_id=1, source_target_pairs={{0,6},{1,7},{2,4},{3,5},{4,2},{5,3},{6,0},{7,1},{8,14},{9,15},{10,... | collective-permute-start | bytes 393224 | tf_op jit(solution)/shard_map/ppermute | solution.py:362
  17.2 0.5 %collective-permute-start.5 = (bf16[128,512]{1,0:T(8,128)(2,1)S(1)}, bf16[128,512]{1,0:T(8,128)(2,1)S(1)}, u32[]{:S(2)}, u32[]{:S(2)}) collective-permute-start(bf16[128,512]{1,0:T(8,128)(2,1)S(1)} %assemble.1), channel_id=1, source_target_pairs={{0,4},{1,5},{2,6},{3,7},{4,0},{5,1},{6,2},{7,3},{8,12},{9,13},{10,... | collective-permute-start | bytes 393224 | tf_op jit(solution)/shard_map/ppermute | solution.py:362
  17.7 0.5 %collective-permute-start.4 = (bf16[128,512]{1,0:T(8,128)(2,1)S(1)}, bf16[128,512]{1,0:T(8,128)(2,1)S(1)}, u32[]{:S(2)}, u32[]{:S(2)}) collective-permute-start(bf16[128,512]{1,0:T(8,128)(2,1)S(1)} %assemble.1), channel_id=1, source_target_pairs={{0,2},{1,3},{2,0},{3,1},{4,6},{5,7},{6,4},{7,5},{8,10},{9,11},{10,... | collective-permute-start | bytes 393224 | tf_op jit(solution)/shard_map/ppermute | solution.py:362
  18.3 0.0 copy-start.9
  18.3 6.0 %project_slots.2 = (bf16[16,512,128]{2,1,0:T(8,128)(2,1)S(1)}, bf16[16,128,512]{2,1,0:T(8,128)(2,1)S(1)}, bf16[12,512,128]{2,1,0:T(8,128)(2,1)S(1)}, bf16[12,128,512]{2,1,0:T(8,128)(2,1)S(1)}) custom-call(s32[1]{0:T(128)} %bitcast.1.me_ref, s32[32]{0:T(128)S(1)} %copy-done.8, bf16[4,512,512]{2,1,0:T(8,128)(2,1)S(1)} %copy-done.2, ...), custom_call_target="tpu_custom_call" | custom-call | flops 3758096384 | bytes 14680064 | tf_op jit(solution)/shard_map/project_slots/pallas_call | solution.py:194
  24.3 0.1 collective-permute-done.5
  24.4 0.1 collective-permute-done.4
  24.5 0.1 collective-permute-start.7
  24.6 1.5 %aggregate_odd.1 = bf16[512,512]{1,0:T(8,128)(2,1)S(1)} custom-call(s32[1]{0:T(128)} %bitcast.1.me_ref, s32[32]{0:T(128)S(1)} %copy-done.8, s32[32]{0:T(128)S(1)} %copy-done.9, f32[4]{0:T(128)S(1)} %copy-done.10, s32[32,128]{1,0:T(8,128)S(1)} %copy-done.5, bf16[512,512]{1,0:T(8,128)(2,1)S(1)} %pad_maximum_fusion.feats, bf16[512,512]{1,0:T(8,128)(2,1)S(1)} %copy-done, ...), custom_call_target="tpu_custom_call" | custom-call | flops 402653184 | bytes 6291456 | tf_op jit(solution)/shard_map/aggregate_odd/pallas_call | solution.py:254
  26.2 0.5 %collective-permute-start.8 = (bf16[512,512]{1,0:T(8,128)(2,1)S(1)}, bf16[512,512]{1,0:T(8,128)(2,1)S(1)}, u32[]{:S(2)}, u32[]{:S(2)}) collective-permute-start(bf16[512,512]{1,0:T(8,128)(2,1)S(1)} %aggregate_odd.1), channel_id=1, source_target_pairs={{0,1},{1,0},{2,3},{3,2},{4,5},{5,4},{6,7},{7,6},{8,9},{9,8},{10,11... | collective-permute-start | bytes 1572872 | tf_op jit(solution)/shard_map/ppermute | solution.py:362
  26.7 1.3 %aggregate_even.2.mine = f32[384,512]{1,0:T(8,128)S(1)} custom-call(s32[1]{0:T(128)} %bitcast.1.me_ref, s32[32]{0:T(128)S(1)} %copy-done.8, s32[32]{0:T(128)S(1)} %copy-done.9, f32[4]{0:T(128)S(1)} %copy-done.10, s32[32,128]{1,0:T(8,128)S(1)} %copy-done.5, bf16[512,512]{1,0:T(8,128)(2,1)S(1)} %collective-permute-done.7.feats, bf16[512,512]{1,0:T(8,128)(2,1)S(1)} %copy-done, ...), custom_call_target="tpu_custom_call" | custom-call | flops 301989888 | bytes 6291456 | tf_op jit(solution)/shard_map/aggregate_even/pallas_call | solution.py:254
  28.1 0.2 collective-permute-done.8.other
  28.3 0.1 combine_cores.2
  28.3 2.4 %collective-permute-start.9 = (bf16[128,512]{1,0:T(8,128)(2,1)S(1)}, bf16[128,512]{1,0:T(8,128)(2,1)S(1)}, u32[]{:S(2)}, u32[]{:S(2)}) collective-permute-start(bf16[128,512]{1,0:T(8,128)(2,1)S(1)} %get-tuple-element.31), channel_id=1, source_target_pairs={{0,6},{1,7},{2,4},{3,5},{4,2},{5,3},{6,0},{7,1},{8,14},{9,15},{10,... | collective-permute-start | bytes 393224 | tf_op jit(solution)/shard_map/ppermute | solution.py:362
  30.7 0.6 %collective-permute-start.10 = (bf16[128,512]{1,0:T(8,128)(2,1)S(1)}, bf16[128,512]{1,0:T(8,128)(2,1)S(1)}, u32[]{:S(2)}, u32[]{:S(2)}) collective-permute-start(bf16[128,512]{1,0:T(8,128)(2,1)S(1)} %get-tuple-element.32), channel_id=1, source_target_pairs={{0,4},{1,5},{2,6},{3,7},{4,0},{5,1},{6,2},{7,3},{8,12},{9,13},{10,... | collective-permute-start | bytes 393224 | tf_op jit(solution)/shard_map/ppermute | solution.py:362
  31.4 0.5 %collective-permute-start.11 = (bf16[128,512]{1,0:T(8,128)(2,1)S(1)}, bf16[128,512]{1,0:T(8,128)(2,1)S(1)}, u32[]{:S(2)}, u32[]{:S(2)}) collective-permute-start(bf16[128,512]{1,0:T(8,128)(2,1)S(1)} %get-tuple-element.33), channel_id=1, source_target_pairs={{0,2},{1,3},{2,0},{3,1},{4,6},{5,7},{6,4},{7,5},{8,10},{9,11},{10,... | collective-permute-start | bytes 393224 | tf_op jit(solution)/shard_map/ppermute | solution.py:362
  31.9 2.5 %pick_rows.1.refs_0_ = bf16[4,128,512]{2,1,0:T(8,128)(2,1)S(1)} custom-call(s32[1]{0:T(128)} %bitcast.1.me_ref, s32[32,128]{1,0:T(8,128)S(1)} %copy-done.7, bf16[4096,512]{1,0:T(8,128)(2,1)S(1)} %copy-done.1), custom_call_target="tpu_custom_call" | custom-call | flops 2147483648 | bytes 8388608 | tf_op jit(solution)/shard_map/pick_rows/pallas_call | solution.py:149
  34.4 1.3 %project_slots.3 = (bf16[4,512,128]{2,1,0:T(8,128)(2,1)S(1)}, bf16[4,128,512]{2,1,0:T(8,128)(2,1)S(1)}) custom-call(s32[1]{0:T(128)} %bitcast.1.me_ref, s32[32]{0:T(128)S(1)} %copy-done.8, bf16[4,512,512]{2,1,0:T(8,128)(2,1)S(1)} %copy-done.2, bf16[4,512,512]{2,1,0:T(8,128)(2,1)S(1)} %copy-done.3, bf16[4,128,512]{2,1,0:T(8,128)(2,1)S(1)} %pick_rows.1.refs_0_), custom_call_target="tpu_custom_call" | custom-call | flops 536870912 | bytes 2097152 | tf_op jit(solution)/shard_map/project_slots/pallas_call | solution.py:194
  35.8 1.1 %aggregate_even.3.mine = f32[128,512]{1,0:T(8,128)S(1)} custom-call(s32[1]{0:T(128)} %bitcast.1.me_ref, s32[32]{0:T(128)S(1)} %copy-done.8, s32[32]{0:T(128)S(1)} %copy-done.9, f32[4]{0:T(128)S(1)} %copy-done.10, s32[32,128]{1,0:T(8,128)S(1)} %copy-done.5, bf16[512,512]{1,0:T(8,128)(2,1)S(1)} %collective-permute-done.7.feats, bf16[512,512]{1,0:T(8,128)(2,1)S(1)} %copy-done, ...), custom_call_target="tpu_custom_call" | custom-call | flops 100663296 | bytes 6291456 | tf_op jit(solution)/shard_map/aggregate_even/pallas_call | solution.py:254
  36.9 0.9 %collective-permute-done.10.refs_2_ = bf16[128,512]{1,0:T(8,128)(2,1)S(1)} collective-permute-done((bf16[128,512]{1,0:T(8,128)(2,1)S(1)}, bf16[128,512]{1,0:T(8,128)(2,1)S(1)}, u32[]{:S(2)}, u32[]{:S(2)}) %collective-permute-start.10) | collective-permute-done | bytes 131104 | tf_op jit(solution)/shard_map/ppermute | solution.py:362
  37.9 0.1 combine_plane.1
  38.0 3.1 %collective-permute-start.12 = (bf16[32,512]{1,0:T(8,128)(2,1)S(1)}, bf16[32,512]{1,0:T(8,128)(2,1)S(1)}, u32[]{:S(2)}, u32[]{:S(2)}) collective-permute-start(bf16[32,512]{1,0:T(8,128)(2,1)S(1)} %get-tuple-element.38), channel_id=1, source_target_pairs={{0,24},{1,25},{2,26},{3,27},{4,28},{5,29},{6,30},{7,31},{8,16},{9,... | collective-permute-start | bytes 98312 | tf_op jit(solution)/shard_map/ppermute | solution.py:362
  41.0 0.3 collective-permute-start.13
  41.4 1.1 %collective-permute-start.14 = (bf16[32,512]{1,0:T(8,128)(2,1)S(1)}, bf16[32,512]{1,0:T(8,128)(2,1)S(1)}, u32[]{:S(2)}, u32[]{:S(2)}) collective-permute-start(bf16[32,512]{1,0:T(8,128)(2,1)S(1)} %get-tuple-element.40), channel_id=1, source_target_pairs={{0,8},{1,9},{2,10},{3,11},{4,12},{5,13},{6,14},{7,15},{8,0},{9,1},... | collective-permute-start | bytes 98312 | tf_op jit(solution)/shard_map/ppermute | solution.py:362
  42.4 1.4 %collective-permute-done.12.refs_1_ = bf16[32,512]{1,0:T(8,128)(2,1)S(1)} collective-permute-done((bf16[32,512]{1,0:T(8,128)(2,1)S(1)}, bf16[32,512]{1,0:T(8,128)(2,1)S(1)}, u32[]{:S(2)}, u32[]{:S(2)}) %collective-permute-start.12) | collective-permute-done | bytes 32800 | tf_op jit(solution)/shard_map/ppermute | solution.py:362
  43.8 2.3 %collective-permute-done.13.refs_2_ = bf16[32,512]{1,0:T(8,128)(2,1)S(1)} collective-permute-done((bf16[32,512]{1,0:T(8,128)(2,1)S(1)}, bf16[32,512]{1,0:T(8,128)(2,1)S(1)}, u32[]{:S(2)}, u32[]{:S(2)}) %collective-permute-start.13) | collective-permute-done | bytes 32800 | tf_op jit(solution)/shard_map/ppermute | solution.py:362
  46.1 0.9 %finish.1 = bf16[32,512]{1,0:T(8,128)(2,1)} custom-call(bf16[32,512]{1,0:T(8,128)(2,1)S(1)} %copy-done.6, f32[1,512]{1,0:T(1,128)S(1)} %bitcast.2, bf16[512,512]{1,0:T(8,128)(2,1)S(1)} %copy-done.4, f32[32,512]{1,0:T(8,128)S(1)} %get-tuple-element.37.refs_0_, bf16[32,512]{1,0:T(8,128)(2,1)S(1)} %collective-permute-done.12.refs_1_, ...), custom_call_target="tpu_custom_call" | custom-call | tf_op jit(solution)/shard_map/finish/pallas_call | solution.py:332
  (35 shorter events, 0.2 us)
Async XLA Ops:
  0.0 14.6 %collective-permute-start.2 = (bf16[32,512]{1,0:T(8,128)(2,1)}, bf16[32,512]{1,0:T(8,128)(2,1)S(1)}, u32[]{:S(2)}, u32[]{:S(2)}) collective-permute-start(bf16[32,512]{1,0:T(8,128)(2,1)} %feat.1), channel_id=1, source_target_pairs={{0,17},{1,16},{2,19},{3,18},{4,21},{5,20},{6,23},{7,22},{8,25},{9,... | collective-permute-start | bytes 98312 | tf_op jit(solution)/shard_map/ppermute | solution.py:362
  3.5 11.2 %collective-permute-start.1 = (bf16[32,512]{1,0:T(8,128)(2,1)}, bf16[32,512]{1,0:T(8,128)(2,1)S(1)}, u32[]{:S(2)}, u32[]{:S(2)}) collective-permute-start(bf16[32,512]{1,0:T(8,128)(2,1)} %feat.1), channel_id=1, source_target_pairs={{0,25},{1,24},{2,27},{3,26},{4,29},{5,28},{6,31},{7,30},{8,17},{9,... | collective-permute-start | bytes 98312 | tf_op jit(solution)/shard_map/ppermute | solution.py:362
  5.1 9.6 %collective-permute-start = (bf16[32,512]{1,0:T(8,128)(2,1)}, bf16[32,512]{1,0:T(8,128)(2,1)S(1)}, u32[]{:S(2)}, u32[]{:S(2)}) collective-permute-start(bf16[32,512]{1,0:T(8,128)(2,1)} %feat.1), channel_id=1, source_target_pairs={{0,9},{1,8},{2,11},{3,10},{4,13},{5,12},{6,15},{7,14},{8,1},{9,0},... | collective-permute-start | bytes 98312 | tf_op jit(solution)/shard_map/ppermute | solution.py:362
  5.3 9.3 %collective-permute-start.3 = (bf16[32,512]{1,0:T(8,128)(2,1)}, bf16[32,512]{1,0:T(8,128)(2,1)S(1)}, u32[]{:S(2)}, u32[]{:S(2)}) collective-permute-start(bf16[32,512]{1,0:T(8,128)(2,1)} %feat.1), channel_id=1, source_target_pairs={{0,1},{1,0},{2,3},{3,2},{4,5},{5,4},{6,7},{7,6},{8,9},{9,8},{10,11... | collective-permute-start | bytes 98312 | tf_op jit(solution)/shard_map/ppermute | solution.py:362
  5.3 0.7 %copy-start.7 = (s32[32,128]{1,0:T(8,128)S(1)}, s32[32,128]{1,0:T(8,128)}, u32[]{:S(2)}) copy-start(s32[32,128]{1,0:T(8,128)} %slots.1) | copy-start | bytes 49156
  6.1 12.2 %copy-start.2 = (bf16[4,512,512]{2,1,0:T(8,128)(2,1)S(1)}, bf16[4,512,512]{2,1,0:T(8,128)(2,1)}, u32[]{:S(2)}) copy-start(bf16[4,512,512]{2,1,0:T(8,128)(2,1)} %kw.3) | copy-start | bytes 6291460
  6.1 12.2 %copy-start.3 = (bf16[4,512,512]{2,1,0:T(8,128)(2,1)S(1)}, bf16[4,512,512]{2,1,0:T(8,128)(2,1)}, u32[]{:S(2)}) copy-start(bf16[4,512,512]{2,1,0:T(8,128)(2,1)} %mw.3) | copy-start | bytes 6291460
  6.1 12.2 %copy-start.8 = (s32[32]{0:T(128)S(1)}, s32[32]{0:T(128)}, u32[]{:S(2)}) copy-start(s32[32]{0:T(128)} %rel_ref.9) | copy-start | bytes 388
  14.7 9.6 %collective-permute-start.6 = (bf16[128,512]{1,0:T(8,128)(2,1)S(1)}, bf16[128,512]{1,0:T(8,128)(2,1)S(1)}, u32[]{:S(2)}, u32[]{:S(2)}) collective-permute-start(bf16[128,512]{1,0:T(8,128)(2,1)S(1)} %assemble.1), channel_id=1, source_target_pairs={{0,6},{1,7},{2,4},{3,5},{4,2},{5,3},{6,0},{7,1},{8,14},{9,15},{10,... | collective-permute-start | bytes 393224 | tf_op jit(solution)/shard_map/ppermute | solution.py:362
  17.2 7.2 %collective-permute-start.5 = (bf16[128,512]{1,0:T(8,128)(2,1)S(1)}, bf16[128,512]{1,0:T(8,128)(2,1)S(1)}, u32[]{:S(2)}, u32[]{:S(2)}) collective-permute-start(bf16[128,512]{1,0:T(8,128)(2,1)S(1)} %assemble.1), channel_id=1, source_target_pairs={{0,4},{1,5},{2,6},{3,7},{4,0},{5,1},{6,2},{7,3},{8,12},{9,13},{10,... | collective-permute-start | bytes 393224 | tf_op jit(solution)/shard_map/ppermute | solution.py:362
  17.7 6.8 %collective-permute-start.4 = (bf16[128,512]{1,0:T(8,128)(2,1)S(1)}, bf16[128,512]{1,0:T(8,128)(2,1)S(1)}, u32[]{:S(2)}, u32[]{:S(2)}) collective-permute-start(bf16[128,512]{1,0:T(8,128)(2,1)S(1)} %assemble.1), channel_id=1, source_target_pairs={{0,2},{1,3},{2,0},{3,1},{4,6},{5,7},{6,4},{7,5},{8,10},{9,11},{10,... | collective-permute-start | bytes 393224 | tf_op jit(solution)/shard_map/ppermute | solution.py:362
  18.3 6.3 %copy-start = (bf16[512,512]{1,0:T(8,128)(2,1)S(1)}, bf16[512,512]{1,0:T(8,128)(2,1)}, u32[]{:S(2)}) copy-start(bf16[512,512]{1,0:T(8,128)(2,1)} %wq.5) | copy-start | bytes 1572868
  18.3 6.3 %copy-start.5 = (s32[32,128]{1,0:T(8,128)S(1)}, s32[32,128]{1,0:T(8,128)}, u32[]{:S(2)}) copy-start(s32[32,128]{1,0:T(8,128)} %merch_slot.5) | copy-start | bytes 49156
  18.3 6.3 %copy-start.9 = (s32[32]{0:T(128)S(1)}, s32[32]{0:T(128)}, u32[]{:S(2)}) copy-start(s32[32]{0:T(128)} %count_ref.5) | copy-start | bytes 388
  18.3 6.3 %copy-start.10 = (f32[4]{0:T(128)S(1)}, f32[4]{0:T(128)}, u32[]{:S(2)}) copy-start(f32[4]{0:T(128)} %bias_ref.5) | copy-start | bytes 52
  24.5 2.2 %collective-permute-start.7 = (bf16[512,512]{1,0:T(8,128)(2,1)S(1)}, bf16[512,512]{1,0:T(8,128)(2,1)S(1)}, u32[]{:S(2)}, u32[]{:S(2)}) collective-permute-start(bf16[512,512]{1,0:T(8,128)(2,1)S(1)} %pad_maximum_fusion.feats), channel_id=1, source_target_pairs={{0,1},{1,0},{2,3},{3,2},{4,5},{5,4},{6,7},{7,6},{8,9},{9,8},{10,11... | collective-permute-start | bytes 1572872 | tf_op jit(solution)/shard_map/ppermute | solution.py:362
  26.2 2.1 %collective-permute-start.8 = (bf16[512,512]{1,0:T(8,128)(2,1)S(1)}, bf16[512,512]{1,0:T(8,128)(2,1)S(1)}, u32[]{:S(2)}, u32[]{:S(2)}) collective-permute-start(bf16[512,512]{1,0:T(8,128)(2,1)S(1)} %aggregate_odd.1), channel_id=1, source_target_pairs={{0,1},{1,0},{2,3},{3,2},{4,5},{5,4},{6,7},{7,6},{8,9},{9,8},{10,11... | collective-permute-start | bytes 1572872 | tf_op jit(solution)/shard_map/ppermute | solution.py:362
  26.7 5.2 %copy-start.1 = (bf16[4096,512]{1,0:T(8,128)(2,1)S(1)}, bf16[4096,512]{1,0:T(8,128)(2,1)}, u32[]{:S(2)}) copy-start(bf16[4096,512]{1,0:T(8,128)(2,1)} %acct.1) | copy-start | bytes 12582916
  28.3 8.6 %collective-permute-start.9 = (bf16[128,512]{1,0:T(8,128)(2,1)S(1)}, bf16[128,512]{1,0:T(8,128)(2,1)S(1)}, u32[]{:S(2)}, u32[]{:S(2)}) collective-permute-start(bf16[128,512]{1,0:T(8,128)(2,1)S(1)} %get-tuple-element.31), channel_id=1, source_target_pairs={{0,6},{1,7},{2,4},{3,5},{4,2},{5,3},{6,0},{7,1},{8,14},{9,15},{10,... | collective-permute-start | bytes 393224 | tf_op jit(solution)/shard_map/ppermute | solution.py:362
  30.7 7.2 %collective-permute-start.10 = (bf16[128,512]{1,0:T(8,128)(2,1)S(1)}, bf16[128,512]{1,0:T(8,128)(2,1)S(1)}, u32[]{:S(2)}, u32[]{:S(2)}) collective-permute-start(bf16[128,512]{1,0:T(8,128)(2,1)S(1)} %get-tuple-element.32), channel_id=1, source_target_pairs={{0,4},{1,5},{2,6},{3,7},{4,0},{5,1},{6,2},{7,3},{8,12},{9,13},{10,... | collective-permute-start | bytes 393224 | tf_op jit(solution)/shard_map/ppermute | solution.py:362
  31.4 6.5 %collective-permute-start.11 = (bf16[128,512]{1,0:T(8,128)(2,1)S(1)}, bf16[128,512]{1,0:T(8,128)(2,1)S(1)}, u32[]{:S(2)}, u32[]{:S(2)}) collective-permute-start(bf16[128,512]{1,0:T(8,128)(2,1)S(1)} %get-tuple-element.33), channel_id=1, source_target_pairs={{0,2},{1,3},{2,0},{3,1},{4,6},{5,7},{6,4},{7,5},{8,10},{9,11},{10,... | collective-permute-start | bytes 393224 | tf_op jit(solution)/shard_map/ppermute | solution.py:362
  35.8 10.4 %copy-start.4 = (bf16[512,512]{1,0:T(8,128)(2,1)S(1)}, bf16[512,512]{1,0:T(8,128)(2,1)}, u32[]{:S(2)}) copy-start(bf16[512,512]{1,0:T(8,128)(2,1)} %wo.1) | copy-start | bytes 1572868
  35.8 10.3 %copy-start.6 = (bf16[32,512]{1,0:T(8,128)(2,1)S(1)}, bf16[32,512]{1,0:T(8,128)(2,1)}, u32[]{:S(2)}) copy-start(bf16[32,512]{1,0:T(8,128)(2,1)} %feat.1) | copy-start | bytes 98308
  35.8 10.3 %copy-start.11 = (f32[512]{0:T(512)S(1)}, f32[512]{0:T(512)}, u32[]{:S(2)}) copy-start(f32[512]{0:T(512)} %param.19) | copy-start | bytes 6148
  38.0 5.9 %collective-permute-start.12 = (bf16[32,512]{1,0:T(8,128)(2,1)S(1)}, bf16[32,512]{1,0:T(8,128)(2,1)S(1)}, u32[]{:S(2)}, u32[]{:S(2)}) collective-permute-start(bf16[32,512]{1,0:T(8,128)(2,1)S(1)} %get-tuple-element.38), channel_id=1, source_target_pairs={{0,24},{1,25},{2,26},{3,27},{4,28},{5,29},{6,30},{7,31},{8,16},{9,... | collective-permute-start | bytes 98312 | tf_op jit(solution)/shard_map/ppermute | solution.py:362
  41.0 5.1 %collective-permute-start.13 = (bf16[32,512]{1,0:T(8,128)(2,1)S(1)}, bf16[32,512]{1,0:T(8,128)(2,1)S(1)}, u32[]{:S(2)}, u32[]{:S(2)}) collective-permute-start(bf16[32,512]{1,0:T(8,128)(2,1)S(1)} %get-tuple-element.39), channel_id=1, source_target_pairs={{0,16},{1,17},{2,18},{3,19},{4,20},{5,21},{6,22},{7,23},{8,24},{9,... | collective-permute-start | bytes 98312 | tf_op jit(solution)/shard_map/ppermute | solution.py:362
  41.4 4.8 %collective-permute-start.14 = (bf16[32,512]{1,0:T(8,128)(2,1)S(1)}, bf16[32,512]{1,0:T(8,128)(2,1)S(1)}, u32[]{:S(2)}, u32[]{:S(2)}) collective-permute-start(bf16[32,512]{1,0:T(8,128)(2,1)S(1)} %get-tuple-element.40), channel_id=1, source_target_pairs={{0,8},{1,9},{2,10},{3,11},{4,12},{5,13},{6,14},{7,15},{8,0},{9,1},... | collective-permute-start | bytes 98312 | tf_op jit(solution)/shard_map/ppermute | solution.py:362

commit v23 on v22

--- a/solution.py
+++ b/solution.py
@@ -159,22 +159,15 @@
 
 
 def project_kernel(outer, spans, me_ref, rel_ref, kw, mw, *refs):
-    width = refs[0].shape[2]
-    half = width // 2
     me = me_ref[0]
     count = len(spans)
 
     def one(i, first, shift, feats, keys, values):
         relation = rel_ref[jnp.bitwise_xor(me, _offset(first + i, outer) + shift)]
-        for n in range(0, width, half):
-            key = jnp.dot(
-                feats[i], kw[relation, :, n : n + half], preferred_element_type=F32
-            )
-            keys[i, n : n + half, :] = key.astype(BF16).T
-            value = jnp.dot(
-                feats[i], mw[relation, :, n : n + half], preferred_element_type=F32
-            )
-            values[i, :, n : n + half] = value.astype(BF16)
+        key = jnp.dot(feats[i], kw[relation], preferred_element_type=F32)
+        keys[i] = key.astype(BF16).T
+        value = jnp.dot(feats[i], mw[relation], preferred_element_type=F32)
+        values[i] = value.astype(BF16)
 
     for s, (first, last, shift) in enumerate(spans):
         outs = refs[count + 2 * s : count + 2 * s + 2]

time: 47.3 us -> 46.9 us (level)
  transfers between devices with their start and end apart: 15 -> 15, of which waited for: 6 -> 6; matrix products, arithmetic and copies ran while one was open for 0% -> 0% of each run, Pallas kernels for 48% -> 47%
where the time goes in v23:
time: 46.9 us; the launch traced here: 46.7 us
  Pallas kernels  23.1 us (49%)
  starting transfers between devices  17.5 us (37%)
  waiting for transfers between devices  5.06 us (11%)
  local copies, waits for them, and re-layouts  0.77 us (2%)
    ppermute x15, starting transfers between devices, swap(): return lax.ppermute(value, AXES, [(s, s ^ mask) for s in range(devices)])  17.5 us
    pallas_call x1, Pallas kernels, gather(): pl.pallas_call(functools.partial(gather_kernel, outer), out_shape=(jax.Sh...  8.57 us
    pallas_call x2, Pallas kernels, project(): pl.pallas_call(functools.partial(project_kernel, outer, spans), out_shape...  6.95 us
    ppermute x15, waiting for transfers between devices, swap(): return lax.ppermute(value, AXES, [(s, s ^ mask) for s in range(devices)])  5.06 us
    pallas_call x3, Pallas kernels, aggregate(): pl.pallas_call(functools.partial(aggregate_kernel, outer, first, shift),...  3.97 us
    pallas_call x1, Pallas kernels, pick(): pl.pallas_call(functools.partial(pick_kernel, outer), out_shape=jax.Shape...  2.51 us
  transfers between devices with their start and end apart: 15, of which 6 were waited for; matrix products, arithmetic and copies ran while one was open for 0% of the time, Pallas kernels for 47%

profile of v23, /device:TPU:0, one launch (start us, length us, event | category | flops | bytes accessed | tf_op | source)
XLA Modules:
  0.0 46.7 jit_solution(9178384011142990651)
XLA Ops:
  0.0 3.5 %collective-permute-start.2 = (bf16[32,512]{1,0:T(8,128)(2,1)}, bf16[32,512]{1,0:T(8,128)(2,1)S(1)}, u32[]{:S(2)}, u32[]{:S(2)}) collective-permute-start(bf16[32,512]{1,0:T(8,128)(2,1)} %feat.1), channel_id=1, source_target_pairs={{0,17},{1,16},{2,19},{3,18},{4,21},{5,20},{6,23},{7,22},{8,25},{9,... | collective-permute-start | bytes 98312 | tf_op jit(solution)/shard_map/ppermute | solution.py:355
  3.5 1.6 %collective-permute-start.1 = (bf16[32,512]{1,0:T(8,128)(2,1)}, bf16[32,512]{1,0:T(8,128)(2,1)S(1)}, u32[]{:S(2)}, u32[]{:S(2)}) collective-permute-start(bf16[32,512]{1,0:T(8,128)(2,1)} %feat.1), channel_id=1, source_target_pairs={{0,25},{1,24},{2,27},{3,26},{4,29},{5,28},{6,31},{7,30},{8,17},{9,... | collective-permute-start | bytes 98312 | tf_op jit(solution)/shard_map/ppermute | solution.py:355
  5.1 0.2 collective-permute-start
  5.3 0.7 %copy-done.7 = s32[32,128]{1,0:T(8,128)S(1)} copy-done((s32[32,128]{1,0:T(8,128)S(1)}, s32[32,128]{1,0:T(8,128)}, u32[]{:S(2)}) %copy-start.7) | copy-done | bytes 16408
  6.1 8.6 %gather_slots.1 = (bf16[16,128,512]{2,1,0:T(8,128)(2,1)S(1)}, bf16[12,128,512]{2,1,0:T(8,128)(2,1)S(1)}) custom-call(s32[1]{0:T(128)} %bitcast.1.me_ref, s32[32,128]{1,0:T(8,128)S(1)} %copy-done.7, bf16[4096,512]{1,0:T(8,128)(2,1)} %acct.1), custom_call_target="tpu_custom_call" | custom-call | bytes 20971520 | tf_op jit(solution)/shard_map/gather_slots/pallas_call | solution.py:103
  14.7 2.5 %collective-permute-start.6 = (bf16[128,512]{1,0:T(8,128)(2,1)S(1)}, bf16[128,512]{1,0:T(8,128)(2,1)S(1)}, u32[]{:S(2)}, u32[]{:S(2)}) collective-permute-start(bf16[128,512]{1,0:T(8,128)(2,1)S(1)} %assemble.1), channel_id=1, source_target_pairs={{0,6},{1,7},{2,4},{3,5},{4,2},{5,3},{6,0},{7,1},{8,14},{9,15},{10,... | collective-permute-start | bytes 393224 | tf_op jit(solution)/shard_map/ppermute | solution.py:355
  17.2 0.5 %collective-permute-start.5 = (bf16[128,512]{1,0:T(8,128)(2,1)S(1)}, bf16[128,512]{1,0:T(8,128)(2,1)S(1)}, u32[]{:S(2)}, u32[]{:S(2)}) collective-permute-start(bf16[128,512]{1,0:T(8,128)(2,1)S(1)} %assemble.1), channel_id=1, source_target_pairs={{0,4},{1,5},{2,6},{3,7},{4,0},{5,1},{6,2},{7,3},{8,12},{9,13},{10,... | collective-permute-start | bytes 393224 | tf_op jit(solution)/shard_map/ppermute | solution.py:355
  17.7 0.5 %collective-permute-start.4 = (bf16[128,512]{1,0:T(8,128)(2,1)S(1)}, bf16[128,512]{1,0:T(8,128)(2,1)S(1)}, u32[]{:S(2)}, u32[]{:S(2)}) collective-permute-start(bf16[128,512]{1,0:T(8,128)(2,1)S(1)} %assemble.1), channel_id=1, source_target_pairs={{0,2},{1,3},{2,0},{3,1},{4,6},{5,7},{6,4},{7,5},{8,10},{9,11},{10,... | collective-permute-start | bytes 393224 | tf_op jit(solution)/shard_map/ppermute | solution.py:355
  18.3 0.0 copy-start.5
  18.3 5.7 %project_slots.2 = (bf16[16,512,128]{2,1,0:T(8,128)(2,1)S(1)}, bf16[16,128,512]{2,1,0:T(8,128)(2,1)S(1)}, bf16[12,512,128]{2,1,0:T(8,128)(2,1)S(1)}, bf16[12,128,512]{2,1,0:T(8,128)(2,1)S(1)}) custom-call(s32[1]{0:T(128)} %bitcast.1.me_ref, s32[32]{0:T(128)S(1)} %copy-done.8, bf16[4,512,512]{2,1,0:T(8,128)(2,1)S(1)} %copy-done.2, ...), custom_call_target="tpu_custom_call" | custom-call | flops 3758096384 | bytes 14680064 | tf_op jit(solution)/shard_map/project_slots/pallas_call | solution.py:187
  24.0 0.4 collective-permute-done.5
  24.4 0.1 collective-permute-done.4
  24.5 0.1 collective-permute-start.7
  24.6 1.5 %aggregate_odd.1 = bf16[512,512]{1,0:T(8,128)(2,1)S(1)} custom-call(s32[1]{0:T(128)} %bitcast.1.me_ref, s32[32]{0:T(128)S(1)} %copy-done.8, s32[32]{0:T(128)S(1)} %copy-done.9, f32[4]{0:T(128)S(1)} %copy-done.10, s32[32,128]{1,0:T(8,128)S(1)} %copy-done.5, bf16[512,512]{1,0:T(8,128)(2,1)S(1)} %pad_maximum_fusion.feats, bf16[512,512]{1,0:T(8,128)(2,1)S(1)} %copy-done, ...), custom_call_target="tpu_custom_call" | custom-call | flops 402653184 | bytes 6291456 | tf_op jit(solution)/shard_map/aggregate_odd/pallas_call | solution.py:247
  26.2 0.5 %collective-permute-start.8 = (bf16[512,512]{1,0:T(8,128)(2,1)S(1)}, bf16[512,512]{1,0:T(8,128)(2,1)S(1)}, u32[]{:S(2)}, u32[]{:S(2)}) collective-permute-start(bf16[512,512]{1,0:T(8,128)(2,1)S(1)} %aggregate_odd.1), channel_id=1, source_target_pairs={{0,1},{1,0},{2,3},{3,2},{4,5},{5,4},{6,7},{7,6},{8,9},{9,8},{10,11... | collective-permute-start | bytes 1572872 | tf_op jit(solution)/shard_map/ppermute | solution.py:355
  26.7 1.3 %aggregate_even.2.mine = f32[384,512]{1,0:T(8,128)S(1)} custom-call(s32[1]{0:T(128)} %bitcast.1.me_ref, s32[32]{0:T(128)S(1)} %copy-done.8, s32[32]{0:T(128)S(1)} %copy-done.9, f32[4]{0:T(128)S(1)} %copy-done.10, s32[32,128]{1,0:T(8,128)S(1)} %copy-done.5, bf16[512,512]{1,0:T(8,128)(2,1)S(1)} %collective-permute-done.7.feats, bf16[512,512]{1,0:T(8,128)(2,1)S(1)} %copy-done, ...), custom_call_target="tpu_custom_call" | custom-call | flops 301989888 | bytes 6291456 | tf_op jit(solution)/shard_map/aggregate_even/pallas_call | solution.py:247
  28.1 0.2 collective-permute-done.8.other
  28.3 0.1 combine_cores.2
  28.3 2.1 %collective-permute-start.9 = (bf16[128,512]{1,0:T(8,128)(2,1)S(1)}, bf16[128,512]{1,0:T(8,128)(2,1)S(1)}, u32[]{:S(2)}, u32[]{:S(2)}) collective-permute-start(bf16[128,512]{1,0:T(8,128)(2,1)S(1)} %get-tuple-element.31), channel_id=1, source_target_pairs={{0,6},{1,7},{2,4},{3,5},{4,2},{5,3},{6,0},{7,1},{8,14},{9,15},{10,... | collective-permute-start | bytes 393224 | tf_op jit(solution)/shard_map/ppermute | solution.py:355
  30.4 1.0 %collective-permute-start.10 = (bf16[128,512]{1,0:T(8,128)(2,1)S(1)}, bf16[128,512]{1,0:T(8,128)(2,1)S(1)}, u32[]{:S(2)}, u32[]{:S(2)}) collective-permute-start(bf16[128,512]{1,0:T(8,128)(2,1)S(1)} %get-tuple-element.32), channel_id=1, source_target_pairs={{0,4},{1,5},{2,6},{3,7},{4,0},{5,1},{6,2},{7,3},{8,12},{9,13},{10,... | collective-permute-start | bytes 393224 | tf_op jit(solution)/shard_map/ppermute | solution.py:355
  31.4 0.5 %collective-permute-start.11 = (bf16[128,512]{1,0:T(8,128)(2,1)S(1)}, bf16[128,512]{1,0:T(8,128)(2,1)S(1)}, u32[]{:S(2)}, u32[]{:S(2)}) collective-permute-start(bf16[128,512]{1,0:T(8,128)(2,1)S(1)} %get-tuple-element.33), channel_id=1, source_target_pairs={{0,2},{1,3},{2,0},{3,1},{4,6},{5,7},{6,4},{7,5},{8,10},{9,11},{10,... | collective-permute-start | bytes 393224 | tf_op jit(solution)/shard_map/ppermute | solution.py:355
  31.9 2.5 %pick_rows.1.refs_0_ = bf16[4,128,512]{2,1,0:T(8,128)(2,1)S(1)} custom-call(s32[1]{0:T(128)} %bitcast.1.me_ref, s32[32,128]{1,0:T(8,128)S(1)} %copy-done.7, bf16[4096,512]{1,0:T(8,128)(2,1)S(1)} %copy-done.1), custom_call_target="tpu_custom_call" | custom-call | flops 2147483648 | bytes 8388608 | tf_op jit(solution)/shard_map/pick_rows/pallas_call | solution.py:149
  34.4 1.3 %project_slots.3 = (bf16[4,512,128]{2,1,0:T(8,128)(2,1)S(1)}, bf16[4,128,512]{2,1,0:T(8,128)(2,1)S(1)}) custom-call(s32[1]{0:T(128)} %bitcast.1.me_ref, s32[32]{0:T(128)S(1)} %copy-done.8, bf16[4,512,512]{2,1,0:T(8,128)(2,1)S(1)} %copy-done.2, bf16[4,512,512]{2,1,0:T(8,128)(2,1)S(1)} %copy-done.3, bf16[4,128,512]{2,1,0:T(8,128)(2,1)S(1)} %pick_rows.1.refs_0_), custom_call_target="tpu_custom_call" | custom-call | flops 536870912 | bytes 2097152 | tf_op jit(solution)/shard_map/project_slots/pallas_call | solution.py:187
  35.8 1.1 %aggregate_even.3.mine = f32[128,512]{1,0:T(8,128)S(1)} custom-call(s32[1]{0:T(128)} %bitcast.1.me_ref, s32[32]{0:T(128)S(1)} %copy-done.8, s32[32]{0:T(128)S(1)} %copy-done.9, f32[4]{0:T(128)S(1)} %copy-done.10, s32[32,128]{1,0:T(8,128)S(1)} %copy-done.5, bf16[512,512]{1,0:T(8,128)(2,1)S(1)} %collective-permute-done.7.feats, bf16[512,512]{1,0:T(8,128)(2,1)S(1)} %copy-done, ...), custom_call_target="tpu_custom_call" | custom-call | flops 100663296 | bytes 6291456 | tf_op jit(solution)/shard_map/aggregate_even/pallas_call | solution.py:247
  36.9 1.0 %collective-permute-done.10.refs_2_ = bf16[128,512]{1,0:T(8,128)(2,1)S(1)} collective-permute-done((bf16[128,512]{1,0:T(8,128)(2,1)S(1)}, bf16[128,512]{1,0:T(8,128)(2,1)S(1)}, u32[]{:S(2)}, u32[]{:S(2)}) %collective-permute-start.10) | collective-permute-done | bytes 131104 | tf_op jit(solution)/shard_map/ppermute | solution.py:355
  37.9 0.1 combine_plane.1
  38.0 2.7 %collective-permute-start.12 = (bf16[32,512]{1,0:T(8,128)(2,1)S(1)}, bf16[32,512]{1,0:T(8,128)(2,1)S(1)}, u32[]{:S(2)}, u32[]{:S(2)}) collective-permute-start(bf16[32,512]{1,0:T(8,128)(2,1)S(1)} %get-tuple-element.38), channel_id=1, source_target_pairs={{0,24},{1,25},{2,26},{3,27},{4,28},{5,29},{6,30},{7,31},{8,16},{9,... | collective-permute-start | bytes 98312 | tf_op jit(solution)/shard_map/ppermute | solution.py:355
  40.7 0.3 collective-permute-start.13
  41.0 1.4 %collective-permute-start.14 = (bf16[32,512]{1,0:T(8,128)(2,1)S(1)}, bf16[32,512]{1,0:T(8,128)(2,1)S(1)}, u32[]{:S(2)}, u32[]{:S(2)}) collective-permute-start(bf16[32,512]{1,0:T(8,128)(2,1)S(1)} %get-tuple-element.40), channel_id=1, source_target_pairs={{0,8},{1,9},{2,10},{3,11},{4,12},{5,13},{6,14},{7,15},{8,0},{9,1},... | collective-permute-start | bytes 98312 | tf_op jit(solution)/shard_map/ppermute | solution.py:355
  42.4 1.3 %collective-permute-done.12.refs_1_ = bf16[32,512]{1,0:T(8,128)(2,1)S(1)} collective-permute-done((bf16[32,512]{1,0:T(8,128)(2,1)S(1)}, bf16[32,512]{1,0:T(8,128)(2,1)S(1)}, u32[]{:S(2)}, u32[]{:S(2)}) %collective-permute-start.12) | collective-permute-done | bytes 32800 | tf_op jit(solution)/shard_map/ppermute | solution.py:355
  43.7 2.0 %collective-permute-done.13.refs_2_ = bf16[32,512]{1,0:T(8,128)(2,1)S(1)} collective-permute-done((bf16[32,512]{1,0:T(8,128)(2,1)S(1)}, bf16[32,512]{1,0:T(8,128)(2,1)S(1)}, u32[]{:S(2)}, u32[]{:S(2)}) %collective-permute-start.13) | collective-permute-done | bytes 32800 | tf_op jit(solution)/shard_map/ppermute | solution.py:355
  45.8 0.9 %finish.1 = bf16[32,512]{1,0:T(8,128)(2,1)} custom-call(bf16[32,512]{1,0:T(8,128)(2,1)S(1)} %copy-done.6, f32[1,512]{1,0:T(1,128)S(1)} %bitcast.2, bf16[512,512]{1,0:T(8,128)(2,1)S(1)} %copy-done.4, f32[32,512]{1,0:T(8,128)S(1)} %get-tuple-element.37.refs_0_, bf16[32,512]{1,0:T(8,128)(2,1)S(1)} %collective-permute-done.12.refs_1_, ...), custom_call_target="tpu_custom_call" | custom-call | tf_op jit(solution)/shard_map/finish/pallas_call | solution.py:325
  (35 shorter events, 0.2 us)
Async XLA Ops:
  0.0 14.6 %collective-permute-start.2 = (bf16[32,512]{1,0:T(8,128)(2,1)}, bf16[32,512]{1,0:T(8,128)(2,1)S(1)}, u32[]{:S(2)}, u32[]{:S(2)}) collective-permute-start(bf16[32,512]{1,0:T(8,128)(2,1)} %feat.1), channel_id=1, source_target_pairs={{0,17},{1,16},{2,19},{3,18},{4,21},{5,20},{6,23},{7,22},{8,25},{9,... | collective-permute-start | bytes 98312 | tf_op jit(solution)/shard_map/ppermute | solution.py:355
  3.5 11.2 %collective-permute-start.1 = (bf16[32,512]{1,0:T(8,128)(2,1)}, bf16[32,512]{1,0:T(8,128)(2,1)S(1)}, u32[]{:S(2)}, u32[]{:S(2)}) collective-permute-start(bf16[32,512]{1,0:T(8,128)(2,1)} %feat.1), channel_id=1, source_target_pairs={{0,25},{1,24},{2,27},{3,26},{4,29},{5,28},{6,31},{7,30},{8,17},{9,... | collective-permute-start | bytes 98312 | tf_op jit(solution)/shard_map/ppermute | solution.py:355
  5.1 9.6 %collective-permute-start = (bf16[32,512]{1,0:T(8,128)(2,1)}, bf16[32,512]{1,0:T(8,128)(2,1)S(1)}, u32[]{:S(2)}, u32[]{:S(2)}) collective-permute-start(bf16[32,512]{1,0:T(8,128)(2,1)} %feat.1), channel_id=1, source_target_pairs={{0,9},{1,8},{2,11},{3,10},{4,13},{5,12},{6,15},{7,14},{8,1},{9,0},... | collective-permute-start | bytes 98312 | tf_op jit(solution)/shard_map/ppermute | solution.py:355
  5.3 9.3 %collective-permute-start.3 = (bf16[32,512]{1,0:T(8,128)(2,1)}, bf16[32,512]{1,0:T(8,128)(2,1)S(1)}, u32[]{:S(2)}, u32[]{:S(2)}) collective-permute-start(bf16[32,512]{1,0:T(8,128)(2,1)} %feat.1), channel_id=1, source_target_pairs={{0,1},{1,0},{2,3},{3,2},{4,5},{5,4},{6,7},{7,6},{8,9},{9,8},{10,11... | collective-permute-start | bytes 98312 | tf_op jit(solution)/shard_map/ppermute | solution.py:355
  5.3 0.7 %copy-start.7 = (s32[32,128]{1,0:T(8,128)S(1)}, s32[32,128]{1,0:T(8,128)}, u32[]{:S(2)}) copy-start(s32[32,128]{1,0:T(8,128)} %slots.1) | copy-start | bytes 49156
  6.1 12.2 %copy-start.2 = (bf16[4,512,512]{2,1,0:T(8,128)(2,1)S(1)}, bf16[4,512,512]{2,1,0:T(8,128)(2,1)}, u32[]{:S(2)}) copy-start(bf16[4,512,512]{2,1,0:T(8,128)(2,1)} %kw.3) | copy-start | bytes 6291460
  6.1 12.2 %copy-start.3 = (bf16[4,512,512]{2,1,0:T(8,128)(2,1)S(1)}, bf16[4,512,512]{2,1,0:T(8,128)(2,1)}, u32[]{:S(2)}) copy-start(bf16[4,512,512]{2,1,0:T(8,128)(2,1)} %mw.3) | copy-start | bytes 6291460
  6.1 12.2 %copy-start.8 = (s32[32]{0:T(128)S(1)}, s32[32]{0:T(128)}, u32[]{:S(2)}) copy-start(s32[32]{0:T(128)} %rel_ref.9) | copy-start | bytes 388
  14.7 9.3 %collective-permute-start.6 = (bf16[128,512]{1,0:T(8,128)(2,1)S(1)}, bf16[128,512]{1,0:T(8,128)(2,1)S(1)}, u32[]{:S(2)}, u32[]{:S(2)}) collective-permute-start(bf16[128,512]{1,0:T(8,128)(2,1)S(1)} %assemble.1), channel_id=1, source_target_pairs={{0,6},{1,7},{2,4},{3,5},{4,2},{5,3},{6,0},{7,1},{8,14},{9,15},{10,... | collective-permute-start | bytes 393224 | tf_op jit(solution)/shard_map/ppermute | solution.py:355
  17.2 7.2 %collective-permute-start.5 = (bf16[128,512]{1,0:T(8,128)(2,1)S(1)}, bf16[128,512]{1,0:T(8,128)(2,1)S(1)}, u32[]{:S(2)}, u32[]{:S(2)}) collective-permute-start(bf16[128,512]{1,0:T(8,128)(2,1)S(1)} %assemble.1), channel_id=1, source_target_pairs={{0,4},{1,5},{2,6},{3,7},{4,0},{5,1},{6,2},{7,3},{8,12},{9,13},{10,... | collective-permute-start | bytes 393224 | tf_op jit(solution)/shard_map/ppermute | solution.py:355
  17.7 6.8 %collective-permute-start.4 = (bf16[128,512]{1,0:T(8,128)(2,1)S(1)}, bf16[128,512]{1,0:T(8,128)(2,1)S(1)}, u32[]{:S(2)}, u32[]{:S(2)}) collective-permute-start(bf16[128,512]{1,0:T(8,128)(2,1)S(1)} %assemble.1), channel_id=1, source_target_pairs={{0,2},{1,3},{2,0},{3,1},{4,6},{5,7},{6,4},{7,5},{8,10},{9,11},{10,... | collective-permute-start | bytes 393224 | tf_op jit(solution)/shard_map/ppermute | solution.py:355
  18.3 6.3 %copy-start = (bf16[512,512]{1,0:T(8,128)(2,1)S(1)}, bf16[512,512]{1,0:T(8,128)(2,1)}, u32[]{:S(2)}) copy-start(bf16[512,512]{1,0:T(8,128)(2,1)} %wq.5) | copy-start | bytes 1572868
  18.3 6.3 %copy-start.5 = (s32[32,128]{1,0:T(8,128)S(1)}, s32[32,128]{1,0:T(8,128)}, u32[]{:S(2)}) copy-start(s32[32,128]{1,0:T(8,128)} %merch_slot.5) | copy-start | bytes 49156
  18.3 6.3 %copy-start.9 = (s32[32]{0:T(128)S(1)}, s32[32]{0:T(128)}, u32[]{:S(2)}) copy-start(s32[32]{0:T(128)} %count_ref.5) | copy-start | bytes 388
  18.3 6.3 %copy-start.10 = (f32[4]{0:T(128)S(1)}, f32[4]{0:T(128)}, u32[]{:S(2)}) copy-start(f32[4]{0:T(128)} %bias_ref.5) | copy-start | bytes 52
  24.5 2.2 %collective-permute-start.7 = (bf16[512,512]{1,0:T(8,128)(2,1)S(1)}, bf16[512,512]{1,0:T(8,128)(2,1)S(1)}, u32[]{:S(2)}, u32[]{:S(2)}) collective-permute-start(bf16[512,512]{1,0:T(8,128)(2,1)S(1)} %pad_maximum_fusion.feats), channel_id=1, source_target_pairs={{0,1},{1,0},{2,3},{3,2},{4,5},{5,4},{6,7},{7,6},{8,9},{9,8},{10,11... | collective-permute-start | bytes 1572872 | tf_op jit(solution)/shard_map/ppermute | solution.py:355
  26.2 2.1 %collective-permute-start.8 = (bf16[512,512]{1,0:T(8,128)(2,1)S(1)}, bf16[512,512]{1,0:T(8,128)(2,1)S(1)}, u32[]{:S(2)}, u32[]{:S(2)}) collective-permute-start(bf16[512,512]{1,0:T(8,128)(2,1)S(1)} %aggregate_odd.1), channel_id=1, source_target_pairs={{0,1},{1,0},{2,3},{3,2},{4,5},{5,4},{6,7},{7,6},{8,9},{9,8},{10,11... | collective-permute-start | bytes 1572872 | tf_op jit(solution)/shard_map/ppermute | solution.py:355
  26.7 5.2 %copy-start.1 = (bf16[4096,512]{1,0:T(8,128)(2,1)S(1)}, bf16[4096,512]{1,0:T(8,128)(2,1)}, u32[]{:S(2)}) copy-start(bf16[4096,512]{1,0:T(8,128)(2,1)} %acct.1) | copy-start | bytes 12582916
  28.3 8.6 %collective-permute-start.9 = (bf16[128,512]{1,0:T(8,128)(2,1)S(1)}, bf16[128,512]{1,0:T(8,128)(2,1)S(1)}, u32[]{:S(2)}, u32[]{:S(2)}) collective-permute-start(bf16[128,512]{1,0:T(8,128)(2,1)S(1)} %get-tuple-element.31), channel_id=1, source_target_pairs={{0,6},{1,7},{2,4},{3,5},{4,2},{5,3},{6,0},{7,1},{8,14},{9,15},{10,... | collective-permute-start | bytes 393224 | tf_op jit(solution)/shard_map/ppermute | solution.py:355
  30.4 7.5 %collective-permute-start.10 = (bf16[128,512]{1,0:T(8,128)(2,1)S(1)}, bf16[128,512]{1,0:T(8,128)(2,1)S(1)}, u32[]{:S(2)}, u32[]{:S(2)}) collective-permute-start(bf16[128,512]{1,0:T(8,128)(2,1)S(1)} %get-tuple-element.32), channel_id=1, source_target_pairs={{0,4},{1,5},{2,6},{3,7},{4,0},{5,1},{6,2},{7,3},{8,12},{9,13},{10,... | collective-permute-start | bytes 393224 | tf_op jit(solution)/shard_map/ppermute | solution.py:355
  31.4 6.5 %collective-permute-start.11 = (bf16[128,512]{1,0:T(8,128)(2,1)S(1)}, bf16[128,512]{1,0:T(8,128)(2,1)S(1)}, u32[]{:S(2)}, u32[]{:S(2)}) collective-permute-start(bf16[128,512]{1,0:T(8,128)(2,1)S(1)} %get-tuple-element.33), channel_id=1, source_target_pairs={{0,2},{1,3},{2,0},{3,1},{4,6},{5,7},{6,4},{7,5},{8,10},{9,11},{10,... | collective-permute-start | bytes 393224 | tf_op jit(solution)/shard_map/ppermute | solution.py:355
  35.7 10.1 %copy-start.4 = (bf16[512,512]{1,0:T(8,128)(2,1)S(1)}, bf16[512,512]{1,0:T(8,128)(2,1)}, u32[]{:S(2)}) copy-start(bf16[512,512]{1,0:T(8,128)(2,1)} %wo.1) | copy-start | bytes 1572868
  35.7 10.1 %copy-start.6 = (bf16[32,512]{1,0:T(8,128)(2,1)S(1)}, bf16[32,512]{1,0:T(8,128)(2,1)}, u32[]{:S(2)}) copy-start(bf16[32,512]{1,0:T(8,128)(2,1)} %feat.1) | copy-start | bytes 98308
  35.7 10.1 %copy-start.11 = (f32[512]{0:T(512)S(1)}, f32[512]{0:T(512)}, u32[]{:S(2)}) copy-start(f32[512]{0:T(512)} %param.19) | copy-start | bytes 6148
  38.0 5.8 %collective-permute-start.12 = (bf16[32,512]{1,0:T(8,128)(2,1)S(1)}, bf16[32,512]{1,0:T(8,128)(2,1)S(1)}, u32[]{:S(2)}, u32[]{:S(2)}) collective-permute-start(bf16[32,512]{1,0:T(8,128)(2,1)S(1)} %get-tuple-element.38), channel_id=1, source_target_pairs={{0,24},{1,25},{2,26},{3,27},{4,28},{5,29},{6,30},{7,31},{8,16},{9,... | collective-permute-start | bytes 98312 | tf_op jit(solution)/shard_map/ppermute | solution.py:355
  40.7 5.1 %collective-permute-start.13 = (bf16[32,512]{1,0:T(8,128)(2,1)S(1)}, bf16[32,512]{1,0:T(8,128)(2,1)S(1)}, u32[]{:S(2)}, u32[]{:S(2)}) collective-permute-start(bf16[32,512]{1,0:T(8,128)(2,1)S(1)} %get-tuple-element.39), channel_id=1, source_target_pairs={{0,16},{1,17},{2,18},{3,19},{4,20},{5,21},{6,22},{7,23},{8,24},{9,... | collective-permute-start | bytes 98312 | tf_op jit(solution)/shard_map/ppermute | solution.py:355
  41.0 4.8 %collective-permute-start.14 = (bf16[32,512]{1,0:T(8,128)(2,1)S(1)}, bf16[32,512]{1,0:T(8,128)(2,1)S(1)}, u32[]{:S(2)}, u32[]{:S(2)}) collective-permute-start(bf16[32,512]{1,0:T(8,128)(2,1)S(1)} %get-tuple-element.40), channel_id=1, source_target_pairs={{0,8},{1,9},{2,10},{3,11},{4,12},{5,13},{6,14},{7,15},{8,0},{9,1},... | collective-permute-start | bytes 98312 | tf_op jit(solution)/shard_map/ppermute | solution.py:355

commit v24 on v23

--- a/solution.py
+++ b/solution.py
@@ -85,7 +85,7 @@
         emit(2 * h, rows0, odd)
         emit(2 * h + 1, rows1, odd)
 
-    @pl.loop(outer, blocks)
+    @pl.loop(outer, blocks, unroll=2)
     def _(i):
         collect(odd_block(i), rows0)
         collect(jnp.bitwise_xor(me, _offset(i, outer)), rows1)

time: 46.9 us -> 46.7 us (level)
  no operation moved by 1% of the time
where the time goes in v24:
time: 46.7 us; the launch traced here: 46.4 us
  Pallas kernels  22.8 us (49%)
  starting transfers between devices  17.5 us (37%)
  waiting for transfers between devices  5.06 us (11%)
  local copies, waits for them, and re-layouts  0.77 us (2%)
    ppermute x15, starting transfers between devices, swap(): return lax.ppermute(value, AXES, [(s, s ^ mask) for s in range(devices)])  17.5 us
    pallas_call x1, Pallas kernels, gather(): pl.pallas_call(functools.partial(gather_kernel, outer), out_shape=(jax.Sh...  8.27 us
    pallas_call x2, Pallas kernels, project(): pl.pallas_call(functools.partial(project_kernel, outer, spans), out_shape...  6.96 us
    ppermute x15, waiting for transfers between devices, swap(): return lax.ppermute(value, AXES, [(s, s ^ mask) for s in range(devices)])  5.06 us
    pallas_call x3, Pallas kernels, aggregate(): pl.pallas_call(functools.partial(aggregate_kernel, outer, first, shift),...  3.97 us
    pallas_call x1, Pallas kernels, pick(): pl.pallas_call(functools.partial(pick_kernel, outer), out_shape=jax.Shape...  2.51 us
  transfers between devices with their start and end apart: 15, of which 6 were waited for; matrix products, arithmetic and copies ran while one was open for 0% of the time, Pallas kernels for 47%

profile of v24, /device:TPU:0, one launch (start us, length us, event | category | flops | bytes accessed | tf_op | source)
XLA Modules:
  0.0 46.4 jit_solution(17686404264050444923)
XLA Ops:
  0.0 3.5 %collective-permute-start.2 = (bf16[32,512]{1,0:T(8,128)(2,1)}, bf16[32,512]{1,0:T(8,128)(2,1)S(1)}, u32[]{:S(2)}, u32[]{:S(2)}) collective-permute-start(bf16[32,512]{1,0:T(8,128)(2,1)} %feat.1), channel_id=1, source_target_pairs={{0,17},{1,16},{2,19},{3,18},{4,21},{5,20},{6,23},{7,22},{8,25},{9,... | collective-permute-start | bytes 98312 | tf_op jit(solution)/shard_map/ppermute | solution.py:355
  3.5 1.6 %collective-permute-start.1 = (bf16[32,512]{1,0:T(8,128)(2,1)}, bf16[32,512]{1,0:T(8,128)(2,1)S(1)}, u32[]{:S(2)}, u32[]{:S(2)}) collective-permute-start(bf16[32,512]{1,0:T(8,128)(2,1)} %feat.1), channel_id=1, source_target_pairs={{0,25},{1,24},{2,27},{3,26},{4,29},{5,28},{6,31},{7,30},{8,17},{9,... | collective-permute-start | bytes 98312 | tf_op jit(solution)/shard_map/ppermute | solution.py:355
  5.1 0.2 collective-permute-start
  5.3 0.7 %copy-done.7 = s32[32,128]{1,0:T(8,128)S(1)} copy-done((s32[32,128]{1,0:T(8,128)S(1)}, s32[32,128]{1,0:T(8,128)}, u32[]{:S(2)}) %copy-start.7) | copy-done | bytes 16408
  6.1 8.3 %gather_slots.1 = (bf16[16,128,512]{2,1,0:T(8,128)(2,1)S(1)}, bf16[12,128,512]{2,1,0:T(8,128)(2,1)S(1)}) custom-call(s32[1]{0:T(128)} %bitcast.1.me_ref, s32[32,128]{1,0:T(8,128)S(1)} %copy-done.7, bf16[4096,512]{1,0:T(8,128)(2,1)} %acct.1), custom_call_target="tpu_custom_call" | custom-call | bytes 20971520 | tf_op jit(solution)/shard_map/gather_slots/pallas_call | solution.py:103
  14.4 2.5 %collective-permute-start.6 = (bf16[128,512]{1,0:T(8,128)(2,1)S(1)}, bf16[128,512]{1,0:T(8,128)(2,1)S(1)}, u32[]{:S(2)}, u32[]{:S(2)}) collective-permute-start(bf16[128,512]{1,0:T(8,128)(2,1)S(1)} %assemble.1), channel_id=1, source_target_pairs={{0,6},{1,7},{2,4},{3,5},{4,2},{5,3},{6,0},{7,1},{8,14},{9,15},{10,... | collective-permute-start | bytes 393224 | tf_op jit(solution)/shard_map/ppermute | solution.py:355
  16.9 0.5 %collective-permute-start.5 = (bf16[128,512]{1,0:T(8,128)(2,1)S(1)}, bf16[128,512]{1,0:T(8,128)(2,1)S(1)}, u32[]{:S(2)}, u32[]{:S(2)}) collective-permute-start(bf16[128,512]{1,0:T(8,128)(2,1)S(1)} %assemble.1), channel_id=1, source_target_pairs={{0,4},{1,5},{2,6},{3,7},{4,0},{5,1},{6,2},{7,3},{8,12},{9,13},{10,... | collective-permute-start | bytes 393224 | tf_op jit(solution)/shard_map/ppermute | solution.py:355
  17.4 0.5 %collective-permute-start.4 = (bf16[128,512]{1,0:T(8,128)(2,1)S(1)}, bf16[128,512]{1,0:T(8,128)(2,1)S(1)}, u32[]{:S(2)}, u32[]{:S(2)}) collective-permute-start(bf16[128,512]{1,0:T(8,128)(2,1)S(1)} %assemble.1), channel_id=1, source_target_pairs={{0,2},{1,3},{2,0},{3,1},{4,6},{5,7},{6,4},{7,5},{8,10},{9,11},{10,... | collective-permute-start | bytes 393224 | tf_op jit(solution)/shard_map/ppermute | solution.py:355
  18.0 0.0 copy-start.5
  18.0 5.7 %project_slots.2 = (bf16[16,512,128]{2,1,0:T(8,128)(2,1)S(1)}, bf16[16,128,512]{2,1,0:T(8,128)(2,1)S(1)}, bf16[12,512,128]{2,1,0:T(8,128)(2,1)S(1)}, bf16[12,128,512]{2,1,0:T(8,128)(2,1)S(1)}) custom-call(s32[1]{0:T(128)} %bitcast.1.me_ref, s32[32]{0:T(128)S(1)} %copy-done.8, bf16[4,512,512]{2,1,0:T(8,128)(2,1)S(1)} %copy-done.2, ...), custom_call_target="tpu_custom_call" | custom-call | flops 3758096384 | bytes 14680064 | tf_op jit(solution)/shard_map/project_slots/pallas_call | solution.py:187
  23.7 0.4 collective-permute-done.5
  24.1 0.1 collective-permute-done.4
  24.2 0.1 collective-permute-start.7
  24.3 1.5 %aggregate_odd.1 = bf16[512,512]{1,0:T(8,128)(2,1)S(1)} custom-call(s32[1]{0:T(128)} %bitcast.1.me_ref, s32[32]{0:T(128)S(1)} %copy-done.8, s32[32]{0:T(128)S(1)} %copy-done.9, f32[4]{0:T(128)S(1)} %copy-done.10, s32[32,128]{1,0:T(8,128)S(1)} %copy-done.5, bf16[512,512]{1,0:T(8,128)(2,1)S(1)} %pad_maximum_fusion.feats, bf16[512,512]{1,0:T(8,128)(2,1)S(1)} %copy-done, ...), custom_call_target="tpu_custom_call" | custom-call | flops 402653184 | bytes 6291456 | tf_op jit(solution)/shard_map/aggregate_odd/pallas_call | solution.py:247
  25.9 0.5 %collective-permute-start.8 = (bf16[512,512]{1,0:T(8,128)(2,1)S(1)}, bf16[512,512]{1,0:T(8,128)(2,1)S(1)}, u32[]{:S(2)}, u32[]{:S(2)}) collective-permute-start(bf16[512,512]{1,0:T(8,128)(2,1)S(1)} %aggregate_odd.1), channel_id=1, source_target_pairs={{0,1},{1,0},{2,3},{3,2},{4,5},{5,4},{6,7},{7,6},{8,9},{9,8},{10,11... | collective-permute-start | bytes 1572872 | tf_op jit(solution)/shard_map/ppermute | solution.py:355
  26.4 1.3 %aggregate_even.2.mine = f32[384,512]{1,0:T(8,128)S(1)} custom-call(s32[1]{0:T(128)} %bitcast.1.me_ref, s32[32]{0:T(128)S(1)} %copy-done.8, s32[32]{0:T(128)S(1)} %copy-done.9, f32[4]{0:T(128)S(1)} %copy-done.10, s32[32,128]{1,0:T(8,128)S(1)} %copy-done.5, bf16[512,512]{1,0:T(8,128)(2,1)S(1)} %collective-permute-done.7.feats, bf16[512,512]{1,0:T(8,128)(2,1)S(1)} %copy-done, ...), custom_call_target="tpu_custom_call" | custom-call | flops 301989888 | bytes 6291456 | tf_op jit(solution)/shard_map/aggregate_even/pallas_call | solution.py:247
  27.8 0.2 collective-permute-done.8.other
  28.0 0.1 combine_cores.2
  28.0 2.1 %collective-permute-start.9 = (bf16[128,512]{1,0:T(8,128)(2,1)S(1)}, bf16[128,512]{1,0:T(8,128)(2,1)S(1)}, u32[]{:S(2)}, u32[]{:S(2)}) collective-permute-start(bf16[128,512]{1,0:T(8,128)(2,1)S(1)} %get-tuple-element.31), channel_id=1, source_target_pairs={{0,6},{1,7},{2,4},{3,5},{4,2},{5,3},{6,0},{7,1},{8,14},{9,15},{10,... | collective-permute-start | bytes 393224 | tf_op jit(solution)/shard_map/ppermute | solution.py:355
  30.1 1.0 %collective-permute-start.10 = (bf16[128,512]{1,0:T(8,128)(2,1)S(1)}, bf16[128,512]{1,0:T(8,128)(2,1)S(1)}, u32[]{:S(2)}, u32[]{:S(2)}) collective-permute-start(bf16[128,512]{1,0:T(8,128)(2,1)S(1)} %get-tuple-element.32), channel_id=1, source_target_pairs={{0,4},{1,5},{2,6},{3,7},{4,0},{5,1},{6,2},{7,3},{8,12},{9,13},{10,... | collective-permute-start | bytes 393224 | tf_op jit(solution)/shard_map/ppermute | solution.py:355
  31.1 0.5 %collective-permute-start.11 = (bf16[128,512]{1,0:T(8,128)(2,1)S(1)}, bf16[128,512]{1,0:T(8,128)(2,1)S(1)}, u32[]{:S(2)}, u32[]{:S(2)}) collective-permute-start(bf16[128,512]{1,0:T(8,128)(2,1)S(1)} %get-tuple-element.33), channel_id=1, source_target_pairs={{0,2},{1,3},{2,0},{3,1},{4,6},{5,7},{6,4},{7,5},{8,10},{9,11},{10,... | collective-permute-start | bytes 393224 | tf_op jit(solution)/shard_map/ppermute | solution.py:355
  31.6 2.5 %pick_rows.1.refs_0_ = bf16[4,128,512]{2,1,0:T(8,128)(2,1)S(1)} custom-call(s32[1]{0:T(128)} %bitcast.1.me_ref, s32[32,128]{1,0:T(8,128)S(1)} %copy-done.7, bf16[4096,512]{1,0:T(8,128)(2,1)S(1)} %copy-done.1), custom_call_target="tpu_custom_call" | custom-call | flops 2147483648 | bytes 8388608 | tf_op jit(solution)/shard_map/pick_rows/pallas_call | solution.py:149
  34.1 1.3 %project_slots.3 = (bf16[4,512,128]{2,1,0:T(8,128)(2,1)S(1)}, bf16[4,128,512]{2,1,0:T(8,128)(2,1)S(1)}) custom-call(s32[1]{0:T(128)} %bitcast.1.me_ref, s32[32]{0:T(128)S(1)} %copy-done.8, bf16[4,512,512]{2,1,0:T(8,128)(2,1)S(1)} %copy-done.2, bf16[4,512,512]{2,1,0:T(8,128)(2,1)S(1)} %copy-done.3, bf16[4,128,512]{2,1,0:T(8,128)(2,1)S(1)} %pick_rows.1.refs_0_), custom_call_target="tpu_custom_call" | custom-call | flops 536870912 | bytes 2097152 | tf_op jit(solution)/shard_map/project_slots/pallas_call | solution.py:187
  35.5 1.1 %aggregate_even.3.mine = f32[128,512]{1,0:T(8,128)S(1)} custom-call(s32[1]{0:T(128)} %bitcast.1.me_ref, s32[32]{0:T(128)S(1)} %copy-done.8, s32[32]{0:T(128)S(1)} %copy-done.9, f32[4]{0:T(128)S(1)} %copy-done.10, s32[32,128]{1,0:T(8,128)S(1)} %copy-done.5, bf16[512,512]{1,0:T(8,128)(2,1)S(1)} %collective-permute-done.7.feats, bf16[512,512]{1,0:T(8,128)(2,1)S(1)} %copy-done, ...), custom_call_target="tpu_custom_call" | custom-call | flops 100663296 | bytes 6291456 | tf_op jit(solution)/shard_map/aggregate_even/pallas_call | solution.py:247
  36.6 1.0 %collective-permute-done.10.refs_2_ = bf16[128,512]{1,0:T(8,128)(2,1)S(1)} collective-permute-done((bf16[128,512]{1,0:T(8,128)(2,1)S(1)}, bf16[128,512]{1,0:T(8,128)(2,1)S(1)}, u32[]{:S(2)}, u32[]{:S(2)}) %collective-permute-start.10) | collective-permute-done | bytes 131104 | tf_op jit(solution)/shard_map/ppermute | solution.py:355
  37.6 0.1 combine_plane.1
  37.7 2.7 %collective-permute-start.12 = (bf16[32,512]{1,0:T(8,128)(2,1)S(1)}, bf16[32,512]{1,0:T(8,128)(2,1)S(1)}, u32[]{:S(2)}, u32[]{:S(2)}) collective-permute-start(bf16[32,512]{1,0:T(8,128)(2,1)S(1)} %get-tuple-element.38), channel_id=1, source_target_pairs={{0,24},{1,25},{2,26},{3,27},{4,28},{5,29},{6,30},{7,31},{8,16},{9,... | collective-permute-start | bytes 98312 | tf_op jit(solution)/shard_map/ppermute | solution.py:355
  40.4 0.3 collective-permute-start.13
  40.7 1.4 %collective-permute-start.14 = (bf16[32,512]{1,0:T(8,128)(2,1)S(1)}, bf16[32,512]{1,0:T(8,128)(2,1)S(1)}, u32[]{:S(2)}, u32[]{:S(2)}) collective-permute-start(bf16[32,512]{1,0:T(8,128)(2,1)S(1)} %get-tuple-element.40), channel_id=1, source_target_pairs={{0,8},{1,9},{2,10},{3,11},{4,12},{5,13},{6,14},{7,15},{8,0},{9,1},... | collective-permute-start | bytes 98312 | tf_op jit(solution)/shard_map/ppermute | solution.py:355
  42.1 1.3 %collective-permute-done.12.refs_1_ = bf16[32,512]{1,0:T(8,128)(2,1)S(1)} collective-permute-done((bf16[32,512]{1,0:T(8,128)(2,1)S(1)}, bf16[32,512]{1,0:T(8,128)(2,1)S(1)}, u32[]{:S(2)}, u32[]{:S(2)}) %collective-permute-start.12) | collective-permute-done | bytes 32800 | tf_op jit(solution)/shard_map/ppermute | solution.py:355
  43.4 2.0 %collective-permute-done.13.refs_2_ = bf16[32,512]{1,0:T(8,128)(2,1)S(1)} collective-permute-done((bf16[32,512]{1,0:T(8,128)(2,1)S(1)}, bf16[32,512]{1,0:T(8,128)(2,1)S(1)}, u32[]{:S(2)}, u32[]{:S(2)}) %collective-permute-start.13) | collective-permute-done | bytes 32800 | tf_op jit(solution)/shard_map/ppermute | solution.py:355
  45.5 0.9 %finish.1 = bf16[32,512]{1,0:T(8,128)(2,1)} custom-call(bf16[32,512]{1,0:T(8,128)(2,1)S(1)} %copy-done.6, f32[1,512]{1,0:T(1,128)S(1)} %bitcast.2, bf16[512,512]{1,0:T(8,128)(2,1)S(1)} %copy-done.4, f32[32,512]{1,0:T(8,128)S(1)} %get-tuple-element.37.refs_0_, bf16[32,512]{1,0:T(8,128)(2,1)S(1)} %collective-permute-done.12.refs_1_, ...), custom_call_target="tpu_custom_call" | custom-call | tf_op jit(solution)/shard_map/finish/pallas_call | solution.py:325
  (35 shorter events, 0.2 us)
Async XLA Ops:
  0.0 14.3 %collective-permute-start.2 = (bf16[32,512]{1,0:T(8,128)(2,1)}, bf16[32,512]{1,0:T(8,128)(2,1)S(1)}, u32[]{:S(2)}, u32[]{:S(2)}) collective-permute-start(bf16[32,512]{1,0:T(8,128)(2,1)} %feat.1), channel_id=1, source_target_pairs={{0,17},{1,16},{2,19},{3,18},{4,21},{5,20},{6,23},{7,22},{8,25},{9,... | collective-permute-start | bytes 98312 | tf_op jit(solution)/shard_map/ppermute | solution.py:355
  3.5 10.9 %collective-permute-start.1 = (bf16[32,512]{1,0:T(8,128)(2,1)}, bf16[32,512]{1,0:T(8,128)(2,1)S(1)}, u32[]{:S(2)}, u32[]{:S(2)}) collective-permute-start(bf16[32,512]{1,0:T(8,128)(2,1)} %feat.1), channel_id=1, source_target_pairs={{0,25},{1,24},{2,27},{3,26},{4,29},{5,28},{6,31},{7,30},{8,17},{9,... | collective-permute-start | bytes 98312 | tf_op jit(solution)/shard_map/ppermute | solution.py:355
  5.1 9.3 %collective-permute-start = (bf16[32,512]{1,0:T(8,128)(2,1)}, bf16[32,512]{1,0:T(8,128)(2,1)S(1)}, u32[]{:S(2)}, u32[]{:S(2)}) collective-permute-start(bf16[32,512]{1,0:T(8,128)(2,1)} %feat.1), channel_id=1, source_target_pairs={{0,9},{1,8},{2,11},{3,10},{4,13},{5,12},{6,15},{7,14},{8,1},{9,0},... | collective-permute-start | bytes 98312 | tf_op jit(solution)/shard_map/ppermute | solution.py:355
  5.3 9.0 %collective-permute-start.3 = (bf16[32,512]{1,0:T(8,128)(2,1)}, bf16[32,512]{1,0:T(8,128)(2,1)S(1)}, u32[]{:S(2)}, u32[]{:S(2)}) collective-permute-start(bf16[32,512]{1,0:T(8,128)(2,1)} %feat.1), channel_id=1, source_target_pairs={{0,1},{1,0},{2,3},{3,2},{4,5},{5,4},{6,7},{7,6},{8,9},{9,8},{10,11... | collective-permute-start | bytes 98312 | tf_op jit(solution)/shard_map/ppermute | solution.py:355
  5.3 0.7 %copy-start.7 = (s32[32,128]{1,0:T(8,128)S(1)}, s32[32,128]{1,0:T(8,128)}, u32[]{:S(2)}) copy-start(s32[32,128]{1,0:T(8,128)} %slots.1) | copy-start | bytes 49156
  6.1 11.9 %copy-start.2 = (bf16[4,512,512]{2,1,0:T(8,128)(2,1)S(1)}, bf16[4,512,512]{2,1,0:T(8,128)(2,1)}, u32[]{:S(2)}) copy-start(bf16[4,512,512]{2,1,0:T(8,128)(2,1)} %kw.3) | copy-start | bytes 6291460
  6.1 11.9 %copy-start.3 = (bf16[4,512,512]{2,1,0:T(8,128)(2,1)S(1)}, bf16[4,512,512]{2,1,0:T(8,128)(2,1)}, u32[]{:S(2)}) copy-start(bf16[4,512,512]{2,1,0:T(8,128)(2,1)} %mw.3) | copy-start | bytes 6291460
  6.1 11.9 %copy-start.8 = (s32[32]{0:T(128)S(1)}, s32[32]{0:T(128)}, u32[]{:S(2)}) copy-start(s32[32]{0:T(128)} %rel_ref.9) | copy-start | bytes 388
  14.4 9.3 %collective-permute-start.6 = (bf16[128,512]{1,0:T(8,128)(2,1)S(1)}, bf16[128,512]{1,0:T(8,128)(2,1)S(1)}, u32[]{:S(2)}, u32[]{:S(2)}) collective-permute-start(bf16[128,512]{1,0:T(8,128)(2,1)S(1)} %assemble.1), channel_id=1, source_target_pairs={{0,6},{1,7},{2,4},{3,5},{4,2},{5,3},{6,0},{7,1},{8,14},{9,15},{10,... | collective-permute-start | bytes 393224 | tf_op jit(solution)/shard_map/ppermute | solution.py:355
  16.9 7.2 %collective-permute-start.5 = (bf16[128,512]{1,0:T(8,128)(2,1)S(1)}, bf16[128,512]{1,0:T(8,128)(2,1)S(1)}, u32[]{:S(2)}, u32[]{:S(2)}) collective-permute-start(bf16[128,512]{1,0:T(8,128)(2,1)S(1)} %assemble.1), channel_id=1, source_target_pairs={{0,4},{1,5},{2,6},{3,7},{4,0},{5,1},{6,2},{7,3},{8,12},{9,13},{10,... | collective-permute-start | bytes 393224 | tf_op jit(solution)/shard_map/ppermute | solution.py:355
  17.4 6.8 %collective-permute-start.4 = (bf16[128,512]{1,0:T(8,128)(2,1)S(1)}, bf16[128,512]{1,0:T(8,128)(2,1)S(1)}, u32[]{:S(2)}, u32[]{:S(2)}) collective-permute-start(bf16[128,512]{1,0:T(8,128)(2,1)S(1)} %assemble.1), channel_id=1, source_target_pairs={{0,2},{1,3},{2,0},{3,1},{4,6},{5,7},{6,4},{7,5},{8,10},{9,11},{10,... | collective-permute-start | bytes 393224 | tf_op jit(solution)/shard_map/ppermute | solution.py:355
  18.0 6.3 %copy-start = (bf16[512,512]{1,0:T(8,128)(2,1)S(1)}, bf16[512,512]{1,0:T(8,128)(2,1)}, u32[]{:S(2)}) copy-start(bf16[512,512]{1,0:T(8,128)(2,1)} %wq.5) | copy-start | bytes 1572868
  18.0 6.3 %copy-start.5 = (s32[32,128]{1,0:T(8,128)S(1)}, s32[32,128]{1,0:T(8,128)}, u32[]{:S(2)}) copy-start(s32[32,128]{1,0:T(8,128)} %merch_slot.5) | copy-start | bytes 49156
  18.0 6.3 %copy-start.9 = (s32[32]{0:T(128)S(1)}, s32[32]{0:T(128)}, u32[]{:S(2)}) copy-start(s32[32]{0:T(128)} %count_ref.5) | copy-start | bytes 388
  18.0 6.3 %copy-start.10 = (f32[4]{0:T(128)S(1)}, f32[4]{0:T(128)}, u32[]{:S(2)}) copy-start(f32[4]{0:T(128)} %bias_ref.5) | copy-start | bytes 52
  24.2 2.2 %collective-permute-start.7 = (bf16[512,512]{1,0:T(8,128)(2,1)S(1)}, bf16[512,512]{1,0:T(8,128)(2,1)S(1)}, u32[]{:S(2)}, u32[]{:S(2)}) collective-permute-start(bf16[512,512]{1,0:T(8,128)(2,1)S(1)} %pad_maximum_fusion.feats), channel_id=1, source_target_pairs={{0,1},{1,0},{2,3},{3,2},{4,5},{5,4},{6,7},{7,6},{8,9},{9,8},{10,11... | collective-permute-start | bytes 1572872 | tf_op jit(solution)/shard_map/ppermute | solution.py:355
  25.9 2.1 %collective-permute-start.8 = (bf16[512,512]{1,0:T(8,128)(2,1)S(1)}, bf16[512,512]{1,0:T(8,128)(2,1)S(1)}, u32[]{:S(2)}, u32[]{:S(2)}) collective-permute-start(bf16[512,512]{1,0:T(8,128)(2,1)S(1)} %aggregate_odd.1), channel_id=1, source_target_pairs={{0,1},{1,0},{2,3},{3,2},{4,5},{5,4},{6,7},{7,6},{8,9},{9,8},{10,11... | collective-permute-start | bytes 1572872 | tf_op jit(solution)/shard_map/ppermute | solution.py:355
  26.4 5.2 %copy-start.1 = (bf16[4096,512]{1,0:T(8,128)(2,1)S(1)}, bf16[4096,512]{1,0:T(8,128)(2,1)}, u32[]{:S(2)}) copy-start(bf16[4096,512]{1,0:T(8,128)(2,1)} %acct.1) | copy-start | bytes 12582916
  28.0 8.5 %collective-permute-start.9 = (bf16[128,512]{1,0:T(8,128)(2,1)S(1)}, bf16[128,512]{1,0:T(8,128)(2,1)S(1)}, u32[]{:S(2)}, u32[]{:S(2)}) collective-permute-start(bf16[128,512]{1,0:T(8,128)(2,1)S(1)} %get-tuple-element.31), channel_id=1, source_target_pairs={{0,6},{1,7},{2,4},{3,5},{4,2},{5,3},{6,0},{7,1},{8,14},{9,15},{10,... | collective-permute-start | bytes 393224 | tf_op jit(solution)/shard_map/ppermute | solution.py:355
  30.1 7.5 %collective-permute-start.10 = (bf16[128,512]{1,0:T(8,128)(2,1)S(1)}, bf16[128,512]{1,0:T(8,128)(2,1)S(1)}, u32[]{:S(2)}, u32[]{:S(2)}) collective-permute-start(bf16[128,512]{1,0:T(8,128)(2,1)S(1)} %get-tuple-element.32), channel_id=1, source_target_pairs={{0,4},{1,5},{2,6},{3,7},{4,0},{5,1},{6,2},{7,3},{8,12},{9,13},{10,... | collective-permute-start | bytes 393224 | tf_op jit(solution)/shard_map/ppermute | solution.py:355
  31.1 6.5 %collective-permute-start.11 = (bf16[128,512]{1,0:T(8,128)(2,1)S(1)}, bf16[128,512]{1,0:T(8,128)(2,1)S(1)}, u32[]{:S(2)}, u32[]{:S(2)}) collective-permute-start(bf16[128,512]{1,0:T(8,128)(2,1)S(1)} %get-tuple-element.33), channel_id=1, source_target_pairs={{0,2},{1,3},{2,0},{3,1},{4,6},{5,7},{6,4},{7,5},{8,10},{9,11},{10,... | collective-permute-start | bytes 393224 | tf_op jit(solution)/shard_map/ppermute | solution.py:355
  35.4 10.1 %copy-start.4 = (bf16[512,512]{1,0:T(8,128)(2,1)S(1)}, bf16[512,512]{1,0:T(8,128)(2,1)}, u32[]{:S(2)}) copy-start(bf16[512,512]{1,0:T(8,128)(2,1)} %wo.1) | copy-start | bytes 1572868
  35.4 10.1 %copy-start.6 = (bf16[32,512]{1,0:T(8,128)(2,1)S(1)}, bf16[32,512]{1,0:T(8,128)(2,1)}, u32[]{:S(2)}) copy-start(bf16[32,512]{1,0:T(8,128)(2,1)} %feat.1) | copy-start | bytes 98308
  35.4 10.1 %copy-start.11 = (f32[512]{0:T(512)S(1)}, f32[512]{0:T(512)}, u32[]{:S(2)}) copy-start(f32[512]{0:T(512)} %param.19) | copy-start | bytes 6148
  37.7 5.8 %collective-permute-start.12 = (bf16[32,512]{1,0:T(8,128)(2,1)S(1)}, bf16[32,512]{1,0:T(8,128)(2,1)S(1)}, u32[]{:S(2)}, u32[]{:S(2)}) collective-permute-start(bf16[32,512]{1,0:T(8,128)(2,1)S(1)} %get-tuple-element.38), channel_id=1, source_target_pairs={{0,24},{1,25},{2,26},{3,27},{4,28},{5,29},{6,30},{7,31},{8,16},{9,... | collective-permute-start | bytes 98312 | tf_op jit(solution)/shard_map/ppermute | solution.py:355
  40.4 5.1 %collective-permute-start.13 = (bf16[32,512]{1,0:T(8,128)(2,1)S(1)}, bf16[32,512]{1,0:T(8,128)(2,1)S(1)}, u32[]{:S(2)}, u32[]{:S(2)}) collective-permute-start(bf16[32,512]{1,0:T(8,128)(2,1)S(1)} %get-tuple-element.39), channel_id=1, source_target_pairs={{0,16},{1,17},{2,18},{3,19},{4,20},{5,21},{6,22},{7,23},{8,24},{9,... | collective-permute-start | bytes 98312 | tf_op jit(solution)/shard_map/ppermute | solution.py:355
  40.7 4.8 %collective-permute-start.14 = (bf16[32,512]{1,0:T(8,128)(2,1)S(1)}, bf16[32,512]{1,0:T(8,128)(2,1)S(1)}, u32[]{:S(2)}, u32[]{:S(2)}) collective-permute-start(bf16[32,512]{1,0:T(8,128)(2,1)S(1)} %get-tuple-element.40), channel_id=1, source_target_pairs={{0,8},{1,9},{2,10},{3,11},{4,12},{5,13},{6,14},{7,15},{8,0},{9,1},... | collective-permute-start | bytes 98312 | tf_op jit(solution)/shard_map/ppermute | solution.py:355

commit v25 on v24

--- a/solution.py
+++ b/solution.py
@@ -85,7 +85,7 @@
         emit(2 * h, rows0, odd)
         emit(2 * h + 1, rows1, odd)
 
-    @pl.loop(outer, blocks, unroll=2)
+    @pl.loop(outer, blocks, unroll=4)
     def _(i):
         collect(odd_block(i), rows0)
         collect(jnp.bitwise_xor(me, _offset(i, outer)), rows1)

time: 46.7 us -> 46.6 us (level)
  no operation moved by 1% of the time
where the time goes in v25:
time: 46.6 us; the launch traced here: 46.3 us
  Pallas kernels  22.7 us (49%)
  starting transfers between devices  17.5 us (38%)
  waiting for transfers between devices  5.06 us (11%)
  local copies, waits for them, and re-layouts  0.77 us (2%)
    ppermute x15, starting transfers between devices, swap(): return lax.ppermute(value, AXES, [(s, s ^ mask) for s in range(devices)])  17.5 us
    pallas_call x1, Pallas kernels, gather(): pl.pallas_call(functools.partial(gather_kernel, outer), out_shape=(jax.Sh...  8.18 us
    pallas_call x2, Pallas kernels, project(): pl.pallas_call(functools.partial(project_kernel, outer, spans), out_shape...  6.96 us
    ppermute x15, waiting for transfers between devices, swap(): return lax.ppermute(value, AXES, [(s, s ^ mask) for s in range(devices)])  5.06 us
    pallas_call x3, Pallas kernels, aggregate(): pl.pallas_call(functools.partial(aggregate_kernel, outer, first, shift),...  3.97 us
    pallas_call x1, Pallas kernels, pick(): pl.pallas_call(functools.partial(pick_kernel, outer), out_shape=jax.Shape...  2.51 us
  transfers between devices with their start and end apart: 15, of which 6 were waited for; matrix products, arithmetic and copies ran while one was open for 0% of the time, Pallas kernels for 47%

profile of v25, /device:TPU:0, one launch (start us, length us, event | category | flops | bytes accessed | tf_op | source)
XLA Modules:
  0.0 46.3 jit_solution(11247966154292583361)
XLA Ops:
  0.0 3.5 %collective-permute-start.2 = (bf16[32,512]{1,0:T(8,128)(2,1)}, bf16[32,512]{1,0:T(8,128)(2,1)S(1)}, u32[]{:S(2)}, u32[]{:S(2)}) collective-permute-start(bf16[32,512]{1,0:T(8,128)(2,1)} %feat.1), channel_id=1, source_target_pairs={{0,17},{1,16},{2,19},{3,18},{4,21},{5,20},{6,23},{7,22},{8,25},{9,... | collective-permute-start | bytes 98312 | tf_op jit(solution)/shard_map/ppermute | solution.py:355
  3.5 1.6 %collective-permute-start.1 = (bf16[32,512]{1,0:T(8,128)(2,1)}, bf16[32,512]{1,0:T(8,128)(2,1)S(1)}, u32[]{:S(2)}, u32[]{:S(2)}) collective-permute-start(bf16[32,512]{1,0:T(8,128)(2,1)} %feat.1), channel_id=1, source_target_pairs={{0,25},{1,24},{2,27},{3,26},{4,29},{5,28},{6,31},{7,30},{8,17},{9,... | collective-permute-start | bytes 98312 | tf_op jit(solution)/shard_map/ppermute | solution.py:355
  5.1 0.2 collective-permute-start
  5.3 0.7 %copy-done.7 = s32[32,128]{1,0:T(8,128)S(1)} copy-done((s32[32,128]{1,0:T(8,128)S(1)}, s32[32,128]{1,0:T(8,128)}, u32[]{:S(2)}) %copy-start.7) | copy-done | bytes 16408
  6.1 8.2 %gather_slots.1 = (bf16[16,128,512]{2,1,0:T(8,128)(2,1)S(1)}, bf16[12,128,512]{2,1,0:T(8,128)(2,1)S(1)}) custom-call(s32[1]{0:T(128)} %bitcast.1.me_ref, s32[32,128]{1,0:T(8,128)S(1)} %copy-done.7, bf16[4096,512]{1,0:T(8,128)(2,1)} %acct.1), custom_call_target="tpu_custom_call" | custom-call | bytes 20971520 | tf_op jit(solution)/shard_map/gather_slots/pallas_call | solution.py:103
  14.3 2.5 %collective-permute-start.6 = (bf16[128,512]{1,0:T(8,128)(2,1)S(1)}, bf16[128,512]{1,0:T(8,128)(2,1)S(1)}, u32[]{:S(2)}, u32[]{:S(2)}) collective-permute-start(bf16[128,512]{1,0:T(8,128)(2,1)S(1)} %assemble.1), channel_id=1, source_target_pairs={{0,6},{1,7},{2,4},{3,5},{4,2},{5,3},{6,0},{7,1},{8,14},{9,15},{10,... | collective-permute-start | bytes 393224 | tf_op jit(solution)/shard_map/ppermute | solution.py:355
  16.8 0.5 %collective-permute-start.5 = (bf16[128,512]{1,0:T(8,128)(2,1)S(1)}, bf16[128,512]{1,0:T(8,128)(2,1)S(1)}, u32[]{:S(2)}, u32[]{:S(2)}) collective-permute-start(bf16[128,512]{1,0:T(8,128)(2,1)S(1)} %assemble.1), channel_id=1, source_target_pairs={{0,4},{1,5},{2,6},{3,7},{4,0},{5,1},{6,2},{7,3},{8,12},{9,13},{10,... | collective-permute-start | bytes 393224 | tf_op jit(solution)/shard_map/ppermute | solution.py:355
  17.3 0.5 %collective-permute-start.4 = (bf16[128,512]{1,0:T(8,128)(2,1)S(1)}, bf16[128,512]{1,0:T(8,128)(2,1)S(1)}, u32[]{:S(2)}, u32[]{:S(2)}) collective-permute-start(bf16[128,512]{1,0:T(8,128)(2,1)S(1)} %assemble.1), channel_id=1, source_target_pairs={{0,2},{1,3},{2,0},{3,1},{4,6},{5,7},{6,4},{7,5},{8,10},{9,11},{10,... | collective-permute-start | bytes 393224 | tf_op jit(solution)/shard_map/ppermute | solution.py:355
  17.9 0.0 copy-start.5
  17.9 5.7 %project_slots.2 = (bf16[16,512,128]{2,1,0:T(8,128)(2,1)S(1)}, bf16[16,128,512]{2,1,0:T(8,128)(2,1)S(1)}, bf16[12,512,128]{2,1,0:T(8,128)(2,1)S(1)}, bf16[12,128,512]{2,1,0:T(8,128)(2,1)S(1)}) custom-call(s32[1]{0:T(128)} %bitcast.1.me_ref, s32[32]{0:T(128)S(1)} %copy-done.8, bf16[4,512,512]{2,1,0:T(8,128)(2,1)S(1)} %copy-done.2, ...), custom_call_target="tpu_custom_call" | custom-call | flops 3758096384 | bytes 14680064 | tf_op jit(solution)/shard_map/project_slots/pallas_call | solution.py:187
  23.6 0.4 collective-permute-done.5
  24.0 0.1 collective-permute-done.4
  24.1 0.1 collective-permute-start.7
  24.3 1.5 %aggregate_odd.1 = bf16[512,512]{1,0:T(8,128)(2,1)S(1)} custom-call(s32[1]{0:T(128)} %bitcast.1.me_ref, s32[32]{0:T(128)S(1)} %copy-done.8, s32[32]{0:T(128)S(1)} %copy-done.9, f32[4]{0:T(128)S(1)} %copy-done.10, s32[32,128]{1,0:T(8,128)S(1)} %copy-done.5, bf16[512,512]{1,0:T(8,128)(2,1)S(1)} %pad_maximum_fusion.feats, bf16[512,512]{1,0:T(8,128)(2,1)S(1)} %copy-done, ...), custom_call_target="tpu_custom_call" | custom-call | flops 402653184 | bytes 6291456 | tf_op jit(solution)/shard_map/aggregate_odd/pallas_call | solution.py:247
  25.8 0.5 %collective-permute-start.8 = (bf16[512,512]{1,0:T(8,128)(2,1)S(1)}, bf16[512,512]{1,0:T(8,128)(2,1)S(1)}, u32[]{:S(2)}, u32[]{:S(2)}) collective-permute-start(bf16[512,512]{1,0:T(8,128)(2,1)S(1)} %aggregate_odd.1), channel_id=1, source_target_pairs={{0,1},{1,0},{2,3},{3,2},{4,5},{5,4},{6,7},{7,6},{8,9},{9,8},{10,11... | collective-permute-start | bytes 1572872 | tf_op jit(solution)/shard_map/ppermute | solution.py:355
  26.3 1.3 %aggregate_even.2.mine = f32[384,512]{1,0:T(8,128)S(1)} custom-call(s32[1]{0:T(128)} %bitcast.1.me_ref, s32[32]{0:T(128)S(1)} %copy-done.8, s32[32]{0:T(128)S(1)} %copy-done.9, f32[4]{0:T(128)S(1)} %copy-done.10, s32[32,128]{1,0:T(8,128)S(1)} %copy-done.5, bf16[512,512]{1,0:T(8,128)(2,1)S(1)} %collective-permute-done.7.feats, bf16[512,512]{1,0:T(8,128)(2,1)S(1)} %copy-done, ...), custom_call_target="tpu_custom_call" | custom-call | flops 301989888 | bytes 6291456 | tf_op jit(solution)/shard_map/aggregate_even/pallas_call | solution.py:247
  27.7 0.2 collective-permute-done.8.other
  27.9 0.1 combine_cores.2
  27.9 2.1 %collective-permute-start.9 = (bf16[128,512]{1,0:T(8,128)(2,1)S(1)}, bf16[128,512]{1,0:T(8,128)(2,1)S(1)}, u32[]{:S(2)}, u32[]{:S(2)}) collective-permute-start(bf16[128,512]{1,0:T(8,128)(2,1)S(1)} %get-tuple-element.31), channel_id=1, source_target_pairs={{0,6},{1,7},{2,4},{3,5},{4,2},{5,3},{6,0},{7,1},{8,14},{9,15},{10,... | collective-permute-start | bytes 393224 | tf_op jit(solution)/shard_map/ppermute | solution.py:355
  30.0 1.0 %collective-permute-start.10 = (bf16[128,512]{1,0:T(8,128)(2,1)S(1)}, bf16[128,512]{1,0:T(8,128)(2,1)S(1)}, u32[]{:S(2)}, u32[]{:S(2)}) collective-permute-start(bf16[128,512]{1,0:T(8,128)(2,1)S(1)} %get-tuple-element.32), channel_id=1, source_target_pairs={{0,4},{1,5},{2,6},{3,7},{4,0},{5,1},{6,2},{7,3},{8,12},{9,13},{10,... | collective-permute-start | bytes 393224 | tf_op jit(solution)/shard_map/ppermute | solution.py:355
  31.0 0.5 %collective-permute-start.11 = (bf16[128,512]{1,0:T(8,128)(2,1)S(1)}, bf16[128,512]{1,0:T(8,128)(2,1)S(1)}, u32[]{:S(2)}, u32[]{:S(2)}) collective-permute-start(bf16[128,512]{1,0:T(8,128)(2,1)S(1)} %get-tuple-element.33), channel_id=1, source_target_pairs={{0,2},{1,3},{2,0},{3,1},{4,6},{5,7},{6,4},{7,5},{8,10},{9,11},{10,... | collective-permute-start | bytes 393224 | tf_op jit(solution)/shard_map/ppermute | solution.py:355
  31.5 2.5 %pick_rows.1.refs_0_ = bf16[4,128,512]{2,1,0:T(8,128)(2,1)S(1)} custom-call(s32[1]{0:T(128)} %bitcast.1.me_ref, s32[32,128]{1,0:T(8,128)S(1)} %copy-done.7, bf16[4096,512]{1,0:T(8,128)(2,1)S(1)} %copy-done.1), custom_call_target="tpu_custom_call" | custom-call | flops 2147483648 | bytes 8388608 | tf_op jit(solution)/shard_map/pick_rows/pallas_call | solution.py:149
  34.0 1.3 %project_slots.3 = (bf16[4,512,128]{2,1,0:T(8,128)(2,1)S(1)}, bf16[4,128,512]{2,1,0:T(8,128)(2,1)S(1)}) custom-call(s32[1]{0:T(128)} %bitcast.1.me_ref, s32[32]{0:T(128)S(1)} %copy-done.8, bf16[4,512,512]{2,1,0:T(8,128)(2,1)S(1)} %copy-done.2, bf16[4,512,512]{2,1,0:T(8,128)(2,1)S(1)} %copy-done.3, bf16[4,128,512]{2,1,0:T(8,128)(2,1)S(1)} %pick_rows.1.refs_0_), custom_call_target="tpu_custom_call" | custom-call | flops 536870912 | bytes 2097152 | tf_op jit(solution)/shard_map/project_slots/pallas_call | solution.py:187
  35.4 1.1 %aggregate_even.3.mine = f32[128,512]{1,0:T(8,128)S(1)} custom-call(s32[1]{0:T(128)} %bitcast.1.me_ref, s32[32]{0:T(128)S(1)} %copy-done.8, s32[32]{0:T(128)S(1)} %copy-done.9, f32[4]{0:T(128)S(1)} %copy-done.10, s32[32,128]{1,0:T(8,128)S(1)} %copy-done.5, bf16[512,512]{1,0:T(8,128)(2,1)S(1)} %collective-permute-done.7.feats, bf16[512,512]{1,0:T(8,128)(2,1)S(1)} %copy-done, ...), custom_call_target="tpu_custom_call" | custom-call | flops 100663296 | bytes 6291456 | tf_op jit(solution)/shard_map/aggregate_even/pallas_call | solution.py:247
  36.5 1.0 %collective-permute-done.10.refs_2_ = bf16[128,512]{1,0:T(8,128)(2,1)S(1)} collective-permute-done((bf16[128,512]{1,0:T(8,128)(2,1)S(1)}, bf16[128,512]{1,0:T(8,128)(2,1)S(1)}, u32[]{:S(2)}, u32[]{:S(2)}) %collective-permute-start.10) | collective-permute-done | bytes 131104 | tf_op jit(solution)/shard_map/ppermute | solution.py:355
  37.5 0.1 combine_plane.1
  37.6 2.7 %collective-permute-start.12 = (bf16[32,512]{1,0:T(8,128)(2,1)S(1)}, bf16[32,512]{1,0:T(8,128)(2,1)S(1)}, u32[]{:S(2)}, u32[]{:S(2)}) collective-permute-start(bf16[32,512]{1,0:T(8,128)(2,1)S(1)} %get-tuple-element.38), channel_id=1, source_target_pairs={{0,24},{1,25},{2,26},{3,27},{4,28},{5,29},{6,30},{7,31},{8,16},{9,... | collective-permute-start | bytes 98312 | tf_op jit(solution)/shard_map/ppermute | solution.py:355
  40.3 0.3 collective-permute-start.13
  40.6 1.4 %collective-permute-start.14 = (bf16[32,512]{1,0:T(8,128)(2,1)S(1)}, bf16[32,512]{1,0:T(8,128)(2,1)S(1)}, u32[]{:S(2)}, u32[]{:S(2)}) collective-permute-start(bf16[32,512]{1,0:T(8,128)(2,1)S(1)} %get-tuple-element.40), channel_id=1, source_target_pairs={{0,8},{1,9},{2,10},{3,11},{4,12},{5,13},{6,14},{7,15},{8,0},{9,1},... | collective-permute-start | bytes 98312 | tf_op jit(solution)/shard_map/ppermute | solution.py:355
  42.0 1.3 %collective-permute-done.12.refs_1_ = bf16[32,512]{1,0:T(8,128)(2,1)S(1)} collective-permute-done((bf16[32,512]{1,0:T(8,128)(2,1)S(1)}, bf16[32,512]{1,0:T(8,128)(2,1)S(1)}, u32[]{:S(2)}, u32[]{:S(2)}) %collective-permute-start.12) | collective-permute-done | bytes 32800 | tf_op jit(solution)/shard_map/ppermute | solution.py:355
  43.4 2.0 %collective-permute-done.13.refs_2_ = bf16[32,512]{1,0:T(8,128)(2,1)S(1)} collective-permute-done((bf16[32,512]{1,0:T(8,128)(2,1)S(1)}, bf16[32,512]{1,0:T(8,128)(2,1)S(1)}, u32[]{:S(2)}, u32[]{:S(2)}) %collective-permute-start.13) | collective-permute-done | bytes 32800 | tf_op jit(solution)/shard_map/ppermute | solution.py:355
  45.4 0.9 %finish.1 = bf16[32,512]{1,0:T(8,128)(2,1)} custom-call(bf16[32,512]{1,0:T(8,128)(2,1)S(1)} %copy-done.6, f32[1,512]{1,0:T(1,128)S(1)} %bitcast.2, bf16[512,512]{1,0:T(8,128)(2,1)S(1)} %copy-done.4, f32[32,512]{1,0:T(8,128)S(1)} %get-tuple-element.37.refs_0_, bf16[32,512]{1,0:T(8,128)(2,1)S(1)} %collective-permute-done.12.refs_1_, ...), custom_call_target="tpu_custom_call" | custom-call | tf_op jit(solution)/shard_map/finish/pallas_call | solution.py:325
  (35 shorter events, 0.2 us)
Async XLA Ops:
  0.0 14.3 %collective-permute-start.2 = (bf16[32,512]{1,0:T(8,128)(2,1)}, bf16[32,512]{1,0:T(8,128)(2,1)S(1)}, u32[]{:S(2)}, u32[]{:S(2)}) collective-permute-start(bf16[32,512]{1,0:T(8,128)(2,1)} %feat.1), channel_id=1, source_target_pairs={{0,17},{1,16},{2,19},{3,18},{4,21},{5,20},{6,23},{7,22},{8,25},{9,... | collective-permute-start | bytes 98312 | tf_op jit(solution)/shard_map/ppermute | solution.py:355
  3.5 10.8 %collective-permute-start.1 = (bf16[32,512]{1,0:T(8,128)(2,1)}, bf16[32,512]{1,0:T(8,128)(2,1)S(1)}, u32[]{:S(2)}, u32[]{:S(2)}) collective-permute-start(bf16[32,512]{1,0:T(8,128)(2,1)} %feat.1), channel_id=1, source_target_pairs={{0,25},{1,24},{2,27},{3,26},{4,29},{5,28},{6,31},{7,30},{8,17},{9,... | collective-permute-start | bytes 98312 | tf_op jit(solution)/shard_map/ppermute | solution.py:355
  5.1 9.2 %collective-permute-start = (bf16[32,512]{1,0:T(8,128)(2,1)}, bf16[32,512]{1,0:T(8,128)(2,1)S(1)}, u32[]{:S(2)}, u32[]{:S(2)}) collective-permute-start(bf16[32,512]{1,0:T(8,128)(2,1)} %feat.1), channel_id=1, source_target_pairs={{0,9},{1,8},{2,11},{3,10},{4,13},{5,12},{6,15},{7,14},{8,1},{9,0},... | collective-permute-start | bytes 98312 | tf_op jit(solution)/shard_map/ppermute | solution.py:355
  5.3 9.0 %collective-permute-start.3 = (bf16[32,512]{1,0:T(8,128)(2,1)}, bf16[32,512]{1,0:T(8,128)(2,1)S(1)}, u32[]{:S(2)}, u32[]{:S(2)}) collective-permute-start(bf16[32,512]{1,0:T(8,128)(2,1)} %feat.1), channel_id=1, source_target_pairs={{0,1},{1,0},{2,3},{3,2},{4,5},{5,4},{6,7},{7,6},{8,9},{9,8},{10,11... | collective-permute-start | bytes 98312 | tf_op jit(solution)/shard_map/ppermute | solution.py:355
  5.3 0.7 %copy-start.7 = (s32[32,128]{1,0:T(8,128)S(1)}, s32[32,128]{1,0:T(8,128)}, u32[]{:S(2)}) copy-start(s32[32,128]{1,0:T(8,128)} %slots.1) | copy-start | bytes 49156
  6.1 11.8 %copy-start.2 = (bf16[4,512,512]{2,1,0:T(8,128)(2,1)S(1)}, bf16[4,512,512]{2,1,0:T(8,128)(2,1)}, u32[]{:S(2)}) copy-start(bf16[4,512,512]{2,1,0:T(8,128)(2,1)} %kw.3) | copy-start | bytes 6291460
  6.1 11.8 %copy-start.3 = (bf16[4,512,512]{2,1,0:T(8,128)(2,1)S(1)}, bf16[4,512,512]{2,1,0:T(8,128)(2,1)}, u32[]{:S(2)}) copy-start(bf16[4,512,512]{2,1,0:T(8,128)(2,1)} %mw.3) | copy-start | bytes 6291460
  6.1 11.8 %copy-start.8 = (s32[32]{0:T(128)S(1)}, s32[32]{0:T(128)}, u32[]{:S(2)}) copy-start(s32[32]{0:T(128)} %rel_ref.9) | copy-start | bytes 388
  14.3 9.3 %collective-permute-start.6 = (bf16[128,512]{1,0:T(8,128)(2,1)S(1)}, bf16[128,512]{1,0:T(8,128)(2,1)S(1)}, u32[]{:S(2)}, u32[]{:S(2)}) collective-permute-start(bf16[128,512]{1,0:T(8,128)(2,1)S(1)} %assemble.1), channel_id=1, source_target_pairs={{0,6},{1,7},{2,4},{3,5},{4,2},{5,3},{6,0},{7,1},{8,14},{9,15},{10,... | collective-permute-start | bytes 393224 | tf_op jit(solution)/shard_map/ppermute | solution.py:355
  16.8 7.2 %collective-permute-start.5 = (bf16[128,512]{1,0:T(8,128)(2,1)S(1)}, bf16[128,512]{1,0:T(8,128)(2,1)S(1)}, u32[]{:S(2)}, u32[]{:S(2)}) collective-permute-start(bf16[128,512]{1,0:T(8,128)(2,1)S(1)} %assemble.1), channel_id=1, source_target_pairs={{0,4},{1,5},{2,6},{3,7},{4,0},{5,1},{6,2},{7,3},{8,12},{9,13},{10,... | collective-permute-start | bytes 393224 | tf_op jit(solution)/shard_map/ppermute | solution.py:355
  17.3 6.8 %collective-permute-start.4 = (bf16[128,512]{1,0:T(8,128)(2,1)S(1)}, bf16[128,512]{1,0:T(8,128)(2,1)S(1)}, u32[]{:S(2)}, u32[]{:S(2)}) collective-permute-start(bf16[128,512]{1,0:T(8,128)(2,1)S(1)} %assemble.1), channel_id=1, source_target_pairs={{0,2},{1,3},{2,0},{3,1},{4,6},{5,7},{6,4},{7,5},{8,10},{9,11},{10,... | collective-permute-start | bytes 393224 | tf_op jit(solution)/shard_map/ppermute | solution.py:355
  17.9 6.3 %copy-start = (bf16[512,512]{1,0:T(8,128)(2,1)S(1)}, bf16[512,512]{1,0:T(8,128)(2,1)}, u32[]{:S(2)}) copy-start(bf16[512,512]{1,0:T(8,128)(2,1)} %wq.5) | copy-start | bytes 1572868
  17.9 6.3 %copy-start.5 = (s32[32,128]{1,0:T(8,128)S(1)}, s32[32,128]{1,0:T(8,128)}, u32[]{:S(2)}) copy-start(s32[32,128]{1,0:T(8,128)} %merch_slot.5) | copy-start | bytes 49156
  17.9 6.3 %copy-start.9 = (s32[32]{0:T(128)S(1)}, s32[32]{0:T(128)}, u32[]{:S(2)}) copy-start(s32[32]{0:T(128)} %count_ref.5) | copy-start | bytes 388
  17.9 6.3 %copy-start.10 = (f32[4]{0:T(128)S(1)}, f32[4]{0:T(128)}, u32[]{:S(2)}) copy-start(f32[4]{0:T(128)} %bias_ref.5) | copy-start | bytes 52
  24.1 2.2 %collective-permute-start.7 = (bf16[512,512]{1,0:T(8,128)(2,1)S(1)}, bf16[512,512]{1,0:T(8,128)(2,1)S(1)}, u32[]{:S(2)}, u32[]{:S(2)}) collective-permute-start(bf16[512,512]{1,0:T(8,128)(2,1)S(1)} %pad_maximum_fusion.feats), channel_id=1, source_target_pairs={{0,1},{1,0},{2,3},{3,2},{4,5},{5,4},{6,7},{7,6},{8,9},{9,8},{10,11... | collective-permute-start | bytes 1572872 | tf_op jit(solution)/shard_map/ppermute | solution.py:355
  25.8 2.1 %collective-permute-start.8 = (bf16[512,512]{1,0:T(8,128)(2,1)S(1)}, bf16[512,512]{1,0:T(8,128)(2,1)S(1)}, u32[]{:S(2)}, u32[]{:S(2)}) collective-permute-start(bf16[512,512]{1,0:T(8,128)(2,1)S(1)} %aggregate_odd.1), channel_id=1, source_target_pairs={{0,1},{1,0},{2,3},{3,2},{4,5},{5,4},{6,7},{7,6},{8,9},{9,8},{10,11... | collective-permute-start | bytes 1572872 | tf_op jit(solution)/shard_map/ppermute | solution.py:355
  26.3 5.2 %copy-start.1 = (bf16[4096,512]{1,0:T(8,128)(2,1)S(1)}, bf16[4096,512]{1,0:T(8,128)(2,1)}, u32[]{:S(2)}) copy-start(bf16[4096,512]{1,0:T(8,128)(2,1)} %acct.1) | copy-start | bytes 12582916
  27.9 8.5 %collective-permute-start.9 = (bf16[128,512]{1,0:T(8,128)(2,1)S(1)}, bf16[128,512]{1,0:T(8,128)(2,1)S(1)}, u32[]{:S(2)}, u32[]{:S(2)}) collective-permute-start(bf16[128,512]{1,0:T(8,128)(2,1)S(1)} %get-tuple-element.31), channel_id=1, source_target_pairs={{0,6},{1,7},{2,4},{3,5},{4,2},{5,3},{6,0},{7,1},{8,14},{9,15},{10,... | collective-permute-start | bytes 393224 | tf_op jit(solution)/shard_map/ppermute | solution.py:355
  30.0 7.5 %collective-permute-start.10 = (bf16[128,512]{1,0:T(8,128)(2,1)S(1)}, bf16[128,512]{1,0:T(8,128)(2,1)S(1)}, u32[]{:S(2)}, u32[]{:S(2)}) collective-permute-start(bf16[128,512]{1,0:T(8,128)(2,1)S(1)} %get-tuple-element.32), channel_id=1, source_target_pairs={{0,4},{1,5},{2,6},{3,7},{4,0},{5,1},{6,2},{7,3},{8,12},{9,13},{10,... | collective-permute-start | bytes 393224 | tf_op jit(solution)/shard_map/ppermute | solution.py:355
  31.0 6.5 %collective-permute-start.11 = (bf16[128,512]{1,0:T(8,128)(2,1)S(1)}, bf16[128,512]{1,0:T(8,128)(2,1)S(1)}, u32[]{:S(2)}, u32[]{:S(2)}) collective-permute-start(bf16[128,512]{1,0:T(8,128)(2,1)S(1)} %get-tuple-element.33), channel_id=1, source_target_pairs={{0,2},{1,3},{2,0},{3,1},{4,6},{5,7},{6,4},{7,5},{8,10},{9,11},{10,... | collective-permute-start | bytes 393224 | tf_op jit(solution)/shard_map/ppermute | solution.py:355
  35.3 10.1 %copy-start.4 = (bf16[512,512]{1,0:T(8,128)(2,1)S(1)}, bf16[512,512]{1,0:T(8,128)(2,1)}, u32[]{:S(2)}) copy-start(bf16[512,512]{1,0:T(8,128)(2,1)} %wo.1) | copy-start | bytes 1572868
  35.3 10.1 %copy-start.6 = (bf16[32,512]{1,0:T(8,128)(2,1)S(1)}, bf16[32,512]{1,0:T(8,128)(2,1)}, u32[]{:S(2)}) copy-start(bf16[32,512]{1,0:T(8,128)(2,1)} %feat.1) | copy-start | bytes 98308
  35.3 10.1 %copy-start.11 = (f32[512]{0:T(512)S(1)}, f32[512]{0:T(512)}, u32[]{:S(2)}) copy-start(f32[512]{0:T(512)} %param.19) | copy-start | bytes 6148
  37.6 5.8 %collective-permute-start.12 = (bf16[32,512]{1,0:T(8,128)(2,1)S(1)}, bf16[32,512]{1,0:T(8,128)(2,1)S(1)}, u32[]{:S(2)}, u32[]{:S(2)}) collective-permute-start(bf16[32,512]{1,0:T(8,128)(2,1)S(1)} %get-tuple-element.38), channel_id=1, source_target_pairs={{0,24},{1,25},{2,26},{3,27},{4,28},{5,29},{6,30},{7,31},{8,16},{9,... | collective-permute-start | bytes 98312 | tf_op jit(solution)/shard_map/ppermute | solution.py:355
  40.3 5.1 %collective-permute-start.13 = (bf16[32,512]{1,0:T(8,128)(2,1)S(1)}, bf16[32,512]{1,0:T(8,128)(2,1)S(1)}, u32[]{:S(2)}, u32[]{:S(2)}) collective-permute-start(bf16[32,512]{1,0:T(8,128)(2,1)S(1)} %get-tuple-element.39), channel_id=1, source_target_pairs={{0,16},{1,17},{2,18},{3,19},{4,20},{5,21},{6,22},{7,23},{8,24},{9,... | collective-permute-start | bytes 98312 | tf_op jit(solution)/shard_map/ppermute | solution.py:355
  40.6 4.8 %collective-permute-start.14 = (bf16[32,512]{1,0:T(8,128)(2,1)S(1)}, bf16[32,512]{1,0:T(8,128)(2,1)S(1)}, u32[]{:S(2)}, u32[]{:S(2)}) collective-permute-start(bf16[32,512]{1,0:T(8,128)(2,1)S(1)} %get-tuple-element.40), channel_id=1, source_target_pairs={{0,8},{1,9},{2,10},{3,11},{4,12},{5,13},{6,14},{7,15},{8,0},{9,1},... | collective-permute-start | bytes 98312 | tf_op jit(solution)/shard_map/ppermute | solution.py:355
